TPU v7x, 32 devices: a whole 2x2x4 slice. The times are simulated.
32 devices in a mesh: replica: 8 (over z, x), fsdp: 4 (over y, core).
Axes of the slice: x: 2, y: 2, z: 4, core: 2. Of those that a mesh axis runs over, the one named last changes fastest.
Arguments:
- inputs: bfloat16 [16384, 4096], P(('replica', 'fsdp')), may hold values from -6 to 6
- kinds: int32 [16384], P(('replica', 'fsdp')), may hold values from 0 to 2
- weights: float32 [8, 2, 4096, 256], P('replica', None, 'fsdp'), may hold values from -0.09375 to 0.09375
- first_moment: float32 [8, 2, 4096, 256], P('replica', None, 'fsdp'), may hold values from -0.75 to 0.75
- second_moment: float32 [8, 2, 4096, 256], P('replica', None, 'fsdp'), may hold values from 0.01 to 1
- anchor: float32 [2, 4096, 256], P(None, 'fsdp'), may hold values from -0.09375 to 0.09375
- momentum: float32 [2, 4096, 256], P(None, 'fsdp'), may hold values from -0.75 to 0.75
- plan: int32 [8], replicated, may hold values from 1 to 8
Outputs:
- new_weights: float32 [8, 2, 4096, 256], P('replica', None, 'fsdp')
- new_first: float32 [8, 2, 4096, 256], P('replica', None, 'fsdp')
- new_second: float32 [8, 2, 4096, 256], P('replica', None, 'fsdp')
- new_anchor: float32 [2, 4096, 256], P(None, 'fsdp')
- new_momentum: float32 [2, 4096, 256], P(None, 'fsdp')
All inputs are finite; a program needn't handle non-finite values.
Results may differ from a plain program's by a relative error of at most 0.014.
Values may be sent and summed in bfloat16 or wider, within the bound.
No kernel may reach another device: no remote copies, remote signals or barrier semaphores. Data moves between devices by JAX's collectives and lax.ppermute only.
A program may use at most 128 MiB of HBM per device.

v0:
```python
import math

import jax
import jax.numpy as jnp
from jax import lax
from jax.sharding import PartitionSpec as P

INNER = 2


inner_rate = 0.003
beta_one = 0.9
beta_two = 0.95
adam_eps = 1e-08
decay_rate = 0.1
outer_rate = 0.7
outer_mu = 0.9
mix_share = 0.5


def token_weight(kinds):
    return jnp.where(kinds == 2, 1.0, jnp.where(kinds == 1, 0.25, 0.0)).astype(jnp.float32)


def silu_slope(pre):
    sig = jax.nn.sigmoid(pre)
    return sig * (1.0 + pre * (1.0 - sig))


def adam_update(theta, first, second, grad):
    first = beta_one * first + (1.0 - beta_one) * grad
    second = beta_two * second + (1.0 - beta_two) * grad * grad
    theta = theta - inner_rate * (first / (jnp.sqrt(second) + adam_eps) + decay_rate * theta)
    return (theta, first, second)


def inner_step(inputs, weight_rows, theta, first, second, scale):
    low = theta.astype(jnp.bfloat16)
    width = theta.shape[2]
    columns = inputs
    pre = jnp.dot(
        columns,
        lax.all_gather(low[0], "fsdp", axis=0, tiled=True),
        preferred_element_type=jnp.float32,
    )
    hidden = jax.nn.silu(pre).astype(jnp.bfloat16)
    output = lax.dot_general(
        hidden,
        lax.all_gather(low[1], "fsdp", axis=0, tiled=True),
        (((1,), (1,)), ((), ())),
        preferred_element_type=jnp.float32,
    )
    resid = output - inputs.astype(jnp.float32)
    slope_out = (weight_rows[:, None] * resid * scale).astype(jnp.bfloat16)
    columns = slope_out
    back = jnp.dot(
        columns,
        lax.all_gather(low[1], "fsdp", axis=0, tiled=True),
        preferred_element_type=jnp.float32,
    )
    slope_pre = (back * silu_slope(pre)).astype(jnp.bfloat16)
    grad_enc = lax.dot_general(
        inputs, slope_pre, (((0,), (0,)), ((), ())), preferred_element_type=jnp.float32
    )
    grad_dec = lax.dot_general(
        slope_out, hidden, (((0,), (0,)), ((), ())), preferred_element_type=jnp.float32
    )
    grads = lax.psum_scatter(
        jnp.concatenate([grad_enc, grad_dec], 1).astype(jnp.bfloat16),
        "fsdp",
        scatter_dimension=0,
        tiled=True,
    ).astype(jnp.float32)
    grad = jnp.stack([grads[:, :width], grads[:, width:]], 0)
    return adam_update(theta, first, second, grad)


def local(inputs, kinds, weights, first_moment, second_moment, anchor, momentum, plan):
    theta = weights[0]
    first = first_moment[0]
    second = second_moment[0]
    scale = 1.0 / math.sqrt(inputs.shape[0] * lax.axis_size("fsdp"))
    weight_rows = token_weight(kinds)
    total_int = jnp.sum(plan)
    frag = total_int % 2
    counts = plan.astype(jnp.float32)
    total = jnp.sum(counts)
    own_count = lax.dynamic_slice_in_dim(counts, lax.axis_index("replica"), 1, 0)[0]
    pick = lax.broadcasted_iota(jnp.int32, (2, 1, 1), 0) == frag
    anchor_frag = jnp.sum(jnp.where(pick, anchor, 0.0), 0)
    mom_frag = jnp.sum(jnp.where(pick, momentum, 0.0), 0)
    delta = own_count * (anchor_frag - jnp.sum(jnp.where(pick, theta, 0.0), 0))
    outer_grad = lax.psum(delta.astype(jnp.bfloat16), "replica").astype(jnp.float32) / total
    new_mom = outer_mu * mom_frag + outer_grad
    new_anc = anchor_frag - outer_rate * (outer_grad + outer_mu * new_mom)
    for step in range(INNER):
        theta, first, second = inner_step(inputs, weight_rows, theta, first, second, scale)
        if step == 0:
            mixed = mix_share * theta + (1.0 - mix_share) * new_anc[None]
            theta = jnp.where(pick, mixed, theta)
    anchor_out = jnp.where(pick, new_anc[None], anchor)
    momentum_out = jnp.where(pick, new_mom[None], momentum)
    return (theta[None], first[None], second[None], anchor_out, momentum_out)


def solution(mesh):
    return jax.shard_map(
        local,
        mesh=mesh,
        in_specs=(
            P(("replica", "fsdp"), None),
            P(("replica", "fsdp")),
            P("replica", None, "fsdp", None),
            P("replica", None, "fsdp", None),
            P("replica", None, "fsdp", None),
            P(None, "fsdp", None),
            P(None, "fsdp", None),
            P(),
        ),
        out_specs=(
            P("replica", None, "fsdp", None),
            P("replica", None, "fsdp", None),
            P("replica", None, "fsdp", None),
            P(None, "fsdp", None),
            P(None, "fsdp", None),
        ),
        check_vma=False,
    )
```

profile of v0, /device:TPU:0, one launch (start us, length us, event | category | flops | bytes accessed | tf_op | source)
XLA Modules:
  0.0 280.2 jit_solution(10581260581822030149)
XLA Ops:
  14.6 2.9 %copy.18 = f32[2,1024,256]{1,2,0:T(8,128)} copy(f32[2,1024,256]{2,1,0:T(8,128)} %param.13) | data formatting | bytes 4194304 | tf_op args[5]
  21.0 4.9 %select_reduce_fusion = (f32[1024,256]{0,1:T(8,128)}, f32[1024,256]{0,1:T(8,128)S(1)}, f32[1024,256]{0,1:T(8,128)S(1)}) fusion(f32[2,1024,256]{1,2,0:T(8,128)} %copy.19, pred[2]{0:T(512)(128)(4,1)S(1)} %iota_compare_fusion, f32[1,2,1024,256]{2,3,1,0:T(8,128)S(1)} %copy.17, f32[2,1024,256]{1,2,0:T(8,128)} %copy.18), kind=kLoop, calls=%fused_computation.49 | loop fusion | flops 2359296 | bytes 9437186 | tf_op jit(solution)/shard_map/reduce_sum | solution.py:91
  28.7 8.0 %all-gather.9.cloned.1.call-done = bf16[1,4096,256]{1,2,0:T(8,128)(2,1)} async-done(((bf16[1,1024,256]{1,2,0:T(8,128)(2,1)}), bf16[1,4096,256]{1,2,0:T(8,128)(2,1)}) %all-gather.9.cloned.1.call-update) | async-done | bytes 2097168 | tf_op jit(solution)/shard_map/all_gather | solution.py:43
  36.7 4.1 %fusion.25 = f32[512,256]{1,0:T(8,128)S(1)} fusion(bf16[512,4096]{1,0:T(8,128)(2,1)} %param.8, bf16[1,4096,256]{1,2,0:T(8,128)(2,1)} %all-gather.9.cloned.1.call-done), kind=kOutput, calls=%fused_computation.40 | convolution fusion | flops 1073741824 | bytes 6815744 | tf_op jit(solution)/shard_map/dot_general | solution.py:41
  40.8 20.6 %all-gather.11.cloned.1.call-done = bf16[1,4096,256]{1,2,0:T(8,128)(2,1)} async-done(((bf16[1,1024,256]{1,2,0:T(8,128)(2,1)}), bf16[1,4096,256]{1,2,0:T(8,128)(2,1)}) %all-gather.11.cloned.1.call-update) | async-done | bytes 2097168 | tf_op jit(solution)/shard_map/all_gather | solution.py:49
  61.5 4.5 %fusion.2 = bf16[512,4096]{1,0:T(8,128)(2,1)S(1)} fusion(bf16[512,4096]{1,0:T(8,128)(2,1)} %param.8, f32[512]{0:T(512)S(1)} %select_select_fusion, bf16[1,4096,256]{1,2,0:T(8,128)(2,1)} %all-gather.11.cloned.1.call-done, f32[512,256]{1,0:T(8,128)S(1)} %fusion.25), kind=kOutput, calls=%fused_computation.4 | convolution fusion | flops 1084882944 | bytes 11012096 | tf_op jit(solution)/shard_map/dot_general | solution.py:47
  70.6 10.0 %fusion.6 = bf16[4096,256]{0,1:T(8,128)(2,1)} fusion(bf16[512,4096]{1,0:T(8,128)(2,1)} %param.8, bf16[512,4096]{1,0:T(8,128)(2,1)} %copy-done.7, bf16[1,4096,256]{1,2,0:T(8,128)(2,1)} %all-gather.11.cloned.1.call-done, f32[512,256]{1,0:T(8,128)S(1)} %fusion.25), kind=kOutput, calls=%fused_computation.12 | convolution fusion | flops 2149711872 | bytes 13107200 | tf_op jit(solution)/shard_map/dot_general | solution.py:62
  80.7 4.7 %pad_maximum_fusion = bf16[4096,512]{0,1:T(8,128)(2,1)} fusion(bf16[4096,256]{0,1:T(8,128)(2,1)} %convolution_convert_fusion.2, bf16[4096,256]{0,1:T(8,128)(2,1)} %fusion.6), kind=kLoop, calls=%fused_computation.14 | loop fusion | flops 8388608 | bytes 8388608 | tf_op jit(solution)/shard_map/concatenate | solution.py:69
  85.6 2.9 %copy.13 = f32[1,2,1024,256]{2,3,1,0:T(8,128)} copy(f32[1,2,1024,256]{3,2,1,0:T(8,128)} %param.11) | data formatting | bytes 4194304 | tf_op args[3]
  88.5 2.9 %copy.15 = f32[1,2,1024,256]{2,3,1,0:T(8,128)} copy(f32[1,2,1024,256]{3,2,1,0:T(8,128)} %param.12) | data formatting | bytes 4194304 | tf_op args[4]
  92.0 11.2 %all-reduce.2.cloned.1.call-done = bf16[1024,256]{0,1:T(8,128)(2,1)} async-done(((bf16[1024,256]{0,1:T(8,128)(2,1)}), bf16[1024,256]{0,1:T(8,128)(2,1)}) %all-reduce.2.cloned.1.call-update) | async-done | bytes 524304 | tf_op jit(solution)/shard_map/psum | solution.py:93
  103.2 4.5 %broadcast_multiply_fusion = (f32[1024,256]{0,1:T(8,128)S(1)}, f32[1024,256]{0,1:T(8,128)}, f32[1024,256]{0,1:T(8,128)}) fusion(f32[1024,256]{0,1:T(8,128)} %copy-done.8, f32[1024,256]{0,1:T(8,128)} %get-tuple-element.10, f32[]{:T(128)} %convert_reduce_fusion, bf16[1024,256]{0,1:T(8,128)(2,1)} %all-reduce.2.cloned.1.call-done), kind=kLoop, calls=%fused_computation.75 | loop fusion | flops 2359296 | bytes 5767172 | tf_op jit(solution)/shard_map/mul | solution.py:99
  107.7 22.4 %reduce-scatter.3.cloned.1.call-done = bf16[1024,512]{0,1:T(8,128)(2,1)} async-done(((bf16[4096,512]{0,1:T(8,128)(2,1)}), bf16[1024,512]{0,1:T(8,128)(2,1)}) %reduce-scatter.3.cloned.1.call-update) | async-done | bytes 1048592 | tf_op jit(solution)/shard_map/reduce_scatter | solution.py:68
  135.4 4.4 %broadcast_select_fusion = (f32[2,1024,256]{1,2,0:T(8,128)}, bf16[2,1024,256]{1,2,0:T(8,128)(2,1)S(1)}, f32[2,1024,256]{1,2,0:T(8,128)}) fusion(f32[2,1024,256]{1,2,0:T(8,128)S(1)} %copy-done.5, f32[1024,256]{0,1:T(8,128)} %get-tuple-element.24, pred[2]{0:T(512)(128)(4,1)S(1)} %iota_compare_fusion, f32[1024,256]{0,1:T(8,128)S(1)} %get-tuple-element.13, ...), kind=kLoop, calls=%fused_computation.59 | loop fusion | flops 10485760 | bytes 20971522 | tf_op jit(solution)/shard_map/jit(_where)/select_n | solution.py:102
  141.4 22.1 %all-gather.13.cloned.1.call-done = bf16[1,4096,256]{1,2,0:T(8,128)(2,1)} async-done(((bf16[1,1024,256]{1,2,0:T(8,128)(2,1)}), bf16[1,4096,256]{1,2,0:T(8,128)(2,1)}) %all-gather.13.cloned.1.call-update) | async-done | bytes 2097168 | tf_op jit(solution)/shard_map/all_gather | solution.py:43
  163.6 4.9 %fusion.31 = f32[512,256]{1,0:T(8,128)} fusion(bf16[512,4096]{1,0:T(8,128)(2,1)} %param.8, bf16[1,4096,256]{1,2,0:T(8,128)(2,1)} %all-gather.13.cloned.1.call-done), kind=kOutput, calls=%fused_computation.53 | convolution fusion | flops 1073741824 | bytes 6815744 | tf_op jit(solution)/shard_map/dot_general | solution.py:41
  168.5 19.1 %all-gather.15.cloned.1.call-done = bf16[1,4096,256]{1,2,0:T(8,128)(2,1)} async-done(((bf16[1,1024,256]{1,2,0:T(8,128)(2,1)}), bf16[1,4096,256]{1,2,0:T(8,128)(2,1)}) %all-gather.15.cloned.1.call-update) | async-done | bytes 2097168 | tf_op jit(solution)/shard_map/all_gather | solution.py:49
  187.6 4.7 %fusion.5 = bf16[512,4096]{1,0:T(8,128)(2,1)S(1)} fusion(bf16[512,4096]{1,0:T(8,128)(2,1)} %param.8, f32[512]{0:T(512)S(1)} %select_select_fusion, bf16[1,4096,256]{1,2,0:T(8,128)(2,1)} %all-gather.15.cloned.1.call-done, f32[512,256]{1,0:T(8,128)} %fusion.31), kind=kOutput, calls=%fused_computation.7 | convolution fusion | flops 1084882944 | bytes 11012096 | tf_op jit(solution)/shard_map/dot_general | solution.py:47
  196.9 10.2 %fusion.7 = bf16[4096,256]{0,1:T(8,128)(2,1)} fusion(bf16[512,4096]{1,0:T(8,128)(2,1)} %param.8, bf16[512,4096]{1,0:T(8,128)(2,1)} %copy-done.6, bf16[1,4096,256]{1,2,0:T(8,128)(2,1)} %all-gather.15.cloned.1.call-done, f32[512,256]{1,0:T(8,128)} %fusion.31), kind=kOutput, calls=%fused_computation.13 | convolution fusion | flops 2149711872 | bytes 13107200 | tf_op jit(solution)/shard_map/dot_general | solution.py:62
  207.1 4.7 %pad_maximum_fusion.1 = bf16[4096,512]{0,1:T(8,128)(2,1)} fusion(bf16[4096,256]{0,1:T(8,128)(2,1)} %convolution_convert_fusion, bf16[4096,256]{0,1:T(8,128)(2,1)} %fusion.7), kind=kLoop, calls=%fused_computation.15 | loop fusion | flops 8388608 | bytes 8388608 | tf_op jit(solution)/shard_map/concatenate | solution.py:69
  214.6 2.9 %copy.27 = f32[2,1024,256]{2,1,0:T(8,128)} copy(f32[2,1024,256]{1,2,0:T(8,128)} %get-tuple-element.29) | data formatting | bytes 4194304
  217.5 38.9 %reduce-scatter.5.cloned.1.call-done = bf16[1024,512]{0,1:T(8,128)(2,1)} async-done(((bf16[4096,512]{0,1:T(8,128)(2,1)}), bf16[1024,512]{0,1:T(8,128)(2,1)}) %reduce-scatter.5.cloned.1.call-update) | async-done | bytes 1048592 | tf_op jit(solution)/shard_map/reduce_scatter | solution.py:68
  260.3 4.7 %fusion.16 = (f32[1,2,1024,256]{2,3,1,0:T(8,128)}, f32[1,2,1024,256]{2,3,1,0:T(8,128)}, f32[1,2,1024,256]{2,3,1,0:T(8,128)}) fusion(f32[1,1,1024,256]{2,3,1,0:T(8,128)S(1)} %get-tuple-element.19, f32[1,1,1024,256]{2,3,1,0:T(8,128)S(1)} %get-tuple-element.18, f32[1,1,1024,256]{2,3,1,0:T(8,128)S(1)} %copy-done.10, f32[1,1,1024,256]{2,3,1,0:T(8,128)S(1)} %copy-done.11, ...), kind=kLoop, calls=%fused_computation.27 | loop fusion | flops 16252928 | bytes 17825794 | tf_op jit(solution)/shard_map/add | solution.py:32
  267.9 3.0 %copy.24 = f32[1,2,1024,256]{3,2,1,0:T(8,128)} copy(f32[1,2,1024,256]{2,3,1,0:T(8,128)} %get-tuple-element.17) | data formatting | bytes 4194304
  (66 shorter events, 39.4 us)
Async XLA Ops:
  8.0 28.7 %all-gather.9.cloned.1.call-start = ((), (), s32[]{:S(2)}) async-start(), calls=%async_computation.5 | async-start | bytes 2621440 | tf_op jit(solution)/shard_map/all_gather | solution.py:43
  10.1 1.9 copy-start.15
  11.2 50.3 %all-gather.11.cloned.1.call-start = ((), (), s32[]{:S(2)}) async-start(), calls=%async_computation.6 | async-start | bytes 2621440 | tf_op jit(solution)/shard_map/all_gather | solution.py:49
  12.0 91.3 %all-reduce.2.cloned.1.call-start = ((), (), s32[]{:S(2)}) async-start(), calls=%async_computation.3 | async-start | bytes 1048576 | tf_op jit(solution)/shard_map/psum | solution.py:93
  25.9 1.0 copy-start.8
  25.9 2.8 copy-start.14
  28.6 101.4 %reduce-scatter.3.cloned.1.call-start = ((), (), s32[]{:S(2)}) async-start(), calls=%async_computation.2 | async-start | bytes 5242880 | tf_op jit(solution)/shard_map/reduce_scatter | solution.py:68
  66.0 1.9 copy-start.7
  85.4 78.2 %all-gather.13.cloned.1.call-start = ((), (), s32[]{:S(2)}) async-start(), calls=%async_computation.7 | async-start | bytes 2621440 | tf_op jit(solution)/shard_map/all_gather | solution.py:43
  130.0 3.4 %copy-start.5 = (f32[2,1024,256]{1,2,0:T(8,128)S(1)}, f32[2,1024,256]{1,2,0:T(8,128)}, u32[]{:S(2)}) copy-start(f32[2,1024,256]{1,2,0:T(8,128)} %copy.19) | copy-start | bytes 6291460
  130.0 3.4 %copy-start.12 = (f32[1024,256]{0,1:T(8,128)S(1)}, f32[1024,256]{0,1:T(8,128)}, u32[]{:S(2)}) copy-start(f32[1024,256]{0,1:T(8,128)} %get-tuple-element.14) | copy-start | bytes 3145732
  131.7 2.3 copy-start
  131.7 3.1 %copy-start.2 = (f32[1,2,1024,256]{2,3,1,0:T(8,128)S(1)}, f32[1,2,1024,256]{2,3,1,0:T(8,128)}, u32[]{:S(2)}) copy-start(f32[1,2,1024,256]{2,3,1,0:T(8,128)} %copy.15) | copy-start | bytes 6291460
  131.7 3.7 %copy-start.4 = (f32[2,1024,256]{1,2,0:T(8,128)S(1)}, f32[2,1024,256]{1,2,0:T(8,128)}, u32[]{:S(2)}) copy-start(f32[2,1024,256]{1,2,0:T(8,128)} %copy.18) | copy-start | bytes 6291460
  140.8 46.8 %all-gather.15.cloned.1.call-start = ((), (), s32[]{:S(2)}) async-start(), calls=%async_computation.8 | async-start | bytes 2621440 | tf_op jit(solution)/shard_map/all_gather | solution.py:49
  141.4 115.0 %reduce-scatter.5.cloned.1.call-start = ((), (), s32[]{:S(2)}) async-start(), calls=%async_computation.4 | async-start | bytes 5242880 | tf_op jit(solution)/shard_map/reduce_scatter | solution.py:68
  187.6 6.6 %copy-start.13 = (f32[512,256]{1,0:T(8,128)S(1)}, f32[512,256]{1,0:T(8,128)}, u32[]{:S(2)}) copy-start(f32[512,256]{1,0:T(8,128)} %fusion.31) | copy-start | bytes 1572868
  192.3 1.9 copy-start.6
  256.4 1.8 copy-start.10
  256.4 1.9 copy-start.11
  258.0 1.7 copy-start.1
  258.1 2.3 copy-start.3
  267.9 3.0 %copy-start.9 = (f32[1,2,1024,256]{2,3,1,0:T(8,128)S(1)}, f32[1,2,1024,256]{2,3,1,0:T(8,128)}, u32[]{:S(2)}) copy-start(f32[1,2,1024,256]{2,3,1,0:T(8,128)} %get-tuple-element.15) | copy-start | bytes 6291460
Sparse Core Ops, SparseCore 0:
  11.3 25.3 all-gather.8
  38.8 22.6 all-gather.10
  85.5 44.5 reduce-scatter.2
  140.9 22.5 all-gather.12
  165.0 22.5 all-gather.14
  211.9 44.4 reduce-scatter.4
Sparse Core Ops, SparseCore 1:
  28.7 74.5 all-reduce.1
where the time goes:
time: 281 us; the launch traced here: 280 us
  waiting for transfers between devices  144 us (51%)
  matrix products  43.8 us (16%)
  local copies, waits for them, and re-layouts  40.5 us (14%)
  other arithmetic  34.1 us (12%)
  between operations  17.7 us (6%)
    reduce_scatter x2, waiting for transfers between devices, inner_step(): lax.psum_scatter(jnp.concatenate([grad_enc, grad_dec], 1).astype(jnp.bflo...  61.2 us
    all_gather x2, waiting for transfers between devices, inner_step(): lax.all_gather(low[1], 'fsdp', axis=0, tiled=True)  39.8 us
    unnamed x42, local copies, waits for them, and re-layouts  35.9 us
    all_gather x2, waiting for transfers between devices, inner_step(): lax.all_gather(low[0], 'fsdp', axis=0, tiled=True)  30.1 us
    dot_general x2, matrix products, inner_step(): lax.dot_general(inputs, slope_pre, (((0,), (0,)), ((), ())), preferred_el...  20.2 us
    psum x1, waiting for transfers between devices, local(): lax.psum(delta.astype(jnp.bfloat16), 'replica').astype(jnp.float32) / total  11.2 us
    concatenate x2, other arithmetic, inner_step(): jnp.concatenate([grad_enc, grad_dec], 1).astype(jnp.bfloat16)  9.32 us
    dot_general x2, matrix products, inner_step(): lax.dot_general(hidden, lax.all_gather(low[1], 'fsdp', axis=0, tiled=True...  9.14 us
  transfers between devices with their start and end apart: 7, of which 7 were waited for; matrix products, arithmetic and copies ran while one was open for 22% of the time, Pallas kernels for 0%

commit v1 on v0

v1 whole, which is shorter than its diff:
```python
import functools
import math

import jax
import jax.numpy as jnp
from jax import lax
from jax.experimental import pallas as pl
from jax.experimental.pallas import tpu as pltpu
from jax.sharding import PartitionSpec as P

INNER = 2

inner_rate = 0.003
beta_one = 0.9
beta_two = 0.95
adam_eps = 1e-08
decay_rate = 0.1
outer_rate = 0.7
outer_mu = 0.9
mix_share = 0.5

bf16 = jnp.bfloat16
f32 = jnp.float32
VMEM_LIMIT = 24 * 1024 * 1024


def token_weight(kinds):
    return jnp.where(kinds == 2, 1.0, jnp.where(kinds == 1, 0.25, 0.0)).astype(f32)


def dot(a, b):
    return jnp.dot(a, b, preferred_element_type=f32)


def dot_rows(a, b):
    return lax.dot_general(a, b, (((0,), (0,)), ((), ())), preferred_element_type=f32)


def whole(shape):
    return pl.BlockSpec(shape, lambda *_: (0,) * len(shape))


def sds(shape, dtype):
    return jax.ShapeDtypeStruct(shape, dtype)


def call(body, name, meta, ins, outs, grid=(1,), scratch=(), aliases=None, flops=0):
    arrays = [a for a, _ in ins]
    moved = sum(math.prod(o.shape) * o.dtype.itemsize for o, _ in outs)
    moved += sum(math.prod(a.shape) * a.dtype.itemsize for a, _ in ins)
    out = pl.pallas_call(
        body,
        name=name,
        out_shape=[o for o, _ in outs],
        grid_spec=pltpu.PrefetchScalarGridSpec(
            num_scalar_prefetch=1,
            grid=grid,
            in_specs=[s for _, s in ins],
            out_specs=[s for _, s in outs],
            scratch_shapes=list(scratch),
        ),
        input_output_aliases=aliases or {},
        compiler_params=pltpu.CompilerParams(vmem_limit_bytes=VMEM_LIMIT),
        cost_estimate=pl.CostEstimate(flops=flops, bytes_accessed=moved, transcendentals=0),
    )(meta, *arrays)
    return out


def cast_body(meta, theta, low):
    width = theta.shape[-1]
    low[:, :width] = theta[0, 0].astype(bf16)
    low[:, width:] = theta[0, 1].astype(bf16)


def cast_chunk(meta, weights, i, cr):
    width = weights.shape[-1]
    return call(
        cast_body, "cast_rows", meta,
        [(weights, pl.BlockSpec((1, 2, cr, width), lambda g, m: (0, 0, i, 0)))],
        [(sds((cr, 2 * width), bf16), whole((cr, 2 * width)))],
    )[0]


def turn_body(meta, x, xt):
    xt[...] = x[...].T


def turn(meta, x, slots, rows, tile):
    tokens = x.shape[0]
    per = rows // tile
    return call(
        turn_body, "turn_tokens", meta,
        [(x, pl.BlockSpec((tokens, tile), lambda g, m: (0, m[slots + g // per] * per + g % per)))],
        [(sds((_chips(meta, slots) * rows, tokens), bf16), pl.BlockSpec((tile, tokens), lambda g, m: (g, 0)))],
        grid=(_chips(meta, slots) * per,),
    )[0]


def _chips(meta, slots):
    return (meta.shape[0] - slots) // 2


def forward_body(count, first_call, *refs):
    meta, refs = refs[0], refs[1:]
    if first_call:
        acc_in = gram_in = None
    else:
        acc_in, gram_in, refs = refs[0], refs[1], refs[2:]
    lows = refs[:count]
    xs = (refs[count:2 * count], refs[2 * count:3 * count])
    acc, gram = refs[3 * count:]
    width = gram.shape[0]
    total = None if first_call else gram_in[...]
    for p in range(count):
        dec = lows[p][:, width:]
        term = dot_rows(dec, dec)
        total = term if total is None else total + term
    gram[...] = total
    for h in range(2):
        value = None if first_call else acc_in[h]
        for p in range(count):
            term = dot(xs[h][p][...], lows[p][...])
            value = term if value is None else value + term
        acc[h] = value


def forward(meta, acc, gram, pieces, x_own, x_par, cr):
    tokens = x_own.shape[0]
    wide = pieces[0][0].shape[1]
    width = wide // 2
    count = len(pieces)
    ins = []
    if acc is not None:
        ins += [(acc, whole(acc.shape)), (gram, whole(gram.shape))]
    ins += [(low, whole(low.shape)) for low, _, _ in pieces]
    for x in (x_own, x_par):
        for low, slot, i in pieces:
            ins.append((x, _columns(tokens, cr, slot, i, meta, x)))
    return call(
        functools.partial(forward_body, count, acc is None), "forward_rows", meta, ins,
        [(sds((2, tokens, wide), f32), whole((2, tokens, wide))), (sds((width, width), f32), whole((width, width)))],
        flops=4 * tokens * cr * wide * count,
    )


def _columns(tokens, cr, slot, i, meta, x):
    per = x.shape[1] // (meta.shape[0] - FIRST_SLOT) // cr
    return pl.BlockSpec((tokens, cr), lambda g, m: (0, m[slot] * per + i))


FIRST_SLOT = 4


def finish_body(scale, count, steps, *refs):
    meta, acc_in, gram_in, cw = refs[:4]
    refs = refs[4:]
    lows = refs[:count]
    xs = (refs[count:2 * count], refs[2 * count:3 * count])
    slopes, w_hi, w_lo, w_acc = refs[3 * count:]
    width = gram_in.shape[0]
    gram = gram_in[...]
    for p in range(count):
        dec = lows[p][:, width:]
        gram = gram + dot_rows(dec, dec)
    g_hi = gram.astype(bf16)
    g_lo = (gram - g_hi.astype(f32)).astype(bf16)
    w_new = None
    for h in range(2):
        value = acc_in[h]
        for p in range(count):
            value = value + dot(xs[h][p][...], lows[p][...])
        pre = value[:, :width]
        sig = 1.0 / (1.0 + jnp.exp(-pre))
        hidden = (pre * sig).astype(bf16)
        back = dot(hidden, g_hi) + dot(hidden, g_lo) - value[:, width:]
        weight = cw[h]
        slope = (weight * scale) * back * (sig * (1.0 + pre * (1.0 - sig)))
        counted = (weight * hidden.astype(f32)).astype(bf16)
        slopes[h, :, :width] = slope.astype(bf16)
        slopes[h, :, width:] = counted
        term = dot_rows(counted, hidden)
        w_new = term if w_new is None else w_new + term
    step = pl.program_id(0)

    @pl.when(step == 0)
    def _():
        w_acc[...] = w_new

    @pl.when(step > 0)
    def _():
        w_acc[...] += w_new

    @pl.when(step == steps - 1)
    def _():
        total = w_acc[...]
        hi = total.astype(bf16)
        w_hi[...] = hi
        w_lo[...] = (total - hi.astype(f32)).astype(bf16)


def finish(meta, acc, gram, cw, pieces, x_own, x_par, cr, scale):
    tokens = x_own.shape[0]
    wide = pieces[0][0].shape[1]
    width = wide // 2
    count = len(pieces)
    steps = 2
    tile = tokens // steps
    per = x_own.shape[1] // (meta.shape[0] - FIRST_SLOT) // cr
    ins = [
        (acc, pl.BlockSpec((2, tile, wide), lambda g, m: (0, g, 0))),
        (gram, whole(gram.shape)),
        (cw, pl.BlockSpec((2, tile, 1), lambda g, m: (0, g, 0))),
    ]
    ins += [(low, whole(low.shape)) for low, _, _ in pieces]
    for x in (x_own, x_par):
        for low, slot, i in pieces:
            ins.append((x, pl.BlockSpec((tile, cr), lambda g, m, slot=slot, i=i: (g, m[slot] * per + i))))
    square = (sds((width, width), bf16), whole((width, width)))
    return call(
        functools.partial(finish_body, scale, count, steps), "finish_slopes", meta, ins,
        [(sds((2, tokens, wide), bf16), pl.BlockSpec((2, tile, wide), lambda g, m: (0, g, 0))), square, square],
        grid=(steps,),
        scratch=[pltpu.VMEM((width, width), f32)],
        flops=4 * tokens * cr * wide * count + 12 * tokens * width * width,
    )


def row_grad(scale, xt_own, xt_par, slopes, w_hi, w_lo, low):
    width = w_hi.shape[0]
    both = dot(xt_own[...], slopes[0]) + dot(xt_par[...], slopes[1])
    dec = low[:, width:]
    grad_dec = scale * (dot(dec, w_hi[...]) + dot(dec, w_lo[...]) - both[:, width:])
    return both[:, :width], grad_dec


def grad_body(scale, meta, xt_own, xt_par, slopes, w_hi, w_lo, low, out):
    width = w_hi.shape[0]
    enc, dec = row_grad(scale, xt_own, xt_par, slopes, w_hi, w_lo, low)
    out[:, :width] = enc.astype(bf16)
    out[:, width:] = dec.astype(bf16)


def grad_inputs(block, cr, xt, slopes, w_hi, w_lo, low):
    tokens = xt[0].shape[1]
    ins = [(x, pl.BlockSpec((cr, tokens), lambda g, m: (block, 0))) for x in xt]
    return ins + [(a, whole(a.shape)) for a in (slopes, w_hi, w_lo, low)]


def grad_rows(meta, scale, block, cr, xt, slopes, w_hi, w_lo, low):
    wide = low.shape[1]
    return call(
        functools.partial(grad_body, scale), "grad_rows", meta,
        grad_inputs(block, cr, xt, slopes, w_hi, w_lo, low),
        [(sds((cr, wide), bf16), whole((cr, wide)))],
        flops=4 * xt[0].shape[1] * cr * wide,
    )[0]


def adam_body(scale, last, count, *refs):
    meta, xt_own, xt_par, slopes, w_hi, w_lo, low = refs[:7]
    got = refs[7:7 + count]
    theta, first, second = refs[7 + count:10 + count]
    refs = refs[10 + count:]
    width = w_hi.shape[0]
    grads = row_grad(scale, xt_own, xt_par, slopes, w_hi, w_lo, low)
    if last:
        theta_out, first_out, second_out = refs[-3:]
    else:
        anchor = refs[0]
        theta_out, first_out, second_out, low_out = refs[-4:]
    for k in range(2):
        grad = grads[k]
        for g in got:
            grad = grad + g[:, k * width:(k + 1) * width].astype(f32)
        one = beta_one * first[0, k] + (1.0 - beta_one) * grad
        two = beta_two * second[0, k] + (1.0 - beta_two) * grad * grad
        old = theta[0, k]
        new = old - inner_rate * (one / (jnp.sqrt(two) + adam_eps) + decay_rate * old)
        if not last:
            mixed = mix_share * new + (1.0 - mix_share) * anchor[...]
            new = jnp.where(meta[0] == k, mixed, new)
            low_out[:, k * width:(k + 1) * width] = new.astype(bf16)
        theta_out[0, k] = new
        first_out[0, k] = one
        second_out[0, k] = two


def adam_rows(meta, scale, i, cr, xt, slopes, w_hi, w_lo, low, got, state, state_block, new_anc, prev, full):
    width = low.shape[1] // 2
    last = new_anc is None
    block = (1, 2, cr, width)
    ins = grad_inputs(i, cr, xt, slopes, w_hi, w_lo, low)
    ins += [(g, whole(g.shape)) for g in got]
    ins += [(s, pl.BlockSpec(block, lambda g, m: (0, 0, state_block, 0))) for s in state]
    aliases = {}
    if last:
        if prev is not None:
            for n, p in enumerate(prev):
                aliases[1 + len(ins)] = n
                ins.append((p, pl.BlockSpec(memory_space=pl.ANY)))
        outs = [(sds(full, f32), pl.BlockSpec(block, lambda g, m: (0, 0, i, 0)))] * 3
    else:
        ins.append((new_anc, pl.BlockSpec((cr, width), lambda g, m: (i, 0))))
        outs = [(sds(block, f32), whole(block))] * 3 + [(sds((cr, 2 * width), bf16), whole((cr, 2 * width)))]
    return call(
        functools.partial(adam_body, scale, last, len(got)), "adam_rows", meta, ins, outs,
        aliases=aliases, flops=8 * xt[0].shape[1] * cr * width,
    )


def delta_body(order, meta, anchor, theta, *outs):
    rows = outs[0].shape[0]
    count = meta[1].astype(f32)
    for m, out in enumerate(outs):
        at = pl.ds(pl.multiple_of(order(meta[2], m) * rows, rows), rows)
        out[...] = (count * (anchor[0, at, :] - theta[0, 0, at, :])).astype(bf16)


def sum_body(meta, *refs):
    total = refs[0][...].astype(f32)
    for r in refs[1:-1]:
        total = total + r[...].astype(f32)
    refs[-1][...] = (total / meta[3].astype(f32)).astype(bf16)


def outer_body(order, meta, anchor, momentum, *refs):
    pieces = refs[:-3]
    new_anc, anchor_out, momentum_out = refs[-3:]
    rows = pieces[0].shape[0]
    frag = meta[0]
    anchor_out[...] = anchor[...]
    momentum_out[...] = momentum[...]
    for m, piece in enumerate(pieces):
        at = pl.ds(pl.multiple_of(order(meta[2], m) * rows, rows), rows)
        grad = piece[...].astype(f32)
        mom = outer_mu * momentum[frag, at, :] + grad
        anc = anchor[frag, at, :] - outer_rate * (grad + outer_mu * mom)
        new_anc[at, :] = anc
        anchor_out[frag, at, :] = anc
        momentum_out[frag, at, :] = mom


def outer(meta, anchor, momentum, weights, n):
    two, rows, width = anchor.shape
    part = rows // n
    if n & (n - 1) == 0:
        order = lambda r, m: jnp.bitwise_xor(r, m)
        dest = lambda r, m: r ^ m
    else:
        order = lambda r, m: lax.rem(r + m, n)
        dest = lambda r, m: (r + m) % n
    back = lambda r, m: dest(r, m) if n & (n - 1) == 0 else (r - m) % n
    order_back = order if n & (n - 1) == 0 else (lambda r, m: lax.rem(r + n - m, n))
    pieces = call(
        functools.partial(delta_body, order), "delta_pieces", meta,
        [
            (anchor, pl.BlockSpec((1, rows, width), lambda g, m: (m[0], 0, 0))),
            (weights, pl.BlockSpec((1, 1, rows, width), lambda g, m: (0, m[0], 0, 0))),
        ],
        [(sds((part, width), bf16), whole((part, width)))] * n,
    )
    send = lambda a, m: lax.ppermute(a, "replica", [(r, dest(r, m)) for r in range(n)])
    got = [pieces[0]] + [send(pieces[m], m) for m in range(1, n)]
    mine = call(
        sum_body, "sum_pieces", meta, [(g, whole(g.shape)) for g in got],
        [(sds((part, width), bf16), whole((part, width)))],
    )[0]
    all_pieces = [mine] + [send(mine, m) for m in range(1, n)]
    return call(
        functools.partial(outer_body, order_back), "outer_step", meta,
        [(anchor, whole(anchor.shape)), (momentum, whole(momentum.shape))] + [(p, whole(p.shape)) for p in all_pieces],
        [(sds((rows, width), f32), whole((rows, width))), (sds(anchor.shape, f32), whole(anchor.shape)), (sds(anchor.shape, f32), whole(anchor.shape))],
    )


def local(n_rep, n_fsdp, inputs, kinds, weights, first_moment, second_moment, anchor, momentum, plan):
    tokens = inputs.shape[0]
    rows, width = weights.shape[2:]
    chips = n_fsdp // 2
    scale = 1.0 / math.sqrt(tokens * n_fsdp)
    chunks = max(1, min(4, rows // 256))
    cr = rows // chunks

    me = lax.axis_index("fsdp")
    rep = lax.axis_index("replica")
    total = jnp.sum(plan)
    chip, core = me // 2, me % 2
    at = [((chip + s) % chips) * 2 for s in range(chips)]
    meta = jnp.stack(
        [total % 2, lax.dynamic_slice_in_dim(plan, rep, 1, 0)[0], rep, total]
        + [a + core for a in at] + [a + 1 - core for a in at]
    ).astype(jnp.int32)

    partner = [(f, f ^ 1) for f in range(n_fsdp)]
    to_partner = lambda a: lax.ppermute(a, "fsdp", partner)
    fetch = lambda a, s: lax.ppermute(
        a, "fsdp", [(((f // 2 + s) % chips) * 2 + f % 2, f) for f in range(n_fsdp)])
    give = lambda a, s: lax.ppermute(
        a, "fsdp", [(f, ((f // 2 + s) % chips) * 2 + f % 2) for f in range(n_fsdp)])

    low_own = [cast_chunk(meta, weights, i, cr) for i in range(chunks)]
    x_par = to_partner(inputs)
    cw_own = token_weight(kinds)
    cw = jnp.stack([cw_own, to_partner(cw_own)])[:, :, None]
    new_anc, anchor_out, momentum_out = outer(meta, anchor, momentum, weights, n_rep)
    xt = [turn(meta, x, FIRST_SLOT, rows, cr) for x in (inputs, x_par)]

    state = [(weights, first_moment, second_moment)] * chunks
    state_block = list(range(chunks))
    for step in range(INNER):
        last = step == INNER - 1
        near = [(low_own[i], FIRST_SLOT, i) for i in range(chunks)]
        near += [(to_partner(low_own[i]), FIRST_SLOT + chips, i) for i in range(chunks)]
        far, low_far = [], {}
        for i in range(chunks):
            for s in range(1, chips):
                low_far[s, i] = fetch(low_own[i], s)
                far.append((low_far[s, i], FIRST_SLOT + s, i))
                far.append((to_partner(low_far[s, i]), FIRST_SLOT + chips + s, i))
        acc, gram = forward(meta, None, None, near, inputs, x_par, cr)
        if len(far) > 2:
            acc, gram = forward(meta, acc, gram, far[:-2], inputs, x_par, cr)
        slopes, w_hi, w_lo = finish(meta, acc, gram, cw, far[-2:], inputs, x_par, cr, scale)
        got = []
        for i in range(chunks):
            got.append([
                give(grad_rows(meta, scale, s * chunks + i, cr, xt, slopes, w_hi, w_lo, low_far[s, i]), s)
                for s in range(1, chips)
            ])
        new_state, new_low, prev = [], [], None
        for i in range(chunks):
            res = adam_rows(
                meta, scale, i, cr, xt, slopes, w_hi, w_lo, low_own[i], got[i],
                state[i], state_block[i], None if last else new_anc, prev, weights.shape,
            )
            if last:
                prev = res
            else:
                new_state.append(tuple(res[:3]))
                new_low.append(res[3])
        state, state_block, low_own = new_state, [0] * chunks, new_low
    return (*prev, anchor_out, momentum_out)


def solution(mesh):
    return jax.shard_map(
        functools.partial(local, mesh.shape["replica"], mesh.shape["fsdp"]),
        mesh=mesh,
        in_specs=(
            P(("replica", "fsdp"), None),
            P(("replica", "fsdp")),
            P("replica", None, "fsdp", None),
            P("replica", None, "fsdp", None),
            P("replica", None, "fsdp", None),
            P(None, "fsdp", None),
            P(None, "fsdp", None),
            P(),
        ),
        out_specs=(
            P("replica", None, "fsdp", None),
            P("replica", None, "fsdp", None),
            P("replica", None, "fsdp", None),
            P(None, "fsdp", None),
            P(None, "fsdp", None),
        ),
        check_vma=False,
    )
```

time: 281 us -> 176 us (0.63)
  waiting for transfers between devices: 144 us -> 42.6 us
  Pallas kernels: 0 us -> 68.6 us
  starting transfers between devices: 0.47 us -> 44.8 us
  matrix products: 43.8 us -> 0 us
  other arithmetic: 34.1 us -> 1.3 us
  local copies, waits for them, and re-layouts: 40.5 us -> 15.3 us
  between operations: 17.7 us -> 3.02 us
    all_gather x4 -> x0, waiting for transfers between devices: 69.9 us -> none  [the longest x2 39.8 us: inner_step(): lax.all_gather(low[1], 'fsdp', axis=0, tiled=True)]
    pallas_call x0 -> x31, Pallas kernels: none -> 68.6 us  [call(): pl.pallas_call(body, name=name, out_shape=[o for o, _ in outs], grid_spec...]
    reduce_scatter x2 -> x0, waiting for transfers between devices: 61.2 us -> none  [inner_step(): lax.psum_scatter(jnp.concatenate([grad_enc, grad_dec], 1).astype(jnp.bflo...]
    ppermute x0 -> x48, starting transfers between devices: none -> 44.8 us  [the longest x14 21.3 us: outer(): lax.ppermute(a, 'replica', [(r, dest(r, m)) for r in range(n)])]
    dot_general x8 -> x0, matrix products: 43.8 us -> none  [the longest x2 20.2 us: inner_step(): lax.dot_general(inputs, slope_pre, (((0,), (0,)), ((), ())), preferred_el...]
    ppermute x0 -> x48, waiting for transfers between devices: none -> 42.6 us  [the longest x8 21.6 us: local(): lax.ppermute(a, 'fsdp', [((f // 2 + s) % chips * 2 + f % 2, f) for f in r...]
    unnamed x42 -> x60, local copies, waits for them, and re-layouts: 35.9 us -> 12.5 us
    psum x1 -> x0, waiting for transfers between devices: 11.2 us -> none  [local(): lax.psum(delta.astype(jnp.bfloat16), 'replica').astype(jnp.float32) / total]
  transfers between devices with their start and end apart: 7 -> 48, of which waited for: 7 -> 18; matrix products, arithmetic and copies ran while one was open for 22% -> 2% of each run, Pallas kernels for 0% -> 35%
where the time goes in v1:
time: 176 us
  Pallas kernels  68.6 us (39%)
  starting transfers between devices  44.8 us (25%)
  waiting for transfers between devices  42.6 us (24%)
  local copies, waits for them, and re-layouts  15.3 us (9%)
  between operations  3.02 us (2%)
    pallas_call x31, Pallas kernels, call(): pl.pallas_call(body, name=name, out_shape=[o for o, _ in outs], grid_spec...  68.6 us
    ppermute x8, waiting for transfers between devices, local(): lax.ppermute(a, 'fsdp', [((f // 2 + s) % chips * 2 + f % 2, f) for f in r...  21.6 us
    ppermute x14, starting transfers between devices, outer(): lax.ppermute(a, 'replica', [(r, dest(r, m)) for r in range(n)])  21.3 us
    unnamed x60, local copies, waits for them, and re-layouts  12.5 us
    ppermute x8, waiting for transfers between devices, local(): lax.ppermute(a, 'fsdp', [(f, (f // 2 + s) % chips * 2 + f % 2) for f in r...  12.3 us
    ppermute x8, starting transfers between devices, local(): lax.ppermute(a, 'fsdp', [((f // 2 + s) % chips * 2 + f % 2, f) for f in r...  11.9 us
    ppermute x8, starting transfers between devices, local(): lax.ppermute(a, 'fsdp', [(f, (f // 2 + s) % chips * 2 + f % 2) for f in r...  8.89 us
    ppermute x14, waiting for transfers between devices, outer(): lax.ppermute(a, 'replica', [(r, dest(r, m)) for r in range(n)])  7.54 us
  transfers between devices with their start and end apart: 48, of which 18 were waited for; matrix products, arithmetic and copies ran while one was open for 2% of the time, Pallas kernels for 35%

profile of v1, /device:TPU:0, one launch (start us, length us, event | category | flops | bytes accessed | tf_op | source)
XLA Modules:
  0.0 175.6 jit_solution(11611051666808678142)
XLA Ops:
  9.2 2.7 %collective-permute-start.5 = (bf16[256,512]{1,0:T(8,128)(2,1)S(1)}, bf16[256,512]{1,0:T(8,128)(2,1)}, u32[]{:S(2)}, u32[]{:S(2)}) collective-permute-start(bf16[256,512]{1,0:T(8,128)(2,1)S(1)} %cast_rows.4.refs_1_.refs_6_), channel_id=1, source_target_pairs={{2,0},{3,1},{0,2},{1,3},{6,4},{7,5},{4,6},{5,7},{10,8},{11,9},{8,1... | collective-permute-start | bytes 786440 | tf_op jit(solution)/shard_map/ppermute | solution.py:396
  16.3 2.8 %collective-permute-done.5.refs_3_.low = bf16[256,512]{1,0:T(8,128)(2,1)} collective-permute-done((bf16[256,512]{1,0:T(8,128)(2,1)S(1)}, bf16[256,512]{1,0:T(8,128)(2,1)}, u32[]{:S(2)}, u32[]{:S(2)}) %collective-permute-start.5) | collective-permute-done | bytes 262176 | tf_op jit(solution)/shard_map/ppermute | solution.py:396
  21.8 3.0 %collective-permute-done.7.refs_5_.low = bf16[256,512]{1,0:T(8,128)(2,1)} collective-permute-done((bf16[256,512]{1,0:T(8,128)(2,1)S(1)}, bf16[256,512]{1,0:T(8,128)(2,1)}, u32[]{:S(2)}, u32[]{:S(2)}) %collective-permute-start.7) | collective-permute-done | bytes 262176 | tf_op jit(solution)/shard_map/ppermute | solution.py:396
  43.4 4.9 %forward_rows.4 = (f32[2,512,512]{2,1,0:T(8,128)S(1)}, f32[256,256]{1,0:T(8,128)S(1)}) custom-call(s32[8]{0:T(128)S(1)} %stack.40.meta.refs_0_, bf16[256,512]{1,0:T(8,128)(2,1)S(1)} %cast_rows.4.refs_1_.refs_6_, bf16[256,512]{1,0:T(8,128)(2,1)S(1)} %cast_rows.5.refs_2_.refs_6_, bf16[256,512]{1,0:T(8,128)(2,1)S(1)} %cast_rows.6.refs_3_.refs_6_, ...), custom_call_target="tpu_custom_call" | custom-call | flops 2147483648 | bytes 71565312 | tf_op jit(solution)/shard_map/forward_rows/pallas_call | solution.py:51
  50.2 2.8 %collective-permute-start.18 = (bf16[128,256]{1,0:T(8,128)(2,1)S(1)}, bf16[128,256]{1,0:T(8,128)(2,1)S(1)}, u32[]{:S(2)}, u32[]{:S(2)}) collective-permute-start(bf16[128,256]{1,0:T(8,128)(2,1)S(1)} %copy-done.23), channel_id=1, source_target_pairs={{0,16},{4,20},{8,24},{12,28},{16,0},{20,4},{24,8},{28,12},{1,17},{... | collective-permute-start | bytes 196616 | tf_op jit(solution)/shard_map/ppermute | solution.py:362
  53.0 4.5 %forward_rows.5 = (f32[2,512,512]{2,1,0:T(8,128)S(1)}, f32[256,256]{1,0:T(8,128)S(1)}) custom-call(s32[8]{0:T(128)S(1)} %stack.40.meta.refs_0_, f32[2,512,512]{2,1,0:T(8,128)S(1)} %get-tuple-element.58.refs_1_, f32[256,256]{1,0:T(8,128)S(1)} %get-tuple-element.59.refs_2_, bf16[256,512]{1,0:T(8,128)(2,1)} %collective-permute-done.5.refs_3_.low, ...), custom_call_target="tpu_custom_call" | custom-call | flops 1610612736 | bytes 56623104 | tf_op jit(solution)/shard_map/forward_rows/pallas_call | solution.py:51
  58.8 3.6 %collective-permute-start.20 = (bf16[128,256]{1,0:T(8,128)(2,1)S(1)}, bf16[128,256]{1,0:T(8,128)(2,1)S(1)}, u32[]{:S(2)}, u32[]{:S(2)}) collective-permute-start(bf16[128,256]{1,0:T(8,128)(2,1)S(1)} %copy-done.19), channel_id=1, source_target_pairs={{0,24},{4,28},{8,16},{12,20},{16,8},{20,12},{24,0},{28,4},{1,25},{... | collective-permute-start | bytes 196616 | tf_op jit(solution)/shard_map/ppermute | solution.py:362
  62.5 4.1 %finish_slopes.2 = (bf16[2,512,512]{2,1,0:T(8,128)(2,1)S(1)}, bf16[256,256]{1,0:T(8,128)(2,1)S(1)}, bf16[256,256]{1,0:T(8,128)(2,1)S(1)}) custom-call(s32[8]{0:T(128)S(1)} %stack.40.meta.refs_0_, f32[2,512,512]{2,1,0:T(8,128)S(1)} %get-tuple-element.60.refs_1_, f32[256,256]{1,0:T(8,128)S(1)} %get-tuple-element.61.refs_2_, f32[2,512,1]{2,1,0:T(8,128)S(1)} %copy.22.refs_3_, ...), custom_call_target="tpu_custom_call" | custom-call | flops 939524096 | bytes 20975616 | tf_op jit(solution)/shard_map/finish_slopes/pallas_call | solution.py:51
  66.6 5.3 %turn_tokens.3.xt_par.refs_2_ = bf16[2048,512]{1,0:T(8,128)(2,1)S(1)} custom-call(s32[8]{0:T(128)S(1)} %stack.40.meta.refs_0_, bf16[512,4096]{1,0:T(8,128)(2,1)} %collective-permute-done.x.refs_17_.refs_18_.refs_19_.refs_20_.refs_21_.refs_22_.refs_23_.refs_24_.refs_15_.refs_16_.refs_8_.refs_9_), custom_call_target="tpu_custom_call" | custom-call | bytes 6291456 | tf_op jit(solution)/shard_map/turn_tokens/pallas_call | solution.py:51
  75.4 4.6 %collective-permute-start.28 = (bf16[128,256]{1,0:T(8,128)(2,1)S(1)}, bf16[128,256]{1,0:T(8,128)(2,1)S(1)}, u32[]{:S(2)}, u32[]{:S(2)}) collective-permute-start(bf16[128,256]{1,0:T(8,128)(2,1)S(1)} %sum_pieces.1.refs_0_), channel_id=1, source_target_pairs={{0,28},{4,24},{8,20},{12,16},{16,12},{20,8},{24,4},{28,0},{1,29},{... | collective-permute-start | bytes 196616 | tf_op jit(solution)/shard_map/ppermute | solution.py:362
  82.8 3.1 %collective-permute-start.25 = (bf16[128,256]{1,0:T(8,128)(2,1)S(1)}, bf16[128,256]{1,0:T(8,128)(2,1)S(1)}, u32[]{:S(2)}, u32[]{:S(2)}) collective-permute-start(bf16[128,256]{1,0:T(8,128)(2,1)S(1)} %sum_pieces.1.refs_0_), channel_id=1, source_target_pairs={{0,16},{4,20},{8,24},{12,28},{16,0},{20,4},{24,8},{28,12},{1,17},{... | collective-permute-start | bytes 196616 | tf_op jit(solution)/shard_map/ppermute | solution.py:362
  85.8 3.4 %collective-permute-done.27.refs_6_ = bf16[128,256]{1,0:T(8,128)(2,1)S(1)} collective-permute-done((bf16[128,256]{1,0:T(8,128)(2,1)S(1)}, bf16[128,256]{1,0:T(8,128)(2,1)S(1)}, u32[]{:S(2)}, u32[]{:S(2)}) %collective-permute-start.27) | collective-permute-done | bytes 65568 | tf_op jit(solution)/shard_map/ppermute | solution.py:362
  95.4 3.1 %outer_step.1 = (f32[1024,256]{1,0:T(8,128)S(1)}, f32[2,1024,256]{2,1,0:T(8,128)}, f32[2,1024,256]{2,1,0:T(8,128)}) custom-call(s32[8]{0:T(128)S(1)} %stack.40.meta.refs_0_, f32[2,1024,256]{2,1,0:T(8,128)S(1)} %copy-done.8, f32[2,1024,256]{2,1,0:T(8,128)S(1)} %copy-done.9, bf16[128,256]{1,0:T(8,128)(2,1)S(1)} %sum_pieces.1.refs_0_, ...), custom_call_target="tpu_custom_call" | custom-call | bytes 9961472 | tf_op jit(solution)/shard_map/outer_step/pallas_call | solution.py:51
  116.9 2.8 %collective-permute-done.42.refs_4_.low = bf16[256,512]{1,0:T(8,128)(2,1)S(1)} collective-permute-done((bf16[256,512]{1,0:T(8,128)(2,1)S(1)}, bf16[256,512]{1,0:T(8,128)(2,1)S(1)}, u32[]{:S(2)}, u32[]{:S(2)}) %collective-permute-start.42) | collective-permute-done | bytes 262176 | tf_op jit(solution)/shard_map/ppermute | solution.py:396
  121.1 4.2 %collective-permute-done.40.refs_7_.low = bf16[256,512]{1,0:T(8,128)(2,1)S(1)} collective-permute-done((bf16[256,512]{1,0:T(8,128)(2,1)S(1)}, bf16[256,512]{1,0:T(8,128)(2,1)S(1)}, u32[]{:S(2)}, u32[]{:S(2)}) %collective-permute-start.40) | collective-permute-done | bytes 262176 | tf_op jit(solution)/shard_map/ppermute | solution.py:396
  125.9 4.7 %collective-permute-done.38.refs_5_.low = bf16[256,512]{1,0:T(8,128)(2,1)S(1)} collective-permute-done((bf16[256,512]{1,0:T(8,128)(2,1)S(1)}, bf16[256,512]{1,0:T(8,128)(2,1)S(1)}, u32[]{:S(2)}, u32[]{:S(2)}) %collective-permute-start.38) | collective-permute-done | bytes 262176 | tf_op jit(solution)/shard_map/ppermute | solution.py:396
  130.5 2.8 %collective-permute-done.36.refs_3_.low = bf16[256,512]{1,0:T(8,128)(2,1)S(1)} collective-permute-done((bf16[256,512]{1,0:T(8,128)(2,1)S(1)}, bf16[256,512]{1,0:T(8,128)(2,1)S(1)}, u32[]{:S(2)}, u32[]{:S(2)}) %collective-permute-start.36) | collective-permute-done | bytes 262176 | tf_op jit(solution)/shard_map/ppermute | solution.py:396
  133.9 4.7 %forward_rows.6 = (f32[2,512,512]{2,1,0:T(8,128)S(1)}, f32[256,256]{1,0:T(8,128)S(1)}) custom-call(s32[8]{0:T(128)S(1)} %stack.40.meta.refs_0_, bf16[256,512]{1,0:T(8,128)(2,1)S(1)} %get-tuple-element.74.refs_1_.refs_6_, bf16[256,512]{1,0:T(8,128)(2,1)S(1)} %get-tuple-element.75.refs_2_.refs_6_, bf16[256,512]{1,0:T(8,128)(2,1)S(1)} %get-tuple-element.76.refs_3_.refs_6_, ...), custom_call_target="tpu_custom_call" | custom-call | flops 2147483648 | bytes 71565312 | tf_op jit(solution)/shard_map/forward_rows/pallas_call | solution.py:51
  138.6 4.0 %forward_rows.7 = (f32[2,512,512]{2,1,0:T(8,128)S(1)}, f32[256,256]{1,0:T(8,128)S(1)}) custom-call(s32[8]{0:T(128)S(1)} %stack.40.meta.refs_0_, f32[2,512,512]{2,1,0:T(8,128)S(1)} %get-tuple-element.78.refs_1_, f32[256,256]{1,0:T(8,128)S(1)} %get-tuple-element.79.refs_2_, bf16[256,512]{1,0:T(8,128)(2,1)S(1)} %collective-permute-done.36.refs_3_.low, ...), custom_call_target="tpu_custom_call" | custom-call | flops 1610612736 | bytes 56623104 | tf_op jit(solution)/shard_map/forward_rows/pallas_call | solution.py:51
  142.7 4.3 %finish_slopes.3 = (bf16[2,512,512]{2,1,0:T(8,128)(2,1)S(1)}, bf16[256,256]{1,0:T(8,128)(2,1)S(1)}, bf16[256,256]{1,0:T(8,128)(2,1)S(1)}) custom-call(s32[8]{0:T(128)S(1)} %stack.40.meta.refs_0_, f32[2,512,512]{2,1,0:T(8,128)S(1)} %get-tuple-element.80.refs_1_, f32[256,256]{1,0:T(8,128)S(1)} %get-tuple-element.81.refs_2_, f32[2,512,1]{2,1,0:T(8,128)S(1)} %copy.22.refs_3_, ...), custom_call_target="tpu_custom_call" | custom-call | flops 939524096 | bytes 20975616 | tf_op jit(solution)/shard_map/finish_slopes/pallas_call | solution.py:51
  157.3 2.4 %adam_rows.12 = (f32[1,2,1024,256]{3,2,1,0:T(8,128)}, f32[1,2,1024,256]{3,2,1,0:T(8,128)}, f32[1,2,1024,256]{3,2,1,0:T(8,128)}) custom-call(s32[8]{0:T(128)S(1)} %stack.40.meta.refs_0_, bf16[2048,512]{1,0:T(8,128)(2,1)S(1)} %turn_tokens.2.xt_own.refs_1_, bf16[2048,512]{1,0:T(8,128)(2,1)S(1)} %turn_tokens.3.xt_par.refs_2_, ...), custom_call_target="tpu_custom_call" | custom-call | flops 268435456 | bytes 13893632 | tf_op jit(solution)/shard_map/adam_rows/pallas_call | solution.py:51
  159.7 3.2 %collective-permute-done.46.refs_7_ = bf16[256,512]{1,0:T(8,128)(2,1)S(1)} collective-permute-done((bf16[256,512]{1,0:T(8,128)(2,1)S(1)}, bf16[256,512]{1,0:T(8,128)(2,1)S(1)}, u32[]{:S(2)}, u32[]{:S(2)}) %collective-permute-start.46) | collective-permute-done | bytes 262176 | tf_op jit(solution)/shard_map/ppermute | solution.py:398
  162.9 2.4 %adam_rows.13 = (f32[1,2,1024,256]{3,2,1,0:T(8,128)}, f32[1,2,1024,256]{3,2,1,0:T(8,128)}, f32[1,2,1024,256]{3,2,1,0:T(8,128)}) custom-call(s32[8]{0:T(128)S(1)} %stack.40.meta.refs_0_, bf16[2048,512]{1,0:T(8,128)(2,1)S(1)} %turn_tokens.2.xt_own.refs_1_, ...), custom_call_target="tpu_custom_call", output_to_operand_aliasing={{0}: (11, {}), {1}: (12, {}), {2}: (13, {})} | custom-call | flops 268435456 | bytes 20185088 | tf_op jit(solution)/shard_map/adam_rows/pallas_call | solution.py:51
  165.3 3.2 %collective-permute-done.45.refs_7_ = bf16[256,512]{1,0:T(8,128)(2,1)S(1)} collective-permute-done((bf16[256,512]{1,0:T(8,128)(2,1)S(1)}, bf16[256,512]{1,0:T(8,128)(2,1)S(1)}, u32[]{:S(2)}, u32[]{:S(2)}) %collective-permute-start.45) | collective-permute-done | bytes 262176 | tf_op jit(solution)/shard_map/ppermute | solution.py:398
  (169 shorter events, 86.0 us)
Async XLA Ops:
  0.6 37.7 %collective-permute-start = (bf16[512,4096]{1,0:T(8,128)(2,1)}, bf16[512,4096]{1,0:T(8,128)(2,1)}, u32[]{:S(2)}, u32[]{:S(2)}) collective-permute-start(bf16[512,4096]{1,0:T(8,128)(2,1)} %refs_7_.3), channel_id=1, source_target_pairs={{0,1},{1,0},{2,3},{3,2},{4,5},{5,4},{6,7},{7,6},{8,9},{9,8},{10,11... | collective-permute-start | bytes 12582920 | tf_op jit(solution)/shard_map/ppermute | solution.py:395
  14.2 12.5 %collective-permute-start.2 = (bf16[256,512]{1,0:T(8,128)(2,1)S(1)}, bf16[256,512]{1,0:T(8,128)(2,1)S(1)}, u32[]{:S(2)}, u32[]{:S(2)}) collective-permute-start(bf16[256,512]{1,0:T(8,128)(2,1)S(1)} %cast_rows.5.refs_2_.refs_6_), channel_id=1, source_target_pairs={{0,1},{1,0},{2,3},{3,2},{4,5},{5,4},{6,7},{7,6},{8,9},{9,8},{10,11... | collective-permute-start | bytes 786440 | tf_op jit(solution)/shard_map/ppermute | solution.py:395
  19.1 14.0 %collective-permute-start.9 = (bf16[256,512]{1,0:T(8,128)(2,1)S(1)}, bf16[256,512]{1,0:T(8,128)(2,1)}, u32[]{:S(2)}, u32[]{:S(2)}) collective-permute-start(bf16[256,512]{1,0:T(8,128)(2,1)S(1)} %cast_rows.6.refs_3_.refs_6_), channel_id=1, source_target_pairs={{2,0},{3,1},{0,2},{1,3},{6,4},{7,5},{4,6},{5,7},{10,8},{11,9},{8,1... | collective-permute-start | bytes 786440 | tf_op jit(solution)/shard_map/ppermute | solution.py:396
  33.1 15.2 %collective-permute-start.6 = (bf16[256,512]{1,0:T(8,128)(2,1)}, bf16[256,512]{1,0:T(8,128)(2,1)}, u32[]{:S(2)}, u32[]{:S(2)}) collective-permute-start(bf16[256,512]{1,0:T(8,128)(2,1)} %collective-permute-done.5.refs_3_.low), channel_id=1, source_target_pairs={{0,1},{1,0},{2,3},{3,2},{4,5},{5,4},{6,7},{7,6},{8,9},{9,8},{10,11... | collective-permute-start | bytes 786440 | tf_op jit(solution)/shard_map/ppermute | solution.py:395
  34.3 15.6 %collective-permute-start.8 = (bf16[256,512]{1,0:T(8,128)(2,1)}, bf16[256,512]{1,0:T(8,128)(2,1)}, u32[]{:S(2)}, u32[]{:S(2)}) collective-permute-start(bf16[256,512]{1,0:T(8,128)(2,1)} %collective-permute-done.7.refs_5_.low), channel_id=1, source_target_pairs={{0,1},{1,0},{2,3},{3,2},{4,5},{5,4},{6,7},{7,6},{8,9},{9,8},{10,11... | collective-permute-start | bytes 786440 | tf_op jit(solution)/shard_map/ppermute | solution.py:395
  35.6 14.6 %collective-permute-start.10 = (bf16[256,512]{1,0:T(8,128)(2,1)}, bf16[256,512]{1,0:T(8,128)(2,1)}, u32[]{:S(2)}, u32[]{:S(2)}) collective-permute-start(bf16[256,512]{1,0:T(8,128)(2,1)} %collective-permute-done.9.refs_7_.low), channel_id=1, source_target_pairs={{0,1},{1,0},{2,3},{3,2},{4,5},{5,4},{6,7},{7,6},{8,9},{9,8},{10,11... | collective-permute-start | bytes 786440 | tf_op jit(solution)/shard_map/ppermute | solution.py:395
  36.6 20.9 %collective-permute-start.15 = (bf16[128,256]{1,0:T(8,128)(2,1)}, bf16[128,256]{1,0:T(8,128)(2,1)S(1)}, u32[]{:S(2)}, u32[]{:S(2)}) collective-permute-start(bf16[128,256]{1,0:T(8,128)(2,1)} %copy-done.28), channel_id=1, source_target_pairs={{0,4},{4,0},{8,12},{12,8},{16,20},{20,16},{24,28},{28,24},{1,5},{5... | collective-permute-start | bytes 196616 | tf_op jit(solution)/shard_map/ppermute | solution.py:362
  38.3 24.1 %collective-permute-start.13 = (bf16[256,512]{1,0:T(8,128)(2,1)}, bf16[256,512]{1,0:T(8,128)(2,1)S(1)}, u32[]{:S(2)}, u32[]{:S(2)}) collective-permute-start(bf16[256,512]{1,0:T(8,128)(2,1)} %copy-done.10), channel_id=1, source_target_pairs={{0,1},{1,0},{2,3},{3,2},{4,5},{5,4},{6,7},{7,6},{8,9},{9,8},{10,11... | collective-permute-start | bytes 786440 | tf_op jit(solution)/shard_map/ppermute | solution.py:395
  50.0 23.0 %collective-permute-start.17 = (bf16[128,256]{1,0:T(8,128)(2,1)S(1)}, bf16[128,256]{1,0:T(8,128)(2,1)S(1)}, u32[]{:S(2)}, u32[]{:S(2)}) collective-permute-start(bf16[128,256]{1,0:T(8,128)(2,1)S(1)} %copy-done.25), channel_id=1, source_target_pairs={{0,12},{4,8},{8,4},{12,0},{16,28},{20,24},{24,20},{28,16},{1,13},{... | collective-permute-start | bytes 196616 | tf_op jit(solution)/shard_map/ppermute | solution.py:362
  50.2 24.5 %collective-permute-start.18 = (bf16[128,256]{1,0:T(8,128)(2,1)S(1)}, bf16[128,256]{1,0:T(8,128)(2,1)S(1)}, u32[]{:S(2)}, u32[]{:S(2)}) collective-permute-start(bf16[128,256]{1,0:T(8,128)(2,1)S(1)} %copy-done.23), channel_id=1, source_target_pairs={{0,16},{4,20},{8,24},{12,28},{16,0},{20,4},{24,8},{28,12},{1,17},{... | collective-permute-start | bytes 196616 | tf_op jit(solution)/shard_map/ppermute | solution.py:362
  57.5 17.2 %collective-permute-start.19 = (bf16[128,256]{1,0:T(8,128)(2,1)S(1)}, bf16[128,256]{1,0:T(8,128)(2,1)S(1)}, u32[]{:S(2)}, u32[]{:S(2)}) collective-permute-start(bf16[128,256]{1,0:T(8,128)(2,1)S(1)} %copy-done.21), channel_id=1, source_target_pairs={{0,20},{4,16},{8,28},{12,24},{16,4},{20,0},{24,12},{28,8},{1,21},{... | collective-permute-start | bytes 196616 | tf_op jit(solution)/shard_map/ppermute | solution.py:362
  58.8 15.9 %collective-permute-start.20 = (bf16[128,256]{1,0:T(8,128)(2,1)S(1)}, bf16[128,256]{1,0:T(8,128)(2,1)S(1)}, u32[]{:S(2)}, u32[]{:S(2)}) collective-permute-start(bf16[128,256]{1,0:T(8,128)(2,1)S(1)} %copy-done.19), channel_id=1, source_target_pairs={{0,24},{4,28},{8,16},{12,20},{16,8},{20,12},{24,0},{28,4},{1,25},{... | collective-permute-start | bytes 196616 | tf_op jit(solution)/shard_map/ppermute | solution.py:362
  73.0 31.9 %collective-permute-start.31 = (bf16[256,512]{1,0:T(8,128)(2,1)S(1)}, bf16[256,512]{1,0:T(8,128)(2,1)S(1)}, u32[]{:S(2)}, u32[]{:S(2)}) collective-permute-start(bf16[256,512]{1,0:T(8,128)(2,1)S(1)} %grad_rows.11), channel_id=1, source_target_pairs={{0,2},{1,3},{2,0},{3,1},{4,6},{5,7},{6,4},{7,5},{8,10},{9,11},{10,... | collective-permute-start | bytes 786440 | tf_op jit(solution)/shard_map/ppermute | solution.py:398
  82.0 26.7 %collective-permute-start.30 = (bf16[256,512]{1,0:T(8,128)(2,1)S(1)}, bf16[256,512]{1,0:T(8,128)(2,1)S(1)}, u32[]{:S(2)}, u32[]{:S(2)}) collective-permute-start(bf16[256,512]{1,0:T(8,128)(2,1)S(1)} %grad_rows.10), channel_id=1, source_target_pairs={{0,2},{1,3},{2,0},{3,1},{4,6},{5,7},{6,4},{7,5},{8,10},{9,11},{10,... | collective-permute-start | bytes 786440 | tf_op jit(solution)/shard_map/ppermute | solution.py:398
  107.2 12.6 %collective-permute-start.42 = (bf16[256,512]{1,0:T(8,128)(2,1)S(1)}, bf16[256,512]{1,0:T(8,128)(2,1)S(1)}, u32[]{:S(2)}, u32[]{:S(2)}) collective-permute-start(bf16[256,512]{1,0:T(8,128)(2,1)S(1)} %get-tuple-element.77.refs_4_.refs_6_), channel_id=1, source_target_pairs={{2,0},{3,1},{0,2},{1,3},{6,4},{7,5},{4,6},{5,7},{10,8},{11,9},{8,1... | collective-permute-start | bytes 786440 | tf_op jit(solution)/shard_map/ppermute | solution.py:396
  108.6 12.5 %collective-permute-start.35 = (bf16[256,512]{1,0:T(8,128)(2,1)S(1)}, bf16[256,512]{1,0:T(8,128)(2,1)S(1)}, u32[]{:S(2)}, u32[]{:S(2)}) collective-permute-start(bf16[256,512]{1,0:T(8,128)(2,1)S(1)} %get-tuple-element.77.refs_4_.refs_6_), channel_id=1, source_target_pairs={{0,1},{1,0},{2,3},{3,2},{4,5},{5,4},{6,7},{7,6},{8,9},{9,8},{10,11... | collective-permute-start | bytes 786440 | tf_op jit(solution)/shard_map/ppermute | solution.py:395
  110.0 15.4 %collective-permute-start.40 = (bf16[256,512]{1,0:T(8,128)(2,1)S(1)}, bf16[256,512]{1,0:T(8,128)(2,1)S(1)}, u32[]{:S(2)}, u32[]{:S(2)}) collective-permute-start(bf16[256,512]{1,0:T(8,128)(2,1)S(1)} %get-tuple-element.76.refs_3_.refs_6_), channel_id=1, source_target_pairs={{2,0},{3,1},{0,2},{1,3},{6,4},{7,5},{4,6},{5,7},{10,8},{11,9},{8,1... | collective-permute-start | bytes 786440 | tf_op jit(solution)/shard_map/ppermute | solution.py:396
  110.7 14.7 %collective-permute-start.34 = (bf16[256,512]{1,0:T(8,128)(2,1)S(1)}, bf16[256,512]{1,0:T(8,128)(2,1)S(1)}, u32[]{:S(2)}, u32[]{:S(2)}) collective-permute-start(bf16[256,512]{1,0:T(8,128)(2,1)S(1)} %get-tuple-element.76.refs_3_.refs_6_), channel_id=1, source_target_pairs={{0,1},{1,0},{2,3},{3,2},{4,5},{5,4},{6,7},{7,6},{8,9},{9,8},{10,11... | collective-permute-start | bytes 786440 | tf_op jit(solution)/shard_map/ppermute | solution.py:395
  114.1 16.4 %collective-permute-start.38 = (bf16[256,512]{1,0:T(8,128)(2,1)S(1)}, bf16[256,512]{1,0:T(8,128)(2,1)S(1)}, u32[]{:S(2)}, u32[]{:S(2)}) collective-permute-start(bf16[256,512]{1,0:T(8,128)(2,1)S(1)} %get-tuple-element.75.refs_2_.refs_6_), channel_id=1, source_target_pairs={{2,0},{3,1},{0,2},{1,3},{6,4},{7,5},{4,6},{5,7},{10,8},{11,9},{8,1... | collective-permute-start | bytes 786440 | tf_op jit(solution)/shard_map/ppermute | solution.py:396
  119.7 13.6 %collective-permute-start.36 = (bf16[256,512]{1,0:T(8,128)(2,1)S(1)}, bf16[256,512]{1,0:T(8,128)(2,1)S(1)}, u32[]{:S(2)}, u32[]{:S(2)}) collective-permute-start(bf16[256,512]{1,0:T(8,128)(2,1)S(1)} %get-tuple-element.74.refs_1_.refs_6_), channel_id=1, source_target_pairs={{2,0},{3,1},{0,2},{1,3},{6,4},{7,5},{4,6},{5,7},{10,8},{11,9},{8,1... | collective-permute-start | bytes 786440 | tf_op jit(solution)/shard_map/ppermute | solution.py:396
  125.4 13.2 %collective-permute-start.41 = (bf16[256,512]{1,0:T(8,128)(2,1)S(1)}, bf16[256,512]{1,0:T(8,128)(2,1)S(1)}, u32[]{:S(2)}, u32[]{:S(2)}) collective-permute-start(bf16[256,512]{1,0:T(8,128)(2,1)S(1)} %collective-permute-done.40.refs_7_.low), channel_id=1, source_target_pairs={{0,1},{1,0},{2,3},{3,2},{4,5},{5,4},{6,7},{7,6},{8,9},{9,8},{10,11... | collective-permute-start | bytes 786440 | tf_op jit(solution)/shard_map/ppermute | solution.py:395
  150.2 12.7 %collective-permute-start.46 = (bf16[256,512]{1,0:T(8,128)(2,1)S(1)}, bf16[256,512]{1,0:T(8,128)(2,1)S(1)}, u32[]{:S(2)}, u32[]{:S(2)}) collective-permute-start(bf16[256,512]{1,0:T(8,128)(2,1)S(1)} %grad_rows.14), channel_id=1, source_target_pairs={{0,2},{1,3},{2,0},{3,1},{4,6},{5,7},{6,4},{7,5},{8,10},{9,11},{10,... | collective-permute-start | bytes 786440 | tf_op jit(solution)/shard_map/ppermute | solution.py:398
  152.3 16.2 %collective-permute-start.45 = (bf16[256,512]{1,0:T(8,128)(2,1)S(1)}, bf16[256,512]{1,0:T(8,128)(2,1)S(1)}, u32[]{:S(2)}, u32[]{:S(2)}) collective-permute-start(bf16[256,512]{1,0:T(8,128)(2,1)S(1)} %grad_rows.13), channel_id=1, source_target_pairs={{0,2},{1,3},{2,0},{3,1},{4,6},{5,7},{6,4},{7,5},{8,10},{9,11},{10,... | collective-permute-start | bytes 786440 | tf_op jit(solution)/shard_map/ppermute | solution.py:398
  154.5 18.8 %collective-permute-start.44 = (bf16[256,512]{1,0:T(8,128)(2,1)S(1)}, bf16[256,512]{1,0:T(8,128)(2,1)S(1)}, u32[]{:S(2)}, u32[]{:S(2)}) collective-permute-start(bf16[256,512]{1,0:T(8,128)(2,1)S(1)} %grad_rows.12), channel_id=1, source_target_pairs={{0,2},{1,3},{2,0},{3,1},{4,6},{5,7},{6,4},{7,5},{8,10},{9,11},{10,... | collective-permute-start | bytes 786440 | tf_op jit(solution)/shard_map/ppermute | solution.py:398
  (54 other events, 361.4 us)

commit v2 on v1

v2 whole, which is shorter than its diff:
```python
import functools
import math

import jax
import jax.numpy as jnp
from jax import lax
from jax.experimental import pallas as pl
from jax.experimental.pallas import tpu as pltpu
from jax.sharding import PartitionSpec as P

INNER = 2

inner_rate = 0.003
beta_one = 0.9
beta_two = 0.95
adam_eps = 1e-08
decay_rate = 0.1
outer_rate = 0.7
outer_mu = 0.9
mix_share = 0.5

bf16 = jnp.bfloat16
f32 = jnp.float32
VMEM_LIMIT = 16 * 1024 * 1024


def token_weight(kinds):
    return jnp.where(kinds == 2, 1.0, jnp.where(kinds == 1, 0.25, 0.0)).astype(f32)


def dot(a, b):
    return jnp.dot(a, b, preferred_element_type=f32)


def dot_rows(a, b):
    return lax.dot_general(a, b, (((0,), (0,)), ((), ())), preferred_element_type=f32)


def once(shape, index):
    return pl.BlockSpec(shape, index, pipeline_mode=pl.Buffered(1))


def whole(shape):
    return once(shape, lambda *_: (0,) * len(shape))


def sds(shape, dtype):
    return jax.ShapeDtypeStruct(shape, dtype)


def call(body, name, meta, ins, outs, grid=(1,), scratch=(), aliases=None, flops=0, after=()):
    arrays = [a for a, _ in ins] + list(after)
    moved = sum(math.prod(o.shape) * o.dtype.itemsize for o, _ in outs)
    moved += sum(math.prod(a.shape) * a.dtype.itemsize for a, _ in ins)
    n_in = len(meta) + len(ins)

    def run(*refs):
        body(*refs[:n_in], *refs[n_in + len(after):])

    return pl.pallas_call(
        run,
        name=name,
        out_shape=[o for o, _ in outs],
        grid_spec=pltpu.PrefetchScalarGridSpec(
            num_scalar_prefetch=len(meta),
            grid=grid,
            in_specs=[s for _, s in ins] + [pl.BlockSpec(memory_space=pl.ANY)] * len(after),
            out_specs=[s for _, s in outs],
            scratch_shapes=list(scratch),
        ),
        input_output_aliases=aliases or {},
        compiler_params=pltpu.CompilerParams(vmem_limit_bytes=VMEM_LIMIT),
        cost_estimate=pl.CostEstimate(flops=flops, bytes_accessed=moved, transcendentals=0),
    )(*meta, *arrays)


def plan_sum(plan):
    total = plan[0]
    for r in range(1, plan.shape[0]):
        total = total + plan[r]
    return total


def fragment(plan):
    return lax.rem(plan_sum(plan), 2)


def cast_body(chunks, theta, *refs):
    outs, (held, sems) = refs[:len(chunks)], refs[len(chunks):]
    cr, wide = outs[0].shape
    width = wide // 2
    copies = []
    for n, i in enumerate(chunks):
        copy = pltpu.make_async_copy(theta.at[0, :, pl.ds(i * cr, cr), :], held.at[n], sems.at[n])
        copy.start()
        copies.append(copy)
    for n, copy in enumerate(copies):
        copy.wait()
        for k in range(2):
            outs[n][:, k * width:(k + 1) * width] = held[n, k].astype(bf16)


def cast_chunks(weights, chunks, cr):
    width = weights.shape[-1]
    return call(
        functools.partial(cast_body, chunks), "cast_rows", (),
        [(weights, pl.BlockSpec(memory_space=pltpu.HBM))],
        [(sds((cr, 2 * width), bf16), whole((cr, 2 * width)))] * len(chunks),
        scratch=[
            pltpu.VMEM((len(chunks), 2, cr, width), f32),
            pltpu.SemaphoreType.DMA((len(chunks),)),
        ],
    )


def weigh_body(kinds, out):
    out[...] = token_weight(kinds[...])


def copy_body(x, out):
    out[...] = x[...]


def relay(x, after):
    return call(copy_body, "relay_rows", (), [(x, whole(x.shape))], [(sds(x.shape, x.dtype), whole(x.shape))], after=after)[0]


def turn_body(pos, x, xt):
    xt[...] = x[...].T


def turn(pos, x, chips, rows, tile):
    tokens = x.shape[0]
    per = rows // tile
    return call(
        turn_body, "turn_tokens", (pos,),
        [(x, pl.BlockSpec((tokens, tile), lambda g, m: (0, m[1 + g // per] * per + g % per)))],
        [(sds((chips * rows, tokens), bf16), pl.BlockSpec((tile, tokens), lambda g, m: (g, 0)))],
        grid=(chips * per,),
    )[0]


def forward_body(count, first_call, pos, *refs):
    if first_call:
        acc_in = gram_in = None
    else:
        acc_in, gram_in, refs = refs[0], refs[1], refs[2:]
    lows = refs[:count]
    xs = (refs[count:2 * count], refs[2 * count:3 * count])
    acc, gram = refs[3 * count:]
    width = gram.shape[0]
    total = None if first_call else gram_in[...]
    for p in range(count):
        dec = lows[p][:, width:]
        term = dot_rows(dec, dec)
        total = term if total is None else total + term
    gram[...] = total
    for h in range(2):
        value = None if first_call else acc_in[h]
        for p in range(count):
            term = dot(xs[h][p][...], lows[p][...])
            value = term if value is None else value + term
        acc[h] = value


def column(slot, i, per):
    return lambda g, m: (0, m[slot] * per + i)


def forward(pos, acc, gram, pieces, xs, cr, per, after=()):
    tokens = xs[0].shape[0]
    wide = pieces[0][0].shape[1]
    width = wide // 2
    count = len(pieces)
    ins = []
    if acc is not None:
        ins += [(acc, whole(acc.shape)), (gram, whole(gram.shape))]
    ins += [(low, whole(low.shape)) for low, _, _ in pieces]
    for x in xs:
        ins += [(x, once((tokens, cr), column(slot, i, per))) for _, slot, i in pieces]
    return call(
        functools.partial(forward_body, count, acc is None), "forward_rows", (pos,), ins,
        [(sds((2, tokens, wide), f32), whole((2, tokens, wide))), (sds((width, width), f32), whole((width, width)))],
        flops=4 * tokens * cr * wide * count, after=after,
    )


def finish_body(scale, count, steps, pos, acc_in, gram_in, cw, *refs):
    lows = refs[:count]
    xs = (refs[count:2 * count], refs[2 * count:3 * count])
    slopes, w_hi, w_lo, w_acc = refs[3 * count:]
    width = gram_in.shape[0]
    gram = gram_in[...]
    for p in range(count):
        dec = lows[p][:, width:]
        gram = gram + dot_rows(dec, dec)
    g_hi = gram.astype(bf16)
    g_lo = (gram - g_hi.astype(f32)).astype(bf16)
    w_new = None
    for h in range(2):
        value = acc_in[h]
        for p in range(count):
            value = value + dot(xs[h][p][...], lows[p][...])
        pre = value[:, :width]
        sig = 1.0 / (1.0 + jnp.exp(-pre))
        hidden = (pre * sig).astype(bf16)
        back = dot(hidden, g_hi) + dot(hidden, g_lo) - value[:, width:]
        weight = cw[h]
        slope = (weight * scale) * back * (sig * (1.0 + pre * (1.0 - sig)))
        counted = (weight * hidden.astype(f32)).astype(bf16)
        slopes[h, :, :width] = slope.astype(bf16)
        slopes[h, :, width:] = counted
        term = dot_rows(counted, hidden)
        w_new = term if w_new is None else w_new + term
    step = pl.program_id(0)

    @pl.when(step == 0)
    def _():
        w_acc[...] = w_new

    @pl.when(step > 0)
    def _():
        w_acc[...] += w_new

    @pl.when(step == steps - 1)
    def _():
        total = w_acc[...]
        hi = total.astype(bf16)
        w_hi[...] = hi
        w_lo[...] = (total - hi.astype(f32)).astype(bf16)


def finish(pos, acc, gram, cw, pieces, xs, cr, per, scale):
    tokens = xs[0].shape[0]
    wide = pieces[0][0].shape[1]
    width = wide // 2
    count = len(pieces)
    steps = 2
    tile = tokens // steps
    ins = [
        (acc, pl.BlockSpec((2, tile, wide), lambda g, m: (0, g, 0))),
        (gram, whole(gram.shape)),
        (cw, pl.BlockSpec((2, tile, 1), lambda g, m: (0, g, 0))),
    ]
    ins += [(low, whole(low.shape)) for low, _, _ in pieces]
    for x in xs:
        for _, slot, i in pieces:
            ins.append((x, pl.BlockSpec((tile, cr), lambda g, m, slot=slot, i=i: (g, m[slot] * per + i))))
    square = (sds((width, width), bf16), whole((width, width)))
    return call(
        functools.partial(finish_body, scale, count, steps), "finish_slopes", (pos,), ins,
        [(sds((2, tokens, wide), bf16), pl.BlockSpec((2, tile, wide), lambda g, m: (0, g, 0))), square, square],
        grid=(steps,),
        scratch=[pltpu.VMEM((width, width), f32)],
        flops=4 * tokens * cr * wide * count + 12 * tokens * width * width,
    )


def grad_body(scale, xt_own, xt_par, slopes, w_hi, w_lo, low, out):
    width = w_hi.shape[0]
    both = dot(xt_own[...], slopes[0]) + dot(xt_par[...], slopes[1])
    dec = low[:, width:]
    grad_dec = scale * (dot(dec, w_hi[...]) + dot(dec, w_lo[...]) - both[:, width:])
    out[:, :width] = both[:, :width].astype(out.dtype)
    out[:, width:] = grad_dec.astype(out.dtype)


def grad_rows(scale, block, cr, xt, slopes, w_hi, w_lo, low, dtype, after=()):
    tokens = xt[0].shape[1]
    wide = low.shape[1]
    ins = [(x, once((cr, tokens), lambda g: (block, 0))) for x in xt]
    ins += [(a, whole(a.shape)) for a in (slopes, w_hi, w_lo, low)]
    return call(
        functools.partial(grad_body, scale), "grad_rows", (), ins,
        [(sds((cr, wide), dtype), whole((cr, wide)))],
        flops=4 * tokens * cr * wide, after=after,
    )[0]


def adam_body(last, count, plan, own, *refs):
    got = refs[:count]
    theta, first, second = refs[count:3 + count]
    refs = refs[3 + count:]
    width = own.shape[1] // 2
    if last:
        theta_out, first_out, second_out = refs[-3:]
    else:
        anchor = refs[0]
        theta_out, first_out, second_out, low_out = refs[-4:]
        frag = fragment(plan)
    for k in range(2):
        grad = own[:, k * width:(k + 1) * width]
        for g in got:
            grad = grad + g[:, k * width:(k + 1) * width].astype(f32)
        one = beta_one * first[0, k] + (1.0 - beta_one) * grad
        two = beta_two * second[0, k] + (1.0 - beta_two) * grad * grad
        old = theta[0, k]
        new = old - inner_rate * (one / (jnp.sqrt(two) + adam_eps) + decay_rate * old)
        if not last:
            mixed = mix_share * new + (1.0 - mix_share) * anchor[...]
            new = jnp.where(frag == k, mixed, new)
            low_out[:, k * width:(k + 1) * width] = new.astype(bf16)
        theta_out[0, k] = new
        first_out[0, k] = one
        second_out[0, k] = two


def adam_rows(plan, i, cr, own, got, state, state_block, new_anc, prev, full):
    width = own.shape[1] // 2
    last = new_anc is None
    block = (1, 2, cr, width)
    ins = [(g, whole(g.shape)) for g in [own] + got]
    ins += [(s, once(block, lambda g, m: (0, 0, state_block, 0))) for s in state]
    aliases = {}
    if last:
        if prev is not None:
            for n, p in enumerate(prev):
                aliases[1 + len(ins)] = n
                ins.append((p, pl.BlockSpec(memory_space=pl.ANY)))
        outs = [(sds(full, f32), once(block, lambda g, m: (0, 0, i, 0)))] * 3
    else:
        ins.append((new_anc, once((cr, width), lambda g, m: (i, 0))))
        outs = [(sds(block, f32), whole(block))] * 3 + [(sds((cr, 2 * width), bf16), whole((cr, 2 * width)))]
    return call(
        functools.partial(adam_body, last, len(got)), "adam_rows", (plan,), ins, outs, aliases=aliases,
    )


def delta_body(pos, plan, anchor, theta, anchor_off, theta_off, keep, send):
    count = plan[pos[0]].astype(f32)
    keep[...] = count * (anchor[0] - theta[0, 0])
    send[...] = (count * (anchor_off[0] - theta_off[0, 0])).astype(bf16)


def add_body(final, plan, a, b, out):
    total = a[...].astype(f32) + b[...].astype(f32)
    if final:
        total = total / plan_sum(plan).astype(f32)
    out[...] = total.astype(bf16)


def outer_body(pos, plan, anchor, momentum, own, other, new_anc, anchor_out, momentum_out):
    half = own.shape[0]
    frag = fragment(plan)
    bit = lax.rem(pos[0], 2)
    anchor_out[...] = anchor[...]
    momentum_out[...] = momentum[...]
    for piece, where in ((own, bit), (other, 1 - bit)):
        at = pl.ds(pl.multiple_of(where * half, half), half)
        grad = piece[...].astype(f32)
        mom = outer_mu * momentum[frag, at, :] + grad
        anc = anchor[frag, at, :] - outer_rate * (grad + outer_mu * mom)
        new_anc[at, :] = anc
        anchor_out[frag, at, :] = anc
        momentum_out[frag, at, :] = mom


def outer_start(pos, plan, anchor, weights, after):
    _, rows, width = anchor.shape
    half = rows // 2

    def at(off):
        def anchor_at(g, p, q):
            return (fragment(q), lax.rem(p[0] + off, 2), 0)

        def theta_at(g, p, q):
            return (0, fragment(q), lax.rem(p[0] + off, 2), 0)

        return [(anchor, once((1, half, width), anchor_at)), (weights, once((1, 1, half, width), theta_at))]

    return call(
        delta_body, "delta_halves", (pos, plan), at(0) + at(1),
        [(sds((half, width), f32), whole((half, width))), (sds((half, width), bf16), whole((half, width)))],
        after=after,
    )


def outer_add(plan, a, b, final, after):
    return call(
        functools.partial(add_body, final), "add_halves", (plan,), [(a, whole(a.shape)), (b, whole(b.shape))],
        [(sds(a.shape, bf16), whole(a.shape))], after=after,
    )[0]


def outer_end(pos, plan, anchor, momentum, own, other):
    _, rows, width = anchor.shape
    return call(
        outer_body, "outer_step", (pos, plan),
        [(a, whole(a.shape)) for a in (anchor, momentum, own, other)],
        [(sds((rows, width), f32), whole((rows, width)))] + [(sds(anchor.shape, f32), whole(anchor.shape))] * 2,
    )


def local(n_rep, n_fsdp, inputs, kinds, weights, first_moment, second_moment, anchor, momentum, plan):
    tokens = inputs.shape[0]
    rows, width = weights.shape[2:]
    chips = n_fsdp // 2
    scale = 1.0 / math.sqrt(tokens * n_fsdp)
    chunks = max(1, min(4, rows // 256))
    cr = rows // chunks

    partner = [(f, f ^ 1) for f in range(n_fsdp)]
    to_partner = lambda a: lax.ppermute(a, "fsdp", partner)
    fetch = lambda a, s: lax.ppermute(
        a, "fsdp", [(((f // 2 + s) % chips) * 2 + f % 2, f) for f in range(n_fsdp)])
    give = lambda a, s: lax.ppermute(
        a, "fsdp", [(f, ((f // 2 + s) % chips) * 2 + f % 2) for f in range(n_fsdp)])
    across = lambda a, bit: lax.ppermute(a, "replica", [(r, r ^ bit) for r in range(n_rep)])

    low_own = cast_chunks(weights, [0], cr)
    if chunks > 1:
        low_own = list(low_own) + list(cast_chunks(weights, list(range(1, chunks)), cr))

    chip = lax.axis_index("fsdp") // 2
    core = lax.axis_index("fsdp") % 2
    at = [((chip + s) % chips) * 2 for s in range(chips)]
    pos = jnp.stack([lax.axis_index("replica")] + [a + core for a in at] + [a + 1 - core for a in at]).astype(jnp.int32)

    x_par = to_partner(inputs)
    xs = (inputs, x_par)
    keep, send = outer_start(pos, plan, anchor, weights, after=[low_own[-1]])
    outer_in = across(send, 1)
    lanes = kinds.reshape(-1, 128)
    cw_own = call(
        weigh_body, "weigh_tokens", (), [(lanes, whole(lanes.shape))],
        [(sds(lanes.shape, f32), whole(lanes.shape))], after=[send],
    )[0]
    cw = jnp.stack([cw_own, to_partner(cw_own)]).reshape(2, tokens, 1)
    xt = [turn(pos, x, chips, rows, cr) for x in xs]

    state = [(weights, first_moment, second_moment)] * chunks
    state_block = list(range(chunks))
    for step in range(INNER):
        last = step == INNER - 1
        near = [(low_own[i], 1, i) for i in range(chunks)]
        near += [(to_partner(low_own[i]), 1 + chips, i) for i in range(chunks)]
        acc, gram = forward(pos, None, None, near, xs, cr, chunks)
        far = [(i, s) for i in range(chunks) for s in range(1, chips)]
        low_far = {(i, s): fetch(low_own[i], s) for i, s in far}

        stages = []
        if step == 0:
            bits = [1 << b for b in range(1, n_rep.bit_length() - 1)]
            own = keep
            took = outer_in
        wait_for = []
        pending = None
        for n, (i, s) in enumerate(far):
            handed = to_partner(relay(low_far[i, s], [acc] + wait_for))
            pieces = [(low_far[i, s], 1 + s, i)]
            if pending is not None:
                pieces = [pending] + pieces
            acc, gram = forward(pos, acc, gram, pieces, xs, cr, chunks)
            pending = (handed, 1 + chips + s, i)
            if step == 0 and bits and n in (0, len(far) - 2):
                own = outer_add(plan, own, took, False, [acc])
                took = across(own, bits.pop(0))
                wait_for = [own]
        slopes, w_hi, w_lo = finish(pos, acc, gram, cw, [pending], xs, cr, chunks, scale)

        mine, got = [], []
        for i in range(chunks):
            sent = [
                grad_rows(scale, s * chunks + i, cr, xt, slopes, w_hi, w_lo, low_far[i, s], bf16)
                for s in range(1, chips)
            ]
            got.append([give(g, s) for s, g in enumerate(sent, 1)])
        for i in range(chunks):
            mine.append(grad_rows(scale, i, cr, xt, slopes, w_hi, w_lo, low_own[i], f32, after=sent))
        if step == 0:
            while bits:
                own = outer_add(plan, own, took, False, sent)
                took = across(own, bits.pop(0))
            own = outer_add(plan, own, took, True, mine[-1:])
            new_anc, anchor_out, momentum_out = outer_end(pos, plan, anchor, momentum, own, across(own, 1))

        new_state, new_low, prev = [], [], None
        for i in range(chunks):
            res = adam_rows(
                plan, i, cr, mine[i], got[i], state[i], state_block[i],
                None if last else new_anc, prev, weights.shape,
            )
            if last:
                prev = res
            else:
                new_state.append(tuple(res[:3]))
                new_low.append(res[3])
        state, state_block, low_own = new_state, [0] * chunks, new_low
    return (*prev, anchor_out, momentum_out)


def solution(mesh):
    return jax.shard_map(
        functools.partial(local, mesh.shape["replica"], mesh.shape["fsdp"]),
        mesh=mesh,
        in_specs=(
            P(("replica", "fsdp"), None),
            P(("replica", "fsdp")),
            P("replica", None, "fsdp", None),
            P("replica", None, "fsdp", None),
            P("replica", None, "fsdp", None),
            P(None, "fsdp", None),
            P(None, "fsdp", None),
            P(),
        ),
        out_specs=(
            P("replica", None, "fsdp", None),
            P("replica", None, "fsdp", None),
            P("replica", None, "fsdp", None),
            P(None, "fsdp", None),
            P(None, "fsdp", None),
        ),
        check_vma=False,
    )
```

time: 176 us -> 145 us (0.82)
  starting transfers between devices: 44.8 us -> 29.6 us
  local copies, waits for them, and re-layouts: 15.3 us -> 5.52 us
  waiting for transfers between devices: 42.6 us -> 33.5 us
  Pallas kernels: 68.6 us -> 73.2 us
    ppermute x14 -> x4, starting transfers between devices: 21.3 us -> 6.76 us  [local(): lax.ppermute(a, 'replica', [(r, r ^ bit) for r in range(n_rep)])]
    ppermute x8, waiting for transfers between devices: 21.6 us -> 9.06 us  [local(): lax.ppermute(a, 'fsdp', [((f // 2 + s) % chips * 2 + f % 2, f) for f in r...]
    unnamed x60 -> x44, local copies, waits for them, and re-layouts: 12.5 us -> 3.7 us
    ppermute x8, waiting for transfers between devices: 12.3 us -> 17.5 us  [local(): lax.ppermute(a, 'fsdp', [(f, (f // 2 + s) % chips * 2 + f % 2) for f in r...]
    ppermute x14 -> x4, waiting for transfers between devices: 7.54 us -> 2.69 us  [local(): lax.ppermute(a, 'replica', [(r, r ^ bit) for r in range(n_rep)])]
    pallas_call x31 -> x54, Pallas kernels: 68.6 us -> 73.2 us  [call(): pl.pallas_call(run, name=name, out_shape=[o for o, _ in outs], grid_spec=...]
    ppermute x18, waiting for transfers between devices: 1.17 us -> 4.21 us  [local(): to_partner = lambda a: lax.ppermute(a, 'fsdp', partner)]
  transfers between devices with their start and end apart: 48 -> 38, of which waited for: 18 -> 11; matrix products, arithmetic and copies ran while one was open for 2% -> 2% of each run, Pallas kernels for 35% -> 47%
where the time goes in v2:
time: 145 us; the launch traced here: 144 us
  Pallas kernels  73.2 us (50%)
  waiting for transfers between devices  33.5 us (23%)
  starting transfers between devices  29.6 us (20%)
  local copies, waits for them, and re-layouts  5.52 us (4%)
    pallas_call x54, Pallas kernels, call(): pl.pallas_call(run, name=name, out_shape=[o for o, _ in outs], grid_spec=...  73.2 us
    ppermute x8, waiting for transfers between devices, local(): lax.ppermute(a, 'fsdp', [(f, (f // 2 + s) % chips * 2 + f % 2) for f in r...  17.5 us
    ppermute x8, starting transfers between devices, local(): lax.ppermute(a, 'fsdp', [((f // 2 + s) % chips * 2 + f % 2, f) for f in r...  10.7 us
    ppermute x8, waiting for transfers between devices, local(): lax.ppermute(a, 'fsdp', [((f // 2 + s) % chips * 2 + f % 2, f) for f in r...  9.06 us
    ppermute x8, starting transfers between devices, local(): lax.ppermute(a, 'fsdp', [(f, (f // 2 + s) % chips * 2 + f % 2) for f in r...  8.56 us
    ppermute x4, starting transfers between devices, local(): lax.ppermute(a, 'replica', [(r, r ^ bit) for r in range(n_rep)])  6.76 us
    ppermute x18, waiting for transfers between devices, local(): to_partner = lambda a: lax.ppermute(a, 'fsdp', partner)  4.21 us
    unnamed x44, local copies, waits for them, and re-layouts  3.7 us
  transfers between devices with their start and end apart: 38, of which 11 were waited for; matrix products, arithmetic and copies ran while one was open for 2% of the time, Pallas kernels for 47%

profile of v2, /device:TPU:0, one launch (start us, length us, event | category | flops | bytes accessed | tf_op | source)
XLA Modules:
  0.0 144.3 jit_solution(17185414060076442640)
XLA Ops:
  4.9 4.2 %collective-permute-done.1.refs_5_ = bf16[256,512]{1,0:T(8,128)(2,1)S(1)} collective-permute-done((bf16[256,512]{1,0:T(8,128)(2,1)S(1)}, bf16[256,512]{1,0:T(8,128)(2,1)S(1)}, u32[]{:S(2)}, u32[]{:S(2)}) %collective-permute-start.1) | collective-permute-done | bytes 262176 | tf_op jit(solution)/shard_map/ppermute | solution.py:403
  9.1 2.9 %collective-permute-start.5 = (bf16[256,512]{1,0:T(8,128)(2,1)S(1)}, bf16[256,512]{1,0:T(8,128)(2,1)S(1)}, u32[]{:S(2)}, u32[]{:S(2)}) collective-permute-start(bf16[256,512]{1,0:T(8,128)(2,1)S(1)} %cast_rows.2.refs_1_.refs_5_), channel_id=1, source_target_pairs={{2,0},{3,1},{0,2},{1,3},{6,4},{7,5},{4,6},{5,7},{10,8},{11,9},{8,1... | collective-permute-start | bytes 786440 | tf_op jit(solution)/shard_map/ppermute | solution.py:404
  16.4 5.1 %forward_rows.10 = (f32[2,512,512]{2,1,0:T(8,128)S(1)}, f32[256,256]{1,0:T(8,128)S(1)}) custom-call(s32[5]{0:T(128)S(1)} %stack.32.refs_0_, bf16[256,512]{1,0:T(8,128)(2,1)S(1)} %cast_rows.2.refs_1_.refs_5_, bf16[256,512]{1,0:T(8,128)(2,1)S(1)} %get-tuple-element.67.refs_2_.refs_5_, bf16[256,512]{1,0:T(8,128)(2,1)} %get-tuple-element.68.refs_3_.refs_5_, ...), custom_call_target="tpu_custom_call" | custom-call | flops 2147483648 | bytes 71565312 | tf_op jit(solution)/shard_map/forward_rows/pallas_call | solution.py:60
  23.2 2.0 %forward_rows.11 = (f32[2,512,512]{2,1,0:T(8,128)S(1)}, f32[256,256]{1,0:T(8,128)S(1)}) custom-call(s32[5]{0:T(128)S(1)} %stack.32.refs_0_, f32[2,512,512]{2,1,0:T(8,128)S(1)} %get-tuple-element.70.refs_1_, f32[256,256]{1,0:T(8,128)S(1)} %get-tuple-element.71.refs_2_, bf16[256,512]{1,0:T(8,128)(2,1)S(1)} %collective-permute-done.5.refs_3_.refs_0_.refs_5_, ...), custom_call_target="tpu_custom_call" | custom-call | flops 268435456 | bytes 13369344 | tf_op jit(solution)/shard_map/forward_rows/pallas_call | solution.py:60
  28.2 2.5 %forward_rows.12 = (f32[2,512,512]{2,1,0:T(8,128)S(1)}, f32[256,256]{1,0:T(8,128)S(1)}) custom-call(s32[5]{0:T(128)S(1)} %stack.32.refs_0_, f32[2,512,512]{2,1,0:T(8,128)S(1)} %get-tuple-element.72.refs_1_.refs_3_, f32[256,256]{1,0:T(8,128)S(1)} %get-tuple-element.73.refs_2_, bf16[256,512]{1,0:T(8,128)(2,1)S(1)} %collective-permute-done.6.refs_3_, ...), custom_call_target="tpu_custom_call" | custom-call | flops 536870912 | bytes 22020096 | tf_op jit(solution)/shard_map/forward_rows/pallas_call | solution.py:60
  31.4 2.5 %forward_rows.13 = (f32[2,512,512]{2,1,0:T(8,128)S(1)}, f32[256,256]{1,0:T(8,128)S(1)}) custom-call(s32[5]{0:T(128)S(1)} %stack.32.refs_0_, f32[2,512,512]{2,1,0:T(8,128)S(1)} %get-tuple-element.74.refs_1_, f32[256,256]{1,0:T(8,128)S(1)} %get-tuple-element.75.refs_2_, bf16[256,512]{1,0:T(8,128)(2,1)S(1)} %collective-permute-done.9.refs_3_, ...), custom_call_target="tpu_custom_call" | custom-call | flops 536870912 | bytes 22020096 | tf_op jit(solution)/shard_map/forward_rows/pallas_call | solution.py:60
  41.2 2.6 %collective-permute-start.17 = (bf16[512,256]{1,0:T(8,128)(2,1)}, bf16[512,256]{1,0:T(8,128)(2,1)S(1)}, u32[]{:S(2)}, u32[]{:S(2)}) collective-permute-start(bf16[512,256]{1,0:T(8,128)(2,1)} %copy-done.13), channel_id=1, source_target_pairs={{0,16},{4,20},{8,24},{12,28},{16,0},{20,4},{24,8},{28,12},{1,17},{... | collective-permute-start | bytes 786440 | tf_op jit(solution)/shard_map/ppermute | solution.py:408
  44.9 5.5 %turn_tokens.3.refs_1_ = bf16[2048,512]{1,0:T(8,128)(2,1)S(1)} custom-call(s32[5]{0:T(128)S(1)} %stack.32.refs_0_, bf16[512,4096]{1,0:T(8,128)(2,1)} %collective-permute-done.refs_1_.refs_17_.refs_18_.refs_19_.refs_20_.refs_21_.refs_22_.refs_23_.refs_24_.refs_5_.refs_7_.refs_8_.refs_6_), custom_call_target="tpu_custom_call" | custom-call | bytes 6291456 | tf_op jit(solution)/shard_map/turn_tokens/pallas_call | solution.py:60
  50.5 2.6 %forward_rows.14 = (f32[2,512,512]{2,1,0:T(8,128)S(1)}, f32[256,256]{1,0:T(8,128)S(1)}) custom-call(s32[5]{0:T(128)S(1)} %stack.32.refs_0_, f32[2,512,512]{2,1,0:T(8,128)S(1)} %copy-done.10, f32[256,256]{1,0:T(8,128)S(1)} %copy-done.19, bf16[256,512]{1,0:T(8,128)(2,1)} %collective-permute-done.11.refs_3_, ...), custom_call_target="tpu_custom_call" | custom-call | flops 536870912 | bytes 22020096 | tf_op jit(solution)/shard_map/forward_rows/pallas_call | solution.py:60
  53.0 3.6 %finish_slopes.2 = (bf16[2,512,512]{2,1,0:T(8,128)(2,1)S(1)}, bf16[256,256]{1,0:T(8,128)(2,1)S(1)}, bf16[256,256]{1,0:T(8,128)(2,1)S(1)}) custom-call(s32[5]{0:T(128)S(1)} %stack.32.refs_0_, f32[2,512,512]{2,1,0:T(8,128)S(1)} %get-tuple-element.80.refs_1_, f32[256,256]{1,0:T(8,128)S(1)} %get-tuple-element.81.refs_2_, ...), custom_call_target="tpu_custom_call" | custom-call | flops 671088640 | bytes 12324864 | tf_op jit(solution)/shard_map/finish_slopes/pallas_call | solution.py:60
  68.7 3.1 %outer_step.1 = (f32[1024,256]{1,0:T(8,128)S(1)}, f32[2,1024,256]{2,1,0:T(8,128)}, f32[2,1024,256]{2,1,0:T(8,128)}) custom-call(s32[5]{0:T(128)S(1)} %stack.32.refs_0_, s32[8]{0:T(128)S(1)} %copy-done.20, f32[2,1024,256]{2,1,0:T(8,128)S(1)} %copy-done.8, f32[2,1024,256]{2,1,0:T(8,128)S(1)} %copy-done.15, bf16[512,256]{1,0:T(8,128)(2,1)S(1)} %add_halves.5.refs_4_, ...), custom_call_target="tpu_custom_call" | custom-call | bytes 9961472 | tf_op jit(solution)/shard_map/outer_step/pallas_call | solution.py:60
  78.5 3.6 %collective-permute-done.21.refs_2_ = bf16[256,512]{1,0:T(8,128)(2,1)S(1)} collective-permute-done((bf16[256,512]{1,0:T(8,128)(2,1)S(1)}, bf16[256,512]{1,0:T(8,128)(2,1)S(1)}, u32[]{:S(2)}, u32[]{:S(2)}) %collective-permute-start.21) | collective-permute-done | bytes 262176 | tf_op jit(solution)/shard_map/ppermute | solution.py:406
  85.4 4.7 %forward_rows.15 = (f32[2,512,512]{2,1,0:T(8,128)S(1)}, f32[256,256]{1,0:T(8,128)S(1)}) custom-call(s32[5]{0:T(128)S(1)} %stack.32.refs_0_, bf16[256,512]{1,0:T(8,128)(2,1)S(1)} %get-tuple-element.86.refs_1_.refs_5_, bf16[256,512]{1,0:T(8,128)(2,1)S(1)} %get-tuple-element.87.refs_2_.refs_5_, bf16[256,512]{1,0:T(8,128)(2,1)S(1)} %get-tuple-element.88.refs_3_.refs_5_, ...), custom_call_target="tpu_custom_call" | custom-call | flops 2147483648 | bytes 71565312 | tf_op jit(solution)/shard_map/forward_rows/pallas_call | solution.py:60
  90.1 2.3 %collective-permute-done.26.refs_3_.refs_0_.refs_5_ = bf16[256,512]{1,0:T(8,128)(2,1)S(1)} collective-permute-done((bf16[256,512]{1,0:T(8,128)(2,1)S(1)}, bf16[256,512]{1,0:T(8,128)(2,1)S(1)}, u32[]{:S(2)}, u32[]{:S(2)}) %collective-permute-start.26) | collective-permute-done | bytes 262176 | tf_op jit(solution)/shard_map/ppermute | solution.py:404
  99.7 2.5 %forward_rows.17 = (f32[2,512,512]{2,1,0:T(8,128)S(1)}, f32[256,256]{1,0:T(8,128)S(1)}) custom-call(s32[5]{0:T(128)S(1)} %stack.32.refs_0_, f32[2,512,512]{2,1,0:T(8,128)S(1)} %get-tuple-element.92.refs_1_, f32[256,256]{1,0:T(8,128)S(1)} %get-tuple-element.93.refs_2_, bf16[256,512]{1,0:T(8,128)(2,1)S(1)} %collective-permute-done.27.refs_3_, ...), custom_call_target="tpu_custom_call" | custom-call | flops 536870912 | bytes 22020096 | tf_op jit(solution)/shard_map/forward_rows/pallas_call | solution.py:60
  103.8 2.5 %forward_rows.18 = (f32[2,512,512]{2,1,0:T(8,128)S(1)}, f32[256,256]{1,0:T(8,128)S(1)}) custom-call(s32[5]{0:T(128)S(1)} %stack.32.refs_0_, f32[2,512,512]{2,1,0:T(8,128)S(1)} %get-tuple-element.94.refs_1_, f32[256,256]{1,0:T(8,128)S(1)} %get-tuple-element.95.refs_2_, bf16[256,512]{1,0:T(8,128)(2,1)S(1)} %collective-permute-done.29.refs_3_, ...), custom_call_target="tpu_custom_call" | custom-call | flops 536870912 | bytes 22020096 | tf_op jit(solution)/shard_map/forward_rows/pallas_call | solution.py:60
  106.3 2.6 %collective-permute-done.32.refs_4_.refs_0_.refs_5_ = bf16[256,512]{1,0:T(8,128)(2,1)S(1)} collective-permute-done((bf16[256,512]{1,0:T(8,128)(2,1)S(1)}, bf16[256,512]{1,0:T(8,128)(2,1)S(1)}, u32[]{:S(2)}, u32[]{:S(2)}) %collective-permute-start.32) | collective-permute-done | bytes 262176 | tf_op jit(solution)/shard_map/ppermute | solution.py:404
  108.9 2.7 %forward_rows.19 = (f32[2,512,512]{2,1,0:T(8,128)S(1)}, f32[256,256]{1,0:T(8,128)S(1)}) custom-call(s32[5]{0:T(128)S(1)} %stack.32.refs_0_, f32[2,512,512]{2,1,0:T(8,128)S(1)} %get-tuple-element.96.refs_1_, f32[256,256]{1,0:T(8,128)S(1)} %get-tuple-element.97.refs_2_, bf16[256,512]{1,0:T(8,128)(2,1)S(1)} %collective-permute-done.31.refs_3_, ...), custom_call_target="tpu_custom_call" | custom-call | flops 536870912 | bytes 22020096 | tf_op jit(solution)/shard_map/forward_rows/pallas_call | solution.py:60
  111.7 3.3 %finish_slopes.3 = (bf16[2,512,512]{2,1,0:T(8,128)(2,1)S(1)}, bf16[256,256]{1,0:T(8,128)(2,1)S(1)}, bf16[256,256]{1,0:T(8,128)(2,1)S(1)}) custom-call(s32[5]{0:T(128)S(1)} %stack.32.refs_0_, f32[2,512,512]{2,1,0:T(8,128)S(1)} %get-tuple-element.98.refs_1_, f32[256,256]{1,0:T(8,128)S(1)} %get-tuple-element.99.refs_2_, ...), custom_call_target="tpu_custom_call" | custom-call | flops 671088640 | bytes 12324864 | tf_op jit(solution)/shard_map/finish_slopes/pallas_call | solution.py:60
  123.4 12.5 %collective-permute-done.37.refs_2_ = bf16[256,512]{1,0:T(8,128)(2,1)S(1)} collective-permute-done((bf16[256,512]{1,0:T(8,128)(2,1)S(1)}, bf16[256,512]{1,0:T(8,128)(2,1)S(1)}, u32[]{:S(2)}, u32[]{:S(2)}) %collective-permute-start.37) | collective-permute-done | bytes 262176 | tf_op jit(solution)/shard_map/ppermute | solution.py:406
  135.9 2.1 %adam_rows.12 = (f32[1,2,1024,256]{3,2,1,0:T(8,128)}, f32[1,2,1024,256]{3,2,1,0:T(8,128)}, f32[1,2,1024,256]{3,2,1,0:T(8,128)}) custom-call(s32[8]{0:T(128)S(1)} %copy-done.20, f32[256,512]{1,0:T(8,128)S(1)} %grad_rows.30.refs_1_, bf16[256,512]{1,0:T(8,128)(2,1)S(1)} %collective-permute-done.37.refs_2_, f32[1,2,256,256]{3,2,1,0:T(8,128)S(1)} %get-tuple-element.112.refs_3_, ...), custom_call_target="tpu_custom_call" | custom-call | bytes 8650752 | tf_op jit(solution)/shard_map/adam_rows/pallas_call | solution.py:60
  138.0 2.1 %adam_rows.13 = (f32[1,2,1024,256]{3,2,1,0:T(8,128)}, f32[1,2,1024,256]{3,2,1,0:T(8,128)}, f32[1,2,1024,256]{3,2,1,0:T(8,128)}) custom-call(s32[8]{0:T(128)S(1)} %copy-done.20, f32[256,512]{1,0:T(8,128)S(1)} %grad_rows.28.refs_1_, bf16[256,512]{1,0:T(8,128)(2,1)S(1)} %collective-permute-done.36.refs_2_, ...), custom_call_target="tpu_custom_call", output_to_operand_aliasing={{0}: (6, {}), {1}: (7, {}), {2}: (8, {})} | custom-call | bytes 14942208 | tf_op jit(solution)/shard_map/adam_rows/pallas_call | solution.py:60
  140.1 2.1 %adam_rows.14 = (f32[1,2,1024,256]{3,2,1,0:T(8,128)}, f32[1,2,1024,256]{3,2,1,0:T(8,128)}, f32[1,2,1024,256]{3,2,1,0:T(8,128)}) custom-call(s32[8]{0:T(128)S(1)} %copy-done.20, f32[256,512]{1,0:T(8,128)S(1)} %grad_rows.26.refs_1_, bf16[256,512]{1,0:T(8,128)(2,1)S(1)} %collective-permute-done.35.refs_2_, ...), custom_call_target="tpu_custom_call", output_to_operand_aliasing={{0}: (6, {}), {1}: (7, {}), {2}: (8, {})} | custom-call | bytes 14942208 | tf_op jit(solution)/shard_map/adam_rows/pallas_call | solution.py:60
  142.2 2.1 %adam_rows.15 = (f32[1,2,1024,256]{3,2,1,0:T(8,128)}, f32[1,2,1024,256]{3,2,1,0:T(8,128)}, f32[1,2,1024,256]{3,2,1,0:T(8,128)}) custom-call(s32[8]{0:T(128)S(1)} %copy-done.20, f32[256,512]{1,0:T(8,128)S(1)} %grad_rows.25.refs_1_, bf16[256,512]{1,0:T(8,128)(2,1)S(1)} %collective-permute-done.34.refs_2_, ...), custom_call_target="tpu_custom_call", output_to_operand_aliasing={{0}: (6, {}), {1}: (7, {}), {2}: (8, {})} | custom-call | bytes 14942208 | tf_op jit(solution)/shard_map/adam_rows/pallas_call | solution.py:60
  (154 shorter events, 61.3 us)
Async XLA Ops:
  0.6 15.7 %collective-permute-start = (bf16[512,4096]{1,0:T(8,128)(2,1)}, bf16[512,4096]{1,0:T(8,128)(2,1)}, u32[]{:S(2)}, u32[]{:S(2)}) collective-permute-start(bf16[512,4096]{1,0:T(8,128)(2,1)} %refs_5_.25), channel_id=1, source_target_pairs={{0,1},{1,0},{2,3},{3,2},{4,5},{5,4},{6,7},{7,6},{8,9},{9,8},{10,11... | collective-permute-start | bytes 12582920 | tf_op jit(solution)/shard_map/ppermute | solution.py:403
  3.9 10.4 %collective-permute-start.2 = (bf16[256,512]{1,0:T(8,128)(2,1)S(1)}, bf16[256,512]{1,0:T(8,128)(2,1)}, u32[]{:S(2)}, u32[]{:S(2)}) collective-permute-start(bf16[256,512]{1,0:T(8,128)(2,1)S(1)} %get-tuple-element.67.refs_2_.refs_5_), channel_id=1, source_target_pairs={{0,1},{1,0},{2,3},{3,2},{4,5},{5,4},{6,7},{7,6},{8,9},{9,8},{10,11... | collective-permute-start | bytes 786440 | tf_op jit(solution)/shard_map/ppermute | solution.py:403
  4.4 11.5 %collective-permute-start.3 = (bf16[256,512]{1,0:T(8,128)(2,1)}, bf16[256,512]{1,0:T(8,128)(2,1)}, u32[]{:S(2)}, u32[]{:S(2)}) collective-permute-start(bf16[256,512]{1,0:T(8,128)(2,1)} %get-tuple-element.68.refs_3_.refs_5_), channel_id=1, source_target_pairs={{0,1},{1,0},{2,3},{3,2},{4,5},{5,4},{6,7},{7,6},{8,9},{9,8},{10,11... | collective-permute-start | bytes 786440 | tf_op jit(solution)/shard_map/ppermute | solution.py:403
  4.5 11.9 %collective-permute-start.4 = (bf16[256,512]{1,0:T(8,128)(2,1)S(1)}, bf16[256,512]{1,0:T(8,128)(2,1)}, u32[]{:S(2)}, u32[]{:S(2)}) collective-permute-start(bf16[256,512]{1,0:T(8,128)(2,1)S(1)} %get-tuple-element.69.refs_4_.refs_6_.refs_5_), channel_id=1, source_target_pairs={{0,1},{1,0},{2,3},{3,2},{4,5},{5,4},{6,7},{7,6},{8,9},{9,8},{10,11... | collective-permute-start | bytes 786440 | tf_op jit(solution)/shard_map/ppermute | solution.py:403
  9.1 12.4 %collective-permute-start.5 = (bf16[256,512]{1,0:T(8,128)(2,1)S(1)}, bf16[256,512]{1,0:T(8,128)(2,1)S(1)}, u32[]{:S(2)}, u32[]{:S(2)}) collective-permute-start(bf16[256,512]{1,0:T(8,128)(2,1)S(1)} %cast_rows.2.refs_1_.refs_5_), channel_id=1, source_target_pairs={{2,0},{3,1},{0,2},{1,3},{6,4},{7,5},{4,6},{5,7},{10,8},{11,9},{8,1... | collective-permute-start | bytes 786440 | tf_op jit(solution)/shard_map/ppermute | solution.py:404
  14.3 10.9 %collective-permute-start.8 = (bf16[512,256]{1,0:T(8,128)(2,1)S(1)}, bf16[512,256]{1,0:T(8,128)(2,1)S(1)}, u32[]{:S(2)}, u32[]{:S(2)}) collective-permute-start(bf16[512,256]{1,0:T(8,128)(2,1)S(1)} %get-tuple-element.77.refs_1_), channel_id=1, source_target_pairs={{0,4},{4,0},{8,12},{12,8},{16,20},{20,16},{24,28},{28,24},{1,5},{5... | collective-permute-start | bytes 786440 | tf_op jit(solution)/shard_map/ppermute | solution.py:408
  15.9 10.0 %collective-permute-start.7 = (bf16[256,512]{1,0:T(8,128)(2,1)S(1)}, bf16[256,512]{1,0:T(8,128)(2,1)S(1)}, u32[]{:S(2)}, u32[]{:S(2)}) collective-permute-start(bf16[256,512]{1,0:T(8,128)(2,1)S(1)} %get-tuple-element.67.refs_2_.refs_5_), channel_id=1, source_target_pairs={{2,0},{3,1},{0,2},{1,3},{6,4},{7,5},{4,6},{5,7},{10,8},{11,9},{8,1... | collective-permute-start | bytes 786440 | tf_op jit(solution)/shard_map/ppermute | solution.py:404
  31.4 19.0 %collective-permute-start.11 = (bf16[256,512]{1,0:T(8,128)(2,1)}, bf16[256,512]{1,0:T(8,128)(2,1)}, u32[]{:S(2)}, u32[]{:S(2)}) collective-permute-start(bf16[256,512]{1,0:T(8,128)(2,1)} %relay_rows.10), channel_id=1, source_target_pairs={{0,1},{1,0},{2,3},{3,2},{4,5},{5,4},{6,7},{7,6},{8,9},{9,8},{10,11... | collective-permute-start | bytes 786440 | tf_op jit(solution)/shard_map/ppermute | solution.py:403
  36.9 16.1 %collective-permute-start.15 = (bf16[256,512]{1,0:T(8,128)(2,1)}, bf16[256,512]{1,0:T(8,128)(2,1)}, u32[]{:S(2)}, u32[]{:S(2)}) collective-permute-start(bf16[256,512]{1,0:T(8,128)(2,1)} %relay_rows.11), channel_id=1, source_target_pairs={{0,1},{1,0},{2,3},{3,2},{4,5},{5,4},{6,7},{7,6},{8,9},{9,8},{10,11... | collective-permute-start | bytes 786440 | tf_op jit(solution)/shard_map/ppermute | solution.py:403
  41.2 18.6 %collective-permute-start.17 = (bf16[512,256]{1,0:T(8,128)(2,1)}, bf16[512,256]{1,0:T(8,128)(2,1)S(1)}, u32[]{:S(2)}, u32[]{:S(2)}) collective-permute-start(bf16[512,256]{1,0:T(8,128)(2,1)} %copy-done.13), channel_id=1, source_target_pairs={{0,16},{4,20},{8,24},{12,28},{16,0},{20,4},{24,8},{28,12},{1,17},{... | collective-permute-start | bytes 786440 | tf_op jit(solution)/shard_map/ppermute | solution.py:408
  57.2 14.6 %collective-permute-start.16 = (bf16[256,512]{1,0:T(8,128)(2,1)S(1)}, bf16[256,512]{1,0:T(8,128)(2,1)S(1)}, u32[]{:S(2)}, u32[]{:S(2)}) collective-permute-start(bf16[256,512]{1,0:T(8,128)(2,1)S(1)} %grad_rows.18), channel_id=1, source_target_pairs={{0,2},{1,3},{2,0},{3,1},{4,6},{5,7},{6,4},{7,5},{8,10},{9,11},{10,... | collective-permute-start | bytes 786440 | tf_op jit(solution)/shard_map/ppermute | solution.py:406
  62.4 12.0 %collective-permute-start.19 = (bf16[256,512]{1,0:T(8,128)(2,1)S(1)}, bf16[256,512]{1,0:T(8,128)(2,1)S(1)}, u32[]{:S(2)}, u32[]{:S(2)}) collective-permute-start(bf16[256,512]{1,0:T(8,128)(2,1)S(1)} %grad_rows.21), channel_id=1, source_target_pairs={{0,2},{1,3},{2,0},{3,1},{4,6},{5,7},{6,4},{7,5},{8,10},{9,11},{10,... | collective-permute-start | bytes 786440 | tf_op jit(solution)/shard_map/ppermute | solution.py:406
  63.5 13.9 %collective-permute-start.20 = (bf16[256,512]{1,0:T(8,128)(2,1)S(1)}, bf16[256,512]{1,0:T(8,128)(2,1)S(1)}, u32[]{:S(2)}, u32[]{:S(2)}) collective-permute-start(bf16[256,512]{1,0:T(8,128)(2,1)S(1)} %grad_rows.23), channel_id=1, source_target_pairs={{0,2},{1,3},{2,0},{3,1},{4,6},{5,7},{6,4},{7,5},{8,10},{9,11},{10,... | collective-permute-start | bytes 786440 | tf_op jit(solution)/shard_map/ppermute | solution.py:406
  65.1 17.0 %collective-permute-start.21 = (bf16[256,512]{1,0:T(8,128)(2,1)S(1)}, bf16[256,512]{1,0:T(8,128)(2,1)S(1)}, u32[]{:S(2)}, u32[]{:S(2)}) collective-permute-start(bf16[256,512]{1,0:T(8,128)(2,1)S(1)} %grad_rows.16.refs_6_), channel_id=1, source_target_pairs={{0,2},{1,3},{2,0},{3,1},{4,6},{5,7},{6,4},{7,5},{8,10},{9,11},{10,... | collective-permute-start | bytes 786440 | tf_op jit(solution)/shard_map/ppermute | solution.py:406
  72.9 12.0 %collective-permute-start.22 = (bf16[256,512]{1,0:T(8,128)(2,1)S(1)}, bf16[256,512]{1,0:T(8,128)(2,1)S(1)}, u32[]{:S(2)}, u32[]{:S(2)}) collective-permute-start(bf16[256,512]{1,0:T(8,128)(2,1)S(1)} %get-tuple-element.86.refs_1_.refs_5_), channel_id=1, source_target_pairs={{0,1},{1,0},{2,3},{3,2},{4,5},{5,4},{6,7},{7,6},{8,9},{9,8},{10,11... | collective-permute-start | bytes 786440 | tf_op jit(solution)/shard_map/ppermute | solution.py:403
  75.4 9.9 %collective-permute-start.23 = (bf16[256,512]{1,0:T(8,128)(2,1)S(1)}, bf16[256,512]{1,0:T(8,128)(2,1)S(1)}, u32[]{:S(2)}, u32[]{:S(2)}) collective-permute-start(bf16[256,512]{1,0:T(8,128)(2,1)S(1)} %get-tuple-element.87.refs_2_.refs_5_), channel_id=1, source_target_pairs={{0,1},{1,0},{2,3},{3,2},{4,5},{5,4},{6,7},{7,6},{8,9},{9,8},{10,11... | collective-permute-start | bytes 786440 | tf_op jit(solution)/shard_map/ppermute | solution.py:403
  83.3 9.2 %collective-permute-start.26 = (bf16[256,512]{1,0:T(8,128)(2,1)S(1)}, bf16[256,512]{1,0:T(8,128)(2,1)S(1)}, u32[]{:S(2)}, u32[]{:S(2)}) collective-permute-start(bf16[256,512]{1,0:T(8,128)(2,1)S(1)} %get-tuple-element.86.refs_1_.refs_5_), channel_id=1, source_target_pairs={{2,0},{3,1},{0,2},{1,3},{6,4},{7,5},{4,6},{5,7},{10,8},{11,9},{8,1... | collective-permute-start | bytes 786440 | tf_op jit(solution)/shard_map/ppermute | solution.py:404
  84.8 13.2 %collective-permute-start.28 = (bf16[256,512]{1,0:T(8,128)(2,1)S(1)}, bf16[256,512]{1,0:T(8,128)(2,1)S(1)}, u32[]{:S(2)}, u32[]{:S(2)}) collective-permute-start(bf16[256,512]{1,0:T(8,128)(2,1)S(1)} %get-tuple-element.87.refs_2_.refs_5_), channel_id=1, source_target_pairs={{2,0},{3,1},{0,2},{1,3},{6,4},{7,5},{4,6},{5,7},{10,8},{11,9},{8,1... | collective-permute-start | bytes 786440 | tf_op jit(solution)/shard_map/ppermute | solution.py:404
  92.5 11.1 %collective-permute-start.30 = (bf16[256,512]{1,0:T(8,128)(2,1)S(1)}, bf16[256,512]{1,0:T(8,128)(2,1)S(1)}, u32[]{:S(2)}, u32[]{:S(2)}) collective-permute-start(bf16[256,512]{1,0:T(8,128)(2,1)S(1)} %get-tuple-element.88.refs_3_.refs_5_), channel_id=1, source_target_pairs={{2,0},{3,1},{0,2},{1,3},{6,4},{7,5},{4,6},{5,7},{10,8},{11,9},{8,1... | collective-permute-start | bytes 786440 | tf_op jit(solution)/shard_map/ppermute | solution.py:404
  98.1 10.7 %collective-permute-start.32 = (bf16[256,512]{1,0:T(8,128)(2,1)S(1)}, bf16[256,512]{1,0:T(8,128)(2,1)S(1)}, u32[]{:S(2)}, u32[]{:S(2)}) collective-permute-start(bf16[256,512]{1,0:T(8,128)(2,1)S(1)} %get-tuple-element.89.refs_4_.refs_5_), channel_id=1, source_target_pairs={{2,0},{3,1},{0,2},{1,3},{6,4},{7,5},{4,6},{5,7},{10,8},{11,9},{8,1... | collective-permute-start | bytes 786440 | tf_op jit(solution)/shard_map/ppermute | solution.py:404
  115.5 24.6 %collective-permute-start.35 = (bf16[256,512]{1,0:T(8,128)(2,1)S(1)}, bf16[256,512]{1,0:T(8,128)(2,1)S(1)}, u32[]{:S(2)}, u32[]{:S(2)}) collective-permute-start(bf16[256,512]{1,0:T(8,128)(2,1)S(1)} %grad_rows.27), channel_id=1, source_target_pairs={{0,2},{1,3},{2,0},{3,1},{4,6},{5,7},{6,4},{7,5},{8,10},{9,11},{10,... | collective-permute-start | bytes 786440 | tf_op jit(solution)/shard_map/ppermute | solution.py:406
  117.6 20.4 %collective-permute-start.36 = (bf16[256,512]{1,0:T(8,128)(2,1)S(1)}, bf16[256,512]{1,0:T(8,128)(2,1)S(1)}, u32[]{:S(2)}, u32[]{:S(2)}) collective-permute-start(bf16[256,512]{1,0:T(8,128)(2,1)S(1)} %grad_rows.29), channel_id=1, source_target_pairs={{0,2},{1,3},{2,0},{3,1},{4,6},{5,7},{6,4},{7,5},{8,10},{9,11},{10,... | collective-permute-start | bytes 786440 | tf_op jit(solution)/shard_map/ppermute | solution.py:406
  118.7 17.2 %collective-permute-start.37 = (bf16[256,512]{1,0:T(8,128)(2,1)S(1)}, bf16[256,512]{1,0:T(8,128)(2,1)S(1)}, u32[]{:S(2)}, u32[]{:S(2)}) collective-permute-start(bf16[256,512]{1,0:T(8,128)(2,1)S(1)} %grad_rows.31), channel_id=1, source_target_pairs={{0,2},{1,3},{2,0},{3,1},{4,6},{5,7},{6,4},{7,5},{8,10},{9,11},{10,... | collective-permute-start | bytes 786440 | tf_op jit(solution)/shard_map/ppermute | solution.py:406
  120.8 21.4 %collective-permute-start.34 = (bf16[256,512]{1,0:T(8,128)(2,1)S(1)}, bf16[256,512]{1,0:T(8,128)(2,1)S(1)}, u32[]{:S(2)}, u32[]{:S(2)}) collective-permute-start(bf16[256,512]{1,0:T(8,128)(2,1)S(1)} %grad_rows.24.refs_6_), channel_id=1, source_target_pairs={{0,2},{1,3},{2,0},{3,1},{4,6},{5,7},{6,4},{7,5},{8,10},{9,11},{10,... | collective-permute-start | bytes 786440 | tf_op jit(solution)/shard_map/ppermute | solution.py:406
  (36 other events, 184.2 us)

commit v3 on v2

--- a/solution.py
+++ b/solution.py
@@ -22,6 +22,7 @@
 bf16 = jnp.bfloat16
 f32 = jnp.float32
 VMEM_LIMIT = 16 * 1024 * 1024
+CAST_VMEM = 63 * 1024 * 1024
 
 
 def token_weight(kinds):
@@ -48,10 +49,8 @@
     return jax.ShapeDtypeStruct(shape, dtype)
 
 
-def call(body, name, meta, ins, outs, grid=(1,), scratch=(), aliases=None, flops=0, after=()):
+def call(body, name, meta, ins, outs, grid=(1,), scratch=(), aliases=None, after=(), vmem=VMEM_LIMIT):
     arrays = [a for a, _ in ins] + list(after)
-    moved = sum(math.prod(o.shape) * o.dtype.itemsize for o, _ in outs)
-    moved += sum(math.prod(a.shape) * a.dtype.itemsize for a, _ in ins)
     n_in = len(meta) + len(ins)
 
     def run(*refs):
@@ -69,8 +68,8 @@
             scratch_shapes=list(scratch),
         ),
         input_output_aliases=aliases or {},
-        compiler_params=pltpu.CompilerParams(vmem_limit_bytes=VMEM_LIMIT),
-        cost_estimate=pl.CostEstimate(flops=flops, bytes_accessed=moved, transcendentals=0),
+        compiler_params=pltpu.CompilerParams(vmem_limit_bytes=vmem),
+        cost_estimate=pl.CostEstimate(flops=1, bytes_accessed=1, transcendentals=0),
     )(*meta, *arrays)
 
 
@@ -85,36 +84,60 @@
     return lax.rem(plan_sum(plan), 2)
 
 
-def cast_body(chunks, theta, *refs):
-    outs, (held, sems) = refs[:len(chunks)], refs[len(chunks):]
-    cr, wide = outs[0].shape
-    width = wide // 2
+def cast_body(blocks, theta, *refs):
+    outs, (held, sems) = refs[:len(blocks)], refs[len(blocks):]
     copies = []
-    for n, i in enumerate(chunks):
-        copy = pltpu.make_async_copy(theta.at[0, :, pl.ds(i * cr, cr), :], held.at[n], sems.at[n])
-        copy.start()
+    for n, (off, size) in enumerate(blocks):
+        copy = pltpu.make_async_copy(
+            theta.at[0, :, pl.ds(off, size), :], held.at[:, pl.ds(off, size), :], sems.at[n])
+        if (off, size) not in blocks[:n]:
+            copy.start()
         copies.append(copy)
-    for n, copy in enumerate(copies):
-        copy.wait()
+    width = held.shape[2]
+    for n, (off, size) in enumerate(blocks):
+        copies[n].wait()
         for k in range(2):
-            outs[n][:, k * width:(k + 1) * width] = held[n, k].astype(bf16)
-
-
-def cast_chunks(weights, chunks, cr):
-    width = weights.shape[-1]
-    return call(
-        functools.partial(cast_body, chunks), "cast_rows", (),
+            outs[n][:, k * width:(k + 1) * width] = held[k, off:off + size].astype(bf16)
+
+
+def cast_blocks(weights, blocks, after=(), vmem=VMEM_LIMIT):
+    _, _, rows, width = weights.shape
+    shapes = [(size, 2 * width) for _, size in blocks]
+    return call(
+        functools.partial(cast_body, blocks), "cast_rows", (),
         [(weights, pl.BlockSpec(memory_space=pltpu.HBM))],
-        [(sds((cr, 2 * width), bf16), whole((cr, 2 * width)))] * len(chunks),
-        scratch=[
-            pltpu.VMEM((len(chunks), 2, cr, width), f32),
-            pltpu.SemaphoreType.DMA((len(chunks),)),
-        ],
-    )
-
-
-def weigh_body(kinds, out):
-    out[...] = token_weight(kinds[...])
+        [(sds(shape, bf16), whole(shape)) for shape in shapes],
+        scratch=[pltpu.VMEM((2, rows, width), f32), pltpu.SemaphoreType.DMA((len(blocks),))],
+        after=after, vmem=vmem,
+    )
+
+
+def join_body(first, *refs):
+    out = refs[-1]
+    off = 0
+    for part in (first,) + refs[:-1]:
+        out[off:off + part.shape[0], :] = part[...]
+        off += part.shape[0]
+
+
+def join_rows(parts, after=()):
+    shape = (sum(p.shape[0] for p in parts), parts[0].shape[1])
+    return call(
+        join_body, "join_rows", (), [(p, whole(p.shape)) for p in parts],
+        [(sds(shape, parts[0].dtype), whole(shape))], after=after,
+    )[0]
+
+
+def weigh_body(own, other, out):
+    for h, kinds in enumerate((own, other)):
+        lanes = kinds.shape[0]
+        pad = jnp.zeros((8 - lanes % 8, 128), f32)
+        value = token_weight(kinds[...])
+        if lanes % 8:
+            value = jnp.concatenate([value, pad], 0)
+        turned = value.T
+        for j in range(lanes):
+            out[h, j * 128:(j + 1) * 128, :] = turned[:, j:j + 1]
 
 
 def copy_body(x, out):
@@ -123,21 +146,6 @@
 
 def relay(x, after):
     return call(copy_body, "relay_rows", (), [(x, whole(x.shape))], [(sds(x.shape, x.dtype), whole(x.shape))], after=after)[0]
-
-
-def turn_body(pos, x, xt):
-    xt[...] = x[...].T
-
-
-def turn(pos, x, chips, rows, tile):
-    tokens = x.shape[0]
-    per = rows // tile
-    return call(
-        turn_body, "turn_tokens", (pos,),
-        [(x, pl.BlockSpec((tokens, tile), lambda g, m: (0, m[1 + g // per] * per + g % per)))],
-        [(sds((chips * rows, tokens), bf16), pl.BlockSpec((tile, tokens), lambda g, m: (g, 0)))],
-        grid=(chips * per,),
-    )[0]
 
 
 def forward_body(count, first_call, pos, *refs):
@@ -167,7 +175,7 @@
     return lambda g, m: (0, m[slot] * per + i)
 
 
-def forward(pos, acc, gram, pieces, xs, cr, per, after=()):
+def forward(pos, acc, gram, pieces, xs, rows, after=()):
     tokens = xs[0].shape[0]
     wide = pieces[0][0].shape[1]
     width = wide // 2
@@ -177,34 +185,44 @@
         ins += [(acc, whole(acc.shape)), (gram, whole(gram.shape))]
     ins += [(low, whole(low.shape)) for low, _, _ in pieces]
     for x in xs:
-        ins += [(x, once((tokens, cr), column(slot, i, per))) for _, slot, i in pieces]
+        ins += [
+            (x, once((tokens, low.shape[0]), column(slot, i, rows // low.shape[0])))
+            for low, slot, i in pieces
+        ]
     return call(
         functools.partial(forward_body, count, acc is None), "forward_rows", (pos,), ins,
         [(sds((2, tokens, wide), f32), whole((2, tokens, wide))), (sds((width, width), f32), whole((width, width)))],
-        flops=4 * tokens * cr * wide * count, after=after,
+        after=after,
     )
 
 
 def finish_body(scale, count, steps, pos, acc_in, gram_in, cw, *refs):
     lows = refs[:count]
     xs = (refs[count:2 * count], refs[2 * count:3 * count])
-    slopes, w_hi, w_lo, w_acc = refs[3 * count:]
+    slopes, w_hi, w_lo, w_acc, g_hi, g_lo = refs[3 * count:]
     width = gram_in.shape[0]
-    gram = gram_in[...]
-    for p in range(count):
-        dec = lows[p][:, width:]
-        gram = gram + dot_rows(dec, dec)
-    g_hi = gram.astype(bf16)
-    g_lo = (gram - g_hi.astype(f32)).astype(bf16)
+    step = pl.program_id(0)
+
+    @pl.when(step == 0)
+    def _():
+        gram = gram_in[...]
+        for p in range(count):
+            dec = lows[p][:, width:]
+            gram = gram + dot_rows(dec, dec)
+        hi = gram.astype(bf16)
+        g_hi[...] = hi
+        g_lo[...] = (gram - hi.astype(f32)).astype(bf16)
+        w_acc[...] = jnp.zeros_like(w_acc)
+
     w_new = None
     for h in range(2):
         value = acc_in[h]
         for p in range(count):
             value = value + dot(xs[h][p][...], lows[p][...])
         pre = value[:, :width]
-        sig = 1.0 / (1.0 + jnp.exp(-pre))
+        sig = 0.5 + 0.5 * jnp.tanh(0.5 * pre)
         hidden = (pre * sig).astype(bf16)
-        back = dot(hidden, g_hi) + dot(hidden, g_lo) - value[:, width:]
+        back = dot(hidden, g_hi[...]) + dot(hidden, g_lo[...]) - value[:, width:]
         weight = cw[h]
         slope = (weight * scale) * back * (sig * (1.0 + pre * (1.0 - sig)))
         counted = (weight * hidden.astype(f32)).astype(bf16)
@@ -212,15 +230,7 @@
         slopes[h, :, width:] = counted
         term = dot_rows(counted, hidden)
         w_new = term if w_new is None else w_new + term
-    step = pl.program_id(0)
-
-    @pl.when(step == 0)
-    def _():
-        w_acc[...] = w_new
-
-    @pl.when(step > 0)
-    def _():
-        w_acc[...] += w_new
+    w_acc[...] += w_new
 
     @pl.when(step == steps - 1)
     def _():
@@ -230,7 +240,7 @@
         w_lo[...] = (total - hi.astype(f32)).astype(bf16)
 
 
-def finish(pos, acc, gram, cw, pieces, xs, cr, per, scale):
+def finish(pos, acc, gram, cw, pieces, xs, rows, scale):
     tokens = xs[0].shape[0]
     wide = pieces[0][0].shape[1]
     width = wide // 2
@@ -244,36 +254,36 @@
     ]
     ins += [(low, whole(low.shape)) for low, _, _ in pieces]
     for x in xs:
-        for _, slot, i in pieces:
-            ins.append((x, pl.BlockSpec((tile, cr), lambda g, m, slot=slot, i=i: (g, m[slot] * per + i))))
+        for low, slot, i in pieces:
+            cr = low.shape[0]
+            ins.append((x, pl.BlockSpec(
+                (tile, cr), lambda g, m, slot=slot, i=i, per=rows // cr: (g, m[slot] * per + i))))
     square = (sds((width, width), bf16), whole((width, width)))
     return call(
         functools.partial(finish_body, scale, count, steps), "finish_slopes", (pos,), ins,
         [(sds((2, tokens, wide), bf16), pl.BlockSpec((2, tile, wide), lambda g, m: (0, g, 0))), square, square],
         grid=(steps,),
-        scratch=[pltpu.VMEM((width, width), f32)],
-        flops=4 * tokens * cr * wide * count + 12 * tokens * width * width,
-    )
-
-
-def grad_body(scale, xt_own, xt_par, slopes, w_hi, w_lo, low, out):
+        scratch=[pltpu.VMEM((width, width), f32)] + [pltpu.VMEM((width, width), bf16)] * 2,
+    )
+
+
+def grad_body(scale, pos, x_own, x_par, slopes, w_hi, w_lo, low, out):
     width = w_hi.shape[0]
-    both = dot(xt_own[...], slopes[0]) + dot(xt_par[...], slopes[1])
+    both = dot_rows(x_own[...], slopes[0]) + dot_rows(x_par[...], slopes[1])
     dec = low[:, width:]
     grad_dec = scale * (dot(dec, w_hi[...]) + dot(dec, w_lo[...]) - both[:, width:])
     out[:, :width] = both[:, :width].astype(out.dtype)
     out[:, width:] = grad_dec.astype(out.dtype)
 
 
-def grad_rows(scale, block, cr, xt, slopes, w_hi, w_lo, low, dtype, after=()):
-    tokens = xt[0].shape[1]
-    wide = low.shape[1]
-    ins = [(x, once((cr, tokens), lambda g: (block, 0))) for x in xt]
+def grad_rows(pos, scale, slot, i, xs, rows, slopes, w_hi, w_lo, low, dtype, after=()):
+    tokens = xs[0].shape[0]
+    cr, wide = low.shape
+    ins = [(x, once((tokens, cr), column(slot, i, rows // cr))) for x in xs]
     ins += [(a, whole(a.shape)) for a in (slopes, w_hi, w_lo, low)]
     return call(
-        functools.partial(grad_body, scale), "grad_rows", (), ins,
-        [(sds((cr, wide), dtype), whole((cr, wide)))],
-        flops=4 * tokens * cr * wide, after=after,
+        functools.partial(grad_body, scale), "grad_rows", (pos,), ins,
+        [(sds((cr, wide), dtype), whole((cr, wide)))], after=after,
     )[0]
 
 
@@ -407,9 +417,10 @@
         a, "fsdp", [(f, ((f // 2 + s) % chips) * 2 + f % 2) for f in range(n_fsdp)])
     across = lambda a, bit: lax.ppermute(a, "replica", [(r, r ^ bit) for r in range(n_rep)])
 
-    low_own = cast_chunks(weights, [0], cr)
+    blocks = [(i * cr, cr) for i in range(chunks)]
+    low_own = list(cast_blocks(weights, blocks[:1], vmem=CAST_VMEM))
     if chunks > 1:
-        low_own = list(low_own) + list(cast_chunks(weights, list(range(1, chunks)), cr))
+        low_own += list(cast_blocks(weights, blocks[1:], low_own, vmem=CAST_VMEM))
 
     chip = lax.axis_index("fsdp") // 2
     core = lax.axis_index("fsdp") % 2
@@ -421,55 +432,55 @@
     keep, send = outer_start(pos, plan, anchor, weights, after=[low_own[-1]])
     outer_in = across(send, 1)
     lanes = kinds.reshape(-1, 128)
-    cw_own = call(
-        weigh_body, "weigh_tokens", (), [(lanes, whole(lanes.shape))],
-        [(sds(lanes.shape, f32), whole(lanes.shape))], after=[send],
+    cw = call(
+        weigh_body, "weigh_tokens", (),
+        [(lanes, whole(lanes.shape)), (to_partner(lanes), whole(lanes.shape))],
+        [(sds((2, tokens, 1), f32), whole((2, tokens, 1)))], after=[send],
     )[0]
-    cw = jnp.stack([cw_own, to_partner(cw_own)]).reshape(2, tokens, 1)
-    xt = [turn(pos, x, chips, rows, cr) for x in xs]
 
     state = [(weights, first_moment, second_moment)] * chunks
     state_block = list(range(chunks))
     for step in range(INNER):
         last = step == INNER - 1
-        near = [(low_own[i], 1, i) for i in range(chunks)]
-        near += [(to_partner(low_own[i]), 1 + chips, i) for i in range(chunks)]
-        acc, gram = forward(pos, None, None, near, xs, cr, chunks)
         far = [(i, s) for i in range(chunks) for s in range(1, chips)]
         low_far = {(i, s): fetch(low_own[i], s) for i, s in far}
-
-        stages = []
+        low_all = join_rows(low_own) if chunks > 1 else low_own[0]
+        near = [(low_all, 1, 0), (to_partner(low_all), 1 + chips, 0)]
+        acc, gram = forward(pos, None, None, near, xs, rows)
+
         if step == 0:
             bits = [1 << b for b in range(1, n_rep.bit_length() - 1)]
             own = keep
             took = outer_in
         wait_for = []
-        pending = None
+        pending = []
         for n, (i, s) in enumerate(far):
             handed = to_partner(relay(low_far[i, s], [acc] + wait_for))
-            pieces = [(low_far[i, s], 1 + s, i)]
-            if pending is not None:
-                pieces = [pending] + pieces
-            acc, gram = forward(pos, acc, gram, pieces, xs, cr, chunks)
-            pending = (handed, 1 + chips + s, i)
+            pending.append((low_far[i, s], 1 + s, i))
+            if n > 0 or len(far) == 1:
+                acc, gram = forward(pos, acc, gram, pending, xs, rows)
+                pending = []
+            pending.append((handed, 1 + chips + s, i))
             if step == 0 and bits and n in (0, len(far) - 2):
                 own = outer_add(plan, own, took, False, [acc])
                 took = across(own, bits.pop(0))
                 wait_for = [own]
-        slopes, w_hi, w_lo = finish(pos, acc, gram, cw, [pending], xs, cr, chunks, scale)
-
-        mine, got = [], []
+        slopes, w_hi, w_lo = finish(pos, acc, gram, cw, pending, xs, rows, scale)
+
+        mine, got, sent = [], [], []
         for i in range(chunks):
-            sent = [
-                grad_rows(scale, s * chunks + i, cr, xt, slopes, w_hi, w_lo, low_far[i, s], bf16)
-                for s in range(1, chips)
-            ]
-            got.append([give(g, s) for s, g in enumerate(sent, 1)])
+            now = []
+            for s in range(1, chips):
+                now.append(grad_rows(
+                    pos, scale, 1 + s, i, xs, rows, slopes, w_hi, w_lo, low_far[i, s], bf16, after=sent[-1:]))
+                sent.append(now[-1])
+            got.append([give(g, s) for s, g in enumerate(now, 1)])
         for i in range(chunks):
-            mine.append(grad_rows(scale, i, cr, xt, slopes, w_hi, w_lo, low_own[i], f32, after=sent))
+            mine.append(grad_rows(
+                pos, scale, 1, i, xs, rows, slopes, w_hi, w_lo, low_own[i], f32, after=(sent + mine)[-1:]))
         if step == 0:
             while bits:
-                own = outer_add(plan, own, took, False, sent)
+                own = outer_add(plan, own, took, False, sent[-1:])
                 took = across(own, bits.pop(0))
             own = outer_add(plan, own, took, True, mine[-1:])
             new_anc, anchor_out, momentum_out = outer_end(pos, plan, anchor, momentum, own, across(own, 1))

time: 145 us -> 156 us (1.076)
  Pallas kernels: 73.2 us -> 91.2 us
  waiting for transfers between devices: 33.5 us -> 30.6 us
  starting transfers between devices: 29.6 us -> 26.8 us
    pallas_call x54 -> x52, Pallas kernels: 73.2 us -> 91.2 us  [call(): pl.pallas_call(run, name=name, out_shape=[o for o, _ in outs], grid_spec=...]
    ppermute x8, waiting for transfers between devices: 17.5 us -> 11.8 us  [local(): lax.ppermute(a, 'fsdp', [(f, (f // 2 + s) % chips * 2 + f % 2) for f in r...]
    ppermute x8, waiting for transfers between devices: 9.06 us -> 14 us  [local(): lax.ppermute(a, 'fsdp', [((f // 2 + s) % chips * 2 + f % 2, f) for f in r...]
    ppermute x18 -> x12, waiting for transfers between devices: 4.21 us -> 1.57 us  [local(): to_partner = lambda a: lax.ppermute(a, 'fsdp', partner)]
    ppermute x18 -> x12, starting transfers between devices: 3.52 us -> 1.54 us  [local(): to_partner = lambda a: lax.ppermute(a, 'fsdp', partner)]
    another operation x2 -> x0, local copies, waits for them, and re-layouts: 1.74 us -> none  [local(): cw = jnp.stack([cw_own, to_partner(cw_own)]).reshape(2, tokens, 1)]
    unnamed x44 -> x30, local copies, waits for them, and re-layouts: 3.7 us -> 4.65 us
  transfers between devices with their start and end apart: 38 -> 32, of which waited for: 11 -> 13; matrix products, arithmetic and copies ran while one was open for 2% -> 0% of each run, Pallas kernels for 47% -> 53%
where the time goes in v3:
time: 156 us; the launch traced here: 155 us
  Pallas kernels  91.2 us (58%)
  waiting for transfers between devices  30.6 us (20%)
  starting transfers between devices  26.8 us (17%)
  local copies, waits for them, and re-layouts  4.73 us (3%)
    pallas_call x52, Pallas kernels, call(): pl.pallas_call(run, name=name, out_shape=[o for o, _ in outs], grid_spec=...  91.2 us
    ppermute x8, waiting for transfers between devices, local(): lax.ppermute(a, 'fsdp', [((f // 2 + s) % chips * 2 + f % 2, f) for f in r...  14 us
    ppermute x8, waiting for transfers between devices, local(): lax.ppermute(a, 'fsdp', [(f, (f // 2 + s) % chips * 2 + f % 2) for f in r...  11.8 us
    ppermute x8, starting transfers between devices, local(): lax.ppermute(a, 'fsdp', [((f // 2 + s) % chips * 2 + f % 2, f) for f in r...  10 us
    ppermute x8, starting transfers between devices, local(): lax.ppermute(a, 'fsdp', [(f, (f // 2 + s) % chips * 2 + f % 2) for f in r...  8.38 us
    ppermute x4, starting transfers between devices, local(): lax.ppermute(a, 'replica', [(r, r ^ bit) for r in range(n_rep)])  6.87 us
    unnamed x30, local copies, waits for them, and re-layouts  4.65 us
    ppermute x4, waiting for transfers between devices, local(): lax.ppermute(a, 'replica', [(r, r ^ bit) for r in range(n_rep)])  3.3 us
  transfers between devices with their start and end apart: 32, of which 13 were waited for; matrix products, arithmetic and copies ran while one was open for 0% of the time, Pallas kernels for 53%

profile of v3, /device:TPU:0, one launch (start us, length us, event | category | flops | bytes accessed | tf_op | source)
XLA Modules:
  0.0 154.6 jit_solution(11337596615589912183)
XLA Ops:
  3.0 2.3 %cast_rows.3 = (bf16[256,512]{1,0:T(8,128)(2,1)}, bf16[256,512]{1,0:T(8,128)(2,1)}, bf16[256,512]{1,0:T(8,128)(2,1)}) custom-call(f32[1,2,1024,256]{3,2,1,0:T(8,128)} %refs_3_.14, bf16[256,512]{1,0:T(8,128)(2,1)} %cast_rows.2.refs_1_.refs_0_.refs_6_), custom_call_target="tpu_custom_call" | custom-call | flops 1 | bytes 1 | tf_op jit(solution)/shard_map/cast_rows/pallas_call | solution.py:59
  9.4 3.0 %collective-permute-start.2 = (bf16[256,512]{1,0:T(8,128)(2,1)S(1)}, bf16[256,512]{1,0:T(8,128)(2,1)S(1)}, u32[]{:S(2)}, u32[]{:S(2)}) collective-permute-start(bf16[256,512]{1,0:T(8,128)(2,1)S(1)} %copy-done.6), channel_id=1, source_target_pairs={{2,0},{3,1},{0,2},{1,3},{6,4},{7,5},{4,6},{5,7},{10,8},{11,9},{8,1... | collective-permute-start | bytes 786440 | tf_op jit(solution)/shard_map/ppermute | solution.py:414
  17.7 5.4 %forward_rows.8 = (f32[2,512,512]{2,1,0:T(8,128)S(1)}, f32[256,256]{1,0:T(8,128)S(1)}) custom-call(s32[5]{0:T(128)S(1)} %stack.23.refs_0_, bf16[1024,512]{1,0:T(8,128)(2,1)} %join_rows.2.refs_1_, bf16[1024,512]{1,0:T(8,128)(2,1)} %collective-permute-done.1.refs_2_, bf16[512,4096]{1,0:T(8,128)(2,1)S(1)} %copy-done, bf16[512,4096]{1,0:T(8,128)(2,1)S(1)} %copy-done, ...), custom_call_target="tpu_custom_call" | custom-call | flops 1 | bytes 1 | tf_op jit(solution)/shard_map/forward_rows/pallas_call | solution.py:59
  27.9 2.8 %forward_rows.9 = (f32[2,512,512]{2,1,0:T(8,128)S(1)}, f32[256,256]{1,0:T(8,128)S(1)}) custom-call(s32[5]{0:T(128)S(1)} %stack.23.refs_0_, f32[2,512,512]{2,1,0:T(8,128)S(1)} %get-tuple-element.66.refs_1_.refs_3_, f32[256,256]{1,0:T(8,128)S(1)} %get-tuple-element.67.refs_2_, bf16[256,512]{1,0:T(8,128)(2,1)S(1)} %collective-permute-done.2.refs_0_.refs_3_.refs_6_, ...), custom_call_target="tpu_custom_call" | custom-call | flops 1 | bytes 1 | tf_op jit(solution)/shard_map/forward_rows/pallas_call | solution.py:59
  32.7 2.5 %forward_rows.10 = (f32[2,512,512]{2,1,0:T(8,128)S(1)}, f32[256,256]{1,0:T(8,128)S(1)}) custom-call(s32[5]{0:T(128)S(1)} %stack.23.refs_0_, f32[2,512,512]{2,1,0:T(8,128)S(1)} %get-tuple-element.68.refs_1_, f32[256,256]{1,0:T(8,128)S(1)} %get-tuple-element.69.refs_2_, bf16[256,512]{1,0:T(8,128)(2,1)S(1)} %collective-permute-done.6.refs_3_, ...), custom_call_target="tpu_custom_call" | custom-call | flops 1 | bytes 1 | tf_op jit(solution)/shard_map/forward_rows/pallas_call | solution.py:59
  37.9 2.7 %collective-permute-start.14 = (bf16[512,256]{1,0:T(8,128)(2,1)S(1)}, bf16[512,256]{1,0:T(8,128)(2,1)S(1)}, u32[]{:S(2)}, u32[]{:S(2)}) collective-permute-start(bf16[512,256]{1,0:T(8,128)(2,1)S(1)} %add_halves.4.refs_2_.refs_1_), channel_id=1, source_target_pairs={{0,16},{4,20},{8,24},{12,28},{16,0},{20,4},{24,8},{28,12},{1,17},{... | collective-permute-start | bytes 786440 | tf_op jit(solution)/shard_map/ppermute | solution.py:418
  41.9 2.5 %forward_rows.11 = (f32[2,512,512]{2,1,0:T(8,128)S(1)}, f32[256,256]{1,0:T(8,128)S(1)}) custom-call(s32[5]{0:T(128)S(1)} %stack.23.refs_0_, f32[2,512,512]{2,1,0:T(8,128)S(1)} %get-tuple-element.72.refs_1_.refs_3_, f32[256,256]{1,0:T(8,128)S(1)} %get-tuple-element.73.refs_2_, bf16[256,512]{1,0:T(8,128)(2,1)S(1)} %collective-permute-done.8.refs_3_, ...), custom_call_target="tpu_custom_call" | custom-call | flops 1 | bytes 1 | tf_op jit(solution)/shard_map/forward_rows/pallas_call | solution.py:59
  44.4 3.6 %finish_slopes.2 = (bf16[2,512,512]{2,1,0:T(8,128)(2,1)S(1)}, bf16[256,256]{1,0:T(8,128)(2,1)S(1)}, bf16[256,256]{1,0:T(8,128)(2,1)S(1)}) custom-call(s32[5]{0:T(128)S(1)} %stack.23.refs_0_, f32[2,512,512]{2,1,0:T(8,128)S(1)} %get-tuple-element.74.refs_1_, f32[256,256]{1,0:T(8,128)S(1)} %get-tuple-element.75.refs_2_, f32[2,512,1]{2,1,0:T(8,128)S(1)} %weigh_tokens.1.refs_3_, ...), custom_call_target="tpu_custom_call" | custom-call | flops 1 | bytes 1 | tf_op jit(solution)/shard_map/finish_slopes/pallas_call | solution.py:59
  60.5 2.1 %grad_rows.22.refs_7_.refs_1_ = f32[256,512]{1,0:T(8,128)S(1)} custom-call(s32[5]{0:T(128)S(1)} %stack.23.refs_0_, bf16[512,4096]{1,0:T(8,128)(2,1)S(1)} %copy-done, bf16[512,4096]{1,0:T(8,128)(2,1)} %collective-permute-done.refs_5_.refs_6_.refs_9_.refs_10_.refs_11_.refs_7_.refs_8_.refs_2_, bf16[2,512,512]{2,1,0:T(8,128)(2,1)S(1)} %get-tuple-element.76.refs_3_, ...), custom_call_target="tpu_custom_call" | custom-call | flops 1 | bytes 1 | tf_op jit(solution)/shard_map/grad_rows/pallas_call | solution.py:59
  62.7 2.4 %grad_rows.23.refs_3_.refs_1_ = f32[256,512]{1,0:T(8,128)S(1)} custom-call(s32[5]{0:T(128)S(1)} %stack.23.refs_0_, bf16[512,4096]{1,0:T(8,128)(2,1)S(1)} %copy-done, bf16[512,4096]{1,0:T(8,128)(2,1)} %collective-permute-done.refs_5_.refs_6_.refs_9_.refs_10_.refs_11_.refs_7_.refs_8_.refs_2_, bf16[2,512,512]{2,1,0:T(8,128)(2,1)S(1)} %get-tuple-element.76.refs_3_, ...), custom_call_target="tpu_custom_call" | custom-call | flops 1 | bytes 1 | tf_op jit(solution)/shard_map/grad_rows/pallas_call | solution.py:59
  70.9 3.3 %collective-permute-done.15.refs_5_ = bf16[512,256]{1,0:T(8,128)(2,1)S(1)} collective-permute-done((bf16[512,256]{1,0:T(8,128)(2,1)S(1)}, bf16[512,256]{1,0:T(8,128)(2,1)S(1)}, u32[]{:S(2)}, u32[]{:S(2)}) %collective-permute-start.15) | collective-permute-done | bytes 262176 | tf_op jit(solution)/shard_map/ppermute | solution.py:418
  74.2 3.1 %outer_step.1 = (f32[1024,256]{1,0:T(8,128)S(1)}, f32[2,1024,256]{2,1,0:T(8,128)}, f32[2,1024,256]{2,1,0:T(8,128)}) custom-call(s32[5]{0:T(128)S(1)} %stack.23.refs_0_, s32[8]{0:T(128)S(1)} %copy-done.13, f32[2,1024,256]{2,1,0:T(8,128)S(1)} %copy-done.5, f32[2,1024,256]{2,1,0:T(8,128)S(1)} %copy-done.10, bf16[512,256]{1,0:T(8,128)(2,1)S(1)} %add_halves.5.refs_4_, ...), custom_call_target="tpu_custom_call" | custom-call | flops 1 | bytes 1 | tf_op jit(solution)/shard_map/outer_step/pallas_call | solution.py:59
  78.4 3.3 %collective-permute-done.17.refs_2_ = bf16[256,512]{1,0:T(8,128)(2,1)S(1)} collective-permute-done((bf16[256,512]{1,0:T(8,128)(2,1)S(1)}, bf16[256,512]{1,0:T(8,128)(2,1)S(1)}, u32[]{:S(2)}, u32[]{:S(2)}) %collective-permute-start.17) | collective-permute-done | bytes 262176 | tf_op jit(solution)/shard_map/ppermute | solution.py:416
  82.7 4.6 %collective-permute-done.16.refs_2_ = bf16[256,512]{1,0:T(8,128)(2,1)S(1)} collective-permute-done((bf16[256,512]{1,0:T(8,128)(2,1)S(1)}, bf16[256,512]{1,0:T(8,128)(2,1)S(1)}, u32[]{:S(2)}, u32[]{:S(2)}) %collective-permute-start.16) | collective-permute-done | bytes 262176 | tf_op jit(solution)/shard_map/ppermute | solution.py:416
  88.3 3.5 %collective-permute-done.13.refs_2_ = bf16[256,512]{1,0:T(8,128)(2,1)S(1)} collective-permute-done((bf16[256,512]{1,0:T(8,128)(2,1)S(1)}, bf16[256,512]{1,0:T(8,128)(2,1)S(1)}, u32[]{:S(2)}, u32[]{:S(2)}) %collective-permute-start.13) | collective-permute-done | bytes 262176 | tf_op jit(solution)/shard_map/ppermute | solution.py:416
  95.6 4.9 %forward_rows.12 = (f32[2,512,512]{2,1,0:T(8,128)S(1)}, f32[256,256]{1,0:T(8,128)S(1)}) custom-call(s32[5]{0:T(128)S(1)} %stack.23.refs_0_, bf16[1024,512]{1,0:T(8,128)(2,1)S(1)} %join_rows.3.refs_1_, bf16[1024,512]{1,0:T(8,128)(2,1)S(1)} %collective-permute-done.19.refs_2_, bf16[512,4096]{1,0:T(8,128)(2,1)S(1)} %copy-done, bf16[512,4096]{1,0:T(8,128)(2,1)S(1)} %copy-done, ...), custom_call_target="tpu_custom_call" | custom-call | flops 1 | bytes 1 | tf_op jit(solution)/shard_map/forward_rows/pallas_call | solution.py:59
  103.3 4.4 %collective-permute-done.22.refs_5_.refs_0_.refs_6_ = bf16[256,512]{1,0:T(8,128)(2,1)S(1)} collective-permute-done((bf16[256,512]{1,0:T(8,128)(2,1)S(1)}, bf16[256,512]{1,0:T(8,128)(2,1)S(1)}, u32[]{:S(2)}, u32[]{:S(2)}) %collective-permute-start.22) | collective-permute-done | bytes 262176 | tf_op jit(solution)/shard_map/ppermute | solution.py:414
  109.0 2.8 %forward_rows.13 = (f32[2,512,512]{2,1,0:T(8,128)S(1)}, f32[256,256]{1,0:T(8,128)S(1)}) custom-call(s32[5]{0:T(128)S(1)} %stack.23.refs_0_, f32[2,512,512]{2,1,0:T(8,128)S(1)} %get-tuple-element.84.refs_1_, f32[256,256]{1,0:T(8,128)S(1)} %get-tuple-element.85.refs_2_, bf16[256,512]{1,0:T(8,128)(2,1)S(1)} %collective-permute-done.20.refs_0_.refs_3_.refs_6_, ...), custom_call_target="tpu_custom_call" | custom-call | flops 1 | bytes 1 | tf_op jit(solution)/shard_map/forward_rows/pallas_call | solution.py:59
  113.5 2.5 %forward_rows.14 = (f32[2,512,512]{2,1,0:T(8,128)S(1)}, f32[256,256]{1,0:T(8,128)S(1)}) custom-call(s32[5]{0:T(128)S(1)} %stack.23.refs_0_, f32[2,512,512]{2,1,0:T(8,128)S(1)} %get-tuple-element.86.refs_1_, f32[256,256]{1,0:T(8,128)S(1)} %get-tuple-element.87.refs_2_, bf16[256,512]{1,0:T(8,128)(2,1)S(1)} %collective-permute-done.23.refs_3_, ...), custom_call_target="tpu_custom_call" | custom-call | flops 1 | bytes 1 | tf_op jit(solution)/shard_map/forward_rows/pallas_call | solution.py:59
  116.0 2.6 %collective-permute-done.26.refs_4_.refs_0_.refs_6_ = bf16[256,512]{1,0:T(8,128)(2,1)S(1)} collective-permute-done((bf16[256,512]{1,0:T(8,128)(2,1)S(1)}, bf16[256,512]{1,0:T(8,128)(2,1)S(1)}, u32[]{:S(2)}, u32[]{:S(2)}) %collective-permute-start.26) | collective-permute-done | bytes 262176 | tf_op jit(solution)/shard_map/ppermute | solution.py:414
  118.7 2.7 %forward_rows.15 = (f32[2,512,512]{2,1,0:T(8,128)S(1)}, f32[256,256]{1,0:T(8,128)S(1)}) custom-call(s32[5]{0:T(128)S(1)} %stack.23.refs_0_, f32[2,512,512]{2,1,0:T(8,128)S(1)} %get-tuple-element.88.refs_1_, f32[256,256]{1,0:T(8,128)S(1)} %get-tuple-element.89.refs_2_, bf16[256,512]{1,0:T(8,128)(2,1)S(1)} %collective-permute-done.25.refs_3_, ...), custom_call_target="tpu_custom_call" | custom-call | flops 1 | bytes 1 | tf_op jit(solution)/shard_map/forward_rows/pallas_call | solution.py:59
  121.4 3.4 %finish_slopes.3 = (bf16[2,512,512]{2,1,0:T(8,128)(2,1)S(1)}, bf16[256,256]{1,0:T(8,128)(2,1)S(1)}, bf16[256,256]{1,0:T(8,128)(2,1)S(1)}) custom-call(s32[5]{0:T(128)S(1)} %stack.23.refs_0_, f32[2,512,512]{2,1,0:T(8,128)S(1)} %get-tuple-element.90.refs_1_, f32[256,256]{1,0:T(8,128)S(1)} %get-tuple-element.91.refs_2_, f32[2,512,1]{2,1,0:T(8,128)S(1)} %weigh_tokens.1.refs_3_, ...), custom_call_target="tpu_custom_call" | custom-call | flops 1 | bytes 1 | tf_op jit(solution)/shard_map/finish_slopes/pallas_call | solution.py:59
  139.5 2.1 %grad_rows.29.refs_7_.refs_1_ = f32[256,512]{1,0:T(8,128)S(1)} custom-call(s32[5]{0:T(128)S(1)} %stack.23.refs_0_, bf16[512,4096]{1,0:T(8,128)(2,1)S(1)} %copy-done, bf16[512,4096]{1,0:T(8,128)(2,1)} %collective-permute-done.refs_5_.refs_6_.refs_9_.refs_10_.refs_11_.refs_7_.refs_8_.refs_2_, bf16[2,512,512]{2,1,0:T(8,128)(2,1)S(1)} %get-tuple-element.92.refs_3_, ...), custom_call_target="tpu_custom_call" | custom-call | flops 1 | bytes 1 | tf_op jit(solution)/shard_map/grad_rows/pallas_call | solution.py:59
  141.6 2.1 %grad_rows.30.refs_7_.refs_1_ = f32[256,512]{1,0:T(8,128)S(1)} custom-call(s32[5]{0:T(128)S(1)} %stack.23.refs_0_, bf16[512,4096]{1,0:T(8,128)(2,1)S(1)} %copy-done, bf16[512,4096]{1,0:T(8,128)(2,1)} %collective-permute-done.refs_5_.refs_6_.refs_9_.refs_10_.refs_11_.refs_7_.refs_8_.refs_2_, bf16[2,512,512]{2,1,0:T(8,128)(2,1)S(1)} %get-tuple-element.92.refs_3_, ...), custom_call_target="tpu_custom_call" | custom-call | flops 1 | bytes 1 | tf_op jit(solution)/shard_map/grad_rows/pallas_call | solution.py:59
  (123 shorter events, 79.1 us)
Async XLA Ops:
  0.6 17.1 %collective-permute-start = (bf16[512,4096]{1,0:T(8,128)(2,1)}, bf16[512,4096]{1,0:T(8,128)(2,1)}, u32[]{:S(2)}, u32[]{:S(2)}) collective-permute-start(bf16[512,4096]{1,0:T(8,128)(2,1)} %refs_1_.35), channel_id=1, source_target_pairs={{0,1},{1,0},{2,3},{3,2},{4,5},{5,4},{6,7},{7,6},{8,9},{9,8},{10,11... | collective-permute-start | bytes 12582920 | tf_op jit(solution)/shard_map/ppermute | solution.py:413
  9.3 8.4 %collective-permute-start.1 = (bf16[1024,512]{1,0:T(8,128)(2,1)}, bf16[1024,512]{1,0:T(8,128)(2,1)}, u32[]{:S(2)}, u32[]{:S(2)}) collective-permute-start(bf16[1024,512]{1,0:T(8,128)(2,1)} %join_rows.2.refs_1_), channel_id=1, source_target_pairs={{0,1},{1,0},{2,3},{3,2},{4,5},{5,4},{6,7},{7,6},{8,9},{9,8},{10,11... | collective-permute-start | bytes 3145736 | tf_op jit(solution)/shard_map/ppermute | solution.py:413
  9.4 13.7 %collective-permute-start.2 = (bf16[256,512]{1,0:T(8,128)(2,1)S(1)}, bf16[256,512]{1,0:T(8,128)(2,1)S(1)}, u32[]{:S(2)}, u32[]{:S(2)}) collective-permute-start(bf16[256,512]{1,0:T(8,128)(2,1)S(1)} %copy-done.6), channel_id=1, source_target_pairs={{2,0},{3,1},{0,2},{1,3},{6,4},{7,5},{4,6},{5,7},{10,8},{11,9},{8,1... | collective-permute-start | bytes 786440 | tf_op jit(solution)/shard_map/ppermute | solution.py:414
  15.6 9.2 %collective-permute-start.5 = (bf16[512,256]{1,0:T(8,128)(2,1)S(1)}, bf16[512,256]{1,0:T(8,128)(2,1)S(1)}, u32[]{:S(2)}, u32[]{:S(2)}) collective-permute-start(bf16[512,256]{1,0:T(8,128)(2,1)S(1)} %get-tuple-element.71.refs_2_), channel_id=1, source_target_pairs={{0,4},{4,0},{8,12},{12,8},{16,20},{20,16},{24,28},{28,24},{1,5},{5... | collective-permute-start | bytes 786440 | tf_op jit(solution)/shard_map/ppermute | solution.py:418
  17.2 8.2 %collective-permute-start.4 = (bf16[256,512]{1,0:T(8,128)(2,1)S(1)}, bf16[256,512]{1,0:T(8,128)(2,1)S(1)}, u32[]{:S(2)}, u32[]{:S(2)}) collective-permute-start(bf16[256,512]{1,0:T(8,128)(2,1)S(1)} %copy-done.12), channel_id=1, source_target_pairs={{2,0},{3,1},{0,2},{1,3},{6,4},{7,5},{4,6},{5,7},{10,8},{11,9},{8,1... | collective-permute-start | bytes 786440 | tf_op jit(solution)/shard_map/ppermute | solution.py:414
  23.2 9.4 %collective-permute-start.7 = (bf16[256,512]{1,0:T(8,128)(2,1)}, bf16[256,512]{1,0:T(8,128)(2,1)S(1)}, u32[]{:S(2)}, u32[]{:S(2)}) collective-permute-start(bf16[256,512]{1,0:T(8,128)(2,1)} %get-tuple-element.64.refs_2_.refs_6_), channel_id=1, source_target_pairs={{2,0},{3,1},{0,2},{1,3},{6,4},{7,5},{4,6},{5,7},{10,8},{11,9},{8,1... | collective-permute-start | bytes 786440 | tf_op jit(solution)/shard_map/ppermute | solution.py:414
  25.4 7.2 %collective-permute-start.6 = (bf16[256,512]{1,0:T(8,128)(2,1)S(1)}, bf16[256,512]{1,0:T(8,128)(2,1)S(1)}, u32[]{:S(2)}, u32[]{:S(2)}) collective-permute-start(bf16[256,512]{1,0:T(8,128)(2,1)S(1)} %relay_rows.9), channel_id=1, source_target_pairs={{0,1},{1,0},{2,3},{3,2},{4,5},{5,4},{6,7},{7,6},{8,9},{9,8},{10,11... | collective-permute-start | bytes 786440 | tf_op jit(solution)/shard_map/ppermute | solution.py:413
  25.7 9.5 %collective-permute-start.11 = (bf16[512,256]{1,0:T(8,128)(2,1)S(1)}, bf16[512,256]{1,0:T(8,128)(2,1)S(1)}, u32[]{:S(2)}, u32[]{:S(2)}) collective-permute-start(bf16[512,256]{1,0:T(8,128)(2,1)S(1)} %add_halves.3.refs_2_.refs_1_), channel_id=1, source_target_pairs={{0,8},{4,12},{8,0},{12,4},{16,24},{20,28},{24,16},{28,20},{1,9},{5... | collective-permute-start | bytes 786440 | tf_op jit(solution)/shard_map/ppermute | solution.py:418
  27.3 10.5 %collective-permute-start.9 = (bf16[256,512]{1,0:T(8,128)(2,1)S(1)}, bf16[256,512]{1,0:T(8,128)(2,1)S(1)}, u32[]{:S(2)}, u32[]{:S(2)}) collective-permute-start(bf16[256,512]{1,0:T(8,128)(2,1)S(1)} %copy-done.9), channel_id=1, source_target_pairs={{2,0},{3,1},{0,2},{1,3},{6,4},{7,5},{4,6},{5,7},{10,8},{11,9},{8,1... | collective-permute-start | bytes 786440 | tf_op jit(solution)/shard_map/ppermute | solution.py:414
  32.6 9.3 %collective-permute-start.8 = (bf16[256,512]{1,0:T(8,128)(2,1)S(1)}, bf16[256,512]{1,0:T(8,128)(2,1)S(1)}, u32[]{:S(2)}, u32[]{:S(2)}) collective-permute-start(bf16[256,512]{1,0:T(8,128)(2,1)S(1)} %relay_rows.10), channel_id=1, source_target_pairs={{0,1},{1,0},{2,3},{3,2},{4,5},{5,4},{6,7},{7,6},{8,9},{9,8},{10,11... | collective-permute-start | bytes 786440 | tf_op jit(solution)/shard_map/ppermute | solution.py:413
  37.9 27.2 %collective-permute-start.14 = (bf16[512,256]{1,0:T(8,128)(2,1)S(1)}, bf16[512,256]{1,0:T(8,128)(2,1)S(1)}, u32[]{:S(2)}, u32[]{:S(2)}) collective-permute-start(bf16[512,256]{1,0:T(8,128)(2,1)S(1)} %add_halves.4.refs_2_.refs_1_), channel_id=1, source_target_pairs={{0,16},{4,20},{8,24},{12,28},{16,0},{20,4},{24,8},{28,12},{1,17},{... | collective-permute-start | bytes 786440 | tf_op jit(solution)/shard_map/ppermute | solution.py:418
  65.7 8.4 %collective-permute-start.15 = (bf16[512,256]{1,0:T(8,128)(2,1)S(1)}, bf16[512,256]{1,0:T(8,128)(2,1)S(1)}, u32[]{:S(2)}, u32[]{:S(2)}) collective-permute-start(bf16[512,256]{1,0:T(8,128)(2,1)S(1)} %add_halves.5.refs_4_), channel_id=1, source_target_pairs={{0,4},{4,0},{8,12},{12,8},{16,20},{20,16},{24,28},{28,24},{1,5},{5... | collective-permute-start | bytes 786440 | tf_op jit(solution)/shard_map/ppermute | solution.py:418
  66.8 10.5 %collective-permute-start.18 = (bf16[256,512]{1,0:T(8,128)(2,1)S(1)}, bf16[256,512]{1,0:T(8,128)(2,1)S(1)}, u32[]{:S(2)}, u32[]{:S(2)}) collective-permute-start(bf16[256,512]{1,0:T(8,128)(2,1)S(1)} %grad_rows.19.refs_7_), channel_id=1, source_target_pairs={{0,2},{1,3},{2,0},{3,1},{4,6},{5,7},{6,4},{7,5},{8,10},{9,11},{10,... | collective-permute-start | bytes 786440 | tf_op jit(solution)/shard_map/ppermute | solution.py:416
  67.9 13.8 %collective-permute-start.17 = (bf16[256,512]{1,0:T(8,128)(2,1)S(1)}, bf16[256,512]{1,0:T(8,128)(2,1)S(1)}, u32[]{:S(2)}, u32[]{:S(2)}) collective-permute-start(bf16[256,512]{1,0:T(8,128)(2,1)S(1)} %grad_rows.18.refs_7_), channel_id=1, source_target_pairs={{0,2},{1,3},{2,0},{3,1},{4,6},{5,7},{6,4},{7,5},{8,10},{9,11},{10,... | collective-permute-start | bytes 786440 | tf_op jit(solution)/shard_map/ppermute | solution.py:416
  68.9 18.4 %collective-permute-start.16 = (bf16[256,512]{1,0:T(8,128)(2,1)S(1)}, bf16[256,512]{1,0:T(8,128)(2,1)S(1)}, u32[]{:S(2)}, u32[]{:S(2)}) collective-permute-start(bf16[256,512]{1,0:T(8,128)(2,1)S(1)} %grad_rows.17.refs_7_), channel_id=1, source_target_pairs={{0,2},{1,3},{2,0},{3,1},{4,6},{5,7},{6,4},{7,5},{8,10},{9,11},{10,... | collective-permute-start | bytes 786440 | tf_op jit(solution)/shard_map/ppermute | solution.py:416
  69.9 21.9 %collective-permute-start.13 = (bf16[256,512]{1,0:T(8,128)(2,1)S(1)}, bf16[256,512]{1,0:T(8,128)(2,1)S(1)}, u32[]{:S(2)}, u32[]{:S(2)}) collective-permute-start(bf16[256,512]{1,0:T(8,128)(2,1)S(1)} %grad_rows.16.refs_7_), channel_id=1, source_target_pairs={{0,2},{1,3},{2,0},{3,1},{4,6},{5,7},{6,4},{7,5},{8,10},{9,11},{10,... | collective-permute-start | bytes 786440 | tf_op jit(solution)/shard_map/ppermute | solution.py:416
  93.0 9.2 %collective-permute-start.20 = (bf16[256,512]{1,0:T(8,128)(2,1)S(1)}, bf16[256,512]{1,0:T(8,128)(2,1)S(1)}, u32[]{:S(2)}, u32[]{:S(2)}) collective-permute-start(bf16[256,512]{1,0:T(8,128)(2,1)S(1)} %get-tuple-element.80.refs_0_.refs_6_), channel_id=1, source_target_pairs={{2,0},{3,1},{0,2},{1,3},{6,4},{7,5},{4,6},{5,7},{10,8},{11,9},{8,1... | collective-permute-start | bytes 786440 | tf_op jit(solution)/shard_map/ppermute | solution.py:414
  94.1 13.7 %collective-permute-start.22 = (bf16[256,512]{1,0:T(8,128)(2,1)S(1)}, bf16[256,512]{1,0:T(8,128)(2,1)S(1)}, u32[]{:S(2)}, u32[]{:S(2)}) collective-permute-start(bf16[256,512]{1,0:T(8,128)(2,1)S(1)} %get-tuple-element.81.refs_1_.refs_6_), channel_id=1, source_target_pairs={{2,0},{3,1},{0,2},{1,3},{6,4},{7,5},{4,6},{5,7},{10,8},{11,9},{8,1... | collective-permute-start | bytes 786440 | tf_op jit(solution)/shard_map/ppermute | solution.py:414
  102.2 11.1 %collective-permute-start.24 = (bf16[256,512]{1,0:T(8,128)(2,1)S(1)}, bf16[256,512]{1,0:T(8,128)(2,1)S(1)}, u32[]{:S(2)}, u32[]{:S(2)}) collective-permute-start(bf16[256,512]{1,0:T(8,128)(2,1)S(1)} %get-tuple-element.82.refs_2_.refs_6_), channel_id=1, source_target_pairs={{2,0},{3,1},{0,2},{1,3},{6,4},{7,5},{4,6},{5,7},{10,8},{11,9},{8,1... | collective-permute-start | bytes 786440 | tf_op jit(solution)/shard_map/ppermute | solution.py:414
  107.9 10.7 %collective-permute-start.26 = (bf16[256,512]{1,0:T(8,128)(2,1)S(1)}, bf16[256,512]{1,0:T(8,128)(2,1)S(1)}, u32[]{:S(2)}, u32[]{:S(2)}) collective-permute-start(bf16[256,512]{1,0:T(8,128)(2,1)S(1)} %get-tuple-element.83.refs_3_.refs_6_), channel_id=1, source_target_pairs={{2,0},{3,1},{0,2},{1,3},{6,4},{7,5},{4,6},{5,7},{10,8},{11,9},{8,1... | collective-permute-start | bytes 786440 | tf_op jit(solution)/shard_map/ppermute | solution.py:414
  126.9 19.0 %collective-permute-start.31 = (bf16[256,512]{1,0:T(8,128)(2,1)S(1)}, bf16[256,512]{1,0:T(8,128)(2,1)S(1)}, u32[]{:S(2)}, u32[]{:S(2)}) collective-permute-start(bf16[256,512]{1,0:T(8,128)(2,1)S(1)} %grad_rows.24.refs_7_), channel_id=1, source_target_pairs={{0,2},{1,3},{2,0},{3,1},{4,6},{5,7},{6,4},{7,5},{8,10},{9,11},{10,... | collective-permute-start | bytes 786440 | tf_op jit(solution)/shard_map/ppermute | solution.py:416
  130.1 17.9 %collective-permute-start.30 = (bf16[256,512]{1,0:T(8,128)(2,1)S(1)}, bf16[256,512]{1,0:T(8,128)(2,1)S(1)}, u32[]{:S(2)}, u32[]{:S(2)}) collective-permute-start(bf16[256,512]{1,0:T(8,128)(2,1)S(1)} %grad_rows.25.refs_7_), channel_id=1, source_target_pairs={{0,2},{1,3},{2,0},{3,1},{4,6},{5,7},{6,4},{7,5},{8,10},{9,11},{10,... | collective-permute-start | bytes 786440 | tf_op jit(solution)/shard_map/ppermute | solution.py:416
  133.2 16.8 %collective-permute-start.29 = (bf16[256,512]{1,0:T(8,128)(2,1)S(1)}, bf16[256,512]{1,0:T(8,128)(2,1)S(1)}, u32[]{:S(2)}, u32[]{:S(2)}) collective-permute-start(bf16[256,512]{1,0:T(8,128)(2,1)S(1)} %grad_rows.26.refs_7_), channel_id=1, source_target_pairs={{0,2},{1,3},{2,0},{3,1},{4,6},{5,7},{6,4},{7,5},{8,10},{9,11},{10,... | collective-permute-start | bytes 786440 | tf_op jit(solution)/shard_map/ppermute | solution.py:416
  136.4 16.1 %collective-permute-start.28 = (bf16[256,512]{1,0:T(8,128)(2,1)S(1)}, bf16[256,512]{1,0:T(8,128)(2,1)S(1)}, u32[]{:S(2)}, u32[]{:S(2)}) collective-permute-start(bf16[256,512]{1,0:T(8,128)(2,1)S(1)} %grad_rows.27.refs_7_), channel_id=1, source_target_pairs={{0,2},{1,3},{2,0},{3,1},{4,6},{5,7},{6,4},{7,5},{8,10},{9,11},{10,... | collective-permute-start | bytes 786440 | tf_op jit(solution)/shard_map/ppermute | solution.py:416
  (23 other events, 117.2 us)

commit v4 on v3

v4 whole, which is shorter than its diff:
```python
import functools
import math

import jax
import jax.numpy as jnp
from jax import lax
from jax.experimental import pallas as pl
from jax.experimental.pallas import tpu as pltpu
from jax.sharding import PartitionSpec as P

INNER = 2

inner_rate = 0.003
beta_one = 0.9
beta_two = 0.95
adam_eps = 1e-08
decay_rate = 0.1
outer_rate = 0.7
outer_mu = 0.9
mix_share = 0.5

bf16 = jnp.bfloat16
f32 = jnp.float32
VMEM_LIMIT = 16 * 1024 * 1024


def token_weight(kinds):
    return jnp.where(kinds == 2, 1.0, jnp.where(kinds == 1, 0.25, 0.0)).astype(f32)


def dot(a, b):
    return jnp.dot(a, b, preferred_element_type=f32)


def dot_rows(a, b):
    return lax.dot_general(a, b, (((0,), (0,)), ((), ())), preferred_element_type=f32)


def once(shape, index):
    return pl.BlockSpec(shape, index, pipeline_mode=pl.Buffered(1))


def whole(shape):
    return once(shape, lambda *_: (0,) * len(shape))


def sds(shape, dtype):
    return jax.ShapeDtypeStruct(shape, dtype)


def call(body, name, meta, ins, outs, grid=(1,), scratch=(), aliases=None, flops=0, after=()):
    arrays = [a for a, _ in ins] + list(after)
    n_in = len(meta) + len(ins)
    moved = sum(math.prod(o.shape) * o.dtype.itemsize for o, _ in outs)
    moved += sum(math.prod(s.block_shape or a.shape) * a.dtype.itemsize for a, s in ins)

    def run(*refs):
        body(*refs[:n_in], *refs[n_in + len(after):])

    return pl.pallas_call(
        run,
        name=name,
        out_shape=[o for o, _ in outs],
        grid_spec=pltpu.PrefetchScalarGridSpec(
            num_scalar_prefetch=len(meta),
            grid=grid,
            in_specs=[s for _, s in ins] + [pl.BlockSpec(memory_space=pl.ANY)] * len(after),
            out_specs=[s for _, s in outs],
            scratch_shapes=list(scratch),
        ),
        input_output_aliases=aliases or {},
        compiler_params=pltpu.CompilerParams(vmem_limit_bytes=VMEM_LIMIT),
        cost_estimate=pl.CostEstimate(flops=flops, bytes_accessed=moved, transcendentals=0),
    )(*meta, *arrays)


def plan_sum(plan):
    total = plan[0]
    for r in range(1, plan.shape[0]):
        total = total + plan[r]
    return total


def fragment(plan):
    return lax.rem(plan_sum(plan), 2)


def cast_body(theta, low):
    width = theta.shape[3]
    for k in range(2):
        low[:, k * width:(k + 1) * width] = theta[0, k].astype(bf16)


def cast_rows(weights):
    _, _, rows, width = weights.shape
    return call(
        cast_body, "cast_rows", (), [(weights, whole(weights.shape))],
        [(sds((rows, 2 * width), bf16), whole((rows, 2 * width)))],
    )[0]


def weigh_body(own, other, out):
    for h, kinds in enumerate((own, other)):
        lanes = kinds.shape[0]
        pad = jnp.zeros((8 - lanes % 8, 128), f32)
        value = token_weight(kinds[...])
        if lanes % 8:
            value = jnp.concatenate([value, pad], 0)
        turned = value.T
        for j in range(lanes):
            out[h, j * 128:(j + 1) * 128, :] = turned[:, j:j + 1]


def copy_body(x, out):
    out[...] = x[...]


def relay(x, after):
    return call(copy_body, "relay_rows", (), [(x, whole(x.shape))], [(sds(x.shape, x.dtype), whole(x.shape))], after=after)[0]


def turn_body(pos, x, xt):
    xt[...] = x[...].T


def turn(pos, x, chips, rows):
    tokens = x.shape[0]
    tile = min(256, tokens)
    return call(
        turn_body, "turn_tokens", (pos,),
        [(x, pl.BlockSpec((tile, rows), lambda s, t, m: (t, m[1 + s])))],
        [(sds((chips * rows, tokens), bf16), pl.BlockSpec((rows, tile), lambda s, t, m: (s, t)))],
        grid=(chips, tokens // tile),
    )[0]


def forward_body(count, tile, first_call, pos, *refs):
    if first_call:
        acc_in = gram_in = None
    else:
        acc_in, gram_in, refs = refs[0], refs[1], refs[2:]
    lows = refs[:count]
    xs = (refs[count:2 * count], refs[2 * count:3 * count])
    acc, gram = refs[3 * count:]
    width = gram.shape[0]
    step = pl.program_id(0)
    at = pl.ds(pl.multiple_of(step * tile, tile), tile)

    @pl.when(step == 0)
    def _():
        total = None if first_call else gram_in[...]
        for p in range(count):
            dec = lows[p][:, width:]
            term = dot_rows(dec, dec)
            total = term if total is None else total + term
        gram[...] = total

    for h in range(2):
        value = None if first_call else acc_in[h, at, :]
        for p in range(count):
            term = dot(xs[h][p][...], lows[p][...])
            value = term if value is None else value + term
        acc[h, at, :] = value


def column(slot):
    return lambda g, m: (g, m[slot])


def token_blocks(x, tile, pieces):
    return [(x, pl.BlockSpec((tile, low.shape[0]), column(slot))) for low, slot in pieces]


def forward(pos, acc, gram, pieces, xs, after=()):
    tokens = xs[0].shape[0]
    tile = min(128, tokens)
    wide = pieces[0][0].shape[1]
    width = wide // 2
    ins = []
    if acc is not None:
        ins += [(acc, whole(acc.shape)), (gram, whole(gram.shape))]
    ins += [(low, whole(low.shape)) for low, _ in pieces]
    for x in xs:
        ins += token_blocks(x, tile, pieces)
    return call(
        functools.partial(forward_body, len(pieces), tile, acc is None), "forward_rows", (pos,), ins,
        [(sds((2, tokens, wide), f32), whole((2, tokens, wide))), (sds((width, width), f32), whole((width, width)))],
        grid=(tokens // tile,), after=after,
    )


def finish_body(scale, tile, count, steps, pos, acc_in, gram_in, cw, *refs):
    lows = refs[:count]
    xs = (refs[count:2 * count], refs[2 * count:3 * count])
    slopes, w_hi, w_lo, w_acc, g_hi, g_lo = refs[3 * count:]
    width = gram_in.shape[0]
    step = pl.program_id(0)
    at = pl.ds(pl.multiple_of(step * tile, tile), tile)

    @pl.when(step == 0)
    def _():
        gram = gram_in[...]
        for p in range(count):
            dec = lows[p][:, width:]
            gram = gram + dot_rows(dec, dec)
        hi = gram.astype(bf16)
        g_hi[...] = hi
        g_lo[...] = (gram - hi.astype(f32)).astype(bf16)
        w_acc[...] = jnp.zeros_like(w_acc)

    total = w_acc[...]
    for h in range(2):
        value = acc_in[h, at, :]
        for p in range(count):
            value = value + dot(xs[h][p][...], lows[p][...])
        pre = value[:, :width]
        sig = 0.5 + 0.5 * jnp.tanh(0.5 * pre)
        hidden = (pre * sig).astype(bf16)
        back = dot(hidden, g_hi[...]) + dot(hidden, g_lo[...]) - value[:, width:]
        weight = cw[h, at, :]
        slope = (weight * scale) * back * (sig * (1.0 + pre * (1.0 - sig)))
        counted = (weight * hidden.astype(f32)).astype(bf16)
        slopes[h, at, :width] = slope.astype(bf16)
        slopes[h, at, width:] = counted
        total = total + dot_rows(counted, hidden)
    w_acc[...] = total

    @pl.when(step == steps - 1)
    def _():
        hi = total.astype(bf16)
        w_hi[...] = hi
        w_lo[...] = (total - hi.astype(f32)).astype(bf16)


def finish(pos, acc, gram, cw, pieces, xs, scale):
    tokens = xs[0].shape[0]
    tile = min(256, tokens)
    wide = pieces[0][0].shape[1]
    width = wide // 2
    ins = [(a, whole(a.shape)) for a in [acc, gram, cw] + [low for low, _ in pieces]]
    for x in xs:
        ins += token_blocks(x, tile, pieces)
    square = (sds((width, width), bf16), whole((width, width)))
    return call(
        functools.partial(finish_body, scale, tile, len(pieces), tokens // tile), "finish_slopes", (pos,), ins,
        [(sds((2, tokens, wide), bf16), whole((2, tokens, wide))), square, square],
        grid=(tokens // tile,),
        scratch=[pltpu.VMEM((width, width), f32)] + [pltpu.VMEM((width, width), bf16)] * 2,
    )


def grad_body(scale, off, xt_own, xt_par, slopes, w_hi, w_lo, low, out):
    width = w_hi.shape[0]
    both = dot(xt_own[...], slopes[0]) + dot(xt_par[...], slopes[1])
    dec = low[off:off + out.shape[0], width:]
    grad_dec = scale * (dot(dec, w_hi[...]) + dot(dec, w_lo[...]) - both[:, width:])
    out[:, :width] = both[:, :width].astype(out.dtype)
    out[:, width:] = grad_dec.astype(out.dtype)


def grad_rows(scale, s, i, cr, xt, slopes, w_hi, w_lo, low, dtype, after=()):
    tokens = xt[0].shape[1]
    rows, wide = low.shape
    block = s * (rows // cr) + i
    ins = [(x, once((cr, tokens), lambda g: (block, 0))) for x in xt]
    ins += [(a, whole(a.shape)) for a in (slopes, w_hi, w_lo, low)]
    return call(
        functools.partial(grad_body, scale, i * cr), "grad_rows", (), ins,
        [(sds((cr, wide), dtype), whole((cr, wide)))], after=after,
    )[0]


def adam_body(last, count, plan, own, *refs):
    got = refs[:count]
    theta, first, second = refs[count:3 + count]
    anchor = refs[3 + count]
    theta_out, first_out, second_out = refs[-3:]
    width = own.shape[1] // 2
    for k in range(2):
        grad = own[:, k * width:(k + 1) * width]
        for g in got:
            grad = grad + g[:, k * width:(k + 1) * width].astype(f32)
        one = beta_one * first[0, k] + (1.0 - beta_one) * grad
        two = beta_two * second[0, k] + (1.0 - beta_two) * grad * grad
        old = theta[0, k]
        if last:
            old = mixed(plan, k, old, anchor[...])
        theta_out[0, k] = old - inner_rate * (one / (jnp.sqrt(two) + adam_eps) + decay_rate * old)
        first_out[0, k] = one
        second_out[0, k] = two


def mixed(plan, k, theta, anchor):
    return jnp.where(fragment(plan) == k, mix_share * theta + (1.0 - mix_share) * anchor, theta)


def adam_rows(plan, i, cr, own, got, state, state_block, new_anc, prev, full):
    width = own.shape[1] // 2
    last = new_anc is not None
    block = (1, 2, cr, width)
    ins = [(g, whole(g.shape)) for g in [own] + got]
    ins += [(s, once(block, lambda g, m: (0, 0, state_block, 0))) for s in state]
    aliases = {}
    if last:
        ins.append((new_anc, once((cr, width), lambda g, m: (i, 0))))
        if prev is not None:
            for n, p in enumerate(prev):
                aliases[1 + len(ins)] = n
                ins.append((p, pl.BlockSpec(memory_space=pl.ANY)))
        outs = [(sds(full, f32), once(block, lambda g, m: (0, 0, i, 0)))] * 3
    else:
        outs = [(sds(block, f32), whole(block))] * 3
    return call(
        functools.partial(adam_body, last, len(got)), "adam_rows", (plan,), ins, outs, aliases=aliases,
    )


def quarter(pos, m, size):
    where = jnp.bitwise_xor(lax.rem(pos[0], 4), m)
    return pl.ds(pl.multiple_of(where * size, size), size)


def delta_body(pos, plan, anchor, theta, *outs):
    count = plan[pos[0]].astype(f32)
    for m, out in enumerate(outs):
        at = quarter(pos, m, out.shape[0])
        out[...] = (count * (anchor[0, at, :] - theta[0, 0, at, :])).astype(out.dtype)


def outer_start(pos, plan, anchor, weights, after):
    _, rows, width = anchor.shape
    part = (rows // 4, width)
    return call(
        delta_body, "delta_quarters", (pos, plan),
        [
            (anchor, once((1, rows, width), lambda g, p, q: (fragment(q), 0, 0))),
            (weights, once((1, 1, rows, width), lambda g, p, q: (0, fragment(q), 0, 0))),
        ],
        [(sds(part, f32), whole(part))] + [(sds(part, bf16), whole(part))] * 3, after=after,
    )


def add_body(final, plan, *refs):
    total = refs[0][...].astype(f32)
    for r in refs[1:-1]:
        total = total + r[...].astype(f32)
    if final:
        total = total / plan_sum(plan).astype(f32)
    refs[-1][...] = total.astype(bf16)


def outer_add(plan, parts, final):
    shape = parts[0].shape
    return call(
        functools.partial(add_body, final), "add_quarters", (plan,), [(a, whole(shape)) for a in parts],
        [(sds(shape, bf16), whole(shape))],
    )[0]


def outer_update(frag, at, anchor, momentum, grad):
    mom = outer_mu * momentum[frag, at, :] + grad
    return anchor[frag, at, :] - outer_rate * (grad + outer_mu * mom), mom


def mix_body(count, pos, plan, anchor, momentum, *refs):
    quarters, thetas = refs[:4], refs[4:4 + count]
    new_anc, low = refs[-2:]
    frag = fragment(plan)
    for m, piece in enumerate(quarters):
        at = quarter(pos, m, piece.shape[0])
        new_anc[at, :] = outer_update(frag, at, anchor, momentum, piece[...].astype(f32))[0]
    cr, width = thetas[0].shape[2:]
    for i, theta in enumerate(thetas):
        for k in range(2):
            value = mixed(plan, k, theta[0, k], new_anc[i * cr:(i + 1) * cr, :])
            low[i * cr:(i + 1) * cr, k * width:(k + 1) * width] = value.astype(bf16)


def outer_mix(pos, plan, anchor, momentum, quarters, thetas):
    _, rows, width = anchor.shape
    return call(
        functools.partial(mix_body, len(thetas)), "mix_rows", (pos, plan),
        [(a, whole(a.shape)) for a in [anchor, momentum] + quarters + thetas],
        [(sds((rows, width), f32), whole((rows, width))), (sds((rows, 2 * width), bf16), whole((rows, 2 * width)))],
    )


def outer_body(pos, plan, anchor, momentum, *refs):
    quarters = refs[:4]
    anchor_out, momentum_out = refs[4:]
    frag = fragment(plan)
    anchor_out[...] = anchor[...]
    momentum_out[...] = momentum[...]
    for m, piece in enumerate(quarters):
        at = quarter(pos, m, piece.shape[0])
        anc, mom = outer_update(frag, at, anchor, momentum, piece[...].astype(f32))
        anchor_out[frag, at, :] = anc
        momentum_out[frag, at, :] = mom


def outer_end(pos, plan, anchor, momentum, quarters, after):
    return call(
        outer_body, "outer_step", (pos, plan),
        [(a, whole(a.shape)) for a in [anchor, momentum] + quarters],
        [(sds(anchor.shape, f32), whole(anchor.shape))] * 2, after=after,
    )


def local(n_rep, n_fsdp, inputs, kinds, weights, first_moment, second_moment, anchor, momentum, plan):
    tokens = inputs.shape[0]
    rows, width = weights.shape[2:]
    chips = n_fsdp // 2
    scale = 1.0 / math.sqrt(tokens * n_fsdp)
    chunks = max(1, min(4, rows // 256))
    cr = rows // chunks

    partner = [(f, f ^ 1) for f in range(n_fsdp)]
    to_partner = lambda a: lax.ppermute(a, "fsdp", partner)
    fetch = lambda a, s: lax.ppermute(
        a, "fsdp", [(((f // 2 + s) % chips) * 2 + f % 2, f) for f in range(n_fsdp)])
    give = lambda a, s: lax.ppermute(
        a, "fsdp", [(f, ((f // 2 + s) % chips) * 2 + f % 2) for f in range(n_fsdp)])
    across = lambda a, bit: lax.ppermute(a, "replica", [(r, r ^ bit) for r in range(n_rep)])

    blocks = [(i * cr, cr) for i in range(chunks)]
    low_own = cast_rows(weights)

    chip = lax.axis_index("fsdp") // 2
    core = lax.axis_index("fsdp") % 2
    at = [((chip + s) % chips) * 2 for s in range(chips)]
    pos = jnp.stack([lax.axis_index("replica")] + [a + core for a in at] + [a + 1 - core for a in at]).astype(jnp.int32)

    x_par = to_partner(inputs)
    xs = (inputs, x_par)
    lanes = kinds.reshape(-1, 128)
    cw = call(
        weigh_body, "weigh_tokens", (),
        [(lanes, whole(lanes.shape)), (to_partner(lanes), whole(lanes.shape))],
        [(sds((2, tokens, 1), f32), whole((2, tokens, 1)))], after=[low_own],
    )[0]

    parts = outer_start(pos, plan, anchor, weights, [low_own])
    own = outer_add(plan, [parts[0]] + [across(parts[m], m) for m in range(1, 4)], n_rep == 4)
    bit = 4
    while bit < n_rep:
        own = outer_add(plan, [own, across(own, bit)], 2 * bit == n_rep)
        bit *= 2
    xt = [turn(pos, x, chips, rows) for x in xs]

    ready = [cw, own] + xt
    state = [(weights, first_moment, second_moment)] * chunks
    state_block = list(range(chunks))
    new_anc = None
    for step in range(INNER):
        last = step == INNER - 1
        low_far = {s: fetch(low_own, s) for s in range(1, chips)}
        near = [(low_own, 1), (to_partner(low_own), 1 + chips)]
        acc, gram = forward(pos, None, None, near, xs)
        far = [(low_far[s], 1 + s) for s in low_far]
        handed = [(to_partner(relay(low, [acc] + ready)), slot + chips) for low, slot in far]
        acc, gram = forward(pos, acc, gram, far, xs)
        slopes, w_hi, w_lo = finish(pos, acc, gram, cw, handed, xs, scale)

        mine, got, sent = [], [], []
        for i in range(chunks):
            now = []
            for s in low_far:
                now.append(grad_rows(
                    scale, s, i, cr, xt, slopes, w_hi, w_lo, low_far[s], bf16, after=sent[-1:]))
                sent.append(now[-1])
            got.append([give(g, s) for s, g in zip(low_far, now)])
        for i in range(chunks):
            mine.append(grad_rows(
                scale, 0, i, cr, xt, slopes, w_hi, w_lo, low_own, f32, after=(sent + mine)[-1:]))

        new_state, prev = [], None
        for i in range(chunks):
            res = adam_rows(
                plan, i, cr, mine[i], got[i], state[i], state_block[i], new_anc, prev, weights.shape)
            if last:
                prev = res
            else:
                new_state.append(tuple(res))
        if not last:
            quarters = [own] + [across(own, m) for m in range(1, 4)]
            new_anc, low_own = outer_mix(pos, plan, anchor, momentum, quarters, [t for t, _, _ in new_state])
            anchor_out, momentum_out = outer_end(pos, plan, anchor, momentum, quarters, [low_own])
            ready = [anchor_out]
            state, state_block = new_state, [0] * chunks
    return (*prev, anchor_out, momentum_out)


def solution(mesh):
    return jax.shard_map(
        functools.partial(local, mesh.shape["replica"], mesh.shape["fsdp"]),
        mesh=mesh,
        in_specs=(
            P(("replica", "fsdp"), None),
            P(("replica", "fsdp")),
            P("replica", None, "fsdp", None),
            P("replica", None, "fsdp", None),
            P("replica", None, "fsdp", None),
            P(None, "fsdp", None),
            P(None, "fsdp", None),
            P(),
        ),
        out_specs=(
            P("replica", None, "fsdp", None),
            P("replica", None, "fsdp", None),
            P("replica", None, "fsdp", None),
            P(None, "fsdp", None),
            P(None, "fsdp", None),
        ),
        check_vma=False,
    )
```

time: 156 us -> 146 us (0.936)
  Pallas kernels: 91.2 us -> 69.1 us
  waiting for transfers between devices: 30.6 us -> 43.7 us
    pallas_call x52 -> x41, Pallas kernels: 91.2 us -> 69.1 us  [call(): pl.pallas_call(run, name=name, out_shape=[o for o, _ in outs], grid_spec=...]
    ppermute x8, waiting for transfers between devices: 11.8 us -> 20.7 us  [local(): lax.ppermute(a, 'fsdp', [(f, (f // 2 + s) % chips * 2 + f % 2) for f in r...]
    ppermute x8 -> x2, starting transfers between devices: 10 us -> 4.79 us  [local(): lax.ppermute(a, 'fsdp', [((f // 2 + s) % chips * 2 + f % 2, f) for f in r...]
    ppermute x4 -> x7, starting transfers between devices: 6.87 us -> 12.1 us  [local(): lax.ppermute(a, 'replica', [(r, r ^ bit) for r in range(n_rep)])]
    ppermute x4 -> x7, waiting for transfers between devices: 3.3 us -> 8.22 us  [local(): lax.ppermute(a, 'replica', [(r, r ^ bit) for r in range(n_rep)])]
    ppermute x8 -> x2, waiting for transfers between devices: 14 us -> 14.8 us  [local(): lax.ppermute(a, 'fsdp', [((f // 2 + s) % chips * 2 + f % 2, f) for f in r...]
    unnamed x30 -> x22, local copies, waits for them, and re-layouts: 4.65 us -> 4.91 us
  transfers between devices with their start and end apart: 32 -> 23, of which waited for: 13 -> 11; matrix products, arithmetic and copies ran while one was open for 0% -> 0% of each run, Pallas kernels for 53% -> 34%
where the time goes in v4:
time: 146 us
  Pallas kernels  69.1 us (47%)
  waiting for transfers between devices  43.7 us (30%)
  starting transfers between devices  26.8 us (18%)
  local copies, waits for them, and re-layouts  4.99 us (3%)
    pallas_call x41, Pallas kernels, call(): pl.pallas_call(run, name=name, out_shape=[o for o, _ in outs], grid_spec=...  69.1 us
    ppermute x8, waiting for transfers between devices, local(): lax.ppermute(a, 'fsdp', [(f, (f // 2 + s) % chips * 2 + f % 2) for f in r...  20.7 us
    ppermute x2, waiting for transfers between devices, local(): lax.ppermute(a, 'fsdp', [((f // 2 + s) % chips * 2 + f % 2, f) for f in r...  14.8 us
    ppermute x7, starting transfers between devices, local(): lax.ppermute(a, 'replica', [(r, r ^ bit) for r in range(n_rep)])  12.1 us
    ppermute x8, starting transfers between devices, local(): lax.ppermute(a, 'fsdp', [(f, (f // 2 + s) % chips * 2 + f % 2) for f in r...  9.1 us
    ppermute x7, waiting for transfers between devices, local(): lax.ppermute(a, 'replica', [(r, r ^ bit) for r in range(n_rep)])  8.22 us
    unnamed x22, local copies, waits for them, and re-layouts  4.91 us
    ppermute x2, starting transfers between devices, local(): lax.ppermute(a, 'fsdp', [((f // 2 + s) % chips * 2 + f % 2, f) for f in r...  4.79 us
  transfers between devices with their start and end apart: 23, of which 11 were waited for; matrix products, arithmetic and copies ran while one was open for 0% of the time, Pallas kernels for 34%

profile of v4, /device:TPU:0, one launch (start us, length us, event | category | flops | bytes accessed | tf_op | source)
XLA Modules:
  0.0 145.6 jit_solution(9323930551682030669)
XLA Ops:
  3.0 3.0 %collective-permute-start.9 = (bf16[1024,512]{1,0:T(8,128)(2,1)S(1)}, bf16[1024,512]{1,0:T(8,128)(2,1)}, u32[]{:S(2)}, u32[]{:S(2)}) collective-permute-start(bf16[1024,512]{1,0:T(8,128)(2,1)S(1)} %cast_rows.1.refs_4_.refs_1_.refs_2_.refs_5_), channel_id=1, source_target_pairs={{2,0},{3,1},{0,2},{1,3},{6,4},{7,5},{4,6},{5,7},{10,8},{11,9},{8,1... | collective-permute-start | bytes 3145736 | tf_op jit(solution)/shard_map/ppermute | solution.py:419
  13.6 2.5 %collective-permute-start.3 = (bf16[256,256]{1,0:T(8,128)(2,1)S(1)}, bf16[256,256]{1,0:T(8,128)(2,1)S(1)}, u32[]{:S(2)}, u32[]{:S(2)}) collective-permute-start(bf16[256,256]{1,0:T(8,128)(2,1)S(1)} %get-tuple-element.54), channel_id=1, source_target_pairs={{0,12},{4,8},{8,4},{12,0},{16,28},{20,24},{24,20},{28,16},{1,13},{... | collective-permute-start | bytes 393224 | tf_op jit(solution)/shard_map/ppermute | solution.py:423
  16.1 3.4 %collective-permute-done.3.refs_4_ = bf16[256,256]{1,0:T(8,128)(2,1)S(1)} collective-permute-done((bf16[256,256]{1,0:T(8,128)(2,1)S(1)}, bf16[256,256]{1,0:T(8,128)(2,1)S(1)}, u32[]{:S(2)}, u32[]{:S(2)}) %collective-permute-start.3) | collective-permute-done | bytes 131104 | tf_op jit(solution)/shard_map/ppermute | solution.py:423
  20.1 2.7 %collective-permute-start.4 = (bf16[256,256]{1,0:T(8,128)(2,1)S(1)}, bf16[256,256]{1,0:T(8,128)(2,1)S(1)}, u32[]{:S(2)}, u32[]{:S(2)}) collective-permute-start(bf16[256,256]{1,0:T(8,128)(2,1)S(1)} %add_quarters.2.refs_1_), channel_id=1, source_target_pairs={{0,16},{4,20},{8,24},{12,28},{16,0},{20,4},{24,8},{28,12},{1,17},{... | collective-permute-start | bytes 393224 | tf_op jit(solution)/shard_map/ppermute | solution.py:423
  24.7 2.7 %collective-permute-done.4.refs_2_ = bf16[256,256]{1,0:T(8,128)(2,1)S(1)} collective-permute-done((bf16[256,256]{1,0:T(8,128)(2,1)S(1)}, bf16[256,256]{1,0:T(8,128)(2,1)S(1)}, u32[]{:S(2)}, u32[]{:S(2)}) %collective-permute-start.4) | collective-permute-done | bytes 131104 | tf_op jit(solution)/shard_map/ppermute | solution.py:423
  28.0 3.4 %turn_tokens.3.refs_5_.refs_1_ = bf16[2048,512]{1,0:T(8,128)(2,1)S(1)} custom-call(s32[5]{0:T(128)S(1)} %stack.23.refs_0_, bf16[512,4096]{1,0:T(8,128)(2,1)} %collective-permute-done.refs_1_.refs_5_.refs_6_), custom_call_target="tpu_custom_call" | custom-call | bytes 2621440 | tf_op jit(solution)/shard_map/turn_tokens/pallas_call | solution.py:60
  31.5 5.9 %forward_rows.4 = (f32[2,512,512]{2,1,0:T(8,128)S(1)}, f32[256,256]{1,0:T(8,128)S(1)}) custom-call(s32[5]{0:T(128)S(1)} %stack.23.refs_0_, bf16[1024,512]{1,0:T(8,128)(2,1)S(1)} %cast_rows.1.refs_4_.refs_1_.refs_2_.refs_5_, bf16[1024,512]{1,0:T(8,128)(2,1)} %collective-permute-done.8.refs_2_, bf16[512,4096]{1,0:T(8,128)(2,1)S(1)} %copy-done, ...), custom_call_target="tpu_custom_call" | custom-call | bytes 5505024 | tf_op jit(solution)/shard_map/forward_rows/pallas_call | solution.py:60
  38.8 4.7 %forward_rows.5 = (f32[2,512,512]{2,1,0:T(8,128)S(1)}, f32[256,256]{1,0:T(8,128)S(1)}) custom-call(s32[5]{0:T(128)S(1)} %stack.23.refs_0_, f32[2,512,512]{2,1,0:T(8,128)S(1)} %get-tuple-element.55.refs_1_, f32[256,256]{1,0:T(8,128)S(1)} %get-tuple-element.56.refs_2_, bf16[1024,512]{1,0:T(8,128)(2,1)} %collective-permute-done.9.refs_3_.refs_0_.refs_5_, ...), custom_call_target="tpu_custom_call" | custom-call | bytes 6291456 | tf_op jit(solution)/shard_map/forward_rows/pallas_call | solution.py:60
  43.5 4.7 %finish_slopes.2 = (bf16[2,512,512]{2,1,0:T(8,128)(2,1)S(1)}, bf16[256,256]{1,0:T(8,128)(2,1)S(1)}, bf16[256,256]{1,0:T(8,128)(2,1)S(1)}) custom-call(s32[5]{0:T(128)S(1)} %stack.23.refs_0_, f32[2,512,512]{2,1,0:T(8,128)S(1)} %get-tuple-element.57.refs_1_, f32[256,256]{1,0:T(8,128)S(1)} %get-tuple-element.58.refs_2_, ...), custom_call_target="tpu_custom_call" | custom-call | bytes 5771264 | tf_op jit(solution)/shard_map/finish_slopes/pallas_call | solution.py:60
  53.4 2.6 %collective-permute-start.14 = (bf16[256,512]{1,0:T(8,128)(2,1)S(1)}, bf16[256,512]{1,0:T(8,128)(2,1)S(1)}, u32[]{:S(2)}, u32[]{:S(2)}) collective-permute-start(bf16[256,512]{1,0:T(8,128)(2,1)S(1)} %grad_rows.18.refs_6_), channel_id=1, source_target_pairs={{0,2},{1,3},{2,0},{3,1},{4,6},{5,7},{6,4},{7,5},{8,10},{9,11},{10,... | collective-permute-start | bytes 786440 | tf_op jit(solution)/shard_map/ppermute | solution.py:421
  63.9 4.9 %collective-permute-done.13.refs_2_ = bf16[256,512]{1,0:T(8,128)(2,1)S(1)} collective-permute-done((bf16[256,512]{1,0:T(8,128)(2,1)S(1)}, bf16[256,512]{1,0:T(8,128)(2,1)S(1)}, u32[]{:S(2)}, u32[]{:S(2)}) %collective-permute-start.13) | collective-permute-done | bytes 262176 | tf_op jit(solution)/shard_map/ppermute | solution.py:421
  77.0 2.9 %collective-permute-done.15.refs_2_ = bf16[256,512]{1,0:T(8,128)(2,1)S(1)} collective-permute-done((bf16[256,512]{1,0:T(8,128)(2,1)S(1)}, bf16[256,512]{1,0:T(8,128)(2,1)S(1)}, u32[]{:S(2)}, u32[]{:S(2)}) %collective-permute-start.15) | collective-permute-done | bytes 262176 | tf_op jit(solution)/shard_map/ppermute | solution.py:421
  84.3 3.1 %outer_step.1 = (f32[2,1024,256]{2,1,0:T(8,128)}, f32[2,1024,256]{2,1,0:T(8,128)}) custom-call(s32[5]{0:T(128)S(1)} %stack.23.refs_0_, s32[8]{0:T(128)S(1)} %copy-done.9, f32[2,1024,256]{2,1,0:T(8,128)S(1)} %copy-done.6, f32[2,1024,256]{2,1,0:T(8,128)S(1)} %copy-done.7, bf16[256,256]{1,0:T(8,128)(2,1)S(1)} %add_quarters.3.refs_3_.refs_4_, ...), custom_call_target="tpu_custom_call" | custom-call | bytes 8912896 | tf_op jit(solution)/shard_map/outer_step/pallas_call | solution.py:60
  87.4 5.9 %forward_rows.6 = (f32[2,512,512]{2,1,0:T(8,128)S(1)}, f32[256,256]{1,0:T(8,128)S(1)}) custom-call(s32[5]{0:T(128)S(1)} %stack.23.refs_0_, bf16[1024,512]{1,0:T(8,128)(2,1)S(1)} %get-tuple-element.66.refs_1_.refs_8_.refs_5_, bf16[1024,512]{1,0:T(8,128)(2,1)S(1)} %collective-permute-done.16.refs_2_, bf16[512,4096]{1,0:T(8,128)(2,1)S(1)} %copy-done, ...), custom_call_target="tpu_custom_call" | custom-call | bytes 5505024 | tf_op jit(solution)/shard_map/forward_rows/pallas_call | solution.py:60
  93.3 14.8 %collective-permute-done.17.refs_3_.refs_0_.refs_5_ = bf16[1024,512]{1,0:T(8,128)(2,1)S(1)} collective-permute-done((bf16[1024,512]{1,0:T(8,128)(2,1)S(1)}, bf16[1024,512]{1,0:T(8,128)(2,1)S(1)}, u32[]{:S(2)}, u32[]{:S(2)}) %collective-permute-start.17) | collective-permute-done | bytes 1048608 | tf_op jit(solution)/shard_map/ppermute | solution.py:419
  108.2 4.4 %forward_rows.7 = (f32[2,512,512]{2,1,0:T(8,128)S(1)}, f32[256,256]{1,0:T(8,128)S(1)}) custom-call(s32[5]{0:T(128)S(1)} %stack.23.refs_0_, f32[2,512,512]{2,1,0:T(8,128)S(1)} %get-tuple-element.67.refs_1_, f32[256,256]{1,0:T(8,128)S(1)} %get-tuple-element.68.refs_2_, bf16[1024,512]{1,0:T(8,128)(2,1)S(1)} %collective-permute-done.17.refs_3_.refs_0_.refs_5_, ...), custom_call_target="tpu_custom_call" | custom-call | bytes 6291456 | tf_op jit(solution)/shard_map/forward_rows/pallas_call | solution.py:60
  112.6 4.7 %finish_slopes.3 = (bf16[2,512,512]{2,1,0:T(8,128)(2,1)S(1)}, bf16[256,256]{1,0:T(8,128)(2,1)S(1)}, bf16[256,256]{1,0:T(8,128)(2,1)S(1)}) custom-call(s32[5]{0:T(128)S(1)} %stack.23.refs_0_, f32[2,512,512]{2,1,0:T(8,128)S(1)} %get-tuple-element.69.refs_1_, f32[256,256]{1,0:T(8,128)S(1)} %get-tuple-element.70.refs_2_, ...), custom_call_target="tpu_custom_call" | custom-call | bytes 5771264 | tf_op jit(solution)/shard_map/finish_slopes/pallas_call | solution.py:60
  127.0 2.1 %adam_rows.12 = (f32[1,2,1024,256]{3,2,1,0:T(8,128)}, f32[1,2,1024,256]{3,2,1,0:T(8,128)}, f32[1,2,1024,256]{3,2,1,0:T(8,128)}) custom-call(s32[8]{0:T(128)S(1)} %copy-done.9, f32[256,512]{1,0:T(8,128)S(1)} %grad_rows.28.refs_6_.refs_1_, bf16[256,512]{1,0:T(8,128)(2,1)S(1)} %collective-permute-done.22.refs_2_, ...), custom_call_target="tpu_custom_call" | custom-call | bytes 8912896 | tf_op jit(solution)/shard_map/adam_rows/pallas_call | solution.py:60
  129.2 3.5 %collective-permute-done.21.refs_2_ = bf16[256,512]{1,0:T(8,128)(2,1)S(1)} collective-permute-done((bf16[256,512]{1,0:T(8,128)(2,1)S(1)}, bf16[256,512]{1,0:T(8,128)(2,1)S(1)}, u32[]{:S(2)}, u32[]{:S(2)}) %collective-permute-start.21) | collective-permute-done | bytes 262176 | tf_op jit(solution)/shard_map/ppermute | solution.py:421
  132.6 2.1 %adam_rows.13 = (f32[1,2,1024,256]{3,2,1,0:T(8,128)}, f32[1,2,1024,256]{3,2,1,0:T(8,128)}, f32[1,2,1024,256]{3,2,1,0:T(8,128)}) custom-call(s32[8]{0:T(128)S(1)} %copy-done.9, f32[256,512]{1,0:T(8,128)S(1)} %grad_rows.29.refs_6_.refs_1_, ...), custom_call_target="tpu_custom_call", output_to_operand_aliasing={{0}: (7, {}), {1}: (8, {}), {2}: (9, {})} | custom-call | bytes 15204352 | tf_op jit(solution)/shard_map/adam_rows/pallas_call | solution.py:60
  134.8 3.5 %collective-permute-done.20.refs_2_ = bf16[256,512]{1,0:T(8,128)(2,1)S(1)} collective-permute-done((bf16[256,512]{1,0:T(8,128)(2,1)S(1)}, bf16[256,512]{1,0:T(8,128)(2,1)S(1)}, u32[]{:S(2)}, u32[]{:S(2)}) %collective-permute-start.20) | collective-permute-done | bytes 262176 | tf_op jit(solution)/shard_map/ppermute | solution.py:421
  138.2 2.2 %adam_rows.14 = (f32[1,2,1024,256]{3,2,1,0:T(8,128)}, f32[1,2,1024,256]{3,2,1,0:T(8,128)}, f32[1,2,1024,256]{3,2,1,0:T(8,128)}) custom-call(s32[8]{0:T(128)S(1)} %copy-done.9, f32[256,512]{1,0:T(8,128)S(1)} %grad_rows.30.refs_6_.refs_1_, ...), custom_call_target="tpu_custom_call", output_to_operand_aliasing={{0}: (7, {}), {1}: (8, {}), {2}: (9, {})} | custom-call | bytes 15204352 | tf_op jit(solution)/shard_map/adam_rows/pallas_call | solution.py:60
  140.4 3.1 %collective-permute-done.19.refs_2_ = bf16[256,512]{1,0:T(8,128)(2,1)S(1)} collective-permute-done((bf16[256,512]{1,0:T(8,128)(2,1)S(1)}, bf16[256,512]{1,0:T(8,128)(2,1)S(1)}, u32[]{:S(2)}, u32[]{:S(2)}) %collective-permute-start.19) | collective-permute-done | bytes 262176 | tf_op jit(solution)/shard_map/ppermute | solution.py:421
  143.5 2.1 %adam_rows.15 = (f32[1,2,1024,256]{3,2,1,0:T(8,128)}, f32[1,2,1024,256]{3,2,1,0:T(8,128)}, f32[1,2,1024,256]{3,2,1,0:T(8,128)}) custom-call(s32[8]{0:T(128)S(1)} %copy-done.9, f32[256,512]{1,0:T(8,128)S(1)} %grad_rows.31.refs_1_, bf16[256,512]{1,0:T(8,128)(2,1)S(1)} %collective-permute-done.19.refs_2_, ...), custom_call_target="tpu_custom_call", output_to_operand_aliasing={{0}: (7, {}), {1}: (8, {}), {2}: (9, {})} | custom-call | bytes 15204352 | tf_op jit(solution)/shard_map/adam_rows/pallas_call | solution.py:60
  (86 shorter events, 49.8 us)
Async XLA Ops:
  0.6 27.4 %collective-permute-start = (bf16[512,4096]{1,0:T(8,128)(2,1)}, bf16[512,4096]{1,0:T(8,128)(2,1)}, u32[]{:S(2)}, u32[]{:S(2)}) collective-permute-start(bf16[512,4096]{1,0:T(8,128)(2,1)} %refs_5_.11), channel_id=1, source_target_pairs={{0,1},{1,0},{2,3},{3,2},{4,5},{5,4},{6,7},{7,6},{8,9},{9,8},{10,11... | collective-permute-start | bytes 12582920 | tf_op jit(solution)/shard_map/ppermute | solution.py:418
  2.9 28.6 %collective-permute-start.8 = (bf16[1024,512]{1,0:T(8,128)(2,1)S(1)}, bf16[1024,512]{1,0:T(8,128)(2,1)}, u32[]{:S(2)}, u32[]{:S(2)}) collective-permute-start(bf16[1024,512]{1,0:T(8,128)(2,1)S(1)} %cast_rows.1.refs_4_.refs_1_.refs_2_.refs_5_), channel_id=1, source_target_pairs={{0,1},{1,0},{2,3},{3,2},{4,5},{5,4},{6,7},{7,6},{8,9},{9,8},{10,11... | collective-permute-start | bytes 3145736 | tf_op jit(solution)/shard_map/ppermute | solution.py:418
  3.0 34.4 %collective-permute-start.9 = (bf16[1024,512]{1,0:T(8,128)(2,1)S(1)}, bf16[1024,512]{1,0:T(8,128)(2,1)}, u32[]{:S(2)}, u32[]{:S(2)}) collective-permute-start(bf16[1024,512]{1,0:T(8,128)(2,1)S(1)} %cast_rows.1.refs_4_.refs_1_.refs_2_.refs_5_), channel_id=1, source_target_pairs={{2,0},{3,1},{0,2},{1,3},{6,4},{7,5},{4,6},{5,7},{10,8},{11,9},{8,1... | collective-permute-start | bytes 3145736 | tf_op jit(solution)/shard_map/ppermute | solution.py:419
  8.4 5.3 %collective-permute-start.1 = (bf16[256,256]{1,0:T(8,128)(2,1)S(1)}, bf16[256,256]{1,0:T(8,128)(2,1)S(1)}, u32[]{:S(2)}, u32[]{:S(2)}) collective-permute-start(bf16[256,256]{1,0:T(8,128)(2,1)S(1)} %get-tuple-element.52), channel_id=1, source_target_pairs={{0,4},{4,0},{8,12},{12,8},{16,20},{20,16},{24,28},{28,24},{1,5},{5... | collective-permute-start | bytes 393224 | tf_op jit(solution)/shard_map/ppermute | solution.py:423
  9.9 6.2 %collective-permute-start.2 = (bf16[256,256]{1,0:T(8,128)(2,1)S(1)}, bf16[256,256]{1,0:T(8,128)(2,1)S(1)}, u32[]{:S(2)}, u32[]{:S(2)}) collective-permute-start(bf16[256,256]{1,0:T(8,128)(2,1)S(1)} %get-tuple-element.53), channel_id=1, source_target_pairs={{0,8},{4,12},{8,0},{12,4},{16,24},{20,28},{24,16},{28,20},{1,9},{5... | collective-permute-start | bytes 393224 | tf_op jit(solution)/shard_map/ppermute | solution.py:423
  13.6 5.9 %collective-permute-start.3 = (bf16[256,256]{1,0:T(8,128)(2,1)S(1)}, bf16[256,256]{1,0:T(8,128)(2,1)S(1)}, u32[]{:S(2)}, u32[]{:S(2)}) collective-permute-start(bf16[256,256]{1,0:T(8,128)(2,1)S(1)} %get-tuple-element.54), channel_id=1, source_target_pairs={{0,12},{4,8},{8,4},{12,0},{16,28},{20,24},{24,20},{28,16},{1,13},{... | collective-permute-start | bytes 393224 | tf_op jit(solution)/shard_map/ppermute | solution.py:423
  20.1 7.3 %collective-permute-start.4 = (bf16[256,256]{1,0:T(8,128)(2,1)S(1)}, bf16[256,256]{1,0:T(8,128)(2,1)S(1)}, u32[]{:S(2)}, u32[]{:S(2)}) collective-permute-start(bf16[256,256]{1,0:T(8,128)(2,1)S(1)} %add_quarters.2.refs_1_), channel_id=1, source_target_pairs={{0,16},{4,20},{8,24},{12,28},{16,0},{20,4},{24,8},{28,12},{1,17},{... | collective-permute-start | bytes 393224 | tf_op jit(solution)/shard_map/ppermute | solution.py:423
  22.8 1.7 %collective-permute-start.10 = (s32[4,128]{1,0:T(4,128)S(1)}, s32[4,128]{1,0:T(4,128)S(1)}, u32[]{:S(2)}, u32[]{:S(2)}) collective-permute-start(s32[4,128]{1,0:T(4,128)S(1)} %bitcast.6), channel_id=1, source_target_pairs={{0,1},{1,0},{2,3},{3,2},{4,5},{5,4},{6,7},{7,6},{8,9},{9,8},{10,11... | collective-permute-start | bytes 6152 | tf_op jit(solution)/shard_map/ppermute | solution.py:418
  38.7 4.8 %collective-permute-start.11 = (bf16[1024,512]{1,0:T(8,128)(2,1)S(1)}, bf16[1024,512]{1,0:T(8,128)(2,1)S(1)}, u32[]{:S(2)}, u32[]{:S(2)}) collective-permute-start(bf16[1024,512]{1,0:T(8,128)(2,1)S(1)} %relay_rows.2), channel_id=1, source_target_pairs={{0,1},{1,0},{2,3},{3,2},{4,5},{5,4},{6,7},{7,6},{8,9},{9,8},{10,11... | collective-permute-start | bytes 3145736 | tf_op jit(solution)/shard_map/ppermute | solution.py:418
  53.4 9.8 %collective-permute-start.14 = (bf16[256,512]{1,0:T(8,128)(2,1)S(1)}, bf16[256,512]{1,0:T(8,128)(2,1)S(1)}, u32[]{:S(2)}, u32[]{:S(2)}) collective-permute-start(bf16[256,512]{1,0:T(8,128)(2,1)S(1)} %grad_rows.18.refs_6_), channel_id=1, source_target_pairs={{0,2},{1,3},{2,0},{3,1},{4,6},{5,7},{6,4},{7,5},{8,10},{9,11},{10,... | collective-permute-start | bytes 786440 | tf_op jit(solution)/shard_map/ppermute | solution.py:421
  56.0 12.8 %collective-permute-start.13 = (bf16[256,512]{1,0:T(8,128)(2,1)S(1)}, bf16[256,512]{1,0:T(8,128)(2,1)S(1)}, u32[]{:S(2)}, u32[]{:S(2)}) collective-permute-start(bf16[256,512]{1,0:T(8,128)(2,1)S(1)} %grad_rows.17.refs_6_), channel_id=1, source_target_pairs={{0,2},{1,3},{2,0},{3,1},{4,6},{5,7},{6,4},{7,5},{8,10},{9,11},{10,... | collective-permute-start | bytes 786440 | tf_op jit(solution)/shard_map/ppermute | solution.py:421
  56.1 19.9 %collective-permute-start.12 = (bf16[256,512]{1,0:T(8,128)(2,1)S(1)}, bf16[256,512]{1,0:T(8,128)(2,1)S(1)}, u32[]{:S(2)}, u32[]{:S(2)}) collective-permute-start(bf16[256,512]{1,0:T(8,128)(2,1)S(1)} %grad_rows.16.refs_6_), channel_id=1, source_target_pairs={{0,2},{1,3},{2,0},{3,1},{4,6},{5,7},{6,4},{7,5},{8,10},{9,11},{10,... | collective-permute-start | bytes 786440 | tf_op jit(solution)/shard_map/ppermute | solution.py:421
  59.8 20.1 %collective-permute-start.15 = (bf16[256,512]{1,0:T(8,128)(2,1)S(1)}, bf16[256,512]{1,0:T(8,128)(2,1)S(1)}, u32[]{:S(2)}, u32[]{:S(2)}) collective-permute-start(bf16[256,512]{1,0:T(8,128)(2,1)S(1)} %grad_rows.19.refs_6_), channel_id=1, source_target_pairs={{0,2},{1,3},{2,0},{3,1},{4,6},{5,7},{6,4},{7,5},{8,10},{9,11},{10,... | collective-permute-start | bytes 786440 | tf_op jit(solution)/shard_map/ppermute | solution.py:421
  60.0 20.9 %collective-permute-start.7 = (bf16[256,256]{1,0:T(8,128)(2,1)S(1)}, bf16[256,256]{1,0:T(8,128)(2,1)S(1)}, u32[]{:S(2)}, u32[]{:S(2)}) collective-permute-start(bf16[256,256]{1,0:T(8,128)(2,1)S(1)} %add_quarters.3.refs_3_.refs_4_), channel_id=1, source_target_pairs={{0,12},{4,8},{8,4},{12,0},{16,28},{20,24},{24,20},{28,16},{1,13},{... | collective-permute-start | bytes 393224 | tf_op jit(solution)/shard_map/ppermute | solution.py:423
  63.2 17.6 %collective-permute-start.6 = (bf16[256,256]{1,0:T(8,128)(2,1)S(1)}, bf16[256,256]{1,0:T(8,128)(2,1)S(1)}, u32[]{:S(2)}, u32[]{:S(2)}) collective-permute-start(bf16[256,256]{1,0:T(8,128)(2,1)S(1)} %add_quarters.3.refs_3_.refs_4_), channel_id=1, source_target_pairs={{0,8},{4,12},{8,0},{12,4},{16,24},{20,28},{24,16},{28,20},{1,9},{5... | collective-permute-start | bytes 393224 | tf_op jit(solution)/shard_map/ppermute | solution.py:423
  68.8 12.0 %collective-permute-start.5 = (bf16[256,256]{1,0:T(8,128)(2,1)S(1)}, bf16[256,256]{1,0:T(8,128)(2,1)S(1)}, u32[]{:S(2)}, u32[]{:S(2)}) collective-permute-start(bf16[256,256]{1,0:T(8,128)(2,1)S(1)} %add_quarters.3.refs_3_.refs_4_), channel_id=1, source_target_pairs={{0,4},{4,0},{8,12},{12,8},{16,20},{20,16},{24,28},{28,24},{1,5},{5... | collective-permute-start | bytes 393224 | tf_op jit(solution)/shard_map/ppermute | solution.py:423
  82.4 5.0 %collective-permute-start.16 = (bf16[1024,512]{1,0:T(8,128)(2,1)S(1)}, bf16[1024,512]{1,0:T(8,128)(2,1)S(1)}, u32[]{:S(2)}, u32[]{:S(2)}) collective-permute-start(bf16[1024,512]{1,0:T(8,128)(2,1)S(1)} %get-tuple-element.66.refs_1_.refs_8_.refs_5_), channel_id=1, source_target_pairs={{0,1},{1,0},{2,3},{3,2},{4,5},{5,4},{6,7},{7,6},{8,9},{9,8},{10,11... | collective-permute-start | bytes 3145736 | tf_op jit(solution)/shard_map/ppermute | solution.py:418
  82.5 25.6 %collective-permute-start.17 = (bf16[1024,512]{1,0:T(8,128)(2,1)S(1)}, bf16[1024,512]{1,0:T(8,128)(2,1)S(1)}, u32[]{:S(2)}, u32[]{:S(2)}) collective-permute-start(bf16[1024,512]{1,0:T(8,128)(2,1)S(1)} %get-tuple-element.66.refs_1_.refs_8_.refs_5_), channel_id=1, source_target_pairs={{2,0},{3,1},{0,2},{1,3},{6,4},{7,5},{4,6},{5,7},{10,8},{11,9},{8,1... | collective-permute-start | bytes 3145736 | tf_op jit(solution)/shard_map/ppermute | solution.py:419
  87.4 20.7 %copy-start.8 = (f32[2,1024,256]{2,1,0:T(8,128)S(1)}, f32[2,1024,256]{2,1,0:T(8,128)}, u32[]{:S(2)}) copy-start(f32[2,1024,256]{2,1,0:T(8,128)} %get-tuple-element.49.refs_2_) | copy-start | bytes 6291460
  108.1 4.5 %collective-permute-start.18 = (bf16[1024,512]{1,0:T(8,128)(2,1)S(1)}, bf16[1024,512]{1,0:T(8,128)(2,1)S(1)}, u32[]{:S(2)}, u32[]{:S(2)}) collective-permute-start(bf16[1024,512]{1,0:T(8,128)(2,1)S(1)} %relay_rows.3), channel_id=1, source_target_pairs={{0,1},{1,0},{2,3},{3,2},{4,5},{5,4},{6,7},{7,6},{8,9},{9,8},{10,11... | collective-permute-start | bytes 3145736 | tf_op jit(solution)/shard_map/ppermute | solution.py:418
  117.8 9.2 %collective-permute-start.22 = (bf16[256,512]{1,0:T(8,128)(2,1)S(1)}, bf16[256,512]{1,0:T(8,128)(2,1)S(1)}, u32[]{:S(2)}, u32[]{:S(2)}) collective-permute-start(bf16[256,512]{1,0:T(8,128)(2,1)S(1)} %grad_rows.24.refs_6_), channel_id=1, source_target_pairs={{0,2},{1,3},{2,0},{3,1},{4,6},{5,7},{6,4},{7,5},{8,10},{9,11},{10,... | collective-permute-start | bytes 786440 | tf_op jit(solution)/shard_map/ppermute | solution.py:421
  120.2 12.5 %collective-permute-start.21 = (bf16[256,512]{1,0:T(8,128)(2,1)S(1)}, bf16[256,512]{1,0:T(8,128)(2,1)S(1)}, u32[]{:S(2)}, u32[]{:S(2)}) collective-permute-start(bf16[256,512]{1,0:T(8,128)(2,1)S(1)} %grad_rows.25.refs_6_), channel_id=1, source_target_pairs={{0,2},{1,3},{2,0},{3,1},{4,6},{5,7},{6,4},{7,5},{8,10},{9,11},{10,... | collective-permute-start | bytes 786440 | tf_op jit(solution)/shard_map/ppermute | solution.py:421
  121.0 17.2 %collective-permute-start.20 = (bf16[256,512]{1,0:T(8,128)(2,1)S(1)}, bf16[256,512]{1,0:T(8,128)(2,1)S(1)}, u32[]{:S(2)}, u32[]{:S(2)}) collective-permute-start(bf16[256,512]{1,0:T(8,128)(2,1)S(1)} %grad_rows.26.refs_6_), channel_id=1, source_target_pairs={{0,2},{1,3},{2,0},{3,1},{4,6},{5,7},{6,4},{7,5},{8,10},{9,11},{10,... | collective-permute-start | bytes 786440 | tf_op jit(solution)/shard_map/ppermute | solution.py:421
  123.4 20.1 %collective-permute-start.19 = (bf16[256,512]{1,0:T(8,128)(2,1)S(1)}, bf16[256,512]{1,0:T(8,128)(2,1)S(1)}, u32[]{:S(2)}, u32[]{:S(2)}) collective-permute-start(bf16[256,512]{1,0:T(8,128)(2,1)S(1)} %grad_rows.27.refs_6_), channel_id=1, source_target_pairs={{0,2},{1,3},{2,0},{3,1},{4,6},{5,7},{6,4},{7,5},{8,10},{9,11},{10,... | collective-permute-start | bytes 786440 | tf_op jit(solution)/shard_map/ppermute | solution.py:421
  (10 other events, 51.6 us)

commit v5 on v4

--- a/solution.py
+++ b/solution.py
@@ -21,7 +21,7 @@
 
 bf16 = jnp.bfloat16
 f32 = jnp.float32
-VMEM_LIMIT = 16 * 1024 * 1024
+VMEM_LIMIT = 12 * 1024 * 1024
 
 
 def token_weight(kinds):
@@ -85,18 +85,21 @@
     return lax.rem(plan_sum(plan), 2)
 
 
-def cast_body(theta, low):
-    width = theta.shape[3]
-    for k in range(2):
-        low[:, k * width:(k + 1) * width] = theta[0, k].astype(bf16)
-
-
-def cast_rows(weights):
+def cast_body(theta, *lows):
+    sub, wide = lows[0].shape
+    width = wide // 2
+    for j, low in enumerate(lows):
+        for k in range(2):
+            low[:, k * width:(k + 1) * width] = theta[0, k, j * sub:(j + 1) * sub, :].astype(bf16)
+
+
+def cast_rows(weights, parts):
     _, _, rows, width = weights.shape
+    shape = (rows // parts, 2 * width)
     return call(
         cast_body, "cast_rows", (), [(weights, whole(weights.shape))],
-        [(sds((rows, 2 * width), bf16), whole((rows, 2 * width)))],
-    )[0]
+        [(sds(shape, bf16), whole(shape))] * parts,
+    )
 
 
 def weigh_body(own, other, out):
@@ -134,118 +137,119 @@
     )[0]
 
 
-def forward_body(count, tile, first_call, pos, *refs):
+def forward_body(offs, first_call, pos, *refs):
+    count = len(offs)
     if first_call:
         acc_in = gram_in = None
     else:
         acc_in, gram_in, refs = refs[0], refs[1], refs[2:]
-    lows = refs[:count]
-    xs = (refs[count:2 * count], refs[2 * count:3 * count])
-    acc, gram = refs[3 * count:]
+    lows, xs = refs[:count], refs[count:count + 2]
+    acc, gram = refs[count + 2:]
     width = gram.shape[0]
-    step = pl.program_id(0)
-    at = pl.ds(pl.multiple_of(step * tile, tile), tile)
-
-    @pl.when(step == 0)
-    def _():
-        total = None if first_call else gram_in[...]
-        for p in range(count):
-            dec = lows[p][:, width:]
-            term = dot_rows(dec, dec)
-            total = term if total is None else total + term
-        gram[...] = total
-
-    for h in range(2):
-        value = None if first_call else acc_in[h, at, :]
-        for p in range(count):
-            term = dot(xs[h][p][...], lows[p][...])
-            value = term if value is None else value + term
-        acc[h, at, :] = value
-
-
-def column(slot):
-    return lambda g, m: (g, m[slot])
-
-
-def token_blocks(x, tile, pieces):
-    return [(x, pl.BlockSpec((tile, low.shape[0]), column(slot))) for low, slot in pieces]
-
-
-def forward(pos, acc, gram, pieces, xs, after=()):
+
+    def step(n):
+        low = lows[n][pl.ds(offs[n], xs[0].shape[1]), :]
+        term = dot_rows(low[:, width:], low[:, width:])
+        prods = [dot(x[...], low) for x in xs]
+        if n > 0:
+            gram[...] += term
+            for h in range(2):
+                acc[h] += prods[h]
+        elif first_call:
+            gram[...] = term
+            for h in range(2):
+                acc[h] = prods[h]
+        else:
+            gram[...] = gram_in[...] + term
+            for h in range(2):
+                acc[h] = acc_in[h] + prods[h]
+
+    for n in range(count):
+        pl.when(pl.program_id(0) == n)(functools.partial(step, n))
+
+
+def token_blocks(xs, pieces, sub):
+
+    def column(g, m):
+        at = 0
+        for n, (_, _, slot, part) in enumerate(pieces):
+            per = xs[0].shape[1] // (m.shape[0] - 1) // sub
+            at = jnp.where(g == n, m[slot] * per + part, at)
+        return (0, at)
+
+    return [(x, pl.BlockSpec((x.shape[0], sub), column)) for x in xs]
+
+
+def forward(pos, acc, gram, pieces, xs, sub, after=()):
     tokens = xs[0].shape[0]
-    tile = min(128, tokens)
     wide = pieces[0][0].shape[1]
     width = wide // 2
     ins = []
     if acc is not None:
         ins += [(acc, whole(acc.shape)), (gram, whole(gram.shape))]
-    ins += [(low, whole(low.shape)) for low, _ in pieces]
-    for x in xs:
-        ins += token_blocks(x, tile, pieces)
-    return call(
-        functools.partial(forward_body, len(pieces), tile, acc is None), "forward_rows", (pos,), ins,
+    ins += [(low, whole(low.shape)) for low, _, _, _ in pieces]
+    return call(
+        functools.partial(forward_body, [off for _, off, _, _ in pieces], acc is None), "forward_rows", (pos,),
+        ins + token_blocks(xs, pieces, sub),
         [(sds((2, tokens, wide), f32), whole((2, tokens, wide))), (sds((width, width), f32), whole((width, width)))],
-        grid=(tokens // tile,), after=after,
-    )
-
-
-def finish_body(scale, tile, count, steps, pos, acc_in, gram_in, cw, *refs):
-    lows = refs[:count]
-    xs = (refs[count:2 * count], refs[2 * count:3 * count])
-    slopes, w_hi, w_lo, w_acc, g_hi, g_lo = refs[3 * count:]
+        grid=(len(pieces),), after=after,
+    )
+
+
+def finish_body(scale, tile, offs, pos, acc_in, gram_in, cw, *refs):
+    count = len(offs)
+    lows, xs = refs[:count], refs[count:count + 2]
+    slopes, w_hi, w_lo, acc, gram = refs[count + 2:]
     width = gram_in.shape[0]
-    step = pl.program_id(0)
-    at = pl.ds(pl.multiple_of(step * tile, tile), tile)
-
-    @pl.when(step == 0)
+
+    def step(n):
+        low = lows[n][pl.ds(offs[n], xs[0].shape[1]), :]
+        term = dot_rows(low[:, width:], low[:, width:])
+        before = (acc_in, gram_in) if n == 0 else (acc, gram)
+        gram[...] = before[1][...] + term
+        for h in range(2):
+            acc[h] = before[0][h] + dot(xs[h][...], low)
+
+    for n in range(count):
+        pl.when(pl.program_id(0) == n)(functools.partial(step, n))
+
+    @pl.when(pl.program_id(0) == count - 1)
     def _():
-        gram = gram_in[...]
-        for p in range(count):
-            dec = lows[p][:, width:]
-            gram = gram + dot_rows(dec, dec)
-        hi = gram.astype(bf16)
-        g_hi[...] = hi
-        g_lo[...] = (gram - hi.astype(f32)).astype(bf16)
-        w_acc[...] = jnp.zeros_like(w_acc)
-
-    total = w_acc[...]
-    for h in range(2):
-        value = acc_in[h, at, :]
-        for p in range(count):
-            value = value + dot(xs[h][p][...], lows[p][...])
-        pre = value[:, :width]
-        sig = 0.5 + 0.5 * jnp.tanh(0.5 * pre)
-        hidden = (pre * sig).astype(bf16)
-        back = dot(hidden, g_hi[...]) + dot(hidden, g_lo[...]) - value[:, width:]
-        weight = cw[h, at, :]
-        slope = (weight * scale) * back * (sig * (1.0 + pre * (1.0 - sig)))
-        counted = (weight * hidden.astype(f32)).astype(bf16)
-        slopes[h, at, :width] = slope.astype(bf16)
-        slopes[h, at, width:] = counted
-        total = total + dot_rows(counted, hidden)
-    w_acc[...] = total
-
-    @pl.when(step == steps - 1)
-    def _():
+        g_all = gram[...]
+        g_hi = g_all.astype(bf16)
+        g_lo = (g_all - g_hi.astype(f32)).astype(bf16)
+        total = None
+        for h in range(2):
+            for t in range(0, acc.shape[1], tile):
+                at = pl.ds(t, tile)
+                pre = acc[h, at, :width]
+                sig = 0.5 + 0.5 * jnp.tanh(0.5 * pre)
+                hidden = (pre * sig).astype(bf16)
+                back = dot(hidden, g_hi) + dot(hidden, g_lo) - acc[h, at, width:]
+                weight = cw[h, at, :]
+                slope = (weight * scale) * back * (sig * (1.0 + pre * (1.0 - sig)))
+                counted = (weight * hidden.astype(f32)).astype(bf16)
+                slopes[h, at, :width] = slope.astype(bf16)
+                slopes[h, at, width:] = counted
+                term = dot_rows(counted, hidden)
+                total = term if total is None else total + term
         hi = total.astype(bf16)
         w_hi[...] = hi
         w_lo[...] = (total - hi.astype(f32)).astype(bf16)
 
 
-def finish(pos, acc, gram, cw, pieces, xs, scale):
+def finish(pos, acc, gram, cw, pieces, xs, sub, scale):
     tokens = xs[0].shape[0]
-    tile = min(256, tokens)
     wide = pieces[0][0].shape[1]
     width = wide // 2
-    ins = [(a, whole(a.shape)) for a in [acc, gram, cw] + [low for low, _ in pieces]]
-    for x in xs:
-        ins += token_blocks(x, tile, pieces)
+    ins = [(a, whole(a.shape)) for a in [acc, gram, cw] + [low for low, _, _, _ in pieces]]
     square = (sds((width, width), bf16), whole((width, width)))
     return call(
-        functools.partial(finish_body, scale, tile, len(pieces), tokens // tile), "finish_slopes", (pos,), ins,
+        functools.partial(finish_body, scale, min(256, tokens), [off for _, off, _, _ in pieces]), "finish_slopes", (pos,),
+        ins + token_blocks(xs, pieces, sub),
         [(sds((2, tokens, wide), bf16), whole((2, tokens, wide))), square, square],
-        grid=(tokens // tile,),
-        scratch=[pltpu.VMEM((width, width), f32)] + [pltpu.VMEM((width, width), bf16)] * 2,
+        grid=(len(pieces),),
+        scratch=[pltpu.VMEM((2, tokens, wide), f32), pltpu.VMEM((width, width), f32)],
     )
 
 
@@ -258,14 +262,15 @@
     out[:, width:] = grad_dec.astype(out.dtype)
 
 
-def grad_rows(scale, s, i, cr, xt, slopes, w_hi, w_lo, low, dtype, after=()):
+def grad_rows(scale, s, i, cr, xt, slopes, w_hi, w_lo, lows, dtype, after=()):
     tokens = xt[0].shape[1]
-    rows, wide = low.shape
-    block = s * (rows // cr) + i
+    sub, wide = lows[0].shape
+    low = lows[i * cr // sub]
+    block = s * (sub * len(lows) // cr) + i
     ins = [(x, once((cr, tokens), lambda g: (block, 0))) for x in xt]
     ins += [(a, whole(a.shape)) for a in (slopes, w_hi, w_lo, low)]
     return call(
-        functools.partial(grad_body, scale, i * cr), "grad_rows", (), ins,
+        functools.partial(grad_body, scale, i * cr % sub), "grad_rows", (), ins,
         [(sds((cr, wide), dtype), whole((cr, wide)))], after=after,
     )[0]
 
@@ -294,7 +299,7 @@
     return jnp.where(fragment(plan) == k, mix_share * theta + (1.0 - mix_share) * anchor, theta)
 
 
-def adam_rows(plan, i, cr, own, got, state, state_block, new_anc, prev, full):
+def adam_rows(plan, i, cr, own, got, state, state_block, new_anc, prev, full, after=()):
     width = own.shape[1] // 2
     last = new_anc is not None
     block = (1, 2, cr, width)
@@ -312,6 +317,7 @@
         outs = [(sds(block, f32), whole(block))] * 3
     return call(
         functools.partial(adam_body, last, len(got)), "adam_rows", (plan,), ins, outs, aliases=aliases,
+        after=after,
     )
 
 
@@ -349,11 +355,11 @@
     refs[-1][...] = total.astype(bf16)
 
 
-def outer_add(plan, parts, final):
+def outer_add(plan, parts, final, after=()):
     shape = parts[0].shape
     return call(
         functools.partial(add_body, final), "add_quarters", (plan,), [(a, whole(shape)) for a in parts],
-        [(sds(shape, bf16), whole(shape))],
+        [(sds(shape, bf16), whole(shape))], after=after,
     )[0]
 
 
@@ -362,27 +368,38 @@
     return anchor[frag, at, :] - outer_rate * (grad + outer_mu * mom), mom
 
 
-def mix_body(count, pos, plan, anchor, momentum, *refs):
-    quarters, thetas = refs[:4], refs[4:4 + count]
-    new_anc, low = refs[-2:]
-    frag = fragment(plan)
-    for m, piece in enumerate(quarters):
+def new_anchor_body(pos, plan, anchor, momentum, *refs):
+    for m, piece in enumerate(refs[:4]):
         at = quarter(pos, m, piece.shape[0])
-        new_anc[at, :] = outer_update(frag, at, anchor, momentum, piece[...].astype(f32))[0]
+        refs[4][at, :] = outer_update(0, at, anchor, momentum, piece[...].astype(f32))[0]
+
+
+def outer_anchor(pos, plan, anchor, momentum, quarters, after):
+    _, rows, width = anchor.shape
+    part = once((1, rows, width), lambda g, p, q: (fragment(q), 0, 0))
+    return call(
+        new_anchor_body, "new_anchor", (pos, plan),
+        [(anchor, part), (momentum, part)] + [(a, whole(a.shape)) for a in quarters],
+        [(sds((rows, width), f32), whole((rows, width)))], after=after,
+    )[0]
+
+
+def mix_body(off, plan, new_anc, *refs):
+    thetas, low = refs[:-1], refs[-1]
     cr, width = thetas[0].shape[2:]
     for i, theta in enumerate(thetas):
         for k in range(2):
-            value = mixed(plan, k, theta[0, k], new_anc[i * cr:(i + 1) * cr, :])
+            value = mixed(plan, k, theta[0, k], new_anc[off + i * cr:off + (i + 1) * cr, :])
             low[i * cr:(i + 1) * cr, k * width:(k + 1) * width] = value.astype(bf16)
 
 
-def outer_mix(pos, plan, anchor, momentum, quarters, thetas):
-    _, rows, width = anchor.shape
-    return call(
-        functools.partial(mix_body, len(thetas)), "mix_rows", (pos, plan),
-        [(a, whole(a.shape)) for a in [anchor, momentum] + quarters + thetas],
-        [(sds((rows, width), f32), whole((rows, width))), (sds((rows, 2 * width), bf16), whole((rows, 2 * width)))],
-    )
+def mix_rows(plan, new_anc, off, thetas):
+    cr, width = thetas[0].shape[2:]
+    shape = (cr * len(thetas), 2 * width)
+    return call(
+        functools.partial(mix_body, off), "mix_rows", (plan,),
+        [(a, whole(a.shape)) for a in [new_anc] + thetas], [(sds(shape, bf16), whole(shape))],
+    )[0]
 
 
 def outer_body(pos, plan, anchor, momentum, *refs):
@@ -413,6 +430,8 @@
     scale = 1.0 / math.sqrt(tokens * n_fsdp)
     chunks = max(1, min(4, rows // 256))
     cr = rows // chunks
+    parts = max(1, chunks // 2)
+    sub = rows // parts
 
     partner = [(f, f ^ 1) for f in range(n_fsdp)]
     to_partner = lambda a: lax.ppermute(a, "fsdp", partner)
@@ -423,7 +442,7 @@
     across = lambda a, bit: lax.ppermute(a, "replica", [(r, r ^ bit) for r in range(n_rep)])
 
     blocks = [(i * cr, cr) for i in range(chunks)]
-    low_own = cast_rows(weights)
+    low_own = cast_rows(weights, 1)
 
     chip = lax.axis_index("fsdp") // 2
     core = lax.axis_index("fsdp") % 2
@@ -436,30 +455,46 @@
     cw = call(
         weigh_body, "weigh_tokens", (),
         [(lanes, whole(lanes.shape)), (to_partner(lanes), whole(lanes.shape))],
-        [(sds((2, tokens, 1), f32), whole((2, tokens, 1)))], after=[low_own],
+        [(sds((2, tokens, 1), f32), whole((2, tokens, 1)))], after=low_own,
     )[0]
 
-    parts = outer_start(pos, plan, anchor, weights, [low_own])
-    own = outer_add(plan, [parts[0]] + [across(parts[m], m) for m in range(1, 4)], n_rep == 4)
-    bit = 4
-    while bit < n_rep:
-        own = outer_add(plan, [own, across(own, bit)], 2 * bit == n_rep)
-        bit *= 2
+    quarters = outer_start(pos, plan, anchor, weights, low_own)
     xt = [turn(pos, x, chips, rows) for x in xs]
-
-    ready = [cw, own] + xt
+    own = outer_add(plan, [quarters[0]] + [across(quarters[m], m) for m in range(1, 4)], n_rep == 4, [xt[0], cw])
+
     state = [(weights, first_moment, second_moment)] * chunks
     state_block = list(range(chunks))
     new_anc = None
     for step in range(INNER):
         last = step == INNER - 1
-        low_far = {s: fetch(low_own, s) for s in range(1, chips)}
-        near = [(low_own, 1), (to_partner(low_own), 1 + chips)]
-        acc, gram = forward(pos, None, None, near, xs)
-        far = [(low_far[s], 1 + s) for s in low_far]
-        handed = [(to_partner(relay(low, [acc] + ready)), slot + chips) for low, slot in far]
-        acc, gram = forward(pos, acc, gram, far, xs)
-        slopes, w_hi, w_lo = finish(pos, acc, gram, cw, handed, xs, scale)
+        def pieces(lows, slot, cut=sub):
+            return [
+                (low, off, slot, (j * low.shape[0] + off) // cut)
+                for j, low in enumerate(lows) for off in range(0, low.shape[0], cut)
+            ]
+
+        low_far = {s: [fetch(low, s) for low in low_own] for s in range(1, chips)}
+        low_near = [to_partner(low) for low in low_own]
+        acc, gram = forward(pos, None, None, pieces(low_own, 1), xs, sub)
+        pending = pieces(low_near, 1 + chips)
+        if step == 0:
+            acc, gram = forward(pos, acc, gram, pending, xs, sub)
+            pending = []
+            bit = 4
+            while bit < n_rep:
+                own = outer_add(plan, [own, across(own, bit)], 2 * bit == n_rep, [acc, xt[1]])
+                bit *= 2
+            ready = [own]
+        for j in range(len(low_own)):
+            handed = {s: to_partner(relay(low_far[s][j], [acc] + ready)) for s in low_far}
+            place = lambda lows, slot: [
+                (low, off, slot + s, j * (rows // len(low_own)) // sub + off // sub)
+                for s, low in lows.items() for off in range(0, low.shape[0], sub)
+            ]
+            acc, gram = forward(
+                pos, acc, gram, pending + place({s: low_far[s][j] for s in low_far}, 1), xs, sub)
+            pending = place(handed, 1 + chips)
+        slopes, w_hi, w_lo = finish(pos, acc, gram, cw, pending, xs, sub, scale)
 
         mine, got, sent = [], [], []
         for i in range(chunks):
@@ -474,19 +509,25 @@
                 scale, 0, i, cr, xt, slopes, w_hi, w_lo, low_own, f32, after=(sent + mine)[-1:]))
 
         new_state, prev = [], None
+        if not last:
+            quarters = [own] + [across(own, m) for m in range(1, 4)]
+            new_anc = outer_anchor(pos, plan, anchor, momentum, quarters, mine[-1:])
+            low_next = []
         for i in range(chunks):
             res = adam_rows(
-                plan, i, cr, mine[i], got[i], state[i], state_block[i], new_anc, prev, weights.shape)
+                plan, i, cr, mine[i], got[i], state[i], state_block[i], new_anc if last else None, prev,
+                weights.shape, [] if last else low_next[-1:])
             if last:
                 prev = res
-            else:
-                new_state.append(tuple(res))
+                continue
+            new_state.append(tuple(res))
+            if (i + 1) * cr % sub == 0:
+                thetas = [t for t, _, _ in new_state[len(low_next) * (sub // cr):]]
+                low_next.append(mix_rows(plan, new_anc, len(low_next) * sub, thetas))
         if not last:
-            quarters = [own] + [across(own, m) for m in range(1, 4)]
-            new_anc, low_own = outer_mix(pos, plan, anchor, momentum, quarters, [t for t, _, _ in new_state])
-            anchor_out, momentum_out = outer_end(pos, plan, anchor, momentum, quarters, [low_own])
+            anchor_out, momentum_out = outer_end(pos, plan, anchor, momentum, quarters, low_next)
             ready = [anchor_out]
-            state, state_block = new_state, [0] * chunks
+            state, state_block, low_own = new_state, [0] * chunks, low_next
     return (*prev, anchor_out, momentum_out)
 
 

time: 146 us -> 132 us (0.904)
  waiting for transfers between devices: 43.7 us -> 27.9 us
    ppermute x2 -> x3, waiting for transfers between devices: 14.8 us -> 5.3 us  [local(): lax.ppermute(a, 'fsdp', [((f // 2 + s) % chips * 2 + f % 2, f) for f in r...]
    ppermute x8, waiting for transfers between devices: 20.7 us -> 15.7 us  [local(): lax.ppermute(a, 'fsdp', [(f, (f // 2 + s) % chips * 2 + f % 2) for f in r...]
    ppermute x7, waiting for transfers between devices: 8.22 us -> 5.73 us  [local(): lax.ppermute(a, 'replica', [(r, r ^ bit) for r in range(n_rep)])]
    ppermute x2 -> x3, starting transfers between devices: 4.79 us -> 6.48 us  [local(): lax.ppermute(a, 'fsdp', [((f // 2 + s) % chips * 2 + f % 2, f) for f in r...]
    pallas_call x41 -> x46, Pallas kernels: 69.1 us -> 69.8 us  [call(): pl.pallas_call(run, name=name, out_shape=[o for o, _ in outs], grid_spec=...]
  transfers between devices with their start and end apart: 23 -> 26, of which waited for: 11 -> 11; matrix products, arithmetic and copies ran while one was open for 0% -> 0% of each run, Pallas kernels for 34% -> 48%
where the time goes in v5:
time: 132 us
  Pallas kernels  69.8 us (53%)
  starting transfers between devices  28 us (21%)
  waiting for transfers between devices  27.9 us (21%)
  local copies, waits for them, and re-layouts  4.9 us (4%)
    pallas_call x46, Pallas kernels, call(): pl.pallas_call(run, name=name, out_shape=[o for o, _ in outs], grid_spec=...  69.8 us
    ppermute x8, waiting for transfers between devices, local(): lax.ppermute(a, 'fsdp', [(f, (f // 2 + s) % chips * 2 + f % 2) for f in r...  15.7 us
    ppermute x7, starting transfers between devices, local(): lax.ppermute(a, 'replica', [(r, r ^ bit) for r in range(n_rep)])  11.9 us
    ppermute x8, starting transfers between devices, local(): lax.ppermute(a, 'fsdp', [(f, (f // 2 + s) % chips * 2 + f % 2) for f in r...  8.62 us
    ppermute x3, starting transfers between devices, local(): lax.ppermute(a, 'fsdp', [((f // 2 + s) % chips * 2 + f % 2, f) for f in r...  6.48 us
    ppermute x7, waiting for transfers between devices, local(): lax.ppermute(a, 'replica', [(r, r ^ bit) for r in range(n_rep)])  5.73 us
    ppermute x3, waiting for transfers between devices, local(): lax.ppermute(a, 'fsdp', [((f // 2 + s) % chips * 2 + f % 2, f) for f in r...  5.3 us
    unnamed x22, local copies, waits for them, and re-layouts  4.81 us
  transfers between devices with their start and end apart: 26, of which 11 were waited for; matrix products, arithmetic and copies ran while one was open for 0% of the time, Pallas kernels for 48%

profile of v5, /device:TPU:0, one launch (start us, length us, event | category | flops | bytes accessed | tf_op | source)
XLA Modules:
  0.0 131.7 jit_solution(4848187308871177390)
XLA Ops:
  3.0 3.0 %collective-permute-start.10 = (bf16[1024,512]{1,0:T(8,128)(2,1)S(1)}, bf16[1024,512]{1,0:T(8,128)(2,1)}, u32[]{:S(2)}, u32[]{:S(2)}) collective-permute-start(bf16[1024,512]{1,0:T(8,128)(2,1)S(1)} %cast_rows.1.refs_4_.refs_2_.refs_1_.refs_5_), channel_id=1, source_target_pairs={{2,0},{3,1},{0,2},{1,3},{6,4},{7,5},{4,6},{5,7},{10,8},{11,9},{8,1... | collective-permute-start | bytes 3145736 | tf_op jit(solution)/shard_map/ppermute | solution.py:438
  13.6 2.5 %collective-permute-start.3 = (bf16[256,256]{1,0:T(8,128)(2,1)S(1)}, bf16[256,256]{1,0:T(8,128)(2,1)S(1)}, u32[]{:S(2)}, u32[]{:S(2)}) collective-permute-start(bf16[256,256]{1,0:T(8,128)(2,1)S(1)} %get-tuple-element.56), channel_id=1, source_target_pairs={{0,12},{4,8},{8,4},{12,0},{16,28},{20,24},{24,20},{28,16},{1,13},{... | collective-permute-start | bytes 393224 | tf_op jit(solution)/shard_map/ppermute | solution.py:442
  18.1 2.0 %collective-permute-done.3.refs_4_ = bf16[256,256]{1,0:T(8,128)(2,1)S(1)} collective-permute-done((bf16[256,256]{1,0:T(8,128)(2,1)S(1)}, bf16[256,256]{1,0:T(8,128)(2,1)S(1)}, u32[]{:S(2)}, u32[]{:S(2)}) %collective-permute-start.3) | collective-permute-done | bytes 131104 | tf_op jit(solution)/shard_map/ppermute | solution.py:442
  20.7 2.7 %collective-permute-start.5 = (bf16[256,256]{1,0:T(8,128)(2,1)S(1)}, bf16[256,256]{1,0:T(8,128)(2,1)S(1)}, u32[]{:S(2)}, u32[]{:S(2)}) collective-permute-start(bf16[256,256]{1,0:T(8,128)(2,1)S(1)} %add_quarters.2.refs_1_), channel_id=1, source_target_pairs={{0,16},{4,20},{8,24},{12,28},{16,0},{20,4},{24,8},{28,12},{1,17},{... | collective-permute-start | bytes 393224 | tf_op jit(solution)/shard_map/ppermute | solution.py:442
  23.4 3.4 %turn_tokens.3.refs_4_.refs_1_ = bf16[2048,512]{1,0:T(8,128)(2,1)S(1)} custom-call(s32[5]{0:T(128)S(1)} %stack.23.refs_0_, bf16[512,4096]{1,0:T(8,128)(2,1)} %collective-permute-done.refs_1_.refs_4_.refs_6_.refs_7_), custom_call_target="tpu_custom_call" | custom-call | bytes 2621440 | tf_op jit(solution)/shard_map/turn_tokens/pallas_call | solution.py:60
  26.8 3.4 %forward_rows.6 = (f32[2,512,512]{2,1,0:T(8,128)S(1)}, f32[256,256]{1,0:T(8,128)S(1)}) custom-call(s32[5]{0:T(128)S(1)} %stack.23.refs_0_, bf16[1024,512]{1,0:T(8,128)(2,1)S(1)} %cast_rows.1.refs_4_.refs_2_.refs_1_.refs_5_, bf16[1024,512]{1,0:T(8,128)(2,1)S(1)} %cast_rows.1.refs_4_.refs_2_.refs_1_.refs_5_, bf16[512,4096]{1,0:T(8,128)(2,1)S(1)} %copy-done, ...), custom_call_target="tpu_custom_call" | custom-call | bytes 5505024 | tf_op jit(solution)/shard_map/forward_rows/pallas_call | solution.py:60
  30.2 4.2 %forward_rows.7 = (f32[2,512,512]{2,1,0:T(8,128)S(1)}, f32[256,256]{1,0:T(8,128)S(1)}) custom-call(s32[5]{0:T(128)S(1)} %stack.23.refs_0_, f32[2,512,512]{2,1,0:T(8,128)S(1)} %get-tuple-element.57.refs_1_, f32[256,256]{1,0:T(8,128)S(1)} %get-tuple-element.58.refs_2_, bf16[1024,512]{1,0:T(8,128)(2,1)} %collective-permute-done.6.refs_3_.refs_4_, ...), custom_call_target="tpu_custom_call" | custom-call | bytes 7864320 | tf_op jit(solution)/shard_map/forward_rows/pallas_call | solution.py:60
  38.9 4.3 %forward_rows.8 = (f32[2,512,512]{2,1,0:T(8,128)S(1)}, f32[256,256]{1,0:T(8,128)S(1)}) custom-call(s32[5]{0:T(128)S(1)} %stack.23.refs_0_, f32[2,512,512]{2,1,0:T(8,128)S(1)} %get-tuple-element.59.refs_3_.refs_1_, f32[256,256]{1,0:T(8,128)S(1)} %get-tuple-element.60.refs_2_, bf16[1024,512]{1,0:T(8,128)(2,1)} %collective-permute-done.10.refs_3_.refs_4_.refs_0_.refs_5_, ...), custom_call_target="tpu_custom_call" | custom-call | bytes 7864320 | tf_op jit(solution)/shard_map/forward_rows/pallas_call | solution.py:60
  43.2 4.0 %finish_slopes.2 = (bf16[2,512,512]{2,1,0:T(8,128)(2,1)S(1)}, bf16[256,256]{1,0:T(8,128)(2,1)S(1)}, bf16[256,256]{1,0:T(8,128)(2,1)S(1)}) custom-call(s32[5]{0:T(128)S(1)} %stack.23.refs_0_, f32[2,512,512]{2,1,0:T(8,128)S(1)} %get-tuple-element.61.refs_1_, f32[256,256]{1,0:T(8,128)S(1)} %get-tuple-element.62.refs_2_, ...), custom_call_target="tpu_custom_call" | custom-call | bytes 6819840 | tf_op jit(solution)/shard_map/finish_slopes/pallas_call | solution.py:60
  61.7 2.7 %collective-permute-done.9.refs_7_ = bf16[256,256]{1,0:T(8,128)(2,1)S(1)} collective-permute-done((bf16[256,256]{1,0:T(8,128)(2,1)S(1)}, bf16[256,256]{1,0:T(8,128)(2,1)S(1)}, u32[]{:S(2)}, u32[]{:S(2)}) %collective-permute-start.9) | collective-permute-done | bytes 131104 | tf_op jit(solution)/shard_map/ppermute | solution.py:442
  70.7 4.4 %collective-permute-done.15.refs_2_ = bf16[256,512]{1,0:T(8,128)(2,1)S(1)} collective-permute-done((bf16[256,512]{1,0:T(8,128)(2,1)S(1)}, bf16[256,512]{1,0:T(8,128)(2,1)S(1)}, u32[]{:S(2)}, u32[]{:S(2)}) %collective-permute-start.15) | collective-permute-done | bytes 262176 | tf_op jit(solution)/shard_map/ppermute | solution.py:440
  78.6 3.3 %forward_rows.9 = (f32[2,512,512]{2,1,0:T(8,128)S(1)}, f32[256,256]{1,0:T(8,128)S(1)}) custom-call(s32[5]{0:T(128)S(1)} %stack.23.refs_0_, bf16[512,512]{1,0:T(8,128)(2,1)S(1)} %mix_rows.2.refs_6_.refs_1_.refs_8_.refs_5_, bf16[512,512]{1,0:T(8,128)(2,1)S(1)} %mix_rows.3.refs_2_.refs_9_.refs_5_, bf16[512,4096]{1,0:T(8,128)(2,1)S(1)} %copy-done, ...), custom_call_target="tpu_custom_call" | custom-call | bytes 4456448 | tf_op jit(solution)/shard_map/forward_rows/pallas_call | solution.py:60
  82.0 3.1 %outer_step.1 = (f32[2,1024,256]{2,1,0:T(8,128)}, f32[2,1024,256]{2,1,0:T(8,128)}) custom-call(s32[5]{0:T(128)S(1)} %stack.23.refs_0_, s32[8]{0:T(128)S(1)} %copy-done.9, f32[2,1024,256]{2,1,0:T(8,128)S(1)} %copy-done.6, f32[2,1024,256]{2,1,0:T(8,128)S(1)} %copy-done.7, bf16[256,256]{1,0:T(8,128)(2,1)S(1)} %add_quarters.3.refs_2_.refs_4_, ...), custom_call_target="tpu_custom_call" | custom-call | bytes 8912896 | tf_op jit(solution)/shard_map/outer_step/pallas_call | solution.py:60
  88.1 4.5 %forward_rows.10 = (f32[2,512,512]{2,1,0:T(8,128)S(1)}, f32[256,256]{1,0:T(8,128)S(1)}) custom-call(s32[5]{0:T(128)S(1)} %stack.23.refs_0_, f32[2,512,512]{2,1,0:T(8,128)S(1)} %get-tuple-element.70.refs_1_, f32[256,256]{1,0:T(8,128)S(1)} %get-tuple-element.71.refs_2_, bf16[512,512]{1,0:T(8,128)(2,1)S(1)} %collective-permute-done.16.refs_3_, ...), custom_call_target="tpu_custom_call" | custom-call | bytes 7340032 | tf_op jit(solution)/shard_map/forward_rows/pallas_call | solution.py:60
  92.6 4.0 %collective-permute-done.20.refs_4_.refs_0_.refs_5_ = bf16[512,512]{1,0:T(8,128)(2,1)S(1)} collective-permute-done((bf16[512,512]{1,0:T(8,128)(2,1)S(1)}, bf16[512,512]{1,0:T(8,128)(2,1)S(1)}, u32[]{:S(2)}, u32[]{:S(2)}) %collective-permute-start.20) | collective-permute-done | bytes 524320 | tf_op jit(solution)/shard_map/ppermute | solution.py:438
  96.7 3.6 %forward_rows.11 = (f32[2,512,512]{2,1,0:T(8,128)S(1)}, f32[256,256]{1,0:T(8,128)S(1)}) custom-call(s32[5]{0:T(128)S(1)} %stack.23.refs_0_, f32[2,512,512]{2,1,0:T(8,128)S(1)} %get-tuple-element.72.refs_1_, f32[256,256]{1,0:T(8,128)S(1)} %get-tuple-element.73.refs_2_, bf16[512,512]{1,0:T(8,128)(2,1)S(1)} %collective-permute-done.19.refs_3_, ...), custom_call_target="tpu_custom_call" | custom-call | bytes 6815744 | tf_op jit(solution)/shard_map/forward_rows/pallas_call | solution.py:60
  100.3 3.0 %finish_slopes.3 = (bf16[2,512,512]{2,1,0:T(8,128)(2,1)S(1)}, bf16[256,256]{1,0:T(8,128)(2,1)S(1)}, bf16[256,256]{1,0:T(8,128)(2,1)S(1)}) custom-call(s32[5]{0:T(128)S(1)} %stack.23.refs_0_, f32[2,512,512]{2,1,0:T(8,128)S(1)} %get-tuple-element.75.refs_1_, f32[256,256]{1,0:T(8,128)S(1)} %get-tuple-element.76.refs_2_, ...), custom_call_target="tpu_custom_call" | custom-call | bytes 5246976 | tf_op jit(solution)/shard_map/finish_slopes/pallas_call | solution.py:60
  113.1 2.1 %adam_rows.12 = (f32[1,2,1024,256]{3,2,1,0:T(8,128)}, f32[1,2,1024,256]{3,2,1,0:T(8,128)}, f32[1,2,1024,256]{3,2,1,0:T(8,128)}) custom-call(s32[8]{0:T(128)S(1)} %copy-done.9, f32[256,512]{1,0:T(8,128)S(1)} %grad_rows.28.refs_6_.refs_1_, bf16[256,512]{1,0:T(8,128)(2,1)S(1)} %collective-permute-done.25.refs_2_, ...), custom_call_target="tpu_custom_call" | custom-call | bytes 8912896 | tf_op jit(solution)/shard_map/adam_rows/pallas_call | solution.py:60
  115.2 3.5 %collective-permute-done.24.refs_2_ = bf16[256,512]{1,0:T(8,128)(2,1)S(1)} collective-permute-done((bf16[256,512]{1,0:T(8,128)(2,1)S(1)}, bf16[256,512]{1,0:T(8,128)(2,1)S(1)}, u32[]{:S(2)}, u32[]{:S(2)}) %collective-permute-start.24) | collective-permute-done | bytes 262176 | tf_op jit(solution)/shard_map/ppermute | solution.py:440
  118.7 2.1 %adam_rows.13 = (f32[1,2,1024,256]{3,2,1,0:T(8,128)}, f32[1,2,1024,256]{3,2,1,0:T(8,128)}, f32[1,2,1024,256]{3,2,1,0:T(8,128)}) custom-call(s32[8]{0:T(128)S(1)} %copy-done.9, f32[256,512]{1,0:T(8,128)S(1)} %grad_rows.29.refs_6_.refs_1_, ...), custom_call_target="tpu_custom_call", output_to_operand_aliasing={{0}: (7, {}), {1}: (8, {}), {2}: (9, {})} | custom-call | bytes 15204352 | tf_op jit(solution)/shard_map/adam_rows/pallas_call | solution.py:60
  120.8 3.5 %collective-permute-done.23.refs_2_ = bf16[256,512]{1,0:T(8,128)(2,1)S(1)} collective-permute-done((bf16[256,512]{1,0:T(8,128)(2,1)S(1)}, bf16[256,512]{1,0:T(8,128)(2,1)S(1)}, u32[]{:S(2)}, u32[]{:S(2)}) %collective-permute-start.23) | collective-permute-done | bytes 262176 | tf_op jit(solution)/shard_map/ppermute | solution.py:440
  124.3 2.1 %adam_rows.14 = (f32[1,2,1024,256]{3,2,1,0:T(8,128)}, f32[1,2,1024,256]{3,2,1,0:T(8,128)}, f32[1,2,1024,256]{3,2,1,0:T(8,128)}) custom-call(s32[8]{0:T(128)S(1)} %copy-done.9, f32[256,512]{1,0:T(8,128)S(1)} %grad_rows.30.refs_6_.refs_1_, ...), custom_call_target="tpu_custom_call", output_to_operand_aliasing={{0}: (7, {}), {1}: (8, {}), {2}: (9, {})} | custom-call | bytes 15204352 | tf_op jit(solution)/shard_map/adam_rows/pallas_call | solution.py:60
  126.4 3.1 %collective-permute-done.22.refs_2_ = bf16[256,512]{1,0:T(8,128)(2,1)S(1)} collective-permute-done((bf16[256,512]{1,0:T(8,128)(2,1)S(1)}, bf16[256,512]{1,0:T(8,128)(2,1)S(1)}, u32[]{:S(2)}, u32[]{:S(2)}) %collective-permute-start.22) | collective-permute-done | bytes 262176 | tf_op jit(solution)/shard_map/ppermute | solution.py:440
  129.5 2.1 %adam_rows.15 = (f32[1,2,1024,256]{3,2,1,0:T(8,128)}, f32[1,2,1024,256]{3,2,1,0:T(8,128)}, f32[1,2,1024,256]{3,2,1,0:T(8,128)}) custom-call(s32[8]{0:T(128)S(1)} %copy-done.9, f32[256,512]{1,0:T(8,128)S(1)} %grad_rows.31.refs_1_, bf16[256,512]{1,0:T(8,128)(2,1)S(1)} %collective-permute-done.22.refs_2_, ...), custom_call_target="tpu_custom_call", output_to_operand_aliasing={{0}: (7, {}), {1}: (8, {}), {2}: (9, {})} | custom-call | bytes 15204352 | tf_op jit(solution)/shard_map/adam_rows/pallas_call | solution.py:60
  (97 shorter events, 53.8 us)
Async XLA Ops:
  0.6 22.7 %collective-permute-start = (bf16[512,4096]{1,0:T(8,128)(2,1)}, bf16[512,4096]{1,0:T(8,128)(2,1)}, u32[]{:S(2)}, u32[]{:S(2)}) collective-permute-start(bf16[512,4096]{1,0:T(8,128)(2,1)} %refs_5_.15), channel_id=1, source_target_pairs={{0,1},{1,0},{2,3},{3,2},{4,5},{5,4},{6,7},{7,6},{8,9},{9,8},{10,11... | collective-permute-start | bytes 12582920 | tf_op jit(solution)/shard_map/ppermute | solution.py:437
  2.9 27.3 %collective-permute-start.6 = (bf16[1024,512]{1,0:T(8,128)(2,1)S(1)}, bf16[1024,512]{1,0:T(8,128)(2,1)}, u32[]{:S(2)}, u32[]{:S(2)}) collective-permute-start(bf16[1024,512]{1,0:T(8,128)(2,1)S(1)} %cast_rows.1.refs_4_.refs_2_.refs_1_.refs_5_), channel_id=1, source_target_pairs={{0,1},{1,0},{2,3},{3,2},{4,5},{5,4},{6,7},{7,6},{8,9},{9,8},{10,11... | collective-permute-start | bytes 3145736 | tf_op jit(solution)/shard_map/ppermute | solution.py:437
  3.0 32.0 %collective-permute-start.10 = (bf16[1024,512]{1,0:T(8,128)(2,1)S(1)}, bf16[1024,512]{1,0:T(8,128)(2,1)}, u32[]{:S(2)}, u32[]{:S(2)}) collective-permute-start(bf16[1024,512]{1,0:T(8,128)(2,1)S(1)} %cast_rows.1.refs_4_.refs_2_.refs_1_.refs_5_), channel_id=1, source_target_pairs={{2,0},{3,1},{0,2},{1,3},{6,4},{7,5},{4,6},{5,7},{10,8},{11,9},{8,1... | collective-permute-start | bytes 3145736 | tf_op jit(solution)/shard_map/ppermute | solution.py:438
  8.4 5.3 %collective-permute-start.1 = (bf16[256,256]{1,0:T(8,128)(2,1)S(1)}, bf16[256,256]{1,0:T(8,128)(2,1)S(1)}, u32[]{:S(2)}, u32[]{:S(2)}) collective-permute-start(bf16[256,256]{1,0:T(8,128)(2,1)S(1)} %get-tuple-element.54), channel_id=1, source_target_pairs={{0,4},{4,0},{8,12},{12,8},{16,20},{20,16},{24,28},{28,24},{1,5},{5... | collective-permute-start | bytes 393224 | tf_op jit(solution)/shard_map/ppermute | solution.py:442
  11.1 7.0 %collective-permute-start.2 = (bf16[256,256]{1,0:T(8,128)(2,1)S(1)}, bf16[256,256]{1,0:T(8,128)(2,1)S(1)}, u32[]{:S(2)}, u32[]{:S(2)}) collective-permute-start(bf16[256,256]{1,0:T(8,128)(2,1)S(1)} %get-tuple-element.55), channel_id=1, source_target_pairs={{0,8},{4,12},{8,0},{12,4},{16,24},{20,28},{24,16},{28,20},{1,9},{5... | collective-permute-start | bytes 393224 | tf_op jit(solution)/shard_map/ppermute | solution.py:442
  13.6 6.5 %collective-permute-start.3 = (bf16[256,256]{1,0:T(8,128)(2,1)S(1)}, bf16[256,256]{1,0:T(8,128)(2,1)S(1)}, u32[]{:S(2)}, u32[]{:S(2)}) collective-permute-start(bf16[256,256]{1,0:T(8,128)(2,1)S(1)} %get-tuple-element.56), channel_id=1, source_target_pairs={{0,12},{4,8},{8,4},{12,0},{16,28},{20,24},{24,20},{28,16},{1,13},{... | collective-permute-start | bytes 393224 | tf_op jit(solution)/shard_map/ppermute | solution.py:442
  20.7 13.7 %collective-permute-start.5 = (bf16[256,256]{1,0:T(8,128)(2,1)S(1)}, bf16[256,256]{1,0:T(8,128)(2,1)S(1)}, u32[]{:S(2)}, u32[]{:S(2)}) collective-permute-start(bf16[256,256]{1,0:T(8,128)(2,1)S(1)} %add_quarters.2.refs_1_), channel_id=1, source_target_pairs={{0,16},{4,20},{8,24},{12,28},{16,0},{20,4},{24,8},{28,12},{1,17},{... | collective-permute-start | bytes 393224 | tf_op jit(solution)/shard_map/ppermute | solution.py:442
  36.3 7.0 %collective-permute-start.11 = (bf16[1024,512]{1,0:T(8,128)(2,1)S(1)}, bf16[1024,512]{1,0:T(8,128)(2,1)S(1)}, u32[]{:S(2)}, u32[]{:S(2)}) collective-permute-start(bf16[1024,512]{1,0:T(8,128)(2,1)S(1)} %relay_rows.3), channel_id=1, source_target_pairs={{0,1},{1,0},{2,3},{3,2},{4,5},{5,4},{6,7},{7,6},{8,9},{9,8},{10,11... | collective-permute-start | bytes 3145736 | tf_op jit(solution)/shard_map/ppermute | solution.py:437
  36.4 21.8 %collective-permute-start.7 = (bf16[256,256]{1,0:T(8,128)(2,1)S(1)}, bf16[256,256]{1,0:T(8,128)(2,1)S(1)}, u32[]{:S(2)}, u32[]{:S(2)}) collective-permute-start(bf16[256,256]{1,0:T(8,128)(2,1)S(1)} %add_quarters.3.refs_2_.refs_4_), channel_id=1, source_target_pairs={{0,4},{4,0},{8,12},{12,8},{16,20},{20,16},{24,28},{28,24},{1,5},{5... | collective-permute-start | bytes 393224 | tf_op jit(solution)/shard_map/ppermute | solution.py:442
  37.3 21.3 %collective-permute-start.8 = (bf16[256,256]{1,0:T(8,128)(2,1)S(1)}, bf16[256,256]{1,0:T(8,128)(2,1)S(1)}, u32[]{:S(2)}, u32[]{:S(2)}) collective-permute-start(bf16[256,256]{1,0:T(8,128)(2,1)S(1)} %add_quarters.3.refs_2_.refs_4_), channel_id=1, source_target_pairs={{0,8},{4,12},{8,0},{12,4},{16,24},{20,28},{24,16},{28,20},{1,9},{5... | collective-permute-start | bytes 393224 | tf_op jit(solution)/shard_map/ppermute | solution.py:442
  49.0 16.2 %collective-permute-start.12 = (bf16[256,512]{1,0:T(8,128)(2,1)S(1)}, bf16[256,512]{1,0:T(8,128)(2,1)S(1)}, u32[]{:S(2)}, u32[]{:S(2)}) collective-permute-start(bf16[256,512]{1,0:T(8,128)(2,1)S(1)} %grad_rows.16.refs_6_), channel_id=1, source_target_pairs={{0,2},{1,3},{2,0},{3,1},{4,6},{5,7},{6,4},{7,5},{8,10},{9,11},{10,... | collective-permute-start | bytes 786440 | tf_op jit(solution)/shard_map/ppermute | solution.py:440
  52.5 13.7 %collective-permute-start.13 = (bf16[256,512]{1,0:T(8,128)(2,1)S(1)}, bf16[256,512]{1,0:T(8,128)(2,1)S(1)}, u32[]{:S(2)}, u32[]{:S(2)}) collective-permute-start(bf16[256,512]{1,0:T(8,128)(2,1)S(1)} %grad_rows.17.refs_6_), channel_id=1, source_target_pairs={{0,2},{1,3},{2,0},{3,1},{4,6},{5,7},{6,4},{7,5},{8,10},{9,11},{10,... | collective-permute-start | bytes 786440 | tf_op jit(solution)/shard_map/ppermute | solution.py:440
  54.7 15.1 %collective-permute-start.14 = (bf16[256,512]{1,0:T(8,128)(2,1)S(1)}, bf16[256,512]{1,0:T(8,128)(2,1)S(1)}, u32[]{:S(2)}, u32[]{:S(2)}) collective-permute-start(bf16[256,512]{1,0:T(8,128)(2,1)S(1)} %grad_rows.18.refs_6_), channel_id=1, source_target_pairs={{0,2},{1,3},{2,0},{3,1},{4,6},{5,7},{6,4},{7,5},{8,10},{9,11},{10,... | collective-permute-start | bytes 786440 | tf_op jit(solution)/shard_map/ppermute | solution.py:440
  58.2 17.0 %collective-permute-start.15 = (bf16[256,512]{1,0:T(8,128)(2,1)S(1)}, bf16[256,512]{1,0:T(8,128)(2,1)S(1)}, u32[]{:S(2)}, u32[]{:S(2)}) collective-permute-start(bf16[256,512]{1,0:T(8,128)(2,1)S(1)} %grad_rows.19.refs_6_), channel_id=1, source_target_pairs={{0,2},{1,3},{2,0},{3,1},{4,6},{5,7},{6,4},{7,5},{8,10},{9,11},{10,... | collective-permute-start | bytes 786440 | tf_op jit(solution)/shard_map/ppermute | solution.py:440
  58.6 5.9 %collective-permute-start.9 = (bf16[256,256]{1,0:T(8,128)(2,1)S(1)}, bf16[256,256]{1,0:T(8,128)(2,1)S(1)}, u32[]{:S(2)}, u32[]{:S(2)}) collective-permute-start(bf16[256,256]{1,0:T(8,128)(2,1)S(1)} %add_quarters.3.refs_2_.refs_4_), channel_id=1, source_target_pairs={{0,12},{4,8},{8,4},{12,0},{16,28},{20,24},{24,20},{28,16},{1,13},{... | collective-permute-start | bytes 393224 | tf_op jit(solution)/shard_map/ppermute | solution.py:442
  67.9 20.1 %collective-permute-start.16 = (bf16[512,512]{1,0:T(8,128)(2,1)S(1)}, bf16[512,512]{1,0:T(8,128)(2,1)S(1)}, u32[]{:S(2)}, u32[]{:S(2)}) collective-permute-start(bf16[512,512]{1,0:T(8,128)(2,1)S(1)} %mix_rows.2.refs_6_.refs_1_.refs_8_.refs_5_), channel_id=1, source_target_pairs={{0,1},{1,0},{2,3},{3,2},{4,5},{5,4},{6,7},{7,6},{8,9},{9,8},{10,11... | collective-permute-start | bytes 1572872 | tf_op jit(solution)/shard_map/ppermute | solution.py:437
  68.0 18.4 %collective-permute-start.18 = (bf16[512,512]{1,0:T(8,128)(2,1)S(1)}, bf16[512,512]{1,0:T(8,128)(2,1)S(1)}, u32[]{:S(2)}, u32[]{:S(2)}) collective-permute-start(bf16[512,512]{1,0:T(8,128)(2,1)S(1)} %mix_rows.2.refs_6_.refs_1_.refs_8_.refs_5_), channel_id=1, source_target_pairs={{2,0},{3,1},{0,2},{1,3},{6,4},{7,5},{4,6},{5,7},{10,8},{11,9},{8,1... | collective-permute-start | bytes 1572872 | tf_op jit(solution)/shard_map/ppermute | solution.py:438
  76.8 11.3 %collective-permute-start.17 = (bf16[512,512]{1,0:T(8,128)(2,1)S(1)}, bf16[512,512]{1,0:T(8,128)(2,1)S(1)}, u32[]{:S(2)}, u32[]{:S(2)}) collective-permute-start(bf16[512,512]{1,0:T(8,128)(2,1)S(1)} %mix_rows.3.refs_2_.refs_9_.refs_5_), channel_id=1, source_target_pairs={{0,1},{1,0},{2,3},{3,2},{4,5},{5,4},{6,7},{7,6},{8,9},{9,8},{10,11... | collective-permute-start | bytes 1572872 | tf_op jit(solution)/shard_map/ppermute | solution.py:437
  76.9 19.7 %collective-permute-start.20 = (bf16[512,512]{1,0:T(8,128)(2,1)S(1)}, bf16[512,512]{1,0:T(8,128)(2,1)S(1)}, u32[]{:S(2)}, u32[]{:S(2)}) collective-permute-start(bf16[512,512]{1,0:T(8,128)(2,1)S(1)} %mix_rows.3.refs_2_.refs_9_.refs_5_), channel_id=1, source_target_pairs={{2,0},{3,1},{0,2},{1,3},{6,4},{7,5},{4,6},{5,7},{10,8},{11,9},{8,1... | collective-permute-start | bytes 1572872 | tf_op jit(solution)/shard_map/ppermute | solution.py:438
  88.0 8.7 %collective-permute-start.19 = (bf16[512,512]{1,0:T(8,128)(2,1)S(1)}, bf16[512,512]{1,0:T(8,128)(2,1)S(1)}, u32[]{:S(2)}, u32[]{:S(2)}) collective-permute-start(bf16[512,512]{1,0:T(8,128)(2,1)S(1)} %relay_rows.4), channel_id=1, source_target_pairs={{0,1},{1,0},{2,3},{3,2},{4,5},{5,4},{6,7},{7,6},{8,9},{9,8},{10,11... | collective-permute-start | bytes 1572872 | tf_op jit(solution)/shard_map/ppermute | solution.py:437
  103.9 9.2 %collective-permute-start.25 = (bf16[256,512]{1,0:T(8,128)(2,1)S(1)}, bf16[256,512]{1,0:T(8,128)(2,1)S(1)}, u32[]{:S(2)}, u32[]{:S(2)}) collective-permute-start(bf16[256,512]{1,0:T(8,128)(2,1)S(1)} %grad_rows.24.refs_6_), channel_id=1, source_target_pairs={{0,2},{1,3},{2,0},{3,1},{4,6},{5,7},{6,4},{7,5},{8,10},{9,11},{10,... | collective-permute-start | bytes 786440 | tf_op jit(solution)/shard_map/ppermute | solution.py:440
  106.1 12.5 %collective-permute-start.24 = (bf16[256,512]{1,0:T(8,128)(2,1)S(1)}, bf16[256,512]{1,0:T(8,128)(2,1)S(1)}, u32[]{:S(2)}, u32[]{:S(2)}) collective-permute-start(bf16[256,512]{1,0:T(8,128)(2,1)S(1)} %grad_rows.25.refs_6_), channel_id=1, source_target_pairs={{0,2},{1,3},{2,0},{3,1},{4,6},{5,7},{6,4},{7,5},{8,10},{9,11},{10,... | collective-permute-start | bytes 786440 | tf_op jit(solution)/shard_map/ppermute | solution.py:440
  107.1 17.2 %collective-permute-start.23 = (bf16[256,512]{1,0:T(8,128)(2,1)S(1)}, bf16[256,512]{1,0:T(8,128)(2,1)S(1)}, u32[]{:S(2)}, u32[]{:S(2)}) collective-permute-start(bf16[256,512]{1,0:T(8,128)(2,1)S(1)} %grad_rows.26.refs_6_), channel_id=1, source_target_pairs={{0,2},{1,3},{2,0},{3,1},{4,6},{5,7},{6,4},{7,5},{8,10},{9,11},{10,... | collective-permute-start | bytes 786440 | tf_op jit(solution)/shard_map/ppermute | solution.py:440
  109.3 20.2 %collective-permute-start.22 = (bf16[256,512]{1,0:T(8,128)(2,1)S(1)}, bf16[256,512]{1,0:T(8,128)(2,1)S(1)}, u32[]{:S(2)}, u32[]{:S(2)}) collective-permute-start(bf16[256,512]{1,0:T(8,128)(2,1)S(1)} %grad_rows.27.refs_6_), channel_id=1, source_target_pairs={{0,2},{1,3},{2,0},{3,1},{4,6},{5,7},{6,4},{7,5},{8,10},{9,11},{10,... | collective-permute-start | bytes 786440 | tf_op jit(solution)/shard_map/ppermute | solution.py:440
  (13 other events, 40.8 us)

commit v6 on v5

--- a/solution.py
+++ b/solution.py
@@ -21,7 +21,7 @@
 
 bf16 = jnp.bfloat16
 f32 = jnp.float32
-VMEM_LIMIT = 12 * 1024 * 1024
+VMEM_LIMIT = 16 * 1024 * 1024
 
 
 def token_weight(kinds):
@@ -85,33 +85,46 @@
     return lax.rem(plan_sum(plan), 2)
 
 
-def cast_body(theta, *lows):
-    sub, wide = lows[0].shape
+EXTRA = 16
+
+
+def cast_body(theta, kinds, low, more):
+    rows, wide = low.shape
     width = wide // 2
-    for j, low in enumerate(lows):
-        for k in range(2):
-            low[:, k * width:(k + 1) * width] = theta[0, k, j * sub:(j + 1) * sub, :].astype(bf16)
-
-
-def cast_rows(weights, parts):
+    for k in range(2):
+        value = theta[0, k].astype(bf16)
+        low[:, k * width:(k + 1) * width] = value
+        more[:rows, k * width:(k + 1) * width] = value
+    weight = token_weight(kinds[...])
+    pad = jnp.zeros((EXTRA - kinds.shape[0], wide), f32)
+    more[rows:, :] = jnp.concatenate([weight, pad], 0).astype(bf16)
+
+
+def cast_rows(weights, kinds):
     _, _, rows, width = weights.shape
-    shape = (rows // parts, 2 * width)
-    return call(
-        cast_body, "cast_rows", (), [(weights, whole(weights.shape))],
-        [(sds(shape, bf16), whole(shape))] * parts,
+    lanes = kinds.reshape(-1, 2 * width)
+    shapes = [(rows, 2 * width), (rows + EXTRA, 2 * width)]
+    return call(
+        cast_body, "cast_rows", (), [(weights, whole(weights.shape)), (lanes, whole(lanes.shape))],
+        [(sds(shape, bf16), whole(shape)) for shape in shapes],
     )
 
 
 def weigh_body(own, other, out):
-    for h, kinds in enumerate((own, other)):
-        lanes = kinds.shape[0]
-        pad = jnp.zeros((8 - lanes % 8, 128), f32)
-        value = token_weight(kinds[...])
-        if lanes % 8:
-            value = jnp.concatenate([value, pad], 0)
-        turned = value.T
-        for j in range(lanes):
-            out[h, j * 128:(j + 1) * 128, :] = turned[:, j:j + 1]
+    wide = own.shape[1]
+    for h, rows in enumerate((own, other)):
+        turned = rows[...].astype(f32).T
+        for j in range(out.shape[1] // wide):
+            out[h, j * wide:(j + 1) * wide, :] = turned[:, j:j + 1]
+
+
+def weigh(own, other, tokens):
+    rows, wide = own.shape
+    last = once((EXTRA, wide), lambda g: (rows // EXTRA - 1, 0))
+    return call(
+        weigh_body, "weigh_tokens", (), [(own, last), (other, last)],
+        [(sds((2, tokens, 1), f32), whole((2, tokens, 1)))],
+    )[0]
 
 
 def copy_body(x, out):
@@ -122,134 +135,135 @@
     return call(copy_body, "relay_rows", (), [(x, whole(x.shape))], [(sds(x.shape, x.dtype), whole(x.shape))], after=after)[0]
 
 
-def turn_body(pos, x, xt):
-    xt[...] = x[...].T
-
-
-def turn(pos, x, chips, rows):
-    tokens = x.shape[0]
-    tile = min(256, tokens)
-    return call(
-        turn_body, "turn_tokens", (pos,),
-        [(x, pl.BlockSpec((tile, rows), lambda s, t, m: (t, m[1 + s])))],
-        [(sds((chips * rows, tokens), bf16), pl.BlockSpec((rows, tile), lambda s, t, m: (s, t)))],
-        grid=(chips, tokens // tile),
-    )[0]
-
-
-def forward_body(offs, first_call, pos, *refs):
-    count = len(offs)
+def turn_block(pos, x, xt, t, tile):
+    rows = x.shape[1] // (pos.shape[0] - 1)
+    for s in range(xt.shape[0] // rows):
+        xt[s * rows:(s + 1) * rows, t:t + tile] = x[t:t + tile, columns(pos, 1 + s, 0, rows, rows)].T
+
+
+def columns(pos, slot, off, size, rows):
+    return pl.ds(pl.multiple_of(pos[slot] * rows + off, size), size)
+
+
+def turn_body(tile, pos, x, xt):
+    for t in range(0, x.shape[0], tile):
+        turn_block(pos, x, xt, t, tile)
+
+
+def stage_body(tile, pos, x, held, xt, sems):
+    copies = []
+    for n, t in enumerate(range(0, x.shape[0], tile)):
+        copy = pltpu.make_async_copy(x.at[pl.ds(t, tile), :], held.at[pl.ds(t, tile), :], sems.at[n])
+        copy.start()
+        copies.append(copy)
+    for n, t in enumerate(range(0, x.shape[0], tile)):
+        copies[n].wait()
+        turn_block(pos, held, xt, t, tile)
+
+
+def turn(pos, x, chips, stage):
+    tokens, depth = x.shape
+    tile = min(128, tokens)
+    xt = [(sds((depth // 2, tokens), bf16), whole((depth // 2, tokens)))]
+    if not stage:
+        return x, call(functools.partial(turn_body, tile), "turn_tokens", (pos,), [(x, whole(x.shape))], xt)[0]
+    return call(
+        functools.partial(stage_body, tile), "stage_tokens", (pos,), [(x, pl.BlockSpec(memory_space=pl.ANY))],
+        [(sds(x.shape, bf16), whole(x.shape))] + xt,
+        scratch=[pltpu.SemaphoreType.DMA((tokens // tile,))],
+    )
+
+
+def product(pos, x, low, slot, off, rows):
+    size = low.shape[0]
+    return dot(x[:, columns(pos, slot, off, size, rows)], low[...])
+
+
+def gram_sum(lows, before):
+    for low in lows:
+        dec = low[:, low.shape[1] // 2:]
+        term = dot_rows(dec, dec)
+        before = term if before is None else before + term
+    return before
+
+
+def forward_body(places, rows, first_call, pos, *refs):
     if first_call:
         acc_in = gram_in = None
     else:
         acc_in, gram_in, refs = refs[0], refs[1], refs[2:]
+    count = len(places)
     lows, xs = refs[:count], refs[count:count + 2]
     acc, gram = refs[count + 2:]
-    width = gram.shape[0]
-
-    def step(n):
-        low = lows[n][pl.ds(offs[n], xs[0].shape[1]), :]
-        term = dot_rows(low[:, width:], low[:, width:])
-        prods = [dot(x[...], low) for x in xs]
-        if n > 0:
-            gram[...] += term
-            for h in range(2):
-                acc[h] += prods[h]
-        elif first_call:
-            gram[...] = term
-            for h in range(2):
-                acc[h] = prods[h]
-        else:
-            gram[...] = gram_in[...] + term
-            for h in range(2):
-                acc[h] = acc_in[h] + prods[h]
-
-    for n in range(count):
-        pl.when(pl.program_id(0) == n)(functools.partial(step, n))
-
-
-def token_blocks(xs, pieces, sub):
-
-    def column(g, m):
-        at = 0
-        for n, (_, _, slot, part) in enumerate(pieces):
-            per = xs[0].shape[1] // (m.shape[0] - 1) // sub
-            at = jnp.where(g == n, m[slot] * per + part, at)
-        return (0, at)
-
-    return [(x, pl.BlockSpec((x.shape[0], sub), column)) for x in xs]
-
-
-def forward(pos, acc, gram, pieces, xs, sub, after=()):
+    gram[...] = gram_sum(lows, None if first_call else gram_in[...])
+    for h in range(2):
+        value = None if first_call else acc_in[h]
+        for low, (slot, off) in zip(lows, places):
+            term = product(pos, xs[h], low, slot, off, rows)
+            value = term if value is None else value + term
+        acc[h] = value
+
+
+def forward(pos, acc, gram, pieces, xs, rows, after=()):
     tokens = xs[0].shape[0]
     wide = pieces[0][0].shape[1]
     width = wide // 2
     ins = []
     if acc is not None:
         ins += [(acc, whole(acc.shape)), (gram, whole(gram.shape))]
-    ins += [(low, whole(low.shape)) for low, _, _, _ in pieces]
-    return call(
-        functools.partial(forward_body, [off for _, off, _, _ in pieces], acc is None), "forward_rows", (pos,),
-        ins + token_blocks(xs, pieces, sub),
+    ins += [(a, whole((min(a.shape[0], rows), wide))) for a, _, _ in pieces] + [(x, whole(x.shape)) for x in xs]
+    return call(
+        functools.partial(forward_body, [(slot, off) for _, slot, off in pieces], rows, acc is None),
+        "forward_rows", (pos,), ins,
         [(sds((2, tokens, wide), f32), whole((2, tokens, wide))), (sds((width, width), f32), whole((width, width)))],
-        grid=(len(pieces),), after=after,
-    )
-
-
-def finish_body(scale, tile, offs, pos, acc_in, gram_in, cw, *refs):
-    count = len(offs)
+        after=after,
+    )
+
+
+def finish_body(scale, tile, places, rows, pos, acc_in, gram_in, cw, *refs):
+    count = len(places)
     lows, xs = refs[:count], refs[count:count + 2]
-    slopes, w_hi, w_lo, acc, gram = refs[count + 2:]
+    slopes, w_hi, w_lo, acc = refs[count + 2:]
     width = gram_in.shape[0]
-
-    def step(n):
-        low = lows[n][pl.ds(offs[n], xs[0].shape[1]), :]
-        term = dot_rows(low[:, width:], low[:, width:])
-        before = (acc_in, gram_in) if n == 0 else (acc, gram)
-        gram[...] = before[1][...] + term
-        for h in range(2):
-            acc[h] = before[0][h] + dot(xs[h][...], low)
-
-    for n in range(count):
-        pl.when(pl.program_id(0) == n)(functools.partial(step, n))
-
-    @pl.when(pl.program_id(0) == count - 1)
-    def _():
-        g_all = gram[...]
-        g_hi = g_all.astype(bf16)
-        g_lo = (g_all - g_hi.astype(f32)).astype(bf16)
-        total = None
-        for h in range(2):
-            for t in range(0, acc.shape[1], tile):
-                at = pl.ds(t, tile)
-                pre = acc[h, at, :width]
-                sig = 0.5 + 0.5 * jnp.tanh(0.5 * pre)
-                hidden = (pre * sig).astype(bf16)
-                back = dot(hidden, g_hi) + dot(hidden, g_lo) - acc[h, at, width:]
-                weight = cw[h, at, :]
-                slope = (weight * scale) * back * (sig * (1.0 + pre * (1.0 - sig)))
-                counted = (weight * hidden.astype(f32)).astype(bf16)
-                slopes[h, at, :width] = slope.astype(bf16)
-                slopes[h, at, width:] = counted
-                term = dot_rows(counted, hidden)
-                total = term if total is None else total + term
-        hi = total.astype(bf16)
-        w_hi[...] = hi
-        w_lo[...] = (total - hi.astype(f32)).astype(bf16)
-
-
-def finish(pos, acc, gram, cw, pieces, xs, sub, scale):
+    gram = gram_sum(lows, gram_in[...])
+    g_hi = gram.astype(bf16)
+    g_lo = (gram - g_hi.astype(f32)).astype(bf16)
+    total = None
+    for h in range(2):
+        value = acc_in[h]
+        for low, (slot, off) in zip(lows, places):
+            value = value + product(pos, xs[h], low, slot, off, rows)
+        acc[h] = value
+        for t in range(0, acc.shape[1], tile):
+            at = pl.ds(t, tile)
+            pre = acc[h, at, :width]
+            sig = 0.5 + 0.5 * jnp.tanh(0.5 * pre)
+            hidden = (pre * sig).astype(bf16)
+            back = dot(hidden, g_hi) + dot(hidden, g_lo) - acc[h, at, width:]
+            weight = cw[h, at, :]
+            slope = (weight * scale) * back * (sig * (1.0 + pre * (1.0 - sig)))
+            counted = (weight * hidden.astype(f32)).astype(bf16)
+            slopes[h, at, :width] = slope.astype(bf16)
+            slopes[h, at, width:] = counted
+            term = dot_rows(counted, hidden)
+            total = term if total is None else total + term
+    hi = total.astype(bf16)
+    w_hi[...] = hi
+    w_lo[...] = (total - hi.astype(f32)).astype(bf16)
+
+
+def finish(pos, acc, gram, cw, pieces, xs, rows, scale):
     tokens = xs[0].shape[0]
     wide = pieces[0][0].shape[1]
     width = wide // 2
-    ins = [(a, whole(a.shape)) for a in [acc, gram, cw] + [low for low, _, _, _ in pieces]]
+    ins = [(a, whole(a.shape)) for a in [acc, gram, cw] + [low for low, _, _ in pieces] + list(xs)]
     square = (sds((width, width), bf16), whole((width, width)))
     return call(
-        functools.partial(finish_body, scale, min(256, tokens), [off for _, off, _, _ in pieces]), "finish_slopes", (pos,),
-        ins + token_blocks(xs, pieces, sub),
+        functools.partial(
+            finish_body, scale, min(256, tokens), [(slot, off) for _, slot, off in pieces], rows),
+        "finish_slopes", (pos,), ins,
         [(sds((2, tokens, wide), bf16), whole((2, tokens, wide))), square, square],
-        grid=(len(pieces),),
-        scratch=[pltpu.VMEM((2, tokens, wide), f32), pltpu.VMEM((width, width), f32)],
+        scratch=[pltpu.VMEM((2, tokens, wide), f32)],
     )
 
 
@@ -404,7 +418,8 @@
 
 def outer_body(pos, plan, anchor, momentum, *refs):
     quarters = refs[:4]
-    anchor_out, momentum_out = refs[4:]
+    anchor_out, momentum_out, token = refs[4:]
+    token[...] = jnp.zeros_like(token)
     frag = fragment(plan)
     anchor_out[...] = anchor[...]
     momentum_out[...] = momentum[...]
@@ -419,7 +434,7 @@
     return call(
         outer_body, "outer_step", (pos, plan),
         [(a, whole(a.shape)) for a in [anchor, momentum] + quarters],
-        [(sds(anchor.shape, f32), whole(anchor.shape))] * 2, after=after,
+        [(sds(anchor.shape, f32), whole(anchor.shape))] * 2 + [(sds((8, 128), f32), whole((8, 128)))], after=after,
     )
 
 
@@ -441,8 +456,8 @@
         a, "fsdp", [(f, ((f // 2 + s) % chips) * 2 + f % 2) for f in range(n_fsdp)])
     across = lambda a, bit: lax.ppermute(a, "replica", [(r, r ^ bit) for r in range(n_rep)])
 
-    blocks = [(i * cr, cr) for i in range(chunks)]
-    low_own = cast_rows(weights, 1)
+    low, more = cast_rows(weights, kinds)
+    low_own, low_send = [low], [more]
 
     chip = lax.axis_index("fsdp") // 2
     core = lax.axis_index("fsdp") % 2
@@ -450,51 +465,39 @@
     pos = jnp.stack([lax.axis_index("replica")] + [a + core for a in at] + [a + 1 - core for a in at]).astype(jnp.int32)
 
     x_par = to_partner(inputs)
-    xs = (inputs, x_par)
-    lanes = kinds.reshape(-1, 128)
-    cw = call(
-        weigh_body, "weigh_tokens", (),
-        [(lanes, whole(lanes.shape)), (to_partner(lanes), whole(lanes.shape))],
-        [(sds((2, tokens, 1), f32), whole((2, tokens, 1)))], after=low_own,
-    )[0]
+    low_near = [to_partner(more)]
+    cw = weigh(more, low_near[0], tokens)
 
     quarters = outer_start(pos, plan, anchor, weights, low_own)
-    xt = [turn(pos, x, chips, rows) for x in xs]
-    own = outer_add(plan, [quarters[0]] + [across(quarters[m], m) for m in range(1, 4)], n_rep == 4, [xt[0], cw])
+    xs, xt = zip(*[turn(pos, x, chips, stage) for x, stage in ((inputs, False), (x_par, True))])
+    own = outer_add(plan, [quarters[0]] + [across(quarters[m], m) for m in range(1, 4)], n_rep == 4, xt)
 
     state = [(weights, first_moment, second_moment)] * chunks
     state_block = list(range(chunks))
     new_anc = None
     for step in range(INNER):
         last = step == INNER - 1
-        def pieces(lows, slot, cut=sub):
-            return [
-                (low, off, slot, (j * low.shape[0] + off) // cut)
-                for j, low in enumerate(lows) for off in range(0, low.shape[0], cut)
-            ]
-
+        size = low_own[0].shape[0]
         low_far = {s: [fetch(low, s) for low in low_own] for s in range(1, chips)}
-        low_near = [to_partner(low) for low in low_own]
-        acc, gram = forward(pos, None, None, pieces(low_own, 1), xs, sub)
-        pending = pieces(low_near, 1 + chips)
+        if step:
+            low_near = [to_partner(low) for low in low_own]
+        acc, gram = forward(pos, None, None, [(low, 1, j * size) for j, low in enumerate(low_own)], xs, rows)
+        pending = [(low, 1 + chips, j * size) for j, low in enumerate(low_near)]
         if step == 0:
-            acc, gram = forward(pos, acc, gram, pending, xs, sub)
+            acc, gram = forward(pos, acc, gram, pending, xs, rows)
             pending = []
             bit = 4
             while bit < n_rep:
-                own = outer_add(plan, [own, across(own, bit)], 2 * bit == n_rep, [acc, xt[1]])
+                own = outer_add(plan, [own, across(own, bit)], 2 * bit == n_rep, [acc, cw])
                 bit *= 2
             ready = [own]
         for j in range(len(low_own)):
-            handed = {s: to_partner(relay(low_far[s][j], [acc] + ready)) for s in low_far}
-            place = lambda lows, slot: [
-                (low, off, slot + s, j * (rows // len(low_own)) // sub + off // sub)
-                for s, low in lows.items() for off in range(0, low.shape[0], sub)
-            ]
+            for s in low_far:
+                low_far[s][j] = relay(low_far[s][j], [acc] + ready)
             acc, gram = forward(
-                pos, acc, gram, pending + place({s: low_far[s][j] for s in low_far}, 1), xs, sub)
-            pending = place(handed, 1 + chips)
-        slopes, w_hi, w_lo = finish(pos, acc, gram, cw, pending, xs, sub, scale)
+                pos, acc, gram, pending + [(low_far[s][j], 1 + s, j * size) for s in low_far], xs, rows)
+            pending = [(to_partner(low_far[s][j]), 1 + chips + s, j * size) for s in low_far]
+        slopes, w_hi, w_lo = finish(pos, acc, gram, cw, pending, xs, rows, scale)
 
         mine, got, sent = [], [], []
         for i in range(chunks):
@@ -525,8 +528,8 @@
                 thetas = [t for t, _, _ in new_state[len(low_next) * (sub // cr):]]
                 low_next.append(mix_rows(plan, new_anc, len(low_next) * sub, thetas))
         if not last:
-            anchor_out, momentum_out = outer_end(pos, plan, anchor, momentum, quarters, low_next)
-            ready = [anchor_out]
+            anchor_out, momentum_out, token = outer_end(pos, plan, anchor, momentum, quarters, low_next)
+            ready = [token]
             state, state_block, low_own = new_state, [0] * chunks, low_next
     return (*prev, anchor_out, momentum_out)
 

time: 132 us -> 121 us (0.917)
  Pallas kernels: 69.8 us -> 53.8 us
  waiting for transfers between devices: 27.9 us -> 36.6 us
  starting transfers between devices: 28 us -> 25.4 us
    pallas_call x46, Pallas kernels: 69.8 us -> 53.8 us  [call(): pl.pallas_call(run, name=name, out_shape=[o for o, _ in outs], grid_spec=...]
    ppermute x3, waiting for transfers between devices: 5.3 us -> 12 us  [local(): lax.ppermute(a, 'fsdp', [((f // 2 + s) % chips * 2 + f % 2, f) for f in r...]
    ppermute x8, waiting for transfers between devices: 15.7 us -> 19.4 us  [local(): lax.ppermute(a, 'fsdp', [(f, (f // 2 + s) % chips * 2 + f % 2) for f in r...]
    ppermute x7, starting transfers between devices: 11.9 us -> 9.77 us  [local(): lax.ppermute(a, 'replica', [(r, r ^ bit) for r in range(n_rep)])]
    unnamed x22 -> x20, local copies, waits for them, and re-layouts: 4.81 us -> 3.9 us
  transfers between devices with their start and end apart: 26 -> 25, of which waited for: 11 -> 13; matrix products, arithmetic and copies ran while one was open for 0% -> 0% of each run, Pallas kernels for 48% -> 39%
where the time goes in v6:
time: 121 us
  Pallas kernels  53.8 us (44%)
  waiting for transfers between devices  36.6 us (30%)
  starting transfers between devices  25.4 us (21%)
  local copies, waits for them, and re-layouts  3.98 us (3%)
    pallas_call x46, Pallas kernels, call(): pl.pallas_call(run, name=name, out_shape=[o for o, _ in outs], grid_spec=...  53.8 us
    ppermute x8, waiting for transfers between devices, local(): lax.ppermute(a, 'fsdp', [(f, (f // 2 + s) % chips * 2 + f % 2) for f in r...  19.4 us
    ppermute x3, waiting for transfers between devices, local(): lax.ppermute(a, 'fsdp', [((f // 2 + s) % chips * 2 + f % 2, f) for f in r...  12 us
    ppermute x7, starting transfers between devices, local(): lax.ppermute(a, 'replica', [(r, r ^ bit) for r in range(n_rep)])  9.77 us
    ppermute x8, starting transfers between devices, local(): lax.ppermute(a, 'fsdp', [(f, (f // 2 + s) % chips * 2 + f % 2) for f in r...  8.56 us
    ppermute x3, starting transfers between devices, local(): lax.ppermute(a, 'fsdp', [((f // 2 + s) % chips * 2 + f % 2, f) for f in r...  6.14 us
    ppermute x7, waiting for transfers between devices, local(): lax.ppermute(a, 'replica', [(r, r ^ bit) for r in range(n_rep)])  5.2 us
    unnamed x20, local copies, waits for them, and re-layouts  3.9 us
  transfers between devices with their start and end apart: 25, of which 13 were waited for; matrix products, arithmetic and copies ran while one was open for 0% of the time, Pallas kernels for 39%

profile of v6, /device:TPU:0, one launch (start us, length us, event | category | flops | bytes accessed | tf_op | source)
XLA Modules:
  0.0 120.9 jit_solution(17693372028818798698)
XLA Ops:
  4.6 3.0 %collective-permute-start.9 = (bf16[1024,512]{1,0:T(8,128)(2,1)S(1)}, bf16[1024,512]{1,0:T(8,128)(2,1)}, u32[]{:S(2)}, u32[]{:S(2)}) collective-permute-start(bf16[1024,512]{1,0:T(8,128)(2,1)S(1)} %get-tuple-element.59.refs_4_.refs_1_.refs_5_), channel_id=1, source_target_pairs={{2,0},{3,1},{0,2},{1,3},{6,4},{7,5},{4,6},{5,7},{10,8},{11,9},{8,1... | collective-permute-start | bytes 3145736 | tf_op jit(solution)/shard_map/ppermute | solution.py:453
  14.7 2.9 %stage_tokens.1 = (bf16[512,4096]{1,0:T(8,128)(2,1)S(1)}, bf16[2048,512]{1,0:T(8,128)(2,1)S(1)}) custom-call(s32[5]{0:T(128)S(1)} %stack.23.refs_0_, bf16[512,4096]{1,0:T(8,128)(2,1)} %collective-permute-done.refs_1_), custom_call_target="tpu_custom_call" | custom-call | bytes 10485760 | tf_op jit(solution)/shard_map/stage_tokens/pallas_call | solution.py:60
  19.9 2.7 %collective-permute-start.4 = (bf16[256,256]{1,0:T(8,128)(2,1)S(1)}, bf16[256,256]{1,0:T(8,128)(2,1)S(1)}, u32[]{:S(2)}, u32[]{:S(2)}) collective-permute-start(bf16[256,256]{1,0:T(8,128)(2,1)S(1)} %add_quarters.2.refs_1_), channel_id=1, source_target_pairs={{0,16},{4,20},{8,24},{12,28},{16,0},{20,4},{24,8},{28,12},{1,17},{... | collective-permute-start | bytes 393224 | tf_op jit(solution)/shard_map/ppermute | solution.py:457
  23.4 2.0 %forward_rows.6 = (f32[2,512,512]{2,1,0:T(8,128)S(1)}, f32[256,256]{1,0:T(8,128)S(1)}) custom-call(s32[5]{0:T(128)S(1)} %stack.23.refs_0_, bf16[1024,512]{1,0:T(8,128)(2,1)S(1)} %get-tuple-element.59.refs_4_.refs_1_.refs_5_, bf16[512,4096]{1,0:T(8,128)(2,1)S(1)} %copy-done, bf16[512,4096]{1,0:T(8,128)(2,1)S(1)} %get-tuple-element.64.refs_3_.refs_5_.refs_6_.refs_4_.refs_7_), custom_call_target="tpu_custom_call" | custom-call | bytes 11796480 | tf_op jit(solution)/shard_map/forward_rows/pallas_call | solution.py:60
  25.4 3.2 %forward_rows.7 = (f32[2,512,512]{2,1,0:T(8,128)S(1)}, f32[256,256]{1,0:T(8,128)S(1)}) custom-call(s32[5]{0:T(128)S(1)} %stack.23.refs_0_, f32[2,512,512]{2,1,0:T(8,128)S(1)} %get-tuple-element.65.refs_1_, f32[256,256]{1,0:T(8,128)S(1)} %get-tuple-element.66.refs_2_, bf16[1040,512]{1,0:T(8,128)(2,1)} %collective-permute-done.5.refs_3_.refs_1_, ...), custom_call_target="tpu_custom_call" | custom-call | bytes 14155776 | tf_op jit(solution)/shard_map/forward_rows/pallas_call | solution.py:60
  35.8 2.0 %forward_rows.8 = (f32[2,512,512]{2,1,0:T(8,128)S(1)}, f32[256,256]{1,0:T(8,128)S(1)}) custom-call(s32[5]{0:T(128)S(1)} %stack.23.refs_0_, f32[2,512,512]{2,1,0:T(8,128)S(1)} %get-tuple-element.68.refs_3_.refs_1_, f32[256,256]{1,0:T(8,128)S(1)} %get-tuple-element.69.refs_2_, bf16[1024,512]{1,0:T(8,128)(2,1)S(1)} %relay_rows.3.refs_3_.refs_5_, ...), custom_call_target="tpu_custom_call" | custom-call | bytes 14155776 | tf_op jit(solution)/shard_map/forward_rows/pallas_call | solution.py:60
  37.7 2.5 %finish_slopes.2 = (bf16[2,512,512]{2,1,0:T(8,128)(2,1)S(1)}, bf16[256,256]{1,0:T(8,128)(2,1)S(1)}, bf16[256,256]{1,0:T(8,128)(2,1)S(1)}) custom-call(s32[5]{0:T(128)S(1)} %stack.23.refs_0_, f32[2,512,512]{2,1,0:T(8,128)S(1)} %get-tuple-element.70.refs_1_, f32[256,256]{1,0:T(8,128)S(1)} %get-tuple-element.71.refs_2_, ...), custom_call_target="tpu_custom_call" | custom-call | bytes 13111296 | tf_op jit(solution)/shard_map/finish_slopes/pallas_call | solution.py:60
  48.9 3.5 %collective-permute-done.8.refs_7_ = bf16[256,256]{1,0:T(8,128)(2,1)S(1)} collective-permute-done((bf16[256,256]{1,0:T(8,128)(2,1)S(1)}, bf16[256,256]{1,0:T(8,128)(2,1)S(1)}, u32[]{:S(2)}, u32[]{:S(2)}) %collective-permute-start.8) | collective-permute-done | bytes 131104 | tf_op jit(solution)/shard_map/ppermute | solution.py:457
  59.1 2.1 %collective-permute-done.13.refs_2_ = bf16[256,512]{1,0:T(8,128)(2,1)S(1)} collective-permute-done((bf16[256,512]{1,0:T(8,128)(2,1)S(1)}, bf16[256,512]{1,0:T(8,128)(2,1)S(1)}, u32[]{:S(2)}, u32[]{:S(2)}) %collective-permute-start.13) | collective-permute-done | bytes 262176 | tf_op jit(solution)/shard_map/ppermute | solution.py:455
  62.2 4.7 %collective-permute-done.14.refs_2_ = bf16[256,512]{1,0:T(8,128)(2,1)S(1)} collective-permute-done((bf16[256,512]{1,0:T(8,128)(2,1)S(1)}, bf16[256,512]{1,0:T(8,128)(2,1)S(1)}, u32[]{:S(2)}, u32[]{:S(2)}) %collective-permute-start.14) | collective-permute-done | bytes 262176 | tf_op jit(solution)/shard_map/ppermute | solution.py:455
  70.2 2.0 %forward_rows.9 = (f32[2,512,512]{2,1,0:T(8,128)S(1)}, f32[256,256]{1,0:T(8,128)S(1)}) custom-call(s32[5]{0:T(128)S(1)} %stack.23.refs_0_, bf16[512,512]{1,0:T(8,128)(2,1)S(1)} %mix_rows.2.refs_6_.refs_1_.refs_8_.refs_5_, bf16[512,512]{1,0:T(8,128)(2,1)S(1)} %mix_rows.3.refs_2_.refs_9_.refs_5_, bf16[512,4096]{1,0:T(8,128)(2,1)S(1)} %copy-done, ...), custom_call_target="tpu_custom_call" | custom-call | bytes 11796480 | tf_op jit(solution)/shard_map/forward_rows/pallas_call | solution.py:60
  72.2 3.1 %outer_step.1 = (f32[2,1024,256]{2,1,0:T(8,128)}, f32[2,1024,256]{2,1,0:T(8,128)}, f32[8,128]{1,0:T(8,128)S(1)}) custom-call(s32[5]{0:T(128)S(1)} %stack.23.refs_0_, s32[8]{0:T(128)S(1)} %copy-done.8, f32[2,1024,256]{2,1,0:T(8,128)S(1)} %copy-done.6, f32[2,1024,256]{2,1,0:T(8,128)S(1)} %copy-done.7, bf16[256,256]{1,0:T(8,128)(2,1)S(1)} %add_quarters.3.refs_2_.refs_4_, ...), custom_call_target="tpu_custom_call" | custom-call | bytes 8916992 | tf_op jit(solution)/shard_map/outer_step/pallas_call | solution.py:60
  75.2 2.8 %collective-permute-done.17.refs_0_ = bf16[512,512]{1,0:T(8,128)(2,1)S(1)} collective-permute-done((bf16[512,512]{1,0:T(8,128)(2,1)S(1)}, bf16[512,512]{1,0:T(8,128)(2,1)S(1)}, u32[]{:S(2)}, u32[]{:S(2)}) %collective-permute-start.17) | collective-permute-done | bytes 524320 | tf_op jit(solution)/shard_map/ppermute | solution.py:453
  78.2 2.6 %forward_rows.10 = (f32[2,512,512]{2,1,0:T(8,128)S(1)}, f32[256,256]{1,0:T(8,128)S(1)}) custom-call(s32[5]{0:T(128)S(1)} %stack.23.refs_0_, f32[2,512,512]{2,1,0:T(8,128)S(1)} %get-tuple-element.79.refs_1_, f32[256,256]{1,0:T(8,128)S(1)} %get-tuple-element.80.refs_2_, bf16[512,512]{1,0:T(8,128)(2,1)S(1)} %collective-permute-done.15.refs_3_, ...), custom_call_target="tpu_custom_call" | custom-call | bytes 14680064 | tf_op jit(solution)/shard_map/forward_rows/pallas_call | solution.py:60
  80.8 7.4 %collective-permute-done.19.refs_0_ = bf16[512,512]{1,0:T(8,128)(2,1)S(1)} collective-permute-done((bf16[512,512]{1,0:T(8,128)(2,1)S(1)}, bf16[512,512]{1,0:T(8,128)(2,1)S(1)}, u32[]{:S(2)}, u32[]{:S(2)}) %collective-permute-start.19) | collective-permute-done | bytes 524320 | tf_op jit(solution)/shard_map/ppermute | solution.py:453
  88.4 2.0 %forward_rows.11 = (f32[2,512,512]{2,1,0:T(8,128)S(1)}, f32[256,256]{1,0:T(8,128)S(1)}) custom-call(s32[5]{0:T(128)S(1)} %stack.23.refs_0_, f32[2,512,512]{2,1,0:T(8,128)S(1)} %get-tuple-element.82.refs_1_, f32[256,256]{1,0:T(8,128)S(1)} %get-tuple-element.83.refs_2_, bf16[512,512]{1,0:T(8,128)(2,1)S(1)} %collective-permute-done.18.refs_3_, ...), custom_call_target="tpu_custom_call" | custom-call | bytes 14155776 | tf_op jit(solution)/shard_map/forward_rows/pallas_call | solution.py:60
  90.4 2.2 %finish_slopes.3 = (bf16[2,512,512]{2,1,0:T(8,128)(2,1)S(1)}, bf16[256,256]{1,0:T(8,128)(2,1)S(1)}, bf16[256,256]{1,0:T(8,128)(2,1)S(1)}) custom-call(s32[5]{0:T(128)S(1)} %stack.23.refs_0_, f32[2,512,512]{2,1,0:T(8,128)S(1)} %get-tuple-element.84.refs_1_, f32[256,256]{1,0:T(8,128)S(1)} %get-tuple-element.85.refs_2_, ...), custom_call_target="tpu_custom_call" | custom-call | bytes 12587008 | tf_op jit(solution)/shard_map/finish_slopes/pallas_call | solution.py:60
  102.2 2.1 %adam_rows.12 = (f32[1,2,1024,256]{3,2,1,0:T(8,128)}, f32[1,2,1024,256]{3,2,1,0:T(8,128)}, f32[1,2,1024,256]{3,2,1,0:T(8,128)}) custom-call(s32[8]{0:T(128)S(1)} %copy-done.8, f32[256,512]{1,0:T(8,128)S(1)} %grad_rows.28.refs_6_.refs_1_, bf16[256,512]{1,0:T(8,128)(2,1)S(1)} %collective-permute-done.24.refs_2_, ...), custom_call_target="tpu_custom_call" | custom-call | bytes 8912896 | tf_op jit(solution)/shard_map/adam_rows/pallas_call | solution.py:60
  104.4 3.5 %collective-permute-done.23.refs_2_ = bf16[256,512]{1,0:T(8,128)(2,1)S(1)} collective-permute-done((bf16[256,512]{1,0:T(8,128)(2,1)S(1)}, bf16[256,512]{1,0:T(8,128)(2,1)S(1)}, u32[]{:S(2)}, u32[]{:S(2)}) %collective-permute-start.23) | collective-permute-done | bytes 262176 | tf_op jit(solution)/shard_map/ppermute | solution.py:455
  107.9 2.1 %adam_rows.13 = (f32[1,2,1024,256]{3,2,1,0:T(8,128)}, f32[1,2,1024,256]{3,2,1,0:T(8,128)}, f32[1,2,1024,256]{3,2,1,0:T(8,128)}) custom-call(s32[8]{0:T(128)S(1)} %copy-done.8, f32[256,512]{1,0:T(8,128)S(1)} %grad_rows.29.refs_6_.refs_1_, ...), custom_call_target="tpu_custom_call", output_to_operand_aliasing={{0}: (7, {}), {1}: (8, {}), {2}: (9, {})} | custom-call | bytes 15204352 | tf_op jit(solution)/shard_map/adam_rows/pallas_call | solution.py:60
  110.0 3.5 %collective-permute-done.22.refs_2_ = bf16[256,512]{1,0:T(8,128)(2,1)S(1)} collective-permute-done((bf16[256,512]{1,0:T(8,128)(2,1)S(1)}, bf16[256,512]{1,0:T(8,128)(2,1)S(1)}, u32[]{:S(2)}, u32[]{:S(2)}) %collective-permute-start.22) | collective-permute-done | bytes 262176 | tf_op jit(solution)/shard_map/ppermute | solution.py:455
  113.5 2.2 %adam_rows.14 = (f32[1,2,1024,256]{3,2,1,0:T(8,128)}, f32[1,2,1024,256]{3,2,1,0:T(8,128)}, f32[1,2,1024,256]{3,2,1,0:T(8,128)}) custom-call(s32[8]{0:T(128)S(1)} %copy-done.8, f32[256,512]{1,0:T(8,128)S(1)} %grad_rows.30.refs_6_.refs_1_, ...), custom_call_target="tpu_custom_call", output_to_operand_aliasing={{0}: (7, {}), {1}: (8, {}), {2}: (9, {})} | custom-call | bytes 15204352 | tf_op jit(solution)/shard_map/adam_rows/pallas_call | solution.py:60
  115.6 3.1 %collective-permute-done.21.refs_2_ = bf16[256,512]{1,0:T(8,128)(2,1)S(1)} collective-permute-done((bf16[256,512]{1,0:T(8,128)(2,1)S(1)}, bf16[256,512]{1,0:T(8,128)(2,1)S(1)}, u32[]{:S(2)}, u32[]{:S(2)}) %collective-permute-start.21) | collective-permute-done | bytes 262176 | tf_op jit(solution)/shard_map/ppermute | solution.py:455
  118.7 2.2 %adam_rows.15 = (f32[1,2,1024,256]{3,2,1,0:T(8,128)}, f32[1,2,1024,256]{3,2,1,0:T(8,128)}, f32[1,2,1024,256]{3,2,1,0:T(8,128)}) custom-call(s32[8]{0:T(128)S(1)} %copy-done.8, f32[256,512]{1,0:T(8,128)S(1)} %grad_rows.31.refs_1_, bf16[256,512]{1,0:T(8,128)(2,1)S(1)} %collective-permute-done.21.refs_2_, ...), custom_call_target="tpu_custom_call", output_to_operand_aliasing={{0}: (7, {}), {1}: (8, {}), {2}: (9, {})} | custom-call | bytes 15204352 | tf_op jit(solution)/shard_map/adam_rows/pallas_call | solution.py:60
  (93 shorter events, 50.7 us)
Async XLA Ops:
  0.6 12.5 %collective-permute-start = (bf16[512,4096]{1,0:T(8,128)(2,1)}, bf16[512,4096]{1,0:T(8,128)(2,1)}, u32[]{:S(2)}, u32[]{:S(2)}) collective-permute-start(bf16[512,4096]{1,0:T(8,128)(2,1)} %refs_5_.13), channel_id=1, source_target_pairs={{0,1},{1,0},{2,3},{3,2},{4,5},{5,4},{6,7},{7,6},{8,9},{9,8},{10,11... | collective-permute-start | bytes 12582920 | tf_op jit(solution)/shard_map/ppermute | solution.py:452
  4.6 18.0 %collective-permute-start.5 = (bf16[1040,512]{1,0:T(8,128)(2,1)}, bf16[1040,512]{1,0:T(8,128)(2,1)}, u32[]{:S(2)}, u32[]{:S(2)}) collective-permute-start(bf16[1040,512]{1,0:T(8,128)(2,1)} %get-tuple-element.67.refs_0_), channel_id=1, source_target_pairs={{0,1},{1,0},{2,3},{3,2},{4,5},{5,4},{6,7},{7,6},{8,9},{9,8},{10,11... | collective-permute-start | bytes 3194888 | tf_op jit(solution)/shard_map/ppermute | solution.py:452
  4.6 26.4 %collective-permute-start.9 = (bf16[1024,512]{1,0:T(8,128)(2,1)S(1)}, bf16[1024,512]{1,0:T(8,128)(2,1)}, u32[]{:S(2)}, u32[]{:S(2)}) collective-permute-start(bf16[1024,512]{1,0:T(8,128)(2,1)S(1)} %get-tuple-element.59.refs_4_.refs_1_.refs_5_), channel_id=1, source_target_pairs={{2,0},{3,1},{0,2},{1,3},{6,4},{7,5},{4,6},{5,7},{10,8},{11,9},{8,1... | collective-permute-start | bytes 3145736 | tf_op jit(solution)/shard_map/ppermute | solution.py:453
  10.0 7.6 %collective-permute-start.1 = (bf16[256,256]{1,0:T(8,128)(2,1)S(1)}, bf16[256,256]{1,0:T(8,128)(2,1)S(1)}, u32[]{:S(2)}, u32[]{:S(2)}) collective-permute-start(bf16[256,256]{1,0:T(8,128)(2,1)S(1)} %get-tuple-element.61), channel_id=1, source_target_pairs={{0,4},{4,0},{8,12},{12,8},{16,20},{20,16},{24,28},{28,24},{1,5},{5... | collective-permute-start | bytes 393224 | tf_op jit(solution)/shard_map/ppermute | solution.py:457
  11.5 6.3 %collective-permute-start.2 = (bf16[256,256]{1,0:T(8,128)(2,1)S(1)}, bf16[256,256]{1,0:T(8,128)(2,1)S(1)}, u32[]{:S(2)}, u32[]{:S(2)}) collective-permute-start(bf16[256,256]{1,0:T(8,128)(2,1)S(1)} %get-tuple-element.62), channel_id=1, source_target_pairs={{0,8},{4,12},{8,0},{12,4},{16,24},{20,28},{24,16},{28,20},{1,9},{5... | collective-permute-start | bytes 393224 | tf_op jit(solution)/shard_map/ppermute | solution.py:457
  13.1 6.2 %collective-permute-start.3 = (bf16[256,256]{1,0:T(8,128)(2,1)S(1)}, bf16[256,256]{1,0:T(8,128)(2,1)S(1)}, u32[]{:S(2)}, u32[]{:S(2)}) collective-permute-start(bf16[256,256]{1,0:T(8,128)(2,1)S(1)} %get-tuple-element.63), channel_id=1, source_target_pairs={{0,12},{4,8},{8,4},{12,0},{16,28},{20,24},{24,20},{28,16},{1,13},{... | collective-permute-start | bytes 393224 | tf_op jit(solution)/shard_map/ppermute | solution.py:457
  19.9 8.7 %collective-permute-start.4 = (bf16[256,256]{1,0:T(8,128)(2,1)S(1)}, bf16[256,256]{1,0:T(8,128)(2,1)S(1)}, u32[]{:S(2)}, u32[]{:S(2)}) collective-permute-start(bf16[256,256]{1,0:T(8,128)(2,1)S(1)} %add_quarters.2.refs_1_), channel_id=1, source_target_pairs={{0,16},{4,20},{8,24},{12,28},{16,0},{20,4},{24,8},{28,12},{1,17},{... | collective-permute-start | bytes 393224 | tf_op jit(solution)/shard_map/ppermute | solution.py:457
  32.3 5.4 %collective-permute-start.10 = (bf16[1024,512]{1,0:T(8,128)(2,1)S(1)}, bf16[1024,512]{1,0:T(8,128)(2,1)S(1)}, u32[]{:S(2)}, u32[]{:S(2)}) collective-permute-start(bf16[1024,512]{1,0:T(8,128)(2,1)S(1)} %relay_rows.3.refs_3_.refs_5_), channel_id=1, source_target_pairs={{0,1},{1,0},{2,3},{3,2},{4,5},{5,4},{6,7},{7,6},{8,9},{9,8},{10,11... | collective-permute-start | bytes 3145736 | tf_op jit(solution)/shard_map/ppermute | solution.py:452
  32.4 13.6 %collective-permute-start.6 = (bf16[256,256]{1,0:T(8,128)(2,1)S(1)}, bf16[256,256]{1,0:T(8,128)(2,1)S(1)}, u32[]{:S(2)}, u32[]{:S(2)}) collective-permute-start(bf16[256,256]{1,0:T(8,128)(2,1)S(1)} %add_quarters.3.refs_2_.refs_4_), channel_id=1, source_target_pairs={{0,4},{4,0},{8,12},{12,8},{16,20},{20,16},{24,28},{28,24},{1,5},{5... | collective-permute-start | bytes 393224 | tf_op jit(solution)/shard_map/ppermute | solution.py:457
  34.2 12.4 %collective-permute-start.7 = (bf16[256,256]{1,0:T(8,128)(2,1)S(1)}, bf16[256,256]{1,0:T(8,128)(2,1)S(1)}, u32[]{:S(2)}, u32[]{:S(2)}) collective-permute-start(bf16[256,256]{1,0:T(8,128)(2,1)S(1)} %add_quarters.3.refs_2_.refs_4_), channel_id=1, source_target_pairs={{0,8},{4,12},{8,0},{12,4},{16,24},{20,28},{24,16},{28,20},{1,9},{5... | collective-permute-start | bytes 393224 | tf_op jit(solution)/shard_map/ppermute | solution.py:457
  40.7 12.5 %collective-permute-start.11 = (bf16[256,512]{1,0:T(8,128)(2,1)S(1)}, bf16[256,512]{1,0:T(8,128)(2,1)S(1)}, u32[]{:S(2)}, u32[]{:S(2)}) collective-permute-start(bf16[256,512]{1,0:T(8,128)(2,1)S(1)} %grad_rows.16.refs_6_), channel_id=1, source_target_pairs={{0,2},{1,3},{2,0},{3,1},{4,6},{5,7},{6,4},{7,5},{8,10},{9,11},{10,... | collective-permute-start | bytes 786440 | tf_op jit(solution)/shard_map/ppermute | solution.py:455
  42.8 12.8 %collective-permute-start.12 = (bf16[256,512]{1,0:T(8,128)(2,1)S(1)}, bf16[256,512]{1,0:T(8,128)(2,1)S(1)}, u32[]{:S(2)}, u32[]{:S(2)}) collective-permute-start(bf16[256,512]{1,0:T(8,128)(2,1)S(1)} %grad_rows.17.refs_6_), channel_id=1, source_target_pairs={{0,2},{1,3},{2,0},{3,1},{4,6},{5,7},{6,4},{7,5},{8,10},{9,11},{10,... | collective-permute-start | bytes 786440 | tf_op jit(solution)/shard_map/ppermute | solution.py:455
  44.4 16.8 %collective-permute-start.13 = (bf16[256,512]{1,0:T(8,128)(2,1)S(1)}, bf16[256,512]{1,0:T(8,128)(2,1)S(1)}, u32[]{:S(2)}, u32[]{:S(2)}) collective-permute-start(bf16[256,512]{1,0:T(8,128)(2,1)S(1)} %grad_rows.18.refs_6_), channel_id=1, source_target_pairs={{0,2},{1,3},{2,0},{3,1},{4,6},{5,7},{6,4},{7,5},{8,10},{9,11},{10,... | collective-permute-start | bytes 786440 | tf_op jit(solution)/shard_map/ppermute | solution.py:455
  46.0 20.8 %collective-permute-start.14 = (bf16[256,512]{1,0:T(8,128)(2,1)S(1)}, bf16[256,512]{1,0:T(8,128)(2,1)S(1)}, u32[]{:S(2)}, u32[]{:S(2)}) collective-permute-start(bf16[256,512]{1,0:T(8,128)(2,1)S(1)} %grad_rows.19.refs_6_), channel_id=1, source_target_pairs={{0,2},{1,3},{2,0},{3,1},{4,6},{5,7},{6,4},{7,5},{8,10},{9,11},{10,... | collective-permute-start | bytes 786440 | tf_op jit(solution)/shard_map/ppermute | solution.py:455
  46.5 5.9 %collective-permute-start.8 = (bf16[256,256]{1,0:T(8,128)(2,1)S(1)}, bf16[256,256]{1,0:T(8,128)(2,1)S(1)}, u32[]{:S(2)}, u32[]{:S(2)}) collective-permute-start(bf16[256,256]{1,0:T(8,128)(2,1)S(1)} %add_quarters.3.refs_2_.refs_4_), channel_id=1, source_target_pairs={{0,12},{4,8},{8,4},{12,0},{16,28},{20,24},{24,20},{28,16},{1,13},{... | collective-permute-start | bytes 393224 | tf_op jit(solution)/shard_map/ppermute | solution.py:457
  57.5 20.7 %collective-permute-start.15 = (bf16[512,512]{1,0:T(8,128)(2,1)S(1)}, bf16[512,512]{1,0:T(8,128)(2,1)S(1)}, u32[]{:S(2)}, u32[]{:S(2)}) collective-permute-start(bf16[512,512]{1,0:T(8,128)(2,1)S(1)} %mix_rows.2.refs_6_.refs_1_.refs_8_.refs_5_), channel_id=1, source_target_pairs={{0,1},{1,0},{2,3},{3,2},{4,5},{5,4},{6,7},{7,6},{8,9},{9,8},{10,11... | collective-permute-start | bytes 1572872 | tf_op jit(solution)/shard_map/ppermute | solution.py:452
  57.5 20.5 %collective-permute-start.17 = (bf16[512,512]{1,0:T(8,128)(2,1)S(1)}, bf16[512,512]{1,0:T(8,128)(2,1)S(1)}, u32[]{:S(2)}, u32[]{:S(2)}) collective-permute-start(bf16[512,512]{1,0:T(8,128)(2,1)S(1)} %mix_rows.2.refs_6_.refs_1_.refs_8_.refs_5_), channel_id=1, source_target_pairs={{2,0},{3,1},{0,2},{1,3},{6,4},{7,5},{4,6},{5,7},{10,8},{11,9},{8,1... | collective-permute-start | bytes 1572872 | tf_op jit(solution)/shard_map/ppermute | solution.py:453
  68.5 9.7 %collective-permute-start.16 = (bf16[512,512]{1,0:T(8,128)(2,1)S(1)}, bf16[512,512]{1,0:T(8,128)(2,1)S(1)}, u32[]{:S(2)}, u32[]{:S(2)}) collective-permute-start(bf16[512,512]{1,0:T(8,128)(2,1)S(1)} %mix_rows.3.refs_2_.refs_9_.refs_5_), channel_id=1, source_target_pairs={{0,1},{1,0},{2,3},{3,2},{4,5},{5,4},{6,7},{7,6},{8,9},{9,8},{10,11... | collective-permute-start | bytes 1572872 | tf_op jit(solution)/shard_map/ppermute | solution.py:452
  68.6 19.6 %collective-permute-start.19 = (bf16[512,512]{1,0:T(8,128)(2,1)S(1)}, bf16[512,512]{1,0:T(8,128)(2,1)S(1)}, u32[]{:S(2)}, u32[]{:S(2)}) collective-permute-start(bf16[512,512]{1,0:T(8,128)(2,1)S(1)} %mix_rows.3.refs_2_.refs_9_.refs_5_), channel_id=1, source_target_pairs={{2,0},{3,1},{0,2},{1,3},{6,4},{7,5},{4,6},{5,7},{10,8},{11,9},{8,1... | collective-permute-start | bytes 1572872 | tf_op jit(solution)/shard_map/ppermute | solution.py:453
  78.1 10.2 %collective-permute-start.18 = (bf16[512,512]{1,0:T(8,128)(2,1)S(1)}, bf16[512,512]{1,0:T(8,128)(2,1)S(1)}, u32[]{:S(2)}, u32[]{:S(2)}) collective-permute-start(bf16[512,512]{1,0:T(8,128)(2,1)S(1)} %relay_rows.4.refs_5_), channel_id=1, source_target_pairs={{0,1},{1,0},{2,3},{3,2},{4,5},{5,4},{6,7},{7,6},{8,9},{9,8},{10,11... | collective-permute-start | bytes 1572872 | tf_op jit(solution)/shard_map/ppermute | solution.py:452
  93.1 9.2 %collective-permute-start.24 = (bf16[256,512]{1,0:T(8,128)(2,1)S(1)}, bf16[256,512]{1,0:T(8,128)(2,1)S(1)}, u32[]{:S(2)}, u32[]{:S(2)}) collective-permute-start(bf16[256,512]{1,0:T(8,128)(2,1)S(1)} %grad_rows.24.refs_6_), channel_id=1, source_target_pairs={{0,2},{1,3},{2,0},{3,1},{4,6},{5,7},{6,4},{7,5},{8,10},{9,11},{10,... | collective-permute-start | bytes 786440 | tf_op jit(solution)/shard_map/ppermute | solution.py:455
  95.2 12.7 %collective-permute-start.23 = (bf16[256,512]{1,0:T(8,128)(2,1)S(1)}, bf16[256,512]{1,0:T(8,128)(2,1)S(1)}, u32[]{:S(2)}, u32[]{:S(2)}) collective-permute-start(bf16[256,512]{1,0:T(8,128)(2,1)S(1)} %grad_rows.25.refs_6_), channel_id=1, source_target_pairs={{0,2},{1,3},{2,0},{3,1},{4,6},{5,7},{6,4},{7,5},{8,10},{9,11},{10,... | collective-permute-start | bytes 786440 | tf_op jit(solution)/shard_map/ppermute | solution.py:455
  96.3 17.2 %collective-permute-start.22 = (bf16[256,512]{1,0:T(8,128)(2,1)S(1)}, bf16[256,512]{1,0:T(8,128)(2,1)S(1)}, u32[]{:S(2)}, u32[]{:S(2)}) collective-permute-start(bf16[256,512]{1,0:T(8,128)(2,1)S(1)} %grad_rows.26.refs_6_), channel_id=1, source_target_pairs={{0,2},{1,3},{2,0},{3,1},{4,6},{5,7},{6,4},{7,5},{8,10},{9,11},{10,... | collective-permute-start | bytes 786440 | tf_op jit(solution)/shard_map/ppermute | solution.py:455
  98.4 20.3 %collective-permute-start.21 = (bf16[256,512]{1,0:T(8,128)(2,1)S(1)}, bf16[256,512]{1,0:T(8,128)(2,1)S(1)}, u32[]{:S(2)}, u32[]{:S(2)}) collective-permute-start(bf16[256,512]{1,0:T(8,128)(2,1)S(1)} %grad_rows.27.refs_6_), channel_id=1, source_target_pairs={{0,2},{1,3},{2,0},{3,1},{4,6},{5,7},{6,4},{7,5},{8,10},{9,11},{10,... | collective-permute-start | bytes 786440 | tf_op jit(solution)/shard_map/ppermute | solution.py:455
  (11 other events, 38.5 us)

commit v7 on v6

v7 whole, which is shorter than its diff:
```python
import functools
import math

import jax
import jax.numpy as jnp
from jax import lax
from jax.experimental import pallas as pl
from jax.experimental.pallas import tpu as pltpu
from jax.sharding import PartitionSpec as P

INNER = 2

inner_rate = 0.003
beta_one = 0.9
beta_two = 0.95
adam_eps = 1e-08
decay_rate = 0.1
outer_rate = 0.7
outer_mu = 0.9
mix_share = 0.5

bf16 = jnp.bfloat16
f32 = jnp.float32
VMEM_LIMIT = 16 * 1024 * 1024


def token_weight(kinds):
    return jnp.where(kinds == 2, 1.0, jnp.where(kinds == 1, 0.25, 0.0)).astype(f32)


def dot(a, b):
    return jnp.dot(a, b, preferred_element_type=f32)


def dot_rows(a, b):
    return lax.dot_general(a, b, (((0,), (0,)), ((), ())), preferred_element_type=f32)


def once(shape, index):
    return pl.BlockSpec(shape, index, pipeline_mode=pl.Buffered(1))


def whole(shape):
    return once(shape, lambda *_: (0,) * len(shape))


def sds(shape, dtype):
    return jax.ShapeDtypeStruct(shape, dtype)


def call(body, name, meta, ins, outs, grid=(1,), scratch=(), aliases=None, flops=0, after=()):
    arrays = [a for a, _ in ins] + list(after)
    n_in = len(meta) + len(ins)
    moved = sum(math.prod(o.shape) * o.dtype.itemsize for o, _ in outs)
    moved += sum(math.prod(s.block_shape or a.shape) * a.dtype.itemsize for a, s in ins)

    def run(*refs):
        body(*refs[:n_in], *refs[n_in + len(after):])

    return pl.pallas_call(
        run,
        name=name,
        out_shape=[o for o, _ in outs],
        grid_spec=pltpu.PrefetchScalarGridSpec(
            num_scalar_prefetch=len(meta),
            grid=grid,
            in_specs=[s for _, s in ins] + [pl.BlockSpec(memory_space=pl.ANY)] * len(after),
            out_specs=[s for _, s in outs],
            scratch_shapes=list(scratch),
        ),
        input_output_aliases=aliases or {},
        compiler_params=pltpu.CompilerParams(vmem_limit_bytes=VMEM_LIMIT),
        cost_estimate=pl.CostEstimate(flops=flops, bytes_accessed=moved, transcendentals=0),
    )(*meta, *arrays)


def plan_sum(plan):
    total = plan[0]
    for r in range(1, plan.shape[0]):
        total = total + plan[r]
    return total


def fragment(plan):
    return lax.rem(plan_sum(plan), 2)


EXTRA = 16


def cast_body(theta, *lows):
    for k, low in enumerate(lows):
        low[...] = theta[0, k].astype(bf16)


def cast_rows(weights):
    _, _, rows, width = weights.shape
    return call(
        cast_body, "cast_rows", (), [(weights, whole(weights.shape))],
        [(sds((rows, width), bf16), whole((rows, width)))] * 2,
    )


def extend_body(low, kinds, more):
    rows, width = low.shape
    more[:rows, :] = low[...]
    pad = jnp.zeros((EXTRA - kinds.shape[0], width), f32)
    more[rows:, :] = jnp.concatenate([token_weight(kinds[...]), pad], 0).astype(bf16)


def extend(low, kinds):
    rows, width = low.shape
    lanes = kinds.reshape(-1, width)
    shape = (rows + EXTRA, width)
    return call(
        extend_body, "extend_rows", (), [(a, whole(a.shape)) for a in (low, lanes)],
        [(sds(shape, bf16), whole(shape))],
    )[0]


def weigh_body(own, other, out):
    wide = own.shape[1]
    for h, rows in enumerate((own, other)):
        turned = rows[...].astype(f32).T
        for j in range(out.shape[1] // wide):
            out[h, j * wide:(j + 1) * wide, :] = turned[:, j:j + 1]


def weigh(own, other, tokens):
    rows, wide = own.shape
    last = once((EXTRA, wide), lambda g: (rows // EXTRA - 1, 0))
    return call(
        weigh_body, "weigh_tokens", (), [(own, last), (other, last)],
        [(sds((2, tokens, 1), f32), whole((2, tokens, 1)))],
    )[0]


def relay_body(x, *outs):
    size = outs[0].shape[0]
    for n, out in enumerate(outs):
        out[...] = x[n * size:(n + 1) * size, :]


def relay(x, cuts, after):
    shape = (x.shape[0] // cuts, x.shape[1])
    return call(
        relay_body, "relay_rows", (), [(x, whole(x.shape))],
        [(sds(shape, x.dtype), whole(shape))] * cuts, after=after,
    )


def turn_block(pos, x, xt, t, tile):
    rows = x.shape[1] // (pos.shape[0] - 1)
    for s in range(xt.shape[0] // rows):
        xt[s * rows:(s + 1) * rows, t:t + tile] = x[t:t + tile, columns(pos, 1 + s, 0, rows, rows)].T


def columns(pos, slot, off, size, rows):
    return pl.ds(pl.multiple_of(pos[slot] * rows + off, size), size)


def turn_body(tile, pos, x, xt):
    for t in range(0, x.shape[0], tile):
        turn_block(pos, x, xt, t, tile)


def stage_body(tile, pos, x, held, xt, sems):
    copies = []
    for n, t in enumerate(range(0, x.shape[0], tile)):
        copy = pltpu.make_async_copy(x.at[pl.ds(t, tile), :], held.at[pl.ds(t, tile), :], sems.at[n])
        copy.start()
        copies.append(copy)
    for n, t in enumerate(range(0, x.shape[0], tile)):
        copies[n].wait()
        turn_block(pos, held, xt, t, tile)


def turn(pos, x, chips, stage):
    tokens, depth = x.shape
    tile = min(128, tokens)
    xt = [(sds((depth // 2, tokens), bf16), whole((depth // 2, tokens)))]
    if not stage:
        return x, call(functools.partial(turn_body, tile), "turn_tokens", (pos,), [(x, whole(x.shape))], xt)[0]
    return call(
        functools.partial(stage_body, tile), "stage_tokens", (pos,), [(x, pl.BlockSpec(memory_space=pl.ANY))],
        [(sds(x.shape, bf16), whole(x.shape))] + xt,
        scratch=[pltpu.SemaphoreType.DMA((tokens // tile,))],
    )


def product(pos, x, low, place, rows):
    slot, off, size = place
    return dot(x[:, columns(pos, slot, off, size, rows)], low[:size, :])


def gram_sum(lows, before):
    for low in lows:
        term = dot_rows(low[...], low[...])
        before = term if before is None else before + term
    return before


def forward_body(places, rows, with_gram, first_call, pos, *refs):
    carry = 2 if with_gram else 1
    before = (None, None) if first_call else refs[:carry]
    if not first_call:
        refs = refs[carry:]
    count = len(places)
    lows, xs = refs[:count], refs[count:count + 2]
    outs = refs[count + 2:]
    if with_gram:
        outs[1][...] = gram_sum(lows, None if first_call else before[1][...])
    for h in range(2):
        value = None if first_call else before[0][h]
        for low, place in zip(lows, places):
            term = product(pos, xs[h], low, place, rows)
            value = term if value is None else value + term
        outs[0][h] = value


def forward(pos, carry, pieces, xs, rows, with_gram, after=()):
    tokens = xs[0].shape[0]
    width = pieces[0][0].shape[1]
    ins = [(a, whole(a.shape)) for a in carry]
    ins += [(p[0], whole((p[3], width))) for p in pieces] + [(x, whole(x.shape)) for x in xs]
    shapes = [(2, tokens, width)] + [(width, width)] * with_gram
    return call(
        functools.partial(forward_body, [p[1:] for p in pieces], rows, with_gram, not carry),
        "forward_decoder" if with_gram else "forward_encoder", (pos,), ins,
        [(sds(shape, f32), whole(shape)) for shape in shapes], after=after,
    )


def split(total):
    hi = total.astype(bf16)
    return hi, (total - hi.astype(f32)).astype(bf16)


def hidden_body(scale, tile, places, rows, pos, acc_in, cw, *refs):
    count = len(places)
    lows, xs = refs[:count], refs[count:count + 2]
    hidden_out, slope_out, counted_out, w_hi, w_lo, acc = refs[count + 2:]
    total = None
    for h in range(2):
        value = acc_in[h]
        for low, place in zip(lows, places):
            value = value + product(pos, xs[h], low, place, rows)
        acc[h] = value
        for t in range(0, acc.shape[1], tile):
            at = pl.ds(t, tile)
            pre = acc[h, at, :]
            sig = 0.5 + 0.5 * jnp.tanh(0.5 * pre)
            hidden = (pre * sig).astype(bf16)
            weight = cw[h, at, :]
            counted = (weight * hidden.astype(f32)).astype(bf16)
            hidden_out[h, at, :] = hidden
            slope_out[h, at, :] = (weight * scale) * (sig * (1.0 + pre * (1.0 - sig)))
            counted_out[h, at, :] = counted
            term = dot_rows(counted, hidden)
            total = term if total is None else total + term
    w_hi[...], w_lo[...] = split(total)


def hidden_rows(pos, acc, cw, pieces, xs, rows, scale):
    shape = acc.shape
    width = shape[2]
    ins = [(a, whole(a.shape)) for a in [acc, cw] + [p[0] for p in pieces] + list(xs)]
    square = (sds((width, width), bf16), whole((width, width)))
    return call(
        functools.partial(hidden_body, scale, min(256, shape[1]), [p[1:] for p in pieces], rows),
        "hidden_units", (pos,), ins,
        [(sds(shape, bf16), whole(shape)), (sds(shape, f32), whole(shape)), (sds(shape, bf16), whole(shape)), square, square],
        scratch=[pltpu.VMEM(shape, f32)],
    )


def slope_body(places, rows, pos, acc_in, gram_in, hidden, slope, *refs):
    count = len(places)
    lows, xs, out = refs[:count], refs[count:count + 2], refs[count + 2]
    g_hi, g_lo = split(gram_sum(lows, gram_in[...]))
    for h in range(2):
        value = acc_in[h]
        for low, place in zip(lows, places):
            value = value + product(pos, xs[h], low, place, rows)
        back = dot(hidden[h], g_hi) + dot(hidden[h], g_lo) - value
        out[h] = (slope[h] * back).astype(bf16)


def slope_rows(pos, acc, gram, hidden, slope, pieces, xs, rows):
    ins = [(a, whole(a.shape)) for a in [acc, gram, hidden, slope] + [p[0] for p in pieces] + list(xs)]
    return call(
        functools.partial(slope_body, [p[1:] for p in pieces], rows), "slope_pre", (pos,), ins,
        [(sds(acc.shape, bf16), whole(acc.shape))],
    )[0]


def encoder_body(xt_own, xt_par, slopes, out):
    out[...] = (dot(xt_own[...], slopes[0]) + dot(xt_par[...], slopes[1])).astype(out.dtype)


def decoder_body(scale, xt_own, xt_par, counted, w_hi, w_lo, low, out):
    dec = low[...]
    both = dot(xt_own[...], counted[0]) + dot(xt_par[...], counted[1])
    out[...] = (scale * (dot(dec, w_hi[...]) + dot(dec, w_lo[...]) - both)).astype(out.dtype)


def grad_rows(body, name, block, cr, xt, others, dtype, after=()):
    tokens = xt[0].shape[1]
    width = others[0].shape[2]
    ins = [(x, once((cr, tokens), lambda g: (block, 0))) for x in xt]
    ins += [(a, whole(a.shape)) for a in others]
    return call(body, name, (), ins, [(sds((cr, width), dtype), whole((cr, width)))], after=after)[0]


def adam_body(last, count, k, i, n_low, plan, own, *refs):
    got = refs[:count]
    theta, first, second = refs[count:3 + count]
    refs = refs[3 + count:]
    grad = own[...]
    for g in got:
        grad = grad + g[...].astype(f32)
    one = beta_one * first[0, 0] + (1.0 - beta_one) * grad
    two = beta_two * second[0, 0] + (1.0 - beta_two) * grad * grad
    old = theta[0, 0]
    if last:
        old = mixed(plan, k, old, refs[0][...])
    new = old - inner_rate * (one / (jnp.sqrt(two) + adam_eps) + decay_rate * old)
    if n_low is not None:
        cr = own.shape[0]
        anchor, before, low = refs[0], refs[1:1 + n_low], refs[1 + n_low]
        for j, b in enumerate(before):
            low[j * cr:(j + 1) * cr, :] = b[...]
        low[n_low * cr:(n_low + 1) * cr, :] = mixed(plan, k, new, anchor[i * cr:(i + 1) * cr, :]).astype(bf16)
    theta_out, first_out, second_out = refs[-3:]
    theta_out[0, 0] = new
    first_out[0, 0] = one
    second_out[0, 0] = two


def mixed(plan, k, theta, anchor):
    return jnp.where(fragment(plan) == k, mix_share * theta + (1.0 - mix_share) * anchor, theta)


def adam_rows(plan, k, i, own, got, state, at, new_anc, prev, full, last, lows=None, after=()):
    cr, width = own.shape
    block = (1, 1, cr, width)
    ins = [(g, whole(g.shape)) for g in [own] + got]
    ins += [(s, once(block, lambda g, m: (0, at[0], at[1], 0))) for s in state]
    aliases = {}
    outs = []
    if last:
        ins.append((new_anc, once((cr, width), lambda g, m: (i, 0))))
        if prev is not None:
            for n, p in enumerate(prev):
                aliases[1 + len(ins)] = n
                ins.append((p, pl.BlockSpec(memory_space=pl.ANY)))
        outs = [(sds(full, f32), once(block, lambda g, m: (0, k, i, 0)))] * 3
    else:
        if lows is not None:
            ins += [(a, whole(a.shape)) for a in [new_anc] + lows]
            shape = (cr * (1 + len(lows)), width)
            outs = [(sds(shape, bf16), whole(shape))]
        outs += [(sds(block, f32), whole(block))] * 3
    return call(
        functools.partial(adam_body, last, len(got), k, i, None if lows is None else len(lows)), "adam_rows",
        (plan,), ins, outs, aliases=aliases, after=after,
    )


def quarter(pos, m, size):
    where = jnp.bitwise_xor(lax.rem(pos[0], 4), m)
    return pl.ds(pl.multiple_of(where * size, size), size)


def delta_body(pos, plan, anchor, theta, *outs):
    count = plan[pos[0]].astype(f32)
    for m, out in enumerate(outs):
        at = quarter(pos, m, out.shape[0])
        out[...] = (count * (anchor[0, at, :] - theta[0, 0, at, :])).astype(out.dtype)


def outer_start(pos, plan, anchor, weights, after):
    _, rows, width = anchor.shape
    part = (rows // 4, width)
    return call(
        delta_body, "delta_quarters", (pos, plan),
        [
            (anchor, once((1, rows, width), lambda g, p, q: (fragment(q), 0, 0))),
            (weights, once((1, 1, rows, width), lambda g, p, q: (0, fragment(q), 0, 0))),
        ],
        [(sds(part, f32), whole(part))] + [(sds(part, bf16), whole(part))] * 3, after=after,
    )


def add_body(final, plan, *refs):
    total = refs[0][...].astype(f32)
    for r in refs[1:-1]:
        total = total + r[...].astype(f32)
    if final:
        total = total / plan_sum(plan).astype(f32)
    refs[-1][...] = total.astype(bf16)


def outer_add(plan, parts, final, after=()):
    shape = parts[0].shape
    return call(
        functools.partial(add_body, final), "add_quarters", (plan,), [(a, whole(shape)) for a in parts],
        [(sds(shape, bf16), whole(shape))], after=after,
    )[0]


def outer_update(frag, at, anchor, momentum, grad):
    mom = outer_mu * momentum[frag, at, :] + grad
    return anchor[frag, at, :] - outer_rate * (grad + outer_mu * mom), mom


def new_anchor_body(pos, plan, anchor, momentum, *refs):
    for m, piece in enumerate(refs[:4]):
        at = quarter(pos, m, piece.shape[0])
        refs[4][at, :] = outer_update(0, at, anchor, momentum, piece[...].astype(f32))[0]


def outer_anchor(pos, plan, anchor, momentum, quarters, after):
    _, rows, width = anchor.shape
    part = once((1, rows, width), lambda g, p, q: (fragment(q), 0, 0))
    return call(
        new_anchor_body, "new_anchor", (pos, plan),
        [(anchor, part), (momentum, part)] + [(a, whole(a.shape)) for a in quarters],
        [(sds((rows, width), f32), whole((rows, width)))], after=after,
    )[0]


def mix_body(k, plan, new_anc, theta, low):
    low[...] = mixed(plan, k, theta[0, 0], new_anc[...]).astype(bf16)


def mix_rows(plan, new_anc, k, theta, after):
    shape = new_anc.shape
    return call(
        functools.partial(mix_body, k), "mix_rows", (plan,), [(a, whole(a.shape)) for a in (new_anc, theta)],
        [(sds(shape, bf16), whole(shape))], after=after,
    )[0]


def outer_body(pos, plan, anchor, momentum, *refs):
    quarters = refs[:4]
    anchor_out, momentum_out, token = refs[4:]
    token[...] = jnp.zeros_like(token)
    frag = fragment(plan)
    anchor_out[...] = anchor[...]
    momentum_out[...] = momentum[...]
    for m, piece in enumerate(quarters):
        at = quarter(pos, m, piece.shape[0])
        anc, mom = outer_update(frag, at, anchor, momentum, piece[...].astype(f32))
        anchor_out[frag, at, :] = anc
        momentum_out[frag, at, :] = mom


def outer_end(pos, plan, anchor, momentum, quarters, after):
    return call(
        outer_body, "outer_step", (pos, plan),
        [(a, whole(a.shape)) for a in [anchor, momentum] + quarters],
        [(sds(anchor.shape, f32), whole(anchor.shape))] * 2 + [(sds((8, 128), f32), whole((8, 128)))], after=after,
    )


def local(n_rep, n_fsdp, inputs, kinds, weights, first_moment, second_moment, anchor, momentum, plan):
    tokens = inputs.shape[0]
    rows, width = weights.shape[2:]
    chips = n_fsdp // 2
    scale = 1.0 / math.sqrt(tokens * n_fsdp)
    chunks = max(1, rows // 512)
    cr = rows // chunks
    cuts = chunks
    cut = rows // cuts
    others = range(1, chips)

    partner = [(f, f ^ 1) for f in range(n_fsdp)]
    to_partner = lambda a: lax.ppermute(a, "fsdp", partner)
    fetch = lambda a, s: lax.ppermute(
        a, "fsdp", [(((f // 2 + s) % chips) * 2 + f % 2, f) for f in range(n_fsdp)])
    give = lambda a, s: lax.ppermute(
        a, "fsdp", [(f, ((f // 2 + s) % chips) * 2 + f % 2) for f in range(n_fsdp)])
    across = lambda a, bit: lax.ppermute(a, "replica", [(r, r ^ bit) for r in range(n_rep)])

    enc, dec = cast_rows(weights)

    chip = lax.axis_index("fsdp") // 2
    core = lax.axis_index("fsdp") % 2
    at = [((chip + s) % chips) * 2 for s in range(chips)]
    pos = jnp.stack([lax.axis_index("replica")] + [a + core for a in at] + [a + 1 - core for a in at]).astype(jnp.int32)

    x_par = to_partner(inputs)
    more = extend(enc, kinds)
    enc_near = to_partner(more)
    cw = weigh(more, enc_near, tokens)

    quarters = outer_start(pos, plan, anchor, weights, [enc])
    xs, xt = zip(*[turn(pos, x, chips, stage) for x, stage in ((inputs, False), (x_par, True))])
    own = outer_add(plan, [quarters[0]] + [across(quarters[m], m) for m in range(1, 4)], n_rep == 4, xt)

    blocks = [(1, 0)] + [(0, i) for i in range(chunks)]
    state = {key: (weights, first_moment, second_moment) for key in blocks}
    state_at = {key: key for key in blocks}
    new_anc = None
    for step in range(INNER):
        last = step == INNER - 1
        enc_far = {s: fetch(enc, s) for s in others}
        dec_far = {s: fetch(dec, s) for s in others}
        if step:
            enc_near = to_partner(enc)
        dec_near = to_partner(dec)

        carry = forward(pos, [], [(enc, 1, 0, rows)], xs, rows, False)
        carry = forward(pos, list(carry), [(enc_near, 1 + chips, 0, rows)], xs, rows, False)
        ready = [cw, own, *xt] if step == 0 else [token]
        part = [(p, 1 + s, n * cut, cut) for s in others for n, p in enumerate(relay(enc_far[s], cuts, [*carry, *ready]))]
        pending = [(to_partner(p), slot + chips, off, size) for p, slot, off, size in part]
        carry = forward(pos, carry, part, xs, rows, False)
        hidden, slope, counted, w_hi, w_lo = hidden_rows(pos, carry[0], cw, pending, xs, rows, scale)
        if step == 0:
            bit = 4
            while bit < n_rep:
                own = outer_add(plan, [own, across(own, bit)], 2 * bit == n_rep)
                bit *= 2

        dec_grad = lambda block, low, dtype, after: grad_rows(
            functools.partial(decoder_body, scale), "decoder_grad", block, rows, xt,
            [counted, w_hi, w_lo, low], dtype, after)
        enc_grad = lambda block, dtype, after: grad_rows(
            encoder_body, "encoder_grad", block, cr, xt, [slopes], dtype, after)
        sent = [own] if step == 0 else []
        got = {key: [] for key in blocks}
        for s in others:
            sent.append(dec_grad(s, dec_far[s], bf16, sent[-1:]))
            got[1, 0].append(give(sent[-1], s))

        carry = forward(pos, [], [(dec, 1, 0, rows)], xs, rows, True, sent[-1:])
        carry = forward(pos, carry, [(dec_near, 1 + chips, 0, rows)], xs, rows, True)
        part = [(p, 1 + s, n * cut, cut) for s in others for n, p in enumerate(relay(dec_far[s], cuts, sent[-1:]))]
        pending = [(to_partner(p), slot + chips, off, size) for p, slot, off, size in part]
        carry = forward(pos, carry, part, xs, rows, True)
        slopes = slope_rows(pos, *carry, hidden, slope, pending, xs, rows)
        for i in range(chunks):
            for s in others:
                sent.append(enc_grad(s * chunks + i, bf16, sent[-1:]))
                got[0, i].append(give(sent[-1], s))
        mine = {(1, 0): dec_grad(0, dec, f32, sent[-1:])}
        for i in range(chunks):
            mine[0, i] = enc_grad(i, f32, sent[-1:])

        if not last:
            quarters = [own] + [across(own, m) for m in range(1, 4)]
            new_anc = outer_anchor(pos, plan, anchor, momentum, quarters, [mine[1, 0]])
        new_state, prev, lows, after = {}, None, [], []
        for key in blocks:
            k, i = key
            more_out = [] if last or k else [lows]
            res = adam_rows(
                plan, k, i, mine[key], got[key], state[key], state_at[key], new_anc, prev, weights.shape, last,
                *more_out, after=after)
            if last:
                prev = res
                continue
            if k == 0:
                lows = lows + [res[0]]
            new_state[key] = tuple(res[-3:])
            after = [] if k == 0 else [res[0]]
        if not last:
            enc = lows[-1]
            dec = mix_rows(plan, new_anc, 1, new_state[1, 0][0], [enc])
            anchor_out, momentum_out, token = outer_end(pos, plan, anchor, momentum, quarters, [dec])
            state, state_at = new_state, {key: (0, 0) for key in blocks}
    return (*prev, anchor_out, momentum_out)


def solution(mesh):
    return jax.shard_map(
        functools.partial(local, mesh.shape["replica"], mesh.shape["fsdp"]),
        mesh=mesh,
        in_specs=(
            P(("replica", "fsdp"), None),
            P(("replica", "fsdp")),
            P("replica", None, "fsdp", None),
            P("replica", None, "fsdp", None),
            P("replica", None, "fsdp", None),
            P(None, "fsdp", None),
            P(None, "fsdp", None),
            P(),
        ),
        out_specs=(
            P("replica", None, "fsdp", None),
            P("replica", None, "fsdp", None),
            P("replica", None, "fsdp", None),
            P(None, "fsdp", None),
            P(None, "fsdp", None),
        ),
        check_vma=False,
    )
```

time: 121 us -> 122 us (level)
  waiting for transfers between devices: 36.6 us -> 31.5 us
  Pallas kernels: 53.8 us -> 58 us
    ppermute x8 -> x6, waiting for transfers between devices: 19.4 us -> 9.88 us  [local(): lax.ppermute(a, 'fsdp', [(f, (f // 2 + s) % chips * 2 + f % 2) for f in r...]
    pallas_call x46 -> x49, Pallas kernels: 53.8 us -> 58 us  [call(): pl.pallas_call(run, name=name, out_shape=[o for o, _ in outs], grid_spec=...]
    ppermute x7, waiting for transfers between devices: 5.2 us -> 8.69 us  [local(): lax.ppermute(a, 'replica', [(r, r ^ bit) for r in range(n_rep)])]
    ppermute x7 -> x13, starting transfers between devices: 0.93 us -> 3.07 us  [local(): to_partner = lambda a: lax.ppermute(a, 'fsdp', partner)]
    ppermute x8 -> x6, starting transfers between devices: 8.56 us -> 7.49 us  [local(): lax.ppermute(a, 'fsdp', [(f, (f // 2 + s) % chips * 2 + f % 2) for f in r...]
    ppermute x3 -> x4, starting transfers between devices: 6.14 us -> 5.16 us  [local(): lax.ppermute(a, 'fsdp', [((f // 2 + s) % chips * 2 + f % 2, f) for f in r...]
    ppermute x3 -> x4, waiting for transfers between devices: 12 us -> 12.8 us  [local(): lax.ppermute(a, 'fsdp', [((f // 2 + s) % chips * 2 + f % 2, f) for f in r...]
    unnamed x20 -> x22, local copies, waits for them, and re-layouts: 3.9 us -> 4.01 us
  transfers between devices with their start and end apart: 25 -> 30, of which waited for: 13 -> 10; matrix products, arithmetic and copies ran while one was open for 0% -> 1% of each run, Pallas kernels for 39% -> 45%
where the time goes in v7:
time: 122 us; the launch traced here: 121 us
  Pallas kernels  58 us (48%)
  waiting for transfers between devices  31.5 us (26%)
  starting transfers between devices  25.8 us (21%)
  local copies, waits for them, and re-layouts  4.79 us (4%)
    pallas_call x49, Pallas kernels, call(): pl.pallas_call(run, name=name, out_shape=[o for o, _ in outs], grid_spec=...  58 us
    ppermute x4, waiting for transfers between devices, local(): lax.ppermute(a, 'fsdp', [((f // 2 + s) % chips * 2 + f % 2, f) for f in r...  12.8 us
    ppermute x7, starting transfers between devices, local(): lax.ppermute(a, 'replica', [(r, r ^ bit) for r in range(n_rep)])  10.1 us
    ppermute x6, waiting for transfers between devices, local(): lax.ppermute(a, 'fsdp', [(f, (f // 2 + s) % chips * 2 + f % 2) for f in r...  9.88 us
    ppermute x7, waiting for transfers between devices, local(): lax.ppermute(a, 'replica', [(r, r ^ bit) for r in range(n_rep)])  8.69 us
    ppermute x6, starting transfers between devices, local(): lax.ppermute(a, 'fsdp', [(f, (f // 2 + s) % chips * 2 + f % 2) for f in r...  7.49 us
    ppermute x4, starting transfers between devices, local(): lax.ppermute(a, 'fsdp', [((f // 2 + s) % chips * 2 + f % 2, f) for f in r...  5.16 us
    unnamed x22, local copies, waits for them, and re-layouts  4.01 us
  transfers between devices with their start and end apart: 30, of which 10 were waited for; matrix products, arithmetic and copies ran while one was open for 1% of the time, Pallas kernels for 45%

profile of v7, /device:TPU:0, one launch (start us, length us, event | category | flops | bytes accessed | tf_op | source)
XLA Modules:
  0.0 121.3 jit_solution(11533366526901540834)
XLA Ops:
  5.2 3.0 %collective-permute-start.9 = (bf16[1024,256]{1,0:T(8,128)(2,1)S(1)}, bf16[1024,256]{1,0:T(8,128)(2,1)}, u32[]{:S(2)}, u32[]{:S(2)}) collective-permute-start(bf16[1024,256]{1,0:T(8,128)(2,1)S(1)} %get-tuple-element.67.refs_4_.refs_1_.refs_0_), channel_id=1, source_target_pairs={{2,0},{3,1},{0,2},{1,3},{6,4},{7,5},{4,6},{5,7},{10,8},{11,9},{8,1... | collective-permute-start | bytes 1572872 | tf_op jit(solution)/shard_map/ppermute | solution.py:480
  8.3 1.6 %copy-done.3 = f32[2,1024,256]{2,1,0:T(8,128)S(1)} copy-done((f32[2,1024,256]{2,1,0:T(8,128)S(1)}, f32[2,1024,256]{2,1,0:T(8,128)}, u32[]{:S(2)}) %copy-start.3) | copy-done | bytes 2097176
  10.6 2.0 %collective-permute-start.1 = (bf16[256,256]{1,0:T(8,128)(2,1)S(1)}, bf16[256,256]{1,0:T(8,128)(2,1)S(1)}, u32[]{:S(2)}, u32[]{:S(2)}) collective-permute-start(bf16[256,256]{1,0:T(8,128)(2,1)S(1)} %get-tuple-element.69), channel_id=1, source_target_pairs={{0,4},{4,0},{8,12},{12,8},{16,20},{20,16},{24,28},{28,24},{1,5},{5... | collective-permute-start | bytes 393224 | tf_op jit(solution)/shard_map/ppermute | solution.py:484
  16.3 2.9 %stage_tokens.1 = (bf16[512,4096]{1,0:T(8,128)(2,1)S(1)}, bf16[2048,512]{1,0:T(8,128)(2,1)S(1)}) custom-call(s32[5]{0:T(128)S(1)} %stack.23.refs_0_, bf16[512,4096]{1,0:T(8,128)(2,1)} %collective-permute-done.refs_1_), custom_call_target="tpu_custom_call" | custom-call | bytes 10485760 | tf_op jit(solution)/shard_map/stage_tokens/pallas_call | solution.py:60
  24.2 3.0 %collective-permute-start.4 = (bf16[256,256]{1,0:T(8,128)(2,1)S(1)}, bf16[256,256]{1,0:T(8,128)(2,1)S(1)}, u32[]{:S(2)}, u32[]{:S(2)}) collective-permute-start(bf16[256,256]{1,0:T(8,128)(2,1)S(1)} %add_quarters.2.refs_1_.refs_3_), channel_id=1, source_target_pairs={{0,16},{4,20},{8,24},{12,28},{16,0},{20,4},{24,8},{28,12},{1,17},{... | collective-permute-start | bytes 393224 | tf_op jit(solution)/shard_map/ppermute | solution.py:484
  28.4 5.6 %collective-permute-done.4.refs_2_ = bf16[256,256]{1,0:T(8,128)(2,1)S(1)} collective-permute-done((bf16[256,256]{1,0:T(8,128)(2,1)S(1)}, bf16[256,256]{1,0:T(8,128)(2,1)S(1)}, u32[]{:S(2)}, u32[]{:S(2)}) %collective-permute-start.4) | collective-permute-done | bytes 131104 | tf_op jit(solution)/shard_map/ppermute | solution.py:484
  34.6 2.3 %hidden_units.2 = (bf16[2,512,256]{2,1,0:T(8,128)(2,1)S(1)}, f32[2,512,256]{2,1,0:T(8,128)S(1)}, bf16[2,512,256]{2,1,0:T(8,128)(2,1)S(1)}, bf16[256,256]{1,0:T(8,128)(2,1)S(1)}, bf16[256,256]{1,0:T(8,128)(2,1)S(1)}) custom-call(s32[5]{0:T(128)S(1)} %stack.23.refs_0_, f32[2,512,256]{2,1,0:T(8,128)S(1)} %forward_encoder.8.refs_1_, ...), custom_call_target="tpu_custom_call" | custom-call | bytes 12324864 | tf_op jit(solution)/shard_map/hidden_units/pallas_call | solution.py:60
  37.0 2.0 %decoder_grad.4.refs_4_.refs_1_.refs_3_ = bf16[1024,256]{1,0:T(8,128)(2,1)S(1)} custom-call(bf16[2048,512]{1,0:T(8,128)(2,1)S(1)} %turn_tokens.1.refs_5_.refs_4_.refs_0_, bf16[2048,512]{1,0:T(8,128)(2,1)S(1)} %get-tuple-element.66.refs_6_.refs_5_.refs_1_, bf16[2,512,256]{2,1,0:T(8,128)(2,1)S(1)} %get-tuple-element.75.refs_2_, ...), custom_call_target="tpu_custom_call" | custom-call | bytes 3932160 | tf_op jit(solution)/shard_map/decoder_grad/pallas_call | solution.py:60
  48.1 1.9 %slope_pre.2.refs_2_ = bf16[2,512,256]{2,1,0:T(8,128)(2,1)S(1)} custom-call(s32[5]{0:T(128)S(1)} %stack.23.refs_0_, f32[2,512,256]{2,1,0:T(8,128)S(1)} %get-tuple-element.85.refs_1_, f32[256,256]{1,0:T(8,128)S(1)} %get-tuple-element.86.refs_2_, bf16[2,512,256]{2,1,0:T(8,128)(2,1)S(1)} %get-tuple-element.87.refs_3_, ...), custom_call_target="tpu_custom_call" | custom-call | bytes 12320768 | tf_op jit(solution)/shard_map/slope_pre/pallas_call | solution.py:60
  57.1 1.7 %collective-permute-done.6.refs_6_ = bf16[256,256]{1,0:T(8,128)(2,1)S(1)} collective-permute-done((bf16[256,256]{1,0:T(8,128)(2,1)S(1)}, bf16[256,256]{1,0:T(8,128)(2,1)S(1)}, u32[]{:S(2)}, u32[]{:S(2)}) %collective-permute-start.6) | collective-permute-done | bytes 131104 | tf_op jit(solution)/shard_map/ppermute | solution.py:484
  63.3 2.5 %collective-permute-done.17.refs_2_ = bf16[512,256]{1,0:T(8,128)(2,1)S(1)} collective-permute-done((bf16[512,256]{1,0:T(8,128)(2,1)S(1)}, bf16[512,256]{1,0:T(8,128)(2,1)S(1)}, u32[]{:S(2)}, u32[]{:S(2)}) %collective-permute-start.17) | collective-permute-done | bytes 262176 | tf_op jit(solution)/shard_map/ppermute | solution.py:482
  67.0 1.7 %collective-permute-start.20 = (bf16[1024,256]{1,0:T(8,128)(2,1)S(1)}, bf16[1024,256]{1,0:T(8,128)(2,1)S(1)}, u32[]{:S(2)}, u32[]{:S(2)}) collective-permute-start(bf16[1024,256]{1,0:T(8,128)(2,1)S(1)} %get-tuple-element.91.refs_3_.refs_1_), channel_id=1, source_target_pairs={{2,0},{3,1},{0,2},{1,3},{6,4},{7,5},{4,6},{5,7},{10,8},{11,9},{8,1... | collective-permute-start | bytes 1572872 | tf_op jit(solution)/shard_map/ppermute | solution.py:480
  71.0 3.1 %outer_step.1 = (f32[2,1024,256]{2,1,0:T(8,128)}, f32[2,1024,256]{2,1,0:T(8,128)}, f32[8,128]{1,0:T(8,128)S(1)}) custom-call(s32[5]{0:T(128)S(1)} %stack.23.refs_0_, s32[8]{0:T(128)S(1)} %copy-done.10, f32[2,1024,256]{2,1,0:T(8,128)S(1)} %copy-done.4, f32[2,1024,256]{2,1,0:T(8,128)S(1)} %copy-done.7, bf16[256,256]{1,0:T(8,128)(2,1)S(1)} %add_quarters.3.refs_6_.refs_4_, ...), custom_call_target="tpu_custom_call" | custom-call | bytes 8916992 | tf_op jit(solution)/shard_map/outer_step/pallas_call | solution.py:60
  75.4 6.4 %collective-permute-done.20.refs_0_ = bf16[1024,256]{1,0:T(8,128)(2,1)S(1)} collective-permute-done((bf16[1024,256]{1,0:T(8,128)(2,1)S(1)}, bf16[1024,256]{1,0:T(8,128)(2,1)S(1)}, u32[]{:S(2)}, u32[]{:S(2)}) %collective-permute-start.20) | collective-permute-done | bytes 524320 | tf_op jit(solution)/shard_map/ppermute | solution.py:480
  83.8 2.3 %hidden_units.3 = (bf16[2,512,256]{2,1,0:T(8,128)(2,1)S(1)}, f32[2,512,256]{2,1,0:T(8,128)S(1)}, bf16[2,512,256]{2,1,0:T(8,128)(2,1)S(1)}, bf16[256,256]{1,0:T(8,128)(2,1)S(1)}, bf16[256,256]{1,0:T(8,128)(2,1)S(1)}) custom-call(s32[5]{0:T(128)S(1)} %stack.23.refs_0_, f32[2,512,256]{2,1,0:T(8,128)S(1)} %forward_encoder.11.refs_1_, ...), custom_call_target="tpu_custom_call" | custom-call | bytes 12324864 | tf_op jit(solution)/shard_map/hidden_units/pallas_call | solution.py:60
  86.1 6.4 %collective-permute-done.23.refs_5_.refs_0_ = bf16[1024,256]{1,0:T(8,128)(2,1)S(1)} collective-permute-done((bf16[1024,256]{1,0:T(8,128)(2,1)S(1)}, bf16[1024,256]{1,0:T(8,128)(2,1)S(1)}, u32[]{:S(2)}, u32[]{:S(2)}) %collective-permute-start.23) | collective-permute-done | bytes 524320 | tf_op jit(solution)/shard_map/ppermute | solution.py:480
  100.0 1.9 %slope_pre.3.refs_2_ = bf16[2,512,256]{2,1,0:T(8,128)(2,1)S(1)} custom-call(s32[5]{0:T(128)S(1)} %stack.23.refs_0_, f32[2,512,256]{2,1,0:T(8,128)S(1)} %get-tuple-element.104.refs_1_, f32[256,256]{1,0:T(8,128)S(1)} %get-tuple-element.105.refs_2_, bf16[2,512,256]{2,1,0:T(8,128)(2,1)S(1)} %get-tuple-element.106.refs_3_, ...), custom_call_target="tpu_custom_call" | custom-call | bytes 12320768 | tf_op jit(solution)/shard_map/slope_pre/pallas_call | solution.py:60
  103.3 1.6 %collective-permute-start.27 = (bf16[512,256]{1,0:T(8,128)(2,1)S(1)}, bf16[512,256]{1,0:T(8,128)(2,1)S(1)}, u32[]{:S(2)}, u32[]{:S(2)}) collective-permute-start(bf16[512,256]{1,0:T(8,128)(2,1)S(1)} %encoder_grad.13.refs_3_.refs_6_), channel_id=1, source_target_pairs={{0,2},{1,3},{2,0},{3,1},{4,6},{5,7},{6,4},{7,5},{8,10},{9,11},{10,... | collective-permute-start | bytes 786440 | tf_op jit(solution)/shard_map/ppermute | solution.py:482
  107.0 1.9 %collective-permute-done.29.refs_2_ = bf16[1024,256]{1,0:T(8,128)(2,1)S(1)} collective-permute-done((bf16[1024,256]{1,0:T(8,128)(2,1)S(1)}, bf16[1024,256]{1,0:T(8,128)(2,1)S(1)}, u32[]{:S(2)}, u32[]{:S(2)}) %collective-permute-start.29) | collective-permute-done | bytes 524320 | tf_op jit(solution)/shard_map/ppermute | solution.py:482
  108.9 2.8 %adam_rows.9 = (f32[1,2,1024,256]{3,2,1,0:T(8,128)}, f32[1,2,1024,256]{3,2,1,0:T(8,128)}, f32[1,2,1024,256]{3,2,1,0:T(8,128)}) custom-call(s32[8]{0:T(128)S(1)} %copy-done.10, f32[1024,256]{1,0:T(8,128)S(1)} %decoder_grad.7.refs_1_, bf16[1024,256]{1,0:T(8,128)(2,1)S(1)} %collective-permute-done.29.refs_2_, ...), custom_call_target="tpu_custom_call" | custom-call | bytes 12058624 | tf_op jit(solution)/shard_map/adam_rows/pallas_call | solution.py:60
  111.8 2.8 %collective-permute-done.28.refs_2_ = bf16[512,256]{1,0:T(8,128)(2,1)S(1)} collective-permute-done((bf16[512,256]{1,0:T(8,128)(2,1)S(1)}, bf16[512,256]{1,0:T(8,128)(2,1)S(1)}, u32[]{:S(2)}, u32[]{:S(2)}) %collective-permute-start.28) | collective-permute-done | bytes 262176 | tf_op jit(solution)/shard_map/ppermute | solution.py:482
  114.5 2.0 %adam_rows.10 = (f32[1,2,1024,256]{3,2,1,0:T(8,128)}, f32[1,2,1024,256]{3,2,1,0:T(8,128)}, f32[1,2,1024,256]{3,2,1,0:T(8,128)}) custom-call(s32[8]{0:T(128)S(1)} %copy-done.10, f32[512,256]{1,0:T(8,128)S(1)} %encoder_grad.15.refs_1_, ...), custom_call_target="tpu_custom_call", output_to_operand_aliasing={{0}: (7, {}), {1}: (8, {}), {2}: (9, {})} | custom-call | bytes 15466496 | tf_op jit(solution)/shard_map/adam_rows/pallas_call | solution.py:60
  116.5 2.7 %collective-permute-done.27.refs_2_ = bf16[512,256]{1,0:T(8,128)(2,1)S(1)} collective-permute-done((bf16[512,256]{1,0:T(8,128)(2,1)S(1)}, bf16[512,256]{1,0:T(8,128)(2,1)S(1)}, u32[]{:S(2)}, u32[]{:S(2)}) %collective-permute-start.27) | collective-permute-done | bytes 262176 | tf_op jit(solution)/shard_map/ppermute | solution.py:482
  119.3 2.0 %adam_rows.11 = (f32[1,2,1024,256]{3,2,1,0:T(8,128)}, f32[1,2,1024,256]{3,2,1,0:T(8,128)}, f32[1,2,1024,256]{3,2,1,0:T(8,128)}) custom-call(s32[8]{0:T(128)S(1)} %copy-done.10, f32[512,256]{1,0:T(8,128)S(1)} %encoder_grad.14.refs_1_, ...), custom_call_target="tpu_custom_call", output_to_operand_aliasing={{0}: (7, {}), {1}: (8, {}), {2}: (9, {})} | custom-call | bytes 15466496 | tf_op jit(solution)/shard_map/adam_rows/pallas_call | solution.py:60
  (109 shorter events, 54.0 us)
Async XLA Ops:
  0.6 13.6 %collective-permute-start = (bf16[512,4096]{1,0:T(8,128)(2,1)}, bf16[512,4096]{1,0:T(8,128)(2,1)}, u32[]{:S(2)}, u32[]{:S(2)}) collective-permute-start(bf16[512,4096]{1,0:T(8,128)(2,1)} %refs_7_.3), channel_id=1, source_target_pairs={{0,1},{1,0},{2,3},{3,2},{4,5},{5,4},{6,7},{7,6},{8,9},{9,8},{10,11... | collective-permute-start | bytes 12582920 | tf_op jit(solution)/shard_map/ppermute | solution.py:479
  5.2 7.4 %collective-permute-start.8 = (bf16[1040,256]{1,0:T(8,128)(2,1)}, bf16[1040,256]{1,0:T(8,128)(2,1)S(1)}, u32[]{:S(2)}, u32[]{:S(2)}) collective-permute-start(bf16[1040,256]{1,0:T(8,128)(2,1)} %extend_rows.1.refs_0_), channel_id=1, source_target_pairs={{0,1},{1,0},{2,3},{3,2},{4,5},{5,4},{6,7},{7,6},{8,9},{9,8},{10,11... | collective-permute-start | bytes 1597448 | tf_op jit(solution)/shard_map/ppermute | solution.py:479
  5.2 17.1 %collective-permute-start.9 = (bf16[1024,256]{1,0:T(8,128)(2,1)S(1)}, bf16[1024,256]{1,0:T(8,128)(2,1)}, u32[]{:S(2)}, u32[]{:S(2)}) collective-permute-start(bf16[1024,256]{1,0:T(8,128)(2,1)S(1)} %get-tuple-element.67.refs_4_.refs_1_.refs_0_), channel_id=1, source_target_pairs={{2,0},{3,1},{0,2},{1,3},{6,4},{7,5},{4,6},{5,7},{10,8},{11,9},{8,1... | collective-permute-start | bytes 1572872 | tf_op jit(solution)/shard_map/ppermute | solution.py:480
  8.2 28.8 %collective-permute-start.12 = (bf16[1024,256]{1,0:T(8,128)(2,1)}, bf16[1024,256]{1,0:T(8,128)(2,1)}, u32[]{:S(2)}, u32[]{:S(2)}) collective-permute-start(bf16[1024,256]{1,0:T(8,128)(2,1)} %copy-done.8), channel_id=1, source_target_pairs={{2,0},{3,1},{0,2},{1,3},{6,4},{7,5},{4,6},{5,7},{10,8},{11,9},{8,1... | collective-permute-start | bytes 1572872 | tf_op jit(solution)/shard_map/ppermute | solution.py:480
  10.6 11.1 %collective-permute-start.1 = (bf16[256,256]{1,0:T(8,128)(2,1)S(1)}, bf16[256,256]{1,0:T(8,128)(2,1)S(1)}, u32[]{:S(2)}, u32[]{:S(2)}) collective-permute-start(bf16[256,256]{1,0:T(8,128)(2,1)S(1)} %get-tuple-element.69), channel_id=1, source_target_pairs={{0,4},{4,0},{8,12},{12,8},{16,20},{20,16},{24,28},{28,24},{1,5},{5... | collective-permute-start | bytes 393224 | tf_op jit(solution)/shard_map/ppermute | solution.py:484
  12.6 9.1 %collective-permute-start.2 = (bf16[256,256]{1,0:T(8,128)(2,1)S(1)}, bf16[256,256]{1,0:T(8,128)(2,1)S(1)}, u32[]{:S(2)}, u32[]{:S(2)}) collective-permute-start(bf16[256,256]{1,0:T(8,128)(2,1)S(1)} %get-tuple-element.70), channel_id=1, source_target_pairs={{0,8},{4,12},{8,0},{12,4},{16,24},{20,28},{24,16},{28,20},{1,9},{5... | collective-permute-start | bytes 393224 | tf_op jit(solution)/shard_map/ppermute | solution.py:484
  14.2 7.5 %collective-permute-start.3 = (bf16[256,256]{1,0:T(8,128)(2,1)S(1)}, bf16[256,256]{1,0:T(8,128)(2,1)S(1)}, u32[]{:S(2)}, u32[]{:S(2)}) collective-permute-start(bf16[256,256]{1,0:T(8,128)(2,1)S(1)} %get-tuple-element.71), channel_id=1, source_target_pairs={{0,12},{4,8},{8,4},{12,0},{16,28},{20,24},{24,20},{28,16},{1,13},{... | collective-permute-start | bytes 393224 | tf_op jit(solution)/shard_map/ppermute | solution.py:484
  23.5 11.1 %collective-permute-start.10 = (bf16[512,256]{1,0:T(8,128)(2,1)S(1)}, bf16[512,256]{1,0:T(8,128)(2,1)S(1)}, u32[]{:S(2)}, u32[]{:S(2)}) collective-permute-start(bf16[512,256]{1,0:T(8,128)(2,1)S(1)} %get-tuple-element.73.refs_2_), channel_id=1, source_target_pairs={{0,1},{1,0},{2,3},{3,2},{4,5},{5,4},{6,7},{7,6},{8,9},{9,8},{10,11... | collective-permute-start | bytes 786440 | tf_op jit(solution)/shard_map/ppermute | solution.py:479
  23.6 11.0 %collective-permute-start.11 = (bf16[512,256]{1,0:T(8,128)(2,1)S(1)}, bf16[512,256]{1,0:T(8,128)(2,1)S(1)}, u32[]{:S(2)}, u32[]{:S(2)}) collective-permute-start(bf16[512,256]{1,0:T(8,128)(2,1)S(1)} %get-tuple-element.74.refs_3_), channel_id=1, source_target_pairs={{0,1},{1,0},{2,3},{3,2},{4,5},{5,4},{6,7},{7,6},{8,9},{9,8},{10,11... | collective-permute-start | bytes 786440 | tf_op jit(solution)/shard_map/ppermute | solution.py:479
  24.1 21.1 %collective-permute-start.13 = (bf16[1024,256]{1,0:T(8,128)(2,1)S(1)}, bf16[1024,256]{1,0:T(8,128)(2,1)S(1)}, u32[]{:S(2)}, u32[]{:S(2)}) collective-permute-start(bf16[1024,256]{1,0:T(8,128)(2,1)S(1)} %copy-done.9), channel_id=1, source_target_pairs={{0,1},{1,0},{2,3},{3,2},{4,5},{5,4},{6,7},{7,6},{8,9},{9,8},{10,11... | collective-permute-start | bytes 1572872 | tf_op jit(solution)/shard_map/ppermute | solution.py:479
  24.2 9.9 %collective-permute-start.4 = (bf16[256,256]{1,0:T(8,128)(2,1)S(1)}, bf16[256,256]{1,0:T(8,128)(2,1)S(1)}, u32[]{:S(2)}, u32[]{:S(2)}) collective-permute-start(bf16[256,256]{1,0:T(8,128)(2,1)S(1)} %add_quarters.2.refs_1_.refs_3_), channel_id=1, source_target_pairs={{0,16},{4,20},{8,24},{12,28},{16,0},{20,4},{24,8},{28,12},{1,17},{... | collective-permute-start | bytes 393224 | tf_op jit(solution)/shard_map/ppermute | solution.py:484
  40.1 7.9 %collective-permute-start.14 = (bf16[512,256]{1,0:T(8,128)(2,1)S(1)}, bf16[512,256]{1,0:T(8,128)(2,1)S(1)}, u32[]{:S(2)}, u32[]{:S(2)}) collective-permute-start(bf16[512,256]{1,0:T(8,128)(2,1)S(1)} %get-tuple-element.83.refs_3_), channel_id=1, source_target_pairs={{0,1},{1,0},{2,3},{3,2},{4,5},{5,4},{6,7},{7,6},{8,9},{9,8},{10,11... | collective-permute-start | bytes 786440 | tf_op jit(solution)/shard_map/ppermute | solution.py:479
  40.2 7.9 %collective-permute-start.15 = (bf16[512,256]{1,0:T(8,128)(2,1)S(1)}, bf16[512,256]{1,0:T(8,128)(2,1)S(1)}, u32[]{:S(2)}, u32[]{:S(2)}) collective-permute-start(bf16[512,256]{1,0:T(8,128)(2,1)S(1)} %get-tuple-element.84.refs_4_), channel_id=1, source_target_pairs={{0,1},{1,0},{2,3},{3,2},{4,5},{5,4},{6,7},{7,6},{8,9},{9,8},{10,11... | collective-permute-start | bytes 786440 | tf_op jit(solution)/shard_map/ppermute | solution.py:479
  40.7 20.2 %collective-permute-start.16 = (bf16[1024,256]{1,0:T(8,128)(2,1)S(1)}, bf16[1024,256]{1,0:T(8,128)(2,1)S(1)}, u32[]{:S(2)}, u32[]{:S(2)}) collective-permute-start(bf16[1024,256]{1,0:T(8,128)(2,1)S(1)} %decoder_grad.4.refs_4_.refs_1_.refs_3_), channel_id=1, source_target_pairs={{0,2},{1,3},{2,0},{3,1},{4,6},{5,7},{6,4},{7,5},{8,10},{9,11},{10,... | collective-permute-start | bytes 1572872 | tf_op jit(solution)/shard_map/ppermute | solution.py:482
  42.3 11.4 %collective-permute-start.5 = (bf16[256,256]{1,0:T(8,128)(2,1)S(1)}, bf16[256,256]{1,0:T(8,128)(2,1)S(1)}, u32[]{:S(2)}, u32[]{:S(2)}) collective-permute-start(bf16[256,256]{1,0:T(8,128)(2,1)S(1)} %add_quarters.3.refs_6_.refs_4_), channel_id=1, source_target_pairs={{0,4},{4,0},{8,12},{12,8},{16,20},{20,16},{24,28},{28,24},{1,5},{5... | collective-permute-start | bytes 393224 | tf_op jit(solution)/shard_map/ppermute | solution.py:484
  50.4 11.9 %collective-permute-start.18 = (bf16[512,256]{1,0:T(8,128)(2,1)S(1)}, bf16[512,256]{1,0:T(8,128)(2,1)S(1)}, u32[]{:S(2)}, u32[]{:S(2)}) collective-permute-start(bf16[512,256]{1,0:T(8,128)(2,1)S(1)} %encoder_grad.8.refs_3_), channel_id=1, source_target_pairs={{0,2},{1,3},{2,0},{3,1},{4,6},{5,7},{6,4},{7,5},{8,10},{9,11},{10,... | collective-permute-start | bytes 786440 | tf_op jit(solution)/shard_map/ppermute | solution.py:482
  51.4 14.4 %collective-permute-start.17 = (bf16[512,256]{1,0:T(8,128)(2,1)S(1)}, bf16[512,256]{1,0:T(8,128)(2,1)S(1)}, u32[]{:S(2)}, u32[]{:S(2)}) collective-permute-start(bf16[512,256]{1,0:T(8,128)(2,1)S(1)} %encoder_grad.9.refs_6_.refs_3_), channel_id=1, source_target_pairs={{0,2},{1,3},{2,0},{3,1},{4,6},{5,7},{6,4},{7,5},{8,10},{9,11},{10,... | collective-permute-start | bytes 786440 | tf_op jit(solution)/shard_map/ppermute | solution.py:482
  66.9 7.2 %collective-permute-start.19 = (bf16[1024,256]{1,0:T(8,128)(2,1)S(1)}, bf16[1024,256]{1,0:T(8,128)(2,1)S(1)}, u32[]{:S(2)}, u32[]{:S(2)}) collective-permute-start(bf16[1024,256]{1,0:T(8,128)(2,1)S(1)} %get-tuple-element.91.refs_3_.refs_1_), channel_id=1, source_target_pairs={{0,1},{1,0},{2,3},{3,2},{4,5},{5,4},{6,7},{7,6},{8,9},{9,8},{10,11... | collective-permute-start | bytes 1572872 | tf_op jit(solution)/shard_map/ppermute | solution.py:479
  67.0 14.8 %collective-permute-start.20 = (bf16[1024,256]{1,0:T(8,128)(2,1)S(1)}, bf16[1024,256]{1,0:T(8,128)(2,1)S(1)}, u32[]{:S(2)}, u32[]{:S(2)}) collective-permute-start(bf16[1024,256]{1,0:T(8,128)(2,1)S(1)} %get-tuple-element.91.refs_3_.refs_1_), channel_id=1, source_target_pairs={{2,0},{3,1},{0,2},{1,3},{6,4},{7,5},{4,6},{5,7},{10,8},{11,9},{8,1... | collective-permute-start | bytes 1572872 | tf_op jit(solution)/shard_map/ppermute | solution.py:480
  69.3 23.2 %collective-permute-start.23 = (bf16[1024,256]{1,0:T(8,128)(2,1)S(1)}, bf16[1024,256]{1,0:T(8,128)(2,1)S(1)}, u32[]{:S(2)}, u32[]{:S(2)}) collective-permute-start(bf16[1024,256]{1,0:T(8,128)(2,1)S(1)} %mix_rows.1.refs_8_.refs_1_.refs_5_), channel_id=1, source_target_pairs={{2,0},{3,1},{0,2},{1,3},{6,4},{7,5},{4,6},{5,7},{10,8},{11,9},{8,1... | collective-permute-start | bytes 1572872 | tf_op jit(solution)/shard_map/ppermute | solution.py:480
  82.4 14.8 %collective-permute-start.24 = (bf16[1024,256]{1,0:T(8,128)(2,1)S(1)}, bf16[1024,256]{1,0:T(8,128)(2,1)S(1)}, u32[]{:S(2)}, u32[]{:S(2)}) collective-permute-start(bf16[1024,256]{1,0:T(8,128)(2,1)S(1)} %mix_rows.1.refs_8_.refs_1_.refs_5_), channel_id=1, source_target_pairs={{0,1},{1,0},{2,3},{3,2},{4,5},{5,4},{6,7},{7,6},{8,9},{9,8},{10,11... | collective-permute-start | bytes 1572872 | tf_op jit(solution)/shard_map/ppermute | solution.py:479
  94.1 14.8 %collective-permute-start.29 = (bf16[1024,256]{1,0:T(8,128)(2,1)S(1)}, bf16[1024,256]{1,0:T(8,128)(2,1)S(1)}, u32[]{:S(2)}, u32[]{:S(2)}) collective-permute-start(bf16[1024,256]{1,0:T(8,128)(2,1)S(1)} %decoder_grad.6.refs_4_.refs_1_.refs_3_), channel_id=1, source_target_pairs={{0,2},{1,3},{2,0},{3,1},{4,6},{5,7},{6,4},{7,5},{8,10},{9,11},{10,... | collective-permute-start | bytes 1572872 | tf_op jit(solution)/shard_map/ppermute | solution.py:482
  102.3 12.2 %collective-permute-start.28 = (bf16[512,256]{1,0:T(8,128)(2,1)S(1)}, bf16[512,256]{1,0:T(8,128)(2,1)S(1)}, u32[]{:S(2)}, u32[]{:S(2)}) collective-permute-start(bf16[512,256]{1,0:T(8,128)(2,1)S(1)} %encoder_grad.12.refs_3_), channel_id=1, source_target_pairs={{0,2},{1,3},{2,0},{3,1},{4,6},{5,7},{6,4},{7,5},{8,10},{9,11},{10,... | collective-permute-start | bytes 786440 | tf_op jit(solution)/shard_map/ppermute | solution.py:482
  103.3 16.0 %collective-permute-start.27 = (bf16[512,256]{1,0:T(8,128)(2,1)S(1)}, bf16[512,256]{1,0:T(8,128)(2,1)S(1)}, u32[]{:S(2)}, u32[]{:S(2)}) collective-permute-start(bf16[512,256]{1,0:T(8,128)(2,1)S(1)} %encoder_grad.13.refs_3_.refs_6_), channel_id=1, source_target_pairs={{0,2},{1,3},{2,0},{3,1},{4,6},{5,7},{6,4},{7,5},{8,10},{9,11},{10,... | collective-permute-start | bytes 786440 | tf_op jit(solution)/shard_map/ppermute | solution.py:482
  (17 other events, 64.8 us)

commit v8 on v7

--- a/solution.py
+++ b/solution.py
@@ -21,7 +21,7 @@
 
 bf16 = jnp.bfloat16
 f32 = jnp.float32
-VMEM_LIMIT = 16 * 1024 * 1024
+VMEM_LIMIT = 10 * 1024 * 1024
 
 
 def token_weight(kinds):
@@ -101,51 +101,41 @@
     )
 
 
-def extend_body(low, kinds, more):
-    rows, width = low.shape
-    more[:rows, :] = low[...]
-    pad = jnp.zeros((EXTRA - kinds.shape[0], width), f32)
-    more[rows:, :] = jnp.concatenate([token_weight(kinds[...]), pad], 0).astype(bf16)
-
-
-def extend(low, kinds):
-    rows, width = low.shape
-    lanes = kinds.reshape(-1, width)
-    shape = (rows + EXTRA, width)
-    return call(
-        extend_body, "extend_rows", (), [(a, whole(a.shape)) for a in (low, lanes)],
-        [(sds(shape, bf16), whole(shape))],
-    )[0]
-
-
-def weigh_body(own, other, out):
-    wide = own.shape[1]
-    for h, rows in enumerate((own, other)):
-        turned = rows[...].astype(f32).T
-        for j in range(out.shape[1] // wide):
+def weigh_body(kinds, other, out):
+    lanes, wide = kinds.shape
+    pad = jnp.zeros((EXTRA - lanes, wide), f32)
+    own = jnp.concatenate([token_weight(kinds[...]), pad], 0)
+    for h, rows in enumerate((own, other[other.shape[0] - EXTRA:, :].astype(f32))):
+        turned = rows.T
+        for j in range(lanes):
             out[h, j * wide:(j + 1) * wide, :] = turned[:, j:j + 1]
 
 
-def weigh(own, other, tokens):
-    rows, wide = own.shape
-    last = once((EXTRA, wide), lambda g: (rows // EXTRA - 1, 0))
-    return call(
-        weigh_body, "weigh_tokens", (), [(own, last), (other, last)],
+def weigh(lanes, other, tokens):
+    return call(
+        weigh_body, "weigh_tokens", (), [(a, whole(a.shape)) for a in (lanes, other)],
         [(sds((2, tokens, 1), f32), whole((2, tokens, 1)))],
     )[0]
 
 
-def relay_body(x, *outs):
-    size = outs[0].shape[0]
+def relay_body(cut, x, *refs):
+    outs = refs
+    if refs[0].dtype != bf16:
+        kinds, outs = refs[0], refs[1:]
+        pad = jnp.zeros((EXTRA - kinds.shape[0], kinds.shape[1]), f32)
+        outs[-1][cut:, :] = jnp.concatenate([token_weight(kinds[...]), pad], 0).astype(bf16)
     for n, out in enumerate(outs):
-        out[...] = x[n * size:(n + 1) * size, :]
-
-
-def relay(x, cuts, after):
-    shape = (x.shape[0] // cuts, x.shape[1])
-    return call(
-        relay_body, "relay_rows", (), [(x, whole(x.shape))],
-        [(sds(shape, x.dtype), whole(shape))] * cuts, after=after,
+        out[:cut, :] = x[n * cut:(n + 1) * cut, :]
+
+
+def relay(x, cuts, after, lanes=None):
+    rows, width = x.shape
+    cut = rows // cuts
+    shapes = [(cut, width)] * (cuts - 1) + [(cut + (0 if lanes is None else EXTRA), width)]
+    ins = [x] if lanes is None else [x, lanes]
+    return call(
+        functools.partial(relay_body, cut), "relay_rows", (), [(a, whole(a.shape)) for a in ins],
+        [(sds(shape, x.dtype), whole(shape)) for shape in shapes], after=after,
     )
 
 
@@ -222,7 +212,7 @@
     tokens = xs[0].shape[0]
     width = pieces[0][0].shape[1]
     ins = [(a, whole(a.shape)) for a in carry]
-    ins += [(p[0], whole((p[3], width))) for p in pieces] + [(x, whole(x.shape)) for x in xs]
+    ins += [(p[0], whole(p[0].shape)) for p in pieces] + [(x, whole(x.shape)) for x in xs]
     shapes = [(2, tokens, width)] + [(width, width)] * with_gram
     return call(
         functools.partial(forward_body, [p[1:] for p in pieces], rows, with_gram, not carry),
@@ -294,25 +284,28 @@
     )[0]
 
 
-def encoder_body(xt_own, xt_par, slopes, out):
-    out[...] = (dot(xt_own[...], slopes[0]) + dot(xt_par[...], slopes[1])).astype(out.dtype)
-
-
-def decoder_body(scale, xt_own, xt_par, counted, w_hi, w_lo, low, out):
-    dec = low[...]
-    both = dot(xt_own[...], counted[0]) + dot(xt_par[...], counted[1])
+def token_sum(start, size, xts, weights):
+    at = pl.ds(start, size)
+    return dot(xts[0][at, :], weights[0]) + dot(xts[1][at, :], weights[1])
+
+
+def encoder_body(start, xt_own, xt_par, slopes, out):
+    out[...] = token_sum(start, out.shape[0], (xt_own, xt_par), slopes).astype(out.dtype)
+
+
+def decoder_body(scale, start, xt_own, xt_par, counted, w_hi, w_lo, low, out):
+    both = token_sum(start, out.shape[0], (xt_own, xt_par), counted)
+    dec = low[:out.shape[0], :]
     out[...] = (scale * (dot(dec, w_hi[...]) + dot(dec, w_lo[...]) - both)).astype(out.dtype)
 
 
-def grad_rows(body, name, block, cr, xt, others, dtype, after=()):
-    tokens = xt[0].shape[1]
-    width = others[0].shape[2]
-    ins = [(x, once((cr, tokens), lambda g: (block, 0))) for x in xt]
-    ins += [(a, whole(a.shape)) for a in others]
-    return call(body, name, (), ins, [(sds((cr, width), dtype), whole((cr, width)))], after=after)[0]
-
-
-def adam_body(last, count, k, i, n_low, plan, own, *refs):
+def grad_rows(body, name, size, xt, others, dtype, after=()):
+    shape = (size, others[0].shape[2])
+    ins = [(a, whole(a.shape)) for a in [*xt, *others]]
+    return call(body, name, (), ins, [(sds(shape, dtype), whole(shape))], after=after)[0]
+
+
+def adam_body(last, count, k, off, n_low, plan, own, *refs):
     got = refs[:count]
     theta, first, second = refs[count:3 + count]
     refs = refs[3 + count:]
@@ -326,11 +319,10 @@
         old = mixed(plan, k, old, refs[0][...])
     new = old - inner_rate * (one / (jnp.sqrt(two) + adam_eps) + decay_rate * old)
     if n_low is not None:
-        cr = own.shape[0]
         anchor, before, low = refs[0], refs[1:1 + n_low], refs[1 + n_low]
-        for j, b in enumerate(before):
-            low[j * cr:(j + 1) * cr, :] = b[...]
-        low[n_low * cr:(n_low + 1) * cr, :] = mixed(plan, k, new, anchor[i * cr:(i + 1) * cr, :]).astype(bf16)
+        for b in before:
+            low[:off, :] = b[...]
+        low[off:, :] = mixed(plan, k, new, anchor[off:off + own.shape[0], :]).astype(bf16)
     theta_out, first_out, second_out = refs[-3:]
     theta_out[0, 0] = new
     first_out[0, 0] = one
@@ -341,8 +333,10 @@
     return jnp.where(fragment(plan) == k, mix_share * theta + (1.0 - mix_share) * anchor, theta)
 
 
-def adam_rows(plan, k, i, own, got, state, at, new_anc, prev, full, last, lows=None, after=()):
-    cr, width = own.shape
+def adam_rows(plan, key, own, got, state, at, new_anc, prev, full, last, lows=None, after=()):
+    k, off, cr = key
+    i = off // cr
+    width = own.shape[1]
     block = (1, 1, cr, width)
     ins = [(g, whole(g.shape)) for g in [own] + got]
     ins += [(s, once(block, lambda g, m: (0, at[0], at[1], 0))) for s in state]
@@ -358,11 +352,11 @@
     else:
         if lows is not None:
             ins += [(a, whole(a.shape)) for a in [new_anc] + lows]
-            shape = (cr * (1 + len(lows)), width)
+            shape = (off + cr, width)
             outs = [(sds(shape, bf16), whole(shape))]
         outs += [(sds(block, f32), whole(block))] * 3
     return call(
-        functools.partial(adam_body, last, len(got), k, i, None if lows is None else len(lows)), "adam_rows",
+        functools.partial(adam_body, last, len(got), k, off, None if lows is None else len(lows)), "adam_rows",
         (plan,), ins, outs, aliases=aliases, after=after,
     )
 
@@ -469,9 +463,7 @@
     rows, width = weights.shape[2:]
     chips = n_fsdp // 2
     scale = 1.0 / math.sqrt(tokens * n_fsdp)
-    chunks = max(1, rows // 512)
-    cr = rows // chunks
-    cuts = chunks
+    cuts = max(1, rows // 512)
     cut = rows // cuts
     others = range(1, chips)
 
@@ -491,32 +483,32 @@
     pos = jnp.stack([lax.axis_index("replica")] + [a + core for a in at] + [a + 1 - core for a in at]).astype(jnp.int32)
 
     x_par = to_partner(inputs)
-    more = extend(enc, kinds)
-    enc_near = to_partner(more)
-    cw = weigh(more, enc_near, tokens)
-
     quarters = outer_start(pos, plan, anchor, weights, [enc])
+    lanes = kinds.reshape(-1, width)
     xs, xt = zip(*[turn(pos, x, chips, stage) for x, stage in ((inputs, False), (x_par, True))])
     own = outer_add(plan, [quarters[0]] + [across(quarters[m], m) for m in range(1, 4)], n_rep == 4, xt)
 
-    blocks = [(1, 0)] + [(0, i) for i in range(chunks)]
+    most = rows - rows // 4 if rows >= 1024 else rows
+    blocks = [(1, 0, rows), (0, 0, most)] + [(0, off, rows - most) for off in range(most, rows, max(1, rows - most))]
     state = {key: (weights, first_moment, second_moment) for key in blocks}
-    state_at = {key: key for key in blocks}
+    state_at = {(k, off, size): (k, off // size) for k, off, size in blocks}
     new_anc = None
     for step in range(INNER):
         last = step == INNER - 1
         enc_far = {s: fetch(enc, s) for s in others}
         dec_far = {s: fetch(dec, s) for s in others}
-        if step:
-            enc_near = to_partner(enc)
-        dec_near = to_partner(dec)
+        enc_near, dec_near = to_partner(enc), to_partner(dec)
 
         carry = forward(pos, [], [(enc, 1, 0, rows)], xs, rows, False)
         carry = forward(pos, list(carry), [(enc_near, 1 + chips, 0, rows)], xs, rows, False)
-        ready = [cw, own, *xt] if step == 0 else [token]
-        part = [(p, 1 + s, n * cut, cut) for s in others for n, p in enumerate(relay(enc_far[s], cuts, [*carry, *ready]))]
+        ready = [own, *xt] if step == 0 else [token]
+        riders = [lanes] if step == 0 else []
+        part = [(p, 1 + s, n * cut, cut) for s in others for n, p in enumerate(
+            relay(enc_far[s], cuts, [*carry, *ready], *riders))]
         pending = [(to_partner(p), slot + chips, off, size) for p, slot, off, size in part]
         carry = forward(pos, carry, part, xs, rows, False)
+        if step == 0:
+            cw = weigh(lanes, pending[-1][0], tokens)
         hidden, slope, counted, w_hi, w_lo = hidden_rows(pos, carry[0], cw, pending, xs, rows, scale)
         if step == 0:
             bit = 4
@@ -524,51 +516,51 @@
                 own = outer_add(plan, [own, across(own, bit)], 2 * bit == n_rep)
                 bit *= 2
 
-        dec_grad = lambda block, low, dtype, after: grad_rows(
-            functools.partial(decoder_body, scale), "decoder_grad", block, rows, xt,
+        dec_grad = lambda s, low, dtype, after: grad_rows(
+            functools.partial(decoder_body, scale, s * rows), "decoder_grad", rows, xt,
             [counted, w_hi, w_lo, low], dtype, after)
-        enc_grad = lambda block, dtype, after: grad_rows(
-            encoder_body, "encoder_grad", block, cr, xt, [slopes], dtype, after)
-        sent = [own] if step == 0 else []
+        enc_grad = lambda s, off, size, dtype, after: grad_rows(
+            functools.partial(encoder_body, s * rows + off), "encoder_grad", size, xt, [slopes], dtype, after)
+        sent = []
         got = {key: [] for key in blocks}
         for s in others:
             sent.append(dec_grad(s, dec_far[s], bf16, sent[-1:]))
-            got[1, 0].append(give(sent[-1], s))
+            got[blocks[0]].append(give(sent[-1], s))
 
         carry = forward(pos, [], [(dec, 1, 0, rows)], xs, rows, True, sent[-1:])
+        part = [(p, 1 + s, n * cut, cut) for s in others for n, p in enumerate(relay(dec_far[s], cuts, sent[-1:]))]
         carry = forward(pos, carry, [(dec_near, 1 + chips, 0, rows)], xs, rows, True)
-        part = [(p, 1 + s, n * cut, cut) for s in others for n, p in enumerate(relay(dec_far[s], cuts, sent[-1:]))]
         pending = [(to_partner(p), slot + chips, off, size) for p, slot, off, size in part]
         carry = forward(pos, carry, part, xs, rows, True)
         slopes = slope_rows(pos, *carry, hidden, slope, pending, xs, rows)
-        for i in range(chunks):
+        for key in blocks[1:]:
             for s in others:
-                sent.append(enc_grad(s * chunks + i, bf16, sent[-1:]))
-                got[0, i].append(give(sent[-1], s))
-        mine = {(1, 0): dec_grad(0, dec, f32, sent[-1:])}
-        for i in range(chunks):
-            mine[0, i] = enc_grad(i, f32, sent[-1:])
+                sent.append(enc_grad(s, *key[1:], bf16, sent[-1:]))
+                got[key].append(give(sent[-1], s))
+        mine = {blocks[0]: dec_grad(0, dec, f32, sent[-1:])}
+        for key in blocks[1:]:
+            mine[key] = enc_grad(0, *key[1:], f32, sent[-1:])
 
         if not last:
             quarters = [own] + [across(own, m) for m in range(1, 4)]
-            new_anc = outer_anchor(pos, plan, anchor, momentum, quarters, [mine[1, 0]])
+            new_anc = outer_anchor(pos, plan, anchor, momentum, quarters, [mine[blocks[0]]])
         new_state, prev, lows, after = {}, None, [], []
         for key in blocks:
-            k, i = key
+            k = key[0]
             more_out = [] if last or k else [lows]
             res = adam_rows(
-                plan, k, i, mine[key], got[key], state[key], state_at[key], new_anc, prev, weights.shape, last,
+                plan, key, mine[key], got[key], state[key], state_at[key], new_anc, prev, weights.shape, last,
                 *more_out, after=after)
             if last:
                 prev = res
                 continue
             if k == 0:
-                lows = lows + [res[0]]
+                lows = [res[0]]
             new_state[key] = tuple(res[-3:])
             after = [] if k == 0 else [res[0]]
         if not last:
             enc = lows[-1]
-            dec = mix_rows(plan, new_anc, 1, new_state[1, 0][0], [enc])
+            dec = mix_rows(plan, new_anc, 1, new_state[blocks[0]][0], [enc])
             anchor_out, momentum_out, token = outer_end(pos, plan, anchor, momentum, quarters, [dec])
             state, state_at = new_state, {key: (0, 0) for key in blocks}
     return (*prev, anchor_out, momentum_out)

time: 122 us -> 116 us (0.951)
  waiting for transfers between devices: 31.5 us -> 24 us
  Pallas kernels: 58 us -> 59.7 us
    ppermute x7, waiting for transfers between devices: 8.69 us -> 1.79 us  [local(): lax.ppermute(a, 'replica', [(r, r ^ bit) for r in range(n_rep)])]
    unnamed x22 -> x24, local copies, waits for them, and re-layouts: 4.01 us -> 5.85 us
    pallas_call x49 -> x48, Pallas kernels: 58 us -> 59.7 us  [call(): pl.pallas_call(run, name=name, out_shape=[o for o, _ in outs], grid_spec=...]
    ppermute x6, waiting for transfers between devices: 9.88 us -> 8.48 us  [local(): lax.ppermute(a, 'fsdp', [(f, (f // 2 + s) % chips * 2 + f % 2) for f in r...]
  transfers between devices with their start and end apart: 30 -> 30, of which waited for: 10 -> 8; matrix products, arithmetic and copies ran while one was open for 1% -> 0% of each run, Pallas kernels for 45% -> 49%
where the time goes in v8:
time: 116 us
  Pallas kernels  59.7 us (51%)
  starting transfers between devices  25 us (22%)
  waiting for transfers between devices  24 us (21%)
  local copies, waits for them, and re-layouts  5.95 us (5%)
    pallas_call x48, Pallas kernels, call(): pl.pallas_call(run, name=name, out_shape=[o for o, _ in outs], grid_spec=...  59.7 us
    ppermute x4, waiting for transfers between devices, local(): lax.ppermute(a, 'fsdp', [((f // 2 + s) % chips * 2 + f % 2, f) for f in r...  13.7 us
    ppermute x7, starting transfers between devices, local(): lax.ppermute(a, 'replica', [(r, r ^ bit) for r in range(n_rep)])  10.3 us
    ppermute x6, waiting for transfers between devices, local(): lax.ppermute(a, 'fsdp', [(f, (f // 2 + s) % chips * 2 + f % 2) for f in r...  8.48 us
    ppermute x6, starting transfers between devices, local(): lax.ppermute(a, 'fsdp', [(f, (f // 2 + s) % chips * 2 + f % 2) for f in r...  6.49 us
    unnamed x24, local copies, waits for them, and re-layouts  5.85 us
    ppermute x4, starting transfers between devices, local(): lax.ppermute(a, 'fsdp', [((f // 2 + s) % chips * 2 + f % 2, f) for f in r...  5.16 us
    ppermute x13, starting transfers between devices, local(): to_partner = lambda a: lax.ppermute(a, 'fsdp', partner)  3.14 us
  transfers between devices with their start and end apart: 30, of which 8 were waited for; matrix products, arithmetic and copies ran while one was open for 0% of the time, Pallas kernels for 49%

profile of v8, /device:TPU:0, one launch (start us, length us, event | category | flops | bytes accessed | tf_op | source)
XLA Modules:
  0.0 115.9 jit_solution(16255652318757202004)
XLA Ops:
  1.2 1.6 %copy-done.2 = f32[1,2,1024,256]{3,2,1,0:T(8,128)S(1)} copy-done((f32[1,2,1024,256]{3,2,1,0:T(8,128)S(1)}, f32[1,2,1024,256]{3,2,1,0:T(8,128)}, u32[]{:S(2)}) %copy-start.2) | copy-done | bytes 2097176
  3.0 3.0 %collective-permute-start.9 = (bf16[1024,256]{1,0:T(8,128)(2,1)S(1)}, bf16[1024,256]{1,0:T(8,128)(2,1)}, u32[]{:S(2)}, u32[]{:S(2)}) collective-permute-start(bf16[1024,256]{1,0:T(8,128)(2,1)S(1)} %get-tuple-element.67.refs_4_.refs_1_), channel_id=1, source_target_pairs={{2,0},{3,1},{0,2},{1,3},{6,4},{7,5},{4,6},{5,7},{10,8},{11,9},{8,1... | collective-permute-start | bytes 1572872 | tf_op jit(solution)/shard_map/ppermute | solution.py:472
  6.1 1.6 %copy-done.5 = f32[2,1024,256]{2,1,0:T(8,128)S(1)} copy-done((f32[2,1024,256]{2,1,0:T(8,128)S(1)}, f32[2,1024,256]{2,1,0:T(8,128)}, u32[]{:S(2)}) %copy-start.5) | copy-done | bytes 2097176
  9.0 2.0 %collective-permute-start.1 = (bf16[256,256]{1,0:T(8,128)(2,1)}, bf16[256,256]{1,0:T(8,128)(2,1)S(1)}, u32[]{:S(2)}, u32[]{:S(2)}) collective-permute-start(bf16[256,256]{1,0:T(8,128)(2,1)} %get-tuple-element.69), channel_id=1, source_target_pairs={{0,4},{4,0},{8,12},{12,8},{16,20},{20,16},{24,28},{28,24},{1,5},{5... | collective-permute-start | bytes 393224 | tf_op jit(solution)/shard_map/ppermute | solution.py:476
  11.0 1.6 %collective-permute-start.2 = (bf16[256,256]{1,0:T(8,128)(2,1)}, bf16[256,256]{1,0:T(8,128)(2,1)}, u32[]{:S(2)}, u32[]{:S(2)}) collective-permute-start(bf16[256,256]{1,0:T(8,128)(2,1)} %get-tuple-element.70), channel_id=1, source_target_pairs={{0,8},{4,12},{8,0},{12,4},{16,24},{20,28},{24,16},{28,20},{1,9},{5... | collective-permute-start | bytes 393224 | tf_op jit(solution)/shard_map/ppermute | solution.py:476
  14.3 3.2 %stage_tokens.1 = (bf16[512,4096]{1,0:T(8,128)(2,1)S(1)}, bf16[2048,512]{1,0:T(8,128)(2,1)S(1)}) custom-call(s32[5]{0:T(128)S(1)} %stack.23.refs_0_, bf16[512,4096]{1,0:T(8,128)(2,1)} %collective-permute-done.refs_1_), custom_call_target="tpu_custom_call" | custom-call | bytes 10485760 | tf_op jit(solution)/shard_map/stage_tokens/pallas_call | solution.py:60
  19.0 2.3 %forward_encoder.7.refs_2_.refs_1_ = f32[2,512,256]{2,1,0:T(8,128)S(1)} custom-call(s32[5]{0:T(128)S(1)} %stack.23.refs_0_, f32[2,512,256]{2,1,0:T(8,128)S(1)} %forward_encoder.6.refs_1_, bf16[1024,256]{1,0:T(8,128)(2,1)} %collective-permute-done.8.refs_2_, bf16[512,4096]{1,0:T(8,128)(2,1)S(1)} %copy-done.1, ...), custom_call_target="tpu_custom_call" | custom-call | bytes 11010048 | tf_op jit(solution)/shard_map/forward_encoder/pallas_call | solution.py:60
  26.2 2.4 %hidden_units.2 = (bf16[2,512,256]{2,1,0:T(8,128)(2,1)S(1)}, f32[2,512,256]{2,1,0:T(8,128)S(1)}, bf16[2,512,256]{2,1,0:T(8,128)(2,1)S(1)}, bf16[256,256]{1,0:T(8,128)(2,1)S(1)}, bf16[256,256]{1,0:T(8,128)(2,1)S(1)}) custom-call(s32[5]{0:T(128)S(1)} %stack.23.refs_0_, f32[2,512,256]{2,1,0:T(8,128)S(1)} %forward_encoder.8.refs_1_, ...), custom_call_target="tpu_custom_call" | custom-call | bytes 12333056 | tf_op jit(solution)/shard_map/hidden_units/pallas_call | solution.py:60
  29.5 2.0 %decoder_grad.4.refs_4_.refs_1_.refs_3_ = bf16[1024,256]{1,0:T(8,128)(2,1)S(1)} custom-call(bf16[2048,512]{1,0:T(8,128)(2,1)S(1)} %turn_tokens.1.refs_5_.refs_4_.refs_0_, bf16[2048,512]{1,0:T(8,128)(2,1)S(1)} %get-tuple-element.66.refs_6_.refs_5_.refs_1_, bf16[2,512,256]{2,1,0:T(8,128)(2,1)S(1)} %get-tuple-element.75.refs_2_, ...), custom_call_target="tpu_custom_call" | custom-call | bytes 6029312 | tf_op jit(solution)/shard_map/decoder_grad/pallas_call | solution.py:60
  33.1 1.7 %collective-permute-start.16 = (bf16[1024,256]{1,0:T(8,128)(2,1)S(1)}, bf16[1024,256]{1,0:T(8,128)(2,1)S(1)}, u32[]{:S(2)}, u32[]{:S(2)}) collective-permute-start(bf16[1024,256]{1,0:T(8,128)(2,1)S(1)} %decoder_grad.4.refs_4_.refs_1_.refs_3_), channel_id=1, source_target_pairs={{0,2},{1,3},{2,0},{3,1},{4,6},{5,7},{6,4},{7,5},{8,10},{9,11},{10,... | collective-permute-start | bytes 1572872 | tf_op jit(solution)/shard_map/ppermute | solution.py:474
  34.9 2.6 %collective-permute-start.4 = (bf16[256,256]{1,0:T(8,128)(2,1)S(1)}, bf16[256,256]{1,0:T(8,128)(2,1)S(1)}, u32[]{:S(2)}, u32[]{:S(2)}) collective-permute-start(bf16[256,256]{1,0:T(8,128)(2,1)S(1)} %add_quarters.2.refs_1_.refs_3_), channel_id=1, source_target_pairs={{0,16},{4,20},{8,24},{12,28},{16,0},{20,4},{24,8},{28,12},{1,17},{... | collective-permute-start | bytes 393224 | tf_op jit(solution)/shard_map/ppermute | solution.py:476
  41.8 1.9 %slope_pre.2.refs_2_ = bf16[2,512,256]{2,1,0:T(8,128)(2,1)S(1)} custom-call(s32[5]{0:T(128)S(1)} %stack.23.refs_0_, f32[2,512,256]{2,1,0:T(8,128)S(1)} %get-tuple-element.85.refs_1_, f32[256,256]{1,0:T(8,128)S(1)} %get-tuple-element.86.refs_2_, bf16[2,512,256]{2,1,0:T(8,128)(2,1)S(1)} %get-tuple-element.87.refs_3_, ...), custom_call_target="tpu_custom_call" | custom-call | bytes 12320768 | tf_op jit(solution)/shard_map/slope_pre/pallas_call | solution.py:60
  46.9 1.6 %collective-permute-start.6 = (bf16[256,256]{1,0:T(8,128)(2,1)S(1)}, bf16[256,256]{1,0:T(8,128)(2,1)S(1)}, u32[]{:S(2)}, u32[]{:S(2)}) collective-permute-start(bf16[256,256]{1,0:T(8,128)(2,1)S(1)} %add_quarters.3.refs_4_), channel_id=1, source_target_pairs={{0,8},{4,12},{8,0},{12,4},{16,24},{20,28},{24,16},{28,20},{1,9},{5... | collective-permute-start | bytes 393224 | tf_op jit(solution)/shard_map/ppermute | solution.py:476
  62.8 1.6 %collective-permute-start.23 = (bf16[1024,256]{1,0:T(8,128)(2,1)S(1)}, bf16[1024,256]{1,0:T(8,128)(2,1)S(1)}, u32[]{:S(2)}, u32[]{:S(2)}) collective-permute-start(bf16[1024,256]{1,0:T(8,128)(2,1)S(1)} %mix_rows.1.refs_8_.refs_1_.refs_5_), channel_id=1, source_target_pairs={{2,0},{3,1},{0,2},{1,3},{6,4},{7,5},{4,6},{5,7},{10,8},{11,9},{8,1... | collective-permute-start | bytes 1572872 | tf_op jit(solution)/shard_map/ppermute | solution.py:472
  65.6 3.1 %outer_step.1 = (f32[2,1024,256]{2,1,0:T(8,128)}, f32[2,1024,256]{2,1,0:T(8,128)}, f32[8,128]{1,0:T(8,128)S(1)}) custom-call(s32[5]{0:T(128)S(1)} %stack.23.refs_0_, s32[8]{0:T(128)S(1)} %copy-done.10, f32[2,1024,256]{2,1,0:T(8,128)S(1)} %copy-done.6, f32[2,1024,256]{2,1,0:T(8,128)S(1)} %copy-done.9, bf16[256,256]{1,0:T(8,128)(2,1)S(1)} %add_quarters.3.refs_4_, ...), custom_call_target="tpu_custom_call" | custom-call | bytes 8916992 | tf_op jit(solution)/shard_map/outer_step/pallas_call | solution.py:60
  69.9 6.4 %collective-permute-done.20.refs_0_ = bf16[1024,256]{1,0:T(8,128)(2,1)S(1)} collective-permute-done((bf16[1024,256]{1,0:T(8,128)(2,1)S(1)}, bf16[1024,256]{1,0:T(8,128)(2,1)S(1)}, u32[]{:S(2)}, u32[]{:S(2)}) %collective-permute-start.20) | collective-permute-done | bytes 524320 | tf_op jit(solution)/shard_map/ppermute | solution.py:472
  78.3 2.4 %hidden_units.3 = (bf16[2,512,256]{2,1,0:T(8,128)(2,1)S(1)}, f32[2,512,256]{2,1,0:T(8,128)S(1)}, bf16[2,512,256]{2,1,0:T(8,128)(2,1)S(1)}, bf16[256,256]{1,0:T(8,128)(2,1)S(1)}, bf16[256,256]{1,0:T(8,128)(2,1)S(1)}) custom-call(s32[5]{0:T(128)S(1)} %stack.23.refs_0_, f32[2,512,256]{2,1,0:T(8,128)S(1)} %forward_encoder.11.refs_1_, ...), custom_call_target="tpu_custom_call" | custom-call | bytes 12324864 | tf_op jit(solution)/shard_map/hidden_units/pallas_call | solution.py:60
  80.7 6.4 %collective-permute-done.23.refs_5_.refs_0_ = bf16[1024,256]{1,0:T(8,128)(2,1)S(1)} collective-permute-done((bf16[1024,256]{1,0:T(8,128)(2,1)S(1)}, bf16[1024,256]{1,0:T(8,128)(2,1)S(1)}, u32[]{:S(2)}, u32[]{:S(2)}) %collective-permute-start.23) | collective-permute-done | bytes 524320 | tf_op jit(solution)/shard_map/ppermute | solution.py:472
  93.5 1.9 %slope_pre.3.refs_2_ = bf16[2,512,256]{2,1,0:T(8,128)(2,1)S(1)} custom-call(s32[5]{0:T(128)S(1)} %stack.23.refs_0_, f32[2,512,256]{2,1,0:T(8,128)S(1)} %get-tuple-element.104.refs_1_, f32[256,256]{1,0:T(8,128)S(1)} %get-tuple-element.105.refs_2_, bf16[2,512,256]{2,1,0:T(8,128)(2,1)S(1)} %get-tuple-element.106.refs_3_, ...), custom_call_target="tpu_custom_call" | custom-call | bytes 12320768 | tf_op jit(solution)/shard_map/slope_pre/pallas_call | solution.py:60
  96.0 1.6 %collective-permute-start.28 = (bf16[768,256]{1,0:T(8,128)(2,1)S(1)}, bf16[768,256]{1,0:T(8,128)(2,1)S(1)}, u32[]{:S(2)}, u32[]{:S(2)}) collective-permute-start(bf16[768,256]{1,0:T(8,128)(2,1)S(1)} %encoder_grad.12.refs_3_), channel_id=1, source_target_pairs={{0,2},{1,3},{2,0},{3,1},{4,6},{5,7},{6,4},{7,5},{8,10},{9,11},{10,... | collective-permute-start | bytes 1179656 | tf_op jit(solution)/shard_map/ppermute | solution.py:474
  100.6 2.9 %collective-permute-done.29.refs_2_ = bf16[1024,256]{1,0:T(8,128)(2,1)S(1)} collective-permute-done((bf16[1024,256]{1,0:T(8,128)(2,1)S(1)}, bf16[1024,256]{1,0:T(8,128)(2,1)S(1)}, u32[]{:S(2)}, u32[]{:S(2)}) %collective-permute-start.29) | collective-permute-done | bytes 524320 | tf_op jit(solution)/shard_map/ppermute | solution.py:474
  103.5 2.9 %adam_rows.9 = (f32[1,2,1024,256]{3,2,1,0:T(8,128)}, f32[1,2,1024,256]{3,2,1,0:T(8,128)}, f32[1,2,1024,256]{3,2,1,0:T(8,128)}) custom-call(s32[8]{0:T(128)S(1)} %copy-done.10, f32[1024,256]{1,0:T(8,128)S(1)} %decoder_grad.7.refs_1_, bf16[1024,256]{1,0:T(8,128)(2,1)S(1)} %collective-permute-done.29.refs_2_, ...), custom_call_target="tpu_custom_call" | custom-call | bytes 12058624 | tf_op jit(solution)/shard_map/adam_rows/pallas_call | solution.py:60
  106.3 5.6 %collective-permute-done.28.refs_2_ = bf16[768,256]{1,0:T(8,128)(2,1)S(1)} collective-permute-done((bf16[768,256]{1,0:T(8,128)(2,1)S(1)}, bf16[768,256]{1,0:T(8,128)(2,1)S(1)}, u32[]{:S(2)}, u32[]{:S(2)}) %collective-permute-start.28) | collective-permute-done | bytes 393248 | tf_op jit(solution)/shard_map/ppermute | solution.py:474
  111.9 2.4 %adam_rows.10 = (f32[1,2,1024,256]{3,2,1,0:T(8,128)}, f32[1,2,1024,256]{3,2,1,0:T(8,128)}, f32[1,2,1024,256]{3,2,1,0:T(8,128)}) custom-call(s32[8]{0:T(128)S(1)} %copy-done.10, f32[768,256]{1,0:T(8,128)S(1)} %encoder_grad.15.refs_1_, ...), custom_call_target="tpu_custom_call", output_to_operand_aliasing={{0}: (7, {}), {1}: (8, {}), {2}: (9, {})} | custom-call | bytes 16908288 | tf_op jit(solution)/shard_map/adam_rows/pallas_call | solution.py:60
  (110 shorter events, 50.4 us)
Async XLA Ops:
  0.6 11.9 %collective-permute-start = (bf16[512,4096]{1,0:T(8,128)(2,1)}, bf16[512,4096]{1,0:T(8,128)(2,1)}, u32[]{:S(2)}, u32[]{:S(2)}) collective-permute-start(bf16[512,4096]{1,0:T(8,128)(2,1)} %refs_7_.3), channel_id=1, source_target_pairs={{0,1},{1,0},{2,3},{3,2},{4,5},{5,4},{6,7},{7,6},{8,9},{9,8},{10,11... | collective-permute-start | bytes 12582920 | tf_op jit(solution)/shard_map/ppermute | solution.py:471
  2.9 8.1 %collective-permute-start.8 = (bf16[1024,256]{1,0:T(8,128)(2,1)S(1)}, bf16[1024,256]{1,0:T(8,128)(2,1)}, u32[]{:S(2)}, u32[]{:S(2)}) collective-permute-start(bf16[1024,256]{1,0:T(8,128)(2,1)S(1)} %get-tuple-element.67.refs_4_.refs_1_), channel_id=1, source_target_pairs={{0,1},{1,0},{2,3},{3,2},{4,5},{5,4},{6,7},{7,6},{8,9},{9,8},{10,11... | collective-permute-start | bytes 1572872 | tf_op jit(solution)/shard_map/ppermute | solution.py:471
  3.0 19.9 %collective-permute-start.9 = (bf16[1024,256]{1,0:T(8,128)(2,1)S(1)}, bf16[1024,256]{1,0:T(8,128)(2,1)}, u32[]{:S(2)}, u32[]{:S(2)}) collective-permute-start(bf16[1024,256]{1,0:T(8,128)(2,1)S(1)} %get-tuple-element.67.refs_4_.refs_1_), channel_id=1, source_target_pairs={{2,0},{3,1},{0,2},{1,3},{6,4},{7,5},{4,6},{5,7},{10,8},{11,9},{8,1... | collective-permute-start | bytes 1572872 | tf_op jit(solution)/shard_map/ppermute | solution.py:472
  5.9 23.5 %collective-permute-start.12 = (bf16[1024,256]{1,0:T(8,128)(2,1)S(1)}, bf16[1024,256]{1,0:T(8,128)(2,1)}, u32[]{:S(2)}, u32[]{:S(2)}) collective-permute-start(bf16[1024,256]{1,0:T(8,128)(2,1)S(1)} %get-tuple-element.78.refs_1_.refs_5_), channel_id=1, source_target_pairs={{2,0},{3,1},{0,2},{1,3},{6,4},{7,5},{4,6},{5,7},{10,8},{11,9},{8,1... | collective-permute-start | bytes 1572872 | tf_op jit(solution)/shard_map/ppermute | solution.py:472
  9.0 12.3 %collective-permute-start.1 = (bf16[256,256]{1,0:T(8,128)(2,1)}, bf16[256,256]{1,0:T(8,128)(2,1)S(1)}, u32[]{:S(2)}, u32[]{:S(2)}) collective-permute-start(bf16[256,256]{1,0:T(8,128)(2,1)} %get-tuple-element.69), channel_id=1, source_target_pairs={{0,4},{4,0},{8,12},{12,8},{16,20},{20,16},{24,28},{28,24},{1,5},{5... | collective-permute-start | bytes 393224 | tf_op jit(solution)/shard_map/ppermute | solution.py:476
  11.0 10.3 %collective-permute-start.2 = (bf16[256,256]{1,0:T(8,128)(2,1)}, bf16[256,256]{1,0:T(8,128)(2,1)}, u32[]{:S(2)}, u32[]{:S(2)}) collective-permute-start(bf16[256,256]{1,0:T(8,128)(2,1)} %get-tuple-element.70), channel_id=1, source_target_pairs={{0,8},{4,12},{8,0},{12,4},{16,24},{20,28},{24,16},{28,20},{1,9},{5... | collective-permute-start | bytes 393224 | tf_op jit(solution)/shard_map/ppermute | solution.py:476
  12.6 8.8 %collective-permute-start.3 = (bf16[256,256]{1,0:T(8,128)(2,1)}, bf16[256,256]{1,0:T(8,128)(2,1)}, u32[]{:S(2)}, u32[]{:S(2)}) collective-permute-start(bf16[256,256]{1,0:T(8,128)(2,1)} %get-tuple-element.71), channel_id=1, source_target_pairs={{0,12},{4,8},{8,4},{12,0},{16,28},{20,24},{24,20},{28,16},{1,13},{... | collective-permute-start | bytes 393224 | tf_op jit(solution)/shard_map/ppermute | solution.py:476
  24.6 14.3 %collective-permute-start.13 = (bf16[1024,256]{1,0:T(8,128)(2,1)S(1)}, bf16[1024,256]{1,0:T(8,128)(2,1)S(1)}, u32[]{:S(2)}, u32[]{:S(2)}) collective-permute-start(bf16[1024,256]{1,0:T(8,128)(2,1)S(1)} %get-tuple-element.78.refs_1_.refs_5_), channel_id=1, source_target_pairs={{0,1},{1,0},{2,3},{3,2},{4,5},{5,4},{6,7},{7,6},{8,9},{9,8},{10,11... | collective-permute-start | bytes 1572872 | tf_op jit(solution)/shard_map/ppermute | solution.py:471
  32.6 9.2 %collective-permute-start.14 = (bf16[512,256]{1,0:T(8,128)(2,1)S(1)}, bf16[512,256]{1,0:T(8,128)(2,1)S(1)}, u32[]{:S(2)}, u32[]{:S(2)}) collective-permute-start(bf16[512,256]{1,0:T(8,128)(2,1)S(1)} %get-tuple-element.83.refs_3_), channel_id=1, source_target_pairs={{0,1},{1,0},{2,3},{3,2},{4,5},{5,4},{6,7},{7,6},{8,9},{9,8},{10,11... | collective-permute-start | bytes 786440 | tf_op jit(solution)/shard_map/ppermute | solution.py:471
  32.6 9.1 %collective-permute-start.15 = (bf16[512,256]{1,0:T(8,128)(2,1)S(1)}, bf16[512,256]{1,0:T(8,128)(2,1)S(1)}, u32[]{:S(2)}, u32[]{:S(2)}) collective-permute-start(bf16[512,256]{1,0:T(8,128)(2,1)S(1)} %get-tuple-element.84.refs_4_), channel_id=1, source_target_pairs={{0,1},{1,0},{2,3},{3,2},{4,5},{5,4},{6,7},{7,6},{8,9},{9,8},{10,11... | collective-permute-start | bytes 786440 | tf_op jit(solution)/shard_map/ppermute | solution.py:471
  33.1 23.7 %collective-permute-start.16 = (bf16[1024,256]{1,0:T(8,128)(2,1)S(1)}, bf16[1024,256]{1,0:T(8,128)(2,1)S(1)}, u32[]{:S(2)}, u32[]{:S(2)}) collective-permute-start(bf16[1024,256]{1,0:T(8,128)(2,1)S(1)} %decoder_grad.4.refs_4_.refs_1_.refs_3_), channel_id=1, source_target_pairs={{0,2},{1,3},{2,0},{3,1},{4,6},{5,7},{6,4},{7,5},{8,10},{9,11},{10,... | collective-permute-start | bytes 1572872 | tf_op jit(solution)/shard_map/ppermute | solution.py:474
  34.9 9.9 %collective-permute-start.4 = (bf16[256,256]{1,0:T(8,128)(2,1)S(1)}, bf16[256,256]{1,0:T(8,128)(2,1)S(1)}, u32[]{:S(2)}, u32[]{:S(2)}) collective-permute-start(bf16[256,256]{1,0:T(8,128)(2,1)S(1)} %add_quarters.2.refs_1_.refs_3_), channel_id=1, source_target_pairs={{0,16},{4,20},{8,24},{12,28},{16,0},{20,4},{24,8},{28,12},{1,17},{... | collective-permute-start | bytes 393224 | tf_op jit(solution)/shard_map/ppermute | solution.py:476
  44.2 15.1 %collective-permute-start.18 = (bf16[768,256]{1,0:T(8,128)(2,1)S(1)}, bf16[768,256]{1,0:T(8,128)(2,1)S(1)}, u32[]{:S(2)}, u32[]{:S(2)}) collective-permute-start(bf16[768,256]{1,0:T(8,128)(2,1)S(1)} %encoder_grad.8.refs_3_), channel_id=1, source_target_pairs={{0,2},{1,3},{2,0},{3,1},{4,6},{5,7},{6,4},{7,5},{8,10},{9,11},{10,... | collective-permute-start | bytes 1179656 | tf_op jit(solution)/shard_map/ppermute | solution.py:474
  46.9 7.2 %collective-permute-start.6 = (bf16[256,256]{1,0:T(8,128)(2,1)S(1)}, bf16[256,256]{1,0:T(8,128)(2,1)S(1)}, u32[]{:S(2)}, u32[]{:S(2)}) collective-permute-start(bf16[256,256]{1,0:T(8,128)(2,1)S(1)} %add_quarters.3.refs_4_), channel_id=1, source_target_pairs={{0,8},{4,12},{8,0},{12,4},{16,24},{20,28},{24,16},{28,20},{1,9},{5... | collective-permute-start | bytes 393224 | tf_op jit(solution)/shard_map/ppermute | solution.py:476
  48.5 6.2 %collective-permute-start.7 = (bf16[256,256]{1,0:T(8,128)(2,1)S(1)}, bf16[256,256]{1,0:T(8,128)(2,1)S(1)}, u32[]{:S(2)}, u32[]{:S(2)}) collective-permute-start(bf16[256,256]{1,0:T(8,128)(2,1)S(1)} %add_quarters.3.refs_4_), channel_id=1, source_target_pairs={{0,12},{4,8},{8,4},{12,0},{16,28},{20,24},{24,20},{28,16},{1,13},{... | collective-permute-start | bytes 393224 | tf_op jit(solution)/shard_map/ppermute | solution.py:476
  50.5 10.1 %collective-permute-start.17 = (bf16[256,256]{1,0:T(8,128)(2,1)S(1)}, bf16[256,256]{1,0:T(8,128)(2,1)S(1)}, u32[]{:S(2)}, u32[]{:S(2)}) collective-permute-start(bf16[256,256]{1,0:T(8,128)(2,1)S(1)} %encoder_grad.9.refs_6_.refs_3_), channel_id=1, source_target_pairs={{0,2},{1,3},{2,0},{3,1},{4,6},{5,7},{6,4},{7,5},{8,10},{9,11},{10,... | collective-permute-start | bytes 393224 | tf_op jit(solution)/shard_map/ppermute | solution.py:474
  61.4 7.3 %collective-permute-start.19 = (bf16[1024,256]{1,0:T(8,128)(2,1)S(1)}, bf16[1024,256]{1,0:T(8,128)(2,1)S(1)}, u32[]{:S(2)}, u32[]{:S(2)}) collective-permute-start(bf16[1024,256]{1,0:T(8,128)(2,1)S(1)} %get-tuple-element.91.refs_3_.refs_1_), channel_id=1, source_target_pairs={{0,1},{1,0},{2,3},{3,2},{4,5},{5,4},{6,7},{7,6},{8,9},{9,8},{10,11... | collective-permute-start | bytes 1572872 | tf_op jit(solution)/shard_map/ppermute | solution.py:471
  61.5 14.8 %collective-permute-start.20 = (bf16[1024,256]{1,0:T(8,128)(2,1)S(1)}, bf16[1024,256]{1,0:T(8,128)(2,1)S(1)}, u32[]{:S(2)}, u32[]{:S(2)}) collective-permute-start(bf16[1024,256]{1,0:T(8,128)(2,1)S(1)} %get-tuple-element.91.refs_3_.refs_1_), channel_id=1, source_target_pairs={{2,0},{3,1},{0,2},{1,3},{6,4},{7,5},{4,6},{5,7},{10,8},{11,9},{8,1... | collective-permute-start | bytes 1572872 | tf_op jit(solution)/shard_map/ppermute | solution.py:472
  62.8 24.3 %collective-permute-start.23 = (bf16[1024,256]{1,0:T(8,128)(2,1)S(1)}, bf16[1024,256]{1,0:T(8,128)(2,1)S(1)}, u32[]{:S(2)}, u32[]{:S(2)}) collective-permute-start(bf16[1024,256]{1,0:T(8,128)(2,1)S(1)} %mix_rows.1.refs_8_.refs_1_.refs_5_), channel_id=1, source_target_pairs={{2,0},{3,1},{0,2},{1,3},{6,4},{7,5},{4,6},{5,7},{10,8},{11,9},{8,1... | collective-permute-start | bytes 1572872 | tf_op jit(solution)/shard_map/ppermute | solution.py:472
  76.9 13.7 %collective-permute-start.24 = (bf16[1024,256]{1,0:T(8,128)(2,1)S(1)}, bf16[1024,256]{1,0:T(8,128)(2,1)S(1)}, u32[]{:S(2)}, u32[]{:S(2)}) collective-permute-start(bf16[1024,256]{1,0:T(8,128)(2,1)S(1)} %mix_rows.1.refs_8_.refs_1_.refs_5_), channel_id=1, source_target_pairs={{0,1},{1,0},{2,3},{3,2},{4,5},{5,4},{6,7},{7,6},{8,9},{9,8},{10,11... | collective-permute-start | bytes 1572872 | tf_op jit(solution)/shard_map/ppermute | solution.py:471
  88.1 5.4 %collective-permute-start.25 = (bf16[512,256]{1,0:T(8,128)(2,1)S(1)}, bf16[512,256]{1,0:T(8,128)(2,1)S(1)}, u32[]{:S(2)}, u32[]{:S(2)}) collective-permute-start(bf16[512,256]{1,0:T(8,128)(2,1)S(1)} %get-tuple-element.102.refs_3_), channel_id=1, source_target_pairs={{0,1},{1,0},{2,3},{3,2},{4,5},{5,4},{6,7},{7,6},{8,9},{9,8},{10,11... | collective-permute-start | bytes 786440 | tf_op jit(solution)/shard_map/ppermute | solution.py:471
  88.7 14.8 %collective-permute-start.29 = (bf16[1024,256]{1,0:T(8,128)(2,1)S(1)}, bf16[1024,256]{1,0:T(8,128)(2,1)S(1)}, u32[]{:S(2)}, u32[]{:S(2)}) collective-permute-start(bf16[1024,256]{1,0:T(8,128)(2,1)S(1)} %decoder_grad.6.refs_4_.refs_1_.refs_3_), channel_id=1, source_target_pairs={{0,2},{1,3},{2,0},{3,1},{4,6},{5,7},{6,4},{7,5},{8,10},{9,11},{10,... | collective-permute-start | bytes 1572872 | tf_op jit(solution)/shard_map/ppermute | solution.py:474
  96.0 15.9 %collective-permute-start.28 = (bf16[768,256]{1,0:T(8,128)(2,1)S(1)}, bf16[768,256]{1,0:T(8,128)(2,1)S(1)}, u32[]{:S(2)}, u32[]{:S(2)}) collective-permute-start(bf16[768,256]{1,0:T(8,128)(2,1)S(1)} %encoder_grad.12.refs_3_), channel_id=1, source_target_pairs={{0,2},{1,3},{2,0},{3,1},{4,6},{5,7},{6,4},{7,5},{8,10},{9,11},{10,... | collective-permute-start | bytes 1179656 | tf_op jit(solution)/shard_map/ppermute | solution.py:474
  97.9 16.4 %collective-permute-start.27 = (bf16[256,256]{1,0:T(8,128)(2,1)S(1)}, bf16[256,256]{1,0:T(8,128)(2,1)S(1)}, u32[]{:S(2)}, u32[]{:S(2)}) collective-permute-start(bf16[256,256]{1,0:T(8,128)(2,1)S(1)} %encoder_grad.13.refs_3_.refs_6_), channel_id=1, source_target_pairs={{0,2},{1,3},{2,0},{3,1},{4,6},{5,7},{6,4},{7,5},{8,10},{9,11},{10,... | collective-permute-start | bytes 393224 | tf_op jit(solution)/shard_map/ppermute | solution.py:474
  (18 other events, 52.2 us)

commit v9 on v8

--- a/solution.py
+++ b/solution.py
@@ -293,10 +293,17 @@
     out[...] = token_sum(start, out.shape[0], (xt_own, xt_par), slopes).astype(out.dtype)
 
 
-def decoder_body(scale, start, xt_own, xt_par, counted, w_hi, w_lo, low, out):
-    both = token_sum(start, out.shape[0], (xt_own, xt_par), counted)
-    dec = low[:out.shape[0], :]
-    out[...] = (scale * (dot(dec, w_hi[...]) + dot(dec, w_lo[...]) - both)).astype(out.dtype)
+def decoder_body(scale, start, pieces, xt_own, xt_par, counted, w_hi, w_lo, *refs):
+    lows, got, out = refs[:pieces], refs[pieces:-1], refs[-1]
+    off = 0
+    for low in lows:
+        size = low.shape[0]
+        both = token_sum(start + off, size, (xt_own, xt_par), counted)
+        value = scale * (dot(low[...], w_hi[...]) + dot(low[...], w_lo[...]) - both)
+        for g in got:
+            value = value + g[off:off + size, :].astype(f32)
+        out[off:off + size, :] = value.astype(out.dtype)
+        off += size
 
 
 def grad_rows(body, name, size, xt, others, dtype, after=()):
@@ -499,8 +506,7 @@
         dec_far = {s: fetch(dec, s) for s in others}
         enc_near, dec_near = to_partner(enc), to_partner(dec)
 
-        carry = forward(pos, [], [(enc, 1, 0, rows)], xs, rows, False)
-        carry = forward(pos, list(carry), [(enc_near, 1 + chips, 0, rows)], xs, rows, False)
+        carry = forward(pos, [], [(enc, 1, 0, rows), (enc_near, 1 + chips, 0, rows)], xs, rows, False)
         ready = [own, *xt] if step == 0 else [token]
         riders = [lanes] if step == 0 else []
         part = [(p, 1 + s, n * cut, cut) for s in others for n, p in enumerate(
@@ -510,56 +516,55 @@
         if step == 0:
             cw = weigh(lanes, pending[-1][0], tokens)
         hidden, slope, counted, w_hi, w_lo = hidden_rows(pos, carry[0], cw, pending, xs, rows, scale)
-        if step == 0:
-            bit = 4
-            while bit < n_rep:
-                own = outer_add(plan, [own, across(own, bit)], 2 * bit == n_rep)
-                bit *= 2
-
-        dec_grad = lambda s, low, dtype, after: grad_rows(
-            functools.partial(decoder_body, scale, s * rows), "decoder_grad", rows, xt,
-            [counted, w_hi, w_lo, low], dtype, after)
+        dec_grad = lambda s, lows, more, dtype, after: grad_rows(
+            functools.partial(decoder_body, scale, s * rows, len(lows)), "decoder_grad", rows, xt,
+            [counted, w_hi, w_lo, *lows, *more], dtype, after)
         enc_grad = lambda s, off, size, dtype, after: grad_rows(
             functools.partial(encoder_body, s * rows + off), "encoder_grad", size, xt, [slopes], dtype, after)
         sent = []
         got = {key: [] for key in blocks}
+        far = {s: relay(dec_far[s], cuts, [counted]) for s in others}
         for s in others:
-            sent.append(dec_grad(s, dec_far[s], bf16, sent[-1:]))
+            sent.append(dec_grad(s, far[s], [], bf16, sent[-1:]))
             got[blocks[0]].append(give(sent[-1], s))
 
-        carry = forward(pos, [], [(dec, 1, 0, rows)], xs, rows, True, sent[-1:])
-        part = [(p, 1 + s, n * cut, cut) for s in others for n, p in enumerate(relay(dec_far[s], cuts, sent[-1:]))]
-        carry = forward(pos, carry, [(dec_near, 1 + chips, 0, rows)], xs, rows, True)
+        part = [(p, 1 + s, n * cut, cut) for s in others for n, p in enumerate(far[s])]
         pending = [(to_partner(p), slot + chips, off, size) for p, slot, off, size in part]
-        carry = forward(pos, carry, part, xs, rows, True)
+        carry = forward(
+            pos, [], [(dec, 1, 0, rows), (dec_near, 1 + chips, 0, rows)] + part, xs, rows, True, sent[-1:])
         slopes = slope_rows(pos, *carry, hidden, slope, pending, xs, rows)
-        for key in blocks[1:]:
+        if step == 0:
+            bit = 4
+            while bit < n_rep:
+                own = outer_add(plan, [own, across(own, bit)], 2 * bit == n_rep, [slopes])
+                bit *= 2
+            sent.append(own)
+        for n, key in enumerate(blocks[1:]):
             for s in others:
                 sent.append(enc_grad(s, *key[1:], bf16, sent[-1:]))
                 got[key].append(give(sent[-1], s))
-        mine = {blocks[0]: dec_grad(0, dec, f32, sent[-1:])}
+            if n == 0:
+                mine = {blocks[0]: dec_grad(0, [dec], got[blocks[0]], f32, sent[-1:])}
+                got[blocks[0]] = []
+                sent.append(mine[blocks[0]])
         for key in blocks[1:]:
             mine[key] = enc_grad(0, *key[1:], f32, sent[-1:])
 
         if not last:
             quarters = [own] + [across(own, m) for m in range(1, 4)]
             new_anc = outer_anchor(pos, plan, anchor, momentum, quarters, [mine[blocks[0]]])
-        new_state, prev, lows, after = {}, None, [], []
-        for key in blocks:
-            k = key[0]
-            more_out = [] if last or k else [lows]
-            res = adam_rows(
-                plan, key, mine[key], got[key], state[key], state_at[key], new_anc, prev, weights.shape, last,
-                *more_out, after=after)
-            if last:
-                prev = res
-                continue
-            if k == 0:
-                lows = [res[0]]
-            new_state[key] = tuple(res[-3:])
-            after = [] if k == 0 else [res[0]]
-        if not last:
-            enc = lows[-1]
+        new_state, prev, lows = {}, None, []
+        adam = lambda key, prev, *more, after=(): adam_rows(
+            plan, key, mine[key], got[key], state[key], state_at[key], new_anc, prev, weights.shape, last,
+            *more, after=after)
+        if last:
+            for key in blocks:
+                prev = adam(key, prev)
+        else:
+            for key in blocks[1:]:
+                enc, *new_state[key] = adam(key, None, lows)
+                lows = [enc]
+            new_state[blocks[0]] = adam(blocks[0], None, after=[enc])
             dec = mix_rows(plan, new_anc, 1, new_state[blocks[0]][0], [enc])
             anchor_out, momentum_out, token = outer_end(pos, plan, anchor, momentum, quarters, [dec])
             state, state_at = new_state, {key: (0, 0) for key in blocks}

time: 116 us -> 113 us (0.974)
  Pallas kernels: 59.7 us -> 53.9 us
  waiting for transfers between devices: 24 us -> 27.9 us
  local copies, waits for them, and re-layouts: 5.95 us -> 3.55 us
  starting transfers between devices: 25 us -> 26.3 us
    pallas_call x48 -> x42, Pallas kernels: 59.7 us -> 53.9 us  [call(): pl.pallas_call(run, name=name, out_shape=[o for o, _ in outs], grid_spec=...]
    unnamed x24, local copies, waits for them, and re-layouts: 5.85 us -> 3.45 us
    ppermute x6, waiting for transfers between devices: 8.48 us -> 10.6 us  [local(): lax.ppermute(a, 'fsdp', [(f, (f // 2 + s) % chips * 2 + f % 2) for f in r...]
    ppermute x7, waiting for transfers between devices: 1.79 us -> 3.32 us  [local(): lax.ppermute(a, 'replica', [(r, r ^ bit) for r in range(n_rep)])]
    ppermute x6, starting transfers between devices: 6.49 us -> 7.84 us  [local(): lax.ppermute(a, 'fsdp', [(f, (f // 2 + s) % chips * 2 + f % 2) for f in r...]
  transfers between devices with their start and end apart: 30 -> 30, of which waited for: 8 -> 9; matrix products, arithmetic and copies ran while one was open for 0% -> 0% of each run, Pallas kernels for 49% -> 46%
where the time goes in v9:
time: 113 us
  Pallas kernels  53.9 us (48%)
  waiting for transfers between devices  27.9 us (25%)
  starting transfers between devices  26.3 us (23%)
  local copies, waits for them, and re-layouts  3.55 us (3%)
    pallas_call x42, Pallas kernels, call(): pl.pallas_call(run, name=name, out_shape=[o for o, _ in outs], grid_spec=...  53.9 us
    ppermute x4, waiting for transfers between devices, local(): lax.ppermute(a, 'fsdp', [((f // 2 + s) % chips * 2 + f % 2, f) for f in r...  13.8 us
    ppermute x6, waiting for transfers between devices, local(): lax.ppermute(a, 'fsdp', [(f, (f // 2 + s) % chips * 2 + f % 2) for f in r...  10.6 us
    ppermute x7, starting transfers between devices, local(): lax.ppermute(a, 'replica', [(r, r ^ bit) for r in range(n_rep)])  10.2 us
    ppermute x6, starting transfers between devices, local(): lax.ppermute(a, 'fsdp', [(f, (f // 2 + s) % chips * 2 + f % 2) for f in r...  7.84 us
    ppermute x4, starting transfers between devices, local(): lax.ppermute(a, 'fsdp', [((f // 2 + s) % chips * 2 + f % 2, f) for f in r...  5.16 us
    unnamed x24, local copies, waits for them, and re-layouts  3.45 us
    ppermute x7, waiting for transfers between devices, local(): lax.ppermute(a, 'replica', [(r, r ^ bit) for r in range(n_rep)])  3.32 us
  transfers between devices with their start and end apart: 30, of which 9 were waited for; matrix products, arithmetic and copies ran while one was open for 0% of the time, Pallas kernels for 46%

profile of v9, /device:TPU:0, one launch (start us, length us, event | category | flops | bytes accessed | tf_op | source)
XLA Modules:
  0.0 112.8 jit_solution(10068221542770175181)
XLA Ops:
  3.0 3.0 %collective-permute-start.8 = (bf16[1024,256]{1,0:T(8,128)(2,1)S(1)}, bf16[1024,256]{1,0:T(8,128)(2,1)}, u32[]{:S(2)}, u32[]{:S(2)}) collective-permute-start(bf16[1024,256]{1,0:T(8,128)(2,1)S(1)} %get-tuple-element.59.refs_4_.refs_1_), channel_id=1, source_target_pairs={{2,0},{3,1},{0,2},{1,3},{6,4},{7,5},{4,6},{5,7},{10,8},{11,9},{8,1... | collective-permute-start | bytes 1572872 | tf_op jit(solution)/shard_map/ppermute | solution.py:479
  9.0 2.0 %collective-permute-start.1 = (bf16[256,256]{1,0:T(8,128)(2,1)}, bf16[256,256]{1,0:T(8,128)(2,1)S(1)}, u32[]{:S(2)}, u32[]{:S(2)}) collective-permute-start(bf16[256,256]{1,0:T(8,128)(2,1)} %get-tuple-element.61), channel_id=1, source_target_pairs={{0,4},{4,0},{8,12},{12,8},{16,20},{20,16},{24,28},{28,24},{1,5},{5... | collective-permute-start | bytes 393224 | tf_op jit(solution)/shard_map/ppermute | solution.py:483
  14.3 3.2 %stage_tokens.1 = (bf16[512,4096]{1,0:T(8,128)(2,1)S(1)}, bf16[2048,512]{1,0:T(8,128)(2,1)S(1)}) custom-call(s32[5]{0:T(128)S(1)} %stack.23.refs_0_, bf16[512,4096]{1,0:T(8,128)(2,1)} %collective-permute-done.refs_1_), custom_call_target="tpu_custom_call" | custom-call | bytes 10485760 | tf_op jit(solution)/shard_map/stage_tokens/pallas_call | solution.py:60
  17.8 2.8 %forward_encoder.4.refs_2_.refs_1_ = f32[2,512,256]{2,1,0:T(8,128)S(1)} custom-call(s32[5]{0:T(128)S(1)} %stack.23.refs_0_, bf16[1024,256]{1,0:T(8,128)(2,1)S(1)} %get-tuple-element.59.refs_4_.refs_1_, bf16[1024,256]{1,0:T(8,128)(2,1)} %collective-permute-done.7.refs_2_, bf16[512,4096]{1,0:T(8,128)(2,1)S(1)} %copy-done.1, ...), custom_call_target="tpu_custom_call" | custom-call | bytes 10485760 | tf_op jit(solution)/shard_map/forward_encoder/pallas_call | solution.py:60
  25.4 2.4 %hidden_units.2 = (bf16[2,512,256]{2,1,0:T(8,128)(2,1)S(1)}, f32[2,512,256]{2,1,0:T(8,128)S(1)}, bf16[2,512,256]{2,1,0:T(8,128)(2,1)S(1)}, bf16[256,256]{1,0:T(8,128)(2,1)S(1)}, bf16[256,256]{1,0:T(8,128)(2,1)S(1)}) custom-call(s32[5]{0:T(128)S(1)} %stack.23.refs_0_, f32[2,512,256]{2,1,0:T(8,128)S(1)} %forward_encoder.5.refs_1_, ...), custom_call_target="tpu_custom_call" | custom-call | bytes 12333056 | tf_op jit(solution)/shard_map/hidden_units/pallas_call | solution.py:60
  32.1 1.8 %collective-permute-start.16 = (bf16[1024,256]{1,0:T(8,128)(2,1)S(1)}, bf16[1024,256]{1,0:T(8,128)(2,1)S(1)}, u32[]{:S(2)}, u32[]{:S(2)}) collective-permute-start(bf16[1024,256]{1,0:T(8,128)(2,1)S(1)} %decoder_grad.4.refs_7_), channel_id=1, source_target_pairs={{0,2},{1,3},{2,0},{3,1},{4,6},{5,7},{6,4},{7,5},{8,10},{9,11},{10,... | collective-permute-start | bytes 1572872 | tf_op jit(solution)/shard_map/ppermute | solution.py:481
  33.9 2.6 %collective-permute-start.4 = (bf16[256,256]{1,0:T(8,128)(2,1)S(1)}, bf16[256,256]{1,0:T(8,128)(2,1)S(1)}, u32[]{:S(2)}, u32[]{:S(2)}) collective-permute-start(bf16[256,256]{1,0:T(8,128)(2,1)S(1)} %add_quarters.2.refs_3_.refs_1_), channel_id=1, source_target_pairs={{0,16},{4,20},{8,24},{12,28},{16,0},{20,4},{24,8},{28,12},{1,17},{... | collective-permute-start | bytes 393224 | tf_op jit(solution)/shard_map/ppermute | solution.py:483
  36.5 2.8 %forward_decoder.2 = (f32[2,512,256]{2,1,0:T(8,128)S(1)}, f32[256,256]{1,0:T(8,128)S(1)}) custom-call(s32[5]{0:T(128)S(1)} %stack.23.refs_0_, bf16[1024,256]{1,0:T(8,128)(2,1)S(1)} %get-tuple-element.64.refs_1_.refs_5_, bf16[1024,256]{1,0:T(8,128)(2,1)S(1)} %collective-permute-done.5.refs_2_, bf16[512,256]{1,0:T(8,128)(2,1)S(1)} %get-tuple-element.69.refs_5_.refs_3_, ...), custom_call_target="tpu_custom_call" | custom-call | bytes 11272192 | tf_op jit(solution)/shard_map/forward_decoder/pallas_call | solution.py:60
  39.3 1.9 %slope_pre.2.refs_3_.refs_2_ = bf16[2,512,256]{2,1,0:T(8,128)(2,1)S(1)} custom-call(s32[5]{0:T(128)S(1)} %stack.23.refs_0_, f32[2,512,256]{2,1,0:T(8,128)S(1)} %get-tuple-element.73.refs_1_, f32[256,256]{1,0:T(8,128)S(1)} %get-tuple-element.74.refs_2_, bf16[2,512,256]{2,1,0:T(8,128)(2,1)S(1)} %get-tuple-element.75.refs_3_, ...), custom_call_target="tpu_custom_call" | custom-call | bytes 12320768 | tf_op jit(solution)/shard_map/slope_pre/pallas_call | solution.py:60
  51.9 1.7 %collective-permute-done.15.refs_7_ = bf16[256,256]{1,0:T(8,128)(2,1)S(1)} collective-permute-done((bf16[256,256]{1,0:T(8,128)(2,1)S(1)}, bf16[256,256]{1,0:T(8,128)(2,1)S(1)}, u32[]{:S(2)}, u32[]{:S(2)}) %collective-permute-start.15) | collective-permute-done | bytes 131104 | tf_op jit(solution)/shard_map/ppermute | solution.py:483
  58.3 1.7 %collective-permute-start.22 = (bf16[1024,256]{1,0:T(8,128)(2,1)S(1)}, bf16[1024,256]{1,0:T(8,128)(2,1)S(1)}, u32[]{:S(2)}, u32[]{:S(2)}) collective-permute-start(bf16[1024,256]{1,0:T(8,128)(2,1)S(1)} %get-tuple-element.78.refs_5_.refs_3_.refs_1_), channel_id=1, source_target_pairs={{2,0},{3,1},{0,2},{1,3},{6,4},{7,5},{4,6},{5,7},{10,8},{11,9},{8,1... | collective-permute-start | bytes 1572872 | tf_op jit(solution)/shard_map/ppermute | solution.py:479
  62.4 3.1 %outer_step.1 = (f32[2,1024,256]{2,1,0:T(8,128)}, f32[2,1024,256]{2,1,0:T(8,128)}, f32[8,128]{1,0:T(8,128)S(1)}) custom-call(s32[5]{0:T(128)S(1)} %stack.23.refs_0_, s32[8]{0:T(128)S(1)} %copy-done.10, f32[2,1024,256]{2,1,0:T(8,128)S(1)} %copy-done.6, f32[2,1024,256]{2,1,0:T(8,128)S(1)} %copy-done.9, bf16[256,256]{1,0:T(8,128)(2,1)S(1)} %add_quarters.3.refs_3_.refs_4_, ...), custom_call_target="tpu_custom_call" | custom-call | bytes 8916992 | tf_op jit(solution)/shard_map/outer_step/pallas_call | solution.py:60
  65.5 1.8 %forward_encoder.6.refs_1_ = f32[2,512,256]{2,1,0:T(8,128)S(1)} custom-call(s32[5]{0:T(128)S(1)} %stack.23.refs_0_, bf16[1024,256]{1,0:T(8,128)(2,1)S(1)} %get-tuple-element.78.refs_5_.refs_3_.refs_1_, bf16[1024,256]{1,0:T(8,128)(2,1)S(1)} %collective-permute-done.21.refs_2_, bf16[512,4096]{1,0:T(8,128)(2,1)S(1)} %copy-done.1, ...), custom_call_target="tpu_custom_call" | custom-call | bytes 10485760 | tf_op jit(solution)/shard_map/forward_encoder/pallas_call | solution.py:60
  67.3 5.8 %collective-permute-done.22.refs_0_ = bf16[1024,256]{1,0:T(8,128)(2,1)S(1)} collective-permute-done((bf16[1024,256]{1,0:T(8,128)(2,1)S(1)}, bf16[1024,256]{1,0:T(8,128)(2,1)S(1)}, u32[]{:S(2)}, u32[]{:S(2)}) %collective-permute-start.22) | collective-permute-done | bytes 524320 | tf_op jit(solution)/shard_map/ppermute | solution.py:479
  75.1 2.4 %hidden_units.3 = (bf16[2,512,256]{2,1,0:T(8,128)(2,1)S(1)}, f32[2,512,256]{2,1,0:T(8,128)S(1)}, bf16[2,512,256]{2,1,0:T(8,128)(2,1)S(1)}, bf16[256,256]{1,0:T(8,128)(2,1)S(1)}, bf16[256,256]{1,0:T(8,128)(2,1)S(1)}) custom-call(s32[5]{0:T(128)S(1)} %stack.23.refs_0_, f32[2,512,256]{2,1,0:T(8,128)S(1)} %forward_encoder.7.refs_1_, ...), custom_call_target="tpu_custom_call" | custom-call | bytes 12324864 | tf_op jit(solution)/shard_map/hidden_units/pallas_call | solution.py:60
  77.5 6.4 %collective-permute-done.20.refs_0_ = bf16[1024,256]{1,0:T(8,128)(2,1)S(1)} collective-permute-done((bf16[1024,256]{1,0:T(8,128)(2,1)S(1)}, bf16[1024,256]{1,0:T(8,128)(2,1)S(1)}, u32[]{:S(2)}, u32[]{:S(2)}) %collective-permute-start.20) | collective-permute-done | bytes 524320 | tf_op jit(solution)/shard_map/ppermute | solution.py:479
  85.5 1.7 %collective-permute-start.27 = (bf16[1024,256]{1,0:T(8,128)(2,1)S(1)}, bf16[1024,256]{1,0:T(8,128)(2,1)S(1)}, u32[]{:S(2)}, u32[]{:S(2)}) collective-permute-start(bf16[1024,256]{1,0:T(8,128)(2,1)S(1)} %decoder_grad.6.refs_7_.refs_3_), channel_id=1, source_target_pairs={{0,2},{1,3},{2,0},{3,1},{4,6},{5,7},{6,4},{7,5},{8,10},{9,11},{10,... | collective-permute-start | bytes 1572872 | tf_op jit(solution)/shard_map/ppermute | solution.py:481
  87.2 2.8 %forward_decoder.3 = (f32[2,512,256]{2,1,0:T(8,128)S(1)}, f32[256,256]{1,0:T(8,128)S(1)}) custom-call(s32[5]{0:T(128)S(1)} %stack.23.refs_0_, bf16[1024,256]{1,0:T(8,128)(2,1)S(1)} %mix_rows.1.refs_8_.refs_1_.refs_5_, bf16[1024,256]{1,0:T(8,128)(2,1)S(1)} %collective-permute-done.19.refs_2_, bf16[512,256]{1,0:T(8,128)(2,1)S(1)} %get-tuple-element.84.refs_5_.refs_3_, ...), custom_call_target="tpu_custom_call" | custom-call | bytes 11272192 | tf_op jit(solution)/shard_map/forward_decoder/pallas_call | solution.py:60
  90.0 1.9 %slope_pre.3.refs_2_ = bf16[2,512,256]{2,1,0:T(8,128)(2,1)S(1)} custom-call(s32[5]{0:T(128)S(1)} %stack.23.refs_0_, f32[2,512,256]{2,1,0:T(8,128)S(1)} %get-tuple-element.88.refs_1_, f32[256,256]{1,0:T(8,128)S(1)} %get-tuple-element.89.refs_2_, bf16[2,512,256]{2,1,0:T(8,128)(2,1)S(1)} %get-tuple-element.90.refs_3_, ...), custom_call_target="tpu_custom_call" | custom-call | bytes 12320768 | tf_op jit(solution)/shard_map/slope_pre/pallas_call | solution.py:60
  92.9 7.4 %collective-permute-done.27.refs_6_ = bf16[1024,256]{1,0:T(8,128)(2,1)S(1)} collective-permute-done((bf16[1024,256]{1,0:T(8,128)(2,1)S(1)}, bf16[1024,256]{1,0:T(8,128)(2,1)S(1)}, u32[]{:S(2)}, u32[]{:S(2)}) %collective-permute-start.27) | collective-permute-done | bytes 524320 | tf_op jit(solution)/shard_map/ppermute | solution.py:481
  101.6 1.7 %collective-permute-start.28 = (bf16[256,256]{1,0:T(8,128)(2,1)S(1)}, bf16[256,256]{1,0:T(8,128)(2,1)S(1)}, u32[]{:S(2)}, u32[]{:S(2)}) collective-permute-start(bf16[256,256]{1,0:T(8,128)(2,1)S(1)} %encoder_grad.13.refs_3_), channel_id=1, source_target_pairs={{0,2},{1,3},{2,0},{3,1},{4,6},{5,7},{6,4},{7,5},{8,10},{9,11},{10,... | collective-permute-start | bytes 393224 | tf_op jit(solution)/shard_map/ppermute | solution.py:481
  104.3 2.8 %adam_rows.9 = (f32[1,2,1024,256]{3,2,1,0:T(8,128)}, f32[1,2,1024,256]{3,2,1,0:T(8,128)}, f32[1,2,1024,256]{3,2,1,0:T(8,128)}) custom-call(s32[8]{0:T(128)S(1)} %copy-done.10, f32[1024,256]{1,0:T(8,128)S(1)} %decoder_grad.7.refs_3_.refs_1_, f32[1,1,1024,256]{3,2,1,0:T(8,128)S(1)} %get-tuple-element.79.refs_2_, ...), custom_call_target="tpu_custom_call" | custom-call | bytes 11534336 | tf_op jit(solution)/shard_map/adam_rows/pallas_call | solution.py:60
  107.0 1.7 %collective-permute-done.29.refs_2_ = bf16[768,256]{1,0:T(8,128)(2,1)S(1)} collective-permute-done((bf16[768,256]{1,0:T(8,128)(2,1)S(1)}, bf16[768,256]{1,0:T(8,128)(2,1)S(1)}, u32[]{:S(2)}, u32[]{:S(2)}) %collective-permute-start.29) | collective-permute-done | bytes 393248 | tf_op jit(solution)/shard_map/ppermute | solution.py:481
  108.8 2.4 %adam_rows.10 = (f32[1,2,1024,256]{3,2,1,0:T(8,128)}, f32[1,2,1024,256]{3,2,1,0:T(8,128)}, f32[1,2,1024,256]{3,2,1,0:T(8,128)}) custom-call(s32[8]{0:T(128)S(1)} %copy-done.10, f32[768,256]{1,0:T(8,128)S(1)} %encoder_grad.15.refs_1_, ...), custom_call_target="tpu_custom_call", output_to_operand_aliasing={{0}: (7, {}), {1}: (8, {}), {2}: (9, {})} | custom-call | bytes 16908288 | tf_op jit(solution)/shard_map/adam_rows/pallas_call | solution.py:60
  (104 shorter events, 44.0 us)
Async XLA Ops:
  0.6 11.9 %collective-permute-start = (bf16[512,4096]{1,0:T(8,128)(2,1)}, bf16[512,4096]{1,0:T(8,128)(2,1)}, u32[]{:S(2)}, u32[]{:S(2)}) collective-permute-start(bf16[512,4096]{1,0:T(8,128)(2,1)} %refs_7_.3), channel_id=1, source_target_pairs={{0,1},{1,0},{2,3},{3,2},{4,5},{5,4},{6,7},{7,6},{8,9},{9,8},{10,11... | collective-permute-start | bytes 12582920 | tf_op jit(solution)/shard_map/ppermute | solution.py:478
  2.9 8.1 %collective-permute-start.7 = (bf16[1024,256]{1,0:T(8,128)(2,1)S(1)}, bf16[1024,256]{1,0:T(8,128)(2,1)}, u32[]{:S(2)}, u32[]{:S(2)}) collective-permute-start(bf16[1024,256]{1,0:T(8,128)(2,1)S(1)} %get-tuple-element.59.refs_4_.refs_1_), channel_id=1, source_target_pairs={{0,1},{1,0},{2,3},{3,2},{4,5},{5,4},{6,7},{7,6},{8,9},{9,8},{10,11... | collective-permute-start | bytes 1572872 | tf_op jit(solution)/shard_map/ppermute | solution.py:478
  3.0 19.2 %collective-permute-start.8 = (bf16[1024,256]{1,0:T(8,128)(2,1)S(1)}, bf16[1024,256]{1,0:T(8,128)(2,1)}, u32[]{:S(2)}, u32[]{:S(2)}) collective-permute-start(bf16[1024,256]{1,0:T(8,128)(2,1)S(1)} %get-tuple-element.59.refs_4_.refs_1_), channel_id=1, source_target_pairs={{2,0},{3,1},{0,2},{1,3},{6,4},{7,5},{4,6},{5,7},{10,8},{11,9},{8,1... | collective-permute-start | bytes 1572872 | tf_op jit(solution)/shard_map/ppermute | solution.py:479
  5.9 23.5 %collective-permute-start.6 = (bf16[1024,256]{1,0:T(8,128)(2,1)S(1)}, bf16[1024,256]{1,0:T(8,128)(2,1)}, u32[]{:S(2)}, u32[]{:S(2)}) collective-permute-start(bf16[1024,256]{1,0:T(8,128)(2,1)S(1)} %get-tuple-element.64.refs_1_.refs_5_), channel_id=1, source_target_pairs={{2,0},{3,1},{0,2},{1,3},{6,4},{7,5},{4,6},{5,7},{10,8},{11,9},{8,1... | collective-permute-start | bytes 1572872 | tf_op jit(solution)/shard_map/ppermute | solution.py:479
  9.0 11.6 %collective-permute-start.1 = (bf16[256,256]{1,0:T(8,128)(2,1)}, bf16[256,256]{1,0:T(8,128)(2,1)S(1)}, u32[]{:S(2)}, u32[]{:S(2)}) collective-permute-start(bf16[256,256]{1,0:T(8,128)(2,1)} %get-tuple-element.61), channel_id=1, source_target_pairs={{0,4},{4,0},{8,12},{12,8},{16,20},{20,16},{24,28},{28,24},{1,5},{5... | collective-permute-start | bytes 393224 | tf_op jit(solution)/shard_map/ppermute | solution.py:483
  11.0 9.6 %collective-permute-start.2 = (bf16[256,256]{1,0:T(8,128)(2,1)}, bf16[256,256]{1,0:T(8,128)(2,1)}, u32[]{:S(2)}, u32[]{:S(2)}) collective-permute-start(bf16[256,256]{1,0:T(8,128)(2,1)} %get-tuple-element.62), channel_id=1, source_target_pairs={{0,8},{4,12},{8,0},{12,4},{16,24},{20,28},{24,16},{28,20},{1,9},{5... | collective-permute-start | bytes 393224 | tf_op jit(solution)/shard_map/ppermute | solution.py:483
  12.6 8.0 %collective-permute-start.3 = (bf16[256,256]{1,0:T(8,128)(2,1)}, bf16[256,256]{1,0:T(8,128)(2,1)}, u32[]{:S(2)}, u32[]{:S(2)}) collective-permute-start(bf16[256,256]{1,0:T(8,128)(2,1)} %get-tuple-element.63), channel_id=1, source_target_pairs={{0,12},{4,8},{8,4},{12,0},{16,28},{20,24},{24,20},{28,16},{1,13},{... | collective-permute-start | bytes 393224 | tf_op jit(solution)/shard_map/ppermute | solution.py:483
  23.9 12.6 %collective-permute-start.5 = (bf16[1024,256]{1,0:T(8,128)(2,1)S(1)}, bf16[1024,256]{1,0:T(8,128)(2,1)S(1)}, u32[]{:S(2)}, u32[]{:S(2)}) collective-permute-start(bf16[1024,256]{1,0:T(8,128)(2,1)S(1)} %get-tuple-element.64.refs_1_.refs_5_), channel_id=1, source_target_pairs={{0,1},{1,0},{2,3},{3,2},{4,5},{5,4},{6,7},{7,6},{8,9},{9,8},{10,11... | collective-permute-start | bytes 1572872 | tf_op jit(solution)/shard_map/ppermute | solution.py:478
  30.5 8.8 %collective-permute-start.11 = (bf16[512,256]{1,0:T(8,128)(2,1)S(1)}, bf16[512,256]{1,0:T(8,128)(2,1)S(1)}, u32[]{:S(2)}, u32[]{:S(2)}) collective-permute-start(bf16[512,256]{1,0:T(8,128)(2,1)S(1)} %get-tuple-element.69.refs_5_.refs_3_), channel_id=1, source_target_pairs={{0,1},{1,0},{2,3},{3,2},{4,5},{5,4},{6,7},{7,6},{8,9},{9,8},{10,11... | collective-permute-start | bytes 786440 | tf_op jit(solution)/shard_map/ppermute | solution.py:478
  30.6 8.7 %collective-permute-start.12 = (bf16[512,256]{1,0:T(8,128)(2,1)S(1)}, bf16[512,256]{1,0:T(8,128)(2,1)S(1)}, u32[]{:S(2)}, u32[]{:S(2)}) collective-permute-start(bf16[512,256]{1,0:T(8,128)(2,1)S(1)} %get-tuple-element.70.refs_6_.refs_4_), channel_id=1, source_target_pairs={{0,1},{1,0},{2,3},{3,2},{4,5},{5,4},{6,7},{7,6},{8,9},{9,8},{10,11... | collective-permute-start | bytes 786440 | tf_op jit(solution)/shard_map/ppermute | solution.py:478
  32.1 15.9 %collective-permute-start.16 = (bf16[1024,256]{1,0:T(8,128)(2,1)S(1)}, bf16[1024,256]{1,0:T(8,128)(2,1)S(1)}, u32[]{:S(2)}, u32[]{:S(2)}) collective-permute-start(bf16[1024,256]{1,0:T(8,128)(2,1)S(1)} %decoder_grad.4.refs_7_), channel_id=1, source_target_pairs={{0,2},{1,3},{2,0},{3,1},{4,6},{5,7},{6,4},{7,5},{8,10},{9,11},{10,... | collective-permute-start | bytes 1572872 | tf_op jit(solution)/shard_map/ppermute | solution.py:481
  33.9 8.9 %collective-permute-start.4 = (bf16[256,256]{1,0:T(8,128)(2,1)S(1)}, bf16[256,256]{1,0:T(8,128)(2,1)S(1)}, u32[]{:S(2)}, u32[]{:S(2)}) collective-permute-start(bf16[256,256]{1,0:T(8,128)(2,1)S(1)} %add_quarters.2.refs_3_.refs_1_), channel_id=1, source_target_pairs={{0,16},{4,20},{8,24},{12,28},{16,0},{20,4},{24,8},{28,12},{1,17},{... | collective-permute-start | bytes 393224 | tf_op jit(solution)/shard_map/ppermute | solution.py:483
  44.0 11.9 %collective-permute-start.18 = (bf16[768,256]{1,0:T(8,128)(2,1)S(1)}, bf16[768,256]{1,0:T(8,128)(2,1)S(1)}, u32[]{:S(2)}, u32[]{:S(2)}) collective-permute-start(bf16[768,256]{1,0:T(8,128)(2,1)S(1)} %encoder_grad.8.refs_7_), channel_id=1, source_target_pairs={{0,2},{1,3},{2,0},{3,1},{4,6},{5,7},{6,4},{7,5},{8,10},{9,11},{10,... | collective-permute-start | bytes 1179656 | tf_op jit(solution)/shard_map/ppermute | solution.py:481
  44.5 7.4 %collective-permute-start.13 = (bf16[256,256]{1,0:T(8,128)(2,1)S(1)}, bf16[256,256]{1,0:T(8,128)(2,1)S(1)}, u32[]{:S(2)}, u32[]{:S(2)}) collective-permute-start(bf16[256,256]{1,0:T(8,128)(2,1)S(1)} %add_quarters.3.refs_3_.refs_4_), channel_id=1, source_target_pairs={{0,4},{4,0},{8,12},{12,8},{16,20},{20,16},{24,28},{28,24},{1,5},{5... | collective-permute-start | bytes 393224 | tf_op jit(solution)/shard_map/ppermute | solution.py:483
  46.7 6.9 %collective-permute-start.15 = (bf16[256,256]{1,0:T(8,128)(2,1)S(1)}, bf16[256,256]{1,0:T(8,128)(2,1)S(1)}, u32[]{:S(2)}, u32[]{:S(2)}) collective-permute-start(bf16[256,256]{1,0:T(8,128)(2,1)S(1)} %add_quarters.3.refs_3_.refs_4_), channel_id=1, source_target_pairs={{0,12},{4,8},{8,4},{12,0},{16,28},{20,24},{24,20},{28,16},{1,13},{... | collective-permute-start | bytes 393224 | tf_op jit(solution)/shard_map/ppermute | solution.py:483
  49.3 8.1 %collective-permute-start.17 = (bf16[256,256]{1,0:T(8,128)(2,1)S(1)}, bf16[256,256]{1,0:T(8,128)(2,1)S(1)}, u32[]{:S(2)}, u32[]{:S(2)}) collective-permute-start(bf16[256,256]{1,0:T(8,128)(2,1)S(1)} %encoder_grad.9.refs_3_), channel_id=1, source_target_pairs={{0,2},{1,3},{2,0},{3,1},{4,6},{5,7},{6,4},{7,5},{8,10},{9,11},{10,... | collective-permute-start | bytes 393224 | tf_op jit(solution)/shard_map/ppermute | solution.py:481
  58.2 7.3 %collective-permute-start.21 = (bf16[1024,256]{1,0:T(8,128)(2,1)S(1)}, bf16[1024,256]{1,0:T(8,128)(2,1)S(1)}, u32[]{:S(2)}, u32[]{:S(2)}) collective-permute-start(bf16[1024,256]{1,0:T(8,128)(2,1)S(1)} %get-tuple-element.78.refs_5_.refs_3_.refs_1_), channel_id=1, source_target_pairs={{0,1},{1,0},{2,3},{3,2},{4,5},{5,4},{6,7},{7,6},{8,9},{9,8},{10,11... | collective-permute-start | bytes 1572872 | tf_op jit(solution)/shard_map/ppermute | solution.py:478
  58.3 14.8 %collective-permute-start.22 = (bf16[1024,256]{1,0:T(8,128)(2,1)S(1)}, bf16[1024,256]{1,0:T(8,128)(2,1)S(1)}, u32[]{:S(2)}, u32[]{:S(2)}) collective-permute-start(bf16[1024,256]{1,0:T(8,128)(2,1)S(1)} %get-tuple-element.78.refs_5_.refs_3_.refs_1_), channel_id=1, source_target_pairs={{2,0},{3,1},{0,2},{1,3},{6,4},{7,5},{4,6},{5,7},{10,8},{11,9},{8,1... | collective-permute-start | bytes 1572872 | tf_op jit(solution)/shard_map/ppermute | solution.py:479
  62.0 21.9 %collective-permute-start.20 = (bf16[1024,256]{1,0:T(8,128)(2,1)S(1)}, bf16[1024,256]{1,0:T(8,128)(2,1)S(1)}, u32[]{:S(2)}, u32[]{:S(2)}) collective-permute-start(bf16[1024,256]{1,0:T(8,128)(2,1)S(1)} %mix_rows.1.refs_8_.refs_1_.refs_5_), channel_id=1, source_target_pairs={{2,0},{3,1},{0,2},{1,3},{6,4},{7,5},{4,6},{5,7},{10,8},{11,9},{8,1... | collective-permute-start | bytes 1572872 | tf_op jit(solution)/shard_map/ppermute | solution.py:479
  73.7 13.5 %collective-permute-start.19 = (bf16[1024,256]{1,0:T(8,128)(2,1)S(1)}, bf16[1024,256]{1,0:T(8,128)(2,1)S(1)}, u32[]{:S(2)}, u32[]{:S(2)}) collective-permute-start(bf16[1024,256]{1,0:T(8,128)(2,1)S(1)} %mix_rows.1.refs_8_.refs_1_.refs_5_), channel_id=1, source_target_pairs={{0,1},{1,0},{2,3},{3,2},{4,5},{5,4},{6,7},{7,6},{8,9},{9,8},{10,11... | collective-permute-start | bytes 1572872 | tf_op jit(solution)/shard_map/ppermute | solution.py:478
  83.9 6.1 %collective-permute-start.25 = (bf16[512,256]{1,0:T(8,128)(2,1)S(1)}, bf16[512,256]{1,0:T(8,128)(2,1)S(1)}, u32[]{:S(2)}, u32[]{:S(2)}) collective-permute-start(bf16[512,256]{1,0:T(8,128)(2,1)S(1)} %get-tuple-element.84.refs_5_.refs_3_), channel_id=1, source_target_pairs={{0,1},{1,0},{2,3},{3,2},{4,5},{5,4},{6,7},{7,6},{8,9},{9,8},{10,11... | collective-permute-start | bytes 786440 | tf_op jit(solution)/shard_map/ppermute | solution.py:478
  85.5 14.8 %collective-permute-start.27 = (bf16[1024,256]{1,0:T(8,128)(2,1)S(1)}, bf16[1024,256]{1,0:T(8,128)(2,1)S(1)}, u32[]{:S(2)}, u32[]{:S(2)}) collective-permute-start(bf16[1024,256]{1,0:T(8,128)(2,1)S(1)} %decoder_grad.6.refs_7_.refs_3_), channel_id=1, source_target_pairs={{0,2},{1,3},{2,0},{3,1},{4,6},{5,7},{6,4},{7,5},{8,10},{9,11},{10,... | collective-permute-start | bytes 1572872 | tf_op jit(solution)/shard_map/ppermute | solution.py:481
  92.5 16.3 %collective-permute-start.29 = (bf16[768,256]{1,0:T(8,128)(2,1)S(1)}, bf16[768,256]{1,0:T(8,128)(2,1)S(1)}, u32[]{:S(2)}, u32[]{:S(2)}) collective-permute-start(bf16[768,256]{1,0:T(8,128)(2,1)S(1)} %encoder_grad.12.refs_7_), channel_id=1, source_target_pairs={{0,2},{1,3},{2,0},{3,1},{4,6},{5,7},{6,4},{7,5},{8,10},{9,11},{10,... | collective-permute-start | bytes 1179656 | tf_op jit(solution)/shard_map/ppermute | solution.py:481
  101.6 9.5 %collective-permute-start.28 = (bf16[256,256]{1,0:T(8,128)(2,1)S(1)}, bf16[256,256]{1,0:T(8,128)(2,1)S(1)}, u32[]{:S(2)}, u32[]{:S(2)}) collective-permute-start(bf16[256,256]{1,0:T(8,128)(2,1)S(1)} %encoder_grad.13.refs_3_), channel_id=1, source_target_pairs={{0,2},{1,3},{2,0},{3,1},{4,6},{5,7},{6,4},{7,5},{8,10},{9,11},{10,... | collective-permute-start | bytes 393224 | tf_op jit(solution)/shard_map/ppermute | solution.py:481
  (18 other events, 57.0 us)

commit v10 on v9

--- a/solution.py
+++ b/solution.py
@@ -93,18 +93,23 @@
         low[...] = theta[0, k].astype(bf16)
 
 
-def cast_rows(weights):
+def cast_rows(weights, pos):
     _, _, rows, width = weights.shape
     return call(
         cast_body, "cast_rows", (), [(weights, whole(weights.shape))],
-        [(sds((rows, width), bf16), whole((rows, width)))] * 2,
-    )
+        [(sds((rows, width), bf16), whole((rows, width)))] * 2, after=[pos],
+    )
+
+
+def weight_rows(kinds, wide):
+    rows = [token_weight(kinds[j:j + wide].reshape(1, wide)) for j in range(0, kinds.shape[0], wide)]
+    return jnp.concatenate(rows + [jnp.zeros((EXTRA - len(rows), wide), f32)], 0)
 
 
 def weigh_body(kinds, other, out):
-    lanes, wide = kinds.shape
-    pad = jnp.zeros((EXTRA - lanes, wide), f32)
-    own = jnp.concatenate([token_weight(kinds[...]), pad], 0)
+    wide = other.shape[1]
+    lanes = kinds.shape[0] // wide
+    own = weight_rows(kinds, wide)
     for h, rows in enumerate((own, other[other.shape[0] - EXTRA:, :].astype(f32))):
         turned = rows.T
         for j in range(lanes):
@@ -122,8 +127,7 @@
     outs = refs
     if refs[0].dtype != bf16:
         kinds, outs = refs[0], refs[1:]
-        pad = jnp.zeros((EXTRA - kinds.shape[0], kinds.shape[1]), f32)
-        outs[-1][cut:, :] = jnp.concatenate([token_weight(kinds[...]), pad], 0).astype(bf16)
+        outs[-1][cut:, :] = weight_rows(kinds, x.shape[1]).astype(bf16)
     for n, out in enumerate(outs):
         out[:cut, :] = x[n * cut:(n + 1) * cut, :]
 
@@ -482,16 +486,14 @@
         a, "fsdp", [(f, ((f // 2 + s) % chips) * 2 + f % 2) for f in range(n_fsdp)])
     across = lambda a, bit: lax.ppermute(a, "replica", [(r, r ^ bit) for r in range(n_rep)])
 
-    enc, dec = cast_rows(weights)
-
     chip = lax.axis_index("fsdp") // 2
     core = lax.axis_index("fsdp") % 2
     at = [((chip + s) % chips) * 2 for s in range(chips)]
     pos = jnp.stack([lax.axis_index("replica")] + [a + core for a in at] + [a + 1 - core for a in at]).astype(jnp.int32)
 
+    enc, dec = cast_rows(weights, pos)
     x_par = to_partner(inputs)
     quarters = outer_start(pos, plan, anchor, weights, [enc])
-    lanes = kinds.reshape(-1, width)
     xs, xt = zip(*[turn(pos, x, chips, stage) for x, stage in ((inputs, False), (x_par, True))])
     own = outer_add(plan, [quarters[0]] + [across(quarters[m], m) for m in range(1, 4)], n_rep == 4, xt)
 
@@ -508,13 +510,13 @@
 
         carry = forward(pos, [], [(enc, 1, 0, rows), (enc_near, 1 + chips, 0, rows)], xs, rows, False)
         ready = [own, *xt] if step == 0 else [token]
-        riders = [lanes] if step == 0 else []
+        riders = [kinds] if step == 0 else []
         part = [(p, 1 + s, n * cut, cut) for s in others for n, p in enumerate(
             relay(enc_far[s], cuts, [*carry, *ready], *riders))]
         pending = [(to_partner(p), slot + chips, off, size) for p, slot, off, size in part]
         carry = forward(pos, carry, part, xs, rows, False)
         if step == 0:
-            cw = weigh(lanes, pending[-1][0], tokens)
+            cw = weigh(kinds, pending[-1][0], tokens)
         hidden, slope, counted, w_hi, w_lo = hidden_rows(pos, carry[0], cw, pending, xs, rows, scale)
         dec_grad = lambda s, lows, more, dtype, after: grad_rows(
             functools.partial(decoder_body, scale, s * rows, len(lows)), "decoder_grad", rows, xt,

time: 113 us -> 112 us (level)
  Pallas kernels: 53.9 us -> 48.9 us
  waiting for transfers between devices: 27.9 us -> 31.5 us
  starting transfers between devices: 26.3 us -> 28.4 us
  local copies, waits for them, and re-layouts: 3.55 us -> 1.77 us
    pallas_call x42, Pallas kernels: 53.9 us -> 48.9 us  [call(): pl.pallas_call(run, name=name, out_shape=[o for o, _ in outs], grid_spec=...]
    ppermute x4, waiting for transfers between devices: 13.8 us -> 17 us  [local(): lax.ppermute(a, 'fsdp', [((f // 2 + s) % chips * 2 + f % 2, f) for f in r...]
    ppermute x7, starting transfers between devices: 10.2 us -> 12.3 us  [local(): lax.ppermute(a, 'replica', [(r, r ^ bit) for r in range(n_rep)])]
    unnamed x24 -> x18, local copies, waits for them, and re-layouts: 3.45 us -> 1.69 us
  transfers between devices with their start and end apart: 30 -> 30, of which waited for: 9 -> 10; matrix products, arithmetic and copies ran while one was open for 0% -> 0% of each run, Pallas kernels for 46% -> 42%
where the time goes in v10:
time: 112 us
  Pallas kernels  48.9 us (44%)
  waiting for transfers between devices  31.5 us (28%)
  starting transfers between devices  28.4 us (25%)
  local copies, waits for them, and re-layouts  1.77 us (2%)
    pallas_call x42, Pallas kernels, call(): pl.pallas_call(run, name=name, out_shape=[o for o, _ in outs], grid_spec=...  48.9 us
    ppermute x4, waiting for transfers between devices, local(): lax.ppermute(a, 'fsdp', [((f // 2 + s) % chips * 2 + f % 2, f) for f in r...  17 us
    ppermute x7, starting transfers between devices, local(): lax.ppermute(a, 'replica', [(r, r ^ bit) for r in range(n_rep)])  12.3 us
    ppermute x6, waiting for transfers between devices, local(): lax.ppermute(a, 'fsdp', [(f, (f // 2 + s) % chips * 2 + f % 2) for f in r...  10.6 us
    ppermute x6, starting transfers between devices, local(): lax.ppermute(a, 'fsdp', [(f, (f // 2 + s) % chips * 2 + f % 2) for f in r...  7.86 us
    ppermute x4, starting transfers between devices, local(): lax.ppermute(a, 'fsdp', [((f // 2 + s) % chips * 2 + f % 2, f) for f in r...  5.14 us
    ppermute x7, waiting for transfers between devices, local(): lax.ppermute(a, 'replica', [(r, r ^ bit) for r in range(n_rep)])  3.75 us
    ppermute x13, starting transfers between devices, local(): to_partner = lambda a: lax.ppermute(a, 'fsdp', partner)  3.15 us
  transfers between devices with their start and end apart: 30, of which 10 were waited for; matrix products, arithmetic and copies ran while one was open for 0% of the time, Pallas kernels for 42%

profile of v10, /device:TPU:0, one launch (start us, length us, event | category | flops | bytes accessed | tf_op | source)
XLA Modules:
  0.0 111.7 jit_solution(2518995766190533307)
XLA Ops:
  3.1 3.0 %collective-permute-start.8 = (bf16[1024,256]{1,0:T(8,128)(2,1)S(1)}, bf16[1024,256]{1,0:T(8,128)(2,1)S(1)}, u32[]{:S(2)}, u32[]{:S(2)}) collective-permute-start(bf16[1024,256]{1,0:T(8,128)(2,1)S(1)} %get-tuple-element.59.refs_4_.refs_1_), channel_id=1, source_target_pairs={{2,0},{3,1},{0,2},{1,3},{6,4},{7,5},{4,6},{5,7},{10,8},{11,9},{8,1... | collective-permute-start | bytes 1572872 | tf_op jit(solution)/shard_map/ppermute | solution.py:483
  6.8 2.0 %collective-permute-start.1 = (bf16[256,256]{1,0:T(8,128)(2,1)S(1)}, bf16[256,256]{1,0:T(8,128)(2,1)S(1)}, u32[]{:S(2)}, u32[]{:S(2)}) collective-permute-start(bf16[256,256]{1,0:T(8,128)(2,1)S(1)} %get-tuple-element.61), channel_id=1, source_target_pairs={{0,4},{4,0},{8,12},{12,8},{16,20},{20,16},{24,28},{28,24},{1,5},{5... | collective-permute-start | bytes 393224 | tf_op jit(solution)/shard_map/ppermute | solution.py:487
  8.8 2.8 %collective-permute-start.2 = (bf16[256,256]{1,0:T(8,128)(2,1)S(1)}, bf16[256,256]{1,0:T(8,128)(2,1)S(1)}, u32[]{:S(2)}, u32[]{:S(2)}) collective-permute-start(bf16[256,256]{1,0:T(8,128)(2,1)S(1)} %get-tuple-element.62), channel_id=1, source_target_pairs={{0,8},{4,12},{8,0},{12,4},{16,24},{20,28},{24,16},{28,20},{1,9},{5... | collective-permute-start | bytes 393224 | tf_op jit(solution)/shard_map/ppermute | solution.py:487
  14.2 2.9 %stage_tokens.1 = (bf16[512,4096]{1,0:T(8,128)(2,1)S(1)}, bf16[2048,512]{1,0:T(8,128)(2,1)S(1)}) custom-call(s32[5]{0:T(128)S(1)} %stack.23.refs_0_.refs_1_, bf16[512,4096]{1,0:T(8,128)(2,1)} %collective-permute-done.refs_1_), custom_call_target="tpu_custom_call" | custom-call | bytes 10485760 | tf_op jit(solution)/shard_map/stage_tokens/pallas_call | solution.py:60
  17.1 1.8 %forward_encoder.4.refs_2_.refs_1_ = f32[2,512,256]{2,1,0:T(8,128)S(1)} custom-call(s32[5]{0:T(128)S(1)} %stack.23.refs_0_.refs_1_, bf16[1024,256]{1,0:T(8,128)(2,1)S(1)} %get-tuple-element.59.refs_4_.refs_1_, bf16[1024,256]{1,0:T(8,128)(2,1)S(1)} %collective-permute-done.7.refs_2_, bf16[512,4096]{1,0:T(8,128)(2,1)S(1)} %copy-done, ...), custom_call_target="tpu_custom_call" | custom-call | bytes 10485760 | tf_op jit(solution)/shard_map/forward_encoder/pallas_call | solution.py:60
  22.2 2.4 %hidden_units.2 = (bf16[2,512,256]{2,1,0:T(8,128)(2,1)S(1)}, f32[2,512,256]{2,1,0:T(8,128)S(1)}, bf16[2,512,256]{2,1,0:T(8,128)(2,1)S(1)}, bf16[256,256]{1,0:T(8,128)(2,1)S(1)}, bf16[256,256]{1,0:T(8,128)(2,1)S(1)}) custom-call(s32[5]{0:T(128)S(1)} %stack.23.refs_0_.refs_1_, f32[2,512,256]{2,1,0:T(8,128)S(1)} %forward_encoder.5.refs_1_, ...), custom_call_target="tpu_custom_call" | custom-call | bytes 12333056 | tf_op jit(solution)/shard_map/hidden_units/pallas_call | solution.py:60
  24.6 4.8 %collective-permute-done.6.refs_0_ = bf16[1024,256]{1,0:T(8,128)(2,1)S(1)} collective-permute-done((bf16[1024,256]{1,0:T(8,128)(2,1)S(1)}, bf16[1024,256]{1,0:T(8,128)(2,1)S(1)}, u32[]{:S(2)}, u32[]{:S(2)}) %collective-permute-start.6) | collective-permute-done | bytes 524320 | tf_op jit(solution)/shard_map/ppermute | solution.py:483
  31.1 1.8 %collective-permute-start.16 = (bf16[1024,256]{1,0:T(8,128)(2,1)S(1)}, bf16[1024,256]{1,0:T(8,128)(2,1)S(1)}, u32[]{:S(2)}, u32[]{:S(2)}) collective-permute-start(bf16[1024,256]{1,0:T(8,128)(2,1)S(1)} %decoder_grad.4.refs_7_), channel_id=1, source_target_pairs={{0,2},{1,3},{2,0},{3,1},{4,6},{5,7},{6,4},{7,5},{8,10},{9,11},{10,... | collective-permute-start | bytes 1572872 | tf_op jit(solution)/shard_map/ppermute | solution.py:485
  32.9 2.6 %collective-permute-start.4 = (bf16[256,256]{1,0:T(8,128)(2,1)S(1)}, bf16[256,256]{1,0:T(8,128)(2,1)S(1)}, u32[]{:S(2)}, u32[]{:S(2)}) collective-permute-start(bf16[256,256]{1,0:T(8,128)(2,1)S(1)} %add_quarters.2.refs_3_.refs_1_), channel_id=1, source_target_pairs={{0,16},{4,20},{8,24},{12,28},{16,0},{20,4},{24,8},{28,12},{1,17},{... | collective-permute-start | bytes 393224 | tf_op jit(solution)/shard_map/ppermute | solution.py:487
  35.5 2.8 %forward_decoder.2 = (f32[2,512,256]{2,1,0:T(8,128)S(1)}, f32[256,256]{1,0:T(8,128)S(1)}) custom-call(s32[5]{0:T(128)S(1)} %stack.23.refs_0_.refs_1_, bf16[1024,256]{1,0:T(8,128)(2,1)S(1)} %get-tuple-element.64.refs_1_.refs_5_, bf16[1024,256]{1,0:T(8,128)(2,1)S(1)} %collective-permute-done.5.refs_2_, bf16[512,256]{1,0:T(8,128)(2,1)S(1)} %get-tuple-element.69.refs_5_.refs_3_, ...), custom_call_target="tpu_custom_call" | custom-call | bytes 11272192 | tf_op jit(solution)/shard_map/forward_decoder/pallas_call | solution.py:60
  38.2 1.9 %slope_pre.2.refs_3_.refs_2_ = bf16[2,512,256]{2,1,0:T(8,128)(2,1)S(1)} custom-call(s32[5]{0:T(128)S(1)} %stack.23.refs_0_.refs_1_, f32[2,512,256]{2,1,0:T(8,128)S(1)} %get-tuple-element.73.refs_1_, f32[256,256]{1,0:T(8,128)S(1)} %get-tuple-element.74.refs_2_, bf16[2,512,256]{2,1,0:T(8,128)(2,1)S(1)} %get-tuple-element.75.refs_3_, ...), custom_call_target="tpu_custom_call" | custom-call | bytes 12320768 | tf_op jit(solution)/shard_map/slope_pre/pallas_call | solution.py:60
  57.2 1.7 %collective-permute-start.22 = (bf16[1024,256]{1,0:T(8,128)(2,1)S(1)}, bf16[1024,256]{1,0:T(8,128)(2,1)S(1)}, u32[]{:S(2)}, u32[]{:S(2)}) collective-permute-start(bf16[1024,256]{1,0:T(8,128)(2,1)S(1)} %get-tuple-element.78.refs_5_.refs_3_.refs_1_), channel_id=1, source_target_pairs={{2,0},{3,1},{0,2},{1,3},{6,4},{7,5},{4,6},{5,7},{10,8},{11,9},{8,1... | collective-permute-start | bytes 1572872 | tf_op jit(solution)/shard_map/ppermute | solution.py:483
  61.4 3.1 %outer_step.1 = (f32[2,1024,256]{2,1,0:T(8,128)}, f32[2,1024,256]{2,1,0:T(8,128)}, f32[8,128]{1,0:T(8,128)S(1)}) custom-call(s32[5]{0:T(128)S(1)} %stack.23.refs_0_.refs_1_, s32[8]{0:T(128)S(1)} %copy-done.7, f32[2,1024,256]{2,1,0:T(8,128)S(1)} %copy-done.3, f32[2,1024,256]{2,1,0:T(8,128)S(1)} %copy-done.6, ...), custom_call_target="tpu_custom_call" | custom-call | bytes 8916992 | tf_op jit(solution)/shard_map/outer_step/pallas_call | solution.py:60
  64.5 1.8 %forward_encoder.6.refs_1_ = f32[2,512,256]{2,1,0:T(8,128)S(1)} custom-call(s32[5]{0:T(128)S(1)} %stack.23.refs_0_.refs_1_, bf16[1024,256]{1,0:T(8,128)(2,1)S(1)} %get-tuple-element.78.refs_5_.refs_3_.refs_1_, bf16[1024,256]{1,0:T(8,128)(2,1)S(1)} %collective-permute-done.21.refs_2_, bf16[512,4096]{1,0:T(8,128)(2,1)S(1)} %copy-done, ...), custom_call_target="tpu_custom_call" | custom-call | bytes 10485760 | tf_op jit(solution)/shard_map/forward_encoder/pallas_call | solution.py:60
  66.2 5.8 %collective-permute-done.22.refs_0_ = bf16[1024,256]{1,0:T(8,128)(2,1)S(1)} collective-permute-done((bf16[1024,256]{1,0:T(8,128)(2,1)S(1)}, bf16[1024,256]{1,0:T(8,128)(2,1)S(1)}, u32[]{:S(2)}, u32[]{:S(2)}) %collective-permute-start.22) | collective-permute-done | bytes 524320 | tf_op jit(solution)/shard_map/ppermute | solution.py:483
  74.1 2.4 %hidden_units.3 = (bf16[2,512,256]{2,1,0:T(8,128)(2,1)S(1)}, f32[2,512,256]{2,1,0:T(8,128)S(1)}, bf16[2,512,256]{2,1,0:T(8,128)(2,1)S(1)}, bf16[256,256]{1,0:T(8,128)(2,1)S(1)}, bf16[256,256]{1,0:T(8,128)(2,1)S(1)}) custom-call(s32[5]{0:T(128)S(1)} %stack.23.refs_0_.refs_1_, f32[2,512,256]{2,1,0:T(8,128)S(1)} %forward_encoder.7.refs_1_, ...), custom_call_target="tpu_custom_call" | custom-call | bytes 12324864 | tf_op jit(solution)/shard_map/hidden_units/pallas_call | solution.py:60
  76.4 6.4 %collective-permute-done.20.refs_0_ = bf16[1024,256]{1,0:T(8,128)(2,1)S(1)} collective-permute-done((bf16[1024,256]{1,0:T(8,128)(2,1)S(1)}, bf16[1024,256]{1,0:T(8,128)(2,1)S(1)}, u32[]{:S(2)}, u32[]{:S(2)}) %collective-permute-start.20) | collective-permute-done | bytes 524320 | tf_op jit(solution)/shard_map/ppermute | solution.py:483
  84.4 1.7 %collective-permute-start.27 = (bf16[1024,256]{1,0:T(8,128)(2,1)S(1)}, bf16[1024,256]{1,0:T(8,128)(2,1)S(1)}, u32[]{:S(2)}, u32[]{:S(2)}) collective-permute-start(bf16[1024,256]{1,0:T(8,128)(2,1)S(1)} %decoder_grad.6.refs_7_.refs_3_), channel_id=1, source_target_pairs={{0,2},{1,3},{2,0},{3,1},{4,6},{5,7},{6,4},{7,5},{8,10},{9,11},{10,... | collective-permute-start | bytes 1572872 | tf_op jit(solution)/shard_map/ppermute | solution.py:485
  86.2 2.8 %forward_decoder.3 = (f32[2,512,256]{2,1,0:T(8,128)S(1)}, f32[256,256]{1,0:T(8,128)S(1)}) custom-call(s32[5]{0:T(128)S(1)} %stack.23.refs_0_.refs_1_, bf16[1024,256]{1,0:T(8,128)(2,1)S(1)} %mix_rows.1.refs_8_.refs_1_.refs_5_, bf16[1024,256]{1,0:T(8,128)(2,1)S(1)} %collective-permute-done.19.refs_2_, bf16[512,256]{1,0:T(8,128)(2,1)S(1)} %get-tuple-element.84.refs_5_.refs_3_, ...), custom_call_target="tpu_custom_call" | custom-call | bytes 11272192 | tf_op jit(solution)/shard_map/forward_decoder/pallas_call | solution.py:60
  89.0 1.9 %slope_pre.3.refs_2_ = bf16[2,512,256]{2,1,0:T(8,128)(2,1)S(1)} custom-call(s32[5]{0:T(128)S(1)} %stack.23.refs_0_.refs_1_, f32[2,512,256]{2,1,0:T(8,128)S(1)} %get-tuple-element.88.refs_1_, f32[256,256]{1,0:T(8,128)S(1)} %get-tuple-element.89.refs_2_, bf16[2,512,256]{2,1,0:T(8,128)(2,1)S(1)} %get-tuple-element.90.refs_3_, ...), custom_call_target="tpu_custom_call" | custom-call | bytes 12320768 | tf_op jit(solution)/shard_map/slope_pre/pallas_call | solution.py:60
  91.9 7.4 %collective-permute-done.27.refs_6_ = bf16[1024,256]{1,0:T(8,128)(2,1)S(1)} collective-permute-done((bf16[1024,256]{1,0:T(8,128)(2,1)S(1)}, bf16[1024,256]{1,0:T(8,128)(2,1)S(1)}, u32[]{:S(2)}, u32[]{:S(2)}) %collective-permute-start.27) | collective-permute-done | bytes 524320 | tf_op jit(solution)/shard_map/ppermute | solution.py:485
  100.6 1.7 %collective-permute-start.28 = (bf16[256,256]{1,0:T(8,128)(2,1)S(1)}, bf16[256,256]{1,0:T(8,128)(2,1)S(1)}, u32[]{:S(2)}, u32[]{:S(2)}) collective-permute-start(bf16[256,256]{1,0:T(8,128)(2,1)S(1)} %encoder_grad.13.refs_3_), channel_id=1, source_target_pairs={{0,2},{1,3},{2,0},{3,1},{4,6},{5,7},{6,4},{7,5},{8,10},{9,11},{10,... | collective-permute-start | bytes 393224 | tf_op jit(solution)/shard_map/ppermute | solution.py:485
  103.2 2.8 %adam_rows.9 = (f32[1,2,1024,256]{3,2,1,0:T(8,128)}, f32[1,2,1024,256]{3,2,1,0:T(8,128)}, f32[1,2,1024,256]{3,2,1,0:T(8,128)}) custom-call(s32[8]{0:T(128)S(1)} %copy-done.7, f32[1024,256]{1,0:T(8,128)S(1)} %decoder_grad.7.refs_3_.refs_1_, f32[1,1,1024,256]{3,2,1,0:T(8,128)S(1)} %get-tuple-element.79.refs_2_, ...), custom_call_target="tpu_custom_call" | custom-call | bytes 11534336 | tf_op jit(solution)/shard_map/adam_rows/pallas_call | solution.py:60
  107.7 2.4 %adam_rows.10 = (f32[1,2,1024,256]{3,2,1,0:T(8,128)}, f32[1,2,1024,256]{3,2,1,0:T(8,128)}, f32[1,2,1024,256]{3,2,1,0:T(8,128)}) custom-call(s32[8]{0:T(128)S(1)} %copy-done.7, f32[768,256]{1,0:T(8,128)S(1)} %encoder_grad.15.refs_1_, bf16[768,256]{1,0:T(8,128)(2,1)S(1)} %collective-permute-done.29.refs_2_, ...), custom_call_target="tpu_custom_call", output_to_operand_aliasing={{0}: (7, {}), {1}: (8, {}), {2}: (9, {})} | custom-call | bytes 16908288 | tf_op jit(solution)/shard_map/adam_rows/pallas_call | solution.py:60
  (97 shorter events, 40.0 us)
Async XLA Ops:
  0.6 11.0 %collective-permute-start = (bf16[512,4096]{1,0:T(8,128)(2,1)}, bf16[512,4096]{1,0:T(8,128)(2,1)}, u32[]{:S(2)}, u32[]{:S(2)}) collective-permute-start(bf16[512,4096]{1,0:T(8,128)(2,1)} %refs_7_.3), channel_id=1, source_target_pairs={{0,1},{1,0},{2,3},{3,2},{4,5},{5,4},{6,7},{7,6},{8,9},{9,8},{10,11... | collective-permute-start | bytes 12582920 | tf_op jit(solution)/shard_map/ppermute | solution.py:482
  3.1 16.9 %collective-permute-start.8 = (bf16[1024,256]{1,0:T(8,128)(2,1)S(1)}, bf16[1024,256]{1,0:T(8,128)(2,1)S(1)}, u32[]{:S(2)}, u32[]{:S(2)}) collective-permute-start(bf16[1024,256]{1,0:T(8,128)(2,1)S(1)} %get-tuple-element.59.refs_4_.refs_1_), channel_id=1, source_target_pairs={{2,0},{3,1},{0,2},{1,3},{6,4},{7,5},{4,6},{5,7},{10,8},{11,9},{8,1... | collective-permute-start | bytes 1572872 | tf_op jit(solution)/shard_map/ppermute | solution.py:483
  6.0 23.4 %collective-permute-start.6 = (bf16[1024,256]{1,0:T(8,128)(2,1)S(1)}, bf16[1024,256]{1,0:T(8,128)(2,1)S(1)}, u32[]{:S(2)}, u32[]{:S(2)}) collective-permute-start(bf16[1024,256]{1,0:T(8,128)(2,1)S(1)} %get-tuple-element.64.refs_1_.refs_5_), channel_id=1, source_target_pairs={{2,0},{3,1},{0,2},{1,3},{6,4},{7,5},{4,6},{5,7},{10,8},{11,9},{8,1... | collective-permute-start | bytes 1572872 | tf_op jit(solution)/shard_map/ppermute | solution.py:483
  6.8 12.1 %collective-permute-start.1 = (bf16[256,256]{1,0:T(8,128)(2,1)S(1)}, bf16[256,256]{1,0:T(8,128)(2,1)S(1)}, u32[]{:S(2)}, u32[]{:S(2)}) collective-permute-start(bf16[256,256]{1,0:T(8,128)(2,1)S(1)} %get-tuple-element.61), channel_id=1, source_target_pairs={{0,4},{4,0},{8,12},{12,8},{16,20},{20,16},{24,28},{28,24},{1,5},{5... | collective-permute-start | bytes 393224 | tf_op jit(solution)/shard_map/ppermute | solution.py:487
  8.8 10.1 %collective-permute-start.2 = (bf16[256,256]{1,0:T(8,128)(2,1)S(1)}, bf16[256,256]{1,0:T(8,128)(2,1)S(1)}, u32[]{:S(2)}, u32[]{:S(2)}) collective-permute-start(bf16[256,256]{1,0:T(8,128)(2,1)S(1)} %get-tuple-element.62), channel_id=1, source_target_pairs={{0,8},{4,12},{8,0},{12,4},{16,24},{20,28},{24,16},{28,20},{1,9},{5... | collective-permute-start | bytes 393224 | tf_op jit(solution)/shard_map/ppermute | solution.py:487
  11.6 7.7 %collective-permute-start.3 = (bf16[256,256]{1,0:T(8,128)(2,1)S(1)}, bf16[256,256]{1,0:T(8,128)(2,1)S(1)}, u32[]{:S(2)}, u32[]{:S(2)}) collective-permute-start(bf16[256,256]{1,0:T(8,128)(2,1)S(1)} %get-tuple-element.63), channel_id=1, source_target_pairs={{0,12},{4,8},{8,4},{12,0},{16,28},{20,24},{24,20},{28,16},{1,13},{... | collective-permute-start | bytes 393224 | tf_op jit(solution)/shard_map/ppermute | solution.py:487
  20.6 14.8 %collective-permute-start.5 = (bf16[1024,256]{1,0:T(8,128)(2,1)S(1)}, bf16[1024,256]{1,0:T(8,128)(2,1)S(1)}, u32[]{:S(2)}, u32[]{:S(2)}) collective-permute-start(bf16[1024,256]{1,0:T(8,128)(2,1)S(1)} %get-tuple-element.64.refs_1_.refs_5_), channel_id=1, source_target_pairs={{0,1},{1,0},{2,3},{3,2},{4,5},{5,4},{6,7},{7,6},{8,9},{9,8},{10,11... | collective-permute-start | bytes 1572872 | tf_op jit(solution)/shard_map/ppermute | solution.py:482
  29.5 8.8 %collective-permute-start.11 = (bf16[512,256]{1,0:T(8,128)(2,1)S(1)}, bf16[512,256]{1,0:T(8,128)(2,1)S(1)}, u32[]{:S(2)}, u32[]{:S(2)}) collective-permute-start(bf16[512,256]{1,0:T(8,128)(2,1)S(1)} %get-tuple-element.69.refs_5_.refs_3_), channel_id=1, source_target_pairs={{0,1},{1,0},{2,3},{3,2},{4,5},{5,4},{6,7},{7,6},{8,9},{9,8},{10,11... | collective-permute-start | bytes 786440 | tf_op jit(solution)/shard_map/ppermute | solution.py:482
  29.6 8.7 %collective-permute-start.12 = (bf16[512,256]{1,0:T(8,128)(2,1)S(1)}, bf16[512,256]{1,0:T(8,128)(2,1)S(1)}, u32[]{:S(2)}, u32[]{:S(2)}) collective-permute-start(bf16[512,256]{1,0:T(8,128)(2,1)S(1)} %get-tuple-element.70.refs_6_.refs_4_), channel_id=1, source_target_pairs={{0,1},{1,0},{2,3},{3,2},{4,5},{5,4},{6,7},{7,6},{8,9},{9,8},{10,11... | collective-permute-start | bytes 786440 | tf_op jit(solution)/shard_map/ppermute | solution.py:482
  31.1 15.9 %collective-permute-start.16 = (bf16[1024,256]{1,0:T(8,128)(2,1)S(1)}, bf16[1024,256]{1,0:T(8,128)(2,1)S(1)}, u32[]{:S(2)}, u32[]{:S(2)}) collective-permute-start(bf16[1024,256]{1,0:T(8,128)(2,1)S(1)} %decoder_grad.4.refs_7_), channel_id=1, source_target_pairs={{0,2},{1,3},{2,0},{3,1},{4,6},{5,7},{6,4},{7,5},{8,10},{9,11},{10,... | collective-permute-start | bytes 1572872 | tf_op jit(solution)/shard_map/ppermute | solution.py:485
  32.9 8.9 %collective-permute-start.4 = (bf16[256,256]{1,0:T(8,128)(2,1)S(1)}, bf16[256,256]{1,0:T(8,128)(2,1)S(1)}, u32[]{:S(2)}, u32[]{:S(2)}) collective-permute-start(bf16[256,256]{1,0:T(8,128)(2,1)S(1)} %add_quarters.2.refs_3_.refs_1_), channel_id=1, source_target_pairs={{0,16},{4,20},{8,24},{12,28},{16,0},{20,4},{24,8},{28,12},{1,17},{... | collective-permute-start | bytes 393224 | tf_op jit(solution)/shard_map/ppermute | solution.py:487
  42.9 11.9 %collective-permute-start.18 = (bf16[768,256]{1,0:T(8,128)(2,1)S(1)}, bf16[768,256]{1,0:T(8,128)(2,1)S(1)}, u32[]{:S(2)}, u32[]{:S(2)}) collective-permute-start(bf16[768,256]{1,0:T(8,128)(2,1)S(1)} %encoder_grad.8.refs_7_), channel_id=1, source_target_pairs={{0,2},{1,3},{2,0},{3,1},{4,6},{5,7},{6,4},{7,5},{8,10},{9,11},{10,... | collective-permute-start | bytes 1179656 | tf_op jit(solution)/shard_map/ppermute | solution.py:485
  43.5 7.4 %collective-permute-start.13 = (bf16[256,256]{1,0:T(8,128)(2,1)S(1)}, bf16[256,256]{1,0:T(8,128)(2,1)S(1)}, u32[]{:S(2)}, u32[]{:S(2)}) collective-permute-start(bf16[256,256]{1,0:T(8,128)(2,1)S(1)} %add_quarters.3.refs_3_.refs_4_), channel_id=1, source_target_pairs={{0,4},{4,0},{8,12},{12,8},{16,20},{20,16},{24,28},{28,24},{1,5},{5... | collective-permute-start | bytes 393224 | tf_op jit(solution)/shard_map/ppermute | solution.py:487
  45.7 6.9 %collective-permute-start.15 = (bf16[256,256]{1,0:T(8,128)(2,1)S(1)}, bf16[256,256]{1,0:T(8,128)(2,1)S(1)}, u32[]{:S(2)}, u32[]{:S(2)}) collective-permute-start(bf16[256,256]{1,0:T(8,128)(2,1)S(1)} %add_quarters.3.refs_3_.refs_4_), channel_id=1, source_target_pairs={{0,12},{4,8},{8,4},{12,0},{16,28},{20,24},{24,20},{28,16},{1,13},{... | collective-permute-start | bytes 393224 | tf_op jit(solution)/shard_map/ppermute | solution.py:487
  48.3 8.1 %collective-permute-start.17 = (bf16[256,256]{1,0:T(8,128)(2,1)S(1)}, bf16[256,256]{1,0:T(8,128)(2,1)S(1)}, u32[]{:S(2)}, u32[]{:S(2)}) collective-permute-start(bf16[256,256]{1,0:T(8,128)(2,1)S(1)} %encoder_grad.9.refs_3_), channel_id=1, source_target_pairs={{0,2},{1,3},{2,0},{3,1},{4,6},{5,7},{6,4},{7,5},{8,10},{9,11},{10,... | collective-permute-start | bytes 393224 | tf_op jit(solution)/shard_map/ppermute | solution.py:485
  57.2 7.3 %collective-permute-start.21 = (bf16[1024,256]{1,0:T(8,128)(2,1)S(1)}, bf16[1024,256]{1,0:T(8,128)(2,1)S(1)}, u32[]{:S(2)}, u32[]{:S(2)}) collective-permute-start(bf16[1024,256]{1,0:T(8,128)(2,1)S(1)} %get-tuple-element.78.refs_5_.refs_3_.refs_1_), channel_id=1, source_target_pairs={{0,1},{1,0},{2,3},{3,2},{4,5},{5,4},{6,7},{7,6},{8,9},{9,8},{10,11... | collective-permute-start | bytes 1572872 | tf_op jit(solution)/shard_map/ppermute | solution.py:482
  57.2 14.8 %collective-permute-start.22 = (bf16[1024,256]{1,0:T(8,128)(2,1)S(1)}, bf16[1024,256]{1,0:T(8,128)(2,1)S(1)}, u32[]{:S(2)}, u32[]{:S(2)}) collective-permute-start(bf16[1024,256]{1,0:T(8,128)(2,1)S(1)} %get-tuple-element.78.refs_5_.refs_3_.refs_1_), channel_id=1, source_target_pairs={{2,0},{3,1},{0,2},{1,3},{6,4},{7,5},{4,6},{5,7},{10,8},{11,9},{8,1... | collective-permute-start | bytes 1572872 | tf_op jit(solution)/shard_map/ppermute | solution.py:483
  61.0 21.9 %collective-permute-start.20 = (bf16[1024,256]{1,0:T(8,128)(2,1)S(1)}, bf16[1024,256]{1,0:T(8,128)(2,1)S(1)}, u32[]{:S(2)}, u32[]{:S(2)}) collective-permute-start(bf16[1024,256]{1,0:T(8,128)(2,1)S(1)} %mix_rows.1.refs_8_.refs_1_.refs_5_), channel_id=1, source_target_pairs={{2,0},{3,1},{0,2},{1,3},{6,4},{7,5},{4,6},{5,7},{10,8},{11,9},{8,1... | collective-permute-start | bytes 1572872 | tf_op jit(solution)/shard_map/ppermute | solution.py:483
  72.7 13.5 %collective-permute-start.19 = (bf16[1024,256]{1,0:T(8,128)(2,1)S(1)}, bf16[1024,256]{1,0:T(8,128)(2,1)S(1)}, u32[]{:S(2)}, u32[]{:S(2)}) collective-permute-start(bf16[1024,256]{1,0:T(8,128)(2,1)S(1)} %mix_rows.1.refs_8_.refs_1_.refs_5_), channel_id=1, source_target_pairs={{0,1},{1,0},{2,3},{3,2},{4,5},{5,4},{6,7},{7,6},{8,9},{9,8},{10,11... | collective-permute-start | bytes 1572872 | tf_op jit(solution)/shard_map/ppermute | solution.py:482
  82.9 6.1 %collective-permute-start.25 = (bf16[512,256]{1,0:T(8,128)(2,1)S(1)}, bf16[512,256]{1,0:T(8,128)(2,1)S(1)}, u32[]{:S(2)}, u32[]{:S(2)}) collective-permute-start(bf16[512,256]{1,0:T(8,128)(2,1)S(1)} %get-tuple-element.84.refs_5_.refs_3_), channel_id=1, source_target_pairs={{0,1},{1,0},{2,3},{3,2},{4,5},{5,4},{6,7},{7,6},{8,9},{9,8},{10,11... | collective-permute-start | bytes 786440 | tf_op jit(solution)/shard_map/ppermute | solution.py:482
  82.9 6.0 %collective-permute-start.26 = (bf16[512,256]{1,0:T(8,128)(2,1)S(1)}, bf16[512,256]{1,0:T(8,128)(2,1)S(1)}, u32[]{:S(2)}, u32[]{:S(2)}) collective-permute-start(bf16[512,256]{1,0:T(8,128)(2,1)S(1)} %get-tuple-element.85.refs_6_.refs_4_), channel_id=1, source_target_pairs={{0,1},{1,0},{2,3},{3,2},{4,5},{5,4},{6,7},{7,6},{8,9},{9,8},{10,11... | collective-permute-start | bytes 786440 | tf_op jit(solution)/shard_map/ppermute | solution.py:482
  84.4 14.8 %collective-permute-start.27 = (bf16[1024,256]{1,0:T(8,128)(2,1)S(1)}, bf16[1024,256]{1,0:T(8,128)(2,1)S(1)}, u32[]{:S(2)}, u32[]{:S(2)}) collective-permute-start(bf16[1024,256]{1,0:T(8,128)(2,1)S(1)} %decoder_grad.6.refs_7_.refs_3_), channel_id=1, source_target_pairs={{0,2},{1,3},{2,0},{3,1},{4,6},{5,7},{6,4},{7,5},{8,10},{9,11},{10,... | collective-permute-start | bytes 1572872 | tf_op jit(solution)/shard_map/ppermute | solution.py:485
  91.4 16.3 %collective-permute-start.29 = (bf16[768,256]{1,0:T(8,128)(2,1)S(1)}, bf16[768,256]{1,0:T(8,128)(2,1)S(1)}, u32[]{:S(2)}, u32[]{:S(2)}) collective-permute-start(bf16[768,256]{1,0:T(8,128)(2,1)S(1)} %encoder_grad.12.refs_7_), channel_id=1, source_target_pairs={{0,2},{1,3},{2,0},{3,1},{4,6},{5,7},{6,4},{7,5},{8,10},{9,11},{10,... | collective-permute-start | bytes 1179656 | tf_op jit(solution)/shard_map/ppermute | solution.py:485
  100.6 9.6 %collective-permute-start.28 = (bf16[256,256]{1,0:T(8,128)(2,1)S(1)}, bf16[256,256]{1,0:T(8,128)(2,1)S(1)}, u32[]{:S(2)}, u32[]{:S(2)}) collective-permute-start(bf16[256,256]{1,0:T(8,128)(2,1)S(1)} %encoder_grad.13.refs_3_), channel_id=1, source_target_pairs={{0,2},{1,3},{2,0},{3,1},{4,6},{5,7},{6,4},{7,5},{8,10},{9,11},{10,... | collective-permute-start | bytes 393224 | tf_op jit(solution)/shard_map/ppermute | solution.py:485
  (15 other events, 52.0 us)

commit v11 on v10

--- a/solution.py
+++ b/solution.py
@@ -88,16 +88,26 @@
 EXTRA = 16
 
 
-def cast_body(theta, *lows):
-    for k, low in enumerate(lows):
-        low[...] = theta[0, k].astype(bf16)
-
-
-def cast_rows(weights, pos):
+def cast_body(sizes, theta, enc, dec, *parts):
+    enc[...] = theta[0, 0].astype(bf16)
+    value = theta[0, 1].astype(bf16)
+    dec[...] = value
+    put_parts(value, sizes, parts)
+
+
+def put_parts(value, sizes, parts):
+    off = 0
+    for size, part in zip(sizes, parts):
+        part[...] = value[off:off + size, :]
+        off += size
+
+
+def cast_rows(weights, sizes, pos):
     _, _, rows, width = weights.shape
-    return call(
-        cast_body, "cast_rows", (), [(weights, whole(weights.shape))],
-        [(sds((rows, width), bf16), whole((rows, width)))] * 2, after=[pos],
+    shapes = [(rows, width)] * 2 + [(size, width) for size in sizes]
+    return call(
+        functools.partial(cast_body, sizes), "cast_rows", (), [(weights, whole(weights.shape))],
+        [(sds(shape, bf16), whole(shape)) for shape in shapes], after=[pos],
     )
 
 
@@ -150,7 +160,7 @@
 
 
 def columns(pos, slot, off, size, rows):
-    return pl.ds(pl.multiple_of(pos[slot] * rows + off, size), size)
+    return pl.ds(pl.multiple_of(pos[slot] * rows + off, 128), size)
 
 
 def turn_body(tile, pos, x, xt):
@@ -297,9 +307,14 @@
     out[...] = token_sum(start, out.shape[0], (xt_own, xt_par), slopes).astype(out.dtype)
 
 
-def decoder_body(scale, start, pieces, xt_own, xt_par, counted, w_hi, w_lo, *refs):
-    lows, got, out = refs[:pieces], refs[pieces:-1], refs[-1]
+def decoder_body(scale, start, pieces, front, xt_own, xt_par, counted, w_hi, w_lo, *refs):
+    lows, more, out = refs[:pieces], refs[pieces:-1], refs[-1]
     off = 0
+    got = more
+    if front:
+        off = more[0].shape[0]
+        out[:off, :] = more[0][...]
+        got = ()
     for low in lows:
         size = low.shape[0]
         both = token_sum(start + off, size, (xt_own, xt_par), counted)
@@ -330,10 +345,12 @@
         old = mixed(plan, k, old, refs[0][...])
     new = old - inner_rate * (one / (jnp.sqrt(two) + adam_eps) + decay_rate * old)
     if n_low is not None:
-        anchor, before, low = refs[0], refs[1:1 + n_low], refs[1 + n_low]
-        for b in before:
-            low[:off, :] = b[...]
-        low[off:, :] = mixed(plan, k, new, anchor[off:off + own.shape[0], :]).astype(bf16)
+        anchor, before, lows = refs[0], refs[1:1 + n_low], refs[1 + n_low:-3]
+        value = mixed(plan, k, new, anchor[off:off + own.shape[0], :]).astype(bf16)
+        lows[0][...] = value
+        if before:
+            lows[1][:off, :] = before[0][...]
+            lows[1][off:, :] = value
     theta_out, first_out, second_out = refs[-3:]
     theta_out[0, 0] = new
     first_out[0, 0] = one
@@ -363,8 +380,8 @@
     else:
         if lows is not None:
             ins += [(a, whole(a.shape)) for a in [new_anc] + lows]
-            shape = (off + cr, width)
-            outs = [(sds(shape, bf16), whole(shape))]
+            shapes = [(cr, width)] + [(off + cr, width)] * len(lows)
+            outs = [(sds(shape, bf16), whole(shape)) for shape in shapes]
         outs += [(sds(block, f32), whole(block))] * 3
     return call(
         functools.partial(adam_body, last, len(got), k, off, None if lows is None else len(lows)), "adam_rows",
@@ -435,16 +452,19 @@
     )[0]
 
 
-def mix_body(k, plan, new_anc, theta, low):
-    low[...] = mixed(plan, k, theta[0, 0], new_anc[...]).astype(bf16)
-
-
-def mix_rows(plan, new_anc, k, theta, after):
-    shape = new_anc.shape
-    return call(
-        functools.partial(mix_body, k), "mix_rows", (plan,), [(a, whole(a.shape)) for a in (new_anc, theta)],
-        [(sds(shape, bf16), whole(shape))], after=after,
-    )[0]
+def mix_body(k, sizes, plan, new_anc, theta, low, *parts):
+    value = mixed(plan, k, theta[0, 0], new_anc[...]).astype(bf16)
+    low[...] = value
+    put_parts(value, sizes, parts)
+
+
+def mix_rows(plan, new_anc, k, theta, sizes, after):
+    rows, width = new_anc.shape
+    shapes = [(rows, width)] + [(size, width) for size in sizes]
+    return call(
+        functools.partial(mix_body, k, sizes), "mix_rows", (plan,), [(a, whole(a.shape)) for a in (new_anc, theta)],
+        [(sds(shape, bf16), whole(shape)) for shape in shapes], after=after,
+    )
 
 
 def outer_body(pos, plan, anchor, momentum, *refs):
@@ -474,8 +494,9 @@
     rows, width = weights.shape[2:]
     chips = n_fsdp // 2
     scale = 1.0 / math.sqrt(tokens * n_fsdp)
-    cuts = max(1, rows // 512)
-    cut = rows // cuts
+    most = rows - rows // 4 if rows >= 1024 else rows
+    sizes = [most] + [rows - most] * (most < rows)
+    starts = [sum(sizes[:n]) for n in range(len(sizes))]
     others = range(1, chips)
 
     partner = [(f, f ^ 1) for f in range(n_fsdp)]
@@ -491,47 +512,64 @@
     at = [((chip + s) % chips) * 2 for s in range(chips)]
     pos = jnp.stack([lax.axis_index("replica")] + [a + core for a in at] + [a + 1 - core for a in at]).astype(jnp.int32)
 
-    enc, dec = cast_rows(weights, pos)
+    enc, dec, *dec_parts = cast_rows(weights, sizes, pos)
+    enc_parts = [enc]
     x_par = to_partner(inputs)
     quarters = outer_start(pos, plan, anchor, weights, [enc])
     xs, xt = zip(*[turn(pos, x, chips, stage) for x, stage in ((inputs, False), (x_par, True))])
     own = outer_add(plan, [quarters[0]] + [across(quarters[m], m) for m in range(1, 4)], n_rep == 4, xt)
 
-    most = rows - rows // 4 if rows >= 1024 else rows
-    blocks = [(1, 0, rows), (0, 0, most)] + [(0, off, rows - most) for off in range(most, rows, max(1, rows - most))]
+    blocks = [(1, 0, rows)] + [(0, off, size) for off, size in zip(starts, sizes)]
     state = {key: (weights, first_moment, second_moment) for key in blocks}
     state_at = {(k, off, size): (k, off // size) for k, off, size in blocks}
     new_anc = None
     for step in range(INNER):
         last = step == INNER - 1
-        enc_far = {s: fetch(enc, s) for s in others}
-        dec_far = {s: fetch(dec, s) for s in others}
+        enc_far = [{s: fetch(part, s) for s in others} for part in enc_parts]
+        dec_far = [{s: fetch(part, s) for s in others} for part in dec_parts]
         enc_near, dec_near = to_partner(enc), to_partner(dec)
+
+        def take(far, off, after, *riders):
+            pieces = []
+            for s in others:
+                cuts = max(1, far[s].shape[0] // 384)
+                cut = far[s].shape[0] // cuts
+                got = relay(far[s], cuts, after, *riders)
+                pieces += [(p, 1 + s, off + n * cut, cut) for n, p in enumerate(got)]
+            return pieces, [(to_partner(p), slot + chips, o, size) for p, slot, o, size in pieces]
 
         carry = forward(pos, [], [(enc, 1, 0, rows), (enc_near, 1 + chips, 0, rows)], xs, rows, False)
         ready = [own, *xt] if step == 0 else [token]
-        riders = [kinds] if step == 0 else []
-        part = [(p, 1 + s, n * cut, cut) for s in others for n, p in enumerate(
-            relay(enc_far[s], cuts, [*carry, *ready], *riders))]
-        pending = [(to_partner(p), slot + chips, off, size) for p, slot, off, size in part]
-        carry = forward(pos, carry, part, xs, rows, False)
+        pending = []
+        off = 0
+        for part in enc_far:
+            pieces, handed = take(part, off, [*carry, *ready], *([kinds] if step == 0 else []))
+            carry = forward(pos, carry, pending + pieces, xs, rows, False)
+            pending = handed
+            off += part[1].shape[0]
         if step == 0:
             cw = weigh(kinds, pending[-1][0], tokens)
         hidden, slope, counted, w_hi, w_lo = hidden_rows(pos, carry[0], cw, pending, xs, rows, scale)
-        dec_grad = lambda s, lows, more, dtype, after: grad_rows(
-            functools.partial(decoder_body, scale, s * rows, len(lows)), "decoder_grad", rows, xt,
+        dec_grad = lambda s, size, lows, more, front, dtype, after: grad_rows(
+            functools.partial(decoder_body, scale, s * rows, len(lows), front), "decoder_grad", size, xt,
             [counted, w_hi, w_lo, *lows, *more], dtype, after)
         enc_grad = lambda s, off, size, dtype, after: grad_rows(
             functools.partial(encoder_body, s * rows + off), "encoder_grad", size, xt, [slopes], dtype, after)
         sent = []
         got = {key: [] for key in blocks}
-        far = {s: relay(dec_far[s], cuts, [counted]) for s in others}
-        for s in others:
-            sent.append(dec_grad(s, far[s], [], bf16, sent[-1:]))
-            got[blocks[0]].append(give(sent[-1], s))
-
-        part = [(p, 1 + s, n * cut, cut) for s in others for n, p in enumerate(far[s])]
-        pending = [(to_partner(p), slot + chips, off, size) for p, slot, off, size in part]
+        part, pending = [], []
+        whole_grad = {s: [] for s in others}
+        for n, far in enumerate(dec_far):
+            pieces, handed = take(far, starts[n], [counted] + sent[-1:])
+            part += pieces
+            pending += handed
+            for s in others:
+                rows_in = [p[0] for p in pieces if p[1] == 1 + s]
+                whole_grad[s] = [dec_grad(
+                    s, starts[n] + sizes[n], rows_in, whole_grad[s], n > 0, bf16, sent[-1:])]
+                sent.append(whole_grad[s][0])
+        back = [give(whole_grad[s][0], s) for s in others]
+
         carry = forward(
             pos, [], [(dec, 1, 0, rows), (dec_near, 1 + chips, 0, rows)] + part, xs, rows, True, sent[-1:])
         slopes = slope_rows(pos, *carry, hidden, slope, pending, xs, rows)
@@ -546,8 +584,7 @@
                 sent.append(enc_grad(s, *key[1:], bf16, sent[-1:]))
                 got[key].append(give(sent[-1], s))
             if n == 0:
-                mine = {blocks[0]: dec_grad(0, [dec], got[blocks[0]], f32, sent[-1:])}
-                got[blocks[0]] = []
+                mine = {blocks[0]: dec_grad(0, rows, dec_parts, back, False, f32, sent[-1:])}
                 sent.append(mine[blocks[0]])
         for key in blocks[1:]:
             mine[key] = enc_grad(0, *key[1:], f32, sent[-1:])
@@ -564,10 +601,13 @@
                 prev = adam(key, prev)
         else:
             for key in blocks[1:]:
-                enc, *new_state[key] = adam(key, None, lows)
-                lows = [enc]
+                *new, a, b, c = adam(key, None, lows)
+                lows.append(new[0])
+                new_state[key] = (a, b, c)
+            enc = new[-1]
+            enc_parts = [enc]
             new_state[blocks[0]] = adam(blocks[0], None, after=[enc])
-            dec = mix_rows(plan, new_anc, 1, new_state[blocks[0]][0], [enc])
+            dec, *dec_parts = mix_rows(plan, new_anc, 1, new_state[blocks[0]][0], sizes, [enc])
             anchor_out, momentum_out, token = outer_end(pos, plan, anchor, momentum, quarters, [dec])
             state, state_at = new_state, {key: (0, 0) for key in blocks}
     return (*prev, anchor_out, momentum_out)

time: 112 us -> 112 us (level)
  waiting for transfers between devices: 31.5 us -> 28.9 us
  Pallas kernels: 48.9 us -> 50.6 us
    ppermute x4 -> x6, waiting for transfers between devices: 17 us -> 11.9 us  [local(): lax.ppermute(a, 'fsdp', [((f // 2 + s) % chips * 2 + f % 2, f) for f in r...]
    ppermute x4 -> x6, starting transfers between devices: 5.14 us -> 7.61 us  [local(): lax.ppermute(a, 'fsdp', [((f // 2 + s) % chips * 2 + f % 2, f) for f in r...]
    ppermute x7, waiting for transfers between devices: 3.75 us -> 5.93 us  [local(): lax.ppermute(a, 'replica', [(r, r ^ bit) for r in range(n_rep)])]
    pallas_call x42 -> x46, Pallas kernels: 48.9 us -> 50.6 us  [call(): pl.pallas_call(run, name=name, out_shape=[o for o, _ in outs], grid_spec=...]
    ppermute x6, starting transfers between devices: 7.86 us -> 6.72 us  [local(): lax.ppermute(a, 'fsdp', [(f, (f // 2 + s) % chips * 2 + f % 2) for f in r...]
    ppermute x13 -> x15, starting transfers between devices: 3.15 us -> 2.91 us  [local(): to_partner = lambda a: lax.ppermute(a, 'fsdp', partner)]
  transfers between devices with their start and end apart: 30 -> 34, of which waited for: 10 -> 12; matrix products, arithmetic and copies ran while one was open for 0% -> 0% of each run, Pallas kernels for 42% -> 43%
where the time goes in v11:
time: 112 us; the launch traced here: 111 us
  Pallas kernels  50.6 us (45%)
  starting transfers between devices  29 us (26%)
  waiting for transfers between devices  28.9 us (26%)
  local copies, waits for them, and re-layouts  1.76 us (2%)
    pallas_call x46, Pallas kernels, call(): pl.pallas_call(run, name=name, out_shape=[o for o, _ in outs], grid_spec=...  50.6 us
    ppermute x6, waiting for transfers between devices, local(): lax.ppermute(a, 'fsdp', [((f // 2 + s) % chips * 2 + f % 2, f) for f in r...  11.9 us
    ppermute x7, starting transfers between devices, local(): lax.ppermute(a, 'replica', [(r, r ^ bit) for r in range(n_rep)])  11.8 us
    ppermute x6, waiting for transfers between devices, local(): lax.ppermute(a, 'fsdp', [(f, (f // 2 + s) % chips * 2 + f % 2) for f in r...  11.1 us
    ppermute x6, starting transfers between devices, local(): lax.ppermute(a, 'fsdp', [((f // 2 + s) % chips * 2 + f % 2, f) for f in r...  7.61 us
    ppermute x6, starting transfers between devices, local(): lax.ppermute(a, 'fsdp', [(f, (f // 2 + s) % chips * 2 + f % 2) for f in r...  6.72 us
    ppermute x7, waiting for transfers between devices, local(): lax.ppermute(a, 'replica', [(r, r ^ bit) for r in range(n_rep)])  5.93 us
    ppermute x15, starting transfers between devices, local(): to_partner = lambda a: lax.ppermute(a, 'fsdp', partner)  2.91 us
  transfers between devices with their start and end apart: 34, of which 12 were waited for; matrix products, arithmetic and copies ran while one was open for 0% of the time, Pallas kernels for 43%

profile of v11, /device:TPU:0, one launch (start us, length us, event | category | flops | bytes accessed | tf_op | source)
XLA Modules:
  0.0 111.4 jit_solution(12898988160965862416)
XLA Ops:
  3.1 3.0 %collective-permute-start.8 = (bf16[1024,256]{1,0:T(8,128)(2,1)S(1)}, bf16[1024,256]{1,0:T(8,128)(2,1)S(1)}, u32[]{:S(2)}, u32[]{:S(2)}) collective-permute-start(bf16[1024,256]{1,0:T(8,128)(2,1)S(1)} %get-tuple-element.64.refs_4_.refs_1_), channel_id=1, source_target_pairs={{2,0},{3,1},{0,2},{1,3},{6,4},{7,5},{4,6},{5,7},{10,8},{11,9},{8,1... | collective-permute-start | bytes 1572872 | tf_op jit(solution)/shard_map/ppermute | solution.py:504
  9.9 2.1 %collective-permute-done.1.refs_2_ = bf16[256,256]{1,0:T(8,128)(2,1)S(1)} collective-permute-done((bf16[256,256]{1,0:T(8,128)(2,1)S(1)}, bf16[256,256]{1,0:T(8,128)(2,1)S(1)}, u32[]{:S(2)}, u32[]{:S(2)}) %collective-permute-start.1) | collective-permute-done | bytes 131104 | tf_op jit(solution)/shard_map/ppermute | solution.py:508
  12.1 2.6 %collective-permute-start.3 = (bf16[256,256]{1,0:T(8,128)(2,1)S(1)}, bf16[256,256]{1,0:T(8,128)(2,1)S(1)}, u32[]{:S(2)}, u32[]{:S(2)}) collective-permute-start(bf16[256,256]{1,0:T(8,128)(2,1)S(1)} %get-tuple-element.68), channel_id=1, source_target_pairs={{0,12},{4,8},{8,4},{12,0},{16,28},{20,24},{24,20},{28,16},{1,13},{... | collective-permute-start | bytes 393224 | tf_op jit(solution)/shard_map/ppermute | solution.py:508
  17.3 2.9 %stage_tokens.1 = (bf16[512,4096]{1,0:T(8,128)(2,1)S(1)}, bf16[2048,512]{1,0:T(8,128)(2,1)S(1)}) custom-call(s32[5]{0:T(128)S(1)} %stack.23.refs_0_.refs_1_, bf16[512,4096]{1,0:T(8,128)(2,1)} %collective-permute-done.refs_1_), custom_call_target="tpu_custom_call" | custom-call | bytes 10485760 | tf_op jit(solution)/shard_map/stage_tokens/pallas_call | solution.py:60
  20.3 1.8 %forward_encoder.4.refs_2_.refs_1_ = f32[2,512,256]{2,1,0:T(8,128)S(1)} custom-call(s32[5]{0:T(128)S(1)} %stack.23.refs_0_.refs_1_, bf16[1024,256]{1,0:T(8,128)(2,1)S(1)} %get-tuple-element.64.refs_4_.refs_1_, bf16[1024,256]{1,0:T(8,128)(2,1)S(1)} %collective-permute-done.7.refs_2_, bf16[512,4096]{1,0:T(8,128)(2,1)S(1)} %copy-done, ...), custom_call_target="tpu_custom_call" | custom-call | bytes 10485760 | tf_op jit(solution)/shard_map/forward_encoder/pallas_call | solution.py:60
  25.4 2.3 %hidden_units.2 = (bf16[2,512,256]{2,1,0:T(8,128)(2,1)S(1)}, f32[2,512,256]{2,1,0:T(8,128)S(1)}, bf16[2,512,256]{2,1,0:T(8,128)(2,1)S(1)}, bf16[256,256]{1,0:T(8,128)(2,1)S(1)}, bf16[256,256]{1,0:T(8,128)(2,1)S(1)}) custom-call(s32[5]{0:T(128)S(1)} %stack.23.refs_0_.refs_1_, f32[2,512,256]{2,1,0:T(8,128)S(1)} %forward_encoder.5.refs_1_, ...), custom_call_target="tpu_custom_call" | custom-call | bytes 12333056 | tf_op jit(solution)/shard_map/hidden_units/pallas_call | solution.py:60
  29.9 1.8 %collective-permute-start.18 = (bf16[1024,256]{1,0:T(8,128)(2,1)S(1)}, bf16[1024,256]{1,0:T(8,128)(2,1)S(1)}, u32[]{:S(2)}, u32[]{:S(2)}) collective-permute-start(bf16[1024,256]{1,0:T(8,128)(2,1)S(1)} %decoder_grad.7.refs_8_), channel_id=1, source_target_pairs={{0,2},{1,3},{2,0},{3,1},{4,6},{5,7},{6,4},{7,5},{8,10},{9,11},{10,... | collective-permute-start | bytes 1572872 | tf_op jit(solution)/shard_map/ppermute | solution.py:506
  32.2 2.6 %collective-permute-start.4 = (bf16[256,256]{1,0:T(8,128)(2,1)S(1)}, bf16[256,256]{1,0:T(8,128)(2,1)S(1)}, u32[]{:S(2)}, u32[]{:S(2)}) collective-permute-start(bf16[256,256]{1,0:T(8,128)(2,1)S(1)} %add_quarters.2.refs_3_.refs_1_), channel_id=1, source_target_pairs={{0,16},{4,20},{8,24},{12,28},{16,0},{20,4},{24,8},{28,12},{1,17},{... | collective-permute-start | bytes 393224 | tf_op jit(solution)/shard_map/ppermute | solution.py:508
  34.8 3.0 %forward_decoder.2 = (f32[2,512,256]{2,1,0:T(8,128)S(1)}, f32[256,256]{1,0:T(8,128)S(1)}) custom-call(s32[5]{0:T(128)S(1)} %stack.23.refs_0_.refs_1_, bf16[1024,256]{1,0:T(8,128)(2,1)S(1)} %get-tuple-element.69.refs_1_, bf16[1024,256]{1,0:T(8,128)(2,1)S(1)} %collective-permute-done.5.refs_2_, bf16[384,256]{1,0:T(8,128)(2,1)S(1)} %get-tuple-element.75.refs_5_.refs_3_, ...), custom_call_target="tpu_custom_call" | custom-call | bytes 11272192 | tf_op jit(solution)/shard_map/forward_decoder/pallas_call | solution.py:60
  37.8 2.0 %slope_pre.2.refs_3_.refs_2_ = bf16[2,512,256]{2,1,0:T(8,128)(2,1)S(1)} custom-call(s32[5]{0:T(128)S(1)} %stack.23.refs_0_.refs_1_, f32[2,512,256]{2,1,0:T(8,128)S(1)} %get-tuple-element.80.refs_1_, f32[256,256]{1,0:T(8,128)S(1)} %get-tuple-element.81.refs_2_, bf16[2,512,256]{2,1,0:T(8,128)(2,1)S(1)} %get-tuple-element.82.refs_3_, ...), custom_call_target="tpu_custom_call" | custom-call | bytes 12320768 | tf_op jit(solution)/shard_map/slope_pre/pallas_call | solution.py:60
  39.8 2.0 %collective-permute-done.4.refs_2_ = bf16[256,256]{1,0:T(8,128)(2,1)S(1)} collective-permute-done((bf16[256,256]{1,0:T(8,128)(2,1)S(1)}, bf16[256,256]{1,0:T(8,128)(2,1)S(1)}, u32[]{:S(2)}, u32[]{:S(2)}) %collective-permute-start.4) | collective-permute-done | bytes 131104 | tf_op jit(solution)/shard_map/ppermute | solution.py:508
  48.3 1.6 %collective-permute-start.19 = (bf16[256,256]{1,0:T(8,128)(2,1)S(1)}, bf16[256,256]{1,0:T(8,128)(2,1)S(1)}, u32[]{:S(2)}, u32[]{:S(2)}) collective-permute-start(bf16[256,256]{1,0:T(8,128)(2,1)S(1)} %encoder_grad.9.refs_3_), channel_id=1, source_target_pairs={{0,2},{1,3},{2,0},{3,1},{4,6},{5,7},{6,4},{7,5},{8,10},{9,11},{10,... | collective-permute-start | bytes 393224 | tf_op jit(solution)/shard_map/ppermute | solution.py:506
  51.0 1.6 %collective-permute-done.17.refs_7_ = bf16[256,256]{1,0:T(8,128)(2,1)S(1)} collective-permute-done((bf16[256,256]{1,0:T(8,128)(2,1)S(1)}, bf16[256,256]{1,0:T(8,128)(2,1)S(1)}, u32[]{:S(2)}, u32[]{:S(2)}) %collective-permute-start.17) | collective-permute-done | bytes 131104 | tf_op jit(solution)/shard_map/ppermute | solution.py:508
  62.1 3.1 %outer_step.1 = (f32[2,1024,256]{2,1,0:T(8,128)}, f32[2,1024,256]{2,1,0:T(8,128)}, f32[8,128]{1,0:T(8,128)S(1)}) custom-call(s32[5]{0:T(128)S(1)} %stack.23.refs_0_.refs_1_, s32[8]{0:T(128)S(1)} %copy-done.7, f32[2,1024,256]{2,1,0:T(8,128)S(1)} %copy-done.3, f32[2,1024,256]{2,1,0:T(8,128)S(1)} %copy-done.6, ...), custom_call_target="tpu_custom_call" | custom-call | bytes 8916992 | tf_op jit(solution)/shard_map/outer_step/pallas_call | solution.py:60
  65.2 1.8 %forward_encoder.6.refs_1_ = f32[2,512,256]{2,1,0:T(8,128)S(1)} custom-call(s32[5]{0:T(128)S(1)} %stack.23.refs_0_.refs_1_, bf16[1024,256]{1,0:T(8,128)(2,1)S(1)} %get-tuple-element.85.refs_5_.refs_3_.refs_1_, bf16[1024,256]{1,0:T(8,128)(2,1)S(1)} %collective-permute-done.23.refs_2_, bf16[512,4096]{1,0:T(8,128)(2,1)S(1)} %copy-done, ...), custom_call_target="tpu_custom_call" | custom-call | bytes 10485760 | tf_op jit(solution)/shard_map/forward_encoder/pallas_call | solution.py:60
  67.0 5.8 %collective-permute-done.24.refs_0_ = bf16[1024,256]{1,0:T(8,128)(2,1)S(1)} collective-permute-done((bf16[1024,256]{1,0:T(8,128)(2,1)S(1)}, bf16[1024,256]{1,0:T(8,128)(2,1)S(1)}, u32[]{:S(2)}, u32[]{:S(2)}) %collective-permute-start.24) | collective-permute-done | bytes 524320 | tf_op jit(solution)/shard_map/ppermute | solution.py:504
  75.2 2.3 %hidden_units.3 = (bf16[2,512,256]{2,1,0:T(8,128)(2,1)S(1)}, f32[2,512,256]{2,1,0:T(8,128)S(1)}, bf16[2,512,256]{2,1,0:T(8,128)(2,1)S(1)}, bf16[256,256]{1,0:T(8,128)(2,1)S(1)}, bf16[256,256]{1,0:T(8,128)(2,1)S(1)}) custom-call(s32[5]{0:T(128)S(1)} %stack.23.refs_0_.refs_1_, f32[2,512,256]{2,1,0:T(8,128)S(1)} %forward_encoder.7.refs_1_, ...), custom_call_target="tpu_custom_call" | custom-call | bytes 12324864 | tf_op jit(solution)/shard_map/hidden_units/pallas_call | solution.py:60
  77.6 3.6 %collective-permute-done.22.refs_0_ = bf16[768,256]{1,0:T(8,128)(2,1)S(1)} collective-permute-done((bf16[768,256]{1,0:T(8,128)(2,1)S(1)}, bf16[768,256]{1,0:T(8,128)(2,1)S(1)}, u32[]{:S(2)}, u32[]{:S(2)}) %collective-permute-start.22) | collective-permute-done | bytes 393248 | tf_op jit(solution)/shard_map/ppermute | solution.py:504
  85.2 3.0 %forward_decoder.3 = (f32[2,512,256]{2,1,0:T(8,128)S(1)}, f32[256,256]{1,0:T(8,128)S(1)}) custom-call(s32[5]{0:T(128)S(1)} %stack.23.refs_0_.refs_1_, bf16[1024,256]{1,0:T(8,128)(2,1)S(1)} %get-tuple-element.87.refs_8_.refs_1_, bf16[1024,256]{1,0:T(8,128)(2,1)S(1)} %collective-permute-done.21.refs_2_, ...), custom_call_target="tpu_custom_call" | custom-call | bytes 11272192 | tf_op jit(solution)/shard_map/forward_decoder/pallas_call | solution.py:60
  88.2 2.1 %slope_pre.3.refs_2_ = bf16[2,512,256]{2,1,0:T(8,128)(2,1)S(1)} custom-call(s32[5]{0:T(128)S(1)} %stack.23.refs_0_.refs_1_, f32[2,512,256]{2,1,0:T(8,128)S(1)} %get-tuple-element.98.refs_1_, f32[256,256]{1,0:T(8,128)S(1)} %get-tuple-element.99.refs_2_, bf16[2,512,256]{2,1,0:T(8,128)(2,1)S(1)} %get-tuple-element.100.refs_3_, ...), custom_call_target="tpu_custom_call" | custom-call | bytes 12320768 | tf_op jit(solution)/shard_map/slope_pre/pallas_call | solution.py:60
  92.4 6.6 %collective-permute-done.31.refs_7_ = bf16[1024,256]{1,0:T(8,128)(2,1)S(1)} collective-permute-done((bf16[1024,256]{1,0:T(8,128)(2,1)S(1)}, bf16[1024,256]{1,0:T(8,128)(2,1)S(1)}, u32[]{:S(2)}, u32[]{:S(2)}) %collective-permute-start.31) | collective-permute-done | bytes 524320 | tf_op jit(solution)/shard_map/ppermute | solution.py:506
  101.7 2.8 %adam_rows.9 = (f32[1,2,1024,256]{3,2,1,0:T(8,128)}, f32[1,2,1024,256]{3,2,1,0:T(8,128)}, f32[1,2,1024,256]{3,2,1,0:T(8,128)}) custom-call(s32[8]{0:T(128)S(1)} %copy-done.7, f32[1024,256]{1,0:T(8,128)S(1)} %decoder_grad.11.refs_3_.refs_1_, f32[1,1,1024,256]{3,2,1,0:T(8,128)S(1)} %get-tuple-element.86.refs_2_, ...), custom_call_target="tpu_custom_call" | custom-call | bytes 11534336 | tf_op jit(solution)/shard_map/adam_rows/pallas_call | solution.py:60
  104.5 2.8 %collective-permute-done.33.refs_2_ = bf16[768,256]{1,0:T(8,128)(2,1)S(1)} collective-permute-done((bf16[768,256]{1,0:T(8,128)(2,1)S(1)}, bf16[768,256]{1,0:T(8,128)(2,1)S(1)}, u32[]{:S(2)}, u32[]{:S(2)}) %collective-permute-start.33) | collective-permute-done | bytes 393248 | tf_op jit(solution)/shard_map/ppermute | solution.py:506
  107.3 2.4 %adam_rows.10 = (f32[1,2,1024,256]{3,2,1,0:T(8,128)}, f32[1,2,1024,256]{3,2,1,0:T(8,128)}, f32[1,2,1024,256]{3,2,1,0:T(8,128)}) custom-call(s32[8]{0:T(128)S(1)} %copy-done.7, f32[768,256]{1,0:T(8,128)S(1)} %encoder_grad.15.refs_1_, bf16[768,256]{1,0:T(8,128)(2,1)S(1)} %collective-permute-done.33.refs_2_, ...), custom_call_target="tpu_custom_call", output_to_operand_aliasing={{0}: (7, {}), {1}: (8, {}), {2}: (9, {})} | custom-call | bytes 16908288 | tf_op jit(solution)/shard_map/adam_rows/pallas_call | solution.py:60
  (109 shorter events, 44.6 us)
Async XLA Ops:
  0.6 15.5 %collective-permute-start = (bf16[512,4096]{1,0:T(8,128)(2,1)}, bf16[512,4096]{1,0:T(8,128)(2,1)}, u32[]{:S(2)}, u32[]{:S(2)}) collective-permute-start(bf16[512,4096]{1,0:T(8,128)(2,1)} %refs_8_.3), channel_id=1, source_target_pairs={{0,1},{1,0},{2,3},{3,2},{4,5},{5,4},{6,7},{7,6},{8,9},{9,8},{10,11... | collective-permute-start | bytes 12582920 | tf_op jit(solution)/shard_map/ppermute | solution.py:503
  3.0 11.7 %collective-permute-start.7 = (bf16[1024,256]{1,0:T(8,128)(2,1)S(1)}, bf16[1024,256]{1,0:T(8,128)(2,1)S(1)}, u32[]{:S(2)}, u32[]{:S(2)}) collective-permute-start(bf16[1024,256]{1,0:T(8,128)(2,1)S(1)} %get-tuple-element.64.refs_4_.refs_1_), channel_id=1, source_target_pairs={{0,1},{1,0},{2,3},{3,2},{4,5},{5,4},{6,7},{7,6},{8,9},{9,8},{10,11... | collective-permute-start | bytes 1572872 | tf_op jit(solution)/shard_map/ppermute | solution.py:503
  3.1 19.6 %collective-permute-start.8 = (bf16[1024,256]{1,0:T(8,128)(2,1)S(1)}, bf16[1024,256]{1,0:T(8,128)(2,1)S(1)}, u32[]{:S(2)}, u32[]{:S(2)}) collective-permute-start(bf16[1024,256]{1,0:T(8,128)(2,1)S(1)} %get-tuple-element.64.refs_4_.refs_1_), channel_id=1, source_target_pairs={{2,0},{3,1},{0,2},{1,3},{6,4},{7,5},{4,6},{5,7},{10,8},{11,9},{8,1... | collective-permute-start | bytes 1572872 | tf_op jit(solution)/shard_map/ppermute | solution.py:504
  8.4 13.7 %collective-permute-start.2 = (bf16[256,256]{1,0:T(8,128)(2,1)S(1)}, bf16[256,256]{1,0:T(8,128)(2,1)S(1)}, u32[]{:S(2)}, u32[]{:S(2)}) collective-permute-start(bf16[256,256]{1,0:T(8,128)(2,1)S(1)} %get-tuple-element.67), channel_id=1, source_target_pairs={{0,8},{4,12},{8,0},{12,4},{16,24},{20,28},{24,16},{28,20},{1,9},{5... | collective-permute-start | bytes 393224 | tf_op jit(solution)/shard_map/ppermute | solution.py:508
  12.1 10.0 %collective-permute-start.3 = (bf16[256,256]{1,0:T(8,128)(2,1)S(1)}, bf16[256,256]{1,0:T(8,128)(2,1)S(1)}, u32[]{:S(2)}, u32[]{:S(2)}) collective-permute-start(bf16[256,256]{1,0:T(8,128)(2,1)S(1)} %get-tuple-element.68), channel_id=1, source_target_pairs={{0,12},{4,8},{8,4},{12,0},{16,28},{20,24},{24,20},{28,16},{1,13},{... | collective-permute-start | bytes 393224 | tf_op jit(solution)/shard_map/ppermute | solution.py:508
  14.6 13.2 %collective-permute-start.6 = (bf16[768,256]{1,0:T(8,128)(2,1)S(1)}, bf16[768,256]{1,0:T(8,128)(2,1)S(1)}, u32[]{:S(2)}, u32[]{:S(2)}) collective-permute-start(bf16[768,256]{1,0:T(8,128)(2,1)S(1)} %get-tuple-element.70.refs_5_), channel_id=1, source_target_pairs={{2,0},{3,1},{0,2},{1,3},{6,4},{7,5},{4,6},{5,7},{10,8},{11,9},{8,1... | collective-permute-start | bytes 1179656 | tf_op jit(solution)/shard_map/ppermute | solution.py:504
  16.2 16.0 %collective-permute-start.5 = (bf16[1024,256]{1,0:T(8,128)(2,1)S(1)}, bf16[1024,256]{1,0:T(8,128)(2,1)S(1)}, u32[]{:S(2)}, u32[]{:S(2)}) collective-permute-start(bf16[1024,256]{1,0:T(8,128)(2,1)S(1)} %get-tuple-element.69.refs_1_), channel_id=1, source_target_pairs={{0,1},{1,0},{2,3},{3,2},{4,5},{5,4},{6,7},{7,6},{8,9},{9,8},{10,11... | collective-permute-start | bytes 1572872 | tf_op jit(solution)/shard_map/ppermute | solution.py:503
  23.4 6.0 %collective-permute-start.11 = (bf16[256,256]{1,0:T(8,128)(2,1)S(1)}, bf16[256,256]{1,0:T(8,128)(2,1)S(1)}, u32[]{:S(2)}, u32[]{:S(2)}) collective-permute-start(bf16[256,256]{1,0:T(8,128)(2,1)S(1)} %get-tuple-element.77.refs_6_), channel_id=1, source_target_pairs={{2,0},{3,1},{0,2},{1,3},{6,4},{7,5},{4,6},{5,7},{10,8},{11,9},{8,1... | collective-permute-start | bytes 393224 | tf_op jit(solution)/shard_map/ppermute | solution.py:504
  29.9 17.1 %collective-permute-start.18 = (bf16[1024,256]{1,0:T(8,128)(2,1)S(1)}, bf16[1024,256]{1,0:T(8,128)(2,1)S(1)}, u32[]{:S(2)}, u32[]{:S(2)}) collective-permute-start(bf16[1024,256]{1,0:T(8,128)(2,1)S(1)} %decoder_grad.7.refs_8_), channel_id=1, source_target_pairs={{0,2},{1,3},{2,0},{3,1},{4,6},{5,7},{6,4},{7,5},{8,10},{9,11},{10,... | collective-permute-start | bytes 1572872 | tf_op jit(solution)/shard_map/ppermute | solution.py:506
  31.7 6.1 %collective-permute-start.12 = (bf16[384,256]{1,0:T(8,128)(2,1)S(1)}, bf16[384,256]{1,0:T(8,128)(2,1)S(1)}, u32[]{:S(2)}, u32[]{:S(2)}) collective-permute-start(bf16[384,256]{1,0:T(8,128)(2,1)S(1)} %get-tuple-element.75.refs_5_.refs_3_), channel_id=1, source_target_pairs={{0,1},{1,0},{2,3},{3,2},{4,5},{5,4},{6,7},{7,6},{8,9},{9,8},{10,11... | collective-permute-start | bytes 589832 | tf_op jit(solution)/shard_map/ppermute | solution.py:503
  31.7 6.1 %collective-permute-start.13 = (bf16[384,256]{1,0:T(8,128)(2,1)S(1)}, bf16[384,256]{1,0:T(8,128)(2,1)S(1)}, u32[]{:S(2)}, u32[]{:S(2)}) collective-permute-start(bf16[384,256]{1,0:T(8,128)(2,1)S(1)} %get-tuple-element.76.refs_6_.refs_4_), channel_id=1, source_target_pairs={{0,1},{1,0},{2,3},{3,2},{4,5},{5,4},{6,7},{7,6},{8,9},{9,8},{10,11... | collective-permute-start | bytes 589832 | tf_op jit(solution)/shard_map/ppermute | solution.py:503
  32.2 9.6 %collective-permute-start.4 = (bf16[256,256]{1,0:T(8,128)(2,1)S(1)}, bf16[256,256]{1,0:T(8,128)(2,1)S(1)}, u32[]{:S(2)}, u32[]{:S(2)}) collective-permute-start(bf16[256,256]{1,0:T(8,128)(2,1)S(1)} %add_quarters.2.refs_3_.refs_1_), channel_id=1, source_target_pairs={{0,16},{4,20},{8,24},{12,28},{16,0},{20,4},{24,8},{28,12},{1,17},{... | collective-permute-start | bytes 393224 | tf_op jit(solution)/shard_map/ppermute | solution.py:508
  43.0 12.1 %collective-permute-start.20 = (bf16[768,256]{1,0:T(8,128)(2,1)S(1)}, bf16[768,256]{1,0:T(8,128)(2,1)S(1)}, u32[]{:S(2)}, u32[]{:S(2)}) collective-permute-start(bf16[768,256]{1,0:T(8,128)(2,1)S(1)} %encoder_grad.8.refs_8_), channel_id=1, source_target_pairs={{0,2},{1,3},{2,0},{3,1},{4,6},{5,7},{6,4},{7,5},{8,10},{9,11},{10,... | collective-permute-start | bytes 1179656 | tf_op jit(solution)/shard_map/ppermute | solution.py:506
  43.5 7.4 %collective-permute-start.15 = (bf16[256,256]{1,0:T(8,128)(2,1)S(1)}, bf16[256,256]{1,0:T(8,128)(2,1)S(1)}, u32[]{:S(2)}, u32[]{:S(2)}) collective-permute-start(bf16[256,256]{1,0:T(8,128)(2,1)S(1)} %add_quarters.3.refs_3_.refs_4_), channel_id=1, source_target_pairs={{0,4},{4,0},{8,12},{12,8},{16,20},{20,16},{24,28},{28,24},{1,5},{5... | collective-permute-start | bytes 393224 | tf_op jit(solution)/shard_map/ppermute | solution.py:508
  45.7 6.9 %collective-permute-start.17 = (bf16[256,256]{1,0:T(8,128)(2,1)S(1)}, bf16[256,256]{1,0:T(8,128)(2,1)S(1)}, u32[]{:S(2)}, u32[]{:S(2)}) collective-permute-start(bf16[256,256]{1,0:T(8,128)(2,1)S(1)} %add_quarters.3.refs_3_.refs_4_), channel_id=1, source_target_pairs={{0,12},{4,8},{8,4},{12,0},{16,28},{20,24},{24,20},{28,16},{1,13},{... | collective-permute-start | bytes 393224 | tf_op jit(solution)/shard_map/ppermute | solution.py:508
  48.3 8.3 %collective-permute-start.19 = (bf16[256,256]{1,0:T(8,128)(2,1)S(1)}, bf16[256,256]{1,0:T(8,128)(2,1)S(1)}, u32[]{:S(2)}, u32[]{:S(2)}) collective-permute-start(bf16[256,256]{1,0:T(8,128)(2,1)S(1)} %encoder_grad.9.refs_3_), channel_id=1, source_target_pairs={{0,2},{1,3},{2,0},{3,1},{4,6},{5,7},{6,4},{7,5},{8,10},{9,11},{10,... | collective-permute-start | bytes 393224 | tf_op jit(solution)/shard_map/ppermute | solution.py:506
  58.1 7.1 %collective-permute-start.23 = (bf16[1024,256]{1,0:T(8,128)(2,1)S(1)}, bf16[1024,256]{1,0:T(8,128)(2,1)S(1)}, u32[]{:S(2)}, u32[]{:S(2)}) collective-permute-start(bf16[1024,256]{1,0:T(8,128)(2,1)S(1)} %get-tuple-element.85.refs_5_.refs_3_.refs_1_), channel_id=1, source_target_pairs={{0,1},{1,0},{2,3},{3,2},{4,5},{5,4},{6,7},{7,6},{8,9},{9,8},{10,11... | collective-permute-start | bytes 1572872 | tf_op jit(solution)/shard_map/ppermute | solution.py:503
  58.1 14.7 %collective-permute-start.24 = (bf16[1024,256]{1,0:T(8,128)(2,1)S(1)}, bf16[1024,256]{1,0:T(8,128)(2,1)S(1)}, u32[]{:S(2)}, u32[]{:S(2)}) collective-permute-start(bf16[1024,256]{1,0:T(8,128)(2,1)S(1)} %get-tuple-element.85.refs_5_.refs_3_.refs_1_), channel_id=1, source_target_pairs={{2,0},{3,1},{0,2},{1,3},{6,4},{7,5},{4,6},{5,7},{10,8},{11,9},{8,1... | collective-permute-start | bytes 1572872 | tf_op jit(solution)/shard_map/ppermute | solution.py:504
  60.6 20.6 %collective-permute-start.22 = (bf16[768,256]{1,0:T(8,128)(2,1)S(1)}, bf16[768,256]{1,0:T(8,128)(2,1)S(1)}, u32[]{:S(2)}, u32[]{:S(2)}) collective-permute-start(bf16[768,256]{1,0:T(8,128)(2,1)S(1)} %get-tuple-element.88.refs_5_), channel_id=1, source_target_pairs={{2,0},{3,1},{0,2},{1,3},{6,4},{7,5},{4,6},{5,7},{10,8},{11,9},{8,1... | collective-permute-start | bytes 1179656 | tf_op jit(solution)/shard_map/ppermute | solution.py:504
  62.1 23.0 %collective-permute-start.21 = (bf16[1024,256]{1,0:T(8,128)(2,1)S(1)}, bf16[1024,256]{1,0:T(8,128)(2,1)S(1)}, u32[]{:S(2)}, u32[]{:S(2)}) collective-permute-start(bf16[1024,256]{1,0:T(8,128)(2,1)S(1)} %get-tuple-element.87.refs_8_.refs_1_), channel_id=1, source_target_pairs={{0,1},{1,0},{2,3},{3,2},{4,5},{5,4},{6,7},{7,6},{8,9},{9,8},{10,11... | collective-permute-start | bytes 1572872 | tf_op jit(solution)/shard_map/ppermute | solution.py:503
  73.4 10.2 %collective-permute-start.27 = (bf16[256,256]{1,0:T(8,128)(2,1)S(1)}, bf16[256,256]{1,0:T(8,128)(2,1)S(1)}, u32[]{:S(2)}, u32[]{:S(2)}) collective-permute-start(bf16[256,256]{1,0:T(8,128)(2,1)S(1)} %get-tuple-element.95.refs_6_), channel_id=1, source_target_pairs={{2,0},{3,1},{0,2},{1,3},{6,4},{7,5},{4,6},{5,7},{10,8},{11,9},{8,1... | collective-permute-start | bytes 393224 | tf_op jit(solution)/shard_map/ppermute | solution.py:504
  84.0 14.9 %collective-permute-start.31 = (bf16[1024,256]{1,0:T(8,128)(2,1)S(1)}, bf16[1024,256]{1,0:T(8,128)(2,1)S(1)}, u32[]{:S(2)}, u32[]{:S(2)}) collective-permute-start(bf16[1024,256]{1,0:T(8,128)(2,1)S(1)} %decoder_grad.10.refs_8_.refs_3_), channel_id=1, source_target_pairs={{0,2},{1,3},{2,0},{3,1},{4,6},{5,7},{6,4},{7,5},{8,10},{9,11},{10,... | collective-permute-start | bytes 1572872 | tf_op jit(solution)/shard_map/ppermute | solution.py:506
  90.8 16.5 %collective-permute-start.33 = (bf16[768,256]{1,0:T(8,128)(2,1)S(1)}, bf16[768,256]{1,0:T(8,128)(2,1)S(1)}, u32[]{:S(2)}, u32[]{:S(2)}) collective-permute-start(bf16[768,256]{1,0:T(8,128)(2,1)S(1)} %encoder_grad.12.refs_8_), channel_id=1, source_target_pairs={{0,2},{1,3},{2,0},{3,1},{4,6},{5,7},{6,4},{7,5},{8,10},{9,11},{10,... | collective-permute-start | bytes 1179656 | tf_op jit(solution)/shard_map/ppermute | solution.py:506
  100.2 9.6 %collective-permute-start.32 = (bf16[256,256]{1,0:T(8,128)(2,1)S(1)}, bf16[256,256]{1,0:T(8,128)(2,1)S(1)}, u32[]{:S(2)}, u32[]{:S(2)}) collective-permute-start(bf16[256,256]{1,0:T(8,128)(2,1)S(1)} %encoder_grad.13.refs_3_), channel_id=1, source_target_pairs={{0,2},{1,3},{2,0},{3,1},{4,6},{5,7},{6,4},{7,5},{8,10},{9,11},{10,... | collective-permute-start | bytes 393224 | tf_op jit(solution)/shard_map/ppermute | solution.py:506
  (19 other events, 75.2 us)

commit v12 on v11

--- a/solution.py
+++ b/solution.py
@@ -347,10 +347,11 @@
     if n_low is not None:
         anchor, before, lows = refs[0], refs[1:1 + n_low], refs[1 + n_low:-3]
         value = mixed(plan, k, new, anchor[off:off + own.shape[0], :]).astype(bf16)
-        lows[0][...] = value
-        if before:
-            lows[1][:off, :] = before[0][...]
-            lows[1][off:, :] = value
+        for b in before:
+            lows[0][:off, :] = b[...]
+        lows[0][off:, :] = value
+    if last and k:
+        refs[-4][...] = jnp.zeros_like(refs[-4])
     theta_out, first_out, second_out = refs[-3:]
     theta_out[0, 0] = new
     first_out[0, 0] = one
@@ -377,11 +378,13 @@
                 aliases[1 + len(ins)] = n
                 ins.append((p, pl.BlockSpec(memory_space=pl.ANY)))
         outs = [(sds(full, f32), once(block, lambda g, m: (0, k, i, 0)))] * 3
+        if prev is None:
+            outs = [(sds((8, 128), f32), whole((8, 128)))] + outs
     else:
         if lows is not None:
             ins += [(a, whole(a.shape)) for a in [new_anc] + lows]
-            shapes = [(cr, width)] + [(off + cr, width)] * len(lows)
-            outs = [(sds(shape, bf16), whole(shape)) for shape in shapes]
+            shape = (off + cr, width)
+            outs = [(sds(shape, bf16), whole(shape))]
         outs += [(sds(block, f32), whole(block))] * 3
     return call(
         functools.partial(adam_body, last, len(got), k, off, None if lows is None else len(lows)), "adam_rows",
@@ -579,32 +582,36 @@
                 own = outer_add(plan, [own, across(own, bit)], 2 * bit == n_rep, [slopes])
                 bit *= 2
             sent.append(own)
+        adam = lambda key, prev, *more, after=(): adam_rows(
+            plan, key, mine[key], got[key], state[key], state_at[key], new_anc, prev, weights.shape, last,
+            *more, after=after)
+        prev = None
+        mine = {}
         for n, key in enumerate(blocks[1:]):
             for s in others:
                 sent.append(enc_grad(s, *key[1:], bf16, sent[-1:]))
                 got[key].append(give(sent[-1], s))
             if n == 0:
-                mine = {blocks[0]: dec_grad(0, rows, dec_parts, back, False, f32, sent[-1:])}
+                mine[blocks[0]] = dec_grad(0, rows, dec_parts, back, False, f32, sent[-1:])
                 sent.append(mine[blocks[0]])
-        for key in blocks[1:]:
-            mine[key] = enc_grad(0, *key[1:], f32, sent[-1:])
+                for other in blocks[1:]:
+                    mine[other] = enc_grad(0, *other[1:], f32, sent[-1:])
+                    sent.append(mine[other])
+                if last:
+                    token, *prev = adam(blocks[0], None)
+                    sent.append(token)
 
         if not last:
             quarters = [own] + [across(own, m) for m in range(1, 4)]
             new_anc = outer_anchor(pos, plan, anchor, momentum, quarters, [mine[blocks[0]]])
-        new_state, prev, lows = {}, None, []
-        adam = lambda key, prev, *more, after=(): adam_rows(
-            plan, key, mine[key], got[key], state[key], state_at[key], new_anc, prev, weights.shape, last,
-            *more, after=after)
+        new_state, lows = {}, []
         if last:
-            for key in blocks:
+            for key in blocks[1:]:
                 prev = adam(key, prev)
         else:
             for key in blocks[1:]:
-                *new, a, b, c = adam(key, None, lows)
-                lows.append(new[0])
-                new_state[key] = (a, b, c)
-            enc = new[-1]
+                enc, *new_state[key] = adam(key, None, lows)
+                lows = [enc]
             enc_parts = [enc]
             new_state[blocks[0]] = adam(blocks[0], None, after=[enc])
             dec, *dec_parts = mix_rows(plan, new_anc, 1, new_state[blocks[0]][0], sizes, [enc])

time: 112 us -> 111 us (level)
  no operation moved by 1% of the time
where the time goes in v12:
time: 111 us
  Pallas kernels  50 us (45%)
  starting transfers between devices  29.2 us (26%)
  waiting for transfers between devices  28.7 us (26%)
  local copies, waits for them, and re-layouts  1.77 us (2%)
    pallas_call x46, Pallas kernels, call(): pl.pallas_call(run, name=name, out_shape=[o for o, _ in outs], grid_spec=...  50 us
    ppermute x7, starting transfers between devices, local(): lax.ppermute(a, 'replica', [(r, r ^ bit) for r in range(n_rep)])  11.8 us
    ppermute x6, waiting for transfers between devices, local(): lax.ppermute(a, 'fsdp', [((f // 2 + s) % chips * 2 + f % 2, f) for f in r...  11.7 us
    ppermute x6, waiting for transfers between devices, local(): lax.ppermute(a, 'fsdp', [(f, (f // 2 + s) % chips * 2 + f % 2) for f in r...  11.1 us
    ppermute x6, starting transfers between devices, local(): lax.ppermute(a, 'fsdp', [((f // 2 + s) % chips * 2 + f % 2, f) for f in r...  7.68 us
    ppermute x6, starting transfers between devices, local(): lax.ppermute(a, 'fsdp', [(f, (f // 2 + s) % chips * 2 + f % 2) for f in r...  6.72 us
    ppermute x7, waiting for transfers between devices, local(): lax.ppermute(a, 'replica', [(r, r ^ bit) for r in range(n_rep)])  5.93 us
    ppermute x15, starting transfers between devices, local(): to_partner = lambda a: lax.ppermute(a, 'fsdp', partner)  3.05 us
  transfers between devices with their start and end apart: 34, of which 12 were waited for; matrix products, arithmetic and copies ran while one was open for 0% of the time, Pallas kernels for 43%

profile of v12, /device:TPU:0, one launch (start us, length us, event | category | flops | bytes accessed | tf_op | source)
XLA Modules:
  0.0 110.8 jit_solution(12345119836449244523)
XLA Ops:
  3.1 3.0 %collective-permute-start.8 = (bf16[1024,256]{1,0:T(8,128)(2,1)S(1)}, bf16[1024,256]{1,0:T(8,128)(2,1)S(1)}, u32[]{:S(2)}, u32[]{:S(2)}) collective-permute-start(bf16[1024,256]{1,0:T(8,128)(2,1)S(1)} %get-tuple-element.65.refs_4_.refs_1_), channel_id=1, source_target_pairs={{2,0},{3,1},{0,2},{1,3},{6,4},{7,5},{4,6},{5,7},{10,8},{11,9},{8,1... | collective-permute-start | bytes 1572872 | tf_op jit(solution)/shard_map/ppermute | solution.py:507
  9.9 2.1 %collective-permute-done.1.refs_2_ = bf16[256,256]{1,0:T(8,128)(2,1)S(1)} collective-permute-done((bf16[256,256]{1,0:T(8,128)(2,1)S(1)}, bf16[256,256]{1,0:T(8,128)(2,1)S(1)}, u32[]{:S(2)}, u32[]{:S(2)}) %collective-permute-start.1) | collective-permute-done | bytes 131104 | tf_op jit(solution)/shard_map/ppermute | solution.py:511
  12.1 2.6 %collective-permute-start.3 = (bf16[256,256]{1,0:T(8,128)(2,1)S(1)}, bf16[256,256]{1,0:T(8,128)(2,1)S(1)}, u32[]{:S(2)}, u32[]{:S(2)}) collective-permute-start(bf16[256,256]{1,0:T(8,128)(2,1)S(1)} %get-tuple-element.69), channel_id=1, source_target_pairs={{0,12},{4,8},{8,4},{12,0},{16,28},{20,24},{24,20},{28,16},{1,13},{... | collective-permute-start | bytes 393224 | tf_op jit(solution)/shard_map/ppermute | solution.py:511
  17.3 2.9 %stage_tokens.1 = (bf16[512,4096]{1,0:T(8,128)(2,1)S(1)}, bf16[2048,512]{1,0:T(8,128)(2,1)S(1)}) custom-call(s32[5]{0:T(128)S(1)} %stack.23.refs_0_.refs_1_, bf16[512,4096]{1,0:T(8,128)(2,1)} %collective-permute-done.refs_1_), custom_call_target="tpu_custom_call" | custom-call | bytes 10485760 | tf_op jit(solution)/shard_map/stage_tokens/pallas_call | solution.py:60
  20.3 1.8 %forward_encoder.4.refs_2_.refs_1_ = f32[2,512,256]{2,1,0:T(8,128)S(1)} custom-call(s32[5]{0:T(128)S(1)} %stack.23.refs_0_.refs_1_, bf16[1024,256]{1,0:T(8,128)(2,1)S(1)} %get-tuple-element.65.refs_4_.refs_1_, bf16[1024,256]{1,0:T(8,128)(2,1)S(1)} %collective-permute-done.7.refs_2_, bf16[512,4096]{1,0:T(8,128)(2,1)S(1)} %copy-done, ...), custom_call_target="tpu_custom_call" | custom-call | bytes 10485760 | tf_op jit(solution)/shard_map/forward_encoder/pallas_call | solution.py:60
  25.4 2.3 %hidden_units.2 = (bf16[2,512,256]{2,1,0:T(8,128)(2,1)S(1)}, f32[2,512,256]{2,1,0:T(8,128)S(1)}, bf16[2,512,256]{2,1,0:T(8,128)(2,1)S(1)}, bf16[256,256]{1,0:T(8,128)(2,1)S(1)}, bf16[256,256]{1,0:T(8,128)(2,1)S(1)}) custom-call(s32[5]{0:T(128)S(1)} %stack.23.refs_0_.refs_1_, f32[2,512,256]{2,1,0:T(8,128)S(1)} %forward_encoder.5.refs_1_, ...), custom_call_target="tpu_custom_call" | custom-call | bytes 12333056 | tf_op jit(solution)/shard_map/hidden_units/pallas_call | solution.py:60
  29.9 1.8 %collective-permute-start.18 = (bf16[1024,256]{1,0:T(8,128)(2,1)S(1)}, bf16[1024,256]{1,0:T(8,128)(2,1)S(1)}, u32[]{:S(2)}, u32[]{:S(2)}) collective-permute-start(bf16[1024,256]{1,0:T(8,128)(2,1)S(1)} %decoder_grad.7.refs_8_), channel_id=1, source_target_pairs={{0,2},{1,3},{2,0},{3,1},{4,6},{5,7},{6,4},{7,5},{8,10},{9,11},{10,... | collective-permute-start | bytes 1572872 | tf_op jit(solution)/shard_map/ppermute | solution.py:509
  32.2 2.6 %collective-permute-start.4 = (bf16[256,256]{1,0:T(8,128)(2,1)S(1)}, bf16[256,256]{1,0:T(8,128)(2,1)S(1)}, u32[]{:S(2)}, u32[]{:S(2)}) collective-permute-start(bf16[256,256]{1,0:T(8,128)(2,1)S(1)} %add_quarters.2.refs_3_.refs_1_), channel_id=1, source_target_pairs={{0,16},{4,20},{8,24},{12,28},{16,0},{20,4},{24,8},{28,12},{1,17},{... | collective-permute-start | bytes 393224 | tf_op jit(solution)/shard_map/ppermute | solution.py:511
  34.8 3.0 %forward_decoder.2 = (f32[2,512,256]{2,1,0:T(8,128)S(1)}, f32[256,256]{1,0:T(8,128)S(1)}) custom-call(s32[5]{0:T(128)S(1)} %stack.23.refs_0_.refs_1_, bf16[1024,256]{1,0:T(8,128)(2,1)S(1)} %get-tuple-element.70.refs_1_, bf16[1024,256]{1,0:T(8,128)(2,1)S(1)} %collective-permute-done.5.refs_2_, bf16[384,256]{1,0:T(8,128)(2,1)S(1)} %get-tuple-element.76.refs_5_.refs_3_, ...), custom_call_target="tpu_custom_call" | custom-call | bytes 11272192 | tf_op jit(solution)/shard_map/forward_decoder/pallas_call | solution.py:60
  37.8 2.0 %slope_pre.2.refs_3_.refs_2_ = bf16[2,512,256]{2,1,0:T(8,128)(2,1)S(1)} custom-call(s32[5]{0:T(128)S(1)} %stack.23.refs_0_.refs_1_, f32[2,512,256]{2,1,0:T(8,128)S(1)} %get-tuple-element.81.refs_1_, f32[256,256]{1,0:T(8,128)S(1)} %get-tuple-element.82.refs_2_, bf16[2,512,256]{2,1,0:T(8,128)(2,1)S(1)} %get-tuple-element.83.refs_3_, ...), custom_call_target="tpu_custom_call" | custom-call | bytes 12320768 | tf_op jit(solution)/shard_map/slope_pre/pallas_call | solution.py:60
  39.8 2.0 %collective-permute-done.4.refs_2_ = bf16[256,256]{1,0:T(8,128)(2,1)S(1)} collective-permute-done((bf16[256,256]{1,0:T(8,128)(2,1)S(1)}, bf16[256,256]{1,0:T(8,128)(2,1)S(1)}, u32[]{:S(2)}, u32[]{:S(2)}) %collective-permute-start.4) | collective-permute-done | bytes 131104 | tf_op jit(solution)/shard_map/ppermute | solution.py:511
  49.2 1.6 %collective-permute-start.19 = (bf16[256,256]{1,0:T(8,128)(2,1)S(1)}, bf16[256,256]{1,0:T(8,128)(2,1)S(1)}, u32[]{:S(2)}, u32[]{:S(2)}) collective-permute-start(bf16[256,256]{1,0:T(8,128)(2,1)S(1)} %encoder_grad.11), channel_id=1, source_target_pairs={{0,2},{1,3},{2,0},{3,1},{4,6},{5,7},{6,4},{7,5},{8,10},{9,11},{10,... | collective-permute-start | bytes 393224 | tf_op jit(solution)/shard_map/ppermute | solution.py:509
  51.0 1.6 %collective-permute-done.17.refs_7_ = bf16[256,256]{1,0:T(8,128)(2,1)S(1)} collective-permute-done((bf16[256,256]{1,0:T(8,128)(2,1)S(1)}, bf16[256,256]{1,0:T(8,128)(2,1)S(1)}, u32[]{:S(2)}, u32[]{:S(2)}) %collective-permute-start.17) | collective-permute-done | bytes 131104 | tf_op jit(solution)/shard_map/ppermute | solution.py:511
  61.6 3.1 %outer_step.1 = (f32[2,1024,256]{2,1,0:T(8,128)}, f32[2,1024,256]{2,1,0:T(8,128)}, f32[8,128]{1,0:T(8,128)S(1)}) custom-call(s32[5]{0:T(128)S(1)} %stack.23.refs_0_.refs_1_, s32[8]{0:T(128)S(1)} %copy-done.7, f32[2,1024,256]{2,1,0:T(8,128)S(1)} %copy-done.3, f32[2,1024,256]{2,1,0:T(8,128)S(1)} %copy-done.6, ...), custom_call_target="tpu_custom_call" | custom-call | bytes 8916992 | tf_op jit(solution)/shard_map/outer_step/pallas_call | solution.py:60
  64.7 1.8 %forward_encoder.6.refs_1_ = f32[2,512,256]{2,1,0:T(8,128)S(1)} custom-call(s32[5]{0:T(128)S(1)} %stack.23.refs_0_.refs_1_, bf16[1024,256]{1,0:T(8,128)(2,1)S(1)} %get-tuple-element.86.refs_5_.refs_3_.refs_1_, bf16[1024,256]{1,0:T(8,128)(2,1)S(1)} %collective-permute-done.23.refs_2_, bf16[512,4096]{1,0:T(8,128)(2,1)S(1)} %copy-done, ...), custom_call_target="tpu_custom_call" | custom-call | bytes 10485760 | tf_op jit(solution)/shard_map/forward_encoder/pallas_call | solution.py:60
  66.5 5.8 %collective-permute-done.24.refs_0_ = bf16[1024,256]{1,0:T(8,128)(2,1)S(1)} collective-permute-done((bf16[1024,256]{1,0:T(8,128)(2,1)S(1)}, bf16[1024,256]{1,0:T(8,128)(2,1)S(1)}, u32[]{:S(2)}, u32[]{:S(2)}) %collective-permute-start.24) | collective-permute-done | bytes 524320 | tf_op jit(solution)/shard_map/ppermute | solution.py:507
  74.8 2.3 %hidden_units.3 = (bf16[2,512,256]{2,1,0:T(8,128)(2,1)S(1)}, f32[2,512,256]{2,1,0:T(8,128)S(1)}, bf16[2,512,256]{2,1,0:T(8,128)(2,1)S(1)}, bf16[256,256]{1,0:T(8,128)(2,1)S(1)}, bf16[256,256]{1,0:T(8,128)(2,1)S(1)}) custom-call(s32[5]{0:T(128)S(1)} %stack.23.refs_0_.refs_1_, f32[2,512,256]{2,1,0:T(8,128)S(1)} %forward_encoder.7.refs_1_, ...), custom_call_target="tpu_custom_call" | custom-call | bytes 12324864 | tf_op jit(solution)/shard_map/hidden_units/pallas_call | solution.py:60
  77.2 3.6 %collective-permute-done.22.refs_0_ = bf16[768,256]{1,0:T(8,128)(2,1)S(1)} collective-permute-done((bf16[768,256]{1,0:T(8,128)(2,1)S(1)}, bf16[768,256]{1,0:T(8,128)(2,1)S(1)}, u32[]{:S(2)}, u32[]{:S(2)}) %collective-permute-start.22) | collective-permute-done | bytes 393248 | tf_op jit(solution)/shard_map/ppermute | solution.py:507
  84.6 3.0 %forward_decoder.3 = (f32[2,512,256]{2,1,0:T(8,128)S(1)}, f32[256,256]{1,0:T(8,128)S(1)}) custom-call(s32[5]{0:T(128)S(1)} %stack.23.refs_0_.refs_1_, bf16[1024,256]{1,0:T(8,128)(2,1)S(1)} %get-tuple-element.88.refs_8_.refs_1_, bf16[1024,256]{1,0:T(8,128)(2,1)S(1)} %collective-permute-done.21.refs_2_, ...), custom_call_target="tpu_custom_call" | custom-call | bytes 11272192 | tf_op jit(solution)/shard_map/forward_decoder/pallas_call | solution.py:60
  87.6 2.1 %slope_pre.3.refs_2_ = bf16[2,512,256]{2,1,0:T(8,128)(2,1)S(1)} custom-call(s32[5]{0:T(128)S(1)} %stack.23.refs_0_.refs_1_, f32[2,512,256]{2,1,0:T(8,128)S(1)} %get-tuple-element.99.refs_1_, f32[256,256]{1,0:T(8,128)S(1)} %get-tuple-element.100.refs_2_, bf16[2,512,256]{2,1,0:T(8,128)(2,1)S(1)} %get-tuple-element.101.refs_3_, ...), custom_call_target="tpu_custom_call" | custom-call | bytes 12320768 | tf_op jit(solution)/shard_map/slope_pre/pallas_call | solution.py:60
  91.8 6.6 %collective-permute-done.31.refs_7_ = bf16[1024,256]{1,0:T(8,128)(2,1)S(1)} collective-permute-done((bf16[1024,256]{1,0:T(8,128)(2,1)S(1)}, bf16[1024,256]{1,0:T(8,128)(2,1)S(1)}, u32[]{:S(2)}, u32[]{:S(2)}) %collective-permute-start.31) | collective-permute-done | bytes 524320 | tf_op jit(solution)/shard_map/ppermute | solution.py:509
  99.4 2.8 %adam_rows.9 = (f32[8,128]{1,0:T(8,128)S(1)}, f32[1,2,1024,256]{3,2,1,0:T(8,128)}, f32[1,2,1024,256]{3,2,1,0:T(8,128)}, f32[1,2,1024,256]{3,2,1,0:T(8,128)}) custom-call(s32[8]{0:T(128)S(1)} %copy-done.7, f32[1024,256]{1,0:T(8,128)S(1)} %decoder_grad.11.refs_3_.refs_1_, f32[1,1,1024,256]{3,2,1,0:T(8,128)S(1)} %get-tuple-element.87.refs_2_, ...), custom_call_target="tpu_custom_call" | custom-call | bytes 11538432 | tf_op jit(solution)/shard_map/adam_rows/pallas_call | solution.py:60
  104.0 2.8 %collective-permute-done.33.refs_2_ = bf16[768,256]{1,0:T(8,128)(2,1)S(1)} collective-permute-done((bf16[768,256]{1,0:T(8,128)(2,1)S(1)}, bf16[768,256]{1,0:T(8,128)(2,1)S(1)}, u32[]{:S(2)}, u32[]{:S(2)}) %collective-permute-start.33) | collective-permute-done | bytes 393248 | tf_op jit(solution)/shard_map/ppermute | solution.py:509
  106.8 2.4 %adam_rows.10 = (f32[1,2,1024,256]{3,2,1,0:T(8,128)}, f32[1,2,1024,256]{3,2,1,0:T(8,128)}, f32[1,2,1024,256]{3,2,1,0:T(8,128)}) custom-call(s32[8]{0:T(128)S(1)} %copy-done.7, f32[768,256]{1,0:T(8,128)S(1)} %encoder_grad.13.refs_3_.refs_1_, ...), custom_call_target="tpu_custom_call", output_to_operand_aliasing={{0}: (7, {}), {1}: (8, {}), {2}: (9, {})} | custom-call | bytes 16908288 | tf_op jit(solution)/shard_map/adam_rows/pallas_call | solution.py:60
  (109 shorter events, 44.1 us)
Async XLA Ops:
  0.6 15.5 %collective-permute-start = (bf16[512,4096]{1,0:T(8,128)(2,1)}, bf16[512,4096]{1,0:T(8,128)(2,1)}, u32[]{:S(2)}, u32[]{:S(2)}) collective-permute-start(bf16[512,4096]{1,0:T(8,128)(2,1)} %refs_8_.3), channel_id=1, source_target_pairs={{0,1},{1,0},{2,3},{3,2},{4,5},{5,4},{6,7},{7,6},{8,9},{9,8},{10,11... | collective-permute-start | bytes 12582920 | tf_op jit(solution)/shard_map/ppermute | solution.py:506
  3.0 11.7 %collective-permute-start.7 = (bf16[1024,256]{1,0:T(8,128)(2,1)S(1)}, bf16[1024,256]{1,0:T(8,128)(2,1)S(1)}, u32[]{:S(2)}, u32[]{:S(2)}) collective-permute-start(bf16[1024,256]{1,0:T(8,128)(2,1)S(1)} %get-tuple-element.65.refs_4_.refs_1_), channel_id=1, source_target_pairs={{0,1},{1,0},{2,3},{3,2},{4,5},{5,4},{6,7},{7,6},{8,9},{9,8},{10,11... | collective-permute-start | bytes 1572872 | tf_op jit(solution)/shard_map/ppermute | solution.py:506
  3.1 19.6 %collective-permute-start.8 = (bf16[1024,256]{1,0:T(8,128)(2,1)S(1)}, bf16[1024,256]{1,0:T(8,128)(2,1)S(1)}, u32[]{:S(2)}, u32[]{:S(2)}) collective-permute-start(bf16[1024,256]{1,0:T(8,128)(2,1)S(1)} %get-tuple-element.65.refs_4_.refs_1_), channel_id=1, source_target_pairs={{2,0},{3,1},{0,2},{1,3},{6,4},{7,5},{4,6},{5,7},{10,8},{11,9},{8,1... | collective-permute-start | bytes 1572872 | tf_op jit(solution)/shard_map/ppermute | solution.py:507
  8.4 13.7 %collective-permute-start.2 = (bf16[256,256]{1,0:T(8,128)(2,1)S(1)}, bf16[256,256]{1,0:T(8,128)(2,1)S(1)}, u32[]{:S(2)}, u32[]{:S(2)}) collective-permute-start(bf16[256,256]{1,0:T(8,128)(2,1)S(1)} %get-tuple-element.68), channel_id=1, source_target_pairs={{0,8},{4,12},{8,0},{12,4},{16,24},{20,28},{24,16},{28,20},{1,9},{5... | collective-permute-start | bytes 393224 | tf_op jit(solution)/shard_map/ppermute | solution.py:511
  12.1 10.0 %collective-permute-start.3 = (bf16[256,256]{1,0:T(8,128)(2,1)S(1)}, bf16[256,256]{1,0:T(8,128)(2,1)S(1)}, u32[]{:S(2)}, u32[]{:S(2)}) collective-permute-start(bf16[256,256]{1,0:T(8,128)(2,1)S(1)} %get-tuple-element.69), channel_id=1, source_target_pairs={{0,12},{4,8},{8,4},{12,0},{16,28},{20,24},{24,20},{28,16},{1,13},{... | collective-permute-start | bytes 393224 | tf_op jit(solution)/shard_map/ppermute | solution.py:511
  14.6 13.2 %collective-permute-start.6 = (bf16[768,256]{1,0:T(8,128)(2,1)S(1)}, bf16[768,256]{1,0:T(8,128)(2,1)S(1)}, u32[]{:S(2)}, u32[]{:S(2)}) collective-permute-start(bf16[768,256]{1,0:T(8,128)(2,1)S(1)} %get-tuple-element.71.refs_5_), channel_id=1, source_target_pairs={{2,0},{3,1},{0,2},{1,3},{6,4},{7,5},{4,6},{5,7},{10,8},{11,9},{8,1... | collective-permute-start | bytes 1179656 | tf_op jit(solution)/shard_map/ppermute | solution.py:507
  16.2 16.0 %collective-permute-start.5 = (bf16[1024,256]{1,0:T(8,128)(2,1)S(1)}, bf16[1024,256]{1,0:T(8,128)(2,1)S(1)}, u32[]{:S(2)}, u32[]{:S(2)}) collective-permute-start(bf16[1024,256]{1,0:T(8,128)(2,1)S(1)} %get-tuple-element.70.refs_1_), channel_id=1, source_target_pairs={{0,1},{1,0},{2,3},{3,2},{4,5},{5,4},{6,7},{7,6},{8,9},{9,8},{10,11... | collective-permute-start | bytes 1572872 | tf_op jit(solution)/shard_map/ppermute | solution.py:506
  23.4 6.0 %collective-permute-start.11 = (bf16[256,256]{1,0:T(8,128)(2,1)S(1)}, bf16[256,256]{1,0:T(8,128)(2,1)S(1)}, u32[]{:S(2)}, u32[]{:S(2)}) collective-permute-start(bf16[256,256]{1,0:T(8,128)(2,1)S(1)} %get-tuple-element.78.refs_6_), channel_id=1, source_target_pairs={{2,0},{3,1},{0,2},{1,3},{6,4},{7,5},{4,6},{5,7},{10,8},{11,9},{8,1... | collective-permute-start | bytes 393224 | tf_op jit(solution)/shard_map/ppermute | solution.py:507
  29.9 17.1 %collective-permute-start.18 = (bf16[1024,256]{1,0:T(8,128)(2,1)S(1)}, bf16[1024,256]{1,0:T(8,128)(2,1)S(1)}, u32[]{:S(2)}, u32[]{:S(2)}) collective-permute-start(bf16[1024,256]{1,0:T(8,128)(2,1)S(1)} %decoder_grad.7.refs_8_), channel_id=1, source_target_pairs={{0,2},{1,3},{2,0},{3,1},{4,6},{5,7},{6,4},{7,5},{8,10},{9,11},{10,... | collective-permute-start | bytes 1572872 | tf_op jit(solution)/shard_map/ppermute | solution.py:509
  31.7 6.1 %collective-permute-start.12 = (bf16[384,256]{1,0:T(8,128)(2,1)S(1)}, bf16[384,256]{1,0:T(8,128)(2,1)S(1)}, u32[]{:S(2)}, u32[]{:S(2)}) collective-permute-start(bf16[384,256]{1,0:T(8,128)(2,1)S(1)} %get-tuple-element.76.refs_5_.refs_3_), channel_id=1, source_target_pairs={{0,1},{1,0},{2,3},{3,2},{4,5},{5,4},{6,7},{7,6},{8,9},{9,8},{10,11... | collective-permute-start | bytes 589832 | tf_op jit(solution)/shard_map/ppermute | solution.py:506
  31.7 6.1 %collective-permute-start.13 = (bf16[384,256]{1,0:T(8,128)(2,1)S(1)}, bf16[384,256]{1,0:T(8,128)(2,1)S(1)}, u32[]{:S(2)}, u32[]{:S(2)}) collective-permute-start(bf16[384,256]{1,0:T(8,128)(2,1)S(1)} %get-tuple-element.77.refs_6_.refs_4_), channel_id=1, source_target_pairs={{0,1},{1,0},{2,3},{3,2},{4,5},{5,4},{6,7},{7,6},{8,9},{9,8},{10,11... | collective-permute-start | bytes 589832 | tf_op jit(solution)/shard_map/ppermute | solution.py:506
  32.2 9.6 %collective-permute-start.4 = (bf16[256,256]{1,0:T(8,128)(2,1)S(1)}, bf16[256,256]{1,0:T(8,128)(2,1)S(1)}, u32[]{:S(2)}, u32[]{:S(2)}) collective-permute-start(bf16[256,256]{1,0:T(8,128)(2,1)S(1)} %add_quarters.2.refs_3_.refs_1_), channel_id=1, source_target_pairs={{0,16},{4,20},{8,24},{12,28},{16,0},{20,4},{24,8},{28,12},{1,17},{... | collective-permute-start | bytes 393224 | tf_op jit(solution)/shard_map/ppermute | solution.py:511
  43.0 12.1 %collective-permute-start.20 = (bf16[768,256]{1,0:T(8,128)(2,1)S(1)}, bf16[768,256]{1,0:T(8,128)(2,1)S(1)}, u32[]{:S(2)}, u32[]{:S(2)}) collective-permute-start(bf16[768,256]{1,0:T(8,128)(2,1)S(1)} %encoder_grad.8.refs_8_), channel_id=1, source_target_pairs={{0,2},{1,3},{2,0},{3,1},{4,6},{5,7},{6,4},{7,5},{8,10},{9,11},{10,... | collective-permute-start | bytes 1179656 | tf_op jit(solution)/shard_map/ppermute | solution.py:509
  43.5 7.4 %collective-permute-start.15 = (bf16[256,256]{1,0:T(8,128)(2,1)S(1)}, bf16[256,256]{1,0:T(8,128)(2,1)S(1)}, u32[]{:S(2)}, u32[]{:S(2)}) collective-permute-start(bf16[256,256]{1,0:T(8,128)(2,1)S(1)} %add_quarters.3.refs_3_.refs_4_), channel_id=1, source_target_pairs={{0,4},{4,0},{8,12},{12,8},{16,20},{20,16},{24,28},{28,24},{1,5},{5... | collective-permute-start | bytes 393224 | tf_op jit(solution)/shard_map/ppermute | solution.py:511
  45.7 6.9 %collective-permute-start.17 = (bf16[256,256]{1,0:T(8,128)(2,1)S(1)}, bf16[256,256]{1,0:T(8,128)(2,1)S(1)}, u32[]{:S(2)}, u32[]{:S(2)}) collective-permute-start(bf16[256,256]{1,0:T(8,128)(2,1)S(1)} %add_quarters.3.refs_3_.refs_4_), channel_id=1, source_target_pairs={{0,12},{4,8},{8,4},{12,0},{16,28},{20,24},{24,20},{28,16},{1,13},{... | collective-permute-start | bytes 393224 | tf_op jit(solution)/shard_map/ppermute | solution.py:511
  49.2 7.4 %collective-permute-start.19 = (bf16[256,256]{1,0:T(8,128)(2,1)S(1)}, bf16[256,256]{1,0:T(8,128)(2,1)S(1)}, u32[]{:S(2)}, u32[]{:S(2)}) collective-permute-start(bf16[256,256]{1,0:T(8,128)(2,1)S(1)} %encoder_grad.11), channel_id=1, source_target_pairs={{0,2},{1,3},{2,0},{3,1},{4,6},{5,7},{6,4},{7,5},{8,10},{9,11},{10,... | collective-permute-start | bytes 393224 | tf_op jit(solution)/shard_map/ppermute | solution.py:509
  57.4 7.3 %collective-permute-start.23 = (bf16[1024,256]{1,0:T(8,128)(2,1)S(1)}, bf16[1024,256]{1,0:T(8,128)(2,1)S(1)}, u32[]{:S(2)}, u32[]{:S(2)}) collective-permute-start(bf16[1024,256]{1,0:T(8,128)(2,1)S(1)} %get-tuple-element.86.refs_5_.refs_3_.refs_1_), channel_id=1, source_target_pairs={{0,1},{1,0},{2,3},{3,2},{4,5},{5,4},{6,7},{7,6},{8,9},{9,8},{10,11... | collective-permute-start | bytes 1572872 | tf_op jit(solution)/shard_map/ppermute | solution.py:506
  57.5 14.8 %collective-permute-start.24 = (bf16[1024,256]{1,0:T(8,128)(2,1)S(1)}, bf16[1024,256]{1,0:T(8,128)(2,1)S(1)}, u32[]{:S(2)}, u32[]{:S(2)}) collective-permute-start(bf16[1024,256]{1,0:T(8,128)(2,1)S(1)} %get-tuple-element.86.refs_5_.refs_3_.refs_1_), channel_id=1, source_target_pairs={{2,0},{3,1},{0,2},{1,3},{6,4},{7,5},{4,6},{5,7},{10,8},{11,9},{8,1... | collective-permute-start | bytes 1572872 | tf_op jit(solution)/shard_map/ppermute | solution.py:507
  60.1 20.6 %collective-permute-start.22 = (bf16[768,256]{1,0:T(8,128)(2,1)S(1)}, bf16[768,256]{1,0:T(8,128)(2,1)S(1)}, u32[]{:S(2)}, u32[]{:S(2)}) collective-permute-start(bf16[768,256]{1,0:T(8,128)(2,1)S(1)} %get-tuple-element.89.refs_5_), channel_id=1, source_target_pairs={{2,0},{3,1},{0,2},{1,3},{6,4},{7,5},{4,6},{5,7},{10,8},{11,9},{8,1... | collective-permute-start | bytes 1179656 | tf_op jit(solution)/shard_map/ppermute | solution.py:507
  72.9 11.7 %collective-permute-start.21 = (bf16[1024,256]{1,0:T(8,128)(2,1)S(1)}, bf16[1024,256]{1,0:T(8,128)(2,1)S(1)}, u32[]{:S(2)}, u32[]{:S(2)}) collective-permute-start(bf16[1024,256]{1,0:T(8,128)(2,1)S(1)} %get-tuple-element.88.refs_8_.refs_1_), channel_id=1, source_target_pairs={{0,1},{1,0},{2,3},{3,2},{4,5},{5,4},{6,7},{7,6},{8,9},{9,8},{10,11... | collective-permute-start | bytes 1572872 | tf_op jit(solution)/shard_map/ppermute | solution.py:506
  73.0 10.1 %collective-permute-start.27 = (bf16[256,256]{1,0:T(8,128)(2,1)S(1)}, bf16[256,256]{1,0:T(8,128)(2,1)S(1)}, u32[]{:S(2)}, u32[]{:S(2)}) collective-permute-start(bf16[256,256]{1,0:T(8,128)(2,1)S(1)} %get-tuple-element.96.refs_6_), channel_id=1, source_target_pairs={{2,0},{3,1},{0,2},{1,3},{6,4},{7,5},{4,6},{5,7},{10,8},{11,9},{8,1... | collective-permute-start | bytes 393224 | tf_op jit(solution)/shard_map/ppermute | solution.py:507
  83.5 14.9 %collective-permute-start.31 = (bf16[1024,256]{1,0:T(8,128)(2,1)S(1)}, bf16[1024,256]{1,0:T(8,128)(2,1)S(1)}, u32[]{:S(2)}, u32[]{:S(2)}) collective-permute-start(bf16[1024,256]{1,0:T(8,128)(2,1)S(1)} %decoder_grad.10.refs_8_.refs_3_), channel_id=1, source_target_pairs={{0,2},{1,3},{2,0},{3,1},{4,6},{5,7},{6,4},{7,5},{8,10},{9,11},{10,... | collective-permute-start | bytes 1572872 | tf_op jit(solution)/shard_map/ppermute | solution.py:509
  90.3 16.5 %collective-permute-start.33 = (bf16[768,256]{1,0:T(8,128)(2,1)S(1)}, bf16[768,256]{1,0:T(8,128)(2,1)S(1)}, u32[]{:S(2)}, u32[]{:S(2)}) collective-permute-start(bf16[768,256]{1,0:T(8,128)(2,1)S(1)} %encoder_grad.12.refs_8_), channel_id=1, source_target_pairs={{0,2},{1,3},{2,0},{3,1},{4,6},{5,7},{6,4},{7,5},{8,10},{9,11},{10,... | collective-permute-start | bytes 1179656 | tf_op jit(solution)/shard_map/ppermute | solution.py:509
  102.5 6.8 %collective-permute-start.32 = (bf16[256,256]{1,0:T(8,128)(2,1)S(1)}, bf16[256,256]{1,0:T(8,128)(2,1)S(1)}, u32[]{:S(2)}, u32[]{:S(2)}) collective-permute-start(bf16[256,256]{1,0:T(8,128)(2,1)S(1)} %encoder_grad.15), channel_id=1, source_target_pairs={{0,2},{1,3},{2,0},{3,1},{4,6},{5,7},{6,4},{7,5},{8,10},{9,11},{10,... | collective-permute-start | bytes 393224 | tf_op jit(solution)/shard_map/ppermute | solution.py:509
  (19 other events, 81.6 us)

commit v13 on v12

--- a/solution.py
+++ b/solution.py
@@ -522,7 +522,8 @@
     xs, xt = zip(*[turn(pos, x, chips, stage) for x, stage in ((inputs, False), (x_par, True))])
     own = outer_add(plan, [quarters[0]] + [across(quarters[m], m) for m in range(1, 4)], n_rep == 4, xt)
 
-    blocks = [(1, 0, rows)] + [(0, off, size) for off, size in zip(starts, sizes)]
+    half, rest = (rows // 2, rows // 4) if rows >= 1024 else (rows, rows)
+    blocks = [(1, 0, rows), (0, 0, half)] + [(0, off, rest) for off in range(half, rows, rest)]
     state = {key: (weights, first_moment, second_moment) for key in blocks}
     state_at = {(k, off, size): (k, off // size) for k, off, size in blocks}
     new_anc = None
@@ -576,12 +577,6 @@
         carry = forward(
             pos, [], [(dec, 1, 0, rows), (dec_near, 1 + chips, 0, rows)] + part, xs, rows, True, sent[-1:])
         slopes = slope_rows(pos, *carry, hidden, slope, pending, xs, rows)
-        if step == 0:
-            bit = 4
-            while bit < n_rep:
-                own = outer_add(plan, [own, across(own, bit)], 2 * bit == n_rep, [slopes])
-                bit *= 2
-            sent.append(own)
         adam = lambda key, prev, *more, after=(): adam_rows(
             plan, key, mine[key], got[key], state[key], state_at[key], new_anc, prev, weights.shape, last,
             *more, after=after)
@@ -592,14 +587,21 @@
                 sent.append(enc_grad(s, *key[1:], bf16, sent[-1:]))
                 got[key].append(give(sent[-1], s))
             if n == 0:
+                if step == 0:
+                    bit = 4
+                    while bit < n_rep:
+                        own = outer_add(plan, [own, across(own, bit)], 2 * bit == n_rep, sent[-1:])
+                        bit *= 2
+                    sent.append(own)
                 mine[blocks[0]] = dec_grad(0, rows, dec_parts, back, False, f32, sent[-1:])
                 sent.append(mine[blocks[0]])
+            if n == len(blocks) - 3 or len(blocks) == 2:
+                if last:
+                    token, *prev = adam(blocks[0], None)
+                    sent.append(token)
                 for other in blocks[1:]:
                     mine[other] = enc_grad(0, *other[1:], f32, sent[-1:])
                     sent.append(mine[other])
-                if last:
-                    token, *prev = adam(blocks[0], None)
-                    sent.append(token)
 
         if not last:
             quarters = [own] + [across(own, m) for m in range(1, 4)]

time: 111 us -> 110 us (level)
  waiting for transfers between devices: 28.7 us -> 22.9 us
  starting transfers between devices: 29.2 us -> 31.9 us
  Pallas kernels: 50 us -> 52.6 us
    ppermute x7, waiting for transfers between devices: 5.93 us -> 1.64 us  [local(): lax.ppermute(a, 'replica', [(r, r ^ bit) for r in range(n_rep)])]
    ppermute x6 -> x8, waiting for transfers between devices: 11.1 us -> 7.82 us  [local(): lax.ppermute(a, 'fsdp', [(f, (f // 2 + s) % chips * 2 + f % 2) for f in r...]
    pallas_call x46 -> x52, Pallas kernels: 50 us -> 52.6 us  [call(): pl.pallas_call(run, name=name, out_shape=[o for o, _ in outs], grid_spec=...]
    ppermute x6 -> x8, starting transfers between devices: 6.72 us -> 8.85 us  [local(): lax.ppermute(a, 'fsdp', [(f, (f // 2 + s) % chips * 2 + f % 2) for f in r...]
    ppermute x6, waiting for transfers between devices: 11.7 us -> 13.4 us  [local(): lax.ppermute(a, 'fsdp', [((f // 2 + s) % chips * 2 + f % 2, f) for f in r...]
  transfers between devices with their start and end apart: 34 -> 36, of which waited for: 12 -> 11; matrix products, arithmetic and copies ran while one was open for 0% -> 0% of each run, Pallas kernels for 43% -> 46%
where the time goes in v13:
time: 110 us
  Pallas kernels  52.6 us (48%)
  starting transfers between devices  31.9 us (29%)
  waiting for transfers between devices  22.9 us (21%)
  local copies, waits for them, and re-layouts  1.77 us (2%)
  between operations  1.14 us (1%)
    pallas_call x52, Pallas kernels, call(): pl.pallas_call(run, name=name, out_shape=[o for o, _ in outs], grid_spec=...  52.6 us
    ppermute x6, waiting for transfers between devices, local(): lax.ppermute(a, 'fsdp', [((f // 2 + s) % chips * 2 + f % 2, f) for f in r...  13.4 us
    ppermute x7, starting transfers between devices, local(): lax.ppermute(a, 'replica', [(r, r ^ bit) for r in range(n_rep)])  11.9 us
    ppermute x8, starting transfers between devices, local(): lax.ppermute(a, 'fsdp', [(f, (f // 2 + s) % chips * 2 + f % 2) for f in r...  8.85 us
    ppermute x6, starting transfers between devices, local(): lax.ppermute(a, 'fsdp', [((f // 2 + s) % chips * 2 + f % 2, f) for f in r...  8.05 us
    ppermute x8, waiting for transfers between devices, local(): lax.ppermute(a, 'fsdp', [(f, (f // 2 + s) % chips * 2 + f % 2) for f in r...  7.82 us
    ppermute x15, starting transfers between devices, local(): to_partner = lambda a: lax.ppermute(a, 'fsdp', partner)  3.04 us
  transfers between devices with their start and end apart: 36, of which 11 were waited for; matrix products, arithmetic and copies ran while one was open for 0% of the time, Pallas kernels for 46%

profile of v13, /device:TPU:0, one launch (start us, length us, event | category | flops | bytes accessed | tf_op | source)
XLA Modules:
  0.0 110.3 jit_solution(12919692558334636918)
XLA Ops:
  1.2 1.6 %copy-done.1 = f32[1,2,1024,256]{3,2,1,0:T(8,128)S(1)} copy-done((f32[1,2,1024,256]{3,2,1,0:T(8,128)S(1)}, f32[1,2,1024,256]{3,2,1,0:T(8,128)}, u32[]{:S(2)}) %copy-start.1) | copy-done | bytes 2097176
  3.1 3.0 %collective-permute-start.8 = (bf16[1024,256]{1,0:T(8,128)(2,1)S(1)}, bf16[1024,256]{1,0:T(8,128)(2,1)S(1)}, u32[]{:S(2)}, u32[]{:S(2)}) collective-permute-start(bf16[1024,256]{1,0:T(8,128)(2,1)S(1)} %get-tuple-element.72.refs_4_.refs_1_), channel_id=1, source_target_pairs={{2,0},{3,1},{0,2},{1,3},{6,4},{7,5},{4,6},{5,7},{10,8},{11,9},{8,1... | collective-permute-start | bytes 1572872 | tf_op jit(solution)/shard_map/ppermute | solution.py:507
  8.4 1.6 %collective-permute-start.2 = (bf16[256,256]{1,0:T(8,128)(2,1)S(1)}, bf16[256,256]{1,0:T(8,128)(2,1)S(1)}, u32[]{:S(2)}, u32[]{:S(2)}) collective-permute-start(bf16[256,256]{1,0:T(8,128)(2,1)S(1)} %get-tuple-element.75), channel_id=1, source_target_pairs={{0,8},{4,12},{8,0},{12,4},{16,24},{20,28},{24,16},{28,20},{1,9},{5... | collective-permute-start | bytes 393224 | tf_op jit(solution)/shard_map/ppermute | solution.py:511
  9.9 2.6 %collective-permute-start.3 = (bf16[256,256]{1,0:T(8,128)(2,1)S(1)}, bf16[256,256]{1,0:T(8,128)(2,1)S(1)}, u32[]{:S(2)}, u32[]{:S(2)}) collective-permute-start(bf16[256,256]{1,0:T(8,128)(2,1)S(1)} %get-tuple-element.76), channel_id=1, source_target_pairs={{0,12},{4,8},{8,4},{12,0},{16,28},{20,24},{24,20},{28,16},{1,13},{... | collective-permute-start | bytes 393224 | tf_op jit(solution)/shard_map/ppermute | solution.py:511
  15.2 2.9 %stage_tokens.1 = (bf16[512,4096]{1,0:T(8,128)(2,1)S(1)}, bf16[2048,512]{1,0:T(8,128)(2,1)S(1)}) custom-call(s32[5]{0:T(128)S(1)} %stack.23.refs_0_.refs_1_, bf16[512,4096]{1,0:T(8,128)(2,1)} %collective-permute-done.refs_1_), custom_call_target="tpu_custom_call" | custom-call | bytes 10485760 | tf_op jit(solution)/shard_map/stage_tokens/pallas_call | solution.py:60
  18.2 1.8 %forward_encoder.4.refs_2_.refs_1_ = f32[2,512,256]{2,1,0:T(8,128)S(1)} custom-call(s32[5]{0:T(128)S(1)} %stack.23.refs_0_.refs_1_, bf16[1024,256]{1,0:T(8,128)(2,1)S(1)} %get-tuple-element.72.refs_4_.refs_1_, bf16[1024,256]{1,0:T(8,128)(2,1)S(1)} %collective-permute-done.7.refs_2_, bf16[512,4096]{1,0:T(8,128)(2,1)S(1)} %copy-done, ...), custom_call_target="tpu_custom_call" | custom-call | bytes 10485760 | tf_op jit(solution)/shard_map/forward_encoder/pallas_call | solution.py:60
  23.4 2.4 %hidden_units.2 = (bf16[2,512,256]{2,1,0:T(8,128)(2,1)S(1)}, f32[2,512,256]{2,1,0:T(8,128)S(1)}, bf16[2,512,256]{2,1,0:T(8,128)(2,1)S(1)}, bf16[256,256]{1,0:T(8,128)(2,1)S(1)}, bf16[256,256]{1,0:T(8,128)(2,1)S(1)}) custom-call(s32[5]{0:T(128)S(1)} %stack.23.refs_0_.refs_1_, f32[2,512,256]{2,1,0:T(8,128)S(1)} %forward_encoder.5.refs_1_, ...), custom_call_target="tpu_custom_call" | custom-call | bytes 12333056 | tf_op jit(solution)/shard_map/hidden_units/pallas_call | solution.py:60
  29.9 1.8 %collective-permute-start.18 = (bf16[1024,256]{1,0:T(8,128)(2,1)S(1)}, bf16[1024,256]{1,0:T(8,128)(2,1)S(1)}, u32[]{:S(2)}, u32[]{:S(2)}) collective-permute-start(bf16[1024,256]{1,0:T(8,128)(2,1)S(1)} %decoder_grad.7.refs_8_.refs_3_), channel_id=1, source_target_pairs={{0,2},{1,3},{2,0},{3,1},{4,6},{5,7},{6,4},{7,5},{8,10},{9,11},{10,... | collective-permute-start | bytes 1572872 | tf_op jit(solution)/shard_map/ppermute | solution.py:509
  32.2 2.6 %collective-permute-start.4 = (bf16[256,256]{1,0:T(8,128)(2,1)S(1)}, bf16[256,256]{1,0:T(8,128)(2,1)S(1)}, u32[]{:S(2)}, u32[]{:S(2)}) collective-permute-start(bf16[256,256]{1,0:T(8,128)(2,1)S(1)} %add_quarters.2.refs_3_.refs_1_), channel_id=1, source_target_pairs={{0,16},{4,20},{8,24},{12,28},{16,0},{20,4},{24,8},{28,12},{1,17},{... | collective-permute-start | bytes 393224 | tf_op jit(solution)/shard_map/ppermute | solution.py:511
  34.8 3.0 %forward_decoder.2 = (f32[2,512,256]{2,1,0:T(8,128)S(1)}, f32[256,256]{1,0:T(8,128)S(1)}) custom-call(s32[5]{0:T(128)S(1)} %stack.23.refs_0_.refs_1_, bf16[1024,256]{1,0:T(8,128)(2,1)S(1)} %get-tuple-element.77.refs_1_, bf16[1024,256]{1,0:T(8,128)(2,1)S(1)} %collective-permute-done.5.refs_2_, bf16[384,256]{1,0:T(8,128)(2,1)S(1)} %get-tuple-element.83.refs_5_.refs_3_, ...), custom_call_target="tpu_custom_call" | custom-call | bytes 11272192 | tf_op jit(solution)/shard_map/forward_decoder/pallas_call | solution.py:60
  37.8 2.0 %slope_pre.2.refs_2_ = bf16[2,512,256]{2,1,0:T(8,128)(2,1)S(1)} custom-call(s32[5]{0:T(128)S(1)} %stack.23.refs_0_.refs_1_, f32[2,512,256]{2,1,0:T(8,128)S(1)} %get-tuple-element.88.refs_1_, f32[256,256]{1,0:T(8,128)S(1)} %get-tuple-element.89.refs_2_, bf16[2,512,256]{2,1,0:T(8,128)(2,1)S(1)} %get-tuple-element.90.refs_3_, ...), custom_call_target="tpu_custom_call" | custom-call | bytes 12320768 | tf_op jit(solution)/shard_map/slope_pre/pallas_call | solution.py:60
  42.4 1.6 %collective-permute-start.15 = (bf16[256,256]{1,0:T(8,128)(2,1)S(1)}, bf16[256,256]{1,0:T(8,128)(2,1)S(1)}, u32[]{:S(2)}, u32[]{:S(2)}) collective-permute-start(bf16[256,256]{1,0:T(8,128)(2,1)S(1)} %add_quarters.3.refs_8_.refs_4_), channel_id=1, source_target_pairs={{0,4},{4,0},{8,12},{12,8},{16,20},{20,16},{24,28},{28,24},{1,5},{5... | collective-permute-start | bytes 393224 | tf_op jit(solution)/shard_map/ppermute | solution.py:511
  60.3 3.1 %outer_step.1 = (f32[2,1024,256]{2,1,0:T(8,128)}, f32[2,1024,256]{2,1,0:T(8,128)}, f32[8,128]{1,0:T(8,128)S(1)}) custom-call(s32[5]{0:T(128)S(1)} %stack.23.refs_0_.refs_1_, s32[8]{0:T(128)S(1)} %copy-done.7, f32[2,1024,256]{2,1,0:T(8,128)S(1)} %copy-done.5, f32[2,1024,256]{2,1,0:T(8,128)S(1)} %copy-done.6, ...), custom_call_target="tpu_custom_call" | custom-call | bytes 8916992 | tf_op jit(solution)/shard_map/outer_step/pallas_call | solution.py:60
  63.4 1.8 %forward_encoder.6.refs_1_ = f32[2,512,256]{2,1,0:T(8,128)S(1)} custom-call(s32[5]{0:T(128)S(1)} %stack.23.refs_0_.refs_1_, bf16[1024,256]{1,0:T(8,128)(2,1)S(1)} %get-tuple-element.94.refs_5_.refs_3_.refs_1_, bf16[1024,256]{1,0:T(8,128)(2,1)S(1)} %collective-permute-done.24.refs_2_, bf16[512,4096]{1,0:T(8,128)(2,1)S(1)} %copy-done, ...), custom_call_target="tpu_custom_call" | custom-call | bytes 10485760 | tf_op jit(solution)/shard_map/forward_encoder/pallas_call | solution.py:60
  65.1 5.8 %collective-permute-done.25.refs_0_ = bf16[1024,256]{1,0:T(8,128)(2,1)S(1)} collective-permute-done((bf16[1024,256]{1,0:T(8,128)(2,1)S(1)}, bf16[1024,256]{1,0:T(8,128)(2,1)S(1)}, u32[]{:S(2)}, u32[]{:S(2)}) %collective-permute-start.25) | collective-permute-done | bytes 524320 | tf_op jit(solution)/shard_map/ppermute | solution.py:507
  73.8 2.4 %hidden_units.3 = (bf16[2,512,256]{2,1,0:T(8,128)(2,1)S(1)}, f32[2,512,256]{2,1,0:T(8,128)S(1)}, bf16[2,512,256]{2,1,0:T(8,128)(2,1)S(1)}, bf16[256,256]{1,0:T(8,128)(2,1)S(1)}, bf16[256,256]{1,0:T(8,128)(2,1)S(1)}) custom-call(s32[5]{0:T(128)S(1)} %stack.23.refs_0_.refs_1_, f32[2,512,256]{2,1,0:T(8,128)S(1)} %forward_encoder.7.refs_1_, ...), custom_call_target="tpu_custom_call" | custom-call | bytes 12324864 | tf_op jit(solution)/shard_map/hidden_units/pallas_call | solution.py:60
  76.1 3.2 %collective-permute-done.23.refs_0_ = bf16[768,256]{1,0:T(8,128)(2,1)S(1)} collective-permute-done((bf16[768,256]{1,0:T(8,128)(2,1)S(1)}, bf16[768,256]{1,0:T(8,128)(2,1)S(1)}, u32[]{:S(2)}, u32[]{:S(2)}) %collective-permute-start.23) | collective-permute-done | bytes 393248 | tf_op jit(solution)/shard_map/ppermute | solution.py:507
  83.6 3.0 %forward_decoder.3 = (f32[2,512,256]{2,1,0:T(8,128)S(1)}, f32[256,256]{1,0:T(8,128)S(1)}) custom-call(s32[5]{0:T(128)S(1)} %stack.23.refs_0_.refs_1_, bf16[1024,256]{1,0:T(8,128)(2,1)S(1)} %get-tuple-element.96.refs_8_.refs_1_, bf16[1024,256]{1,0:T(8,128)(2,1)S(1)} %collective-permute-done.22.refs_2_, ...), custom_call_target="tpu_custom_call" | custom-call | bytes 11272192 | tf_op jit(solution)/shard_map/forward_decoder/pallas_call | solution.py:60
  86.6 2.0 %slope_pre.3.refs_2_ = bf16[2,512,256]{2,1,0:T(8,128)(2,1)S(1)} custom-call(s32[5]{0:T(128)S(1)} %stack.23.refs_0_.refs_1_, f32[2,512,256]{2,1,0:T(8,128)S(1)} %get-tuple-element.107.refs_1_, f32[256,256]{1,0:T(8,128)S(1)} %get-tuple-element.108.refs_2_, bf16[2,512,256]{2,1,0:T(8,128)(2,1)S(1)} %get-tuple-element.109.refs_3_, ...), custom_call_target="tpu_custom_call" | custom-call | bytes 12320768 | tf_op jit(solution)/shard_map/slope_pre/pallas_call | solution.py:60
  90.2 6.8 %collective-permute-done.32.refs_7_ = bf16[1024,256]{1,0:T(8,128)(2,1)S(1)} collective-permute-done((bf16[1024,256]{1,0:T(8,128)(2,1)S(1)}, bf16[1024,256]{1,0:T(8,128)(2,1)S(1)}, u32[]{:S(2)}, u32[]{:S(2)}) %collective-permute-start.32) | collective-permute-done | bytes 524320 | tf_op jit(solution)/shard_map/ppermute | solution.py:509
  99.3 3.0 %adam_rows.12 = (f32[8,128]{1,0:T(8,128)S(1)}, f32[1,2,1024,256]{3,2,1,0:T(8,128)}, f32[1,2,1024,256]{3,2,1,0:T(8,128)}, f32[1,2,1024,256]{3,2,1,0:T(8,128)}) custom-call(s32[8]{0:T(128)S(1)} %copy-done.7, f32[1024,256]{1,0:T(8,128)S(1)} %decoder_grad.11.refs_1_.refs_3_, f32[1,1,1024,256]{3,2,1,0:T(8,128)S(1)} %get-tuple-element.95.refs_2_, ...), custom_call_target="tpu_custom_call" | custom-call | bytes 11538432 | tf_op jit(solution)/shard_map/adam_rows/pallas_call | solution.py:60
  104.8 2.0 %adam_rows.13 = (f32[1,2,1024,256]{3,2,1,0:T(8,128)}, f32[1,2,1024,256]{3,2,1,0:T(8,128)}, f32[1,2,1024,256]{3,2,1,0:T(8,128)}) custom-call(s32[8]{0:T(128)S(1)} %copy-done.7, f32[512,256]{1,0:T(8,128)S(1)} %encoder_grad.19.refs_3_.refs_1_, ...), custom_call_target="tpu_custom_call", output_to_operand_aliasing={{0}: (7, {}), {1}: (8, {}), {2}: (9, {})} | custom-call | bytes 15466496 | tf_op jit(solution)/shard_map/adam_rows/pallas_call | solution.py:60
  106.8 1.6 %adam_rows.14 = (f32[1,2,1024,256]{3,2,1,0:T(8,128)}, f32[1,2,1024,256]{3,2,1,0:T(8,128)}, f32[1,2,1024,256]{3,2,1,0:T(8,128)}) custom-call(s32[8]{0:T(128)S(1)} %copy-done.7, f32[256,256]{1,0:T(8,128)S(1)} %encoder_grad.20.refs_3_.refs_1_, ...), custom_call_target="tpu_custom_call", output_to_operand_aliasing={{0}: (7, {}), {1}: (8, {}), {2}: (9, {})} | custom-call | bytes 14024704 | tf_op jit(solution)/shard_map/adam_rows/pallas_call | solution.py:60
  108.7 1.6 %adam_rows.15 = (f32[1,2,1024,256]{3,2,1,0:T(8,128)}, f32[1,2,1024,256]{3,2,1,0:T(8,128)}, f32[1,2,1024,256]{3,2,1,0:T(8,128)}) custom-call(s32[8]{0:T(128)S(1)} %copy-done.7, f32[256,256]{1,0:T(8,128)S(1)} %encoder_grad.21.refs_3_.refs_1_, ...), custom_call_target="tpu_custom_call", output_to_operand_aliasing={{0}: (7, {}), {1}: (8, {}), {2}: (9, {})} | custom-call | bytes 14024704 | tf_op jit(solution)/shard_map/adam_rows/pallas_call | solution.py:60
  (119 shorter events, 46.3 us)
Async XLA Ops:
  0.6 11.9 %collective-permute-start = (bf16[512,4096]{1,0:T(8,128)(2,1)}, bf16[512,4096]{1,0:T(8,128)(2,1)}, u32[]{:S(2)}, u32[]{:S(2)}) collective-permute-start(bf16[512,4096]{1,0:T(8,128)(2,1)} %refs_8_.3), channel_id=1, source_target_pairs={{0,1},{1,0},{2,3},{3,2},{4,5},{5,4},{6,7},{7,6},{8,9},{9,8},{10,11... | collective-permute-start | bytes 12582920 | tf_op jit(solution)/shard_map/ppermute | solution.py:506
  3.0 7.0 %collective-permute-start.7 = (bf16[1024,256]{1,0:T(8,128)(2,1)S(1)}, bf16[1024,256]{1,0:T(8,128)(2,1)S(1)}, u32[]{:S(2)}, u32[]{:S(2)}) collective-permute-start(bf16[1024,256]{1,0:T(8,128)(2,1)S(1)} %get-tuple-element.72.refs_4_.refs_1_), channel_id=1, source_target_pairs={{0,1},{1,0},{2,3},{3,2},{4,5},{5,4},{6,7},{7,6},{8,9},{9,8},{10,11... | collective-permute-start | bytes 1572872 | tf_op jit(solution)/shard_map/ppermute | solution.py:506
  3.1 17.5 %collective-permute-start.8 = (bf16[1024,256]{1,0:T(8,128)(2,1)S(1)}, bf16[1024,256]{1,0:T(8,128)(2,1)S(1)}, u32[]{:S(2)}, u32[]{:S(2)}) collective-permute-start(bf16[1024,256]{1,0:T(8,128)(2,1)S(1)} %get-tuple-element.72.refs_4_.refs_1_), channel_id=1, source_target_pairs={{2,0},{3,1},{0,2},{1,3},{6,4},{7,5},{4,6},{5,7},{10,8},{11,9},{8,1... | collective-permute-start | bytes 1572872 | tf_op jit(solution)/shard_map/ppermute | solution.py:507
  6.8 13.2 %collective-permute-start.1 = (bf16[256,256]{1,0:T(8,128)(2,1)S(1)}, bf16[256,256]{1,0:T(8,128)(2,1)S(1)}, u32[]{:S(2)}, u32[]{:S(2)}) collective-permute-start(bf16[256,256]{1,0:T(8,128)(2,1)S(1)} %get-tuple-element.74), channel_id=1, source_target_pairs={{0,4},{4,0},{8,12},{12,8},{16,20},{20,16},{24,28},{28,24},{1,5},{5... | collective-permute-start | bytes 393224 | tf_op jit(solution)/shard_map/ppermute | solution.py:511
  8.4 11.6 %collective-permute-start.2 = (bf16[256,256]{1,0:T(8,128)(2,1)S(1)}, bf16[256,256]{1,0:T(8,128)(2,1)S(1)}, u32[]{:S(2)}, u32[]{:S(2)}) collective-permute-start(bf16[256,256]{1,0:T(8,128)(2,1)S(1)} %get-tuple-element.75), channel_id=1, source_target_pairs={{0,8},{4,12},{8,0},{12,4},{16,24},{20,28},{24,16},{28,20},{1,9},{5... | collective-permute-start | bytes 393224 | tf_op jit(solution)/shard_map/ppermute | solution.py:511
  9.9 10.1 %collective-permute-start.3 = (bf16[256,256]{1,0:T(8,128)(2,1)S(1)}, bf16[256,256]{1,0:T(8,128)(2,1)S(1)}, u32[]{:S(2)}, u32[]{:S(2)}) collective-permute-start(bf16[256,256]{1,0:T(8,128)(2,1)S(1)} %get-tuple-element.76), channel_id=1, source_target_pairs={{0,12},{4,8},{8,4},{12,0},{16,28},{20,24},{24,20},{28,16},{1,13},{... | collective-permute-start | bytes 393224 | tf_op jit(solution)/shard_map/ppermute | solution.py:511
  12.6 14.6 %collective-permute-start.6 = (bf16[768,256]{1,0:T(8,128)(2,1)S(1)}, bf16[768,256]{1,0:T(8,128)(2,1)S(1)}, u32[]{:S(2)}, u32[]{:S(2)}) collective-permute-start(bf16[768,256]{1,0:T(8,128)(2,1)S(1)} %get-tuple-element.78.refs_5_), channel_id=1, source_target_pairs={{2,0},{3,1},{0,2},{1,3},{6,4},{7,5},{4,6},{5,7},{10,8},{11,9},{8,1... | collective-permute-start | bytes 1179656 | tf_op jit(solution)/shard_map/ppermute | solution.py:507
  21.3 10.9 %collective-permute-start.5 = (bf16[1024,256]{1,0:T(8,128)(2,1)S(1)}, bf16[1024,256]{1,0:T(8,128)(2,1)S(1)}, u32[]{:S(2)}, u32[]{:S(2)}) collective-permute-start(bf16[1024,256]{1,0:T(8,128)(2,1)S(1)} %get-tuple-element.77.refs_1_), channel_id=1, source_target_pairs={{0,1},{1,0},{2,3},{3,2},{4,5},{5,4},{6,7},{7,6},{8,9},{9,8},{10,11... | collective-permute-start | bytes 1572872 | tf_op jit(solution)/shard_map/ppermute | solution.py:506
  21.4 8.1 %collective-permute-start.11 = (bf16[256,256]{1,0:T(8,128)(2,1)S(1)}, bf16[256,256]{1,0:T(8,128)(2,1)S(1)}, u32[]{:S(2)}, u32[]{:S(2)}) collective-permute-start(bf16[256,256]{1,0:T(8,128)(2,1)S(1)} %get-tuple-element.85.refs_6_), channel_id=1, source_target_pairs={{2,0},{3,1},{0,2},{1,3},{6,4},{7,5},{4,6},{5,7},{10,8},{11,9},{8,1... | collective-permute-start | bytes 393224 | tf_op jit(solution)/shard_map/ppermute | solution.py:507
  29.9 16.1 %collective-permute-start.18 = (bf16[1024,256]{1,0:T(8,128)(2,1)S(1)}, bf16[1024,256]{1,0:T(8,128)(2,1)S(1)}, u32[]{:S(2)}, u32[]{:S(2)}) collective-permute-start(bf16[1024,256]{1,0:T(8,128)(2,1)S(1)} %decoder_grad.7.refs_8_.refs_3_), channel_id=1, source_target_pairs={{0,2},{1,3},{2,0},{3,1},{4,6},{5,7},{6,4},{7,5},{8,10},{9,11},{10,... | collective-permute-start | bytes 1572872 | tf_op jit(solution)/shard_map/ppermute | solution.py:509
  31.7 6.1 %collective-permute-start.13 = (bf16[384,256]{1,0:T(8,128)(2,1)S(1)}, bf16[384,256]{1,0:T(8,128)(2,1)S(1)}, u32[]{:S(2)}, u32[]{:S(2)}) collective-permute-start(bf16[384,256]{1,0:T(8,128)(2,1)S(1)} %get-tuple-element.84.refs_6_.refs_4_), channel_id=1, source_target_pairs={{0,1},{1,0},{2,3},{3,2},{4,5},{5,4},{6,7},{7,6},{8,9},{9,8},{10,11... | collective-permute-start | bytes 589832 | tf_op jit(solution)/shard_map/ppermute | solution.py:506
  32.2 9.6 %collective-permute-start.4 = (bf16[256,256]{1,0:T(8,128)(2,1)S(1)}, bf16[256,256]{1,0:T(8,128)(2,1)S(1)}, u32[]{:S(2)}, u32[]{:S(2)}) collective-permute-start(bf16[256,256]{1,0:T(8,128)(2,1)S(1)} %add_quarters.2.refs_3_.refs_1_), channel_id=1, source_target_pairs={{0,16},{4,20},{8,24},{12,28},{16,0},{20,4},{24,8},{28,12},{1,17},{... | collective-permute-start | bytes 393224 | tf_op jit(solution)/shard_map/ppermute | solution.py:511
  40.3 12.2 %collective-permute-start.21 = (bf16[512,256]{1,0:T(8,128)(2,1)S(1)}, bf16[512,256]{1,0:T(8,128)(2,1)S(1)}, u32[]{:S(2)}, u32[]{:S(2)}) collective-permute-start(bf16[512,256]{1,0:T(8,128)(2,1)S(1)} %encoder_grad.12.refs_3_), channel_id=1, source_target_pairs={{0,2},{1,3},{2,0},{3,1},{4,6},{5,7},{6,4},{7,5},{8,10},{9,11},{10,... | collective-permute-start | bytes 786440 | tf_op jit(solution)/shard_map/ppermute | solution.py:509
  42.4 7.1 %collective-permute-start.15 = (bf16[256,256]{1,0:T(8,128)(2,1)S(1)}, bf16[256,256]{1,0:T(8,128)(2,1)S(1)}, u32[]{:S(2)}, u32[]{:S(2)}) collective-permute-start(bf16[256,256]{1,0:T(8,128)(2,1)S(1)} %add_quarters.3.refs_8_.refs_4_), channel_id=1, source_target_pairs={{0,4},{4,0},{8,12},{12,8},{16,20},{20,16},{24,28},{28,24},{1,5},{5... | collective-permute-start | bytes 393224 | tf_op jit(solution)/shard_map/ppermute | solution.py:511
  44.0 7.1 %collective-permute-start.16 = (bf16[256,256]{1,0:T(8,128)(2,1)S(1)}, bf16[256,256]{1,0:T(8,128)(2,1)S(1)}, u32[]{:S(2)}, u32[]{:S(2)}) collective-permute-start(bf16[256,256]{1,0:T(8,128)(2,1)S(1)} %add_quarters.3.refs_8_.refs_4_), channel_id=1, source_target_pairs={{0,8},{4,12},{8,0},{12,4},{16,24},{20,28},{24,16},{28,20},{1,9},{5... | collective-permute-start | bytes 393224 | tf_op jit(solution)/shard_map/ppermute | solution.py:511
  44.6 7.1 %collective-permute-start.17 = (bf16[256,256]{1,0:T(8,128)(2,1)S(1)}, bf16[256,256]{1,0:T(8,128)(2,1)S(1)}, u32[]{:S(2)}, u32[]{:S(2)}) collective-permute-start(bf16[256,256]{1,0:T(8,128)(2,1)S(1)} %add_quarters.3.refs_8_.refs_4_), channel_id=1, source_target_pairs={{0,12},{4,8},{8,4},{12,0},{16,28},{20,24},{24,20},{28,16},{1,13},{... | collective-permute-start | bytes 393224 | tf_op jit(solution)/shard_map/ppermute | solution.py:511
  56.0 7.3 %collective-permute-start.24 = (bf16[1024,256]{1,0:T(8,128)(2,1)S(1)}, bf16[1024,256]{1,0:T(8,128)(2,1)S(1)}, u32[]{:S(2)}, u32[]{:S(2)}) collective-permute-start(bf16[1024,256]{1,0:T(8,128)(2,1)S(1)} %get-tuple-element.94.refs_5_.refs_3_.refs_1_), channel_id=1, source_target_pairs={{0,1},{1,0},{2,3},{3,2},{4,5},{5,4},{6,7},{7,6},{8,9},{9,8},{10,11... | collective-permute-start | bytes 1572872 | tf_op jit(solution)/shard_map/ppermute | solution.py:506
  56.1 14.8 %collective-permute-start.25 = (bf16[1024,256]{1,0:T(8,128)(2,1)S(1)}, bf16[1024,256]{1,0:T(8,128)(2,1)S(1)}, u32[]{:S(2)}, u32[]{:S(2)}) collective-permute-start(bf16[1024,256]{1,0:T(8,128)(2,1)S(1)} %get-tuple-element.94.refs_5_.refs_3_.refs_1_), channel_id=1, source_target_pairs={{2,0},{3,1},{0,2},{1,3},{6,4},{7,5},{4,6},{5,7},{10,8},{11,9},{8,1... | collective-permute-start | bytes 1572872 | tf_op jit(solution)/shard_map/ppermute | solution.py:507
  59.1 20.2 %collective-permute-start.23 = (bf16[768,256]{1,0:T(8,128)(2,1)S(1)}, bf16[768,256]{1,0:T(8,128)(2,1)S(1)}, u32[]{:S(2)}, u32[]{:S(2)}) collective-permute-start(bf16[768,256]{1,0:T(8,128)(2,1)S(1)} %get-tuple-element.97.refs_5_), channel_id=1, source_target_pairs={{2,0},{3,1},{0,2},{1,3},{6,4},{7,5},{4,6},{5,7},{10,8},{11,9},{8,1... | collective-permute-start | bytes 1179656 | tf_op jit(solution)/shard_map/ppermute | solution.py:507
  71.5 12.1 %collective-permute-start.22 = (bf16[1024,256]{1,0:T(8,128)(2,1)S(1)}, bf16[1024,256]{1,0:T(8,128)(2,1)S(1)}, u32[]{:S(2)}, u32[]{:S(2)}) collective-permute-start(bf16[1024,256]{1,0:T(8,128)(2,1)S(1)} %get-tuple-element.96.refs_8_.refs_1_), channel_id=1, source_target_pairs={{0,1},{1,0},{2,3},{3,2},{4,5},{5,4},{6,7},{7,6},{8,9},{9,8},{10,11... | collective-permute-start | bytes 1572872 | tf_op jit(solution)/shard_map/ppermute | solution.py:506
  71.6 10.1 %collective-permute-start.28 = (bf16[256,256]{1,0:T(8,128)(2,1)S(1)}, bf16[256,256]{1,0:T(8,128)(2,1)S(1)}, u32[]{:S(2)}, u32[]{:S(2)}) collective-permute-start(bf16[256,256]{1,0:T(8,128)(2,1)S(1)} %get-tuple-element.104.refs_6_), channel_id=1, source_target_pairs={{2,0},{3,1},{0,2},{1,3},{6,4},{7,5},{4,6},{5,7},{10,8},{11,9},{8,1... | collective-permute-start | bytes 393224 | tf_op jit(solution)/shard_map/ppermute | solution.py:507
  82.1 14.9 %collective-permute-start.32 = (bf16[1024,256]{1,0:T(8,128)(2,1)S(1)}, bf16[1024,256]{1,0:T(8,128)(2,1)S(1)}, u32[]{:S(2)}, u32[]{:S(2)}) collective-permute-start(bf16[1024,256]{1,0:T(8,128)(2,1)S(1)} %decoder_grad.10.refs_8_.refs_3_), channel_id=1, source_target_pairs={{0,2},{1,3},{2,0},{3,1},{4,6},{5,7},{6,4},{7,5},{8,10},{9,11},{10,... | collective-permute-start | bytes 1572872 | tf_op jit(solution)/shard_map/ppermute | solution.py:509
  89.0 15.8 %collective-permute-start.35 = (bf16[512,256]{1,0:T(8,128)(2,1)S(1)}, bf16[512,256]{1,0:T(8,128)(2,1)S(1)}, u32[]{:S(2)}, u32[]{:S(2)}) collective-permute-start(bf16[512,256]{1,0:T(8,128)(2,1)S(1)} %encoder_grad.18.refs_8_), channel_id=1, source_target_pairs={{0,2},{1,3},{2,0},{3,1},{4,6},{5,7},{6,4},{7,5},{8,10},{9,11},{10,... | collective-permute-start | bytes 786440 | tf_op jit(solution)/shard_map/ppermute | solution.py:509
  98.3 8.6 %collective-permute-start.34 = (bf16[256,256]{1,0:T(8,128)(2,1)S(1)}, bf16[256,256]{1,0:T(8,128)(2,1)S(1)}, u32[]{:S(2)}, u32[]{:S(2)}) collective-permute-start(bf16[256,256]{1,0:T(8,128)(2,1)S(1)} %encoder_grad.23), channel_id=1, source_target_pairs={{0,2},{1,3},{2,0},{3,1},{4,6},{5,7},{6,4},{7,5},{8,10},{9,11},{10,... | collective-permute-start | bytes 393224 | tf_op jit(solution)/shard_map/ppermute | solution.py:509
  (21 other events, 83.2 us)

commit v14 on v13

--- a/solution.py
+++ b/solution.py
@@ -582,30 +582,32 @@
             *more, after=after)
         prev = None
         mine = {}
+        own_dec = lambda after: dec_grad(0, rows, dec_parts, [], False, f32, after)
         for n, key in enumerate(blocks[1:]):
+            hold = back if n == 1 else []
             for s in others:
-                sent.append(enc_grad(s, *key[1:], bf16, sent[-1:]))
+                sent.append(enc_grad(s, *key[1:], bf16, sent[-1:] + hold))
                 got[key].append(give(sent[-1], s))
-            if n == 0:
-                if step == 0:
-                    bit = 4
-                    while bit < n_rep:
-                        own = outer_add(plan, [own, across(own, bit)], 2 * bit == n_rep, sent[-1:])
-                        bit *= 2
-                    sent.append(own)
-                mine[blocks[0]] = dec_grad(0, rows, dec_parts, back, False, f32, sent[-1:])
-                sent.append(mine[blocks[0]])
-            if n == len(blocks) - 3 or len(blocks) == 2:
-                if last:
-                    token, *prev = adam(blocks[0], None)
-                    sent.append(token)
+            if n == 0 and step == 0:
+                bit = 4
+                while bit < n_rep:
+                    own = outer_add(plan, [own, across(own, bit)], 2 * bit == n_rep, sent[-1:])
+                    bit *= 2
+                sent.append(own)
+            if n == (0 if last else len(blocks) - 2):
                 for other in blocks[1:]:
                     mine[other] = enc_grad(0, *other[1:], f32, sent[-1:])
                     sent.append(mine[other])
+                if last:
+                    mine[blocks[0]] = own_dec(sent[-1:])
+                    sent.append(mine[blocks[0]])
+        got[blocks[0]] = back
+        if last:
+            token, *prev = adam(blocks[0], None, after=sent[-1:])
 
         if not last:
             quarters = [own] + [across(own, m) for m in range(1, 4)]
-            new_anc = outer_anchor(pos, plan, anchor, momentum, quarters, [mine[blocks[0]]])
+            new_anc = outer_anchor(pos, plan, anchor, momentum, quarters, sent[-1:])
         new_state, lows = {}, []
         if last:
             for key in blocks[1:]:
@@ -615,6 +617,7 @@
                 enc, *new_state[key] = adam(key, None, lows)
                 lows = [enc]
             enc_parts = [enc]
+            mine[blocks[0]] = own_dec([enc])
             new_state[blocks[0]] = adam(blocks[0], None, after=[enc])
             dec, *dec_parts = mix_rows(plan, new_anc, 1, new_state[blocks[0]][0], sizes, [enc])
             anchor_out, momentum_out, token = outer_end(pos, plan, anchor, momentum, quarters, [dec])

time: 110 us -> 109 us (level)
  waiting for transfers between devices: 22.9 us -> 20.6 us
    ppermute x8, waiting for transfers between devices: 7.82 us -> 4.94 us  [local(): lax.ppermute(a, 'fsdp', [(f, (f // 2 + s) % chips * 2 + f % 2) for f in r...]
    ppermute x7, waiting for transfers between devices: 1.64 us -> 3.26 us  [local(): lax.ppermute(a, 'replica', [(r, r ^ bit) for r in range(n_rep)])]
  transfers between devices with their start and end apart: 36 -> 36, of which waited for: 11 -> 11; matrix products, arithmetic and copies ran while one was open for 0% -> 0% of each run, Pallas kernels for 46% -> 47%
where the time goes in v14:
time: 109 us; the launch traced here: 108 us
  Pallas kernels  53 us (49%)
  starting transfers between devices  31.4 us (29%)
  waiting for transfers between devices  20.6 us (19%)
  local copies, waits for them, and re-layouts  2.26 us (2%)
  between operations  1.15 us (1%)
    pallas_call x52, Pallas kernels, call(): pl.pallas_call(run, name=name, out_shape=[o for o, _ in outs], grid_spec=...  53 us
    ppermute x6, waiting for transfers between devices, local(): lax.ppermute(a, 'fsdp', [((f // 2 + s) % chips * 2 + f % 2, f) for f in r...  12.4 us
    ppermute x7, starting transfers between devices, local(): lax.ppermute(a, 'replica', [(r, r ^ bit) for r in range(n_rep)])  11.9 us
    ppermute x8, starting transfers between devices, local(): lax.ppermute(a, 'fsdp', [(f, (f // 2 + s) % chips * 2 + f % 2) for f in r...  8.45 us
    ppermute x6, starting transfers between devices, local(): lax.ppermute(a, 'fsdp', [((f // 2 + s) % chips * 2 + f % 2, f) for f in r...  8.01 us
    ppermute x8, waiting for transfers between devices, local(): lax.ppermute(a, 'fsdp', [(f, (f // 2 + s) % chips * 2 + f % 2) for f in r...  4.94 us
    ppermute x7, waiting for transfers between devices, local(): lax.ppermute(a, 'replica', [(r, r ^ bit) for r in range(n_rep)])  3.26 us
    ppermute x15, starting transfers between devices, local(): to_partner = lambda a: lax.ppermute(a, 'fsdp', partner)  3.04 us
  transfers between devices with their start and end apart: 36, of which 11 were waited for; matrix products, arithmetic and copies ran while one was open for 0% of the time, Pallas kernels for 47%

profile of v14, /device:TPU:0, one launch (start us, length us, event | category | flops | bytes accessed | tf_op | source)
XLA Modules:
  0.0 108.5 jit_solution(15995280742253108094)
XLA Ops:
  1.2 1.6 %copy-done.1 = f32[1,2,1024,256]{3,2,1,0:T(8,128)S(1)} copy-done((f32[1,2,1024,256]{3,2,1,0:T(8,128)S(1)}, f32[1,2,1024,256]{3,2,1,0:T(8,128)}, u32[]{:S(2)}) %copy-start.1) | copy-done | bytes 2097176
  3.1 3.0 %collective-permute-start.8 = (bf16[1024,256]{1,0:T(8,128)(2,1)S(1)}, bf16[1024,256]{1,0:T(8,128)(2,1)S(1)}, u32[]{:S(2)}, u32[]{:S(2)}) collective-permute-start(bf16[1024,256]{1,0:T(8,128)(2,1)S(1)} %get-tuple-element.71.refs_4_.refs_1_), channel_id=1, source_target_pairs={{2,0},{3,1},{0,2},{1,3},{6,4},{7,5},{4,6},{5,7},{10,8},{11,9},{8,1... | collective-permute-start | bytes 1572872 | tf_op jit(solution)/shard_map/ppermute | solution.py:507
  8.4 1.6 %collective-permute-start.2 = (bf16[256,256]{1,0:T(8,128)(2,1)S(1)}, bf16[256,256]{1,0:T(8,128)(2,1)S(1)}, u32[]{:S(2)}, u32[]{:S(2)}) collective-permute-start(bf16[256,256]{1,0:T(8,128)(2,1)S(1)} %get-tuple-element.74), channel_id=1, source_target_pairs={{0,8},{4,12},{8,0},{12,4},{16,24},{20,28},{24,16},{28,20},{1,9},{5... | collective-permute-start | bytes 393224 | tf_op jit(solution)/shard_map/ppermute | solution.py:511
  9.9 2.6 %collective-permute-start.3 = (bf16[256,256]{1,0:T(8,128)(2,1)S(1)}, bf16[256,256]{1,0:T(8,128)(2,1)S(1)}, u32[]{:S(2)}, u32[]{:S(2)}) collective-permute-start(bf16[256,256]{1,0:T(8,128)(2,1)S(1)} %get-tuple-element.75), channel_id=1, source_target_pairs={{0,12},{4,8},{8,4},{12,0},{16,28},{20,24},{24,20},{28,16},{1,13},{... | collective-permute-start | bytes 393224 | tf_op jit(solution)/shard_map/ppermute | solution.py:511
  15.2 2.9 %stage_tokens.1 = (bf16[512,4096]{1,0:T(8,128)(2,1)S(1)}, bf16[2048,512]{1,0:T(8,128)(2,1)S(1)}) custom-call(s32[5]{0:T(128)S(1)} %stack.23.refs_0_.refs_1_, bf16[512,4096]{1,0:T(8,128)(2,1)} %collective-permute-done.refs_1_), custom_call_target="tpu_custom_call" | custom-call | bytes 10485760 | tf_op jit(solution)/shard_map/stage_tokens/pallas_call | solution.py:60
  18.2 1.8 %forward_encoder.4.refs_2_.refs_1_ = f32[2,512,256]{2,1,0:T(8,128)S(1)} custom-call(s32[5]{0:T(128)S(1)} %stack.23.refs_0_.refs_1_, bf16[1024,256]{1,0:T(8,128)(2,1)S(1)} %get-tuple-element.71.refs_4_.refs_1_, bf16[1024,256]{1,0:T(8,128)(2,1)S(1)} %collective-permute-done.7.refs_2_, bf16[512,4096]{1,0:T(8,128)(2,1)S(1)} %copy-done, ...), custom_call_target="tpu_custom_call" | custom-call | bytes 10485760 | tf_op jit(solution)/shard_map/forward_encoder/pallas_call | solution.py:60
  23.4 2.4 %hidden_units.2 = (bf16[2,512,256]{2,1,0:T(8,128)(2,1)S(1)}, f32[2,512,256]{2,1,0:T(8,128)S(1)}, bf16[2,512,256]{2,1,0:T(8,128)(2,1)S(1)}, bf16[256,256]{1,0:T(8,128)(2,1)S(1)}, bf16[256,256]{1,0:T(8,128)(2,1)S(1)}) custom-call(s32[5]{0:T(128)S(1)} %stack.23.refs_0_.refs_1_, f32[2,512,256]{2,1,0:T(8,128)S(1)} %forward_encoder.5.refs_1_, ...), custom_call_target="tpu_custom_call" | custom-call | bytes 12333056 | tf_op jit(solution)/shard_map/hidden_units/pallas_call | solution.py:60
  29.9 1.8 %collective-permute-start.18 = (bf16[1024,256]{1,0:T(8,128)(2,1)S(1)}, bf16[1024,256]{1,0:T(8,128)(2,1)S(1)}, u32[]{:S(2)}, u32[]{:S(2)}) collective-permute-start(bf16[1024,256]{1,0:T(8,128)(2,1)S(1)} %decoder_grad.7.refs_8_.refs_3_), channel_id=1, source_target_pairs={{0,2},{1,3},{2,0},{3,1},{4,6},{5,7},{6,4},{7,5},{8,10},{9,11},{10,... | collective-permute-start | bytes 1572872 | tf_op jit(solution)/shard_map/ppermute | solution.py:509
  32.2 2.6 %collective-permute-start.4 = (bf16[256,256]{1,0:T(8,128)(2,1)S(1)}, bf16[256,256]{1,0:T(8,128)(2,1)S(1)}, u32[]{:S(2)}, u32[]{:S(2)}) collective-permute-start(bf16[256,256]{1,0:T(8,128)(2,1)S(1)} %add_quarters.2.refs_3_.refs_1_), channel_id=1, source_target_pairs={{0,16},{4,20},{8,24},{12,28},{16,0},{20,4},{24,8},{28,12},{1,17},{... | collective-permute-start | bytes 393224 | tf_op jit(solution)/shard_map/ppermute | solution.py:511
  34.8 3.0 %forward_decoder.2 = (f32[2,512,256]{2,1,0:T(8,128)S(1)}, f32[256,256]{1,0:T(8,128)S(1)}) custom-call(s32[5]{0:T(128)S(1)} %stack.23.refs_0_.refs_1_, bf16[1024,256]{1,0:T(8,128)(2,1)S(1)} %get-tuple-element.76.refs_1_, bf16[1024,256]{1,0:T(8,128)(2,1)S(1)} %collective-permute-done.5.refs_2_, bf16[384,256]{1,0:T(8,128)(2,1)S(1)} %get-tuple-element.82.refs_5_.refs_3_, ...), custom_call_target="tpu_custom_call" | custom-call | bytes 11272192 | tf_op jit(solution)/shard_map/forward_decoder/pallas_call | solution.py:60
  37.8 2.0 %slope_pre.2.refs_2_ = bf16[2,512,256]{2,1,0:T(8,128)(2,1)S(1)} custom-call(s32[5]{0:T(128)S(1)} %stack.23.refs_0_.refs_1_, f32[2,512,256]{2,1,0:T(8,128)S(1)} %get-tuple-element.87.refs_1_, f32[256,256]{1,0:T(8,128)S(1)} %get-tuple-element.88.refs_2_, bf16[2,512,256]{2,1,0:T(8,128)(2,1)S(1)} %get-tuple-element.89.refs_3_, ...), custom_call_target="tpu_custom_call" | custom-call | bytes 12320768 | tf_op jit(solution)/shard_map/slope_pre/pallas_call | solution.py:60
  42.4 1.6 %collective-permute-start.15 = (bf16[256,256]{1,0:T(8,128)(2,1)S(1)}, bf16[256,256]{1,0:T(8,128)(2,1)S(1)}, u32[]{:S(2)}, u32[]{:S(2)}) collective-permute-start(bf16[256,256]{1,0:T(8,128)(2,1)S(1)} %add_quarters.3.refs_3_.refs_4_), channel_id=1, source_target_pairs={{0,4},{4,0},{8,12},{12,8},{16,20},{20,16},{24,28},{28,24},{1,5},{5... | collective-permute-start | bytes 393224 | tf_op jit(solution)/shard_map/ppermute | solution.py:511
  61.2 3.1 %outer_step.1 = (f32[2,1024,256]{2,1,0:T(8,128)}, f32[2,1024,256]{2,1,0:T(8,128)}, f32[8,128]{1,0:T(8,128)S(1)}) custom-call(s32[5]{0:T(128)S(1)} %stack.23.refs_0_.refs_1_, s32[8]{0:T(128)S(1)} %copy-done.7, f32[2,1024,256]{2,1,0:T(8,128)S(1)} %copy-done.5, f32[2,1024,256]{2,1,0:T(8,128)S(1)} %copy-done.6, ...), custom_call_target="tpu_custom_call" | custom-call | bytes 8916992 | tf_op jit(solution)/shard_map/outer_step/pallas_call | solution.py:60
  64.3 1.8 %forward_encoder.6.refs_1_ = f32[2,512,256]{2,1,0:T(8,128)S(1)} custom-call(s32[5]{0:T(128)S(1)} %stack.23.refs_0_.refs_1_, bf16[1024,256]{1,0:T(8,128)(2,1)S(1)} %get-tuple-element.93.refs_7_.refs_6_.refs_3_.refs_1_, bf16[1024,256]{1,0:T(8,128)(2,1)S(1)} %collective-permute-done.24.refs_2_, bf16[512,4096]{1,0:T(8,128)(2,1)S(1)} %copy-done, ...), custom_call_target="tpu_custom_call" | custom-call | bytes 10485760 | tf_op jit(solution)/shard_map/forward_encoder/pallas_call | solution.py:60
  66.1 4.7 %collective-permute-done.25.refs_0_ = bf16[1024,256]{1,0:T(8,128)(2,1)S(1)} collective-permute-done((bf16[1024,256]{1,0:T(8,128)(2,1)S(1)}, bf16[1024,256]{1,0:T(8,128)(2,1)S(1)}, u32[]{:S(2)}, u32[]{:S(2)}) %collective-permute-start.25) | collective-permute-done | bytes 524320 | tf_op jit(solution)/shard_map/ppermute | solution.py:507
  73.6 2.3 %hidden_units.3 = (bf16[2,512,256]{2,1,0:T(8,128)(2,1)S(1)}, f32[2,512,256]{2,1,0:T(8,128)S(1)}, bf16[2,512,256]{2,1,0:T(8,128)(2,1)S(1)}, bf16[256,256]{1,0:T(8,128)(2,1)S(1)}, bf16[256,256]{1,0:T(8,128)(2,1)S(1)}) custom-call(s32[5]{0:T(128)S(1)} %stack.23.refs_0_.refs_1_, f32[2,512,256]{2,1,0:T(8,128)S(1)} %forward_encoder.7.refs_1_, ...), custom_call_target="tpu_custom_call" | custom-call | bytes 12324864 | tf_op jit(solution)/shard_map/hidden_units/pallas_call | solution.py:60
  76.0 3.2 %collective-permute-done.23.refs_0_ = bf16[768,256]{1,0:T(8,128)(2,1)S(1)} collective-permute-done((bf16[768,256]{1,0:T(8,128)(2,1)S(1)}, bf16[768,256]{1,0:T(8,128)(2,1)S(1)}, u32[]{:S(2)}, u32[]{:S(2)}) %collective-permute-start.23) | collective-permute-done | bytes 393248 | tf_op jit(solution)/shard_map/ppermute | solution.py:507
  83.4 3.0 %forward_decoder.3 = (f32[2,512,256]{2,1,0:T(8,128)S(1)}, f32[256,256]{1,0:T(8,128)S(1)}) custom-call(s32[5]{0:T(128)S(1)} %stack.23.refs_0_.refs_1_, bf16[1024,256]{1,0:T(8,128)(2,1)S(1)} %get-tuple-element.95.refs_8_.refs_1_, bf16[1024,256]{1,0:T(8,128)(2,1)S(1)} %collective-permute-done.22.refs_2_, ...), custom_call_target="tpu_custom_call" | custom-call | bytes 11272192 | tf_op jit(solution)/shard_map/forward_decoder/pallas_call | solution.py:60
  86.5 2.0 %slope_pre.3.refs_2_ = bf16[2,512,256]{2,1,0:T(8,128)(2,1)S(1)} custom-call(s32[5]{0:T(128)S(1)} %stack.23.refs_0_.refs_1_, f32[2,512,256]{2,1,0:T(8,128)S(1)} %get-tuple-element.106.refs_1_, f32[256,256]{1,0:T(8,128)S(1)} %get-tuple-element.107.refs_2_, bf16[2,512,256]{2,1,0:T(8,128)(2,1)S(1)} %get-tuple-element.108.refs_3_, ...), custom_call_target="tpu_custom_call" | custom-call | bytes 12320768 | tf_op jit(solution)/shard_map/slope_pre/pallas_call | solution.py:60
  92.4 4.4 %collective-permute-done.32.refs_4_.refs_2_ = bf16[1024,256]{1,0:T(8,128)(2,1)S(1)} collective-permute-done((bf16[1024,256]{1,0:T(8,128)(2,1)S(1)}, bf16[1024,256]{1,0:T(8,128)(2,1)S(1)}, u32[]{:S(2)}, u32[]{:S(2)}) %collective-permute-start.32) | collective-permute-done | bytes 524320 | tf_op jit(solution)/shard_map/ppermute | solution.py:509
  99.6 3.1 %adam_rows.12 = (f32[8,128]{1,0:T(8,128)}, f32[1,2,1024,256]{3,2,1,0:T(8,128)}, f32[1,2,1024,256]{3,2,1,0:T(8,128)}, f32[1,2,1024,256]{3,2,1,0:T(8,128)}) custom-call(s32[8]{0:T(128)S(1)} %copy-done.7, f32[1024,256]{1,0:T(8,128)S(1)} %decoder_grad.11.refs_3_.refs_1_, bf16[1024,256]{1,0:T(8,128)(2,1)S(1)} %collective-permute-done.32.refs_4_.refs_2_, ...), custom_call_target="tpu_custom_call" | custom-call | bytes 12062720 | tf_op jit(solution)/shard_map/adam_rows/pallas_call | solution.py:60
  102.8 2.0 %adam_rows.13 = (f32[1,2,1024,256]{3,2,1,0:T(8,128)}, f32[1,2,1024,256]{3,2,1,0:T(8,128)}, f32[1,2,1024,256]{3,2,1,0:T(8,128)}) custom-call(s32[8]{0:T(128)S(1)} %copy-done.7, f32[512,256]{1,0:T(8,128)S(1)} %encoder_grad.19.refs_3_.refs_1_, ...), custom_call_target="tpu_custom_call", output_to_operand_aliasing={{0}: (7, {}), {1}: (8, {}), {2}: (9, {})} | custom-call | bytes 15466496 | tf_op jit(solution)/shard_map/adam_rows/pallas_call | solution.py:60
  105.3 1.6 %adam_rows.14 = (f32[1,2,1024,256]{3,2,1,0:T(8,128)}, f32[1,2,1024,256]{3,2,1,0:T(8,128)}, f32[1,2,1024,256]{3,2,1,0:T(8,128)}) custom-call(s32[8]{0:T(128)S(1)} %copy-done.7, f32[256,256]{1,0:T(8,128)S(1)} %encoder_grad.20.refs_3_.refs_1_, ...), custom_call_target="tpu_custom_call", output_to_operand_aliasing={{0}: (7, {}), {1}: (8, {}), {2}: (9, {})} | custom-call | bytes 14024704 | tf_op jit(solution)/shard_map/adam_rows/pallas_call | solution.py:60
  106.9 1.6 %adam_rows.15 = (f32[1,2,1024,256]{3,2,1,0:T(8,128)}, f32[1,2,1024,256]{3,2,1,0:T(8,128)}, f32[1,2,1024,256]{3,2,1,0:T(8,128)}) custom-call(s32[8]{0:T(128)S(1)} %copy-done.7, f32[256,256]{1,0:T(8,128)S(1)} %encoder_grad.21.refs_7_.refs_1_, ...), custom_call_target="tpu_custom_call", output_to_operand_aliasing={{0}: (7, {}), {1}: (8, {}), {2}: (9, {})} | custom-call | bytes 14024704 | tf_op jit(solution)/shard_map/adam_rows/pallas_call | solution.py:60
  (119 shorter events, 47.7 us)
Async XLA Ops:
  0.6 11.9 %collective-permute-start = (bf16[512,4096]{1,0:T(8,128)(2,1)}, bf16[512,4096]{1,0:T(8,128)(2,1)}, u32[]{:S(2)}, u32[]{:S(2)}) collective-permute-start(bf16[512,4096]{1,0:T(8,128)(2,1)} %refs_8_.3), channel_id=1, source_target_pairs={{0,1},{1,0},{2,3},{3,2},{4,5},{5,4},{6,7},{7,6},{8,9},{9,8},{10,11... | collective-permute-start | bytes 12582920 | tf_op jit(solution)/shard_map/ppermute | solution.py:506
  3.0 7.0 %collective-permute-start.7 = (bf16[1024,256]{1,0:T(8,128)(2,1)S(1)}, bf16[1024,256]{1,0:T(8,128)(2,1)S(1)}, u32[]{:S(2)}, u32[]{:S(2)}) collective-permute-start(bf16[1024,256]{1,0:T(8,128)(2,1)S(1)} %get-tuple-element.71.refs_4_.refs_1_), channel_id=1, source_target_pairs={{0,1},{1,0},{2,3},{3,2},{4,5},{5,4},{6,7},{7,6},{8,9},{9,8},{10,11... | collective-permute-start | bytes 1572872 | tf_op jit(solution)/shard_map/ppermute | solution.py:506
  3.1 17.5 %collective-permute-start.8 = (bf16[1024,256]{1,0:T(8,128)(2,1)S(1)}, bf16[1024,256]{1,0:T(8,128)(2,1)S(1)}, u32[]{:S(2)}, u32[]{:S(2)}) collective-permute-start(bf16[1024,256]{1,0:T(8,128)(2,1)S(1)} %get-tuple-element.71.refs_4_.refs_1_), channel_id=1, source_target_pairs={{2,0},{3,1},{0,2},{1,3},{6,4},{7,5},{4,6},{5,7},{10,8},{11,9},{8,1... | collective-permute-start | bytes 1572872 | tf_op jit(solution)/shard_map/ppermute | solution.py:507
  6.8 13.2 %collective-permute-start.1 = (bf16[256,256]{1,0:T(8,128)(2,1)S(1)}, bf16[256,256]{1,0:T(8,128)(2,1)S(1)}, u32[]{:S(2)}, u32[]{:S(2)}) collective-permute-start(bf16[256,256]{1,0:T(8,128)(2,1)S(1)} %get-tuple-element.73), channel_id=1, source_target_pairs={{0,4},{4,0},{8,12},{12,8},{16,20},{20,16},{24,28},{28,24},{1,5},{5... | collective-permute-start | bytes 393224 | tf_op jit(solution)/shard_map/ppermute | solution.py:511
  8.4 11.6 %collective-permute-start.2 = (bf16[256,256]{1,0:T(8,128)(2,1)S(1)}, bf16[256,256]{1,0:T(8,128)(2,1)S(1)}, u32[]{:S(2)}, u32[]{:S(2)}) collective-permute-start(bf16[256,256]{1,0:T(8,128)(2,1)S(1)} %get-tuple-element.74), channel_id=1, source_target_pairs={{0,8},{4,12},{8,0},{12,4},{16,24},{20,28},{24,16},{28,20},{1,9},{5... | collective-permute-start | bytes 393224 | tf_op jit(solution)/shard_map/ppermute | solution.py:511
  9.9 10.1 %collective-permute-start.3 = (bf16[256,256]{1,0:T(8,128)(2,1)S(1)}, bf16[256,256]{1,0:T(8,128)(2,1)S(1)}, u32[]{:S(2)}, u32[]{:S(2)}) collective-permute-start(bf16[256,256]{1,0:T(8,128)(2,1)S(1)} %get-tuple-element.75), channel_id=1, source_target_pairs={{0,12},{4,8},{8,4},{12,0},{16,28},{20,24},{24,20},{28,16},{1,13},{... | collective-permute-start | bytes 393224 | tf_op jit(solution)/shard_map/ppermute | solution.py:511
  12.6 14.6 %collective-permute-start.6 = (bf16[768,256]{1,0:T(8,128)(2,1)S(1)}, bf16[768,256]{1,0:T(8,128)(2,1)S(1)}, u32[]{:S(2)}, u32[]{:S(2)}) collective-permute-start(bf16[768,256]{1,0:T(8,128)(2,1)S(1)} %get-tuple-element.77.refs_5_), channel_id=1, source_target_pairs={{2,0},{3,1},{0,2},{1,3},{6,4},{7,5},{4,6},{5,7},{10,8},{11,9},{8,1... | collective-permute-start | bytes 1179656 | tf_op jit(solution)/shard_map/ppermute | solution.py:507
  21.3 10.9 %collective-permute-start.5 = (bf16[1024,256]{1,0:T(8,128)(2,1)S(1)}, bf16[1024,256]{1,0:T(8,128)(2,1)S(1)}, u32[]{:S(2)}, u32[]{:S(2)}) collective-permute-start(bf16[1024,256]{1,0:T(8,128)(2,1)S(1)} %get-tuple-element.76.refs_1_), channel_id=1, source_target_pairs={{0,1},{1,0},{2,3},{3,2},{4,5},{5,4},{6,7},{7,6},{8,9},{9,8},{10,11... | collective-permute-start | bytes 1572872 | tf_op jit(solution)/shard_map/ppermute | solution.py:506
  21.4 8.1 %collective-permute-start.11 = (bf16[256,256]{1,0:T(8,128)(2,1)S(1)}, bf16[256,256]{1,0:T(8,128)(2,1)S(1)}, u32[]{:S(2)}, u32[]{:S(2)}) collective-permute-start(bf16[256,256]{1,0:T(8,128)(2,1)S(1)} %get-tuple-element.84.refs_6_), channel_id=1, source_target_pairs={{2,0},{3,1},{0,2},{1,3},{6,4},{7,5},{4,6},{5,7},{10,8},{11,9},{8,1... | collective-permute-start | bytes 393224 | tf_op jit(solution)/shard_map/ppermute | solution.py:507
  29.9 16.1 %collective-permute-start.18 = (bf16[1024,256]{1,0:T(8,128)(2,1)S(1)}, bf16[1024,256]{1,0:T(8,128)(2,1)S(1)}, u32[]{:S(2)}, u32[]{:S(2)}) collective-permute-start(bf16[1024,256]{1,0:T(8,128)(2,1)S(1)} %decoder_grad.7.refs_8_.refs_3_), channel_id=1, source_target_pairs={{0,2},{1,3},{2,0},{3,1},{4,6},{5,7},{6,4},{7,5},{8,10},{9,11},{10,... | collective-permute-start | bytes 1572872 | tf_op jit(solution)/shard_map/ppermute | solution.py:509
  32.2 9.6 %collective-permute-start.4 = (bf16[256,256]{1,0:T(8,128)(2,1)S(1)}, bf16[256,256]{1,0:T(8,128)(2,1)S(1)}, u32[]{:S(2)}, u32[]{:S(2)}) collective-permute-start(bf16[256,256]{1,0:T(8,128)(2,1)S(1)} %add_quarters.2.refs_3_.refs_1_), channel_id=1, source_target_pairs={{0,16},{4,20},{8,24},{12,28},{16,0},{20,4},{24,8},{28,12},{1,17},{... | collective-permute-start | bytes 393224 | tf_op jit(solution)/shard_map/ppermute | solution.py:511
  40.3 12.3 %collective-permute-start.21 = (bf16[512,256]{1,0:T(8,128)(2,1)S(1)}, bf16[512,256]{1,0:T(8,128)(2,1)S(1)}, u32[]{:S(2)}, u32[]{:S(2)}) collective-permute-start(bf16[512,256]{1,0:T(8,128)(2,1)S(1)} %encoder_grad.12.refs_3_), channel_id=1, source_target_pairs={{0,2},{1,3},{2,0},{3,1},{4,6},{5,7},{6,4},{7,5},{8,10},{9,11},{10,... | collective-permute-start | bytes 786440 | tf_op jit(solution)/shard_map/ppermute | solution.py:509
  44.6 7.1 %collective-permute-start.17 = (bf16[256,256]{1,0:T(8,128)(2,1)S(1)}, bf16[256,256]{1,0:T(8,128)(2,1)S(1)}, u32[]{:S(2)}, u32[]{:S(2)}) collective-permute-start(bf16[256,256]{1,0:T(8,128)(2,1)S(1)} %add_quarters.3.refs_3_.refs_4_), channel_id=1, source_target_pairs={{0,12},{4,8},{8,4},{12,0},{16,28},{20,24},{24,20},{28,16},{1,13},{... | collective-permute-start | bytes 393224 | tf_op jit(solution)/shard_map/ppermute | solution.py:511
  46.3 8.0 %collective-permute-start.20 = (bf16[256,256]{1,0:T(8,128)(2,1)S(1)}, bf16[256,256]{1,0:T(8,128)(2,1)S(1)}, u32[]{:S(2)}, u32[]{:S(2)}) collective-permute-start(bf16[256,256]{1,0:T(8,128)(2,1)S(1)} %encoder_grad.13.refs_3_), channel_id=1, source_target_pairs={{0,2},{1,3},{2,0},{3,1},{4,6},{5,7},{6,4},{7,5},{8,10},{9,11},{10,... | collective-permute-start | bytes 393224 | tf_op jit(solution)/shard_map/ppermute | solution.py:509
  47.6 7.5 %collective-permute-start.19 = (bf16[256,256]{1,0:T(8,128)(2,1)S(1)}, bf16[256,256]{1,0:T(8,128)(2,1)S(1)}, u32[]{:S(2)}, u32[]{:S(2)}) collective-permute-start(bf16[256,256]{1,0:T(8,128)(2,1)S(1)} %encoder_grad.14.refs_3_), channel_id=1, source_target_pairs={{0,2},{1,3},{2,0},{3,1},{4,6},{5,7},{6,4},{7,5},{8,10},{9,11},{10,... | collective-permute-start | bytes 393224 | tf_op jit(solution)/shard_map/ppermute | solution.py:509
  55.9 8.4 %collective-permute-start.24 = (bf16[1024,256]{1,0:T(8,128)(2,1)S(1)}, bf16[1024,256]{1,0:T(8,128)(2,1)S(1)}, u32[]{:S(2)}, u32[]{:S(2)}) collective-permute-start(bf16[1024,256]{1,0:T(8,128)(2,1)S(1)} %get-tuple-element.93.refs_7_.refs_6_.refs_3_.refs_1_), channel_id=1, source_target_pairs={{0,1},{1,0},{2,3},{3,2},{4,5},{5,4},{6,7},{7,6},{8,9},{9,8},{10,11... | collective-permute-start | bytes 1572872 | tf_op jit(solution)/shard_map/ppermute | solution.py:506
  56.0 14.8 %collective-permute-start.25 = (bf16[1024,256]{1,0:T(8,128)(2,1)S(1)}, bf16[1024,256]{1,0:T(8,128)(2,1)S(1)}, u32[]{:S(2)}, u32[]{:S(2)}) collective-permute-start(bf16[1024,256]{1,0:T(8,128)(2,1)S(1)} %get-tuple-element.93.refs_7_.refs_6_.refs_3_.refs_1_), channel_id=1, source_target_pairs={{2,0},{3,1},{0,2},{1,3},{6,4},{7,5},{4,6},{5,7},{10,8},{11,9},{8,1... | collective-permute-start | bytes 1572872 | tf_op jit(solution)/shard_map/ppermute | solution.py:507
  60.0 19.2 %collective-permute-start.23 = (bf16[768,256]{1,0:T(8,128)(2,1)S(1)}, bf16[768,256]{1,0:T(8,128)(2,1)S(1)}, u32[]{:S(2)}, u32[]{:S(2)}) collective-permute-start(bf16[768,256]{1,0:T(8,128)(2,1)S(1)} %get-tuple-element.96.refs_5_), channel_id=1, source_target_pairs={{2,0},{3,1},{0,2},{1,3},{6,4},{7,5},{4,6},{5,7},{10,8},{11,9},{8,1... | collective-permute-start | bytes 1179656 | tf_op jit(solution)/shard_map/ppermute | solution.py:507
  71.4 12.0 %collective-permute-start.22 = (bf16[1024,256]{1,0:T(8,128)(2,1)S(1)}, bf16[1024,256]{1,0:T(8,128)(2,1)S(1)}, u32[]{:S(2)}, u32[]{:S(2)}) collective-permute-start(bf16[1024,256]{1,0:T(8,128)(2,1)S(1)} %get-tuple-element.95.refs_8_.refs_1_), channel_id=1, source_target_pairs={{0,1},{1,0},{2,3},{3,2},{4,5},{5,4},{6,7},{7,6},{8,9},{9,8},{10,11... | collective-permute-start | bytes 1572872 | tf_op jit(solution)/shard_map/ppermute | solution.py:506
  71.5 10.1 %collective-permute-start.28 = (bf16[256,256]{1,0:T(8,128)(2,1)S(1)}, bf16[256,256]{1,0:T(8,128)(2,1)S(1)}, u32[]{:S(2)}, u32[]{:S(2)}) collective-permute-start(bf16[256,256]{1,0:T(8,128)(2,1)S(1)} %get-tuple-element.103.refs_6_), channel_id=1, source_target_pairs={{2,0},{3,1},{0,2},{1,3},{6,4},{7,5},{4,6},{5,7},{10,8},{11,9},{8,1... | collective-permute-start | bytes 393224 | tf_op jit(solution)/shard_map/ppermute | solution.py:507
  82.0 14.9 %collective-permute-start.32 = (bf16[1024,256]{1,0:T(8,128)(2,1)S(1)}, bf16[1024,256]{1,0:T(8,128)(2,1)S(1)}, u32[]{:S(2)}, u32[]{:S(2)}) collective-permute-start(bf16[1024,256]{1,0:T(8,128)(2,1)S(1)} %decoder_grad.10.refs_8_.refs_3_), channel_id=1, source_target_pairs={{0,2},{1,3},{2,0},{3,1},{4,6},{5,7},{6,4},{7,5},{8,10},{9,11},{10,... | collective-permute-start | bytes 1572872 | tf_op jit(solution)/shard_map/ppermute | solution.py:509
  88.9 13.9 %collective-permute-start.35 = (bf16[512,256]{1,0:T(8,128)(2,1)S(1)}, bf16[512,256]{1,0:T(8,128)(2,1)S(1)}, u32[]{:S(2)}, u32[]{:S(2)}) collective-permute-start(bf16[512,256]{1,0:T(8,128)(2,1)S(1)} %encoder_grad.18.refs_3_), channel_id=1, source_target_pairs={{0,2},{1,3},{2,0},{3,1},{4,6},{5,7},{6,4},{7,5},{8,10},{9,11},{10,... | collective-permute-start | bytes 786440 | tf_op jit(solution)/shard_map/ppermute | solution.py:509
  97.2 8.1 %collective-permute-start.34 = (bf16[256,256]{1,0:T(8,128)(2,1)S(1)}, bf16[256,256]{1,0:T(8,128)(2,1)S(1)}, u32[]{:S(2)}, u32[]{:S(2)}) collective-permute-start(bf16[256,256]{1,0:T(8,128)(2,1)S(1)} %encoder_grad.22.refs_3_), channel_id=1, source_target_pairs={{0,2},{1,3},{2,0},{3,1},{4,6},{5,7},{6,4},{7,5},{8,10},{9,11},{10,... | collective-permute-start | bytes 393224 | tf_op jit(solution)/shard_map/ppermute | solution.py:509
  98.4 8.4 %collective-permute-start.33 = (bf16[256,256]{1,0:T(8,128)(2,1)S(1)}, bf16[256,256]{1,0:T(8,128)(2,1)S(1)}, u32[]{:S(2)}, u32[]{:S(2)}) collective-permute-start(bf16[256,256]{1,0:T(8,128)(2,1)S(1)} %encoder_grad.23.refs_7_), channel_id=1, source_target_pairs={{0,2},{1,3},{2,0},{3,1},{4,6},{5,7},{6,4},{7,5},{8,10},{9,11},{10,... | collective-permute-start | bytes 393224 | tf_op jit(solution)/shard_map/ppermute | solution.py:509
  (21 other events, 82.9 us)

commit v15 on v14

--- a/solution.py
+++ b/solution.py
@@ -307,20 +307,13 @@
     out[...] = token_sum(start, out.shape[0], (xt_own, xt_par), slopes).astype(out.dtype)
 
 
-def decoder_body(scale, start, pieces, front, xt_own, xt_par, counted, w_hi, w_lo, *refs):
-    lows, more, out = refs[:pieces], refs[pieces:-1], refs[-1]
+def decoder_body(scale, start, xt_own, xt_par, counted, w_hi, w_lo, *refs):
+    lows, out = refs[:-1], refs[-1]
     off = 0
-    got = more
-    if front:
-        off = more[0].shape[0]
-        out[:off, :] = more[0][...]
-        got = ()
     for low in lows:
         size = low.shape[0]
         both = token_sum(start + off, size, (xt_own, xt_par), counted)
         value = scale * (dot(low[...], w_hi[...]) + dot(low[...], w_lo[...]) - both)
-        for g in got:
-            value = value + g[off:off + size, :].astype(f32)
         out[off:off + size, :] = value.astype(out.dtype)
         off += size
 
@@ -336,8 +329,12 @@
     theta, first, second = refs[count:3 + count]
     refs = refs[3 + count:]
     grad = own[...]
-    for g in got:
-        grad = grad + g[...].astype(f32)
+    got = [g[...].astype(f32) for g in got]
+    while got:
+        value = got.pop(0)
+        while value.shape[0] < own.shape[0]:
+            value = jnp.concatenate([value, got.pop(0)], 0)
+        grad = grad + value
     one = beta_one * first[0, 0] + (1.0 - beta_one) * grad
     two = beta_two * second[0, 0] + (1.0 - beta_two) * grad * grad
     old = theta[0, 0]
@@ -554,25 +551,24 @@
         if step == 0:
             cw = weigh(kinds, pending[-1][0], tokens)
         hidden, slope, counted, w_hi, w_lo = hidden_rows(pos, carry[0], cw, pending, xs, rows, scale)
-        dec_grad = lambda s, size, lows, more, front, dtype, after: grad_rows(
-            functools.partial(decoder_body, scale, s * rows, len(lows), front), "decoder_grad", size, xt,
-            [counted, w_hi, w_lo, *lows, *more], dtype, after)
+        dec_grad = lambda start, size, lows, dtype, after: grad_rows(
+            functools.partial(decoder_body, scale, start), "decoder_grad", size, xt,
+            [counted, w_hi, w_lo, *lows], dtype, after)
         enc_grad = lambda s, off, size, dtype, after: grad_rows(
             functools.partial(encoder_body, s * rows + off), "encoder_grad", size, xt, [slopes], dtype, after)
         sent = []
         got = {key: [] for key in blocks}
         part, pending = [], []
-        whole_grad = {s: [] for s in others}
+        back = {}
         for n, far in enumerate(dec_far):
             pieces, handed = take(far, starts[n], [counted] + sent[-1:])
             part += pieces
             pending += handed
             for s in others:
                 rows_in = [p[0] for p in pieces if p[1] == 1 + s]
-                whole_grad[s] = [dec_grad(
-                    s, starts[n] + sizes[n], rows_in, whole_grad[s], n > 0, bf16, sent[-1:])]
-                sent.append(whole_grad[s][0])
-        back = [give(whole_grad[s][0], s) for s in others]
+                sent.append(dec_grad(s * rows + starts[n], sizes[n], rows_in, bf16, sent[-1:]))
+                back[s, n] = give(sent[-1], s)
+        back = [back[key] for key in sorted(back)]
 
         carry = forward(
             pos, [], [(dec, 1, 0, rows), (dec_near, 1 + chips, 0, rows)] + part, xs, rows, True, sent[-1:])
@@ -582,7 +578,7 @@
             *more, after=after)
         prev = None
         mine = {}
-        own_dec = lambda after: dec_grad(0, rows, dec_parts, [], False, f32, after)
+        own_dec = lambda after: dec_grad(0, rows, dec_parts, f32, after)
         for n, key in enumerate(blocks[1:]):
             hold = back if n == 1 else []
             for s in others:

time: 109 us -> 110 us (level)
  starting transfers between devices: 31.4 us -> 33.6 us
    ppermute x6, waiting for transfers between devices: 12.4 us -> 8.34 us  [local(): lax.ppermute(a, 'fsdp', [((f // 2 + s) % chips * 2 + f % 2, f) for f in r...]
    ppermute x8 -> x10, waiting for transfers between devices: 4.94 us -> 7.21 us  [local(): lax.ppermute(a, 'fsdp', [(f, (f // 2 + s) % chips * 2 + f % 2) for f in r...]
    ppermute x8 -> x10, starting transfers between devices: 8.45 us -> 10.7 us  [local(): lax.ppermute(a, 'fsdp', [(f, (f // 2 + s) % chips * 2 + f % 2) for f in r...]
  transfers between devices with their start and end apart: 36 -> 38, of which waited for: 11 -> 8; matrix products, arithmetic and copies ran while one was open for 0% -> 0% of each run, Pallas kernels for 47% -> 46%
where the time goes in v15:
time: 110 us
  Pallas kernels  53.1 us (48%)
  starting transfers between devices  33.6 us (31%)
  waiting for transfers between devices  19.9 us (18%)
  local copies, waits for them, and re-layouts  2.27 us (2%)
  between operations  1.17 us (1%)
    pallas_call x52, Pallas kernels, call(): pl.pallas_call(run, name=name, out_shape=[o for o, _ in outs], grid_spec=...  53.1 us
    ppermute x7, starting transfers between devices, local(): lax.ppermute(a, 'replica', [(r, r ^ bit) for r in range(n_rep)])  11.9 us
    ppermute x10, starting transfers between devices, local(): lax.ppermute(a, 'fsdp', [(f, (f // 2 + s) % chips * 2 + f % 2) for f in r...  10.7 us
    ppermute x6, waiting for transfers between devices, local(): lax.ppermute(a, 'fsdp', [((f // 2 + s) % chips * 2 + f % 2, f) for f in r...  8.34 us
    ppermute x6, starting transfers between devices, local(): lax.ppermute(a, 'fsdp', [((f // 2 + s) % chips * 2 + f % 2, f) for f in r...  7.89 us
    ppermute x10, waiting for transfers between devices, local(): lax.ppermute(a, 'fsdp', [(f, (f // 2 + s) % chips * 2 + f % 2) for f in r...  7.21 us
    ppermute x7, waiting for transfers between devices, local(): lax.ppermute(a, 'replica', [(r, r ^ bit) for r in range(n_rep)])  4.29 us
    ppermute x15, starting transfers between devices, local(): to_partner = lambda a: lax.ppermute(a, 'fsdp', partner)  3.11 us
  transfers between devices with their start and end apart: 38, of which 8 were waited for; matrix products, arithmetic and copies ran while one was open for 0% of the time, Pallas kernels for 46%

profile of v15, /device:TPU:0, one launch (start us, length us, event | category | flops | bytes accessed | tf_op | source)
XLA Modules:
  0.0 109.9 jit_solution(15570895285538578044)
XLA Ops:
  1.2 1.6 %copy-done.1 = f32[1,2,1024,256]{3,2,1,0:T(8,128)S(1)} copy-done((f32[1,2,1024,256]{3,2,1,0:T(8,128)S(1)}, f32[1,2,1024,256]{3,2,1,0:T(8,128)}, u32[]{:S(2)}) %copy-start.1) | copy-done | bytes 2097176
  3.1 3.0 %collective-permute-start.8 = (bf16[1024,256]{1,0:T(8,128)(2,1)S(1)}, bf16[1024,256]{1,0:T(8,128)(2,1)S(1)}, u32[]{:S(2)}, u32[]{:S(2)}) collective-permute-start(bf16[1024,256]{1,0:T(8,128)(2,1)S(1)} %get-tuple-element.71.refs_4_.refs_1_), channel_id=1, source_target_pairs={{2,0},{3,1},{0,2},{1,3},{6,4},{7,5},{4,6},{5,7},{10,8},{11,9},{8,1... | collective-permute-start | bytes 1572872 | tf_op jit(solution)/shard_map/ppermute | solution.py:504
  9.9 2.1 %collective-permute-done.1.refs_2_ = bf16[256,256]{1,0:T(8,128)(2,1)S(1)} collective-permute-done((bf16[256,256]{1,0:T(8,128)(2,1)S(1)}, bf16[256,256]{1,0:T(8,128)(2,1)S(1)}, u32[]{:S(2)}, u32[]{:S(2)}) %collective-permute-start.1) | collective-permute-done | bytes 131104 | tf_op jit(solution)/shard_map/ppermute | solution.py:508
  12.1 2.6 %collective-permute-start.3 = (bf16[256,256]{1,0:T(8,128)(2,1)S(1)}, bf16[256,256]{1,0:T(8,128)(2,1)S(1)}, u32[]{:S(2)}, u32[]{:S(2)}) collective-permute-start(bf16[256,256]{1,0:T(8,128)(2,1)S(1)} %get-tuple-element.75), channel_id=1, source_target_pairs={{0,12},{4,8},{8,4},{12,0},{16,28},{20,24},{24,20},{28,16},{1,13},{... | collective-permute-start | bytes 393224 | tf_op jit(solution)/shard_map/ppermute | solution.py:508
  17.3 2.9 %stage_tokens.1 = (bf16[512,4096]{1,0:T(8,128)(2,1)S(1)}, bf16[2048,512]{1,0:T(8,128)(2,1)S(1)}) custom-call(s32[5]{0:T(128)S(1)} %stack.23.refs_0_.refs_1_, bf16[512,4096]{1,0:T(8,128)(2,1)} %collective-permute-done.refs_1_), custom_call_target="tpu_custom_call" | custom-call | bytes 10485760 | tf_op jit(solution)/shard_map/stage_tokens/pallas_call | solution.py:60
  20.3 1.8 %forward_encoder.4.refs_2_.refs_1_ = f32[2,512,256]{2,1,0:T(8,128)S(1)} custom-call(s32[5]{0:T(128)S(1)} %stack.23.refs_0_.refs_1_, bf16[1024,256]{1,0:T(8,128)(2,1)S(1)} %get-tuple-element.71.refs_4_.refs_1_, bf16[1024,256]{1,0:T(8,128)(2,1)S(1)} %collective-permute-done.7.refs_2_, bf16[512,4096]{1,0:T(8,128)(2,1)S(1)} %copy-done, ...), custom_call_target="tpu_custom_call" | custom-call | bytes 10485760 | tf_op jit(solution)/shard_map/forward_encoder/pallas_call | solution.py:60
  25.4 2.4 %hidden_units.2 = (bf16[2,512,256]{2,1,0:T(8,128)(2,1)S(1)}, f32[2,512,256]{2,1,0:T(8,128)S(1)}, bf16[2,512,256]{2,1,0:T(8,128)(2,1)S(1)}, bf16[256,256]{1,0:T(8,128)(2,1)S(1)}, bf16[256,256]{1,0:T(8,128)(2,1)S(1)}) custom-call(s32[5]{0:T(128)S(1)} %stack.23.refs_0_.refs_1_, f32[2,512,256]{2,1,0:T(8,128)S(1)} %forward_encoder.5.refs_1_, ...), custom_call_target="tpu_custom_call" | custom-call | bytes 12333056 | tf_op jit(solution)/shard_map/hidden_units/pallas_call | solution.py:60
  30.8 2.7 %collective-permute-start.4 = (bf16[256,256]{1,0:T(8,128)(2,1)S(1)}, bf16[256,256]{1,0:T(8,128)(2,1)S(1)}, u32[]{:S(2)}, u32[]{:S(2)}) collective-permute-start(bf16[256,256]{1,0:T(8,128)(2,1)S(1)} %add_quarters.2.refs_3_.refs_1_), channel_id=1, source_target_pairs={{0,16},{4,20},{8,24},{12,28},{16,0},{20,4},{24,8},{28,12},{1,17},{... | collective-permute-start | bytes 393224 | tf_op jit(solution)/shard_map/ppermute | solution.py:508
  33.9 3.0 %forward_decoder.2 = (f32[2,512,256]{2,1,0:T(8,128)S(1)}, f32[256,256]{1,0:T(8,128)S(1)}) custom-call(s32[5]{0:T(128)S(1)} %stack.23.refs_0_.refs_1_, bf16[1024,256]{1,0:T(8,128)(2,1)S(1)} %get-tuple-element.76.refs_1_, bf16[1024,256]{1,0:T(8,128)(2,1)S(1)} %collective-permute-done.5.refs_2_, bf16[384,256]{1,0:T(8,128)(2,1)S(1)} %get-tuple-element.82.refs_5_.refs_3_, ...), custom_call_target="tpu_custom_call" | custom-call | bytes 11272192 | tf_op jit(solution)/shard_map/forward_decoder/pallas_call | solution.py:60
  37.4 2.0 %slope_pre.2.refs_2_ = bf16[2,512,256]{2,1,0:T(8,128)(2,1)S(1)} custom-call(s32[5]{0:T(128)S(1)} %stack.23.refs_0_.refs_1_, f32[2,512,256]{2,1,0:T(8,128)S(1)} %get-tuple-element.87.refs_1_, f32[256,256]{1,0:T(8,128)S(1)} %get-tuple-element.88.refs_2_, bf16[2,512,256]{2,1,0:T(8,128)(2,1)S(1)} %get-tuple-element.89.refs_3_, ...), custom_call_target="tpu_custom_call" | custom-call | bytes 12320768 | tf_op jit(solution)/shard_map/slope_pre/pallas_call | solution.py:60
  39.9 1.6 %collective-permute-start.22 = (bf16[512,256]{1,0:T(8,128)(2,1)S(1)}, bf16[512,256]{1,0:T(8,128)(2,1)S(1)}, u32[]{:S(2)}, u32[]{:S(2)}) collective-permute-start(bf16[512,256]{1,0:T(8,128)(2,1)S(1)} %encoder_grad.12.refs_3_), channel_id=1, source_target_pairs={{0,2},{1,3},{2,0},{3,1},{4,6},{5,7},{6,4},{7,5},{8,10},{9,11},{10,... | collective-permute-start | bytes 786440 | tf_op jit(solution)/shard_map/ppermute | solution.py:506
  49.7 1.7 %collective-permute-done.17.refs_7_ = bf16[256,256]{1,0:T(8,128)(2,1)S(1)} collective-permute-done((bf16[256,256]{1,0:T(8,128)(2,1)S(1)}, bf16[256,256]{1,0:T(8,128)(2,1)S(1)}, u32[]{:S(2)}, u32[]{:S(2)}) %collective-permute-start.17) | collective-permute-done | bytes 131104 | tf_op jit(solution)/shard_map/ppermute | solution.py:508
  60.9 3.1 %outer_step.1 = (f32[2,1024,256]{2,1,0:T(8,128)}, f32[2,1024,256]{2,1,0:T(8,128)}, f32[8,128]{1,0:T(8,128)S(1)}) custom-call(s32[5]{0:T(128)S(1)} %stack.23.refs_0_.refs_1_, s32[8]{0:T(128)S(1)} %copy-done.7, f32[2,1024,256]{2,1,0:T(8,128)S(1)} %copy-done.5, f32[2,1024,256]{2,1,0:T(8,128)S(1)} %copy-done.6, ...), custom_call_target="tpu_custom_call" | custom-call | bytes 8916992 | tf_op jit(solution)/shard_map/outer_step/pallas_call | solution.py:60
  64.0 1.8 %forward_encoder.6.refs_1_ = f32[2,512,256]{2,1,0:T(8,128)S(1)} custom-call(s32[5]{0:T(128)S(1)} %stack.23.refs_0_.refs_1_, bf16[1024,256]{1,0:T(8,128)(2,1)S(1)} %get-tuple-element.93.refs_7_.refs_3_.refs_1_, bf16[1024,256]{1,0:T(8,128)(2,1)S(1)} %collective-permute-done.25.refs_2_, bf16[512,4096]{1,0:T(8,128)(2,1)S(1)} %copy-done, ...), custom_call_target="tpu_custom_call" | custom-call | bytes 10485760 | tf_op jit(solution)/shard_map/forward_encoder/pallas_call | solution.py:60
  65.8 4.7 %collective-permute-done.26.refs_0_ = bf16[1024,256]{1,0:T(8,128)(2,1)S(1)} collective-permute-done((bf16[1024,256]{1,0:T(8,128)(2,1)S(1)}, bf16[1024,256]{1,0:T(8,128)(2,1)S(1)}, u32[]{:S(2)}, u32[]{:S(2)}) %collective-permute-start.26) | collective-permute-done | bytes 524320 | tf_op jit(solution)/shard_map/ppermute | solution.py:504
  73.1 2.3 %hidden_units.3 = (bf16[2,512,256]{2,1,0:T(8,128)(2,1)S(1)}, f32[2,512,256]{2,1,0:T(8,128)S(1)}, bf16[2,512,256]{2,1,0:T(8,128)(2,1)S(1)}, bf16[256,256]{1,0:T(8,128)(2,1)S(1)}, bf16[256,256]{1,0:T(8,128)(2,1)S(1)}) custom-call(s32[5]{0:T(128)S(1)} %stack.23.refs_0_.refs_1_, f32[2,512,256]{2,1,0:T(8,128)S(1)} %forward_encoder.7.refs_1_, ...), custom_call_target="tpu_custom_call" | custom-call | bytes 12324864 | tf_op jit(solution)/shard_map/hidden_units/pallas_call | solution.py:60
  75.5 3.4 %collective-permute-done.24.refs_0_ = bf16[768,256]{1,0:T(8,128)(2,1)S(1)} collective-permute-done((bf16[768,256]{1,0:T(8,128)(2,1)S(1)}, bf16[768,256]{1,0:T(8,128)(2,1)S(1)}, u32[]{:S(2)}, u32[]{:S(2)}) %collective-permute-start.24) | collective-permute-done | bytes 393248 | tf_op jit(solution)/shard_map/ppermute | solution.py:504
  81.8 3.0 %forward_decoder.3 = (f32[2,512,256]{2,1,0:T(8,128)S(1)}, f32[256,256]{1,0:T(8,128)S(1)}) custom-call(s32[5]{0:T(128)S(1)} %stack.23.refs_0_.refs_1_, bf16[1024,256]{1,0:T(8,128)(2,1)S(1)} %get-tuple-element.95.refs_8_.refs_1_, bf16[1024,256]{1,0:T(8,128)(2,1)S(1)} %collective-permute-done.23.refs_2_, ...), custom_call_target="tpu_custom_call" | custom-call | bytes 11272192 | tf_op jit(solution)/shard_map/forward_decoder/pallas_call | solution.py:60
  84.8 2.0 %slope_pre.3.refs_2_ = bf16[2,512,256]{2,1,0:T(8,128)(2,1)S(1)} custom-call(s32[5]{0:T(128)S(1)} %stack.23.refs_0_.refs_1_, f32[2,512,256]{2,1,0:T(8,128)S(1)} %get-tuple-element.106.refs_1_, f32[256,256]{1,0:T(8,128)S(1)} %get-tuple-element.107.refs_2_, bf16[2,512,256]{2,1,0:T(8,128)(2,1)S(1)} %get-tuple-element.108.refs_3_, ...), custom_call_target="tpu_custom_call" | custom-call | bytes 12320768 | tf_op jit(solution)/shard_map/slope_pre/pallas_call | solution.py:60
  91.6 7.2 %collective-permute-done.34.refs_5_.refs_3_ = bf16[256,256]{1,0:T(8,128)(2,1)S(1)} collective-permute-done((bf16[256,256]{1,0:T(8,128)(2,1)S(1)}, bf16[256,256]{1,0:T(8,128)(2,1)S(1)}, u32[]{:S(2)}, u32[]{:S(2)}) %collective-permute-start.34) | collective-permute-done | bytes 131104 | tf_op jit(solution)/shard_map/ppermute | solution.py:506
  101.6 3.2 %adam_rows.12 = (f32[8,128]{1,0:T(8,128)}, f32[1,2,1024,256]{3,2,1,0:T(8,128)}, f32[1,2,1024,256]{3,2,1,0:T(8,128)}, f32[1,2,1024,256]{3,2,1,0:T(8,128)}) custom-call(s32[8]{0:T(128)S(1)} %copy-done.7, f32[1024,256]{1,0:T(8,128)S(1)} %decoder_grad.11.refs_3_.refs_1_, bf16[768,256]{1,0:T(8,128)(2,1)S(1)} %collective-permute-done.33.refs_4_.refs_2_, ...), custom_call_target="tpu_custom_call" | custom-call | bytes 12062720 | tf_op jit(solution)/shard_map/adam_rows/pallas_call | solution.py:60
  104.8 2.0 %adam_rows.13 = (f32[1,2,1024,256]{3,2,1,0:T(8,128)}, f32[1,2,1024,256]{3,2,1,0:T(8,128)}, f32[1,2,1024,256]{3,2,1,0:T(8,128)}) custom-call(s32[8]{0:T(128)S(1)} %copy-done.7, f32[512,256]{1,0:T(8,128)S(1)} %encoder_grad.19.refs_3_.refs_1_, ...), custom_call_target="tpu_custom_call", output_to_operand_aliasing={{0}: (7, {}), {1}: (8, {}), {2}: (9, {})} | custom-call | bytes 15466496 | tf_op jit(solution)/shard_map/adam_rows/pallas_call | solution.py:60
  106.8 1.6 %adam_rows.14 = (f32[1,2,1024,256]{3,2,1,0:T(8,128)}, f32[1,2,1024,256]{3,2,1,0:T(8,128)}, f32[1,2,1024,256]{3,2,1,0:T(8,128)}) custom-call(s32[8]{0:T(128)S(1)} %copy-done.7, f32[256,256]{1,0:T(8,128)S(1)} %encoder_grad.20.refs_3_.refs_1_, ...), custom_call_target="tpu_custom_call", output_to_operand_aliasing={{0}: (7, {}), {1}: (8, {}), {2}: (9, {})} | custom-call | bytes 14024704 | tf_op jit(solution)/shard_map/adam_rows/pallas_call | solution.py:60
  108.3 1.6 %adam_rows.15 = (f32[1,2,1024,256]{3,2,1,0:T(8,128)}, f32[1,2,1024,256]{3,2,1,0:T(8,128)}, f32[1,2,1024,256]{3,2,1,0:T(8,128)}) custom-call(s32[8]{0:T(128)S(1)} %copy-done.7, f32[256,256]{1,0:T(8,128)S(1)} %encoder_grad.21.refs_7_.refs_1_, ...), custom_call_target="tpu_custom_call", output_to_operand_aliasing={{0}: (7, {}), {1}: (8, {}), {2}: (9, {})} | custom-call | bytes 14024704 | tf_op jit(solution)/shard_map/adam_rows/pallas_call | solution.py:60
  (123 shorter events, 45.7 us)
Async XLA Ops:
  0.6 15.5 %collective-permute-start = (bf16[512,4096]{1,0:T(8,128)(2,1)}, bf16[512,4096]{1,0:T(8,128)(2,1)}, u32[]{:S(2)}, u32[]{:S(2)}) collective-permute-start(bf16[512,4096]{1,0:T(8,128)(2,1)} %refs_8_.3), channel_id=1, source_target_pairs={{0,1},{1,0},{2,3},{3,2},{4,5},{5,4},{6,7},{7,6},{8,9},{9,8},{10,11... | collective-permute-start | bytes 12582920 | tf_op jit(solution)/shard_map/ppermute | solution.py:503
  3.0 11.7 %collective-permute-start.7 = (bf16[1024,256]{1,0:T(8,128)(2,1)S(1)}, bf16[1024,256]{1,0:T(8,128)(2,1)S(1)}, u32[]{:S(2)}, u32[]{:S(2)}) collective-permute-start(bf16[1024,256]{1,0:T(8,128)(2,1)S(1)} %get-tuple-element.71.refs_4_.refs_1_), channel_id=1, source_target_pairs={{0,1},{1,0},{2,3},{3,2},{4,5},{5,4},{6,7},{7,6},{8,9},{9,8},{10,11... | collective-permute-start | bytes 1572872 | tf_op jit(solution)/shard_map/ppermute | solution.py:503
  3.1 19.6 %collective-permute-start.8 = (bf16[1024,256]{1,0:T(8,128)(2,1)S(1)}, bf16[1024,256]{1,0:T(8,128)(2,1)S(1)}, u32[]{:S(2)}, u32[]{:S(2)}) collective-permute-start(bf16[1024,256]{1,0:T(8,128)(2,1)S(1)} %get-tuple-element.71.refs_4_.refs_1_), channel_id=1, source_target_pairs={{2,0},{3,1},{0,2},{1,3},{6,4},{7,5},{4,6},{5,7},{10,8},{11,9},{8,1... | collective-permute-start | bytes 1572872 | tf_op jit(solution)/shard_map/ppermute | solution.py:504
  8.4 13.7 %collective-permute-start.2 = (bf16[256,256]{1,0:T(8,128)(2,1)S(1)}, bf16[256,256]{1,0:T(8,128)(2,1)S(1)}, u32[]{:S(2)}, u32[]{:S(2)}) collective-permute-start(bf16[256,256]{1,0:T(8,128)(2,1)S(1)} %get-tuple-element.74), channel_id=1, source_target_pairs={{0,8},{4,12},{8,0},{12,4},{16,24},{20,28},{24,16},{28,20},{1,9},{5... | collective-permute-start | bytes 393224 | tf_op jit(solution)/shard_map/ppermute | solution.py:508
  12.1 10.0 %collective-permute-start.3 = (bf16[256,256]{1,0:T(8,128)(2,1)S(1)}, bf16[256,256]{1,0:T(8,128)(2,1)S(1)}, u32[]{:S(2)}, u32[]{:S(2)}) collective-permute-start(bf16[256,256]{1,0:T(8,128)(2,1)S(1)} %get-tuple-element.75), channel_id=1, source_target_pairs={{0,12},{4,8},{8,4},{12,0},{16,28},{20,24},{24,20},{28,16},{1,13},{... | collective-permute-start | bytes 393224 | tf_op jit(solution)/shard_map/ppermute | solution.py:508
  14.6 13.2 %collective-permute-start.6 = (bf16[768,256]{1,0:T(8,128)(2,1)S(1)}, bf16[768,256]{1,0:T(8,128)(2,1)S(1)}, u32[]{:S(2)}, u32[]{:S(2)}) collective-permute-start(bf16[768,256]{1,0:T(8,128)(2,1)S(1)} %get-tuple-element.77.refs_5_), channel_id=1, source_target_pairs={{2,0},{3,1},{0,2},{1,3},{6,4},{7,5},{4,6},{5,7},{10,8},{11,9},{8,1... | collective-permute-start | bytes 1179656 | tf_op jit(solution)/shard_map/ppermute | solution.py:504
  16.2 14.7 %collective-permute-start.5 = (bf16[1024,256]{1,0:T(8,128)(2,1)S(1)}, bf16[1024,256]{1,0:T(8,128)(2,1)S(1)}, u32[]{:S(2)}, u32[]{:S(2)}) collective-permute-start(bf16[1024,256]{1,0:T(8,128)(2,1)S(1)} %get-tuple-element.76.refs_1_), channel_id=1, source_target_pairs={{0,1},{1,0},{2,3},{3,2},{4,5},{5,4},{6,7},{7,6},{8,9},{9,8},{10,11... | collective-permute-start | bytes 1572872 | tf_op jit(solution)/shard_map/ppermute | solution.py:503
  23.4 7.3 %collective-permute-start.11 = (bf16[256,256]{1,0:T(8,128)(2,1)S(1)}, bf16[256,256]{1,0:T(8,128)(2,1)S(1)}, u32[]{:S(2)}, u32[]{:S(2)}) collective-permute-start(bf16[256,256]{1,0:T(8,128)(2,1)S(1)} %get-tuple-element.84.refs_6_), channel_id=1, source_target_pairs={{2,0},{3,1},{0,2},{1,3},{6,4},{7,5},{4,6},{5,7},{10,8},{11,9},{8,1... | collective-permute-start | bytes 393224 | tf_op jit(solution)/shard_map/ppermute | solution.py:504
  28.6 17.0 %collective-permute-start.18 = (bf16[768,256]{1,0:T(8,128)(2,1)S(1)}, bf16[768,256]{1,0:T(8,128)(2,1)S(1)}, u32[]{:S(2)}, u32[]{:S(2)}) collective-permute-start(bf16[768,256]{1,0:T(8,128)(2,1)S(1)} %decoder_grad.6.refs_2_.refs_6_), channel_id=1, source_target_pairs={{0,2},{1,3},{2,0},{3,1},{4,6},{5,7},{6,4},{7,5},{8,10},{9,11},{10,... | collective-permute-start | bytes 1179656 | tf_op jit(solution)/shard_map/ppermute | solution.py:506
  30.8 10.7 %collective-permute-start.4 = (bf16[256,256]{1,0:T(8,128)(2,1)S(1)}, bf16[256,256]{1,0:T(8,128)(2,1)S(1)}, u32[]{:S(2)}, u32[]{:S(2)}) collective-permute-start(bf16[256,256]{1,0:T(8,128)(2,1)S(1)} %add_quarters.2.refs_3_.refs_1_), channel_id=1, source_target_pairs={{0,16},{4,20},{8,24},{12,28},{16,0},{20,4},{24,8},{28,12},{1,17},{... | collective-permute-start | bytes 393224 | tf_op jit(solution)/shard_map/ppermute | solution.py:508
  36.9 8.3 %collective-permute-start.19 = (bf16[256,256]{1,0:T(8,128)(2,1)S(1)}, bf16[256,256]{1,0:T(8,128)(2,1)S(1)}, u32[]{:S(2)}, u32[]{:S(2)}) collective-permute-start(bf16[256,256]{1,0:T(8,128)(2,1)S(1)} %decoder_grad.7.refs_8_.refs_3_), channel_id=1, source_target_pairs={{0,2},{1,3},{2,0},{3,1},{4,6},{5,7},{6,4},{7,5},{8,10},{9,11},{10,... | collective-permute-start | bytes 393224 | tf_op jit(solution)/shard_map/ppermute | solution.py:506
  39.9 12.3 %collective-permute-start.22 = (bf16[512,256]{1,0:T(8,128)(2,1)S(1)}, bf16[512,256]{1,0:T(8,128)(2,1)S(1)}, u32[]{:S(2)}, u32[]{:S(2)}) collective-permute-start(bf16[512,256]{1,0:T(8,128)(2,1)S(1)} %encoder_grad.12.refs_3_), channel_id=1, source_target_pairs={{0,2},{1,3},{2,0},{3,1},{4,6},{5,7},{6,4},{7,5},{8,10},{9,11},{10,... | collective-permute-start | bytes 786440 | tf_op jit(solution)/shard_map/ppermute | solution.py:506
  46.0 8.0 %collective-permute-start.21 = (bf16[256,256]{1,0:T(8,128)(2,1)S(1)}, bf16[256,256]{1,0:T(8,128)(2,1)S(1)}, u32[]{:S(2)}, u32[]{:S(2)}) collective-permute-start(bf16[256,256]{1,0:T(8,128)(2,1)S(1)} %encoder_grad.13.refs_3_), channel_id=1, source_target_pairs={{0,2},{1,3},{2,0},{3,1},{4,6},{5,7},{6,4},{7,5},{8,10},{9,11},{10,... | collective-permute-start | bytes 393224 | tf_op jit(solution)/shard_map/ppermute | solution.py:506
  47.2 7.6 %collective-permute-start.20 = (bf16[256,256]{1,0:T(8,128)(2,1)S(1)}, bf16[256,256]{1,0:T(8,128)(2,1)S(1)}, u32[]{:S(2)}, u32[]{:S(2)}) collective-permute-start(bf16[256,256]{1,0:T(8,128)(2,1)S(1)} %encoder_grad.14.refs_3_), channel_id=1, source_target_pairs={{0,2},{1,3},{2,0},{3,1},{4,6},{5,7},{6,4},{7,5},{8,10},{9,11},{10,... | collective-permute-start | bytes 393224 | tf_op jit(solution)/shard_map/ppermute | solution.py:506
  55.6 8.4 %collective-permute-start.25 = (bf16[1024,256]{1,0:T(8,128)(2,1)S(1)}, bf16[1024,256]{1,0:T(8,128)(2,1)S(1)}, u32[]{:S(2)}, u32[]{:S(2)}) collective-permute-start(bf16[1024,256]{1,0:T(8,128)(2,1)S(1)} %get-tuple-element.93.refs_7_.refs_3_.refs_1_), channel_id=1, source_target_pairs={{0,1},{1,0},{2,3},{3,2},{4,5},{5,4},{6,7},{7,6},{8,9},{9,8},{10,11... | collective-permute-start | bytes 1572872 | tf_op jit(solution)/shard_map/ppermute | solution.py:503
  55.7 14.8 %collective-permute-start.26 = (bf16[1024,256]{1,0:T(8,128)(2,1)S(1)}, bf16[1024,256]{1,0:T(8,128)(2,1)S(1)}, u32[]{:S(2)}, u32[]{:S(2)}) collective-permute-start(bf16[1024,256]{1,0:T(8,128)(2,1)S(1)} %get-tuple-element.93.refs_7_.refs_3_.refs_1_), channel_id=1, source_target_pairs={{2,0},{3,1},{0,2},{1,3},{6,4},{7,5},{4,6},{5,7},{10,8},{11,9},{8,1... | collective-permute-start | bytes 1572872 | tf_op jit(solution)/shard_map/ppermute | solution.py:504
  59.6 19.3 %collective-permute-start.24 = (bf16[768,256]{1,0:T(8,128)(2,1)S(1)}, bf16[768,256]{1,0:T(8,128)(2,1)S(1)}, u32[]{:S(2)}, u32[]{:S(2)}) collective-permute-start(bf16[768,256]{1,0:T(8,128)(2,1)S(1)} %get-tuple-element.96.refs_5_), channel_id=1, source_target_pairs={{2,0},{3,1},{0,2},{1,3},{6,4},{7,5},{4,6},{5,7},{10,8},{11,9},{8,1... | collective-permute-start | bytes 1179656 | tf_op jit(solution)/shard_map/ppermute | solution.py:504
  60.9 20.8 %collective-permute-start.23 = (bf16[1024,256]{1,0:T(8,128)(2,1)S(1)}, bf16[1024,256]{1,0:T(8,128)(2,1)S(1)}, u32[]{:S(2)}, u32[]{:S(2)}) collective-permute-start(bf16[1024,256]{1,0:T(8,128)(2,1)S(1)} %get-tuple-element.95.refs_8_.refs_1_), channel_id=1, source_target_pairs={{0,1},{1,0},{2,3},{3,2},{4,5},{5,4},{6,7},{7,6},{8,9},{9,8},{10,11... | collective-permute-start | bytes 1572872 | tf_op jit(solution)/shard_map/ppermute | solution.py:503
  71.1 10.2 %collective-permute-start.29 = (bf16[256,256]{1,0:T(8,128)(2,1)S(1)}, bf16[256,256]{1,0:T(8,128)(2,1)S(1)}, u32[]{:S(2)}, u32[]{:S(2)}) collective-permute-start(bf16[256,256]{1,0:T(8,128)(2,1)S(1)} %get-tuple-element.103.refs_6_), channel_id=1, source_target_pairs={{2,0},{3,1},{0,2},{1,3},{6,4},{7,5},{4,6},{5,7},{10,8},{11,9},{8,1... | collective-permute-start | bytes 393224 | tf_op jit(solution)/shard_map/ppermute | solution.py:504
  79.7 19.1 %collective-permute-start.33 = (bf16[768,256]{1,0:T(8,128)(2,1)S(1)}, bf16[768,256]{1,0:T(8,128)(2,1)S(1)}, u32[]{:S(2)}, u32[]{:S(2)}) collective-permute-start(bf16[768,256]{1,0:T(8,128)(2,1)S(1)} %decoder_grad.9.refs_2_.refs_6_), channel_id=1, source_target_pairs={{0,2},{1,3},{2,0},{3,1},{4,6},{5,7},{6,4},{7,5},{8,10},{9,11},{10,... | collective-permute-start | bytes 1179656 | tf_op jit(solution)/shard_map/ppermute | solution.py:506
  87.2 17.5 %collective-permute-start.37 = (bf16[512,256]{1,0:T(8,128)(2,1)S(1)}, bf16[512,256]{1,0:T(8,128)(2,1)S(1)}, u32[]{:S(2)}, u32[]{:S(2)}) collective-permute-start(bf16[512,256]{1,0:T(8,128)(2,1)S(1)} %encoder_grad.18.refs_3_), channel_id=1, source_target_pairs={{0,2},{1,3},{2,0},{3,1},{4,6},{5,7},{6,4},{7,5},{8,10},{9,11},{10,... | collective-permute-start | bytes 786440 | tf_op jit(solution)/shard_map/ppermute | solution.py:506
  88.4 10.4 %collective-permute-start.34 = (bf16[256,256]{1,0:T(8,128)(2,1)S(1)}, bf16[256,256]{1,0:T(8,128)(2,1)S(1)}, u32[]{:S(2)}, u32[]{:S(2)}) collective-permute-start(bf16[256,256]{1,0:T(8,128)(2,1)S(1)} %decoder_grad.10.refs_8_.refs_3_), channel_id=1, source_target_pairs={{0,2},{1,3},{2,0},{3,1},{4,6},{5,7},{6,4},{7,5},{8,10},{9,11},{10,... | collective-permute-start | bytes 393224 | tf_op jit(solution)/shard_map/ppermute | solution.py:506
  99.1 7.6 %collective-permute-start.36 = (bf16[256,256]{1,0:T(8,128)(2,1)S(1)}, bf16[256,256]{1,0:T(8,128)(2,1)S(1)}, u32[]{:S(2)}, u32[]{:S(2)}) collective-permute-start(bf16[256,256]{1,0:T(8,128)(2,1)S(1)} %encoder_grad.22.refs_3_), channel_id=1, source_target_pairs={{0,2},{1,3},{2,0},{3,1},{4,6},{5,7},{6,4},{7,5},{8,10},{9,11},{10,... | collective-permute-start | bytes 393224 | tf_op jit(solution)/shard_map/ppermute | solution.py:506
  100.6 7.8 %collective-permute-start.35 = (bf16[256,256]{1,0:T(8,128)(2,1)S(1)}, bf16[256,256]{1,0:T(8,128)(2,1)S(1)}, u32[]{:S(2)}, u32[]{:S(2)}) collective-permute-start(bf16[256,256]{1,0:T(8,128)(2,1)S(1)} %encoder_grad.23.refs_8_), channel_id=1, source_target_pairs={{0,2},{1,3},{2,0},{3,1},{4,6},{5,7},{6,4},{7,5},{8,10},{9,11},{10,... | collective-permute-start | bytes 393224 | tf_op jit(solution)/shard_map/ppermute | solution.py:506
  (23 other events, 100.0 us)

commit v16 on v15

--- a/solution.py
+++ b/solution.py
@@ -372,10 +372,10 @@
         ins.append((new_anc, once((cr, width), lambda g, m: (i, 0))))
         if prev is not None:
             for n, p in enumerate(prev):
-                aliases[1 + len(ins)] = n
+                aliases[1 + len(ins)] = n + (k == 1)
                 ins.append((p, pl.BlockSpec(memory_space=pl.ANY)))
         outs = [(sds(full, f32), once(block, lambda g, m: (0, k, i, 0)))] * 3
-        if prev is None:
+        if k == 1:
             outs = [(sds((8, 128), f32), whole((8, 128)))] + outs
     else:
         if lows is not None:
@@ -452,17 +452,23 @@
     )[0]
 
 
-def mix_body(k, sizes, plan, new_anc, theta, low, *parts):
-    value = mixed(plan, k, theta[0, 0], new_anc[...]).astype(bf16)
-    low[...] = value
-    put_parts(value, sizes, parts)
-
-
-def mix_rows(plan, new_anc, k, theta, sizes, after):
+def mix_body(k, count, plan, new_anc, *refs):
+    thetas, low, parts = refs[:count], refs[count], refs[count + 1:]
+    off = 0
+    for theta, part in zip(thetas, parts):
+        size = part.shape[0]
+        value = mixed(plan, k, theta[0, 0], new_anc[off:off + size, :]).astype(bf16)
+        low[off:off + size, :] = value
+        part[...] = value
+        off += size
+
+
+def mix_rows(plan, new_anc, k, thetas, after):
     rows, width = new_anc.shape
-    shapes = [(rows, width)] + [(size, width) for size in sizes]
-    return call(
-        functools.partial(mix_body, k, sizes), "mix_rows", (plan,), [(a, whole(a.shape)) for a in (new_anc, theta)],
+    shapes = [(rows, width)] + [theta.shape[2:] for theta in thetas]
+    return call(
+        functools.partial(mix_body, k, len(thetas)), "mix_rows", (plan,),
+        [(a, whole(a.shape)) for a in [new_anc, *thetas]],
         [(sds(shape, bf16), whole(shape)) for shape in shapes], after=after,
     )
 
@@ -520,7 +526,9 @@
     own = outer_add(plan, [quarters[0]] + [across(quarters[m], m) for m in range(1, 4)], n_rep == 4, xt)
 
     half, rest = (rows // 2, rows // 4) if rows >= 1024 else (rows, rows)
-    blocks = [(1, 0, rows), (0, 0, half)] + [(0, off, rest) for off in range(half, rows, rest)]
+    dec_blocks = [(1, off, size) for off, size in zip(starts, sizes)]
+    enc_blocks = [(0, 0, half)] + [(0, off, rest) for off in range(half, rows, rest)]
+    blocks = dec_blocks + enc_blocks
     state = {key: (weights, first_moment, second_moment) for key in blocks}
     state_at = {(k, off, size): (k, off // size) for k, off, size in blocks}
     new_anc = None
@@ -559,7 +567,6 @@
         sent = []
         got = {key: [] for key in blocks}
         part, pending = [], []
-        back = {}
         for n, far in enumerate(dec_far):
             pieces, handed = take(far, starts[n], [counted] + sent[-1:])
             part += pieces
@@ -567,8 +574,8 @@
             for s in others:
                 rows_in = [p[0] for p in pieces if p[1] == 1 + s]
                 sent.append(dec_grad(s * rows + starts[n], sizes[n], rows_in, bf16, sent[-1:]))
-                back[s, n] = give(sent[-1], s)
-        back = [back[key] for key in sorted(back)]
+                got[dec_blocks[n]].append(give(sent[-1], s))
+        back = [g for key in dec_blocks for g in got[key]]
 
         carry = forward(
             pos, [], [(dec, 1, 0, rows), (dec_near, 1 + chips, 0, rows)] + part, xs, rows, True, sent[-1:])
@@ -578,9 +585,9 @@
             *more, after=after)
         prev = None
         mine = {}
-        own_dec = lambda after: dec_grad(0, rows, dec_parts, f32, after)
-        for n, key in enumerate(blocks[1:]):
-            hold = back if n == 1 else []
+        own_dec = lambda n, after: dec_grad(starts[n], sizes[n], [dec_parts[n]], f32, after)
+        hold = []
+        for n, key in enumerate(enc_blocks):
             for s in others:
                 sent.append(enc_grad(s, *key[1:], bf16, sent[-1:] + hold))
                 got[key].append(give(sent[-1], s))
@@ -590,32 +597,36 @@
                     own = outer_add(plan, [own, across(own, bit)], 2 * bit == n_rep, sent[-1:])
                     bit *= 2
                 sent.append(own)
-            if n == (0 if last else len(blocks) - 2):
-                for other in blocks[1:]:
+            hold = back if n == 0 and not last else []
+            if n == (0 if last else len(enc_blocks) - 1):
+                for other in enc_blocks:
                     mine[other] = enc_grad(0, *other[1:], f32, sent[-1:])
                     sent.append(mine[other])
-                if last:
-                    mine[blocks[0]] = own_dec(sent[-1:])
-                    sent.append(mine[blocks[0]])
-        got[blocks[0]] = back
-        if last:
-            token, *prev = adam(blocks[0], None, after=sent[-1:])
+            if last:
+                for m, other in enumerate(dec_blocks):
+                    if n == 0:
+                        mine[other] = own_dec(m, sent[-1:])
+                        sent.append(mine[other])
+                for other in dec_blocks[n:n + 1]:
+                    token, *prev = adam(other, prev, after=sent[-1:])
+                    sent.append(token)
 
         if not last:
             quarters = [own] + [across(own, m) for m in range(1, 4)]
             new_anc = outer_anchor(pos, plan, anchor, momentum, quarters, sent[-1:])
         new_state, lows = {}, []
         if last:
-            for key in blocks[1:]:
+            for key in enc_blocks:
                 prev = adam(key, prev)
         else:
-            for key in blocks[1:]:
+            for key in enc_blocks:
                 enc, *new_state[key] = adam(key, None, lows)
                 lows = [enc]
             enc_parts = [enc]
-            mine[blocks[0]] = own_dec([enc])
-            new_state[blocks[0]] = adam(blocks[0], None, after=[enc])
-            dec, *dec_parts = mix_rows(plan, new_anc, 1, new_state[blocks[0]][0], sizes, [enc])
+            for n, key in enumerate(dec_blocks):
+                mine[key] = own_dec(n, [enc])
+                new_state[key] = adam(key, None, after=[enc])
+            dec, *dec_parts = mix_rows(plan, new_anc, 1, [new_state[key][0] for key in dec_blocks], [enc])
             anchor_out, momentum_out, token = outer_end(pos, plan, anchor, momentum, quarters, [dec])
             state, state_at = new_state, {key: (0, 0) for key in blocks}
     return (*prev, anchor_out, momentum_out)

time: 110 us -> 110 us (level)
  waiting for transfers between devices: 19.9 us -> 15.6 us
  local copies, waits for them, and re-layouts: 2.27 us -> 4.1 us
  Pallas kernels: 53.1 us -> 54.9 us
    ppermute x10, waiting for transfers between devices: 7.21 us -> 4.07 us  [local(): lax.ppermute(a, 'fsdp', [(f, (f // 2 + s) % chips * 2 + f % 2) for f in r...]
    unnamed x18, local copies, waits for them, and re-layouts: 2.19 us -> 4.02 us
    pallas_call x52 -> x56, Pallas kernels: 53.1 us -> 54.9 us  [call(): pl.pallas_call(run, name=name, out_shape=[o for o, _ in outs], grid_spec=...]
    ppermute x6, waiting for transfers between devices: 8.34 us -> 6.61 us  [local(): lax.ppermute(a, 'fsdp', [((f // 2 + s) % chips * 2 + f % 2, f) for f in r...]
  transfers between devices with their start and end apart: 38 -> 38, of which waited for: 8 -> 6; matrix products, arithmetic and copies ran while one was open for 0% -> 0% of each run, Pallas kernels for 46% -> 48%
where the time goes in v16:
time: 110 us
  Pallas kernels  54.9 us (50%)
  starting transfers between devices  34.2 us (31%)
  waiting for transfers between devices  15.6 us (14%)
  local copies, waits for them, and re-layouts  4.1 us (4%)
  between operations  1.2 us (1%)
    pallas_call x56, Pallas kernels, call(): pl.pallas_call(run, name=name, out_shape=[o for o, _ in outs], grid_spec=...  54.9 us
    ppermute x7, starting transfers between devices, local(): lax.ppermute(a, 'replica', [(r, r ^ bit) for r in range(n_rep)])  11.9 us
    ppermute x10, starting transfers between devices, local(): lax.ppermute(a, 'fsdp', [(f, (f // 2 + s) % chips * 2 + f % 2) for f in r...  10.5 us
    ppermute x6, starting transfers between devices, local(): lax.ppermute(a, 'fsdp', [((f // 2 + s) % chips * 2 + f % 2, f) for f in r...  8.66 us
    ppermute x6, waiting for transfers between devices, local(): lax.ppermute(a, 'fsdp', [((f // 2 + s) % chips * 2 + f % 2, f) for f in r...  6.61 us
    ppermute x7, waiting for transfers between devices, local(): lax.ppermute(a, 'replica', [(r, r ^ bit) for r in range(n_rep)])  4.86 us
    ppermute x10, waiting for transfers between devices, local(): lax.ppermute(a, 'fsdp', [(f, (f // 2 + s) % chips * 2 + f % 2) for f in r...  4.07 us
    unnamed x18, local copies, waits for them, and re-layouts  4.02 us
  transfers between devices with their start and end apart: 38, of which 6 were waited for; matrix products, arithmetic and copies ran while one was open for 0% of the time, Pallas kernels for 48%

profile of v16, /device:TPU:0, one launch (start us, length us, event | category | flops | bytes accessed | tf_op | source)
XLA Modules:
  0.0 110.0 jit_solution(13903717853799443060)
XLA Ops:
  1.2 1.6 %copy-done.1 = f32[1,2,1024,256]{3,2,1,0:T(8,128)S(1)} copy-done((f32[1,2,1024,256]{3,2,1,0:T(8,128)S(1)}, f32[1,2,1024,256]{3,2,1,0:T(8,128)}, u32[]{:S(2)}) %copy-start.1) | copy-done | bytes 2097176
  3.1 3.0 %collective-permute-start.8 = (bf16[1024,256]{1,0:T(8,128)(2,1)S(1)}, bf16[1024,256]{1,0:T(8,128)(2,1)S(1)}, u32[]{:S(2)}, u32[]{:S(2)}) collective-permute-start(bf16[1024,256]{1,0:T(8,128)(2,1)S(1)} %get-tuple-element.79.refs_4_.refs_1_), channel_id=1, source_target_pairs={{2,0},{3,1},{0,2},{1,3},{6,4},{7,5},{4,6},{5,7},{10,8},{11,9},{8,1... | collective-permute-start | bytes 1572872 | tf_op jit(solution)/shard_map/ppermute | solution.py:510
  9.9 2.1 %collective-permute-done.1.refs_2_ = bf16[256,256]{1,0:T(8,128)(2,1)S(1)} collective-permute-done((bf16[256,256]{1,0:T(8,128)(2,1)S(1)}, bf16[256,256]{1,0:T(8,128)(2,1)S(1)}, u32[]{:S(2)}, u32[]{:S(2)}) %collective-permute-start.1) | collective-permute-done | bytes 131104 | tf_op jit(solution)/shard_map/ppermute | solution.py:514
  12.1 2.6 %collective-permute-start.3 = (bf16[256,256]{1,0:T(8,128)(2,1)S(1)}, bf16[256,256]{1,0:T(8,128)(2,1)S(1)}, u32[]{:S(2)}, u32[]{:S(2)}) collective-permute-start(bf16[256,256]{1,0:T(8,128)(2,1)S(1)} %get-tuple-element.83), channel_id=1, source_target_pairs={{0,12},{4,8},{8,4},{12,0},{16,28},{20,24},{24,20},{28,16},{1,13},{... | collective-permute-start | bytes 393224 | tf_op jit(solution)/shard_map/ppermute | solution.py:514
  17.3 2.9 %stage_tokens.1 = (bf16[512,4096]{1,0:T(8,128)(2,1)S(1)}, bf16[2048,512]{1,0:T(8,128)(2,1)S(1)}) custom-call(s32[5]{0:T(128)S(1)} %stack.23.refs_0_.refs_1_, bf16[512,4096]{1,0:T(8,128)(2,1)} %collective-permute-done.refs_1_), custom_call_target="tpu_custom_call" | custom-call | bytes 10485760 | tf_op jit(solution)/shard_map/stage_tokens/pallas_call | solution.py:60
  20.3 1.8 %forward_encoder.4.refs_2_.refs_1_ = f32[2,512,256]{2,1,0:T(8,128)S(1)} custom-call(s32[5]{0:T(128)S(1)} %stack.23.refs_0_.refs_1_, bf16[1024,256]{1,0:T(8,128)(2,1)S(1)} %get-tuple-element.79.refs_4_.refs_1_, bf16[1024,256]{1,0:T(8,128)(2,1)S(1)} %collective-permute-done.7.refs_2_, bf16[512,4096]{1,0:T(8,128)(2,1)S(1)} %copy-done, ...), custom_call_target="tpu_custom_call" | custom-call | bytes 10485760 | tf_op jit(solution)/shard_map/forward_encoder/pallas_call | solution.py:60
  25.4 2.4 %hidden_units.2 = (bf16[2,512,256]{2,1,0:T(8,128)(2,1)S(1)}, f32[2,512,256]{2,1,0:T(8,128)S(1)}, bf16[2,512,256]{2,1,0:T(8,128)(2,1)S(1)}, bf16[256,256]{1,0:T(8,128)(2,1)S(1)}, bf16[256,256]{1,0:T(8,128)(2,1)S(1)}) custom-call(s32[5]{0:T(128)S(1)} %stack.23.refs_0_.refs_1_, f32[2,512,256]{2,1,0:T(8,128)S(1)} %forward_encoder.5.refs_1_, ...), custom_call_target="tpu_custom_call" | custom-call | bytes 12333056 | tf_op jit(solution)/shard_map/hidden_units/pallas_call | solution.py:60
  28.7 1.6 %collective-permute-start.18 = (bf16[768,256]{1,0:T(8,128)(2,1)S(1)}, bf16[768,256]{1,0:T(8,128)(2,1)S(1)}, u32[]{:S(2)}, u32[]{:S(2)}) collective-permute-start(bf16[768,256]{1,0:T(8,128)(2,1)S(1)} %decoder_grad.8.refs_2_.refs_6_), channel_id=1, source_target_pairs={{0,2},{1,3},{2,0},{3,1},{4,6},{5,7},{6,4},{7,5},{8,10},{9,11},{10,... | collective-permute-start | bytes 1179656 | tf_op jit(solution)/shard_map/ppermute | solution.py:512
  30.9 2.7 %collective-permute-start.4 = (bf16[256,256]{1,0:T(8,128)(2,1)S(1)}, bf16[256,256]{1,0:T(8,128)(2,1)S(1)}, u32[]{:S(2)}, u32[]{:S(2)}) collective-permute-start(bf16[256,256]{1,0:T(8,128)(2,1)S(1)} %add_quarters.2.refs_3_.refs_1_), channel_id=1, source_target_pairs={{0,16},{4,20},{8,24},{12,28},{16,0},{20,4},{24,8},{28,12},{1,17},{... | collective-permute-start | bytes 393224 | tf_op jit(solution)/shard_map/ppermute | solution.py:514
  33.9 3.0 %forward_decoder.2 = (f32[2,512,256]{2,1,0:T(8,128)S(1)}, f32[256,256]{1,0:T(8,128)S(1)}) custom-call(s32[5]{0:T(128)S(1)} %stack.23.refs_0_.refs_1_, bf16[1024,256]{1,0:T(8,128)(2,1)S(1)} %get-tuple-element.84.refs_1_, bf16[1024,256]{1,0:T(8,128)(2,1)S(1)} %collective-permute-done.5.refs_2_, bf16[384,256]{1,0:T(8,128)(2,1)S(1)} %get-tuple-element.90.refs_5_.refs_3_, ...), custom_call_target="tpu_custom_call" | custom-call | bytes 11272192 | tf_op jit(solution)/shard_map/forward_decoder/pallas_call | solution.py:60
  37.5 2.0 %slope_pre.2.refs_2_ = bf16[2,512,256]{2,1,0:T(8,128)(2,1)S(1)} custom-call(s32[5]{0:T(128)S(1)} %stack.23.refs_0_.refs_1_, f32[2,512,256]{2,1,0:T(8,128)S(1)} %get-tuple-element.95.refs_1_, f32[256,256]{1,0:T(8,128)S(1)} %get-tuple-element.96.refs_2_, bf16[2,512,256]{2,1,0:T(8,128)(2,1)S(1)} %get-tuple-element.97.refs_3_, ...), custom_call_target="tpu_custom_call" | custom-call | bytes 12320768 | tf_op jit(solution)/shard_map/slope_pre/pallas_call | solution.py:60
  42.1 2.5 %collective-permute-start.17 = (bf16[256,256]{1,0:T(8,128)(2,1)S(1)}, bf16[256,256]{1,0:T(8,128)(2,1)S(1)}, u32[]{:S(2)}, u32[]{:S(2)}) collective-permute-start(bf16[256,256]{1,0:T(8,128)(2,1)S(1)} %add_quarters.3.refs_3_.refs_4_), channel_id=1, source_target_pairs={{0,12},{4,8},{8,4},{12,0},{16,28},{20,24},{24,20},{28,16},{1,13},{... | collective-permute-start | bytes 393224 | tf_op jit(solution)/shard_map/ppermute | solution.py:514
  46.9 2.7 %collective-permute-done.17.refs_7_ = bf16[256,256]{1,0:T(8,128)(2,1)S(1)} collective-permute-done((bf16[256,256]{1,0:T(8,128)(2,1)S(1)}, bf16[256,256]{1,0:T(8,128)(2,1)S(1)}, u32[]{:S(2)}, u32[]{:S(2)}) %collective-permute-start.17) | collective-permute-done | bytes 131104 | tf_op jit(solution)/shard_map/ppermute | solution.py:514
  63.4 3.1 %outer_step.1 = (f32[2,1024,256]{2,1,0:T(8,128)}, f32[2,1024,256]{2,1,0:T(8,128)}, f32[8,128]{1,0:T(8,128)S(1)}) custom-call(s32[5]{0:T(128)S(1)} %stack.23.refs_0_.refs_1_, s32[8]{0:T(128)S(1)} %copy-done.7, f32[2,1024,256]{2,1,0:T(8,128)S(1)} %copy-done.5, f32[2,1024,256]{2,1,0:T(8,128)S(1)} %copy-done.6, ...), custom_call_target="tpu_custom_call" | custom-call | bytes 8916992 | tf_op jit(solution)/shard_map/outer_step/pallas_call | solution.py:60
  66.4 1.8 %forward_encoder.6.refs_1_ = f32[2,512,256]{2,1,0:T(8,128)S(1)} custom-call(s32[5]{0:T(128)S(1)} %stack.23.refs_0_.refs_1_, bf16[1024,256]{1,0:T(8,128)(2,1)S(1)} %get-tuple-element.101.refs_6_.refs_4_.refs_1_, bf16[1024,256]{1,0:T(8,128)(2,1)S(1)} %collective-permute-done.25.refs_2_, bf16[512,4096]{1,0:T(8,128)(2,1)S(1)} %copy-done, ...), custom_call_target="tpu_custom_call" | custom-call | bytes 10485760 | tf_op jit(solution)/shard_map/forward_encoder/pallas_call | solution.py:60
  68.2 4.0 %collective-permute-done.26.refs_0_ = bf16[1024,256]{1,0:T(8,128)(2,1)S(1)} collective-permute-done((bf16[1024,256]{1,0:T(8,128)(2,1)S(1)}, bf16[1024,256]{1,0:T(8,128)(2,1)S(1)}, u32[]{:S(2)}, u32[]{:S(2)}) %collective-permute-start.26) | collective-permute-done | bytes 524320 | tf_op jit(solution)/shard_map/ppermute | solution.py:510
  75.6 2.4 %hidden_units.3 = (bf16[2,512,256]{2,1,0:T(8,128)(2,1)S(1)}, f32[2,512,256]{2,1,0:T(8,128)S(1)}, bf16[2,512,256]{2,1,0:T(8,128)(2,1)S(1)}, bf16[256,256]{1,0:T(8,128)(2,1)S(1)}, bf16[256,256]{1,0:T(8,128)(2,1)S(1)}) custom-call(s32[5]{0:T(128)S(1)} %stack.23.refs_0_.refs_1_, f32[2,512,256]{2,1,0:T(8,128)S(1)} %forward_encoder.7.refs_1_, ...), custom_call_target="tpu_custom_call" | custom-call | bytes 12324864 | tf_op jit(solution)/shard_map/hidden_units/pallas_call | solution.py:60
  78.0 2.6 %collective-permute-done.24.refs_0_ = bf16[768,256]{1,0:T(8,128)(2,1)S(1)} collective-permute-done((bf16[768,256]{1,0:T(8,128)(2,1)S(1)}, bf16[768,256]{1,0:T(8,128)(2,1)S(1)}, u32[]{:S(2)}, u32[]{:S(2)}) %collective-permute-start.24) | collective-permute-done | bytes 393248 | tf_op jit(solution)/shard_map/ppermute | solution.py:510
  81.4 1.6 %collective-permute-start.34 = (bf16[768,256]{1,0:T(8,128)(2,1)S(1)}, bf16[768,256]{1,0:T(8,128)(2,1)S(1)}, u32[]{:S(2)}, u32[]{:S(2)}) collective-permute-start(bf16[768,256]{1,0:T(8,128)(2,1)S(1)} %decoder_grad.12.refs_2_.refs_6_), channel_id=1, source_target_pairs={{0,2},{1,3},{2,0},{3,1},{4,6},{5,7},{6,4},{7,5},{8,10},{9,11},{10,... | collective-permute-start | bytes 1179656 | tf_op jit(solution)/shard_map/ppermute | solution.py:512
  84.0 3.0 %forward_decoder.3 = (f32[2,512,256]{2,1,0:T(8,128)S(1)}, f32[256,256]{1,0:T(8,128)S(1)}) custom-call(s32[5]{0:T(128)S(1)} %stack.23.refs_0_.refs_1_, bf16[1024,256]{1,0:T(8,128)(2,1)S(1)} %get-tuple-element.104.refs_8_.refs_1_, bf16[1024,256]{1,0:T(8,128)(2,1)S(1)} %collective-permute-done.23.refs_2_, ...), custom_call_target="tpu_custom_call" | custom-call | bytes 11272192 | tf_op jit(solution)/shard_map/forward_decoder/pallas_call | solution.py:60
  87.1 2.0 %slope_pre.3.refs_2_ = bf16[2,512,256]{2,1,0:T(8,128)(2,1)S(1)} custom-call(s32[5]{0:T(128)S(1)} %stack.23.refs_0_.refs_1_, f32[2,512,256]{2,1,0:T(8,128)S(1)} %get-tuple-element.115.refs_1_, f32[256,256]{1,0:T(8,128)S(1)} %get-tuple-element.116.refs_2_, bf16[2,512,256]{2,1,0:T(8,128)(2,1)S(1)} %get-tuple-element.117.refs_3_, ...), custom_call_target="tpu_custom_call" | custom-call | bytes 12320768 | tf_op jit(solution)/shard_map/slope_pre/pallas_call | solution.py:60
  94.1 2.4 %adam_rows.15 = (f32[8,128]{1,0:T(8,128)S(1)}, f32[1,2,1024,256]{3,2,1,0:T(8,128)}, f32[1,2,1024,256]{3,2,1,0:T(8,128)}, f32[1,2,1024,256]{3,2,1,0:T(8,128)}) custom-call(s32[8]{0:T(128)S(1)} %copy-done.7, f32[768,256]{1,0:T(8,128)S(1)} %decoder_grad.14.refs_6_.refs_1_, bf16[768,256]{1,0:T(8,128)(2,1)S(1)} %collective-permute-done.34.refs_2_, ...), custom_call_target="tpu_custom_call" | custom-call | bytes 10620928 | tf_op jit(solution)/shard_map/adam_rows/pallas_call | solution.py:60
  97.8 3.6 %collective-permute-done.33.refs_2_ = bf16[256,256]{1,0:T(8,128)(2,1)S(1)} collective-permute-done((bf16[256,256]{1,0:T(8,128)(2,1)S(1)}, bf16[256,256]{1,0:T(8,128)(2,1)S(1)}, u32[]{:S(2)}, u32[]{:S(2)}) %collective-permute-start.33) | collective-permute-done | bytes 131104 | tf_op jit(solution)/shard_map/ppermute | solution.py:512
  104.4 2.0 %adam_rows.17 = (f32[1,2,1024,256]{3,2,1,0:T(8,128)}, f32[1,2,1024,256]{3,2,1,0:T(8,128)}, f32[1,2,1024,256]{3,2,1,0:T(8,128)}) custom-call(s32[8]{0:T(128)S(1)} %copy-done.7, f32[512,256]{1,0:T(8,128)S(1)} %encoder_grad.19.refs_3_.refs_1_, ...), custom_call_target="tpu_custom_call", output_to_operand_aliasing={{0}: (7, {}), {1}: (8, {}), {2}: (9, {})} | custom-call | bytes 15466496 | tf_op jit(solution)/shard_map/adam_rows/pallas_call | solution.py:60
  (127 shorter events, 49.5 us)
Async XLA Ops:
  0.6 15.5 %collective-permute-start = (bf16[512,4096]{1,0:T(8,128)(2,1)}, bf16[512,4096]{1,0:T(8,128)(2,1)}, u32[]{:S(2)}, u32[]{:S(2)}) collective-permute-start(bf16[512,4096]{1,0:T(8,128)(2,1)} %refs_8_.3), channel_id=1, source_target_pairs={{0,1},{1,0},{2,3},{3,2},{4,5},{5,4},{6,7},{7,6},{8,9},{9,8},{10,11... | collective-permute-start | bytes 12582920 | tf_op jit(solution)/shard_map/ppermute | solution.py:509
  3.0 11.7 %collective-permute-start.7 = (bf16[1024,256]{1,0:T(8,128)(2,1)S(1)}, bf16[1024,256]{1,0:T(8,128)(2,1)S(1)}, u32[]{:S(2)}, u32[]{:S(2)}) collective-permute-start(bf16[1024,256]{1,0:T(8,128)(2,1)S(1)} %get-tuple-element.79.refs_4_.refs_1_), channel_id=1, source_target_pairs={{0,1},{1,0},{2,3},{3,2},{4,5},{5,4},{6,7},{7,6},{8,9},{9,8},{10,11... | collective-permute-start | bytes 1572872 | tf_op jit(solution)/shard_map/ppermute | solution.py:509
  3.1 19.6 %collective-permute-start.8 = (bf16[1024,256]{1,0:T(8,128)(2,1)S(1)}, bf16[1024,256]{1,0:T(8,128)(2,1)S(1)}, u32[]{:S(2)}, u32[]{:S(2)}) collective-permute-start(bf16[1024,256]{1,0:T(8,128)(2,1)S(1)} %get-tuple-element.79.refs_4_.refs_1_), channel_id=1, source_target_pairs={{2,0},{3,1},{0,2},{1,3},{6,4},{7,5},{4,6},{5,7},{10,8},{11,9},{8,1... | collective-permute-start | bytes 1572872 | tf_op jit(solution)/shard_map/ppermute | solution.py:510
  8.4 13.7 %collective-permute-start.2 = (bf16[256,256]{1,0:T(8,128)(2,1)S(1)}, bf16[256,256]{1,0:T(8,128)(2,1)S(1)}, u32[]{:S(2)}, u32[]{:S(2)}) collective-permute-start(bf16[256,256]{1,0:T(8,128)(2,1)S(1)} %get-tuple-element.82), channel_id=1, source_target_pairs={{0,8},{4,12},{8,0},{12,4},{16,24},{20,28},{24,16},{28,20},{1,9},{5... | collective-permute-start | bytes 393224 | tf_op jit(solution)/shard_map/ppermute | solution.py:514
  12.1 10.0 %collective-permute-start.3 = (bf16[256,256]{1,0:T(8,128)(2,1)S(1)}, bf16[256,256]{1,0:T(8,128)(2,1)S(1)}, u32[]{:S(2)}, u32[]{:S(2)}) collective-permute-start(bf16[256,256]{1,0:T(8,128)(2,1)S(1)} %get-tuple-element.83), channel_id=1, source_target_pairs={{0,12},{4,8},{8,4},{12,0},{16,28},{20,24},{24,20},{28,16},{1,13},{... | collective-permute-start | bytes 393224 | tf_op jit(solution)/shard_map/ppermute | solution.py:514
  14.6 13.2 %collective-permute-start.6 = (bf16[768,256]{1,0:T(8,128)(2,1)S(1)}, bf16[768,256]{1,0:T(8,128)(2,1)S(1)}, u32[]{:S(2)}, u32[]{:S(2)}) collective-permute-start(bf16[768,256]{1,0:T(8,128)(2,1)S(1)} %get-tuple-element.85.refs_5_), channel_id=1, source_target_pairs={{2,0},{3,1},{0,2},{1,3},{6,4},{7,5},{4,6},{5,7},{10,8},{11,9},{8,1... | collective-permute-start | bytes 1179656 | tf_op jit(solution)/shard_map/ppermute | solution.py:510
  16.2 14.7 %collective-permute-start.5 = (bf16[1024,256]{1,0:T(8,128)(2,1)S(1)}, bf16[1024,256]{1,0:T(8,128)(2,1)S(1)}, u32[]{:S(2)}, u32[]{:S(2)}) collective-permute-start(bf16[1024,256]{1,0:T(8,128)(2,1)S(1)} %get-tuple-element.84.refs_1_), channel_id=1, source_target_pairs={{0,1},{1,0},{2,3},{3,2},{4,5},{5,4},{6,7},{7,6},{8,9},{9,8},{10,11... | collective-permute-start | bytes 1572872 | tf_op jit(solution)/shard_map/ppermute | solution.py:509
  23.4 7.3 %collective-permute-start.11 = (bf16[256,256]{1,0:T(8,128)(2,1)S(1)}, bf16[256,256]{1,0:T(8,128)(2,1)S(1)}, u32[]{:S(2)}, u32[]{:S(2)}) collective-permute-start(bf16[256,256]{1,0:T(8,128)(2,1)S(1)} %get-tuple-element.92.refs_5_), channel_id=1, source_target_pairs={{2,0},{3,1},{0,2},{1,3},{6,4},{7,5},{4,6},{5,7},{10,8},{11,9},{8,1... | collective-permute-start | bytes 393224 | tf_op jit(solution)/shard_map/ppermute | solution.py:510
  28.7 17.0 %collective-permute-start.18 = (bf16[768,256]{1,0:T(8,128)(2,1)S(1)}, bf16[768,256]{1,0:T(8,128)(2,1)S(1)}, u32[]{:S(2)}, u32[]{:S(2)}) collective-permute-start(bf16[768,256]{1,0:T(8,128)(2,1)S(1)} %decoder_grad.8.refs_2_.refs_6_), channel_id=1, source_target_pairs={{0,2},{1,3},{2,0},{3,1},{4,6},{5,7},{6,4},{7,5},{8,10},{9,11},{10,... | collective-permute-start | bytes 1179656 | tf_op jit(solution)/shard_map/ppermute | solution.py:512
  30.2 7.2 %collective-permute-start.12 = (bf16[384,256]{1,0:T(8,128)(2,1)S(1)}, bf16[384,256]{1,0:T(8,128)(2,1)S(1)}, u32[]{:S(2)}, u32[]{:S(2)}) collective-permute-start(bf16[384,256]{1,0:T(8,128)(2,1)S(1)} %get-tuple-element.90.refs_5_.refs_3_), channel_id=1, source_target_pairs={{0,1},{1,0},{2,3},{3,2},{4,5},{5,4},{6,7},{7,6},{8,9},{9,8},{10,11... | collective-permute-start | bytes 589832 | tf_op jit(solution)/shard_map/ppermute | solution.py:509
  30.9 10.7 %collective-permute-start.4 = (bf16[256,256]{1,0:T(8,128)(2,1)S(1)}, bf16[256,256]{1,0:T(8,128)(2,1)S(1)}, u32[]{:S(2)}, u32[]{:S(2)}) collective-permute-start(bf16[256,256]{1,0:T(8,128)(2,1)S(1)} %add_quarters.2.refs_3_.refs_1_), channel_id=1, source_target_pairs={{0,16},{4,20},{8,24},{12,28},{16,0},{20,4},{24,8},{28,12},{1,17},{... | collective-permute-start | bytes 393224 | tf_op jit(solution)/shard_map/ppermute | solution.py:514
  36.9 8.2 %collective-permute-start.19 = (bf16[256,256]{1,0:T(8,128)(2,1)S(1)}, bf16[256,256]{1,0:T(8,128)(2,1)S(1)}, u32[]{:S(2)}, u32[]{:S(2)}) collective-permute-start(bf16[256,256]{1,0:T(8,128)(2,1)S(1)} %decoder_grad.9.refs_8_.refs_3_), channel_id=1, source_target_pairs={{0,2},{1,3},{2,0},{3,1},{4,6},{5,7},{6,4},{7,5},{8,10},{9,11},{10,... | collective-permute-start | bytes 393224 | tf_op jit(solution)/shard_map/ppermute | solution.py:512
  40.0 13.3 %collective-permute-start.22 = (bf16[512,256]{1,0:T(8,128)(2,1)S(1)}, bf16[512,256]{1,0:T(8,128)(2,1)S(1)}, u32[]{:S(2)}, u32[]{:S(2)}) collective-permute-start(bf16[512,256]{1,0:T(8,128)(2,1)S(1)} %encoder_grad.12.refs_3_), channel_id=1, source_target_pairs={{0,2},{1,3},{2,0},{3,1},{4,6},{5,7},{6,4},{7,5},{8,10},{9,11},{10,... | collective-permute-start | bytes 786440 | tf_op jit(solution)/shard_map/ppermute | solution.py:512
  42.1 7.5 %collective-permute-start.17 = (bf16[256,256]{1,0:T(8,128)(2,1)S(1)}, bf16[256,256]{1,0:T(8,128)(2,1)S(1)}, u32[]{:S(2)}, u32[]{:S(2)}) collective-permute-start(bf16[256,256]{1,0:T(8,128)(2,1)S(1)} %add_quarters.3.refs_3_.refs_4_), channel_id=1, source_target_pairs={{0,12},{4,8},{8,4},{12,0},{16,28},{20,24},{24,20},{28,16},{1,13},{... | collective-permute-start | bytes 393224 | tf_op jit(solution)/shard_map/ppermute | solution.py:514
  46.0 9.6 %collective-permute-start.21 = (bf16[256,256]{1,0:T(8,128)(2,1)S(1)}, bf16[256,256]{1,0:T(8,128)(2,1)S(1)}, u32[]{:S(2)}, u32[]{:S(2)}) collective-permute-start(bf16[256,256]{1,0:T(8,128)(2,1)S(1)} %encoder_grad.13.refs_3_), channel_id=1, source_target_pairs={{0,2},{1,3},{2,0},{3,1},{4,6},{5,7},{6,4},{7,5},{8,10},{9,11},{10,... | collective-permute-start | bytes 393224 | tf_op jit(solution)/shard_map/ppermute | solution.py:512
  57.3 9.1 %collective-permute-start.25 = (bf16[1024,256]{1,0:T(8,128)(2,1)S(1)}, bf16[1024,256]{1,0:T(8,128)(2,1)S(1)}, u32[]{:S(2)}, u32[]{:S(2)}) collective-permute-start(bf16[1024,256]{1,0:T(8,128)(2,1)S(1)} %get-tuple-element.101.refs_6_.refs_4_.refs_1_), channel_id=1, source_target_pairs={{0,1},{1,0},{2,3},{3,2},{4,5},{5,4},{6,7},{7,6},{8,9},{9,8},{10,11... | collective-permute-start | bytes 1572872 | tf_op jit(solution)/shard_map/ppermute | solution.py:509
  57.4 14.8 %collective-permute-start.26 = (bf16[1024,256]{1,0:T(8,128)(2,1)S(1)}, bf16[1024,256]{1,0:T(8,128)(2,1)S(1)}, u32[]{:S(2)}, u32[]{:S(2)}) collective-permute-start(bf16[1024,256]{1,0:T(8,128)(2,1)S(1)} %get-tuple-element.101.refs_6_.refs_4_.refs_1_), channel_id=1, source_target_pairs={{2,0},{3,1},{0,2},{1,3},{6,4},{7,5},{4,6},{5,7},{10,8},{11,9},{8,1... | collective-permute-start | bytes 1572872 | tf_op jit(solution)/shard_map/ppermute | solution.py:510
  62.8 17.8 %collective-permute-start.24 = (bf16[768,256]{1,0:T(8,128)(2,1)S(1)}, bf16[768,256]{1,0:T(8,128)(2,1)S(1)}, u32[]{:S(2)}, u32[]{:S(2)}) collective-permute-start(bf16[768,256]{1,0:T(8,128)(2,1)S(1)} %get-tuple-element.105.refs_5_), channel_id=1, source_target_pairs={{2,0},{3,1},{0,2},{1,3},{6,4},{7,5},{4,6},{5,7},{10,8},{11,9},{8,1... | collective-permute-start | bytes 1179656 | tf_op jit(solution)/shard_map/ppermute | solution.py:510
  63.3 20.7 %collective-permute-start.23 = (bf16[1024,256]{1,0:T(8,128)(2,1)S(1)}, bf16[1024,256]{1,0:T(8,128)(2,1)S(1)}, u32[]{:S(2)}, u32[]{:S(2)}) collective-permute-start(bf16[1024,256]{1,0:T(8,128)(2,1)S(1)} %get-tuple-element.104.refs_8_.refs_1_), channel_id=1, source_target_pairs={{0,1},{1,0},{2,3},{3,2},{4,5},{5,4},{6,7},{7,6},{8,9},{9,8},{10,11... | collective-permute-start | bytes 1572872 | tf_op jit(solution)/shard_map/ppermute | solution.py:509
  72.8 10.7 %collective-permute-start.29 = (bf16[256,256]{1,0:T(8,128)(2,1)S(1)}, bf16[256,256]{1,0:T(8,128)(2,1)S(1)}, u32[]{:S(2)}, u32[]{:S(2)}) collective-permute-start(bf16[256,256]{1,0:T(8,128)(2,1)S(1)} %get-tuple-element.112.refs_5_), channel_id=1, source_target_pairs={{2,0},{3,1},{0,2},{1,3},{6,4},{7,5},{4,6},{5,7},{10,8},{11,9},{8,1... | collective-permute-start | bytes 393224 | tf_op jit(solution)/shard_map/ppermute | solution.py:510
  81.4 12.6 %collective-permute-start.34 = (bf16[768,256]{1,0:T(8,128)(2,1)S(1)}, bf16[768,256]{1,0:T(8,128)(2,1)S(1)}, u32[]{:S(2)}, u32[]{:S(2)}) collective-permute-start(bf16[768,256]{1,0:T(8,128)(2,1)S(1)} %decoder_grad.12.refs_2_.refs_6_), channel_id=1, source_target_pairs={{0,2},{1,3},{2,0},{3,1},{4,6},{5,7},{6,4},{7,5},{8,10},{9,11},{10,... | collective-permute-start | bytes 1179656 | tf_op jit(solution)/shard_map/ppermute | solution.py:512
  89.5 14.9 %collective-permute-start.37 = (bf16[512,256]{1,0:T(8,128)(2,1)S(1)}, bf16[512,256]{1,0:T(8,128)(2,1)S(1)}, u32[]{:S(2)}, u32[]{:S(2)}) collective-permute-start(bf16[512,256]{1,0:T(8,128)(2,1)S(1)} %encoder_grad.18.refs_3_), channel_id=1, source_target_pairs={{0,2},{1,3},{2,0},{3,1},{4,6},{5,7},{6,4},{7,5},{8,10},{9,11},{10,... | collective-permute-start | bytes 786440 | tf_op jit(solution)/shard_map/ppermute | solution.py:512
  90.5 11.0 %collective-permute-start.33 = (bf16[256,256]{1,0:T(8,128)(2,1)S(1)}, bf16[256,256]{1,0:T(8,128)(2,1)S(1)}, u32[]{:S(2)}, u32[]{:S(2)}) collective-permute-start(bf16[256,256]{1,0:T(8,128)(2,1)S(1)} %decoder_grad.13.refs_8_.refs_3_), channel_id=1, source_target_pairs={{0,2},{1,3},{2,0},{3,1},{4,6},{5,7},{6,4},{7,5},{8,10},{9,11},{10,... | collective-permute-start | bytes 393224 | tf_op jit(solution)/shard_map/ppermute | solution.py:512
  96.8 9.6 %collective-permute-start.36 = (bf16[256,256]{1,0:T(8,128)(2,1)S(1)}, bf16[256,256]{1,0:T(8,128)(2,1)S(1)}, u32[]{:S(2)}, u32[]{:S(2)}) collective-permute-start(bf16[256,256]{1,0:T(8,128)(2,1)S(1)} %encoder_grad.22.refs_10_), channel_id=1, source_target_pairs={{0,2},{1,3},{2,0},{3,1},{4,6},{5,7},{6,4},{7,5},{8,10},{9,11},{10,... | collective-permute-start | bytes 393224 | tf_op jit(solution)/shard_map/ppermute | solution.py:512
  (23 other events, 99.8 us)

commit v17 on v14

--- a/solution.py
+++ b/solution.py
@@ -336,8 +336,12 @@
     theta, first, second = refs[count:3 + count]
     refs = refs[3 + count:]
     grad = own[...]
-    for g in got:
-        grad = grad + g[...].astype(f32)
+    got = [g[...].astype(f32) for g in got]
+    while got:
+        value = got.pop(0)
+        while value.shape[0] < own.shape[0]:
+            value = jnp.concatenate([value, got.pop(0)], 0)
+        grad = grad + value
     one = beta_one * first[0, 0] + (1.0 - beta_one) * grad
     two = beta_two * second[0, 0] + (1.0 - beta_two) * grad * grad
     old = theta[0, 0]
@@ -554,8 +558,8 @@
         if step == 0:
             cw = weigh(kinds, pending[-1][0], tokens)
         hidden, slope, counted, w_hi, w_lo = hidden_rows(pos, carry[0], cw, pending, xs, rows, scale)
-        dec_grad = lambda s, size, lows, more, front, dtype, after: grad_rows(
-            functools.partial(decoder_body, scale, s * rows, len(lows), front), "decoder_grad", size, xt,
+        dec_grad = lambda s, size, lows, more, front, dtype, after, off=0: grad_rows(
+            functools.partial(decoder_body, scale, s * rows + off, len(lows), front), "decoder_grad", size, xt,
             [counted, w_hi, w_lo, *lows, *more], dtype, after)
         enc_grad = lambda s, off, size, dtype, after: grad_rows(
             functools.partial(encoder_body, s * rows + off), "encoder_grad", size, xt, [slopes], dtype, after)
@@ -569,10 +573,13 @@
             pending += handed
             for s in others:
                 rows_in = [p[0] for p in pieces if p[1] == 1 + s]
-                whole_grad[s] = [dec_grad(
-                    s, starts[n] + sizes[n], rows_in, whole_grad[s], n > 0, bf16, sent[-1:])]
-                sent.append(whole_grad[s][0])
-        back = [give(whole_grad[s][0], s) for s in others]
+                if last:
+                    whole_grad[s] = [dec_grad(
+                        s, starts[n] + sizes[n], rows_in, whole_grad[s], n > 0, bf16, sent[-1:])]
+                else:
+                    whole_grad[s].append(dec_grad(s, sizes[n], rows_in, [], False, bf16, sent[-1:], starts[n]))
+                sent.append(whole_grad[s][-1])
+        back = [give(g, s) for s in others for g in whole_grad[s]]
 
         carry = forward(
             pos, [], [(dec, 1, 0, rows), (dec_near, 1 + chips, 0, rows)] + part, xs, rows, True, sent[-1:])

time: 109 us -> 108 us (level)
  waiting for transfers between devices: 20.6 us -> 18.9 us
  starting transfers between devices: 31.4 us -> 32.8 us
    ppermute x6, waiting for transfers between devices: 12.4 us -> 9.62 us  [local(): lax.ppermute(a, 'fsdp', [((f // 2 + s) % chips * 2 + f % 2, f) for f in r...]
    ppermute x8 -> x9, starting transfers between devices: 8.45 us -> 9.91 us  [local(): lax.ppermute(a, 'fsdp', [(f, (f // 2 + s) % chips * 2 + f % 2) for f in r...]
    ppermute x8 -> x9, waiting for transfers between devices: 4.94 us -> 4.95 us  [local(): lax.ppermute(a, 'fsdp', [(f, (f // 2 + s) % chips * 2 + f % 2) for f in r...]
  transfers between devices with their start and end apart: 36 -> 37, of which waited for: 11 -> 9; matrix products, arithmetic and copies ran while one was open for 0% -> 0% of each run, Pallas kernels for 47% -> 47%
where the time goes in v17:
time: 108 us
  Pallas kernels  53 us (49%)
  starting transfers between devices  32.8 us (30%)
  waiting for transfers between devices  18.9 us (17%)
  local copies, waits for them, and re-layouts  2.27 us (2%)
  between operations  1.15 us (1%)
    pallas_call x52, Pallas kernels, call(): pl.pallas_call(run, name=name, out_shape=[o for o, _ in outs], grid_spec=...  53 us
    ppermute x7, starting transfers between devices, local(): lax.ppermute(a, 'replica', [(r, r ^ bit) for r in range(n_rep)])  11.9 us
    ppermute x9, starting transfers between devices, local(): lax.ppermute(a, 'fsdp', [(f, (f // 2 + s) % chips * 2 + f % 2) for f in r...  9.91 us
    ppermute x6, waiting for transfers between devices, local(): lax.ppermute(a, 'fsdp', [((f // 2 + s) % chips * 2 + f % 2, f) for f in r...  9.62 us
    ppermute x6, starting transfers between devices, local(): lax.ppermute(a, 'fsdp', [((f // 2 + s) % chips * 2 + f % 2, f) for f in r...  7.89 us
    ppermute x9, waiting for transfers between devices, local(): lax.ppermute(a, 'fsdp', [(f, (f // 2 + s) % chips * 2 + f % 2) for f in r...  4.95 us
    ppermute x7, waiting for transfers between devices, local(): lax.ppermute(a, 'replica', [(r, r ^ bit) for r in range(n_rep)])  4.29 us
    ppermute x15, starting transfers between devices, local(): to_partner = lambda a: lax.ppermute(a, 'fsdp', partner)  3.12 us
  transfers between devices with their start and end apart: 37, of which 9 were waited for; matrix products, arithmetic and copies ran while one was open for 0% of the time, Pallas kernels for 47%

profile of v17, /device:TPU:0, one launch (start us, length us, event | category | flops | bytes accessed | tf_op | source)
XLA Modules:
  0.0 108.2 jit_solution(12806154749587816440)
XLA Ops:
  1.2 1.6 %copy-done.1 = f32[1,2,1024,256]{3,2,1,0:T(8,128)S(1)} copy-done((f32[1,2,1024,256]{3,2,1,0:T(8,128)S(1)}, f32[1,2,1024,256]{3,2,1,0:T(8,128)}, u32[]{:S(2)}) %copy-start.1) | copy-done | bytes 2097176
  3.1 3.0 %collective-permute-start.8 = (bf16[1024,256]{1,0:T(8,128)(2,1)S(1)}, bf16[1024,256]{1,0:T(8,128)(2,1)S(1)}, u32[]{:S(2)}, u32[]{:S(2)}) collective-permute-start(bf16[1024,256]{1,0:T(8,128)(2,1)S(1)} %get-tuple-element.71.refs_4_.refs_1_), channel_id=1, source_target_pairs={{2,0},{3,1},{0,2},{1,3},{6,4},{7,5},{4,6},{5,7},{10,8},{11,9},{8,1... | collective-permute-start | bytes 1572872 | tf_op jit(solution)/shard_map/ppermute | solution.py:511
  9.9 2.1 %collective-permute-done.1.refs_2_ = bf16[256,256]{1,0:T(8,128)(2,1)S(1)} collective-permute-done((bf16[256,256]{1,0:T(8,128)(2,1)S(1)}, bf16[256,256]{1,0:T(8,128)(2,1)S(1)}, u32[]{:S(2)}, u32[]{:S(2)}) %collective-permute-start.1) | collective-permute-done | bytes 131104 | tf_op jit(solution)/shard_map/ppermute | solution.py:515
  12.1 2.6 %collective-permute-start.3 = (bf16[256,256]{1,0:T(8,128)(2,1)S(1)}, bf16[256,256]{1,0:T(8,128)(2,1)S(1)}, u32[]{:S(2)}, u32[]{:S(2)}) collective-permute-start(bf16[256,256]{1,0:T(8,128)(2,1)S(1)} %get-tuple-element.75), channel_id=1, source_target_pairs={{0,12},{4,8},{8,4},{12,0},{16,28},{20,24},{24,20},{28,16},{1,13},{... | collective-permute-start | bytes 393224 | tf_op jit(solution)/shard_map/ppermute | solution.py:515
  17.3 2.9 %stage_tokens.1 = (bf16[512,4096]{1,0:T(8,128)(2,1)S(1)}, bf16[2048,512]{1,0:T(8,128)(2,1)S(1)}) custom-call(s32[5]{0:T(128)S(1)} %stack.23.refs_0_.refs_1_, bf16[512,4096]{1,0:T(8,128)(2,1)} %collective-permute-done.refs_1_), custom_call_target="tpu_custom_call" | custom-call | bytes 10485760 | tf_op jit(solution)/shard_map/stage_tokens/pallas_call | solution.py:60
  20.3 1.8 %forward_encoder.4.refs_2_.refs_1_ = f32[2,512,256]{2,1,0:T(8,128)S(1)} custom-call(s32[5]{0:T(128)S(1)} %stack.23.refs_0_.refs_1_, bf16[1024,256]{1,0:T(8,128)(2,1)S(1)} %get-tuple-element.71.refs_4_.refs_1_, bf16[1024,256]{1,0:T(8,128)(2,1)S(1)} %collective-permute-done.7.refs_2_, bf16[512,4096]{1,0:T(8,128)(2,1)S(1)} %copy-done, ...), custom_call_target="tpu_custom_call" | custom-call | bytes 10485760 | tf_op jit(solution)/shard_map/forward_encoder/pallas_call | solution.py:60
  25.4 2.4 %hidden_units.2 = (bf16[2,512,256]{2,1,0:T(8,128)(2,1)S(1)}, f32[2,512,256]{2,1,0:T(8,128)S(1)}, bf16[2,512,256]{2,1,0:T(8,128)(2,1)S(1)}, bf16[256,256]{1,0:T(8,128)(2,1)S(1)}, bf16[256,256]{1,0:T(8,128)(2,1)S(1)}) custom-call(s32[5]{0:T(128)S(1)} %stack.23.refs_0_.refs_1_, f32[2,512,256]{2,1,0:T(8,128)S(1)} %forward_encoder.5.refs_1_, ...), custom_call_target="tpu_custom_call" | custom-call | bytes 12333056 | tf_op jit(solution)/shard_map/hidden_units/pallas_call | solution.py:60
  30.8 2.7 %collective-permute-start.4 = (bf16[256,256]{1,0:T(8,128)(2,1)S(1)}, bf16[256,256]{1,0:T(8,128)(2,1)S(1)}, u32[]{:S(2)}, u32[]{:S(2)}) collective-permute-start(bf16[256,256]{1,0:T(8,128)(2,1)S(1)} %add_quarters.2.refs_3_.refs_1_), channel_id=1, source_target_pairs={{0,16},{4,20},{8,24},{12,28},{16,0},{20,4},{24,8},{28,12},{1,17},{... | collective-permute-start | bytes 393224 | tf_op jit(solution)/shard_map/ppermute | solution.py:515
  33.9 3.0 %forward_decoder.2 = (f32[2,512,256]{2,1,0:T(8,128)S(1)}, f32[256,256]{1,0:T(8,128)S(1)}) custom-call(s32[5]{0:T(128)S(1)} %stack.23.refs_0_.refs_1_, bf16[1024,256]{1,0:T(8,128)(2,1)S(1)} %get-tuple-element.76.refs_1_, bf16[1024,256]{1,0:T(8,128)(2,1)S(1)} %collective-permute-done.5.refs_2_, bf16[384,256]{1,0:T(8,128)(2,1)S(1)} %get-tuple-element.82.refs_5_.refs_3_, ...), custom_call_target="tpu_custom_call" | custom-call | bytes 11272192 | tf_op jit(solution)/shard_map/forward_decoder/pallas_call | solution.py:60
  37.4 2.0 %slope_pre.2.refs_2_ = bf16[2,512,256]{2,1,0:T(8,128)(2,1)S(1)} custom-call(s32[5]{0:T(128)S(1)} %stack.23.refs_0_.refs_1_, f32[2,512,256]{2,1,0:T(8,128)S(1)} %get-tuple-element.87.refs_1_, f32[256,256]{1,0:T(8,128)S(1)} %get-tuple-element.88.refs_2_, bf16[2,512,256]{2,1,0:T(8,128)(2,1)S(1)} %get-tuple-element.89.refs_3_, ...), custom_call_target="tpu_custom_call" | custom-call | bytes 12320768 | tf_op jit(solution)/shard_map/slope_pre/pallas_call | solution.py:60
  39.9 1.6 %collective-permute-start.22 = (bf16[512,256]{1,0:T(8,128)(2,1)S(1)}, bf16[512,256]{1,0:T(8,128)(2,1)S(1)}, u32[]{:S(2)}, u32[]{:S(2)}) collective-permute-start(bf16[512,256]{1,0:T(8,128)(2,1)S(1)} %encoder_grad.12.refs_3_), channel_id=1, source_target_pairs={{0,2},{1,3},{2,0},{3,1},{4,6},{5,7},{6,4},{7,5},{8,10},{9,11},{10,... | collective-permute-start | bytes 786440 | tf_op jit(solution)/shard_map/ppermute | solution.py:513
  49.7 1.7 %collective-permute-done.17.refs_7_ = bf16[256,256]{1,0:T(8,128)(2,1)S(1)} collective-permute-done((bf16[256,256]{1,0:T(8,128)(2,1)S(1)}, bf16[256,256]{1,0:T(8,128)(2,1)S(1)}, u32[]{:S(2)}, u32[]{:S(2)}) %collective-permute-start.17) | collective-permute-done | bytes 131104 | tf_op jit(solution)/shard_map/ppermute | solution.py:515
  60.9 3.1 %outer_step.1 = (f32[2,1024,256]{2,1,0:T(8,128)}, f32[2,1024,256]{2,1,0:T(8,128)}, f32[8,128]{1,0:T(8,128)S(1)}) custom-call(s32[5]{0:T(128)S(1)} %stack.23.refs_0_.refs_1_, s32[8]{0:T(128)S(1)} %copy-done.7, f32[2,1024,256]{2,1,0:T(8,128)S(1)} %copy-done.5, f32[2,1024,256]{2,1,0:T(8,128)S(1)} %copy-done.6, ...), custom_call_target="tpu_custom_call" | custom-call | bytes 8916992 | tf_op jit(solution)/shard_map/outer_step/pallas_call | solution.py:60
  64.0 1.8 %forward_encoder.6.refs_1_ = f32[2,512,256]{2,1,0:T(8,128)S(1)} custom-call(s32[5]{0:T(128)S(1)} %stack.23.refs_0_.refs_1_, bf16[1024,256]{1,0:T(8,128)(2,1)S(1)} %get-tuple-element.93.refs_7_.refs_3_.refs_1_, bf16[1024,256]{1,0:T(8,128)(2,1)S(1)} %collective-permute-done.25.refs_2_, bf16[512,4096]{1,0:T(8,128)(2,1)S(1)} %copy-done, ...), custom_call_target="tpu_custom_call" | custom-call | bytes 10485760 | tf_op jit(solution)/shard_map/forward_encoder/pallas_call | solution.py:60
  65.8 4.7 %collective-permute-done.26.refs_0_ = bf16[1024,256]{1,0:T(8,128)(2,1)S(1)} collective-permute-done((bf16[1024,256]{1,0:T(8,128)(2,1)S(1)}, bf16[1024,256]{1,0:T(8,128)(2,1)S(1)}, u32[]{:S(2)}, u32[]{:S(2)}) %collective-permute-start.26) | collective-permute-done | bytes 524320 | tf_op jit(solution)/shard_map/ppermute | solution.py:511
  73.2 2.3 %hidden_units.3 = (bf16[2,512,256]{2,1,0:T(8,128)(2,1)S(1)}, f32[2,512,256]{2,1,0:T(8,128)S(1)}, bf16[2,512,256]{2,1,0:T(8,128)(2,1)S(1)}, bf16[256,256]{1,0:T(8,128)(2,1)S(1)}, bf16[256,256]{1,0:T(8,128)(2,1)S(1)}) custom-call(s32[5]{0:T(128)S(1)} %stack.23.refs_0_.refs_1_, f32[2,512,256]{2,1,0:T(8,128)S(1)} %forward_encoder.7.refs_1_, ...), custom_call_target="tpu_custom_call" | custom-call | bytes 12324864 | tf_op jit(solution)/shard_map/hidden_units/pallas_call | solution.py:60
  75.6 3.4 %collective-permute-done.24.refs_0_ = bf16[768,256]{1,0:T(8,128)(2,1)S(1)} collective-permute-done((bf16[768,256]{1,0:T(8,128)(2,1)S(1)}, bf16[768,256]{1,0:T(8,128)(2,1)S(1)}, u32[]{:S(2)}, u32[]{:S(2)}) %collective-permute-start.24) | collective-permute-done | bytes 393248 | tf_op jit(solution)/shard_map/ppermute | solution.py:511
  83.0 3.0 %forward_decoder.3 = (f32[2,512,256]{2,1,0:T(8,128)S(1)}, f32[256,256]{1,0:T(8,128)S(1)}) custom-call(s32[5]{0:T(128)S(1)} %stack.23.refs_0_.refs_1_, bf16[1024,256]{1,0:T(8,128)(2,1)S(1)} %get-tuple-element.95.refs_8_.refs_1_, bf16[1024,256]{1,0:T(8,128)(2,1)S(1)} %collective-permute-done.23.refs_2_, ...), custom_call_target="tpu_custom_call" | custom-call | bytes 11272192 | tf_op jit(solution)/shard_map/forward_decoder/pallas_call | solution.py:60
  86.0 2.0 %slope_pre.3.refs_2_ = bf16[2,512,256]{2,1,0:T(8,128)(2,1)S(1)} custom-call(s32[5]{0:T(128)S(1)} %stack.23.refs_0_.refs_1_, f32[2,512,256]{2,1,0:T(8,128)S(1)} %get-tuple-element.106.refs_1_, f32[256,256]{1,0:T(8,128)S(1)} %get-tuple-element.107.refs_2_, bf16[2,512,256]{2,1,0:T(8,128)(2,1)S(1)} %get-tuple-element.108.refs_3_, ...), custom_call_target="tpu_custom_call" | custom-call | bytes 12320768 | tf_op jit(solution)/shard_map/slope_pre/pallas_call | solution.py:60
  92.1 4.4 %collective-permute-done.33.refs_4_.refs_2_ = bf16[1024,256]{1,0:T(8,128)(2,1)S(1)} collective-permute-done((bf16[1024,256]{1,0:T(8,128)(2,1)S(1)}, bf16[1024,256]{1,0:T(8,128)(2,1)S(1)}, u32[]{:S(2)}, u32[]{:S(2)}) %collective-permute-start.33) | collective-permute-done | bytes 524320 | tf_op jit(solution)/shard_map/ppermute | solution.py:513
  99.3 3.1 %adam_rows.12 = (f32[8,128]{1,0:T(8,128)}, f32[1,2,1024,256]{3,2,1,0:T(8,128)}, f32[1,2,1024,256]{3,2,1,0:T(8,128)}, f32[1,2,1024,256]{3,2,1,0:T(8,128)}) custom-call(s32[8]{0:T(128)S(1)} %copy-done.7, f32[1024,256]{1,0:T(8,128)S(1)} %decoder_grad.11.refs_3_.refs_1_, bf16[1024,256]{1,0:T(8,128)(2,1)S(1)} %collective-permute-done.33.refs_4_.refs_2_, ...), custom_call_target="tpu_custom_call" | custom-call | bytes 12062720 | tf_op jit(solution)/shard_map/adam_rows/pallas_call | solution.py:60
  102.5 2.0 %adam_rows.13 = (f32[1,2,1024,256]{3,2,1,0:T(8,128)}, f32[1,2,1024,256]{3,2,1,0:T(8,128)}, f32[1,2,1024,256]{3,2,1,0:T(8,128)}) custom-call(s32[8]{0:T(128)S(1)} %copy-done.7, f32[512,256]{1,0:T(8,128)S(1)} %encoder_grad.19.refs_3_.refs_1_, ...), custom_call_target="tpu_custom_call", output_to_operand_aliasing={{0}: (7, {}), {1}: (8, {}), {2}: (9, {})} | custom-call | bytes 15466496 | tf_op jit(solution)/shard_map/adam_rows/pallas_call | solution.py:60
  105.0 1.6 %adam_rows.14 = (f32[1,2,1024,256]{3,2,1,0:T(8,128)}, f32[1,2,1024,256]{3,2,1,0:T(8,128)}, f32[1,2,1024,256]{3,2,1,0:T(8,128)}) custom-call(s32[8]{0:T(128)S(1)} %copy-done.7, f32[256,256]{1,0:T(8,128)S(1)} %encoder_grad.20.refs_3_.refs_1_, ...), custom_call_target="tpu_custom_call", output_to_operand_aliasing={{0}: (7, {}), {1}: (8, {}), {2}: (9, {})} | custom-call | bytes 14024704 | tf_op jit(solution)/shard_map/adam_rows/pallas_call | solution.py:60
  106.6 1.6 %adam_rows.15 = (f32[1,2,1024,256]{3,2,1,0:T(8,128)}, f32[1,2,1024,256]{3,2,1,0:T(8,128)}, f32[1,2,1024,256]{3,2,1,0:T(8,128)}) custom-call(s32[8]{0:T(128)S(1)} %copy-done.7, f32[256,256]{1,0:T(8,128)S(1)} %encoder_grad.21.refs_7_.refs_1_, ...), custom_call_target="tpu_custom_call", output_to_operand_aliasing={{0}: (7, {}), {1}: (8, {}), {2}: (9, {})} | custom-call | bytes 14024704 | tf_op jit(solution)/shard_map/adam_rows/pallas_call | solution.py:60
  (121 shorter events, 46.8 us)
Async XLA Ops:
  0.6 15.5 %collective-permute-start = (bf16[512,4096]{1,0:T(8,128)(2,1)}, bf16[512,4096]{1,0:T(8,128)(2,1)}, u32[]{:S(2)}, u32[]{:S(2)}) collective-permute-start(bf16[512,4096]{1,0:T(8,128)(2,1)} %refs_8_.3), channel_id=1, source_target_pairs={{0,1},{1,0},{2,3},{3,2},{4,5},{5,4},{6,7},{7,6},{8,9},{9,8},{10,11... | collective-permute-start | bytes 12582920 | tf_op jit(solution)/shard_map/ppermute | solution.py:510
  3.0 11.7 %collective-permute-start.7 = (bf16[1024,256]{1,0:T(8,128)(2,1)S(1)}, bf16[1024,256]{1,0:T(8,128)(2,1)S(1)}, u32[]{:S(2)}, u32[]{:S(2)}) collective-permute-start(bf16[1024,256]{1,0:T(8,128)(2,1)S(1)} %get-tuple-element.71.refs_4_.refs_1_), channel_id=1, source_target_pairs={{0,1},{1,0},{2,3},{3,2},{4,5},{5,4},{6,7},{7,6},{8,9},{9,8},{10,11... | collective-permute-start | bytes 1572872 | tf_op jit(solution)/shard_map/ppermute | solution.py:510
  3.1 19.6 %collective-permute-start.8 = (bf16[1024,256]{1,0:T(8,128)(2,1)S(1)}, bf16[1024,256]{1,0:T(8,128)(2,1)S(1)}, u32[]{:S(2)}, u32[]{:S(2)}) collective-permute-start(bf16[1024,256]{1,0:T(8,128)(2,1)S(1)} %get-tuple-element.71.refs_4_.refs_1_), channel_id=1, source_target_pairs={{2,0},{3,1},{0,2},{1,3},{6,4},{7,5},{4,6},{5,7},{10,8},{11,9},{8,1... | collective-permute-start | bytes 1572872 | tf_op jit(solution)/shard_map/ppermute | solution.py:511
  8.4 13.7 %collective-permute-start.2 = (bf16[256,256]{1,0:T(8,128)(2,1)S(1)}, bf16[256,256]{1,0:T(8,128)(2,1)S(1)}, u32[]{:S(2)}, u32[]{:S(2)}) collective-permute-start(bf16[256,256]{1,0:T(8,128)(2,1)S(1)} %get-tuple-element.74), channel_id=1, source_target_pairs={{0,8},{4,12},{8,0},{12,4},{16,24},{20,28},{24,16},{28,20},{1,9},{5... | collective-permute-start | bytes 393224 | tf_op jit(solution)/shard_map/ppermute | solution.py:515
  12.1 10.0 %collective-permute-start.3 = (bf16[256,256]{1,0:T(8,128)(2,1)S(1)}, bf16[256,256]{1,0:T(8,128)(2,1)S(1)}, u32[]{:S(2)}, u32[]{:S(2)}) collective-permute-start(bf16[256,256]{1,0:T(8,128)(2,1)S(1)} %get-tuple-element.75), channel_id=1, source_target_pairs={{0,12},{4,8},{8,4},{12,0},{16,28},{20,24},{24,20},{28,16},{1,13},{... | collective-permute-start | bytes 393224 | tf_op jit(solution)/shard_map/ppermute | solution.py:515
  14.6 13.2 %collective-permute-start.6 = (bf16[768,256]{1,0:T(8,128)(2,1)S(1)}, bf16[768,256]{1,0:T(8,128)(2,1)S(1)}, u32[]{:S(2)}, u32[]{:S(2)}) collective-permute-start(bf16[768,256]{1,0:T(8,128)(2,1)S(1)} %get-tuple-element.77.refs_5_), channel_id=1, source_target_pairs={{2,0},{3,1},{0,2},{1,3},{6,4},{7,5},{4,6},{5,7},{10,8},{11,9},{8,1... | collective-permute-start | bytes 1179656 | tf_op jit(solution)/shard_map/ppermute | solution.py:511
  16.2 14.7 %collective-permute-start.5 = (bf16[1024,256]{1,0:T(8,128)(2,1)S(1)}, bf16[1024,256]{1,0:T(8,128)(2,1)S(1)}, u32[]{:S(2)}, u32[]{:S(2)}) collective-permute-start(bf16[1024,256]{1,0:T(8,128)(2,1)S(1)} %get-tuple-element.76.refs_1_), channel_id=1, source_target_pairs={{0,1},{1,0},{2,3},{3,2},{4,5},{5,4},{6,7},{7,6},{8,9},{9,8},{10,11... | collective-permute-start | bytes 1572872 | tf_op jit(solution)/shard_map/ppermute | solution.py:510
  23.4 7.3 %collective-permute-start.11 = (bf16[256,256]{1,0:T(8,128)(2,1)S(1)}, bf16[256,256]{1,0:T(8,128)(2,1)S(1)}, u32[]{:S(2)}, u32[]{:S(2)}) collective-permute-start(bf16[256,256]{1,0:T(8,128)(2,1)S(1)} %get-tuple-element.84.refs_6_), channel_id=1, source_target_pairs={{2,0},{3,1},{0,2},{1,3},{6,4},{7,5},{4,6},{5,7},{10,8},{11,9},{8,1... | collective-permute-start | bytes 393224 | tf_op jit(solution)/shard_map/ppermute | solution.py:511
  28.6 17.0 %collective-permute-start.18 = (bf16[768,256]{1,0:T(8,128)(2,1)S(1)}, bf16[768,256]{1,0:T(8,128)(2,1)S(1)}, u32[]{:S(2)}, u32[]{:S(2)}) collective-permute-start(bf16[768,256]{1,0:T(8,128)(2,1)S(1)} %decoder_grad.6.refs_2_.refs_6_), channel_id=1, source_target_pairs={{0,2},{1,3},{2,0},{3,1},{4,6},{5,7},{6,4},{7,5},{8,10},{9,11},{10,... | collective-permute-start | bytes 1179656 | tf_op jit(solution)/shard_map/ppermute | solution.py:513
  30.2 7.2 %collective-permute-start.12 = (bf16[384,256]{1,0:T(8,128)(2,1)S(1)}, bf16[384,256]{1,0:T(8,128)(2,1)S(1)}, u32[]{:S(2)}, u32[]{:S(2)}) collective-permute-start(bf16[384,256]{1,0:T(8,128)(2,1)S(1)} %get-tuple-element.82.refs_5_.refs_3_), channel_id=1, source_target_pairs={{0,1},{1,0},{2,3},{3,2},{4,5},{5,4},{6,7},{7,6},{8,9},{9,8},{10,11... | collective-permute-start | bytes 589832 | tf_op jit(solution)/shard_map/ppermute | solution.py:510
  30.8 10.7 %collective-permute-start.4 = (bf16[256,256]{1,0:T(8,128)(2,1)S(1)}, bf16[256,256]{1,0:T(8,128)(2,1)S(1)}, u32[]{:S(2)}, u32[]{:S(2)}) collective-permute-start(bf16[256,256]{1,0:T(8,128)(2,1)S(1)} %add_quarters.2.refs_3_.refs_1_), channel_id=1, source_target_pairs={{0,16},{4,20},{8,24},{12,28},{16,0},{20,4},{24,8},{28,12},{1,17},{... | collective-permute-start | bytes 393224 | tf_op jit(solution)/shard_map/ppermute | solution.py:515
  36.9 8.3 %collective-permute-start.19 = (bf16[256,256]{1,0:T(8,128)(2,1)S(1)}, bf16[256,256]{1,0:T(8,128)(2,1)S(1)}, u32[]{:S(2)}, u32[]{:S(2)}) collective-permute-start(bf16[256,256]{1,0:T(8,128)(2,1)S(1)} %decoder_grad.7.refs_8_.refs_3_), channel_id=1, source_target_pairs={{0,2},{1,3},{2,0},{3,1},{4,6},{5,7},{6,4},{7,5},{8,10},{9,11},{10,... | collective-permute-start | bytes 393224 | tf_op jit(solution)/shard_map/ppermute | solution.py:513
  39.9 12.3 %collective-permute-start.22 = (bf16[512,256]{1,0:T(8,128)(2,1)S(1)}, bf16[512,256]{1,0:T(8,128)(2,1)S(1)}, u32[]{:S(2)}, u32[]{:S(2)}) collective-permute-start(bf16[512,256]{1,0:T(8,128)(2,1)S(1)} %encoder_grad.12.refs_3_), channel_id=1, source_target_pairs={{0,2},{1,3},{2,0},{3,1},{4,6},{5,7},{6,4},{7,5},{8,10},{9,11},{10,... | collective-permute-start | bytes 786440 | tf_op jit(solution)/shard_map/ppermute | solution.py:513
  46.0 8.0 %collective-permute-start.21 = (bf16[256,256]{1,0:T(8,128)(2,1)S(1)}, bf16[256,256]{1,0:T(8,128)(2,1)S(1)}, u32[]{:S(2)}, u32[]{:S(2)}) collective-permute-start(bf16[256,256]{1,0:T(8,128)(2,1)S(1)} %encoder_grad.13.refs_3_), channel_id=1, source_target_pairs={{0,2},{1,3},{2,0},{3,1},{4,6},{5,7},{6,4},{7,5},{8,10},{9,11},{10,... | collective-permute-start | bytes 393224 | tf_op jit(solution)/shard_map/ppermute | solution.py:513
  47.2 7.6 %collective-permute-start.20 = (bf16[256,256]{1,0:T(8,128)(2,1)S(1)}, bf16[256,256]{1,0:T(8,128)(2,1)S(1)}, u32[]{:S(2)}, u32[]{:S(2)}) collective-permute-start(bf16[256,256]{1,0:T(8,128)(2,1)S(1)} %encoder_grad.14.refs_3_), channel_id=1, source_target_pairs={{0,2},{1,3},{2,0},{3,1},{4,6},{5,7},{6,4},{7,5},{8,10},{9,11},{10,... | collective-permute-start | bytes 393224 | tf_op jit(solution)/shard_map/ppermute | solution.py:513
  55.6 8.4 %collective-permute-start.25 = (bf16[1024,256]{1,0:T(8,128)(2,1)S(1)}, bf16[1024,256]{1,0:T(8,128)(2,1)S(1)}, u32[]{:S(2)}, u32[]{:S(2)}) collective-permute-start(bf16[1024,256]{1,0:T(8,128)(2,1)S(1)} %get-tuple-element.93.refs_7_.refs_3_.refs_1_), channel_id=1, source_target_pairs={{0,1},{1,0},{2,3},{3,2},{4,5},{5,4},{6,7},{7,6},{8,9},{9,8},{10,11... | collective-permute-start | bytes 1572872 | tf_op jit(solution)/shard_map/ppermute | solution.py:510
  55.7 14.8 %collective-permute-start.26 = (bf16[1024,256]{1,0:T(8,128)(2,1)S(1)}, bf16[1024,256]{1,0:T(8,128)(2,1)S(1)}, u32[]{:S(2)}, u32[]{:S(2)}) collective-permute-start(bf16[1024,256]{1,0:T(8,128)(2,1)S(1)} %get-tuple-element.93.refs_7_.refs_3_.refs_1_), channel_id=1, source_target_pairs={{2,0},{3,1},{0,2},{1,3},{6,4},{7,5},{4,6},{5,7},{10,8},{11,9},{8,1... | collective-permute-start | bytes 1572872 | tf_op jit(solution)/shard_map/ppermute | solution.py:511
  59.6 19.3 %collective-permute-start.24 = (bf16[768,256]{1,0:T(8,128)(2,1)S(1)}, bf16[768,256]{1,0:T(8,128)(2,1)S(1)}, u32[]{:S(2)}, u32[]{:S(2)}) collective-permute-start(bf16[768,256]{1,0:T(8,128)(2,1)S(1)} %get-tuple-element.96.refs_5_), channel_id=1, source_target_pairs={{2,0},{3,1},{0,2},{1,3},{6,4},{7,5},{4,6},{5,7},{10,8},{11,9},{8,1... | collective-permute-start | bytes 1179656 | tf_op jit(solution)/shard_map/ppermute | solution.py:511
  71.1 11.9 %collective-permute-start.23 = (bf16[1024,256]{1,0:T(8,128)(2,1)S(1)}, bf16[1024,256]{1,0:T(8,128)(2,1)S(1)}, u32[]{:S(2)}, u32[]{:S(2)}) collective-permute-start(bf16[1024,256]{1,0:T(8,128)(2,1)S(1)} %get-tuple-element.95.refs_8_.refs_1_), channel_id=1, source_target_pairs={{0,1},{1,0},{2,3},{3,2},{4,5},{5,4},{6,7},{7,6},{8,9},{9,8},{10,11... | collective-permute-start | bytes 1572872 | tf_op jit(solution)/shard_map/ppermute | solution.py:510
  71.2 10.1 %collective-permute-start.29 = (bf16[256,256]{1,0:T(8,128)(2,1)S(1)}, bf16[256,256]{1,0:T(8,128)(2,1)S(1)}, u32[]{:S(2)}, u32[]{:S(2)}) collective-permute-start(bf16[256,256]{1,0:T(8,128)(2,1)S(1)} %get-tuple-element.103.refs_6_), channel_id=1, source_target_pairs={{2,0},{3,1},{0,2},{1,3},{6,4},{7,5},{4,6},{5,7},{10,8},{11,9},{8,1... | collective-permute-start | bytes 393224 | tf_op jit(solution)/shard_map/ppermute | solution.py:511
  81.7 14.9 %collective-permute-start.33 = (bf16[1024,256]{1,0:T(8,128)(2,1)S(1)}, bf16[1024,256]{1,0:T(8,128)(2,1)S(1)}, u32[]{:S(2)}, u32[]{:S(2)}) collective-permute-start(bf16[1024,256]{1,0:T(8,128)(2,1)S(1)} %decoder_grad.10.refs_8_.refs_3_), channel_id=1, source_target_pairs={{0,2},{1,3},{2,0},{3,1},{4,6},{5,7},{6,4},{7,5},{8,10},{9,11},{10,... | collective-permute-start | bytes 1572872 | tf_op jit(solution)/shard_map/ppermute | solution.py:513
  88.5 14.0 %collective-permute-start.36 = (bf16[512,256]{1,0:T(8,128)(2,1)S(1)}, bf16[512,256]{1,0:T(8,128)(2,1)S(1)}, u32[]{:S(2)}, u32[]{:S(2)}) collective-permute-start(bf16[512,256]{1,0:T(8,128)(2,1)S(1)} %encoder_grad.18.refs_3_), channel_id=1, source_target_pairs={{0,2},{1,3},{2,0},{3,1},{4,6},{5,7},{6,4},{7,5},{8,10},{9,11},{10,... | collective-permute-start | bytes 786440 | tf_op jit(solution)/shard_map/ppermute | solution.py:513
  96.9 8.1 %collective-permute-start.35 = (bf16[256,256]{1,0:T(8,128)(2,1)S(1)}, bf16[256,256]{1,0:T(8,128)(2,1)S(1)}, u32[]{:S(2)}, u32[]{:S(2)}) collective-permute-start(bf16[256,256]{1,0:T(8,128)(2,1)S(1)} %encoder_grad.22.refs_3_), channel_id=1, source_target_pairs={{0,2},{1,3},{2,0},{3,1},{4,6},{5,7},{6,4},{7,5},{8,10},{9,11},{10,... | collective-permute-start | bytes 393224 | tf_op jit(solution)/shard_map/ppermute | solution.py:513
  98.0 8.6 %collective-permute-start.34 = (bf16[256,256]{1,0:T(8,128)(2,1)S(1)}, bf16[256,256]{1,0:T(8,128)(2,1)S(1)}, u32[]{:S(2)}, u32[]{:S(2)}) collective-permute-start(bf16[256,256]{1,0:T(8,128)(2,1)S(1)} %encoder_grad.23.refs_7_), channel_id=1, source_target_pairs={{0,2},{1,3},{2,0},{3,1},{4,6},{5,7},{6,4},{7,5},{8,10},{9,11},{10,... | collective-permute-start | bytes 393224 | tf_op jit(solution)/shard_map/ppermute | solution.py:513
  (22 other events, 91.1 us)
